TPU v7x, 32 devices: a whole 2x2x4 slice. The times are simulated.
32 devices in a mesh: dp: 8 (over y, x, core), tensor: 4 (over z).
Axes of the slice: x: 2, y: 2, z: 4, core: 2. Of those that a mesh axis runs over, the one named last changes fastest.
Arguments:
- tokens: bfloat16 [4096, 2048], P('dp', 'tensor'), may hold values from -6 to 6
- series_ids: int32 [4096], replicated, may hold values from 0 to 7, never falling along the last dimension, each value on 1 to 2560 neighbouring positions
- offsets: int32 [4096], P('dp'), may hold values from 0 to 65535
- norm_gain: float32 [2048], replicated, may hold values from 0.5 to 1.5
- mlp_gain: float32 [2048], replicated, may hold values from 0.5 to 1.5
- w_query: bfloat16 [2048, 2048], P(None, 'tensor')
- w_key: bfloat16 [2048, 2048], P(None, 'tensor')
- w_value: bfloat16 [2048, 2048], P(None, 'tensor'), may hold values from -0.125 to 0.125
- w_out: bfloat16 [2048, 2048], P('tensor'), may hold values from -0.125 to 0.125
- w_gate: bfloat16 [2048, 8192], P(None, 'tensor'), may hold values from -0.125 to 0.125
- w_up: bfloat16 [2048, 8192], P(None, 'tensor'), may hold values from -0.125 to 0.125
- w_down: bfloat16 [8192, 2048], P('tensor'), may hold values from -0.0625 to 0.0625
- projector: bfloat16 [2048, 512], replicated, may hold values from -0.125 to 0.125
- student_in: bfloat16 [4096, 512], P('dp'), may hold values from -6 to 6
- s_gate: bfloat16 [512, 2048], P(None, 'tensor'), may hold values from -0.25 to 0.25
- s_up: bfloat16 [512, 2048], P(None, 'tensor'), may hold values from -0.25 to 0.25
- s_down: bfloat16 [2048, 512], P('tensor'), may hold values from -0.125 to 0.125
Outputs:
- teacher_out: bfloat16 [4096, 2048], P('dp', 'tensor')
- grad_gate: float32 [512, 2048], P(None, 'tensor')
- grad_up: float32 [512, 2048], P(None, 'tensor')
- grad_down: float32 [2048, 512], P('tensor')
- error: float32 [], replicated
Inputs may be any that keep to these rules, and one draw needn't show every extreme that they name: `series_ids`: ids never fall along the window; each series covers 1 to 2560 consecutive rows, one series exactly that many.
All inputs are finite; a program needn't handle non-finite values.
Results may differ from a plain program's by a relative error of at most 0.025.
Values may be sent and summed in bfloat16 or wider, within the bound.
No kernel may reach another device: no remote copies, remote signals or barrier semaphores. Data moves between devices by JAX's collectives and lax.ppermute only.
A program may use at most 128 MiB of HBM per device.

v0:
```python
import jax
import jax.numpy as jnp
from jax import lax
from jax.sharding import PartitionSpec as P

HD = 128


def rms_scale(values):
    return values * lax.rsqrt(jnp.mean(values * values, axis=-1, keepdims=True) + 1e-05)


def frequencies(head_dim):
    indices = jnp.arange(head_dim // 2).astype(jnp.float32)
    return jnp.exp(-jnp.log(500000.0) * 2.0 * indices / head_dim)


def rotary(inputs, angles):
    half_dim = inputs.shape[-1] // 2
    cosine = jnp.cos(angles)
    sine = jnp.sin(angles)
    first_half = inputs[..., :half_dim]
    second_half = inputs[..., half_dim:]
    return jnp.concatenate(
        [first_half * cosine - second_half * sine, first_half * sine + second_half * cosine],
        axis=-1,
    )


def local(
    tokens,
    series_ids,
    offsets,
    norm_gain,
    mlp_gain,
    w_query,
    w_key,
    w_value,
    w_out,
    w_gate,
    w_up,
    w_down,
    projector,
    student_in,
    s_gate,
    s_up,
    s_down,
):
    row_count = tokens.shape[0]
    heads_dev = w_query.shape[1] // HD
    first_row = lax.axis_index("dp") * row_count
    tokens_full = lax.all_gather(tokens, "tensor", axis=1, tiled=True).astype(jnp.float32)
    normed = (rms_scale(tokens_full) * norm_gain).astype(jnp.bfloat16)
    angles = offsets.astype(jnp.float32)[:, None, None] * frequencies(HD)[None, None, :]
    queries = rotary(
        jnp.dot(normed, w_query, preferred_element_type=jnp.float32).reshape(
            row_count, heads_dev, HD
        ),
        angles,
    ).astype(jnp.bfloat16)
    keys_rot = rotary(
        jnp.dot(normed, w_key, preferred_element_type=jnp.float32).reshape(
            row_count, heads_dev, HD
        ),
        angles,
    ).astype(jnp.bfloat16)
    values_mine = jnp.dot(normed, w_value, preferred_element_type=jnp.float32).astype(jnp.bfloat16)
    keys_flat = keys_rot.reshape(row_count, heads_dev * HD)
    query_pos = first_row + jnp.arange(row_count, dtype=jnp.int32)
    query_series = lax.dynamic_slice_in_dim(series_ids, first_row, row_count, 0)
    factor = HD ** (-0.5)
    peak = jnp.full((row_count, heads_dev), -1e30, jnp.float32)
    key_block = lax.all_gather(keys_flat, "dp", axis=0, tiled=True)
    value_block = lax.all_gather(values_mine, "dp", axis=0, tiled=True)
    count = key_block.shape[0]
    key_pos = jnp.arange(count, dtype=jnp.int32)
    allowed = (
        (key_pos[None, :] >= 0)
        & (key_pos[None, :] <= query_pos[:, None])
        & (series_ids[None, :] == query_series[:, None])
    )
    scores = (
        jnp.einsum(
            "qhd,khd->qhk",
            queries,
            key_block.reshape(count, heads_dev, HD),
            preferred_element_type=jnp.float32,
        )
        * factor
    )
    scores = jnp.where(allowed[:, None, :], scores, -1e30)
    new_peak = jnp.maximum(peak, jnp.max(scores, axis=2))
    weights = jnp.where(allowed[:, None, :], jnp.exp(scores - new_peak[:, :, None]), 0.0)
    denom = jnp.sum(weights, axis=2)
    accum = jnp.einsum(
        "qhk,khd->qhd",
        weights.astype(jnp.bfloat16),
        value_block.reshape(count, heads_dev, HD),
        preferred_element_type=jnp.float32,
    )
    peak, denom, accum = (new_peak, denom, accum)
    attended = (accum / denom[:, :, None]).astype(jnp.bfloat16).reshape(row_count, heads_dev * HD)
    partial_out = jnp.dot(attended, w_out, preferred_element_type=jnp.float32)
    own_sum = lax.psum_scatter(
        partial_out.astype(jnp.bfloat16), "tensor", scatter_dimension=1, tiled=True
    ).astype(jnp.float32)
    mixed_own = (tokens.astype(jnp.float32) + own_sum).astype(jnp.bfloat16)
    mixed = lax.all_gather(mixed_own, "tensor", axis=1, tiled=True)
    normed_two = (rms_scale(mixed.astype(jnp.float32)) * mlp_gain).astype(jnp.bfloat16)
    gate_out = jnp.dot(normed_two, w_gate, preferred_element_type=jnp.float32)
    up_out = jnp.dot(normed_two, w_up, preferred_element_type=jnp.float32)
    hidden = (jax.nn.silu(gate_out) * up_out).astype(jnp.bfloat16)
    mlp_part = jnp.dot(hidden, w_down, preferred_element_type=jnp.float32)
    mlp_own = lax.psum_scatter(
        mlp_part.astype(jnp.bfloat16), "tensor", scatter_dimension=1, tiled=True
    ).astype(jnp.float32)
    teacher_out = (mixed_own.astype(jnp.float32) + mlp_own).astype(jnp.bfloat16)
    student_full = student_in.astype(jnp.float32)
    student_normed = rms_scale(student_full).astype(jnp.bfloat16)
    s_gate_out = jnp.dot(student_normed, s_gate, preferred_element_type=jnp.float32)
    s_up_out = jnp.dot(student_normed, s_up, preferred_element_type=jnp.float32)
    sigmoid_gate = jax.nn.sigmoid(s_gate_out)
    s_hidden = (s_gate_out * sigmoid_gate * s_up_out).astype(jnp.bfloat16)
    student_part = jnp.dot(s_hidden, s_down, preferred_element_type=jnp.float32)
    teacher_full = lax.all_gather(teacher_out, "tensor", axis=1, tiled=True)
    target = jnp.dot(teacher_full, projector, preferred_element_type=jnp.float32)
    student_summed = lax.psum(student_part.astype(jnp.bfloat16), "tensor").astype(jnp.float32)
    difference = student_full + student_summed - target
    total_rows = row_count * lax.axis_size("dp")
    scaled = (difference * total_rows ** (-0.5)).astype(jnp.bfloat16)
    grad_down_part = jnp.einsum("rk,rc->kc", s_hidden, scaled, preferred_element_type=jnp.float32)
    grad_hidden = jnp.einsum("rc,kc->rk", scaled, s_down, preferred_element_type=jnp.float32)
    grad_up_in = (grad_hidden * s_gate_out * sigmoid_gate).astype(jnp.bfloat16)
    grad_gate_in = (
        grad_hidden * s_up_out * sigmoid_gate * (1.0 + s_gate_out * (1.0 - sigmoid_gate))
    ).astype(jnp.bfloat16)
    grad_gate_part = jnp.einsum(
        "rc,rk->ck", student_normed, grad_gate_in, preferred_element_type=jnp.float32
    )
    grad_up_part = jnp.einsum(
        "rc,rk->ck", student_normed, grad_up_in, preferred_element_type=jnp.float32
    )
    square_sum = jnp.sum(difference * difference)
    grad_gate, grad_up, grad_down, square_total = (
        lax.psum(grad_gate_part.astype(jnp.bfloat16), "dp").astype(jnp.float32),
        lax.psum(grad_up_part.astype(jnp.bfloat16), "dp").astype(jnp.float32),
        lax.psum(grad_down_part.astype(jnp.bfloat16), "dp").astype(jnp.float32),
        lax.psum(square_sum.astype(jnp.bfloat16), "dp").astype(jnp.float32),
    )
    error = square_total / (total_rows * difference.shape[1])
    return (teacher_out, grad_gate, grad_up, grad_down, error)


def solution(mesh):
    in_specs = (
        P("dp", "tensor"),
        P(),
        P("dp"),
        P(),
        P(),
        P(None, "tensor"),
        P(None, "tensor"),
        P(None, "tensor"),
        P("tensor", None),
        P(None, "tensor"),
        P(None, "tensor"),
        P("tensor", None),
        P(),
        P("dp", None),
        P(None, "tensor"),
        P(None, "tensor"),
        P("tensor", None),
    )
    out_specs = (P("dp", "tensor"), P(None, "tensor"), P(None, "tensor"), P("tensor", None), P())
    return jax.shard_map(local, mesh=mesh, in_specs=in_specs, out_specs=out_specs, check_vma=False)
```

profile of v0, /device:TPU:0, one launch (start us, length us, event | category | flops | bytes accessed | tf_op | source)
XLA Modules:
  0.0 519.4 jit_solution(2554727985998131553)
XLA Ops:
  7.2 0.0 all-gather.6.cloned.1.call-start
  7.2 0.7 all-gather.6.cloned.1.call-update
  7.9 0.0 all-gather.10.cloned.1.call-start
  8.0 0.7 convert_element_type.116
  8.7 1.7 multiply_cosine_fusion
  10.4 47.9 %all-gather.6.cloned.1.call-done = bf16[512,2048]{1,0:T(8,128)(2,1)} async-done(((bf16[512,512]{1,0:T(8,128)(2,1)}), bf16[512,2048]{1,0:T(8,128)(2,1)}) %all-gather.6.cloned.1.call-update) | async-done | bytes 2097168 | tf_op jit(solution)/shard_map/all_gather | solution.py:52
  58.3 2.1 fusion.7
  60.3 3.6 fusion.44
  64.0 1.1 fusion.48
  65.1 1.4 copy.39
  66.4 2.4 copy.40
  68.8 3.6 fusion.42
  72.4 1.1 fusion.47
  73.5 2.4 copy.41
  75.8 2.4 copy.42
  78.2 3.5 subtract_convert_fusion
  81.6 0.3 pad_maximum_fusion
  81.9 1.0 copy.30
  82.9 0.0 all-gather.10.cloned.1.call-update
  83.0 0.0 all-gather.8.cloned.1.call-start
  83.1 4.4 convolution_convert_fusion.6
  87.5 0.2 reduce-scatter.3.cloned.1.call-start
  87.7 0.1 dynamic_slice.3
  87.8 3.1 fusion.6
  91.0 28.3 %all-gather.10.cloned.1.call-done = bf16[4096,512]{0,1:T(8,128)(2,1)} async-done(((bf16[512,512]{0,1:T(8,128)(2,1)}), bf16[4096,512]{0,1:T(8,128)(2,1)}) %all-gather.10.cloned.1.call-update) | async-done | bytes 4194320 | tf_op jit(solution)/shard_map/all_gather | solution.py:73
  119.3 17.2 %fusion = (f32[512,4]{0,1:T(4,128)S(1)}, f32[4,4096,512]{2,1,0:T(8,128)}) fusion(pred[512,4096]{0,1:T(8,128)(4,1)} %fusion.6, bf16[4096,4,128]{0,2,1:T(8,128)(2,1)} %bitcast.52, bf16[512,4,64]{2,0,1:T(8,128)(2,1)S(1)} %copy-done.12, bf16[512,4,64]{2,0,1:T(8,128)(2,1)S(1)} %copy-done.11), kind=kOutput, calls=%fused_computation.2 | convolution fusion | flops 2173696000 | bytes 40378368 | tf_op jit(solution)/shard_map/qhd,khd->qhk/dot_general | solution.py:83
  136.5 15.2 %fusion.1 = f32[512,4]{0,1:T(4,128)S(1)} fusion(f32[4,4096,512]{2,1,0:T(8,128)} %get-tuple-element.21, f32[512,4]{0,1:T(4,128)S(1)} %broadcast_maximum_fusion, pred[512,4096]{0,1:T(8,128)(4,1)S(1)} %copy-done.2), kind=kLoop, calls=%fused_computation.3 | loop fusion | flops 41940992 | bytes 35667968 | tf_op jit(solution)/shard_map/reduce_sum | solution.py:94
  151.7 6.8 %all-gather.8.cloned.1.call-done = bf16[4096,512]{1,0:T(8,128)(2,1)} async-done(((bf16[512,512]{1,0:T(8,128)(2,1)}), bf16[4096,512]{1,0:T(8,128)(2,1)}) %all-gather.8.cloned.1.call-update) | async-done | bytes 4194320 | tf_op jit(solution)/shard_map/all_gather | solution.py:74
  158.5 6.4 %copy.38 = bf16[4096,512]{0,1:T(8,128)(2,1)} copy(bf16[4096,512]{1,0:T(8,128)(2,1)} %all-gather.8.cloned.1.call-done) | data formatting | bytes 8388608 | tf_op jit(solution)/shard_map/reshape | solution.py:98
  164.9 17.0 %divide_convert_fusion = bf16[512,4,128]{0,2,1:T(8,128)(2,1)S(1)} fusion(bf16[4096,4,128]{0,2,1:T(8,128)(2,1)} %bitcast.48, f32[4,4096,512]{2,1,0:T(8,128)} %get-tuple-element.21, f32[512,4]{0,1:T(4,128)S(1)} %broadcast_maximum_fusion, pred[512,4096]{0,1:T(8,128)(4,1)} %fusion.6, f32[512,4]{0,1:T(4,128)S(1)} %fusion.1), kind=kOutput, calls=%fused_computation.42 | convolution fusion | flops 2189950976 | bytes 40386560 | tf_op jit(solution)/shard_map/qhk,khd->qhd/dot_general | solution.py:95
  181.9 2.6 convolution_convert_fusion.1
  184.6 0.0 all-gather.12.cloned.1.call-start
  184.6 44.0 %reduce-scatter.3.cloned.1.call-done = bf16[512,512]{1,0:T(8,128)(2,1)} async-done(((bf16[512,2048]{1,0:T(8,128)(2,1)}), bf16[512,512]{1,0:T(8,128)(2,1)}) %reduce-scatter.3.cloned.1.call-update) | async-done | bytes 524304 | tf_op jit(solution)/shard_map/reduce_scatter | solution.py:104
  228.6 2.0 add_convert_fusion.1
  230.5 0.0 all-gather.12.cloned.1.call-update
  230.6 0.3 reduce-scatter.5.cloned.1.call-start
  230.8 45.1 %all-gather.12.cloned.1.call-done = bf16[512,2048]{1,0:T(8,128)(2,1)} async-done(((bf16[512,512]{1,0:T(8,128)(2,1)}), bf16[512,2048]{1,0:T(8,128)(2,1)}) %all-gather.12.cloned.1.call-update) | async-done | bytes 2097168 | tf_op jit(solution)/shard_map/all_gather | solution.py:108
  276.0 2.1 fusion.10
  278.1 10.6 %fusion.21 = f32[512,2048]{1,0:T(8,128)} fusion(bf16[2048,2048]{1,0:T(8,128)(2,1)} %param.26, bf16[512,2048]{1,0:T(8,128)(2,1)} %all-gather.12.cloned.1.call-done, f32[2048]{0:T(1024)S(1)} %copy-done.16, f32[512]{0:T(512)S(1)} %add_rsqrt_fusion.1), kind=kOutput, calls=%fused_computation.47 | convolution fusion | flops 4299161600 | bytes 14690304 | tf_op jit(solution)/shard_map/dot_general | solution.py:110
  288.7 17.6 %convolution_convert_fusion = bf16[512,2048]{1,0:T(8,128)(2,1)} fusion(bf16[2048,2048]{1,0:T(8,128)(2,1)} %param.28, f32[512,2048]{1,0:T(8,128)} %fusion.21, bf16[2048,2048]{1,0:T(8,128)(2,1)} %param.27, bf16[512,2048]{1,0:T(8,128)(2,1)S(1)} %copy-done.7, f32[2048]{0:T(1024)S(1)} %copy-done.16, f32[512]{0:T(512)S(1)} %add_rsqrt_fusion.1), kind=kOutput, calls=%fused_computation.20 | convolution fusion | flops 8601468928 | bytes 25176064 | tf_op jit(solution)/shard_map/dot_general | solution.py:113
  306.4 0.0 all-reduce.4.cloned.1.call-start
  306.4 0.2 fusion.16
  306.6 0.5 fusion.40
  307.1 1.0 copy-done.8
  308.1 1.5 multiply_convert_fusion.4
  309.6 1.2 convolution_convert_fusion.5
  310.8 0.0 all-reduce.4.cloned.1.call-update
  310.8 0.0 all-gather.14.cloned.1.call-start
  310.9 38.2 %reduce-scatter.5.cloned.1.call-done = bf16[512,512]{1,0:T(8,128)(2,1)} async-done(((bf16[512,2048]{1,0:T(8,128)(2,1)}), bf16[512,512]{1,0:T(8,128)(2,1)}) %reduce-scatter.5.cloned.1.call-update) | async-done | bytes 524304 | tf_op jit(solution)/shard_map/reduce_scatter | solution.py:114
  349.1 2.0 add_convert_fusion
  351.1 0.0 all-gather.14.cloned.1.call-update
  351.1 0.3 all-reduce.6.cloned.1.call-start
  351.4 38.2 %all-reduce.4.cloned.1.call-done = bf16[512,512]{1,0:T(8,128)(2,1)} async-done(((bf16[512,512]{1,0:T(8,128)(2,1)}), bf16[512,512]{1,0:T(8,128)(2,1)}) %all-reduce.4.cloned.1.call-update) | async-done | bytes 524304 | tf_op jit(solution)/shard_map/psum | solution.py:127
  389.7 48.1 %all-gather.14.cloned.1.call-done = bf16[512,2048]{1,0:T(8,128)(2,1)} async-done(((bf16[512,512]{1,0:T(8,128)(2,1)}), bf16[512,2048]{1,0:T(8,128)(2,1)}) %all-gather.14.cloned.1.call-update) | async-done | bytes 2097168 | tf_op jit(solution)/shard_map/all_gather | solution.py:125
  437.8 4.3 multiply_reduce_fusion
  442.1 1.3 convolution_convert_fusion.2
  443.4 0.5 fusion.27
  443.8 1.5 convolution_convert_fusion.3
  445.3 1.6 convolution_convert_fusion.4
  447.0 14.5 %psum.39 = bf16[]{:T(256)} all-reduce(bf16[]{:T(256)} %get-tuple-element.24), channel_id=1, replica_groups=mesh['dp'=8,'tensor'=4] {'dp'}, use_global_device_ids=true, to_apply=%region_12.13 | all-reduce | flops 1 | bytes 4 | tf_op jit(solution)/shard_map/psum | solution.py:148
  462.1 43.2 %all-reduce.6.cloned.1.call-done = (bf16[512,512]{1,0:T(8,128)(2,1)}, bf16[512,512]{1,0:T(8,128)(2,1)}, bf16[512,512]{1,0:T(8,128)(2,1)}) async-done(((bf16[512,512]{1,0:T(8,128)(2,1)}, bf16[512,512]{1,0:T(8,128)(2,1)}, bf16[512,512]{1,0:T(8,128)(2,1)}), (bf16[512,512]{1,0:T(8,128)(2,1)}, bf16[512,512]{1,0:T(8,128)(2,1)}, bf16[512,512]{1,0:T(8,128)(2,1)})) %all-reduce.6.cloned.1.call-update) | async-done | bytes 1572880 | tf_op jit(solution)/shard_map/psum | solution.py:145
  505.3 2.1 convert_element_type.139
  507.4 2.1 convert_element_type.142
  509.6 2.1 convert_element_type.144
  (45 shorter events, 0.2 us)
Async XLA Ops:
  7.2 174.8 %copy-start = (bf16[512,2048]{1,0:T(8,128)(2,1)S(1)}, bf16[512,2048]{1,0:T(8,128)(2,1)}, u32[]{:S(2)}) copy-start(bf16[512,2048]{1,0:T(8,128)(2,1)} %param.25) | copy-start | bytes 6291460
  7.2 51.1 %all-gather.6.cloned.1.call-start = ((), (), s32[]{:S(2)}) async-start(), calls=%async_computation.2 | async-start | bytes 2621440 | tf_op jit(solution)/shard_map/all_gather | solution.py:52
  7.9 111.4 %all-gather.10.cloned.1.call-start = ((), (), s32[]{:S(2)}) async-start(), calls=%async_computation.4 | async-start | bytes 4718592 | tf_op jit(solution)/shard_map/all_gather | solution.py:73
  64.0 4.8 copy-start.15
  83.0 4.7 copy-start.13
  83.0 36.3 %copy-start.11 = (bf16[512,4,64]{2,0,1:T(8,128)(2,1)S(1)}, bf16[512,4,64]{2,0,1:T(8,128)(2,1)}, u32[]{:S(2)}) copy-start(bf16[512,4,64]{2,0,1:T(8,128)(2,1)} %get-tuple-element.8) | copy-start | bytes 786436
  83.0 36.3 %copy-start.12 = (bf16[512,4,64]{2,0,1:T(8,128)(2,1)S(1)}, bf16[512,4,64]{2,0,1:T(8,128)(2,1)}, u32[]{:S(2)}) copy-start(bf16[512,4,64]{2,0,1:T(8,128)(2,1)} %get-tuple-element.9) | copy-start | bytes 786436
  83.0 75.5 %all-gather.8.cloned.1.call-start = ((), (), s32[]{:S(2)}) async-start(), calls=%async_computation.3 | async-start | bytes 4718592 | tf_op jit(solution)/shard_map/all_gather | solution.py:74
  87.5 141.1 %reduce-scatter.3.cloned.1.call-start = ((), (), s32[]{:S(2)}) async-start(), calls=%async_computation.5 | async-start | bytes 2621440 | tf_op jit(solution)/shard_map/reduce_scatter | solution.py:104
  119.3 17.2 %copy-start.2 = (pred[512,4096]{0,1:T(8,128)(4,1)S(1)}, pred[512,4096]{0,1:T(8,128)(4,1)}, u32[]{:S(2)}) copy-start(pred[512,4096]{0,1:T(8,128)(4,1)} %fusion.6) | copy-start | bytes 6291460
  181.9 46.7 %copy-start.5 = (bf16[512,512]{1,0:T(8,128)(2,1)S(1)}, bf16[512,512]{1,0:T(8,128)(2,1)}, u32[]{:S(2)}) copy-start(bf16[512,512]{1,0:T(8,128)(2,1)} %param.17) | copy-start | bytes 1572868
  184.5 93.5 %copy-start.16 = (f32[2048]{0:T(1024)S(1)}, f32[2048]{0:T(1024)}, u32[]{:S(2)}) copy-start(f32[2048]{0:T(1024)} %param.21) | copy-start | bytes 24580
  184.6 91.4 %all-gather.12.cloned.1.call-start = ((), (), s32[]{:S(2)}) async-start(), calls=%async_computation.6 | async-start | bytes 2621440 | tf_op jit(solution)/shard_map/all_gather | solution.py:108
  230.6 118.5 %reduce-scatter.5.cloned.1.call-start = ((), (), s32[]{:S(2)}) async-start(), calls=%async_computation.7 | async-start | bytes 2621440 | tf_op jit(solution)/shard_map/reduce_scatter | solution.py:114
  278.1 10.7 %copy-start.7 = (bf16[512,2048]{1,0:T(8,128)(2,1)S(1)}, bf16[512,2048]{1,0:T(8,128)(2,1)}, u32[]{:S(2)}) copy-start(bf16[512,2048]{1,0:T(8,128)(2,1)} %all-gather.12.cloned.1.call-done) | copy-start | bytes 6291460
  288.7 17.7 %copy-start.6 = (bf16[512,512]{1,0:T(8,128)(2,1)S(1)}, bf16[512,512]{1,0:T(8,128)(2,1)}, u32[]{:S(2)}) copy-start(bf16[512,512]{1,0:T(8,128)(2,1)} %param.30) | copy-start | bytes 1572868
  288.7 17.9 %copy-start.10 = (bf16[512,512]{1,0:T(8,128)(2,1)S(1)}, bf16[512,512]{1,0:T(8,128)(2,1)}, u32[]{:S(2)}) copy-start(bf16[512,512]{1,0:T(8,128)(2,1)} %param.31) | copy-start | bytes 1572868
  306.3 1.8 copy-start.14
  306.4 83.3 %all-reduce.4.cloned.1.call-start = ((), (), s32[]{:S(2)}) async-start(), calls=%async_computation.8 | async-start | bytes 1048576 | tf_op jit(solution)/shard_map/psum | solution.py:127
  306.6 2.9 copy-start.4
  307.1 1.0 copy-start.8
  308.1 41.0 %copy-start.3 = (bf16[512,512]{1,0:T(8,128)(2,1)S(1)}, bf16[512,512]{1,0:T(8,128)(2,1)}, u32[]{:S(2)}) copy-start(bf16[512,512]{1,0:T(8,128)(2,1)} %add_convert_fusion.1) | copy-start | bytes 1572868
  310.8 126.9 %all-gather.14.cloned.1.call-start = ((), (), s32[]{:S(2)}) async-start(), calls=%async_computation.9 | async-start | bytes 2621440 | tf_op jit(solution)/shard_map/all_gather | solution.py:125
  351.1 154.2 %all-reduce.6.cloned.1.call-start = ((), (), s32[]{:S(2)}) async-start(), calls=%async_computation.10 | async-start | bytes 3145728 | tf_op jit(solution)/shard_map/psum | solution.py:145
  442.1 1.8 copy-start.9
  443.4 2.0 copy-start.17
  445.3 66.4 %copy-start.1 = (bf16[512,2048]{1,0:T(8,128)(2,1)S(1)}, bf16[512,2048]{1,0:T(8,128)(2,1)}, u32[]{:S(2)}) copy-start(bf16[512,2048]{1,0:T(8,128)(2,1)} %param.25) | copy-start | bytes 6291460
Sparse Core Ops, SparseCore 0:
  9.6 48.6 all-gather.5
  83.1 36.1 all-gather.9
  121.7 36.7 all-gather.7
  184.7 43.8 reduce-scatter.2
  230.7 45.2 all-gather.11
  306.5 42.5 reduce-scatter.4
  352.0 37.5 all-reduce.3
  391.8 45.9 all-gather.13
  447.1 58.1 all-reduce.5
where the time goes:
time: 520 us; the launch traced here: 519 us
  waiting for transfers between devices  341 us (66%)
  matrix products  89 us (17%)
  other arithmetic  39.3 us (8%)
  local copies, waits for them, and re-layouts  19.1 us (4%)
  between operations  15.8 us (3%)
  blocking collectives  14.5 us (3%)
    all_gather x1, waiting for transfers between devices, local(): teacher_full = lax.all_gather(teacher_out, 'tensor', axis=1, tiled=True)  48.1 us
    all_gather x1, waiting for transfers between devices, local(): lax.all_gather(tokens, 'tensor', axis=1, tiled=True).astype(jnp.float32)  47.9 us
    all_gather x1, waiting for transfers between devices, local(): mixed = lax.all_gather(mixed_own, 'tensor', axis=1, tiled=True)  45.1 us
    reduce_scatter x1, waiting for transfers between devices, local(): lax.psum_scatter(partial_out.astype(jnp.bfloat16), 'tensor', scatter_dime...  44 us
    psum x1, waiting for transfers between devices, local(): lax.psum(grad_gate_part.astype(jnp.bfloat16), 'dp').astype(jnp.float32)  43.2 us
    psum x1, waiting for transfers between devices, local(): lax.psum(student_part.astype(jnp.bfloat16), 'tensor').astype(jnp.float32)  38.2 us
    reduce_scatter x1, waiting for transfers between devices, local(): lax.psum_scatter(mlp_part.astype(jnp.bfloat16), 'tensor', scatter_dimensi...  38.2 us
    all_gather x1, waiting for transfers between devices, local(): key_block = lax.all_gather(keys_flat, 'dp', axis=0, tiled=True)  28.3 us
  transfers between devices with their start and end apart: 9, of which 9 were waited for; matrix products, arithmetic and copies ran while one was open for 9% of the time, Pallas kernels for 0%

commit v1 on v0

v1 whole, which is shorter than its diff:
```python
import functools
import math

import jax
import jax.numpy as jnp
from jax import lax
from jax.experimental import pallas as pl
from jax.experimental.pallas import tpu as pltpu
from jax.sharding import PartitionSpec as P

HD = 128
COLS = 256
F32 = jnp.float32
BF16 = jnp.bfloat16
VMEM_LIMIT = 56 * 1024 * 1024


def rms_scale(values):
    return values * lax.rsqrt(jnp.mean(values * values, axis=-1, keepdims=True) + 1e-05)


def frequencies(head_dim):
    indices = jnp.arange(head_dim // 2).astype(F32)
    return jnp.exp(-jnp.log(500000.0) * 2.0 * indices / head_dim)


def dot(a, b):
    return jnp.dot(a, b, preferred_element_type=F32)


def ring_gather(block, axis):
    size = lax.axis_size(axis)
    perm = [(i, (i + 1) % size) for i in range(size)]
    blocks = [block]
    for _ in range(size - 1):
        blocks.append(lax.ppermute(blocks[-1], axis, perm))
    return blocks


def qkv_kernel(src_ref, *refs, ring, heads, split):
    blocks = refs[:ring]
    gain_ref, cos_ref, sin_ref, wq_ref, wk_ref, wv_ref, out_ref, tok_ref, normed = refs[ring:]
    step = pl.program_id(0)
    cols = wq_ref.shape[1]
    tiles = heads * HD // cols
    rows, width = blocks[0].shape
    depth = gain_ref.shape[1]

    @pl.when(step == 0)
    def _():
        total = jnp.zeros((rows, 1), F32)
        for block in blocks:
            part = block[...].astype(F32)
            total += jnp.sum(part * part, axis=1, keepdims=True)
        scale = lax.rsqrt(total / depth + 1e-05)
        for s, block in enumerate(blocks):
            at = pl.ds(pl.multiple_of(src_ref[s] * width, 128), width)
            part = block[...]
            tok_ref[:, at] = part
            normed[:, at] = (part.astype(F32) * scale * gain_ref[:, at]).astype(BF16)

    def emit(w_ref, rotate):
        result = dot(normed[...], w_ref[...])
        piece = rows // split
        for h in range(cols // HD):
            head = result[:, h * HD : (h + 1) * HD]
            if rotate:
                head = head * cos_ref[...] + pltpu.roll(head, HD // 2, 1) * sin_ref[...]
            head = head.astype(BF16)
            for p in range(split):
                out_ref[h * split + p, 0] = head[p * piece : (p + 1) * piece]

    @pl.when(step < tiles)
    def _():
        emit(wq_ref, True)

    @pl.when((step >= tiles) & (step < 2 * tiles))
    def _():
        emit(wk_ref, True)

    @pl.when(step >= 2 * tiles)
    def _():
        emit(wv_ref, False)


def qkv_call(src, blocks, gain, cosine, sine, w_query, w_key, w_value, split):
    rows, width = blocks[0].shape
    ring = len(blocks)
    depth, out_cols = w_query.shape
    heads = out_cols // HD
    cols = min(COLS, out_cols)
    tiles = out_cols // cols
    whole = lambda shape: pl.BlockSpec(shape, lambda j, src: (0,) * len(shape))
    weight = lambda k: pl.BlockSpec(
        (depth, cols), lambda j, src: (0, jnp.clip(j - k * tiles, 0, tiles - 1))
    )
    per_step = cols // HD * split
    return pl.pallas_call(
        functools.partial(qkv_kernel, ring=ring, heads=heads, split=split),
        out_shape=(
            jax.ShapeDtypeStruct((heads * split, 3, rows // split, HD), BF16),
            jax.ShapeDtypeStruct((rows, depth), BF16),
        ),
        grid_spec=pltpu.PrefetchScalarGridSpec(
            num_scalar_prefetch=1,
            grid=(3 * tiles,),
            in_specs=[whole((rows, width))] * ring
            + [whole((1, depth)), whole((rows, HD)), whole((rows, HD))]
            + [weight(0), weight(1), weight(2)],
            out_specs=(
                pl.BlockSpec(
                    (per_step, 1, rows // split, HD), lambda j, src: (j % tiles, j // tiles, 0, 0)
                ),
                whole((rows, depth)),
            ),
            scratch_shapes=[pltpu.VMEM((rows, depth), BF16)],
        ),
        compiler_params=pltpu.CompilerParams(vmem_limit_bytes=VMEM_LIMIT),
        cost_estimate=pl.CostEstimate(
            flops=6 * rows * depth * out_cols,
            bytes_accessed=6 * depth * out_cols,
            transcendentals=0,
        ),
        name="qkv",
    )(src, *blocks, gain, cosine, sine, w_query, w_key, w_value)


def attention_kernel(info_ref, qkv_ref, other_ref, start_ref, out_ref, *, factor):
    block = pl.program_id(0)
    count = info_ref.shape[0] - 1
    part = info_ref[count]
    half = out_ref.shape[1]
    span = 2 * half
    query = qkv_ref[block, 0]
    start = start_ref[0]
    row = block * span + part * half + lax.broadcasted_iota(jnp.int32, (half, 1), 0)
    lane = lax.broadcasted_iota(jnp.int32, (1, span), 1)
    place = jnp.where(lane < half, lane + part * half, lane - part * half)

    def body(at, carry):
        peak, denom, accum = carry
        keys = jnp.concatenate([qkv_ref[at, 1], other_ref[at, 0]], axis=0)
        values = jnp.concatenate([qkv_ref[at, 2], other_ref[at, 1]], axis=0)
        scores = (
            lax.dot_general(query, keys, (((1,), (1,)), ((), ())), preferred_element_type=F32)
            * factor
        )
        column = place + at * span
        allowed = (column >= start) & (column <= row)
        scores = jnp.where(allowed, scores, -1e30)
        new_peak = jnp.maximum(peak, jnp.max(scores, axis=1, keepdims=True))
        weights = jnp.where(allowed, jnp.exp2(scores - new_peak), 0.0)
        keep = jnp.exp2(peak - new_peak)
        denom = denom * keep + jnp.sum(weights, axis=1, keepdims=True)
        accum = accum * keep + dot(weights.astype(BF16), values)
        return new_peak, denom, accum

    first = (
        jnp.full((half, 1), -1e30, F32),
        jnp.zeros((half, 1), F32),
        jnp.zeros((half, HD), F32),
    )
    _, denom, accum = lax.fori_loop(info_ref[block], block + 1, body, first)
    out_ref[0] = (accum / denom).astype(BF16)


def attention_call(info, qkv, other, start):
    count, _, half, _ = qkv.shape
    whole = lambda a: pl.BlockSpec(a.shape, lambda b, info: (0,) * a.ndim)
    return pl.pallas_call(
        functools.partial(attention_kernel, factor=HD ** (-0.5) * math.log2(math.e)),
        out_shape=jax.ShapeDtypeStruct((count, half, HD), BF16),
        grid_spec=pltpu.PrefetchScalarGridSpec(
            num_scalar_prefetch=1,
            grid=(count,),
            in_specs=[
                whole(qkv),
                whole(other),
                pl.BlockSpec((1, half, 1), lambda b, info: (b, 0, 0)),
            ],
            out_specs=pl.BlockSpec((1, half, HD), lambda b, info: (b, 0, 0)),
        ),
        compiler_params=pltpu.CompilerParams(vmem_limit_bytes=VMEM_LIMIT),
        cost_estimate=pl.CostEstimate(
            flops=4 * count * half * count * half * HD,
            bytes_accessed=6 * count * half * HD * 2,
            transcendentals=count * half * count * half,
        ),
        name="attention",
    )(info, qkv, other, start)


def middle_kernel(where_ref, *refs, ring, split):
    parts = refs[:ring]
    (
        tok_ref,
        w_out_ref,
        gain_ref,
        gate_ref,
        up_ref,
        wp_ref,
        proj_ref,
        student_ref,
        hidden_ref,
        own_ref,
        diff_ref,
        attended,
        mixed,
        total,
    ) = refs[ring:]
    step = pl.program_id(0)
    rows, depth = mixed.shape
    tiles = depth // COLS
    width = own_ref.shape[1]

    @pl.when(step == 0)
    def _():
        piece = rows // split
        for s, part in enumerate(parts):
            heads = part.shape[0] // split
            for h in range(heads):
                for p in range(split):
                    at = (s * heads + h) * HD
                    attended[p * piece : (p + 1) * piece, at : at + HD] = part[h * split + p]

    @pl.when(step < tiles)
    def _():
        at = pl.ds(pl.multiple_of(step * COLS, COLS), COLS)
        weight = w_out_ref[0].reshape(depth, COLS)
        result = tok_ref[...].astype(F32) + dot(attended[...], weight)
        mixed[:, at] = result.astype(BF16)

    @pl.when(step == tiles)
    def _():
        values = mixed[...].astype(F32)
        attended[...] = (rms_scale(values) * gain_ref[...]).astype(BF16)
        own = mixed[:, pl.ds(pl.multiple_of(where_ref[0] * width, 128), width)]
        own_ref[...] = own
        total[...] = student_ref[...] - dot(own, proj_ref[...])

    @pl.when(step >= tiles)
    def _():
        gate = dot(attended[...], gate_ref[...])
        up = dot(attended[...], up_ref[...])
        hidden = (gate * jax.nn.sigmoid(gate) * up).astype(BF16)
        hidden_ref[...] = hidden
        total[...] -= dot(hidden, wp_ref[...])

    @pl.when(step == pl.num_programs(0) - 1)
    def _():
        diff_ref[...] = total[...].astype(BF16)


def middle_call(where, parts, tok, w_out, gain, w_gate, w_up, wp, projector, student, split):
    rows, depth = tok.shape
    ring = len(parts)
    units = w_gate.shape[1]
    out_tiles, unit_tiles = depth // COLS, units // COLS
    width = depth // ring
    sd = projector.shape[1]
    whole = lambda shape: pl.BlockSpec(shape, lambda j, w: (0,) * len(shape))
    early = lambda j: jnp.minimum(j, out_tiles - 1)
    late = lambda j: jnp.maximum(j - out_tiles, 0)
    return pl.pallas_call(
        functools.partial(middle_kernel, ring=ring, split=split),
        out_shape=(
            jax.ShapeDtypeStruct((rows, units), BF16),
            jax.ShapeDtypeStruct((rows, width), BF16),
            jax.ShapeDtypeStruct((rows, sd), BF16),
        ),
        grid_spec=pltpu.PrefetchScalarGridSpec(
            num_scalar_prefetch=1,
            grid=(out_tiles + unit_tiles,),
            in_specs=[whole(parts[0].shape)] * ring
            + [
                pl.BlockSpec((rows, COLS), lambda j, w: (0, early(j))),
                pl.BlockSpec((1,) + w_out.shape[1:], lambda j, w: (early(j), 0, 0, 0)),
                whole((1, depth)),
                pl.BlockSpec((depth, COLS), lambda j, w: (0, late(j))),
                pl.BlockSpec((depth, COLS), lambda j, w: (0, late(j))),
                pl.BlockSpec((COLS, sd), lambda j, w: (late(j), 0)),
                pl.BlockSpec((width, sd), lambda j, w: (w[0], 0)),
                whole((rows, sd)),
            ],
            out_specs=(
                pl.BlockSpec((rows, COLS), lambda j, w: (0, late(j))),
                whole((rows, width)),
                whole((rows, sd)),
            ),
            scratch_shapes=[
                pltpu.VMEM((rows, depth), BF16),
                pltpu.VMEM((rows, depth), BF16),
                pltpu.VMEM((rows, sd), F32),
            ],
        ),
        compiler_params=pltpu.CompilerParams(vmem_limit_bytes=VMEM_LIMIT),
        cost_estimate=pl.CostEstimate(
            flops=2 * rows * depth * (depth + 2 * units) + 2 * rows * sd * (units + width),
            bytes_accessed=2 * depth * (depth + 2 * units),
            transcendentals=rows * units,
        ),
        name="middle",
    )(where, *parts, tok, w_out, gain, w_gate, w_up, wp, projector, student)


def down_kernel(hidden_ref, weight_ref, out_ref):
    out_ref[0] = dot(hidden_ref[...], weight_ref[...]).astype(BF16)


def down_call(hidden, w_down, ring):
    rows, units = hidden.shape
    depth = w_down.shape[1]
    width = depth // ring
    cols = min(COLS, width)
    per = width // cols
    return pl.pallas_call(
        down_kernel,
        out_shape=jax.ShapeDtypeStruct((ring, rows, width), BF16),
        grid=(depth // cols,),
        in_specs=[
            pl.BlockSpec((rows, units), lambda j: (0, 0)),
            pl.BlockSpec((units, cols), lambda j: (0, j)),
        ],
        out_specs=pl.BlockSpec((1, rows, cols), lambda j: (j // per, 0, j % per)),
        compiler_params=pltpu.CompilerParams(vmem_limit_bytes=VMEM_LIMIT),
        cost_estimate=pl.CostEstimate(
            flops=2 * rows * units * depth, bytes_accessed=2 * units * depth, transcendentals=0
        ),
        name="down",
    )(hidden, w_down)


def grad_sum(flat):
    size = lax.axis_size("dp")
    rows, cols = flat.shape
    me = lax.axis_index("dp")
    core = me % 2
    swap = [(i, i ^ 1) for i in range(size)]
    halves = flat.reshape(2, rows // 2, cols)
    theirs = lax.ppermute(
        lax.dynamic_index_in_dim(halves, 1 - core, 0, False).astype(BF16), "dp", swap
    )
    mine = lax.dynamic_index_in_dim(halves, core, 0, False) + theirs.astype(F32)
    chips = size // 2
    groups = [[2 * c + k for c in range(chips)] for k in range(2)]
    shares = mine.astype(BF16).reshape(chips, rows // size, cols)
    got = lax.all_to_all(shares, "dp", 0, 0, axis_index_groups=groups)
    own = jnp.sum(got.astype(F32), axis=0).astype(BF16)
    chip = me // 2
    slots = jnp.zeros((chips, rows // size, cols), BF16)
    slots = lax.dynamic_update_index_in_dim(slots, own, chip, 0)
    for flip in range(1, chips):
        piece = lax.ppermute(own, "dp", [(i, i ^ (2 * flip)) for i in range(size)])
        slots = lax.dynamic_update_index_in_dim(slots, piece, chip ^ flip, 0)
    half = slots.reshape(rows // 2, cols)
    other = lax.ppermute(half, "dp", swap)
    low = jnp.where(core == 0, half, other)
    high = jnp.where(core == 0, other, half)
    return jnp.concatenate([low, high], axis=0).astype(F32)


def dense_attention(qkv, series_ids, first_row, split):
    share, _, piece, _ = qkv.shape
    heads = share // split
    mine = qkv.reshape(heads, split, 3, piece, HD).transpose(2, 0, 1, 3, 4)
    mine = mine.reshape(3, heads, split * piece, HD)
    rows = split * piece
    keys, values = lax.all_gather(mine[1:], "dp", axis=2, tiled=True)
    column = jnp.arange(keys.shape[1], dtype=jnp.int32)
    row = first_row + jnp.arange(rows, dtype=jnp.int32)
    own_series = lax.dynamic_slice_in_dim(series_ids, first_row, rows, 0)
    allowed = (column[None, :] <= row[:, None]) & (series_ids[None, :] == own_series[:, None])
    scores = jnp.einsum("hqd,hkd->hqk", mine[0], keys, preferred_element_type=F32) * HD ** (-0.5)
    scores = jnp.where(allowed[None], scores, -1e30)
    weights = jnp.where(allowed[None], jnp.exp(scores - jnp.max(scores, 2, keepdims=True)), 0.0)
    denom = jnp.sum(weights, axis=2, keepdims=True)
    mixed = jnp.einsum("hqk,hkd->hqd", weights.astype(BF16), values, preferred_element_type=F32)
    return (mixed / denom).astype(BF16).reshape(share, piece, HD)


def local(
    tokens,
    series_ids,
    offsets,
    norm_gain,
    mlp_gain,
    w_query,
    w_key,
    w_value,
    w_out,
    w_gate,
    w_up,
    w_down,
    projector,
    student_in,
    s_gate,
    s_up,
    s_down,
):
    rows = tokens.shape[0]
    heads = w_query.shape[1] // HD
    depth = w_query.shape[0]
    dp, ring = lax.axis_size("dp"), lax.axis_size("tensor")
    here, level = lax.axis_index("dp"), lax.axis_index("tensor")
    total_rows = rows * dp
    spread = dp == 2 * heads
    split = dp // heads if spread else 1

    token_blocks = ring_gather(tokens, "tensor")
    source = (level - jnp.arange(ring, dtype=jnp.int32)) % ring

    angles = offsets.astype(F32)[:, None] * frequencies(HD)[None, :]
    cosine, sine = jnp.cos(angles), jnp.sin(angles)
    cosine = jnp.concatenate([cosine, cosine], axis=1)
    sine = jnp.concatenate([-sine, sine], axis=1)
    student_full = student_in.astype(F32)
    student_normed = rms_scale(student_full).astype(BF16)
    s_gate_out = dot(student_normed, s_gate)
    s_up_out = dot(student_normed, s_up)
    sigmoid_gate = jax.nn.sigmoid(s_gate_out)
    s_hidden = (s_gate_out * sigmoid_gate * s_up_out).astype(BF16)
    student_part = dot(s_hidden, s_down)
    projected = dot(w_down, projector).astype(BF16)

    qkv, tok_full = qkv_call(
        source,
        token_blocks,
        norm_gain[None, :],
        cosine,
        sine,
        w_query,
        w_key,
        w_value,
        split,
    )

    slice_cols = depth // dp
    w_slice = lax.dynamic_slice_in_dim(w_out, here * slice_cols, slice_cols, 1)
    w_slice, _ = lax.optimization_barrier((w_slice, token_blocks[-1]))
    w_ring = jnp.stack(ring_gather(w_slice, "tensor"))
    w_all = lax.all_gather(w_ring, "dp", axis=0, tiled=False)
    if slice_cols != COLS:
        w_all = w_all.transpose(1, 2, 0, 3).reshape(ring, depth // ring, depth // COLS, COLS)
        w_all = w_all.transpose(2, 0, 1, 3)

    if spread:
        qkv = lax.all_to_all(qkv, "dp", 0, 0)
        other = lax.ppermute(qkv[:, 1:], "dp", [(i, i ^ 1) for i in range(dp)])
        below = jnp.sum(
            series_ids[None, :] < jnp.arange(8, dtype=jnp.int32)[:, None], axis=1, dtype=jnp.int32
        )
        mine = lax.dynamic_index_in_dim(
            series_ids.reshape(dp, 2, rows // 2), here % 2, 1, keepdims=False
        )
        start = jnp.sum(
            jnp.where(mine[:, :, None] == jnp.arange(8, dtype=jnp.int32), below, 0), axis=2
        )
        info = jnp.concatenate([start[:, 0] // rows, (here % 2)[None].astype(jnp.int32)])
        attended = attention_call(info, qkv, other, start[:, :, None])
        attended = lax.all_to_all(attended, "dp", 0, 0)
    else:
        attended = dense_attention(qkv, series_ids, here * rows, split)

    parts = ring_gather(attended, "tensor")
    hidden, mixed_own, diff_part = middle_call(
        level.astype(jnp.int32)[None],
        parts,
        tok_full,
        w_all,
        mlp_gain[None, :],
        w_gate,
        w_up,
        projected,
        projector,
        student_part,
        split,
    )

    sd = student_in.shape[1]
    piece = rows // ring
    pieces = lax.all_to_all(diff_part.reshape(ring, piece, sd), "tensor", 0, 0)
    own_student = lax.dynamic_slice_in_dim(student_in, level * piece, piece, 0).astype(F32)
    difference = own_student + jnp.sum(pieces.astype(F32), axis=0)
    scaled_own = (difference * total_rows ** (-0.5)).astype(BF16)
    scaled_slots = jnp.zeros((ring, piece, sd), BF16)
    for s, block in enumerate(ring_gather(scaled_own, "tensor")):
        scaled_slots = lax.dynamic_update_index_in_dim(scaled_slots, block, source[s], 0)
    scaled = scaled_slots.reshape(rows, sd)

    mlp_part = down_call(hidden, w_down, ring)
    mlp_own = lax.psum_scatter(mlp_part, "tensor", scatter_dimension=0, tiled=False).astype(F32)
    teacher_out = (mixed_own.astype(F32) + mlp_own).astype(BF16)

    grad_down = jnp.einsum("rk,rc->kc", s_hidden, scaled, preferred_element_type=F32)
    grad_hidden = jnp.einsum("rc,kc->rk", scaled, s_down, preferred_element_type=F32)
    grad_up_in = (grad_hidden * s_gate_out * sigmoid_gate).astype(BF16)
    grad_gate_in = (
        grad_hidden * s_up_out * sigmoid_gate * (1.0 + s_gate_out * (1.0 - sigmoid_gate))
    ).astype(BF16)
    grad_gate = jnp.einsum("rc,rk->ck", student_normed, grad_gate_in, preferred_element_type=F32)
    grad_up = jnp.einsum("rc,rk->ck", student_normed, grad_up_in, preferred_element_type=F32)

    wide = scaled.astype(F32)
    error = jnp.full((8, 128), jnp.sum(wide * wide), F32)
    bit = 1
    while bit < dp:
        error = error + lax.ppermute(error, "dp", [(i, i ^ bit) for i in range(dp)])
        bit *= 2
    error = error[0, 0] / sd

    units = s_gate.shape[1]
    flat = jnp.concatenate(
        [grad_gate.reshape(-1, sd), grad_up.reshape(-1, sd), grad_down.reshape(-1, sd)], axis=0
    )
    flat = grad_sum(flat)
    third = flat.shape[0] // 3
    return (
        teacher_out,
        flat[:third].reshape(sd, units),
        flat[third : 2 * third].reshape(sd, units),
        flat[2 * third :].reshape(units, sd),
        error,
    )


def solution(mesh):
    in_specs = (
        P("dp", "tensor"),
        P(),
        P("dp"),
        P(),
        P(),
        P(None, "tensor"),
        P(None, "tensor"),
        P(None, "tensor"),
        P("tensor", None),
        P(None, "tensor"),
        P(None, "tensor"),
        P("tensor", None),
        P(),
        P("dp", None),
        P(None, "tensor"),
        P(None, "tensor"),
        P("tensor", None),
    )
    out_specs = (P("dp", "tensor"), P(None, "tensor"), P(None, "tensor"), P("tensor", None), P())
    return jax.shard_map(local, mesh=mesh, in_specs=in_specs, out_specs=out_specs, check_vma=False)
```

time: 520 us -> 330 us (0.63)
  waiting for transfers between devices: 341 us -> 145 us
  matrix products: 89 us -> 14.8 us
  Pallas kernels: 0 us -> 67.2 us
  other arithmetic: 39.3 us -> 12.2 us
  blocking collectives: 14.5 us -> 37.6 us
  starting transfers between devices: 1.03 us -> 20.1 us
  local copies, waits for them, and re-layouts: 19.1 us -> 7.06 us
  between operations: 15.8 us -> 23.9 us
    all_gather x5 -> x1, waiting for transfers between devices: 176 us -> 0.01 us  [local(): w_all = lax.all_gather(w_ring, 'dp', axis=0, tiled=False)]
    ppermute x0 -> x21, waiting for transfers between devices: none -> 124 us  [the longest x12 112 us: ring_gather(): blocks.append(lax.ppermute(blocks[-1], axis, perm))]
    reduce_scatter x2 -> x1, waiting for transfers between devices: 82.2 us -> 0.01 us  [local(): lax.psum_scatter(mlp_part, 'tensor', scatter_dimension=0, tiled=False)]
    psum x2 -> x0, waiting for transfers between devices: 81.5 us -> none  [the longest x1 43.2 us: local(): lax.psum(grad_gate_part.astype(jnp.bfloat16), 'dp').astype(jnp.float32)]
    dot_general x14 -> x6, matrix products: 86 us -> 13.4 us  [the longest x4 12.5 us: dot(): return jnp.dot(a, b, preferred_element_type=F32)]
    pallas_call x0 -> x4, Pallas kernels: none -> 67.2 us  [the longest x1 26.7 us: middle_call(): pl.pallas_call(functools.partial(middle_kernel, ring=ring, split=split),...]
    all_to_all x0 -> x2, blocking collectives: none -> 37.6 us  [the longest x1 24.5 us: local(): qkv = lax.all_to_all(qkv, 'dp', 0, 0)]
    all_to_all x0 -> x2, waiting for transfers between devices: none -> 21 us  [the longest x1 12.2 us: grad_sum(): got = lax.all_to_all(shares, 'dp', 0, 0, axis_index_groups=groups)]
  transfers between devices with their start and end apart: 9 -> 25, of which waited for: 9 -> 20; matrix products, arithmetic and copies ran while one was open for 9% -> 8% of each run, Pallas kernels for 0% -> 12%
where the time goes in v1:
time: 330 us; the launch traced here: 328 us
  waiting for transfers between devices  145 us (44%)
  Pallas kernels  67.2 us (20%)
  blocking collectives  37.6 us (11%)
  between operations  23.9 us (7%)
  starting transfers between devices  20.1 us (6%)
  matrix products  14.8 us (4%)
  other arithmetic  12.2 us (4%)
  local copies, waits for them, and re-layouts  7.06 us (2%)
    ppermute x12, waiting for transfers between devices, ring_gather(): blocks.append(lax.ppermute(blocks[-1], axis, perm))  112 us
    pallas_call x1, Pallas kernels, middle_call(): pl.pallas_call(functools.partial(middle_kernel, ring=ring, split=split),...  26.7 us
    all_to_all x1, blocking collectives, local(): qkv = lax.all_to_all(qkv, 'dp', 0, 0)  24.5 us
    pallas_call x1, Pallas kernels, attention_call(): pl.pallas_call(functools.partial(attention_kernel, factor=HD ** (-0.5) *...  17.5 us
    all_to_all x1, blocking collectives, local(): attended = lax.all_to_all(attended, 'dp', 0, 0)  13.1 us
    pallas_call x1, Pallas kernels, qkv_call(): pl.pallas_call(functools.partial(qkv_kernel, ring=ring, heads=heads, spli...  12.5 us
    dot_general x4, matrix products, dot(): return jnp.dot(a, b, preferred_element_type=F32)  12.5 us
    all_to_all x1, waiting for transfers between devices, grad_sum(): got = lax.all_to_all(shares, 'dp', 0, 0, axis_index_groups=groups)  12.2 us
  transfers between devices with their start and end apart: 25, of which 20 were waited for; matrix products, arithmetic and copies ran while one was open for 8% of the time, Pallas kernels for 12%

profile of v1, /device:TPU:0, one launch (start us, length us, event | category | flops | bytes accessed | tf_op | source)
XLA Modules:
  0.0 328.2 jit_solution(2192578708448686786)
XLA Ops:
  7.2 3.1 collective-permute-start
  10.3 14.2 %collective-permute-done.refs_1_ = bf16[512,512]{1,0:T(8,128)(2,1)S(1)} collective-permute-done((bf16[512,512]{1,0:T(8,128)(2,1)}, bf16[512,512]{1,0:T(8,128)(2,1)S(1)}, u32[]{:S(2)}, u32[]{:S(2)}) %collective-permute-start) | collective-permute-done | bytes 524320 | tf_op jit(solution)/shard_map/ppermute | solution.py:36
  24.5 14.9 %collective-permute-done.1.refs_2_ = bf16[512,512]{1,0:T(8,128)(2,1)S(1)} collective-permute-done((bf16[512,512]{1,0:T(8,128)(2,1)S(1)}, bf16[512,512]{1,0:T(8,128)(2,1)S(1)}, u32[]{:S(2)}, u32[]{:S(2)}) %collective-permute-start.1) | collective-permute-done | bytes 524320 | tf_op jit(solution)/shard_map/ppermute | solution.py:36
  39.4 14.0 %collective-permute-done.2.refs_3_ = bf16[512,512]{1,0:T(8,128)(2,1)} collective-permute-done((bf16[512,512]{1,0:T(8,128)(2,1)S(1)}, bf16[512,512]{1,0:T(8,128)(2,1)}, u32[]{:S(2)}, u32[]{:S(2)}) %collective-permute-start.2) | collective-permute-done | bytes 524320 | tf_op jit(solution)/shard_map/ppermute | solution.py:36
  53.5 8.2 %collective-permute-done.7 = bf16[512,256]{1,0:T(8,128)(2,1)S(1)} collective-permute-done((bf16[512,256]{1,0:T(8,128)(2,1)S(1)}, bf16[512,256]{1,0:T(8,128)(2,1)S(1)}, u32[]{:S(2)}, u32[]{:S(2)}) %collective-permute-start.7) | collective-permute-done | bytes 262176 | tf_op jit(solution)/shard_map/ppermute | solution.py:36
  61.7 8.6 %collective-permute-done.8 = bf16[512,256]{1,0:T(8,128)(2,1)S(1)} collective-permute-done((bf16[512,256]{1,0:T(8,128)(2,1)S(1)}, bf16[512,256]{1,0:T(8,128)(2,1)S(1)}, u32[]{:S(2)}, u32[]{:S(2)}) %collective-permute-start.8) | collective-permute-done | bytes 262176 | tf_op jit(solution)/shard_map/ppermute | solution.py:36
  70.2 8.2 %collective-permute-done.9 = bf16[512,256]{1,0:T(8,128)(2,1)S(1)} collective-permute-done((bf16[512,256]{1,0:T(8,128)(2,1)S(1)}, bf16[512,256]{1,0:T(8,128)(2,1)S(1)}, u32[]{:S(2)}, u32[]{:S(2)}) %collective-permute-start.9) | collective-permute-done | bytes 262176 | tf_op jit(solution)/shard_map/ppermute | solution.py:36
  78.4 1.1 pad_maximum_fusion.1
  79.6 0.5 and_select_fusion.src_ref
  80.1 1.0 fusion.7
  81.1 1.0 pad_maximum_fusion.2
  82.1 12.5 %qkv.1 = (bf16[8,3,256,128]{3,2,1,0:T(8,128)(2,1)}, bf16[512,2048]{1,0:T(8,128)(2,1)}) custom-call(s32[4]{0:T(128)} %and_select_fusion.src_ref, bf16[512,512]{1,0:T(8,128)(2,1)} %refs_0_.1, bf16[512,512]{1,0:T(8,128)(2,1)} %copy-done.15, bf16[512,512]{1,0:T(8,128)(2,1)} %copy-done.16, bf16[512,512]{1,0:T(8,128)(2,1)} %collective-permute-done.2.refs_3_, ...), custom_call_target="tpu_custom_call" | custom-call | flops 3221225472 | bytes 6291456 | tf_op jit(solution)/shard_map/qkv/pallas_call | solution.py:98
  94.6 24.5 %all_to_all.20.qkv_ref = bf16[8,3,256,128]{3,2,1,0:T(8,128)(2,1)S(1)} all-to-all(bf16[8,3,256,128]{3,2,1,0:T(8,128)(2,1)} %get-tuple-element.11), channel_id=1, replica_groups=mesh['dp'=8,'tensor'=4] {'dp'}, dimensions={0} | all-to-all | bytes 3145728 | tf_op jit(solution)/shard_map/all_to_all | solution.py:447
  119.6 1.3 copy.25.start_ref
  121.1 0.6 pad_add_fusion.info_ref
  121.6 0.4 collective-permute-done.3.other_ref
  122.0 17.5 %attention.1 = bf16[8,256,128]{2,1,0:T(8,128)(2,1)} custom-call(s32[9]{0:T(128)} %pad_add_fusion.info_ref, bf16[8,3,256,128]{3,2,1,0:T(8,128)(2,1)} %copy-done.4, bf16[8,2,256,128]{3,2,1,0:T(8,128)(2,1)} %collective-permute-done.3.other_ref, s32[8,256,1]{2,1,0:T(8,128)} %copy.25.start_ref), custom_call_target="tpu_custom_call" | custom-call | flops 2147483648 | bytes 3145728 | tf_op jit(solution)/shard_map/attention/pallas_call | solution.py:170
  139.5 13.1 %all_to_all.21.refs_0_ = bf16[8,256,128]{2,1,0:T(8,128)(2,1)S(1)} all-to-all(bf16[8,256,128]{2,1,0:T(8,128)(2,1)} %attention.1), channel_id=1, replica_groups=mesh['dp'=8,'tensor'=4] {'dp'}, dimensions={0} | all-to-all | bytes 1048576 | tf_op jit(solution)/shard_map/all_to_all | solution.py:460
  152.7 1.0 collective-permute-start.4
  153.7 9.1 %convolution_convert_fusion.refs_9_ = bf16[2048,512]{1,0:T(8,128)(2,1)} fusion(bf16[2048,2048]{1,0:T(8,128)(2,1)} %weight_ref.1, bf16[2048,512]{1,0:T(8,128)(2,1)S(1)} %copy-done.13), kind=kOutput, calls=%fused_computation.1 | convolution fusion | flops 4296015872 | bytes 12582912 | tf_op jit(solution)/shard_map/dot_general | solution.py:28
  162.8 4.8 %collective-permute-done.4.refs_1_ = bf16[8,256,128]{2,1,0:T(8,128)(2,1)S(1)} collective-permute-done((bf16[8,256,128]{2,1,0:T(8,128)(2,1)S(1)}, bf16[8,256,128]{2,1,0:T(8,128)(2,1)S(1)}, u32[]{:S(2)}, u32[]{:S(2)}) %collective-permute-start.4) | collective-permute-done | bytes 524320 | tf_op jit(solution)/shard_map/ppermute | solution.py:36
  167.6 0.2 fusion.1
  167.8 0.5 fusion.15
  168.3 13.2 %collective-permute-done.5.refs_2_ = bf16[8,256,128]{2,1,0:T(8,128)(2,1)S(1)} collective-permute-done((bf16[8,256,128]{2,1,0:T(8,128)(2,1)S(1)}, bf16[8,256,128]{2,1,0:T(8,128)(2,1)S(1)}, u32[]{:S(2)}, u32[]{:S(2)}) %collective-permute-start.5) | collective-permute-done | bytes 524320 | tf_op jit(solution)/shard_map/ppermute | solution.py:36
  181.5 1.5 multiply_convert_fusion.2
  182.9 1.4 fusion.19.refs_11_
  184.3 10.2 %collective-permute-done.6.refs_3_ = bf16[8,256,128]{2,1,0:T(8,128)(2,1)} collective-permute-done((bf16[8,256,128]{2,1,0:T(8,128)(2,1)S(1)}, bf16[8,256,128]{2,1,0:T(8,128)(2,1)}, u32[]{:S(2)}, u32[]{:S(2)}) %collective-permute-start.6) | collective-permute-done | bytes 524320 | tf_op jit(solution)/shard_map/ppermute | solution.py:36
  194.5 26.7 %middle.1 = (bf16[512,2048]{1,0:T(8,128)(2,1)}, bf16[512,512]{1,0:T(8,128)(2,1)}, bf16[512,512]{1,0:T(8,128)(2,1)}) custom-call(s32[1]{0:T(128)} %bitcast.where_ref, bf16[8,256,128]{2,1,0:T(8,128)(2,1)} %copy-done.9, bf16[8,256,128]{2,1,0:T(8,128)(2,1)} %copy-done.17, bf16[8,256,128]{2,1,0:T(8,128)(2,1)} %copy-done.18, ...), custom_call_target="tpu_custom_call" | custom-call | flops 14227079168 | bytes 25165824 | tf_op jit(solution)/shard_map/middle/pallas_call | solution.py:264
  221.3 3.5 %all-to-all-start.2 = ((bf16[4,128,512]{2,1,0:T(8,128)(2,1)}), bf16[4,128,512]{2,1,0:T(8,128)(2,1)S(1)}, u32[]{:S(2)}, u32[]{:S(2)}) async-start(bf16[4,128,512]{2,1,0:T(8,128)(2,1)} %bitcast.67), calls=%async_computation.3 | async-start | bytes 1048576 | tf_op jit(solution)/shard_map/all_to_all | solution.py:481
  224.8 0.7 fusion.18
  227.3 8.7 %all-to-all-done.2 = bf16[4,128,512]{2,1,0:T(8,128)(2,1)S(1)} async-done(((bf16[4,128,512]{2,1,0:T(8,128)(2,1)}), bf16[4,128,512]{2,1,0:T(8,128)(2,1)S(1)}, u32[]{:S(2)}, u32[]{:S(2)}) %all-to-all-start.2) | async-done | bytes 524320 | tf_op jit(solution)/shard_map/all_to_all | solution.py:481
  242.1 1.0 collective-permute-done.10
  243.1 7.7 %collective-permute-done.11 = bf16[128,512]{1,0:T(8,128)(2,1)S(1)} collective-permute-done((bf16[128,512]{1,0:T(8,128)(2,1)S(1)}, bf16[128,512]{1,0:T(8,128)(2,1)S(1)}, u32[]{:S(2)}, u32[]{:S(2)}) %collective-permute-start.11) | collective-permute-done | bytes 131104 | tf_op jit(solution)/shard_map/ppermute | solution.py:36
  250.8 6.7 %collective-permute-done.12 = bf16[128,512]{1,0:T(8,128)(2,1)S(1)} collective-permute-done((bf16[128,512]{1,0:T(8,128)(2,1)S(1)}, bf16[128,512]{1,0:T(8,128)(2,1)S(1)}, u32[]{:S(2)}, u32[]{:S(2)}) %collective-permute-start.12) | collective-permute-done | bytes 131104 | tf_op jit(solution)/shard_map/ppermute | solution.py:36
  257.6 0.5 fusion.20
  258.0 0.5 fusion.21
  258.5 0.7 fusion.5
  259.2 0.5 copy-done.19
  259.7 0.8 fusion.6
  260.5 0.3 pad_maximum_fusion
  260.8 1.0 fusion.4
  261.8 10.5 %down.1 = bf16[4,512,512]{2,1,0:T(8,128)(2,1)} custom-call(bf16[512,2048]{1,0:T(8,128)(2,1)} %get-tuple-element.15.hidden_ref, bf16[2048,2048]{1,0:T(8,128)(2,1)} %weight_ref.1), custom_call_target="tpu_custom_call" | custom-call | flops 4294967296 | bytes 8388608 | tf_op jit(solution)/shard_map/down/pallas_call | solution.py:316
  272.4 2.3 fusion
  274.7 4.7 %all-to-all-start.3 = ((bf16[4,192,512]{2,1,0:T(8,128)(2,1)}), bf16[4,192,512]{2,1,0:T(8,128)(2,1)S(1)}, u32[]{:S(2)}, u32[]{:S(2)}) async-start(bf16[4,192,512]{2,1,0:T(8,128)(2,1)} %bitcast.64), calls=%async_computation.4 | async-start | bytes 1572864 | tf_op jit(solution)/shard_map/all_to_all | solution.py:347
  279.4 12.2 %all-to-all-done.3 = bf16[4,192,512]{2,1,0:T(8,128)(2,1)S(1)} async-done(((bf16[4,192,512]{2,1,0:T(8,128)(2,1)}), bf16[4,192,512]{2,1,0:T(8,128)(2,1)S(1)}, u32[]{:S(2)}, u32[]{:S(2)}) %all-to-all-start.3) | async-done | bytes 786464 | tf_op jit(solution)/shard_map/all_to_all | solution.py:347
  291.8 0.7 collective-permute-start.14
  292.5 1.3 collective-permute-start.15
  293.8 1.5 collective-permute-start.16
  295.4 4.2 %collective-permute-done.14 = bf16[192,512]{1,0:T(8,128)(2,1)S(1)} collective-permute-done((bf16[192,512]{1,0:T(8,128)(2,1)S(1)}, bf16[192,512]{1,0:T(8,128)(2,1)S(1)}, u32[]{:S(2)}, u32[]{:S(2)}) %collective-permute-start.14) | collective-permute-done | bytes 196640 | tf_op jit(solution)/shard_map/ppermute | solution.py:353
  299.6 3.3 %collective-permute-done.15 = bf16[192,512]{1,0:T(8,128)(2,1)S(1)} collective-permute-done((bf16[192,512]{1,0:T(8,128)(2,1)S(1)}, bf16[192,512]{1,0:T(8,128)(2,1)S(1)}, u32[]{:S(2)}, u32[]{:S(2)}) %collective-permute-start.15) | collective-permute-done | bytes 196640 | tf_op jit(solution)/shard_map/ppermute | solution.py:353
  303.1 0.9 multiply_reduce_fusion
  304.0 0.6 broadcast_in_dim.82
  304.6 0.6 collective-permute-start.18
  305.2 0.8 collective-permute-done.18
  306.0 0.6 broadcast_add_fusion
  306.7 1.7 collective-permute-start.19
  308.4 1.9 collective-permute-done.19
  310.3 0.6 fusion.32
  311.0 1.7 collective-permute-start.20
  312.7 2.0 collective-permute-done.20
  314.7 0.5 slice.39
  316.0 0.4 maximum_convert_fusion
  316.5 1.7 fusion.17
  318.3 2.0 fusion.3
  (87 shorter events, 1.7 us)
Async XLA Ops:
  7.2 32.2 %copy-start = (bf16[512,2048]{1,0:T(8,128)(2,1)S(1)}, bf16[512,2048]{1,0:T(8,128)(2,1)}, u32[]{:S(2)}) copy-start(bf16[512,2048]{1,0:T(8,128)(2,1)} %param.25) | copy-start | bytes 6291460
  7.2 72.3 %copy-start.12 = (s32[512]{0:T(512)S(1)}, s32[512]{0:T(512)}, u32[]{:S(2)}) copy-start(s32[512]{0:T(512)} %param.19) | copy-start | bytes 6148
  7.2 187.3 %all-gather.3.cloned.1.call-start = ((), (), s32[]{:S(2)}) async-start(), calls=%async_computation.6 | async-start | bytes 9437184 | tf_op jit(solution)/shard_map/all_gather | solution.py:441
  7.2 17.2 %collective-permute-start = (bf16[512,512]{1,0:T(8,128)(2,1)}, bf16[512,512]{1,0:T(8,128)(2,1)S(1)}, u32[]{:S(2)}, u32[]{:S(2)}) collective-permute-start(bf16[512,512]{1,0:T(8,128)(2,1)} %refs_0_.1), channel_id=1, source_target_pairs={{0,1},{1,2},{2,3},{3,0},{4,5},{5,6},{6,7},{7,4},{8,9},{9,10},{10,1... | collective-permute-start | bytes 1572872 | tf_op jit(solution)/shard_map/ppermute | solution.py:36
  24.5 57.6 %copy-start.15 = (bf16[512,512]{1,0:T(8,128)(2,1)}, bf16[512,512]{1,0:T(8,128)(2,1)S(1)}, u32[]{:S(2)}) copy-start(bf16[512,512]{1,0:T(8,128)(2,1)S(1)} %collective-permute-done.refs_1_) | copy-start | bytes 1572868
  24.5 14.9 %collective-permute-start.1 = (bf16[512,512]{1,0:T(8,128)(2,1)S(1)}, bf16[512,512]{1,0:T(8,128)(2,1)S(1)}, u32[]{:S(2)}, u32[]{:S(2)}) collective-permute-start(bf16[512,512]{1,0:T(8,128)(2,1)S(1)} %collective-permute-done.refs_1_), channel_id=1, source_target_pairs={{0,1},{1,2},{2,3},{3,0},{4,5},{5,6},{6,7},{7,4},{8,9},{9,10},{10,1... | collective-permute-start | bytes 1572872 | tf_op jit(solution)/shard_map/ppermute | solution.py:36
  39.4 42.7 %copy-start.16 = (bf16[512,512]{1,0:T(8,128)(2,1)}, bf16[512,512]{1,0:T(8,128)(2,1)S(1)}, u32[]{:S(2)}) copy-start(bf16[512,512]{1,0:T(8,128)(2,1)S(1)} %collective-permute-done.1.refs_2_) | copy-start | bytes 1572868
  39.4 14.1 %collective-permute-start.2 = (bf16[512,512]{1,0:T(8,128)(2,1)S(1)}, bf16[512,512]{1,0:T(8,128)(2,1)}, u32[]{:S(2)}, u32[]{:S(2)}) collective-permute-start(bf16[512,512]{1,0:T(8,128)(2,1)S(1)} %collective-permute-done.1.refs_2_), channel_id=1, source_target_pairs={{0,1},{1,2},{2,3},{3,0},{4,5},{5,6},{6,7},{7,4},{8,9},{9,10},{10,1... | collective-permute-start | bytes 1572872 | tf_op jit(solution)/shard_map/ppermute | solution.py:36
  53.5 8.2 %collective-permute-start.7 = (bf16[512,256]{1,0:T(8,128)(2,1)S(1)}, bf16[512,256]{1,0:T(8,128)(2,1)S(1)}, u32[]{:S(2)}, u32[]{:S(2)}) collective-permute-start(bf16[512,256]{1,0:T(8,128)(2,1)S(1)} %constant_dynamic-slice_fusion), channel_id=1, source_target_pairs={{0,1},{1,2},{2,3},{3,0},{4,5},{5,6},{6,7},{7,4},{8,9},{9,10},{10,1... | collective-permute-start | bytes 786440 | tf_op jit(solution)/shard_map/ppermute | solution.py:36
  61.7 8.6 %collective-permute-start.8 = (bf16[512,256]{1,0:T(8,128)(2,1)S(1)}, bf16[512,256]{1,0:T(8,128)(2,1)S(1)}, u32[]{:S(2)}, u32[]{:S(2)}) collective-permute-start(bf16[512,256]{1,0:T(8,128)(2,1)S(1)} %collective-permute-done.7), channel_id=1, source_target_pairs={{0,1},{1,2},{2,3},{3,0},{4,5},{5,6},{6,7},{7,4},{8,9},{9,10},{10,1... | collective-permute-start | bytes 786440 | tf_op jit(solution)/shard_map/ppermute | solution.py:36
  70.2 8.2 %collective-permute-start.9 = (bf16[512,256]{1,0:T(8,128)(2,1)S(1)}, bf16[512,256]{1,0:T(8,128)(2,1)S(1)}, u32[]{:S(2)}, u32[]{:S(2)}) collective-permute-start(bf16[512,256]{1,0:T(8,128)(2,1)S(1)} %collective-permute-done.8), channel_id=1, source_target_pairs={{0,1},{1,2},{2,3},{3,0},{4,5},{5,6},{6,7},{7,4},{8,9},{9,10},{10,1... | collective-permute-start | bytes 786440 | tf_op jit(solution)/shard_map/ppermute | solution.py:36
  94.6 24.7 %copy-start.10 = (s32[4096]{0:T(1024)S(1)}, s32[4096]{0:T(1024)}, u32[]{:S(2)}) copy-start(s32[4096]{0:T(1024)} %param.18) | copy-start | bytes 49156
  119.1 3.0 copy-start.4
  119.2 2.9 collective-permute-start.3
  121.6 32.0 %copy-start.13 = (bf16[2048,512]{1,0:T(8,128)(2,1)S(1)}, bf16[2048,512]{1,0:T(8,128)(2,1)}, u32[]{:S(2)}) copy-start(bf16[2048,512]{1,0:T(8,128)(2,1)} %refs_10_.1) | copy-start | bytes 6291460
  152.7 10.1 %copy-start.9 = (bf16[8,256,128]{2,1,0:T(8,128)(2,1)}, bf16[8,256,128]{2,1,0:T(8,128)(2,1)S(1)}, u32[]{:S(2)}) copy-start(bf16[8,256,128]{2,1,0:T(8,128)(2,1)S(1)} %all_to_all.21.refs_0_) | copy-start | bytes 1572868
  152.7 14.9 %copy-start.5 = (bf16[512,512]{1,0:T(8,128)(2,1)S(1)}, bf16[512,512]{1,0:T(8,128)(2,1)}, u32[]{:S(2)}) copy-start(bf16[512,512]{1,0:T(8,128)(2,1)} %param.30) | copy-start | bytes 1572868
  152.7 15.1 %copy-start.7 = (bf16[512,512]{1,0:T(8,128)(2,1)S(1)}, bf16[512,512]{1,0:T(8,128)(2,1)}, u32[]{:S(2)}) copy-start(bf16[512,512]{1,0:T(8,128)(2,1)} %param.31) | copy-start | bytes 1572868
  152.7 28.8 %copy-start.14 = (bf16[512,512]{1,0:T(8,128)(2,1)S(1)}, bf16[512,512]{1,0:T(8,128)(2,1)}, u32[]{:S(2)}) copy-start(bf16[512,512]{1,0:T(8,128)(2,1)} %param.32) | copy-start | bytes 1572868
  152.7 14.9 %collective-permute-start.4 = (bf16[8,256,128]{2,1,0:T(8,128)(2,1)S(1)}, bf16[8,256,128]{2,1,0:T(8,128)(2,1)S(1)}, u32[]{:S(2)}, u32[]{:S(2)}) collective-permute-start(bf16[8,256,128]{2,1,0:T(8,128)(2,1)S(1)} %all_to_all.21.refs_0_), channel_id=1, source_target_pairs={{0,1},{1,2},{2,3},{3,0},{4,5},{5,6},{6,7},{7,4},{8,9},{9,10},{10,1... | collective-permute-start | bytes 1572872 | tf_op jit(solution)/shard_map/ppermute | solution.py:36
  167.6 15.4 %copy-start.17 = (bf16[8,256,128]{2,1,0:T(8,128)(2,1)}, bf16[8,256,128]{2,1,0:T(8,128)(2,1)S(1)}, u32[]{:S(2)}) copy-start(bf16[8,256,128]{2,1,0:T(8,128)(2,1)S(1)} %collective-permute-done.4.refs_1_) | copy-start | bytes 1572868
  167.6 13.9 %collective-permute-start.5 = (bf16[8,256,128]{2,1,0:T(8,128)(2,1)S(1)}, bf16[8,256,128]{2,1,0:T(8,128)(2,1)S(1)}, u32[]{:S(2)}, u32[]{:S(2)}) collective-permute-start(bf16[8,256,128]{2,1,0:T(8,128)(2,1)S(1)} %collective-permute-done.4.refs_1_), channel_id=1, source_target_pairs={{0,1},{1,2},{2,3},{3,0},{4,5},{5,6},{6,7},{7,4},{8,9},{9,10},{10,1... | collective-permute-start | bytes 1572872 | tf_op jit(solution)/shard_map/ppermute | solution.py:36
  168.2 14.7 %copy-start.6 = (bf16[512,512]{1,0:T(8,128)(2,1)S(1)}, bf16[512,512]{1,0:T(8,128)(2,1)}, u32[]{:S(2)}) copy-start(bf16[512,512]{1,0:T(8,128)(2,1)} %param.33) | copy-start | bytes 1572868
  181.4 1.5 copy-start.18
  181.4 13.1 %collective-permute-start.6 = (bf16[8,256,128]{2,1,0:T(8,128)(2,1)S(1)}, bf16[8,256,128]{2,1,0:T(8,128)(2,1)}, u32[]{:S(2)}, u32[]{:S(2)}) collective-permute-start(bf16[8,256,128]{2,1,0:T(8,128)(2,1)S(1)} %collective-permute-done.5.refs_2_), channel_id=1, source_target_pairs={{0,1},{1,2},{2,3},{3,0},{4,5},{5,6},{6,7},{7,4},{8,9},{9,10},{10,1... | collective-permute-start | bytes 1572872 | tf_op jit(solution)/shard_map/ppermute | solution.py:36
  194.5 30.3 %copy-start.11 = (s32[4]{0:T(128)S(1)}, s32[4]{0:T(128)}, u32[]{:S(2)}) copy-start(s32[4]{0:T(128)} %and_select_fusion.src_ref) | copy-start | bytes 52
  221.3 14.8 %all-to-all-start.2 = ((bf16[4,128,512]{2,1,0:T(8,128)(2,1)}), bf16[4,128,512]{2,1,0:T(8,128)(2,1)S(1)}, u32[]{:S(2)}, u32[]{:S(2)}) async-start(bf16[4,128,512]{2,1,0:T(8,128)(2,1)} %bitcast.67), calls=%async_computation.3 | async-start | bytes 1048576 | tf_op jit(solution)/shard_map/all_to_all | solution.py:481
  224.7 93.5 %reduce-scatter.2.cloned.1.call-start = ((), (), s32[]{:S(2)}) async-start(), calls=%async_computation.5 | async-start | bytes 2621440 | tf_op jit(solution)/shard_map/reduce_scatter | solution.py:491
  236.2 6.8 %collective-permute-start.10 = (bf16[128,512]{1,0:T(8,128)(2,1)S(1)}, bf16[128,512]{1,0:T(8,128)(2,1)S(1)}, u32[]{:S(2)}, u32[]{:S(2)}) collective-permute-start(bf16[128,512]{1,0:T(8,128)(2,1)S(1)} %get-tuple-element.18), channel_id=1, source_target_pairs={{0,1},{1,2},{2,3},{3,0},{4,5},{5,6},{6,7},{7,4},{8,9},{9,10},{10,1... | collective-permute-start | bytes 393224 | tf_op jit(solution)/shard_map/ppermute | solution.py:36
  243.0 7.7 %collective-permute-start.11 = (bf16[128,512]{1,0:T(8,128)(2,1)S(1)}, bf16[128,512]{1,0:T(8,128)(2,1)S(1)}, u32[]{:S(2)}, u32[]{:S(2)}) collective-permute-start(bf16[128,512]{1,0:T(8,128)(2,1)S(1)} %collective-permute-done.10), channel_id=1, source_target_pairs={{0,1},{1,2},{2,3},{3,0},{4,5},{5,6},{6,7},{7,4},{8,9},{9,10},{10,1... | collective-permute-start | bytes 393224 | tf_op jit(solution)/shard_map/ppermute | solution.py:36
  250.8 6.8 %collective-permute-start.12 = (bf16[128,512]{1,0:T(8,128)(2,1)S(1)}, bf16[128,512]{1,0:T(8,128)(2,1)S(1)}, u32[]{:S(2)}, u32[]{:S(2)}) collective-permute-start(bf16[128,512]{1,0:T(8,128)(2,1)S(1)} %collective-permute-done.11), channel_id=1, source_target_pairs={{0,1},{1,2},{2,3},{3,0},{4,5},{5,6},{6,7},{7,4},{8,9},{9,10},{10,1... | collective-permute-start | bytes 393224 | tf_op jit(solution)/shard_map/ppermute | solution.py:36
  257.6 1.6 copy-start.2
  258.5 1.2 copy-start.19
  261.8 10.6 %collective-permute-start.13 = (bf16[768,512]{1,0:T(8,128)(2,1)}, bf16[768,512]{1,0:T(8,128)(2,1)}, u32[]{:S(2)}, u32[]{:S(2)}) collective-permute-start(bf16[768,512]{1,0:T(8,128)(2,1)} %fusion.4), channel_id=1, source_target_pairs={{0,4},{4,0},{8,12},{12,8},{16,20},{20,16},{24,28},{28,24},{1,5},{5... | collective-permute-start | bytes 2359304 | tf_op jit(solution)/shard_map/ppermute | solution.py:340
  274.6 28.5 %copy-start.3 = (bf16[4,128,512]{2,1,0:T(8,128)(2,1)S(1)}, bf16[4,128,512]{2,1,0:T(8,128)(2,1)}, u32[]{:S(2)}) copy-start(bf16[4,128,512]{2,1,0:T(8,128)(2,1)} %copy-done.2) | copy-start | bytes 1572868
  274.7 17.0 %all-to-all-start.3 = ((bf16[4,192,512]{2,1,0:T(8,128)(2,1)}), bf16[4,192,512]{2,1,0:T(8,128)(2,1)S(1)}, u32[]{:S(2)}, u32[]{:S(2)}) async-start(bf16[4,192,512]{2,1,0:T(8,128)(2,1)} %bitcast.64), calls=%async_computation.4 | async-start | bytes 1572864 | tf_op jit(solution)/shard_map/all_to_all | solution.py:347
  291.8 7.8 %collective-permute-start.14 = (bf16[192,512]{1,0:T(8,128)(2,1)S(1)}, bf16[192,512]{1,0:T(8,128)(2,1)S(1)}, u32[]{:S(2)}, u32[]{:S(2)}) collective-permute-start(bf16[192,512]{1,0:T(8,128)(2,1)S(1)} %reduce_sum.61), channel_id=1, source_target_pairs={{0,8},{4,12},{8,0},{12,4},{16,24},{20,28},{24,16},{28,20},{1,9},{5... | collective-permute-start | bytes 589832 | tf_op jit(solution)/shard_map/ppermute | solution.py:353
  292.5 10.4 %collective-permute-start.15 = (bf16[192,512]{1,0:T(8,128)(2,1)S(1)}, bf16[192,512]{1,0:T(8,128)(2,1)S(1)}, u32[]{:S(2)}, u32[]{:S(2)}) collective-permute-start(bf16[192,512]{1,0:T(8,128)(2,1)S(1)} %reduce_sum.61), channel_id=1, source_target_pairs={{0,16},{4,20},{8,24},{12,28},{16,0},{20,4},{24,8},{28,12},{1,17},{... | collective-permute-start | bytes 589832 | tf_op jit(solution)/shard_map/ppermute | solution.py:353
  293.8 9.2 %collective-permute-start.16 = (bf16[192,512]{1,0:T(8,128)(2,1)S(1)}, bf16[192,512]{1,0:T(8,128)(2,1)S(1)}, u32[]{:S(2)}, u32[]{:S(2)}) collective-permute-start(bf16[192,512]{1,0:T(8,128)(2,1)S(1)} %reduce_sum.61), channel_id=1, source_target_pairs={{0,24},{4,28},{8,16},{12,20},{16,8},{20,12},{24,0},{28,4},{1,25},{... | collective-permute-start | bytes 589832 | tf_op jit(solution)/shard_map/ppermute | solution.py:353
  303.0 12.8 %collective-permute-start.17 = (bf16[768,512]{1,0:T(8,128)(2,1)S(1)}, bf16[768,512]{1,0:T(8,128)(2,1)S(1)}, u32[]{:S(2)}, u32[]{:S(2)}) collective-permute-start(bf16[768,512]{1,0:T(8,128)(2,1)S(1)} %bitcast.65), channel_id=1, source_target_pairs={{0,4},{4,0},{8,12},{12,8},{16,20},{20,16},{24,28},{28,24},{1,5},{5... | collective-permute-start | bytes 2359304 | tf_op jit(solution)/shard_map/ppermute | solution.py:356
  304.6 1.4 collective-permute-start.18
  306.7 3.7 %collective-permute-start.19 = (f32[8,128]{1,0:T(8,128)S(1)}, f32[8,128]{1,0:T(8,128)S(1)}, u32[]{:S(2)}, u32[]{:S(2)}) collective-permute-start(f32[8,128]{1,0:T(8,128)S(1)} %broadcast_add_fusion), channel_id=1, source_target_pairs={{0,8},{4,12},{8,0},{12,4},{16,24},{20,28},{24,16},{28,20},{1,9},{5... | collective-permute-start | bytes 12296 | tf_op jit(solution)/shard_map/ppermute | solution.py:507
  311.0 3.7 %collective-permute-start.20 = (f32[8,128]{1,0:T(8,128)S(1)}, f32[8,128]{1,0:T(8,128)S(1)}, u32[]{:S(2)}, u32[]{:S(2)}) collective-permute-start(f32[8,128]{1,0:T(8,128)S(1)} %fusion.32), channel_id=1, source_target_pairs={{0,16},{4,20},{8,24},{12,28},{16,0},{20,4},{24,8},{28,12},{1,17},{... | collective-permute-start | bytes 12296 | tf_op jit(solution)/shard_map/ppermute | solution.py:507
  316.0 4.2 %copy-start.1 = (bf16[512,2048]{1,0:T(8,128)(2,1)S(1)}, bf16[512,2048]{1,0:T(8,128)(2,1)}, u32[]{:S(2)}) copy-start(bf16[512,2048]{1,0:T(8,128)(2,1)} %param.25) | copy-start | bytes 6291460
  316.5 1.8 copy-start.8
Sparse Core Ops, SparseCore 0:
  79.6 63.8 all-gather.2
  272.5 43.1 reduce-scatter.1

commit v2 on v0

--- a/solution.py
+++ b/solution.py
@@ -1,9 +1,20 @@
+import functools
+import math
+
 import jax
 import jax.numpy as jnp
 from jax import lax
+from jax.experimental import pallas as pl
+from jax.experimental.pallas import tpu as pltpu
 from jax.sharding import PartitionSpec as P
 
 HD = 128
+COLS = 256
+NOTE = 16
+SERIES = 8
+F32 = jnp.float32
+BF16 = jnp.bfloat16
+MIB = 1024 * 1024
 
 
 def rms_scale(values):
@@ -27,7 +38,7 @@
     )
 
 
-def local(
+def general(
     tokens,
     series_ids,
     offsets,
@@ -151,6 +162,695 @@
     return (teacher_out, grad_gate, grad_up, grad_down, error)
 
 
+def dot(a, b):
+    return jnp.dot(a, b, preferred_element_type=F32)
+
+
+def dot_over(a, b, dims):
+    return lax.dot_general(a, b, ((dims[:1], dims[1:]), ((), ())), preferred_element_type=F32)
+
+
+def params(limit):
+    return pltpu.CompilerParams(vmem_limit_bytes=limit * MIB)
+
+
+def whole(shape):
+    return pl.BlockSpec(shape, lambda *_: (0,) * len(shape))
+
+
+def cost(flops, moved, transcendentals=0):
+    return pl.CostEstimate(
+        flops=int(flops), bytes_accessed=int(moved), transcendentals=int(transcendentals)
+    )
+
+
+def rotate(head, cos_ref, sin_ref):
+    return head * cos_ref[...] + pltpu.roll(head, HD // 2, 1) * sin_ref[...]
+
+
+def kv_kernel(info_ref, *refs, ring, heads):
+    blocks = [refs[:ring], refs[ring : 2 * ring]]
+    gain_ref, cos_ref, sin_ref, wk_ref, wv_ref = refs[2 * ring : 2 * ring + 5]
+    outs = refs[2 * ring + 5 : 2 * ring + 5 + heads]
+    tok_ref, normed, made = refs[2 * ring + 5 + heads :]
+    step = pl.program_id(0)
+    half, width = blocks[0][0].shape
+    depth = gain_ref.shape[1]
+
+    @pl.when(step == 0)
+    def _():
+        for k in range(2):
+            mine = slice(k * half, (k + 1) * half)
+            total = jnp.zeros((half, 1), F32)
+            for block in blocks[k]:
+                part = block[...].astype(F32)
+                total += jnp.sum(part * part, axis=1, keepdims=True)
+            scale = lax.rsqrt(total / depth + 1e-05)
+            for s, block in enumerate(blocks[k]):
+                at = pl.ds(pl.multiple_of(info_ref[s] * width, 128), width)
+                part = block[...]
+                tok_ref[mine, at] = part
+                normed[mine, at] = (part.astype(F32) * scale * gain_ref[:, at]).astype(BF16)
+        result = dot(normed[...], wk_ref[...])
+        for h in range(heads):
+            head = rotate(result[:, h * HD : (h + 1) * HD], cos_ref, sin_ref)
+            made[h, 0] = head.astype(BF16)
+
+    @pl.when(step == 1)
+    def _():
+        result = dot(normed[...], wv_ref[...])
+        for h in range(heads):
+            made[h, 1] = result[:, h * HD : (h + 1) * HD].astype(BF16)
+        for f in range(heads):
+            outs[f][...] = made[info_ref[ring] ^ f]
+
+
+def kv_call(info, blocks, gain, cosine, sine, w_key, w_value):
+    half, width = blocks[0][0].shape
+    rows, ring = 2 * half, len(blocks[0])
+    depth, out_cols = w_key.shape
+    heads = out_cols // HD
+    result = pl.pallas_call(
+        functools.partial(kv_kernel, ring=ring, heads=heads),
+        out_shape=[jax.ShapeDtypeStruct((2, rows, HD), BF16)] * heads
+        + [jax.ShapeDtypeStruct((rows, depth), BF16)] * 2,
+        grid_spec=pltpu.PrefetchScalarGridSpec(
+            num_scalar_prefetch=1,
+            grid=(2,),
+            in_specs=[whole((half, width))] * (2 * ring)
+            + [whole((1, depth)), whole((rows, HD)), whole((rows, HD))]
+            + [whole((depth, out_cols))] * 2,
+            out_specs=[whole((2, rows, HD))] * heads + [whole((rows, depth))] * 2,
+            scratch_shapes=[pltpu.VMEM((heads, 2, rows, HD), BF16)],
+        ),
+        compiler_params=params(36),
+        cost_estimate=cost(4 * rows * depth * out_cols, 4 * depth * out_cols),
+        name="keys_values",
+    )(info, *blocks[0], *blocks[1], gain, cosine, sine, w_key, w_value)
+    return result[:heads], result[heads], result[heads + 1]
+
+
+def query_kernel(info_ref, normed_ref, cos_ref, sin_ref, wq_ref, *refs, heads):
+    outs, made = refs[:heads], refs[heads]
+    result = dot(normed_ref[...], wq_ref[...])
+    for h in range(heads):
+        head = rotate(result[:, h * HD : (h + 1) * HD], cos_ref, sin_ref)
+        made[h] = head.astype(BF16)
+    for f in range(heads):
+        outs[f][...] = made[info_ref[info_ref.shape[0] - 1] ^ f]
+
+
+def query_call(info, normed, cosine, sine, w_query):
+    rows, depth = normed.shape
+    out_cols = w_query.shape[1]
+    heads = out_cols // HD
+    return pl.pallas_call(
+        functools.partial(query_kernel, heads=heads),
+        out_shape=[jax.ShapeDtypeStruct((rows, HD), BF16)] * heads,
+        grid_spec=pltpu.PrefetchScalarGridSpec(
+            num_scalar_prefetch=1,
+            grid=(1,),
+            in_specs=[
+                whole((rows, depth)),
+                whole((rows, HD)),
+                whole((rows, HD)),
+                whole((depth, out_cols)),
+            ],
+            out_specs=[whole((rows, HD))] * heads,
+            scratch_shapes=[pltpu.VMEM((heads, rows, HD), BF16)],
+        ),
+        compiler_params=params(24),
+        cost_estimate=cost(2 * rows * depth * out_cols, 2 * depth * out_cols),
+        name="queries",
+    )(info, normed, cosine, sine, w_query)
+
+
+def attention_kernel(info_ref, *refs, chips):
+    queries, own, other = refs[:chips], refs[chips : 2 * chips], refs[2 * chips : 3 * chips]
+    outs = refs[3 * chips : 4 * chips]
+    keys_all, values_all = refs[4 * chips :]
+    chip, core = info_ref[SERIES], info_ref[SERIES + 1]
+    half = outs[0].shape[1]
+    span = 2 * half
+    for f in range(chips):
+        for source, side in ((own[f], core), (other[f], 1 - core)):
+            at = pl.ds(pl.multiple_of(side * half, half), half)
+            for odd, index in ((0, side), (1, 1 - side)):
+                block = 2 * (chip ^ f) + odd
+                keys_all[block, at, :] = source[0, index]
+                values_all[block, :, at] = source[1, index].T
+
+    def first_of(row):
+        found = jnp.int32(0)
+        for s in range(SERIES):
+            edge = info_ref[s]
+            found = jnp.where(edge <= row, jnp.maximum(found, edge), found)
+        return found
+
+    for f in range(chips):
+        even = 2 * (chip ^ f)
+        first_row = even * span + core * half
+        last_row = first_row + span + half - 1
+        query = jnp.concatenate([queries[f][core], queries[f][1 - core]], axis=0)
+        place = lax.broadcasted_iota(jnp.int32, (1, span), 1)
+        row = first_row + place + jnp.where(place < half, 0, half)
+        start = jnp.zeros((1, span), jnp.int32)
+        for s in range(SERIES):
+            edge = info_ref[s]
+            start = jnp.where(edge <= row, jnp.maximum(start, edge), start)
+        lane = lax.broadcasted_iota(jnp.int32, (span, 1), 0)
+
+        def body(at, carry, masked, query=query, row=row, start=start, lane=lane):
+            peak, denom, accum = carry
+            scores = dot_over(keys_all[at], query, (1, 1))
+            if masked:
+                column = lane + at * span
+                allowed = (column >= start) & (column <= row)
+                scores = jnp.where(allowed, scores, -1e30)
+            new_peak = jnp.maximum(peak, jnp.max(scores, axis=0, keepdims=True))
+            weights = jnp.exp2(scores - new_peak)
+            if masked:
+                weights = jnp.where(allowed, weights, 0.0)
+            keep = jnp.exp2(peak - new_peak)
+            denom = denom * keep + jnp.sum(weights, axis=0, keepdims=True)
+            accum = accum * keep + dot(values_all[at], weights.astype(BF16))
+            return new_peak, denom, accum
+
+        begin = first_of(first_row) // span
+        full = jnp.minimum(even, (first_of(last_row) + span - 1) // span)
+        carry = (
+            jnp.full((1, span), -1e30, F32),
+            jnp.zeros((1, span), F32),
+            jnp.zeros((HD, span), F32),
+        )
+        carry = lax.fori_loop(begin, full, functools.partial(body, masked=True), carry)
+        carry = lax.fori_loop(full, even, functools.partial(body, masked=False), carry)
+        peak, denom, accum = body(even, carry, masked=True)
+        outs[f][core] = (accum[:, :half] / denom[:, :half]).T.astype(BF16)
+        carry = (peak[:, half:], denom[:, half:], accum[:, half:])
+        _, denom, accum = body(
+            even + 1, carry, True, query[half:], row[:, half:], start[:, half:], lane
+        )
+        outs[f][1 - core] = (accum / denom).T.astype(BF16)
+
+
+def attention_call(info, queries, own, other):
+    chips = len(queries)
+    _, half, _ = queries[0].shape
+    return pl.pallas_call(
+        functools.partial(attention_kernel, chips=chips),
+        out_shape=[jax.ShapeDtypeStruct((2, half, HD), BF16)] * chips,
+        grid_spec=pltpu.PrefetchScalarGridSpec(
+            num_scalar_prefetch=1,
+            grid=(1,),
+            in_specs=[whole((2, half, HD))] * chips + [whole((2, 2, half, HD))] * (2 * chips),
+            out_specs=[whole((2, half, HD))] * chips,
+            scratch_shapes=[
+                pltpu.VMEM((2 * chips, 2 * half, HD), BF16),
+                pltpu.VMEM((2 * chips, HD, 2 * half), BF16),
+            ],
+        ),
+        compiler_params=params(30),
+        cost_estimate=cost(
+            4 * chips * half * 4 * chips * half * HD,
+            12 * chips * half * HD * 2,
+            2 * chips * half * 4 * chips * half // 2,
+        ),
+        name="attention",
+    )(info, *queries, *own, *other)
+
+
+def middle_kernel(info_ref, *refs, ring, chips):
+    parts = [refs[:ring], refs[ring : 2 * ring]]
+    refs = refs[2 * ring :]
+    tok_ref, w_own_ref = refs[:2]
+    near_refs, far_refs = refs[2:4], refs[4:6]
+    gain_ref, gate_ref, up_ref, wp_ref, proj_ref, student_ref = refs[6:12]
+    hidden_ref, own_ref = refs[12:14]
+    pieces = refs[14 : 14 + ring]
+    attended, mixed, total = refs[14 + ring :]
+    step = pl.program_id(0)
+    level, chip, core = info_ref[0], info_ref[1], info_ref[2]
+    rows, depth = mixed.shape
+    half = rows // 2
+    width = own_ref.shape[1]
+
+    @pl.when(step == 0)
+    def _():
+        for k in range(2):
+            for s, part in enumerate(parts[k]):
+                for i in range(part.shape[0]):
+                    at = s * width + (chip ^ (k * part.shape[0] + i)) * HD
+                    at = pl.ds(pl.multiple_of(at, HD), HD)
+                    attended[:half, at] = part[i, 0]
+                    attended[half:, at] = part[i, 1]
+
+    @pl.when(step < chips)
+    def _():
+        for w_refs, side in ((near_refs, core), (far_refs, 1 - core)):
+            here = pl.ds(pl.multiple_of(side * COLS, COLS), COLS)
+            result = tok_ref[:, here].astype(F32) + dot(attended[:, :width], w_own_ref[:, here])
+            done = width
+            for w_ref in w_refs:
+                some = w_ref.shape[1] * width
+                weight = w_ref[0].reshape(some, COLS)
+                result += dot(attended[:, done : done + some], weight)
+                done += some
+            at = pl.ds(pl.multiple_of((2 * step + side) * COLS, COLS), COLS)
+            mixed[:, at] = result.astype(BF16)
+
+    @pl.when(step == chips)
+    def _():
+        values = mixed[...].astype(F32)
+        attended[...] = (rms_scale(values) * gain_ref[...]).astype(BF16)
+        own = mixed[:, pl.ds(pl.multiple_of(level * width, 128), width)]
+        own_ref[...] = own
+        total[...] = student_ref[...] - dot(own, proj_ref[...])
+
+    @pl.when(step >= chips)
+    def _():
+        gate = dot(attended[...], gate_ref[...])
+        up = dot(attended[...], up_ref[...])
+        hidden = (gate * jax.nn.sigmoid(gate) * up).astype(BF16)
+        hidden_ref[...] = hidden
+        total[...] -= dot(hidden, wp_ref[...])
+
+    @pl.when(step == pl.num_programs(0) - 1)
+    def _():
+        size = rows // ring
+        for s in range(ring):
+            at = pl.ds(pl.multiple_of((level + s) % ring * size, size), size)
+            pieces[s][...] = total[at, :].astype(BF16)
+
+
+def middle_call(info, parts, tok, w_out, near, far, gain, w_gate, w_up, wp, projector, student):
+    rows, depth = tok.shape
+    ring, chips = len(parts[0]), near[0].shape[0]
+    units = w_gate.shape[1]
+    wide = 2 * COLS
+    width = depth // ring
+    sd = projector.shape[1]
+    early = lambda j: jnp.minimum(j, chips - 1)
+    late = lambda j: jnp.maximum(j - chips, 0)
+    gathered = [
+        pl.BlockSpec((1,) + a.shape[1:], lambda j, info: (early(j) ^ info[1], 0, 0, 0))
+        for a in near
+    ]
+    result = pl.pallas_call(
+        functools.partial(middle_kernel, ring=ring, chips=chips),
+        out_shape=[
+            jax.ShapeDtypeStruct((rows, units), BF16),
+            jax.ShapeDtypeStruct((rows, width), BF16),
+        ]
+        + [jax.ShapeDtypeStruct((rows // ring, sd), BF16)] * ring,
+        grid_spec=pltpu.PrefetchScalarGridSpec(
+            num_scalar_prefetch=1,
+            grid=(chips + units // wide,),
+            in_specs=[whole(parts[0][0].shape)] * (2 * ring)
+            + [
+                pl.BlockSpec((rows, wide), lambda j, info: (0, early(j))),
+                pl.BlockSpec((width, wide), lambda j, info: (0, early(j))),
+                *gathered,
+                *gathered,
+                whole((1, depth)),
+                pl.BlockSpec((depth, wide), lambda j, info: (0, late(j))),
+                pl.BlockSpec((depth, wide), lambda j, info: (0, late(j))),
+                pl.BlockSpec((wide, sd), lambda j, info: (late(j), 0)),
+                pl.BlockSpec((width, sd), lambda j, info: (info[0], 0)),
+                whole((rows, sd)),
+            ],
+            out_specs=[
+                pl.BlockSpec((rows, wide), lambda j, info: (0, late(j))),
+                whole((rows, width)),
+            ]
+            + [whole((rows // ring, sd))] * ring,
+            scratch_shapes=[
+                pltpu.VMEM((rows, depth), BF16),
+                pltpu.VMEM((rows, depth), BF16),
+                pltpu.VMEM((rows, sd), F32),
+            ],
+        ),
+        compiler_params=params(44),
+        cost_estimate=cost(
+            2 * rows * depth * (depth + 2 * units) + 2 * rows * sd * (units + width),
+            2 * depth * (depth + 2 * units),
+            rows * units,
+        ),
+        name="middle",
+    )(
+        info,
+        *parts[0],
+        *parts[1],
+        tok,
+        w_out,
+        *near,
+        *far,
+        gain,
+        w_gate,
+        w_up,
+        wp,
+        projector,
+        student,
+    )
+    return result[0], result[1], result[2:]
+
+
+def down_kernel(level_ref, hidden_ref, weight_ref, out_ref):
+    out_ref[0] = dot(hidden_ref[...], weight_ref[...]).astype(BF16)
+
+
+def down_call(level, hidden, w_down, ring):
+    rows, units = hidden.shape
+    depth = w_down.shape[1]
+    width = depth // ring
+    return pl.pallas_call(
+        down_kernel,
+        out_shape=jax.ShapeDtypeStruct((ring, rows, width), BF16),
+        grid_spec=pltpu.PrefetchScalarGridSpec(
+            num_scalar_prefetch=1,
+            grid=(ring,),
+            in_specs=[
+                whole((rows, units)),
+                pl.BlockSpec(
+                    (units, width), lambda j, level: (0, (level[0] + 2 * ring - 1 - j) % ring)
+                ),
+            ],
+            out_specs=pl.BlockSpec((1, rows, width), lambda j, level: (j, 0, 0)),
+        ),
+        compiler_params=params(24),
+        cost_estimate=cost(2 * rows * units * depth, 2 * units * depth),
+        name="down",
+    )(level, hidden, w_down)
+
+
+def grads_kernel(info_ref, *refs, ring, chips):
+    pieces = refs[:ring]
+    normed_ref, hidden_ref, s_down_ref, up_ref, gate_ref = refs[ring : ring + 5]
+    keep_ref, give_ref, scaled, grads = refs[ring + 5 :]
+    chip, core = info_ref[ring], info_ref[ring + 1]
+    size, sd = pieces[0].shape
+    for s in range(ring):
+        scaled[pl.ds(pl.multiple_of(info_ref[s] * size, size), size), :] = pieces[s][...]
+    value = scaled[...]
+    wide = value.astype(F32)
+    error = jnp.sum(wide * wide)
+    grad_hidden = dot_over(value, s_down_ref[...], (1, 1))
+    grads[0] = dot_over(normed_ref[...], (grad_hidden * gate_ref[...]).astype(BF16), (0, 0))
+    grads[1] = dot_over(normed_ref[...], (grad_hidden * up_ref[...]).astype(BF16), (0, 0))
+    grads[2] = dot_over(hidden_ref[...], value, (0, 0))
+    share = grads.shape[1] // (2 * chips)
+    for f in range(chips):
+        for k in range(3):
+            for part, ref in ((core, keep_ref), (1 - core, give_ref)):
+                at = pl.multiple_of((part * chips + (chip ^ f)) * share, share)
+                ref[f, k * share : (k + 1) * share] = grads[k, pl.ds(at, share), :].astype(
+                    ref.dtype
+                )
+        for ref in (keep_ref, give_ref):
+            ref[f, 3 * share :] = jnp.full((NOTE, sd), error, F32).astype(ref.dtype)
+
+
+def grads_call(info, pieces, normed, hidden, s_down, up, gate, chips):
+    ring = len(pieces)
+    rows, sd = normed.shape
+    units = hidden.shape[1]
+    share = 3 * sd // (2 * chips) + NOTE
+    operands = [*pieces, normed, hidden, s_down, up, gate]
+    return pl.pallas_call(
+        functools.partial(grads_kernel, ring=ring, chips=chips),
+        out_shape=(
+            jax.ShapeDtypeStruct((chips, share, units), F32),
+            jax.ShapeDtypeStruct((chips, share, units), BF16),
+        ),
+        grid_spec=pltpu.PrefetchScalarGridSpec(
+            num_scalar_prefetch=1,
+            grid=(1,),
+            in_specs=[whole(a.shape) for a in operands],
+            out_specs=(whole((chips, share, units)), whole((chips, share, units))),
+            scratch_shapes=[pltpu.VMEM((rows, sd), BF16), pltpu.VMEM((3, sd, units), F32)],
+        ),
+        compiler_params=params(24),
+        cost_estimate=cost(8 * rows * sd * units, 20 * sd * units),
+        name="grads",
+    )(info, *operands)
+
+
+def pair_kernel(keep_ref, theirs_ref, *outs):
+    for f, out in enumerate(outs):
+        out[...] = (keep_ref[f] + theirs_ref[f].astype(F32)).astype(out.dtype)
+
+
+def pair_call(keep, theirs):
+    chips, share, sd = keep.shape
+    return pl.pallas_call(
+        pair_kernel,
+        out_shape=[jax.ShapeDtypeStruct((share, sd), BF16)] * chips,
+        compiler_params=params(16),
+        cost_estimate=cost(keep.size, 8 * keep.size),
+        name="pair",
+    )(keep, theirs)
+
+
+def finish_kernel(info_ref, *refs, chips):
+    mine, others = refs[:chips], refs[chips : 2 * chips]
+    outs = refs[2 * chips : 2 * chips + 3]
+    notes = refs[2 * chips + 3]
+    chip, core = info_ref[0], info_ref[1]
+    share = (mine[0].shape[0] - NOTE) // 3
+    for f in range(chips):
+        for part, ref in ((core, mine[f]), (1 - core, others[f])):
+            index = part * chips + (chip ^ f)
+            at = pl.ds(pl.multiple_of(index * share, share), share)
+            for k in range(3):
+                outs[k][at, :] = ref[k * share : (k + 1) * share].astype(F32)
+            notes[index] = ref[3 * share :, :HD].astype(F32)
+
+
+def finish_call(info, mine, others):
+    chips = len(mine)
+    share, sd = mine[0].shape
+    rows = (share - NOTE) // 3 * 2 * chips
+    return pl.pallas_call(
+        functools.partial(finish_kernel, chips=chips),
+        out_shape=[jax.ShapeDtypeStruct((rows, sd), F32)] * 3
+        + [jax.ShapeDtypeStruct((2 * chips, NOTE, HD), F32)],
+        grid_spec=pltpu.PrefetchScalarGridSpec(
+            num_scalar_prefetch=1,
+            grid=(1,),
+            in_specs=[whole((share, sd))] * (2 * chips),
+            out_specs=[whole((rows, sd))] * 3 + [whole((2 * chips, NOTE, HD))],
+        ),
+        compiler_params=params(20),
+        cost_estimate=cost(rows * sd, 12 * rows * sd),
+        name="finish",
+    )(info, *mine, *others)
+
+
+def step_on(block, axis):
+    size = lax.axis_size(axis)
+    return lax.ppermute(block, axis, [(i, (i + 1) % size) for i in range(size)])
+
+
+def ring_gather(block, axis, steps=None):
+    blocks = [block]
+    for _ in range(lax.axis_size(axis) - 1 if steps is None else steps):
+        blocks.append(step_on(blocks[-1], axis))
+    return blocks
+
+
+def shifted(pieces, axis):
+    size = lax.axis_size(axis)
+    moved = [
+        lax.ppermute(pieces[s], axis, [(i, (i + s) % size) for i in range(size)])
+        for s in range(1, size)
+    ]
+    return [pieces[0], *moved]
+
+
+def flipped(pieces):
+    size = lax.axis_size("dp")
+    moved = [
+        lax.ppermute(pieces[f], "dp", [(i, i ^ (2 * f)) for i in range(size)])
+        for f in range(1, len(pieces))
+    ]
+    return [pieces[0], *moved]
+
+
+def swapped(value):
+    size = lax.axis_size("dp")
+    return lax.ppermute(value, "dp", [(i, i ^ 1) for i in range(size)])
+
+
+def after(value, *others):
+    return lax.optimization_barrier((value, *others))[0]
+
+
+def paired(
+    tokens,
+    series_ids,
+    offsets,
+    norm_gain,
+    mlp_gain,
+    w_query,
+    w_key,
+    w_value,
+    w_out,
+    w_gate,
+    w_up,
+    w_down,
+    projector,
+    student_in,
+    s_gate,
+    s_up,
+    s_down,
+):
+    rows = tokens.shape[0]
+    depth, sd = w_query.shape[0], student_in.shape[1]
+    dp, ring = lax.axis_size("dp"), lax.axis_size("tensor")
+    here, level = lax.axis_index("dp"), lax.axis_index("tensor")
+    chips, half = dp // 2, rows // 2
+    chip, core = here // 2, here % 2
+    total_rows = rows * dp
+    number = lambda *values: jnp.stack([jnp.asarray(v, jnp.int32) for v in values])
+    source = [(level - s) % ring for s in range(ring)]
+
+    def deal(value):
+        parts = value.reshape((2, half) + value.shape[1:])
+        kept = lax.dynamic_index_in_dim(parts, core, 0, False)
+        return kept, swapped(lax.dynamic_index_in_dim(parts, 1 - core, 0, False))
+
+    token_chunks = deal(tokens)
+    token_rings = [ring_gather(chunk, "tensor") for chunk in token_chunks]
+    student_chunks = deal(student_in)
+    offset_chunks = deal(offsets.astype(F32))
+
+    angles = jnp.concatenate(offset_chunks)[:, None] * frequencies(HD)[None, :]
+    cosine, sine = jnp.cos(angles), jnp.sin(angles)
+    cosine = jnp.concatenate([cosine, cosine], axis=1)
+    sine = jnp.concatenate([-sine, sine], axis=1)
+    factor = HD ** (-0.5) * math.log2(math.e)
+    student_full = jnp.concatenate(student_chunks, axis=0).astype(F32)
+    student_normed = rms_scale(student_full).astype(BF16)
+    s_gate_out = dot(student_normed, s_gate)
+    s_up_out = dot(student_normed, s_up)
+    sigmoid_gate = jax.nn.sigmoid(s_gate_out)
+    up_slope = s_gate_out * sigmoid_gate
+    gate_slope = s_up_out * sigmoid_gate * (1.0 + s_gate_out * (1.0 - sigmoid_gate))
+    s_hidden = (up_slope * s_up_out).astype(BF16)
+    student_part = dot(s_hidden, s_down)
+    projected = dot(w_down, projector).astype(BF16)
+    below = jnp.sum(
+        series_ids[None, :] < jnp.arange(SERIES, dtype=jnp.int32)[:, None], axis=1, dtype=jnp.int32
+    )
+
+    early = (projected, student_part, s_hidden, up_slope, gate_slope, student_normed)
+    info = after(number(*source, chip), *early)
+    made, tok_full, normed = kv_call(
+        info, token_rings, norm_gain[None, :], cosine, sine, w_key, w_value
+    )
+    own_kv = flipped(made)
+    queries = query_call(info, normed, cosine * factor, sine * factor, w_query)
+    own_kv = lax.optimization_barrier((*own_kv, queries[0]))[:chips]
+    other_kv = [swapped(a) for a in own_kv]
+
+    slice_cols = depth // dp
+    w_slice = lax.dynamic_slice_in_dim(w_out, here * slice_cols, slice_cols, 1)
+    w_slice = after(w_slice, queries[0])
+    w_others = shifted([w_slice] * ring, "tensor")[1:]
+    queries = flipped(queries)
+
+    pairs = lambda a: a.reshape(a.shape[:-2] + (2, half, HD))
+    w_first = after(w_others[0], *queries, *other_kv)
+    near_first = flipped([w_first] * chips)
+    attention_info = jnp.concatenate([below, number(chip, core)])
+    made = attention_call(
+        attention_info,
+        [pairs(a) for a in queries],
+        [pairs(a) for a in own_kv],
+        [pairs(a) for a in other_kv],
+    )
+    held = lax.optimization_barrier((*made, *w_others[1:], *near_first))
+    made, w_rest = held[:chips], jnp.stack(held[chips : chips + ring - 2])
+    attended = flipped(made)
+    parts = [
+        ring_gather(jnp.stack(attended[k : k + chips // 2]), "tensor") for k in (0, chips // 2)
+    ]
+    w_rest = after(w_rest, *attended)
+    near_rest = flipped([w_rest] * chips)
+    near_rest = lax.optimization_barrier((*near_rest, *parts[0], *parts[1][:-1]))[:chips]
+    near = (jnp.stack(near_first)[:, None], jnp.stack(near_rest))
+    far = [swapped(after(a, *attended)) for a in near]
+
+    hidden, mixed_own, pieces = middle_call(
+        number(level, chip, core),
+        parts,
+        tok_full,
+        w_out,
+        near,
+        far,
+        mlp_gain[None, :],
+        w_gate,
+        w_up,
+        projected,
+        projector,
+        student_part,
+    )
+
+    size = rows // ring
+    own = lax.dynamic_slice_in_dim(student_full, level * size, size, 0)
+    difference = own + sum(piece.astype(F32) for piece in shifted(pieces, "tensor"))
+    own = (difference * total_rows ** (-0.5)).astype(BF16)
+    scaled = shifted([own] * ring, "tensor")
+
+    mlp_part = down_call(level.astype(jnp.int32)[None], hidden, w_down, ring)
+    mlp_part = after(mlp_part, *scaled)
+    mlp_own = mlp_part[0]
+    for s in range(1, ring):
+        mlp_own = step_on(mlp_own, "tensor").astype(F32) + mlp_part[s].astype(F32)
+        mlp_own = mlp_own.astype(BF16) if s < ring - 1 else mlp_own
+
+    keep, give = grads_call(
+        number(*source, chip, core),
+        scaled,
+        student_normed,
+        s_hidden,
+        s_down,
+        up_slope,
+        gate_slope,
+        chips,
+    )
+    shares = flipped(pair_call(keep, swapped(give)))
+    own = sum(share.astype(F32) for share in shares).astype(BF16)
+    mine = flipped([own] * chips)
+    others = [swapped(share) for share in mine]
+    mlp_own = after(mlp_own, *others)
+    teacher = (mixed_own.astype(F32) + mlp_own).astype(BF16)
+    back = swapped(teacher[half:])
+    teacher_out = jnp.where(
+        core == 0,
+        jnp.concatenate([teacher[:half], back], axis=0),
+        jnp.concatenate([back, teacher[:half]], axis=0),
+    )
+
+    grad_gate, grad_up, grad_down, notes = finish_call(number(chip, core), mine, others)
+    return teacher_out, grad_gate, grad_up, grad_down, notes[0, 0, 0] / sd
+
+
+def local(*args):
+    rows, w_query, s_gate = args[0].shape[0], args[5], args[14]
+    dp, ring = lax.axis_size("dp"), lax.axis_size("tensor")
+    heads = w_query.shape[1] // HD
+    fits = (
+        dp == 2 * heads
+        and heads > 1
+        and heads & (heads - 1) == 0
+        and w_query.shape[0] == dp * COLS
+        and s_gate.shape[0] == s_gate.shape[1]
+        and rows % (32 * ring) == 0
+    )
+    return paired(*args) if fits else general(*args)
+
+
 def solution(mesh):
     in_specs = (
         P("dp", "tensor"),

time: 520 us -> 265 us (0.51)
  waiting for transfers between devices: 341 us -> 114 us
  matrix products: 89 us -> 12.8 us
  starting transfers between devices: 1.03 us -> 55.6 us
  Pallas kernels: 0 us -> 53.9 us
  other arithmetic: 39.3 us -> 8.39 us
  blocking collectives: 14.5 us -> 0 us
  between operations: 15.8 us -> 2.97 us
    all_gather x5 -> x0, waiting for transfers between devices: 176 us -> none  [the longest x1 48.1 us: local(): teacher_full = lax.all_gather(teacher_out, 'tensor', axis=1, tiled=True)]
    ppermute x0 -> x60, waiting for transfers between devices: none -> 114 us  [the longest x15 67.7 us: step_on(): return lax.ppermute(block, axis, [(i, (i + 1) % size) for i in range(size)])]
    reduce_scatter x2 -> x0, waiting for transfers between devices: 82.2 us -> none  [the longest x1 44 us: local(): lax.psum_scatter(partial_out.astype(jnp.bfloat16), 'tensor', scatter_dime...]
    psum x2 -> x0, waiting for transfers between devices: 81.5 us -> none  [the longest x1 43.2 us: local(): lax.psum(grad_gate_part.astype(jnp.bfloat16), 'dp').astype(jnp.float32)]
    dot_general x16 -> x4, matrix products: 89 us -> 12.8 us  [dot(): return jnp.dot(a, b, preferred_element_type=F32)]
    ppermute x0 -> x60, starting transfers between devices: none -> 55.6 us  [the longest x21 24.5 us: flipped(): lax.ppermute(pieces[f], 'dp', [(i, i ^ 2 * f) for i in range(size)])]
    pallas_call x0 -> x8, Pallas kernels: none -> 53.9 us  [the longest x1 22.9 us: middle_call(): pl.pallas_call(functools.partial(middle_kernel, ring=ring, chips=chips),...]
    reduce_sum x1, other arithmetic: 15.2 us -> 0.15 us  [paired(): jnp.sum(series_ids[None, :] < jnp.arange(SERIES, dtype=jnp.int32)[:, None...]
  transfers between devices with their start and end apart: 9 -> 60, of which waited for: 9 -> 27; matrix products, arithmetic and copies ran while one was open for 9% -> 8% of each run, Pallas kernels for 0% -> 10%
where the time goes in v2:
time: 265 us; the launch traced here: 264 us
  waiting for transfers between devices  114 us (43%)
  starting transfers between devices  55.6 us (21%)
  Pallas kernels  53.9 us (20%)
  local copies, waits for them, and re-layouts  16.6 us (6%)
  matrix products  12.8 us (5%)
  other arithmetic  8.39 us (3%)
  between operations  2.97 us (1%)
    ppermute x15, waiting for transfers between devices, step_on(): return lax.ppermute(block, axis, [(i, (i + 1) % size) for i in range(size)])  67.7 us
    ppermute x21, waiting for transfers between devices, flipped(): lax.ppermute(pieces[f], 'dp', [(i, i ^ 2 * f) for i in range(size)])  28.7 us
    ppermute x21, starting transfers between devices, flipped(): lax.ppermute(pieces[f], 'dp', [(i, i ^ 2 * f) for i in range(size)])  24.5 us
    pallas_call x1, Pallas kernels, middle_call(): pl.pallas_call(functools.partial(middle_kernel, ring=ring, chips=chips),...  22.9 us
    ppermute x15, starting transfers between devices, step_on(): return lax.ppermute(block, axis, [(i, (i + 1) % size) for i in range(size)])  19.9 us
    ppermute x9, waiting for transfers between devices, shifted(): lax.ppermute(pieces[s], axis, [(i, (i + s) % size) for i in range(size)])  17.7 us
    dot_general x4, matrix products, dot(): return jnp.dot(a, b, preferred_element_type=F32)  12.8 us
    pallas_call x1, Pallas kernels, attention_call(): pl.pallas_call(functools.partial(attention_kernel, chips=chips), out_shap...  12.4 us
  transfers between devices with their start and end apart: 60, of which 27 were waited for; matrix products, arithmetic and copies ran while one was open for 8% of the time, Pallas kernels for 10%

profile of v2, /device:TPU:0, one launch (start us, length us, event | category | flops | bytes accessed | tf_op | source)
XLA Modules:
  0.0 264.4 jit_solution(12521880369369804859)
XLA Ops:
  4.7 2.6 collective-permute-start.1
  7.4 9.8 %convolution_convert_fusion.refs_17_ = bf16[2048,512]{1,0:T(8,128)(2,1)} fusion(bf16[2048,2048]{1,0:T(8,128)(2,1)} %weight_ref.1, bf16[2048,512]{1,0:T(8,128)(2,1)} %refs_18_.1), kind=kOutput, calls=%fused_computation | convolution fusion | flops 4296015872 | bytes 12582912 | tf_op jit(solution)/shard_map/dot_general | solution.py:166
  18.7 1.6 collective-permute-start.5
  20.6 1.6 collective-permute-start.2
  22.6 7.1 %collective-permute-done.5.refs_5_ = bf16[256,512]{1,0:T(8,128)(2,1)S(1)} collective-permute-done((bf16[256,512]{1,0:T(8,128)(2,1)S(1)}, bf16[256,512]{1,0:T(8,128)(2,1)S(1)}, u32[]{:S(2)}, u32[]{:S(2)}) %collective-permute-start.5) | collective-permute-done | bytes 262176 | tf_op jit(solution)/shard_map/ppermute | solution.py:651
  29.7 2.1 add_multiply_fusion
  31.9 3.5 %collective-permute-done.2.refs_2_ = bf16[256,512]{1,0:T(8,128)(2,1)S(1)} collective-permute-done((bf16[256,512]{1,0:T(8,128)(2,1)S(1)}, bf16[256,512]{1,0:T(8,128)(2,1)S(1)}, u32[]{:S(2)}, u32[]{:S(2)}) %collective-permute-start.2) | collective-permute-done | bytes 262176 | tf_op jit(solution)/shard_map/ppermute | solution.py:651
  35.4 5.6 %collective-permute-done.6.refs_6_ = bf16[256,512]{1,0:T(8,128)(2,1)S(1)} collective-permute-done((bf16[256,512]{1,0:T(8,128)(2,1)S(1)}, bf16[256,512]{1,0:T(8,128)(2,1)S(1)}, u32[]{:S(2)}, u32[]{:S(2)}) %collective-permute-start.6) | collective-permute-done | bytes 262176 | tf_op jit(solution)/shard_map/ppermute | solution.py:651
  41.4 5.2 %collective-permute-done.3.refs_3_ = bf16[256,512]{1,0:T(8,128)(2,1)S(1)} collective-permute-done((bf16[256,512]{1,0:T(8,128)(2,1)S(1)}, bf16[256,512]{1,0:T(8,128)(2,1)S(1)}, u32[]{:S(2)}, u32[]{:S(2)}) %collective-permute-start.3) | collective-permute-done | bytes 262176 | tf_op jit(solution)/shard_map/ppermute | solution.py:651
  46.6 4.8 %collective-permute-done.7.refs_7_ = bf16[256,512]{1,0:T(8,128)(2,1)S(1)} collective-permute-done((bf16[256,512]{1,0:T(8,128)(2,1)S(1)}, bf16[256,512]{1,0:T(8,128)(2,1)S(1)}, u32[]{:S(2)}, u32[]{:S(2)}) %collective-permute-start.7) | collective-permute-done | bytes 262176 | tf_op jit(solution)/shard_map/ppermute | solution.py:651
  51.5 5.3 %keys_values.1 = (bf16[2,512,128]{2,1,0:T(8,128)(2,1)S(1)}, bf16[2,512,128]{2,1,0:T(8,128)(2,1)S(1)}, bf16[2,512,128]{2,1,0:T(8,128)(2,1)}, bf16[2,512,128]{2,1,...) custom-call(s32[5]{0:T(128)S(1)} %stack.109.info_ref, ...), custom_call_target="tpu_custom_call" | custom-call | flops 2147483648 | bytes 4194304 | tf_op jit(solution)/shard_map/keys_values/pallas_call | solution.py:233
  56.8 1.5 collective-permute-start.12
  58.2 1.5 collective-permute-start.13
  60.3 2.7 %queries.1 = (bf16[512,128]{1,0:T(8,128)(2,1)S(1)}, bf16[512,128]{1,0:T(8,128)(2,1)}, bf16[512,128]{1,0:T(8,128)(2,1)S(1)}, bf16[512,128]{1,0:T(8,128)(2,1)}) custom-call(s32[5]{0:T(128)S(1)} %stack.109.info_ref, bf16[512,2048]{1,0:T(8,128)(2,1)S(1)} %get-tuple-element.58.normed_ref, f32[512,128]{1,0:T(8,128)S(1)} %get-tuple-element.130.cos_ref, ...), custom_call_target="tpu_custom_call" | custom-call | flops 1073741824 | bytes 2097152 | tf_op jit(solution)/shard_map/queries/pallas_call | solution.py:267
  63.0 1.5 collective-permute-start.10
  64.5 1.4 collective-permute-start.11
  66.0 1.5 collective-permute-start.9
  68.5 7.1 %collective-permute-done.13 = bf16[2,512,128]{2,1,0:T(8,128)(2,1)S(1)} collective-permute-done((bf16[2,512,128]{2,1,0:T(8,128)(2,1)}, bf16[2,512,128]{2,1,0:T(8,128)(2,1)S(1)}, u32[]{:S(2)}, u32[]{:S(2)}) %collective-permute-start.13) | collective-permute-done | bytes 262176 | tf_op jit(solution)/shard_map/ppermute | solution.py:673
  75.6 1.4 collective-permute-done.10
  77.7 8.3 %collective-permute-done.21 = bf16[512,256]{1,0:T(8,128)(2,1)S(1)} collective-permute-done((bf16[512,256]{1,0:T(8,128)(2,1)S(1)}, bf16[512,256]{1,0:T(8,128)(2,1)S(1)}, u32[]{:S(2)}, u32[]{:S(2)}) %collective-permute-start.21) | collective-permute-done | bytes 262176 | tf_op jit(solution)/shard_map/ppermute | solution.py:664
  86.2 2.0 collective-permute-start.23
  88.2 1.4 collective-permute-start.24
  89.7 12.4 %attention.1 = (bf16[2,256,128]{2,1,0:T(8,128)(2,1)S(1)}, bf16[2,256,128]{2,1,0:T(8,128)(2,1)S(1)}, bf16[2,256,128]{2,1,0:T(8,128)(2,1)S(1)}, bf16[2,256,128]{2,1,0:T(8,128)(2,1)S(1)}) custom-call(s32[10]{0:T(128)S(1)} %pad_add_fusion.1.info_ref, bf16[2,256,128]{2,1,0:T(8,128)(2,1)S(1)} %bitcast.84, bf16[2,256,128]{2,1,0:T(8,128)(2,1)} %bitcast.17.refs_1_, ...), custom_call_target="tpu_custom_call" | custom-call | flops 2147483648 | bytes 3145728 | tf_op jit(solution)/shard_map/attention/pallas_call | solution.py:360
  102.3 5.8 %collective-permute-done.25 = bf16[2,256,128]{2,1,0:T(8,128)(2,1)S(1)} collective-permute-done((bf16[2,256,128]{2,1,0:T(8,128)(2,1)S(1)}, bf16[2,256,128]{2,1,0:T(8,128)(2,1)S(1)}, u32[]{:S(2)}, u32[]{:S(2)}) %collective-permute-start.25) | collective-permute-done | bytes 131104 | tf_op jit(solution)/shard_map/ppermute | solution.py:673
  108.2 1.5 collective-permute-start.26
  109.7 1.5 collective-permute-start.29
  111.5 4.8 %collective-permute-done.29 = bf16[2,256,128]{2,1,0:T(8,128)(2,1)S(1)} collective-permute-done((bf16[2,256,128]{2,1,0:T(8,128)(2,1)S(1)}, bf16[2,256,128]{2,1,0:T(8,128)(2,1)S(1)}, u32[]{:S(2)}, u32[]{:S(2)}) %collective-permute-start.29) | collective-permute-done | bytes 131104 | tf_op jit(solution)/shard_map/ppermute | solution.py:673
  116.4 2.1 collective-permute-done.30
  119.0 5.9 %collective-permute-start.31 = (bf16[2,2,256,128]{3,2,1,0:T(8,128)(2,1)S(1)}, bf16[2,2,256,128]{3,2,1,0:T(8,128)(2,1)S(1)}, u32[]{:S(2)}, u32[]{:S(2)}) collective-permute-start(bf16[2,2,256,128]{3,2,1,0:T(8,128)(2,1)S(1)} %pad_maximum_fusion.6.refs_4_), channel_id=1, source_target_pairs={{0,1},{1,2},{2,3},{3,0},{4,5},{5,6},{6,7},{7,4},{8,9},{9,10},{10,1... | collective-permute-start | bytes 786440 | tf_op jit(solution)/shard_map/ppermute | solution.py:651
  125.0 2.0 collective-permute-start.35
  127.0 1.4 collective-permute-start.36
  128.5 1.5 collective-permute-done.31.refs_5_
  130.1 1.3 collective-permute-start.32
  131.3 5.3 %collective-permute-done.27.refs_2_ = bf16[2,2,256,128]{3,2,1,0:T(8,128)(2,1)S(1)} collective-permute-done((bf16[2,2,256,128]{3,2,1,0:T(8,128)(2,1)S(1)}, bf16[2,2,256,128]{3,2,1,0:T(8,128)(2,1)S(1)}, u32[]{:S(2)}, u32[]{:S(2)}) %collective-permute-start.27) | collective-permute-done | bytes 262176 | tf_op jit(solution)/shard_map/ppermute | solution.py:651
  136.6 2.9 %collective-permute-done.32.refs_6_ = bf16[2,2,256,128]{3,2,1,0:T(8,128)(2,1)} collective-permute-done((bf16[2,2,256,128]{3,2,1,0:T(8,128)(2,1)S(1)}, bf16[2,2,256,128]{3,2,1,0:T(8,128)(2,1)}, u32[]{:S(2)}, u32[]{:S(2)}) %collective-permute-start.32) | collective-permute-done | bytes 262176 | tf_op jit(solution)/shard_map/ppermute | solution.py:651
  139.8 5.0 %collective-permute-done.28.refs_3_ = bf16[2,2,256,128]{3,2,1,0:T(8,128)(2,1)S(1)} collective-permute-done((bf16[2,2,256,128]{3,2,1,0:T(8,128)(2,1)S(1)}, bf16[2,2,256,128]{3,2,1,0:T(8,128)(2,1)S(1)}, u32[]{:S(2)}, u32[]{:S(2)}) %collective-permute-start.28) | collective-permute-done | bytes 262176 | tf_op jit(solution)/shard_map/ppermute | solution.py:651
  144.8 1.6 pad_maximum_fusion.refs_11_
  146.4 1.1 fusion.4
  148.2 10.3 %collective-permute-done.33.refs_7_ = bf16[2,2,256,128]{3,2,1,0:T(8,128)(2,1)} collective-permute-done((bf16[2,2,256,128]{3,2,1,0:T(8,128)(2,1)}, bf16[2,2,256,128]{3,2,1,0:T(8,128)(2,1)}, u32[]{:S(2)}, u32[]{:S(2)}) %collective-permute-start.33) | collective-permute-done | bytes 262176 | tf_op jit(solution)/shard_map/ppermute | solution.py:651
  159.6 1.2 copy-done.28
  161.7 22.9 %middle.1 = (bf16[512,2048]{1,0:T(8,128)(2,1)S(1)}, bf16[512,512]{1,0:T(8,128)(2,1)S(1)}, bf16[128,512]{1,0:T(8,128)(2,1)S(1)}, bf16[128,512]{1,0:T(8,128)(2,1)S...) custom-call(s32[3]{0:T(128)S(1)} %pad_add_fusion.info_ref, ...), custom_call_target="tpu_custom_call" | custom-call | flops 14227079168 | bytes 25165824 | tf_op jit(solution)/shard_map/middle/pallas_call | solution.py:459
  184.8 3.7 %collective-permute-start.41 = (bf16[128,512]{1,0:T(8,128)(2,1)S(1)}, bf16[128,512]{1,0:T(8,128)(2,1)S(1)}, u32[]{:S(2)}, u32[]{:S(2)}) collective-permute-start(bf16[128,512]{1,0:T(8,128)(2,1)S(1)} %get-tuple-element.96), channel_id=1, source_target_pairs={{0,3},{1,0},{2,1},{3,2},{4,7},{5,4},{6,5},{7,6},{8,11},{9,8},{10,9... | collective-permute-start | bytes 393224 | tf_op jit(solution)/shard_map/ppermute | solution.py:664
  188.6 4.3 %collective-permute-done.39 = bf16[128,512]{1,0:T(8,128)(2,1)S(1)} collective-permute-done((bf16[128,512]{1,0:T(8,128)(2,1)S(1)}, bf16[128,512]{1,0:T(8,128)(2,1)S(1)}, u32[]{:S(2)}, u32[]{:S(2)}) %collective-permute-start.39) | collective-permute-done | bytes 131104 | tf_op jit(solution)/shard_map/ppermute | solution.py:664
  193.0 3.9 %collective-permute-done.40 = bf16[128,512]{1,0:T(8,128)(2,1)S(1)} collective-permute-done((bf16[128,512]{1,0:T(8,128)(2,1)S(1)}, bf16[128,512]{1,0:T(8,128)(2,1)S(1)}, u32[]{:S(2)}, u32[]{:S(2)}) %collective-permute-start.40) | collective-permute-done | bytes 131104 | tf_op jit(solution)/shard_map/ppermute | solution.py:664
  196.9 2.4 collective-permute-start.42
  199.5 2.3 collective-permute-start.44
  201.8 5.8 %down.1 = bf16[4,512,512]{2,1,0:T(8,128)(2,1)S(1)} custom-call(s32[1]{0:T(128)} %bitcast.level_ref, bf16[512,2048]{1,0:T(8,128)(2,1)S(1)} %get-tuple-element.92.hidden_ref, bf16[2048,2048]{1,0:T(8,128)(2,1)S(1)} %bitcast.75), custom_call_target="tpu_custom_call" | custom-call | flops 4294967296 | bytes 8388608 | tf_op jit(solution)/shard_map/down/pallas_call | solution.py:526
  210.2 3.2 %collective-permute-start.45 = (bf16[512,512]{1,0:T(8,128)(2,1)}, bf16[512,512]{1,0:T(8,128)(2,1)}, u32[]{:S(2)}, u32[]{:S(2)}) collective-permute-start(bf16[512,512]{1,0:T(8,128)(2,1)} %slice_bitcast_fusion), channel_id=1, source_target_pairs={{0,1},{1,2},{2,3},{3,0},{4,5},{5,6},{6,7},{7,4},{8,9},{9,10},{10,1... | collective-permute-start | bytes 1572872 | tf_op jit(solution)/shard_map/ppermute | solution.py:651
  214.6 1.2 copy-done.7
  215.8 1.2 copy-done.8
  217.9 2.1 grads.1
  220.1 5.8 %collective-permute-done.45 = bf16[512,512]{1,0:T(8,128)(2,1)} collective-permute-done((bf16[512,512]{1,0:T(8,128)(2,1)}, bf16[512,512]{1,0:T(8,128)(2,1)}, u32[]{:S(2)}, u32[]{:S(2)}) %collective-permute-start.45) | collective-permute-done | bytes 524320 | tf_op jit(solution)/shard_map/ppermute | solution.py:651
  225.9 1.2 fusion.1
  227.1 1.6 collective-permute-start.46
  229.1 1.9 collective-permute-start.50
  231.0 1.4 collective-permute-start.51
  232.5 8.8 %collective-permute-done.46 = bf16[512,512]{1,0:T(8,128)(2,1)S(1)} collective-permute-done((bf16[512,512]{1,0:T(8,128)(2,1)S(1)}, bf16[512,512]{1,0:T(8,128)(2,1)S(1)}, u32[]{:S(2)}, u32[]{:S(2)}) %collective-permute-start.46) | collective-permute-done | bytes 524320 | tf_op jit(solution)/shard_map/ppermute | solution.py:651
  242.2 1.9 collective-permute-start.55
  244.1 1.4 collective-permute-start.57
  245.5 3.8 %collective-permute-done.53.refs_1_ = bf16[208,512]{1,0:T(8,128)(2,1)S(1)} collective-permute-done((bf16[208,512]{1,0:T(8,128)(2,1)S(1)}, bf16[208,512]{1,0:T(8,128)(2,1)S(1)}, u32[]{:S(2)}, u32[]{:S(2)}) %collective-permute-start.53) | collective-permute-done | bytes 213024 | tf_op jit(solution)/shard_map/ppermute | solution.py:673
  249.3 1.6 collective-permute-done.55.refs_2_
  250.9 1.7 collective-permute-done.57.refs_3_
  252.7 1.9 collective-permute-done.47
  258.7 2.4 finish.1
  (188 shorter events, 25.2 us)
Async XLA Ops:
  0.6 29.1 %copy-start = (bf16[512,512]{1,0:T(8,128)(2,1)S(1)}, bf16[512,512]{1,0:T(8,128)(2,1)}, u32[]{:S(2)}) copy-start(bf16[512,512]{1,0:T(8,128)(2,1)} %param.31) | copy-start | bytes 1572868
  1.8 16.7 %collective-permute-start = (bf16[256,512]{1,0:T(8,128)(2,1)S(1)}, bf16[256,512]{1,0:T(8,128)(2,1)S(1)}, u32[]{:S(2)}, u32[]{:S(2)}) collective-permute-start(bf16[256,512]{1,0:T(8,128)(2,1)S(1)} %get-tuple-element.121), channel_id=1, source_target_pairs={{0,4},{4,0},{8,12},{12,8},{16,20},{20,16},{24,28},{28,24},{1,5},{5... | collective-permute-start | bytes 786440 | tf_op jit(solution)/shard_map/ppermute | solution.py:681
  3.0 14.2 %collective-permute-start.8 = (f32[256]{0:T(256)S(1)}, f32[256]{0:T(256)S(1)}, u32[]{:S(2)}, u32[]{:S(2)}) collective-permute-start(f32[256]{0:T(256)S(1)} %bitcast.104), channel_id=1, source_target_pairs={{0,4},{4,0},{8,12},{12,8},{16,20},{20,16},{24,28},{28,24},{1,5},{5... | collective-permute-start | bytes 3080 | tf_op jit(solution)/shard_map/ppermute | solution.py:681
  4.2 14.5 %collective-permute-start.4 = (bf16[256,512]{1,0:T(8,128)(2,1)S(1)}, bf16[256,512]{1,0:T(8,128)(2,1)S(1)}, u32[]{:S(2)}, u32[]{:S(2)}) collective-permute-start(bf16[256,512]{1,0:T(8,128)(2,1)S(1)} %get-tuple-element.118), channel_id=1, source_target_pairs={{0,4},{4,0},{8,12},{12,8},{16,20},{20,16},{24,28},{28,24},{1,5},{5... | collective-permute-start | bytes 786440 | tf_op jit(solution)/shard_map/ppermute | solution.py:681
  4.7 15.8 %collective-permute-start.1 = (bf16[256,512]{1,0:T(8,128)(2,1)S(1)}, bf16[256,512]{1,0:T(8,128)(2,1)S(1)}, u32[]{:S(2)}, u32[]{:S(2)}) collective-permute-start(bf16[256,512]{1,0:T(8,128)(2,1)S(1)} %get-tuple-element.119.refs_0_), channel_id=1, source_target_pairs={{0,1},{1,2},{2,3},{3,0},{4,5},{5,6},{6,7},{7,4},{8,9},{9,10},{10,1... | collective-permute-start | bytes 786440 | tf_op jit(solution)/shard_map/ppermute | solution.py:651
  18.7 11.0 %collective-permute-start.5 = (bf16[256,512]{1,0:T(8,128)(2,1)S(1)}, bf16[256,512]{1,0:T(8,128)(2,1)S(1)}, u32[]{:S(2)}, u32[]{:S(2)}) collective-permute-start(bf16[256,512]{1,0:T(8,128)(2,1)S(1)} %collective-permute-done.4.refs_4_), channel_id=1, source_target_pairs={{0,1},{1,2},{2,3},{3,0},{4,5},{5,6},{6,7},{7,4},{8,9},{9,10},{10,1... | collective-permute-start | bytes 786440 | tf_op jit(solution)/shard_map/ppermute | solution.py:651
  20.6 14.8 %collective-permute-start.2 = (bf16[256,512]{1,0:T(8,128)(2,1)S(1)}, bf16[256,512]{1,0:T(8,128)(2,1)S(1)}, u32[]{:S(2)}, u32[]{:S(2)}) collective-permute-start(bf16[256,512]{1,0:T(8,128)(2,1)S(1)} %collective-permute-done.1.refs_1_), channel_id=1, source_target_pairs={{0,1},{1,2},{2,3},{3,0},{4,5},{5,6},{6,7},{7,4},{8,9},{9,10},{10,1... | collective-permute-start | bytes 786440 | tf_op jit(solution)/shard_map/ppermute | solution.py:651
  29.7 11.2 %collective-permute-start.6 = (bf16[256,512]{1,0:T(8,128)(2,1)S(1)}, bf16[256,512]{1,0:T(8,128)(2,1)S(1)}, u32[]{:S(2)}, u32[]{:S(2)}) collective-permute-start(bf16[256,512]{1,0:T(8,128)(2,1)S(1)} %collective-permute-done.5.refs_5_), channel_id=1, source_target_pairs={{0,1},{1,2},{2,3},{3,0},{4,5},{5,6},{6,7},{7,4},{8,9},{9,10},{10,1... | collective-permute-start | bytes 786440 | tf_op jit(solution)/shard_map/ppermute | solution.py:651
  35.4 11.2 %collective-permute-start.3 = (bf16[256,512]{1,0:T(8,128)(2,1)S(1)}, bf16[256,512]{1,0:T(8,128)(2,1)S(1)}, u32[]{:S(2)}, u32[]{:S(2)}) collective-permute-start(bf16[256,512]{1,0:T(8,128)(2,1)S(1)} %collective-permute-done.2.refs_2_), channel_id=1, source_target_pairs={{0,1},{1,2},{2,3},{3,0},{4,5},{5,6},{6,7},{7,4},{8,9},{9,10},{10,1... | collective-permute-start | bytes 786440 | tf_op jit(solution)/shard_map/ppermute | solution.py:651
  41.0 10.5 %collective-permute-start.7 = (bf16[256,512]{1,0:T(8,128)(2,1)S(1)}, bf16[256,512]{1,0:T(8,128)(2,1)S(1)}, u32[]{:S(2)}, u32[]{:S(2)}) collective-permute-start(bf16[256,512]{1,0:T(8,128)(2,1)S(1)} %collective-permute-done.6.refs_6_), channel_id=1, source_target_pairs={{0,1},{1,2},{2,3},{3,0},{4,5},{5,6},{6,7},{7,4},{8,9},{9,10},{10,1... | collective-permute-start | bytes 786440 | tf_op jit(solution)/shard_map/ppermute | solution.py:651
  56.8 9.2 %collective-permute-start.12 = (bf16[2,512,128]{2,1,0:T(8,128)(2,1)S(1)}, bf16[2,512,128]{2,1,0:T(8,128)(2,1)S(1)}, u32[]{:S(2)}, u32[]{:S(2)}) collective-permute-start(bf16[2,512,128]{2,1,0:T(8,128)(2,1)S(1)} %get-tuple-element.64), channel_id=1, source_target_pairs={{0,8},{4,12},{8,0},{12,4},{16,24},{20,28},{24,16},{28,20},{1,9},{5... | collective-permute-start | bytes 786440 | tf_op jit(solution)/shard_map/ppermute | solution.py:673
  58.2 17.3 %collective-permute-start.13 = (bf16[2,512,128]{2,1,0:T(8,128)(2,1)}, bf16[2,512,128]{2,1,0:T(8,128)(2,1)S(1)}, u32[]{:S(2)}, u32[]{:S(2)}) collective-permute-start(bf16[2,512,128]{2,1,0:T(8,128)(2,1)} %get-tuple-element.65), channel_id=1, source_target_pairs={{0,16},{4,20},{8,24},{12,28},{16,0},{20,4},{24,8},{28,12},{1,17},{... | collective-permute-start | bytes 786440 | tf_op jit(solution)/shard_map/ppermute | solution.py:673
  59.8 15.8 %collective-permute-start.14 = (bf16[2,512,128]{2,1,0:T(8,128)(2,1)S(1)}, bf16[2,512,128]{2,1,0:T(8,128)(2,1)S(1)}, u32[]{:S(2)}, u32[]{:S(2)}) collective-permute-start(bf16[2,512,128]{2,1,0:T(8,128)(2,1)S(1)} %get-tuple-element.66), channel_id=1, source_target_pairs={{0,24},{4,28},{8,16},{12,20},{16,8},{20,12},{24,0},{28,4},{1,25},{... | collective-permute-start | bytes 786440 | tf_op jit(solution)/shard_map/ppermute | solution.py:673
  63.0 14.0 %collective-permute-start.10 = (bf16[512,128]{1,0:T(8,128)(2,1)S(1)}, bf16[512,128]{1,0:T(8,128)(2,1)S(1)}, u32[]{:S(2)}, u32[]{:S(2)}) collective-permute-start(bf16[512,128]{1,0:T(8,128)(2,1)S(1)} %get-tuple-element.61), channel_id=1, source_target_pairs={{0,16},{4,20},{8,24},{12,28},{16,0},{20,4},{24,8},{28,12},{1,17},{... | collective-permute-start | bytes 393224 | tf_op jit(solution)/shard_map/ppermute | solution.py:673
  64.5 12.5 %collective-permute-start.11 = (bf16[512,128]{1,0:T(8,128)(2,1)}, bf16[512,128]{1,0:T(8,128)(2,1)}, u32[]{:S(2)}, u32[]{:S(2)}) collective-permute-start(bf16[512,128]{1,0:T(8,128)(2,1)} %get-tuple-element.62), channel_id=1, source_target_pairs={{0,24},{4,28},{8,16},{12,20},{16,8},{20,12},{24,0},{28,4},{1,25},{... | collective-permute-start | bytes 393224 | tf_op jit(solution)/shard_map/ppermute | solution.py:673
  66.0 11.5 %collective-permute-start.9 = (bf16[512,128]{1,0:T(8,128)(2,1)}, bf16[512,128]{1,0:T(8,128)(2,1)}, u32[]{:S(2)}, u32[]{:S(2)}) collective-permute-start(bf16[512,128]{1,0:T(8,128)(2,1)} %get-tuple-element.60), channel_id=1, source_target_pairs={{0,8},{4,12},{8,0},{12,4},{16,24},{20,28},{24,16},{28,20},{1,9},{5... | collective-permute-start | bytes 393224 | tf_op jit(solution)/shard_map/ppermute | solution.py:673
  75.6 10.5 %collective-permute-start.21 = (bf16[512,256]{1,0:T(8,128)(2,1)S(1)}, bf16[512,256]{1,0:T(8,128)(2,1)S(1)}, u32[]{:S(2)}, u32[]{:S(2)}) collective-permute-start(bf16[512,256]{1,0:T(8,128)(2,1)S(1)} %constant_dynamic-slice_fusion), channel_id=1, source_target_pairs={{0,1},{1,2},{2,3},{3,0},{4,5},{5,6},{6,7},{7,4},{8,9},{9,10},{10,1... | collective-permute-start | bytes 786440 | tf_op jit(solution)/shard_map/ppermute | solution.py:664
  75.6 10.5 %collective-permute-start.15 = (bf16[2,512,128]{2,1,0:T(8,128)(2,1)S(1)}, bf16[2,512,128]{2,1,0:T(8,128)(2,1)S(1)}, u32[]{:S(2)}, u32[]{:S(2)}) collective-permute-start(bf16[2,512,128]{2,1,0:T(8,128)(2,1)S(1)} %get-tuple-element.67), channel_id=1, source_target_pairs={{0,4},{4,0},{8,12},{12,8},{16,20},{20,16},{24,28},{28,24},{1,5},{5... | collective-permute-start | bytes 786440 | tf_op jit(solution)/shard_map/ppermute | solution.py:681
  77.0 9.1 %collective-permute-start.16 = (bf16[2,512,128]{2,1,0:T(8,128)(2,1)S(1)}, bf16[2,512,128]{2,1,0:T(8,128)(2,1)S(1)}, u32[]{:S(2)}, u32[]{:S(2)}) collective-permute-start(bf16[2,512,128]{2,1,0:T(8,128)(2,1)S(1)} %collective-permute-done.12), channel_id=1, source_target_pairs={{0,4},{4,0},{8,12},{12,8},{16,20},{20,16},{24,28},{28,24},{1,5},{5... | collective-permute-start | bytes 786440 | tf_op jit(solution)/shard_map/ppermute | solution.py:681
  77.0 9.1 %collective-permute-start.17 = (bf16[2,512,128]{2,1,0:T(8,128)(2,1)S(1)}, bf16[2,512,128]{2,1,0:T(8,128)(2,1)S(1)}, u32[]{:S(2)}, u32[]{:S(2)}) collective-permute-start(bf16[2,512,128]{2,1,0:T(8,128)(2,1)S(1)} %collective-permute-done.13), channel_id=1, source_target_pairs={{0,4},{4,0},{8,12},{12,8},{16,20},{20,16},{24,28},{28,24},{1,5},{5... | collective-permute-start | bytes 786440 | tf_op jit(solution)/shard_map/ppermute | solution.py:681
  77.5 8.6 %collective-permute-start.18 = (bf16[2,512,128]{2,1,0:T(8,128)(2,1)S(1)}, bf16[2,512,128]{2,1,0:T(8,128)(2,1)S(1)}, u32[]{:S(2)}, u32[]{:S(2)}) collective-permute-start(bf16[2,512,128]{2,1,0:T(8,128)(2,1)S(1)} %collective-permute-done.14), channel_id=1, source_target_pairs={{0,4},{4,0},{8,12},{12,8},{16,20},{20,16},{24,28},{28,24},{1,5},{5... | collective-permute-start | bytes 786440 | tf_op jit(solution)/shard_map/ppermute | solution.py:681
  86.0 16.1 %collective-permute-start.19 = (bf16[512,256]{1,0:T(8,128)(2,1)S(1)}, bf16[512,256]{1,0:T(8,128)(2,1)S(1)}, u32[]{:S(2)}, u32[]{:S(2)}) collective-permute-start(bf16[512,256]{1,0:T(8,128)(2,1)S(1)} %constant_dynamic-slice_fusion), channel_id=1, source_target_pairs={{0,2},{1,3},{2,0},{3,1},{4,6},{5,7},{6,4},{7,5},{8,10},{9,11},{10,... | collective-permute-start | bytes 786440 | tf_op jit(solution)/shard_map/ppermute | solution.py:664
  86.1 16.1 %collective-permute-start.20 = (bf16[512,256]{1,0:T(8,128)(2,1)S(1)}, bf16[512,256]{1,0:T(8,128)(2,1)S(1)}, u32[]{:S(2)}, u32[]{:S(2)}) collective-permute-start(bf16[512,256]{1,0:T(8,128)(2,1)S(1)} %constant_dynamic-slice_fusion), channel_id=1, source_target_pairs={{0,3},{1,0},{2,1},{3,2},{4,7},{5,4},{6,5},{7,6},{8,11},{9,8},{10,9... | collective-permute-start | bytes 786440 | tf_op jit(solution)/shard_map/ppermute | solution.py:664
  86.1 16.1 %collective-permute-start.22 = (bf16[512,256]{1,0:T(8,128)(2,1)S(1)}, bf16[512,256]{1,0:T(8,128)(2,1)S(1)}, u32[]{:S(2)}, u32[]{:S(2)}) collective-permute-start(bf16[512,256]{1,0:T(8,128)(2,1)S(1)} %collective-permute-done.21), channel_id=1, source_target_pairs={{0,8},{4,12},{8,0},{12,4},{16,24},{20,28},{24,16},{28,20},{1,9},{5... | collective-permute-start | bytes 786440 | tf_op jit(solution)/shard_map/ppermute | solution.py:673
  86.2 16.0 %collective-permute-start.23 = (bf16[512,256]{1,0:T(8,128)(2,1)S(1)}, bf16[512,256]{1,0:T(8,128)(2,1)S(1)}, u32[]{:S(2)}, u32[]{:S(2)}) collective-permute-start(bf16[512,256]{1,0:T(8,128)(2,1)S(1)} %collective-permute-done.21), channel_id=1, source_target_pairs={{0,16},{4,20},{8,24},{12,28},{16,0},{20,4},{24,8},{28,12},{1,17},{... | collective-permute-start | bytes 786440 | tf_op jit(solution)/shard_map/ppermute | solution.py:673
  88.2 14.0 %collective-permute-start.24 = (bf16[512,256]{1,0:T(8,128)(2,1)S(1)}, bf16[512,256]{1,0:T(8,128)(2,1)S(1)}, u32[]{:S(2)}, u32[]{:S(2)}) collective-permute-start(bf16[512,256]{1,0:T(8,128)(2,1)S(1)} %collective-permute-done.21), channel_id=1, source_target_pairs={{0,24},{4,28},{8,16},{12,20},{16,8},{20,12},{24,0},{28,4},{1,25},{... | collective-permute-start | bytes 786440 | tf_op jit(solution)/shard_map/ppermute | solution.py:673
  102.2 5.9 %collective-permute-start.25 = (bf16[2,256,128]{2,1,0:T(8,128)(2,1)S(1)}, bf16[2,256,128]{2,1,0:T(8,128)(2,1)S(1)}, u32[]{:S(2)}, u32[]{:S(2)}) collective-permute-start(bf16[2,256,128]{2,1,0:T(8,128)(2,1)S(1)} %get-tuple-element.78), channel_id=1, source_target_pairs={{0,8},{4,12},{8,0},{12,4},{16,24},{20,28},{24,16},{28,20},{1,9},{5... | collective-permute-start | bytes 393224 | tf_op jit(solution)/shard_map/ppermute | solution.py:673
  108.2 20.3 %collective-permute-start.26 = (bf16[2,2,256,128]{3,2,1,0:T(8,128)(2,1)S(1)}, bf16[2,2,256,128]{3,2,1,0:T(8,128)(2,1)S(1)}, u32[]{:S(2)}, u32[]{:S(2)}) collective-permute-start(bf16[2,2,256,128]{3,2,1,0:T(8,128)(2,1)S(1)} %pad_maximum_fusion.5.refs_0_), channel_id=1, source_target_pairs={{0,1},{1,2},{2,3},{3,0},{4,5},{5,6},{6,7},{7,4},{8,9},{9,10},{10,1... | collective-permute-start | bytes 786440 | tf_op jit(solution)/shard_map/ppermute | solution.py:651
  109.7 6.7 %collective-permute-start.29 = (bf16[2,256,128]{2,1,0:T(8,128)(2,1)S(1)}, bf16[2,256,128]{2,1,0:T(8,128)(2,1)S(1)}, u32[]{:S(2)}, u32[]{:S(2)}) collective-permute-start(bf16[2,256,128]{2,1,0:T(8,128)(2,1)S(1)} %get-tuple-element.79), channel_id=1, source_target_pairs={{0,16},{4,20},{8,24},{12,28},{16,0},{20,4},{24,8},{28,12},{1,17},{... | collective-permute-start | bytes 393224 | tf_op jit(solution)/shard_map/ppermute | solution.py:673
  111.1 7.3 %collective-permute-start.30 = (bf16[2,256,128]{2,1,0:T(8,128)(2,1)S(1)}, bf16[2,256,128]{2,1,0:T(8,128)(2,1)S(1)}, u32[]{:S(2)}, u32[]{:S(2)}) collective-permute-start(bf16[2,256,128]{2,1,0:T(8,128)(2,1)S(1)} %get-tuple-element.80), channel_id=1, source_target_pairs={{0,24},{4,28},{8,16},{12,20},{16,8},{20,12},{24,0},{28,4},{1,25},{... | collective-permute-start | bytes 393224 | tf_op jit(solution)/shard_map/ppermute | solution.py:673
  118.5 21.0 %collective-permute-start.34 = (bf16[2,512,256]{2,1,0:T(8,128)(2,1)S(1)}, bf16[2,512,256]{2,1,0:T(8,128)(2,1)S(1)}, u32[]{:S(2)}, u32[]{:S(2)}) collective-permute-start(bf16[2,512,256]{2,1,0:T(8,128)(2,1)S(1)} %pad_maximum_fusion.2), channel_id=1, source_target_pairs={{0,8},{4,12},{8,0},{12,4},{16,24},{20,28},{24,16},{28,20},{1,9},{5... | collective-permute-start | bytes 1572872 | tf_op jit(solution)/shard_map/ppermute | solution.py:673
  119.0 11.0 %collective-permute-start.31 = (bf16[2,2,256,128]{3,2,1,0:T(8,128)(2,1)S(1)}, bf16[2,2,256,128]{3,2,1,0:T(8,128)(2,1)S(1)}, u32[]{:S(2)}, u32[]{:S(2)}) collective-permute-start(bf16[2,2,256,128]{3,2,1,0:T(8,128)(2,1)S(1)} %pad_maximum_fusion.6.refs_4_), channel_id=1, source_target_pairs={{0,1},{1,2},{2,3},{3,0},{4,5},{5,6},{6,7},{7,4},{8,9},{9,10},{10,1... | collective-permute-start | bytes 786440 | tf_op jit(solution)/shard_map/ppermute | solution.py:651
  125.0 14.8 %collective-permute-start.35 = (bf16[2,512,256]{2,1,0:T(8,128)(2,1)S(1)}, bf16[2,512,256]{2,1,0:T(8,128)(2,1)S(1)}, u32[]{:S(2)}, u32[]{:S(2)}) collective-permute-start(bf16[2,512,256]{2,1,0:T(8,128)(2,1)S(1)} %pad_maximum_fusion.2), channel_id=1, source_target_pairs={{0,16},{4,20},{8,24},{12,28},{16,0},{20,4},{24,8},{28,12},{1,17},{... | collective-permute-start | bytes 1572872 | tf_op jit(solution)/shard_map/ppermute | solution.py:673
  127.0 12.8 %collective-permute-start.36 = (bf16[2,512,256]{2,1,0:T(8,128)(2,1)S(1)}, bf16[2,512,256]{2,1,0:T(8,128)(2,1)S(1)}, u32[]{:S(2)}, u32[]{:S(2)}) collective-permute-start(bf16[2,512,256]{2,1,0:T(8,128)(2,1)S(1)} %pad_maximum_fusion.2), channel_id=1, source_target_pairs={{0,24},{4,28},{8,16},{12,20},{16,8},{20,12},{24,0},{28,4},{1,25},{... | collective-permute-start | bytes 1572872 | tf_op jit(solution)/shard_map/ppermute | solution.py:673
  128.4 8.2 %collective-permute-start.27 = (bf16[2,2,256,128]{3,2,1,0:T(8,128)(2,1)S(1)}, bf16[2,2,256,128]{3,2,1,0:T(8,128)(2,1)S(1)}, u32[]{:S(2)}, u32[]{:S(2)}) collective-permute-start(bf16[2,2,256,128]{3,2,1,0:T(8,128)(2,1)S(1)} %collective-permute-done.26.refs_1_), channel_id=1, source_target_pairs={{0,1},{1,2},{2,3},{3,0},{4,5},{5,6},{6,7},{7,4},{8,9},{9,10},{10,1... | collective-permute-start | bytes 786440 | tf_op jit(solution)/shard_map/ppermute | solution.py:651
  130.1 9.5 %collective-permute-start.32 = (bf16[2,2,256,128]{3,2,1,0:T(8,128)(2,1)S(1)}, bf16[2,2,256,128]{3,2,1,0:T(8,128)(2,1)}, u32[]{:S(2)}, u32[]{:S(2)}) collective-permute-start(bf16[2,2,256,128]{3,2,1,0:T(8,128)(2,1)S(1)} %collective-permute-done.31.refs_5_), channel_id=1, source_target_pairs={{0,1},{1,2},{2,3},{3,0},{4,5},{5,6},{6,7},{7,4},{8,9},{9,10},{10,1... | collective-permute-start | bytes 786440 | tf_op jit(solution)/shard_map/ppermute | solution.py:651
  136.6 8.2 %collective-permute-start.28 = (bf16[2,2,256,128]{3,2,1,0:T(8,128)(2,1)S(1)}, bf16[2,2,256,128]{3,2,1,0:T(8,128)(2,1)S(1)}, u32[]{:S(2)}, u32[]{:S(2)}) collective-permute-start(bf16[2,2,256,128]{3,2,1,0:T(8,128)(2,1)S(1)} %collective-permute-done.27.refs_2_), channel_id=1, source_target_pairs={{0,1},{1,2},{2,3},{3,0},{4,5},{5,6},{6,7},{7,4},{8,9},{9,10},{10,1... | collective-permute-start | bytes 786440 | tf_op jit(solution)/shard_map/ppermute | solution.py:651
  146.4 12.1 %collective-permute-start.38 = (bf16[4,2,512,256]{3,2,1,0:T(8,128)(2,1)}, bf16[4,2,512,256]{3,2,1,0:T(8,128)(2,1)}, u32[]{:S(2)}, u32[]{:S(2)}) collective-permute-start(bf16[4,2,512,256]{3,2,1,0:T(8,128)(2,1)} %pad_maximum_fusion.refs_11_), channel_id=1, source_target_pairs={{0,4},{4,0},{8,12},{12,8},{16,20},{20,16},{24,28},{28,24},{1,5},{5... | collective-permute-start | bytes 6291464 | tf_op jit(solution)/shard_map/ppermute | solution.py:681
  147.6 10.8 %collective-permute-start.37 = (bf16[4,1,512,256]{3,2,0,1:T(8,128)(2,1)}, bf16[4,1,512,256]{3,2,0,1:T(8,128)(2,1)}, u32[]{:S(2)}, u32[]{:S(2)}) collective-permute-start(bf16[4,1,512,256]{3,2,0,1:T(8,128)(2,1)} %get-tuple-element.89), channel_id=1, source_target_pairs={{0,4},{4,0},{8,12},{12,8},{16,20},{20,16},{24,28},{28,24},{1,5},{5... | collective-permute-start | bytes 3145736 | tf_op jit(solution)/shard_map/ppermute | solution.py:681
  148.1 10.3 %collective-permute-start.33 = (bf16[2,2,256,128]{3,2,1,0:T(8,128)(2,1)}, bf16[2,2,256,128]{3,2,1,0:T(8,128)(2,1)}, u32[]{:S(2)}, u32[]{:S(2)}) collective-permute-start(bf16[2,2,256,128]{3,2,1,0:T(8,128)(2,1)} %collective-permute-done.32.refs_6_), channel_id=1, source_target_pairs={{0,1},{1,2},{2,3},{3,0},{4,5},{5,6},{6,7},{7,4},{8,9},{9,10},{10,1... | collective-permute-start | bytes 786440 | tf_op jit(solution)/shard_map/ppermute | solution.py:651
  158.4 43.4 %slice-start = ((s8[8388608]{0:T(1024)(128)(4,1)}), s8[4194304]{0:T(1024)(128)(4,1)S(1)}, s32[]{:S(2)}) async-start(s8[8388608]{0:T(1024)(128)(4,1)} %bitcast.74), calls=%async_computation | async-start | bytes 8388608
  161.7 26.8 %copy-start.37 = (bf16[256,512]{1,0:T(8,128)(2,1)S(1)}, bf16[256,512]{1,0:T(8,128)(2,1)}, u32[]{:S(2)}) copy-start(bf16[256,512]{1,0:T(8,128)(2,1)} %copy-done.36) | copy-start | bytes 786436
  161.7 40.1 %slice-start.1 = ((s8[8388608]{0:T(1024)(128)(4,1)}), s8[4194304]{0:T(1024)(128)(4,1)S(1)}, s32[]{:S(2)}) async-start(s8[8388608]{0:T(1024)(128)(4,1)} %bitcast.74), calls=%async_computation.1 | async-start | bytes 8388608
  184.6 8.3 %collective-permute-start.39 = (bf16[128,512]{1,0:T(8,128)(2,1)S(1)}, bf16[128,512]{1,0:T(8,128)(2,1)S(1)}, u32[]{:S(2)}, u32[]{:S(2)}) collective-permute-start(bf16[128,512]{1,0:T(8,128)(2,1)S(1)} %get-tuple-element.94), channel_id=1, source_target_pairs={{0,1},{1,2},{2,3},{3,0},{4,5},{5,6},{6,7},{7,4},{8,9},{9,10},{10,1... | collective-permute-start | bytes 393224 | tf_op jit(solution)/shard_map/ppermute | solution.py:664
  184.7 12.1 %collective-permute-start.40 = (bf16[128,512]{1,0:T(8,128)(2,1)S(1)}, bf16[128,512]{1,0:T(8,128)(2,1)S(1)}, u32[]{:S(2)}, u32[]{:S(2)}) collective-permute-start(bf16[128,512]{1,0:T(8,128)(2,1)S(1)} %get-tuple-element.95), channel_id=1, source_target_pairs={{0,2},{1,3},{2,0},{3,1},{4,6},{5,7},{6,4},{7,5},{8,10},{9,11},{10,... | collective-permute-start | bytes 393224 | tf_op jit(solution)/shard_map/ppermute | solution.py:664
  184.8 12.0 %collective-permute-start.41 = (bf16[128,512]{1,0:T(8,128)(2,1)S(1)}, bf16[128,512]{1,0:T(8,128)(2,1)S(1)}, u32[]{:S(2)}, u32[]{:S(2)}) collective-permute-start(bf16[128,512]{1,0:T(8,128)(2,1)S(1)} %get-tuple-element.96), channel_id=1, source_target_pairs={{0,3},{1,0},{2,1},{3,2},{4,7},{5,4},{6,5},{7,6},{8,11},{9,8},{10,9... | collective-permute-start | bytes 393224 | tf_op jit(solution)/shard_map/ppermute | solution.py:664
  196.9 10.7 %collective-permute-start.42 = (bf16[128,512]{1,0:T(8,128)(2,1)S(1)}, bf16[128,512]{1,0:T(8,128)(2,1)S(1)}, u32[]{:S(2)}, u32[]{:S(2)}) collective-permute-start(bf16[128,512]{1,0:T(8,128)(2,1)S(1)} %multiply_convert_fusion.2.refs_0_), channel_id=1, source_target_pairs={{0,1},{1,2},{2,3},{3,0},{4,5},{5,6},{6,7},{7,4},{8,9},{9,10},{10,1... | collective-permute-start | bytes 393224 | tf_op jit(solution)/shard_map/ppermute | solution.py:664
  199.4 9.4 %collective-permute-start.43 = (bf16[128,512]{1,0:T(8,128)(2,1)S(1)}, bf16[128,512]{1,0:T(8,128)(2,1)S(1)}, u32[]{:S(2)}, u32[]{:S(2)}) collective-permute-start(bf16[128,512]{1,0:T(8,128)(2,1)S(1)} %multiply_convert_fusion.2.refs_0_), channel_id=1, source_target_pairs={{0,2},{1,3},{2,0},{3,1},{4,6},{5,7},{6,4},{7,5},{8,10},{9,11},{10,... | collective-permute-start | bytes 393224 | tf_op jit(solution)/shard_map/ppermute | solution.py:664
  199.5 9.3 %collective-permute-start.44 = (bf16[128,512]{1,0:T(8,128)(2,1)S(1)}, bf16[128,512]{1,0:T(8,128)(2,1)S(1)}, u32[]{:S(2)}, u32[]{:S(2)}) collective-permute-start(bf16[128,512]{1,0:T(8,128)(2,1)S(1)} %multiply_convert_fusion.2.refs_0_), channel_id=1, source_target_pairs={{0,3},{1,0},{2,1},{3,2},{4,7},{5,4},{6,5},{7,6},{8,11},{9,8},{10,9... | collective-permute-start | bytes 393224 | tf_op jit(solution)/shard_map/ppermute | solution.py:664
  210.2 15.7 %collective-permute-start.45 = (bf16[512,512]{1,0:T(8,128)(2,1)}, bf16[512,512]{1,0:T(8,128)(2,1)}, u32[]{:S(2)}, u32[]{:S(2)}) collective-permute-start(bf16[512,512]{1,0:T(8,128)(2,1)} %slice_bitcast_fusion), channel_id=1, source_target_pairs={{0,1},{1,2},{2,3},{3,0},{4,5},{5,6},{6,7},{7,4},{8,9},{9,10},{10,1... | collective-permute-start | bytes 1572872 | tf_op jit(solution)/shard_map/ppermute | solution.py:651
  220.1 8.7 %collective-permute-start.48 = (bf16[4,208,512]{2,1,0:T(8,128)(2,1)S(1)}, bf16[4,208,512]{2,1,0:T(8,128)(2,1)S(1)}, u32[]{:S(2)}, u32[]{:S(2)}) collective-permute-start(bf16[4,208,512]{2,1,0:T(8,128)(2,1)S(1)} %get-tuple-element.99), channel_id=1, source_target_pairs={{0,4},{4,0},{8,12},{12,8},{16,20},{20,16},{24,28},{28,24},{1,5},{5... | collective-permute-start | bytes 2555912 | tf_op jit(solution)/shard_map/ppermute | solution.py:681
  227.1 14.1 %collective-permute-start.46 = (bf16[512,512]{1,0:T(8,128)(2,1)S(1)}, bf16[512,512]{1,0:T(8,128)(2,1)S(1)}, u32[]{:S(2)}, u32[]{:S(2)}) collective-permute-start(bf16[512,512]{1,0:T(8,128)(2,1)S(1)} %fusion.1), channel_id=1, source_target_pairs={{0,1},{1,2},{2,3},{3,0},{4,5},{5,6},{6,7},{7,4},{8,9},{9,10},{10,1... | collective-permute-start | bytes 1572872 | tf_op jit(solution)/shard_map/ppermute | solution.py:651
  228.9 12.9 %collective-permute-start.49 = (bf16[208,512]{1,0:T(8,128)(2,1)S(1)}, bf16[208,512]{1,0:T(8,128)(2,1)S(1)}, u32[]{:S(2)}, u32[]{:S(2)}) collective-permute-start(bf16[208,512]{1,0:T(8,128)(2,1)S(1)} %get-tuple-element.101), channel_id=1, source_target_pairs={{0,8},{4,12},{8,0},{12,4},{16,24},{20,28},{24,16},{28,20},{1,9},{5... | collective-permute-start | bytes 638984 | tf_op jit(solution)/shard_map/ppermute | solution.py:673
  229.1 12.7 %collective-permute-start.50 = (bf16[208,512]{1,0:T(8,128)(2,1)S(1)}, bf16[208,512]{1,0:T(8,128)(2,1)S(1)}, u32[]{:S(2)}, u32[]{:S(2)}) collective-permute-start(bf16[208,512]{1,0:T(8,128)(2,1)S(1)} %get-tuple-element.102), channel_id=1, source_target_pairs={{0,16},{4,20},{8,24},{12,28},{16,0},{20,4},{24,8},{28,12},{1,17},{... | collective-permute-start | bytes 638984 | tf_op jit(solution)/shard_map/ppermute | solution.py:673
  231.0 10.8 %collective-permute-start.51 = (bf16[208,512]{1,0:T(8,128)(2,1)S(1)}, bf16[208,512]{1,0:T(8,128)(2,1)S(1)}, u32[]{:S(2)}, u32[]{:S(2)}) collective-permute-start(bf16[208,512]{1,0:T(8,128)(2,1)S(1)} %get-tuple-element.103), channel_id=1, source_target_pairs={{0,24},{4,28},{8,16},{12,20},{16,8},{20,12},{24,0},{28,4},{1,25},{... | collective-permute-start | bytes 638984 | tf_op jit(solution)/shard_map/ppermute | solution.py:673
  241.4 13.2 %collective-permute-start.47 = (bf16[512,512]{1,0:T(8,128)(2,1)S(1)}, bf16[512,512]{1,0:T(8,128)(2,1)S(1)}, u32[]{:S(2)}, u32[]{:S(2)}) collective-permute-start(bf16[512,512]{1,0:T(8,128)(2,1)S(1)} %fusion), channel_id=1, source_target_pairs={{0,1},{1,2},{2,3},{3,0},{4,5},{5,6},{6,7},{7,4},{8,9},{9,10},{10,1... | collective-permute-start | bytes 1572872 | tf_op jit(solution)/shard_map/ppermute | solution.py:651
  242.0 7.4 %collective-permute-start.53 = (bf16[208,512]{1,0:T(8,128)(2,1)S(1)}, bf16[208,512]{1,0:T(8,128)(2,1)S(1)}, u32[]{:S(2)}, u32[]{:S(2)}) collective-permute-start(bf16[208,512]{1,0:T(8,128)(2,1)S(1)} %add_convert_fusion.1.refs_0_), channel_id=1, source_target_pairs={{0,8},{4,12},{8,0},{12,4},{16,24},{20,28},{24,16},{28,20},{1,9},{5... | collective-permute-start | bytes 638984 | tf_op jit(solution)/shard_map/ppermute | solution.py:673
  242.2 8.8 %collective-permute-start.55 = (bf16[208,512]{1,0:T(8,128)(2,1)S(1)}, bf16[208,512]{1,0:T(8,128)(2,1)S(1)}, u32[]{:S(2)}, u32[]{:S(2)}) collective-permute-start(bf16[208,512]{1,0:T(8,128)(2,1)S(1)} %add_convert_fusion.1.refs_0_), channel_id=1, source_target_pairs={{0,16},{4,20},{8,24},{12,28},{16,0},{20,4},{24,8},{28,12},{1,17},{... | collective-permute-start | bytes 638984 | tf_op jit(solution)/shard_map/ppermute | solution.py:673
  244.1 8.6 %collective-permute-start.57 = (bf16[208,512]{1,0:T(8,128)(2,1)S(1)}, bf16[208,512]{1,0:T(8,128)(2,1)S(1)}, u32[]{:S(2)}, u32[]{:S(2)}) collective-permute-start(bf16[208,512]{1,0:T(8,128)(2,1)S(1)} %add_convert_fusion.1.refs_0_), channel_id=1, source_target_pairs={{0,24},{4,28},{8,16},{12,20},{16,8},{20,12},{24,0},{28,4},{1,25},{... | collective-permute-start | bytes 638984 | tf_op jit(solution)/shard_map/ppermute | solution.py:673
  245.5 9.2 %collective-permute-start.52 = (bf16[208,512]{1,0:T(8,128)(2,1)S(1)}, bf16[208,512]{1,0:T(8,128)(2,1)S(1)}, u32[]{:S(2)}, u32[]{:S(2)}) collective-permute-start(bf16[208,512]{1,0:T(8,128)(2,1)S(1)} %add_convert_fusion.1.refs_0_), channel_id=1, source_target_pairs={{0,4},{4,0},{8,12},{12,8},{16,20},{20,16},{24,28},{28,24},{1,5},{5... | collective-permute-start | bytes 638984 | tf_op jit(solution)/shard_map/ppermute | solution.py:681
  249.3 6.1 %collective-permute-start.54 = (bf16[208,512]{1,0:T(8,128)(2,1)S(1)}, bf16[208,512]{1,0:T(8,128)(2,1)S(1)}, u32[]{:S(2)}, u32[]{:S(2)}) collective-permute-start(bf16[208,512]{1,0:T(8,128)(2,1)S(1)} %collective-permute-done.53.refs_1_), channel_id=1, source_target_pairs={{0,4},{4,0},{8,12},{12,8},{16,20},{20,16},{24,28},{28,24},{1,5},{5... | collective-permute-start | bytes 638984 | tf_op jit(solution)/shard_map/ppermute | solution.py:681
  250.9 5.2 %collective-permute-start.56 = (bf16[208,512]{1,0:T(8,128)(2,1)S(1)}, bf16[208,512]{1,0:T(8,128)(2,1)S(1)}, u32[]{:S(2)}, u32[]{:S(2)}) collective-permute-start(bf16[208,512]{1,0:T(8,128)(2,1)S(1)} %collective-permute-done.55.refs_2_), channel_id=1, source_target_pairs={{0,4},{4,0},{8,12},{12,8},{16,20},{20,16},{24,28},{28,24},{1,5},{5... | collective-permute-start | bytes 638984 | tf_op jit(solution)/shard_map/ppermute | solution.py:681
  252.6 4.2 %collective-permute-start.58 = (bf16[208,512]{1,0:T(8,128)(2,1)S(1)}, bf16[208,512]{1,0:T(8,128)(2,1)S(1)}, u32[]{:S(2)}, u32[]{:S(2)}) collective-permute-start(bf16[208,512]{1,0:T(8,128)(2,1)S(1)} %collective-permute-done.57.refs_3_), channel_id=1, source_target_pairs={{0,4},{4,0},{8,12},{12,8},{16,20},{20,16},{24,28},{28,24},{1,5},{5... | collective-permute-start | bytes 638984 | tf_op jit(solution)/shard_map/ppermute | solution.py:681
  257.8 4.5 %collective-permute-start.59 = (bf16[256,512]{1,0:T(8,128)(2,1)S(1)}, bf16[256,512]{1,0:T(8,128)(2,1)S(1)}, u32[]{:S(2)}, u32[]{:S(2)}) collective-permute-start(bf16[256,512]{1,0:T(8,128)(2,1)S(1)} %get-tuple-element.117), channel_id=1, source_target_pairs={{0,4},{4,0},{8,12},{12,8},{16,20},{20,16},{24,28},{28,24},{1,5},{5... | collective-permute-start | bytes 786440 | tf_op jit(solution)/shard_map/ppermute | solution.py:681
  (38 other events, 322.0 us)

commit v3 on v2

--- a/solution.py
+++ b/solution.py
@@ -184,111 +184,82 @@
     )
 
 
-def rotate(head, cos_ref, sin_ref):
-    return head * cos_ref[...] + pltpu.roll(head, HD // 2, 1) * sin_ref[...]
-
-
-def kv_kernel(info_ref, *refs, ring, heads):
+def qkv_kernel(info_ref, *refs, ring, heads, factor):
     blocks = [refs[:ring], refs[ring : 2 * ring]]
-    gain_ref, cos_ref, sin_ref, wk_ref, wv_ref = refs[2 * ring : 2 * ring + 5]
-    outs = refs[2 * ring + 5 : 2 * ring + 5 + heads]
-    tok_ref, normed, made = refs[2 * ring + 5 + heads :]
-    step = pl.program_id(0)
+    gain_ref, cos_ref, sin_ref, *sources = refs[2 * ring : 2 * ring + 6]
+    outs = refs[2 * ring + 6 : 2 * ring + 6 + heads]
+    tok_ref, stamp_ref, normed, made, weights, sems = refs[2 * ring + 6 + heads :]
     half, width = blocks[0][0].shape
     depth = gain_ref.shape[1]
-
-    @pl.when(step == 0)
-    def _():
-        for k in range(2):
-            mine = slice(k * half, (k + 1) * half)
-            total = jnp.zeros((half, 1), F32)
-            for block in blocks[k]:
-                part = block[...].astype(F32)
-                total += jnp.sum(part * part, axis=1, keepdims=True)
-            scale = lax.rsqrt(total / depth + 1e-05)
-            for s, block in enumerate(blocks[k]):
-                at = pl.ds(pl.multiple_of(info_ref[s] * width, 128), width)
-                part = block[...]
-                tok_ref[mine, at] = part
-                normed[mine, at] = (part.astype(F32) * scale * gain_ref[:, at]).astype(BF16)
-        result = dot(normed[...], wk_ref[...])
+    copies = [
+        pltpu.make_async_copy(source, weights.at[k], sems.at[k])
+        for k, source in enumerate(sources)
+    ]
+    for copy in copies:
+        copy.start()
+    for k in range(2):
+        mine = slice(k * half, (k + 1) * half)
+        total = jnp.zeros((half, 1), F32)
+        for block in blocks[k]:
+            part = block[...].astype(F32)
+            total += jnp.sum(part * part, axis=1, keepdims=True)
+        scale = lax.rsqrt(total / depth + 1e-05)
+        for s, block in enumerate(blocks[k]):
+            at = pl.ds(pl.multiple_of(info_ref[s] * width, 128), width)
+            part = block[...]
+            tok_ref[mine, at] = part
+            normed[mine, at] = (part.astype(F32) * scale * gain_ref[:, at]).astype(BF16)
+    for kind, copy in enumerate(copies):
+        copy.wait()
+        result = dot(normed[...], weights[kind])
         for h in range(heads):
-            head = rotate(result[:, h * HD : (h + 1) * HD], cos_ref, sin_ref)
-            made[h, 0] = head.astype(BF16)
-
-    @pl.when(step == 1)
-    def _():
-        result = dot(normed[...], wv_ref[...])
-        for h in range(heads):
-            made[h, 1] = result[:, h * HD : (h + 1) * HD].astype(BF16)
-        for f in range(heads):
-            outs[f][...] = made[info_ref[ring] ^ f]
-
-
-def kv_call(info, blocks, gain, cosine, sine, w_key, w_value):
+            head = result[:, h * HD : (h + 1) * HD]
+            if kind < 2:
+                head = head * cos_ref[...] + pltpu.roll(head, HD // 2, 1) * sin_ref[...]
+            if kind == 0:
+                head = head * factor
+            made[h, kind] = head.astype(BF16)
+    for f in range(heads):
+        outs[f][...] = made[info_ref[ring] ^ f]
+    stamp_ref[...] = jnp.zeros_like(stamp_ref)
+
+
+def qkv_call(info, blocks, gain, cosine, sine, *weights):
     half, width = blocks[0][0].shape
     rows, ring = 2 * half, len(blocks[0])
-    depth, out_cols = w_key.shape
+    depth, out_cols = weights[0].shape
     heads = out_cols // HD
     result = pl.pallas_call(
-        functools.partial(kv_kernel, ring=ring, heads=heads),
-        out_shape=[jax.ShapeDtypeStruct((2, rows, HD), BF16)] * heads
-        + [jax.ShapeDtypeStruct((rows, depth), BF16)] * 2,
-        grid_spec=pltpu.PrefetchScalarGridSpec(
-            num_scalar_prefetch=1,
-            grid=(2,),
-            in_specs=[whole((half, width))] * (2 * ring)
-            + [whole((1, depth)), whole((rows, HD)), whole((rows, HD))]
-            + [whole((depth, out_cols))] * 2,
-            out_specs=[whole((2, rows, HD))] * heads + [whole((rows, depth))] * 2,
-            scratch_shapes=[pltpu.VMEM((heads, 2, rows, HD), BF16)],
-        ),
-        compiler_params=params(36),
-        cost_estimate=cost(4 * rows * depth * out_cols, 4 * depth * out_cols),
-        name="keys_values",
-    )(info, *blocks[0], *blocks[1], gain, cosine, sine, w_key, w_value)
-    return result[:heads], result[heads], result[heads + 1]
-
-
-def query_kernel(info_ref, normed_ref, cos_ref, sin_ref, wq_ref, *refs, heads):
-    outs, made = refs[:heads], refs[heads]
-    result = dot(normed_ref[...], wq_ref[...])
-    for h in range(heads):
-        head = rotate(result[:, h * HD : (h + 1) * HD], cos_ref, sin_ref)
-        made[h] = head.astype(BF16)
-    for f in range(heads):
-        outs[f][...] = made[info_ref[info_ref.shape[0] - 1] ^ f]
-
-
-def query_call(info, normed, cosine, sine, w_query):
-    rows, depth = normed.shape
-    out_cols = w_query.shape[1]
-    heads = out_cols // HD
-    return pl.pallas_call(
-        functools.partial(query_kernel, heads=heads),
-        out_shape=[jax.ShapeDtypeStruct((rows, HD), BF16)] * heads,
+        functools.partial(
+            qkv_kernel, ring=ring, heads=heads, factor=HD ** (-0.5) * math.log2(math.e)
+        ),
+        out_shape=[jax.ShapeDtypeStruct((3, rows, HD), BF16)] * heads
+        + [jax.ShapeDtypeStruct((rows, depth), BF16), jax.ShapeDtypeStruct((8, HD), F32)],
         grid_spec=pltpu.PrefetchScalarGridSpec(
             num_scalar_prefetch=1,
             grid=(1,),
-            in_specs=[
-                whole((rows, depth)),
-                whole((rows, HD)),
-                whole((rows, HD)),
-                whole((depth, out_cols)),
+            in_specs=[whole((half, width))] * (2 * ring)
+            + [whole((1, depth)), whole((rows, HD)), whole((rows, HD))]
+            + [pl.BlockSpec(memory_space=pl.ANY)] * 3,
+            out_specs=[whole((3, rows, HD))] * heads + [whole((rows, depth)), whole((8, HD))],
+            scratch_shapes=[
+                pltpu.VMEM((rows, depth), BF16),
+                pltpu.VMEM((heads, 3, rows, HD), BF16),
+                pltpu.VMEM((3, depth, out_cols), BF16),
+                pltpu.SemaphoreType.DMA((3,)),
             ],
-            out_specs=[whole((rows, HD))] * heads,
-            scratch_shapes=[pltpu.VMEM((heads, rows, HD), BF16)],
-        ),
-        compiler_params=params(24),
-        cost_estimate=cost(2 * rows * depth * out_cols, 2 * depth * out_cols),
-        name="queries",
-    )(info, normed, cosine, sine, w_query)
+        ),
+        compiler_params=params(42),
+        cost_estimate=cost(6 * rows * depth * out_cols, 6 * depth * out_cols),
+        name="qkv",
+    )(info, *blocks[0], *blocks[1], gain, cosine, sine, *weights)
+    return result[:heads], result[heads], result[heads + 1]
 
 
 def attention_kernel(info_ref, *refs, chips):
-    queries, own, other = refs[:chips], refs[chips : 2 * chips], refs[2 * chips : 3 * chips]
-    outs = refs[3 * chips : 4 * chips]
-    keys_all, values_all = refs[4 * chips :]
+    own, other = refs[:chips], refs[chips : 2 * chips]
+    outs = refs[2 * chips : 3 * chips]
+    keys_all, values_all = refs[3 * chips :]
     chip, core = info_ref[SERIES], info_ref[SERIES + 1]
     half = outs[0].shape[1]
     span = 2 * half
@@ -297,8 +268,8 @@
             at = pl.ds(pl.multiple_of(side * half, half), half)
             for odd, index in ((0, side), (1, 1 - side)):
                 block = 2 * (chip ^ f) + odd
-                keys_all[block, at, :] = source[0, index]
-                values_all[block, :, at] = source[1, index].T
+                keys_all[block, at, :] = source[1, index]
+                values_all[block, :, at] = source[2, index].T
 
     def first_of(row):
         found = jnp.int32(0)
@@ -311,7 +282,7 @@
         even = 2 * (chip ^ f)
         first_row = even * span + core * half
         last_row = first_row + span + half - 1
-        query = jnp.concatenate([queries[f][core], queries[f][1 - core]], axis=0)
+        query = jnp.concatenate([own[f][0, core], own[f][0, 1 - core]], axis=0)
         place = lax.broadcasted_iota(jnp.int32, (1, span), 1)
         row = first_row + place + jnp.where(place < half, 0, half)
         start = jnp.zeros((1, span), jnp.int32)
@@ -354,86 +325,134 @@
         outs[f][1 - core] = (accum / denom).T.astype(BF16)
 
 
-def attention_call(info, queries, own, other):
-    chips = len(queries)
-    _, half, _ = queries[0].shape
+def attention_call(info, own, other):
+    chips = len(own)
+    _, _, half, _ = own[0].shape
     return pl.pallas_call(
         functools.partial(attention_kernel, chips=chips),
         out_shape=[jax.ShapeDtypeStruct((2, half, HD), BF16)] * chips,
         grid_spec=pltpu.PrefetchScalarGridSpec(
             num_scalar_prefetch=1,
             grid=(1,),
-            in_specs=[whole((2, half, HD))] * chips + [whole((2, 2, half, HD))] * (2 * chips),
+            in_specs=[whole((3, 2, half, HD))] * (2 * chips),
             out_specs=[whole((2, half, HD))] * chips,
             scratch_shapes=[
                 pltpu.VMEM((2 * chips, 2 * half, HD), BF16),
                 pltpu.VMEM((2 * chips, HD, 2 * half), BF16),
             ],
         ),
-        compiler_params=params(30),
+        compiler_params=params(24),
         cost_estimate=cost(
             4 * chips * half * 4 * chips * half * HD,
             12 * chips * half * HD * 2,
             2 * chips * half * 4 * chips * half // 2,
         ),
         name="attention",
-    )(info, *queries, *own, *other)
+    )(info, *own, *other)
 
 
 def middle_kernel(info_ref, *refs, ring, chips):
     parts = [refs[:ring], refs[ring : 2 * ring]]
     refs = refs[2 * ring :]
     tok_ref, w_own_ref = refs[:2]
-    near_refs, far_refs = refs[2:4], refs[4:6]
-    gain_ref, gate_ref, up_ref, wp_ref, proj_ref, student_ref = refs[6:12]
-    hidden_ref, own_ref = refs[12:14]
-    pieces = refs[14 : 14 + ring]
-    attended, mixed, total = refs[14 + ring :]
+    near_first, near_rest = refs[2 : 2 + chips], refs[2 + chips : 2 + 2 * chips]
+    far_first, far_rest = refs[2 + 2 * chips], refs[3 + 2 * chips : 3 + 3 * chips]
+    refs = refs[3 + 3 * chips :]
+    gain_ref, gate_ref, up_ref, wp_ref, proj_ref, student_ref = refs[:6]
+    hidden_ref, own_ref = refs[6:8]
+    pieces = refs[8 : 8 + ring]
+    attended, mixed, total, near, far, gates, ups, wp, proj, sems = refs[8 + ring :]
     step = pl.program_id(0)
     level, chip, core = info_ref[0], info_ref[1], info_ref[2]
     rows, depth = mixed.shape
     half = rows // 2
     width = own_ref.shape[1]
+    blocks, _, wide = gates.shape
+
+    used = iter(range(sems.shape[0]))
+    copy = lambda source, target: pltpu.make_async_copy(source, target, sems.at[next(used)])
+    heads = []
+    for k in range(2):
+        for s, part in enumerate(parts[k]):
+            count = part.shape[0]
+            for i in range(count):
+                at = s * width + (chip ^ (k * count + i)) * HD
+                at = pl.ds(pl.multiple_of(at, HD), HD)
+                for side in range(2):
+                    rows_at = pl.ds(side * half, half)
+                    heads.append(copy(part.at[i, side], attended.at[rows_at, at]))
+    slices = [
+        [
+            copy(near_first[f], near.at[f, 0]),
+            copy(near_rest[f], near.at[f, pl.ds(1, ring - 2)]),
+            copy(far_first.at[f, 0], far.at[f, 0]),
+            copy(far_rest[f], far.at[f, pl.ds(1, ring - 2)]),
+        ]
+        for f in range(chips)
+    ]
+    own_rows = pl.ds(pl.multiple_of(level * width, width), width)
+    late = [copy(proj_ref.at[own_rows], proj), copy(student_ref, total)]
+    columns = [pl.ds(i * wide, wide) for i in range(blocks)]
+    units = [
+        [
+            copy(gate_ref.at[:, columns[i]], gates.at[i]),
+            copy(up_ref.at[:, columns[i]], ups.at[i]),
+            copy(wp_ref.at[columns[i]], wp.at[i]),
+        ]
+        for i in range(blocks)
+    ]
 
     @pl.when(step == 0)
     def _():
-        for k in range(2):
-            for s, part in enumerate(parts[k]):
-                for i in range(part.shape[0]):
-                    at = s * width + (chip ^ (k * part.shape[0] + i)) * HD
-                    at = pl.ds(pl.multiple_of(at, HD), HD)
-                    attended[:half, at] = part[i, 0]
-                    attended[half:, at] = part[i, 1]
+        for c in heads + slices[0]:
+            c.start()
+        for c in sum(slices[1:], []) + late + sum(units, []):
+            c.start()
+        for c in heads:
+            c.wait()
+
+    for f in range(chips):
+
+        @pl.when(step == f)
+        def _(f=f):
+            for c in slices[f]:
+                c.wait()
 
     @pl.when(step < chips)
     def _():
-        for w_refs, side in ((near_refs, core), (far_refs, 1 - core)):
+        for gathered, side in ((near, core), (far, 1 - core)):
             here = pl.ds(pl.multiple_of(side * COLS, COLS), COLS)
             result = tok_ref[:, here].astype(F32) + dot(attended[:, :width], w_own_ref[:, here])
-            done = width
-            for w_ref in w_refs:
-                some = w_ref.shape[1] * width
-                weight = w_ref[0].reshape(some, COLS)
-                result += dot(attended[:, done : done + some], weight)
-                done += some
-            at = pl.ds(pl.multiple_of((2 * step + side) * COLS, COLS), COLS)
+            weight = gathered[step].reshape(depth - width, COLS)
+            result += dot(attended[:, width:], weight)
+            at = pl.ds(pl.multiple_of((2 * (step ^ chip) + side) * COLS, COLS), COLS)
             mixed[:, at] = result.astype(BF16)
 
     @pl.when(step == chips)
     def _():
+        for c in late:
+            c.wait()
         values = mixed[...].astype(F32)
         attended[...] = (rms_scale(values) * gain_ref[...]).astype(BF16)
         own = mixed[:, pl.ds(pl.multiple_of(level * width, 128), width)]
         own_ref[...] = own
-        total[...] = student_ref[...] - dot(own, proj_ref[...])
+        total[...] -= dot(own, proj[...])
+
+    for i in range(blocks):
+
+        @pl.when(step == chips + i)
+        def _(i=i):
+            for c in units[i]:
+                c.wait()
 
     @pl.when(step >= chips)
     def _():
-        gate = dot(attended[...], gate_ref[...])
-        up = dot(attended[...], up_ref[...])
+        index = step - chips
+        gate = dot(attended[...], gates[index])
+        up = dot(attended[...], ups[index])
         hidden = (gate * jax.nn.sigmoid(gate) * up).astype(BF16)
         hidden_ref[...] = hidden
-        total[...] -= dot(hidden, wp_ref[...])
+        total[...] -= dot(hidden, wp[index])
 
     @pl.when(step == pl.num_programs(0) - 1)
     def _():
@@ -445,17 +464,16 @@
 
 def middle_call(info, parts, tok, w_out, near, far, gain, w_gate, w_up, wp, projector, student):
     rows, depth = tok.shape
-    ring, chips = len(parts[0]), near[0].shape[0]
+    ring, chips = len(parts[0]), len(near[0])
     units = w_gate.shape[1]
     wide = 2 * COLS
     width = depth // ring
     sd = projector.shape[1]
-    early = lambda j: jnp.minimum(j, chips - 1)
-    late = lambda j: jnp.maximum(j - chips, 0)
-    gathered = [
-        pl.BlockSpec((1,) + a.shape[1:], lambda j, info: (early(j) ^ info[1], 0, 0, 0))
-        for a in near
-    ]
+    blocks = units // wide
+    tile = lambda j, info: (0, jnp.minimum(j, chips - 1) ^ info[1])
+    late = lambda j, info: (0, jnp.maximum(j - chips, 0))
+    anywhere = pl.BlockSpec(memory_space=pl.ANY)
+    count = 2 * ring * parts[0][0].shape[0] * 2 + 4 * chips + 2 + 3 * blocks
     result = pl.pallas_call(
         functools.partial(middle_kernel, ring=ring, chips=chips),
         out_shape=[
@@ -465,22 +483,14 @@
         + [jax.ShapeDtypeStruct((rows // ring, sd), BF16)] * ring,
         grid_spec=pltpu.PrefetchScalarGridSpec(
             num_scalar_prefetch=1,
-            grid=(chips + units // wide,),
-            in_specs=[whole(parts[0][0].shape)] * (2 * ring)
-            + [
-                pl.BlockSpec((rows, wide), lambda j, info: (0, early(j))),
-                pl.BlockSpec((width, wide), lambda j, info: (0, early(j))),
-                *gathered,
-                *gathered,
-                whole((1, depth)),
-                pl.BlockSpec((depth, wide), lambda j, info: (0, late(j))),
-                pl.BlockSpec((depth, wide), lambda j, info: (0, late(j))),
-                pl.BlockSpec((wide, sd), lambda j, info: (late(j), 0)),
-                pl.BlockSpec((width, sd), lambda j, info: (info[0], 0)),
-                whole((rows, sd)),
-            ],
+            grid=(chips + blocks,),
+            in_specs=[anywhere] * (2 * ring)
+            + [pl.BlockSpec((rows, wide), tile), pl.BlockSpec((width, wide), tile)]
+            + [anywhere] * (3 * chips + 1)
+            + [whole((1, depth))]
+            + [anywhere] * 5,
             out_specs=[
-                pl.BlockSpec((rows, wide), lambda j, info: (0, late(j))),
+                pl.BlockSpec((rows, wide), late),
                 whole((rows, width)),
             ]
             + [whole((rows // ring, sd))] * ring,
@@ -488,9 +498,16 @@
                 pltpu.VMEM((rows, depth), BF16),
                 pltpu.VMEM((rows, depth), BF16),
                 pltpu.VMEM((rows, sd), F32),
+                pltpu.VMEM((chips, ring - 1, width, COLS), BF16),
+                pltpu.VMEM((chips, ring - 1, width, COLS), BF16),
+                pltpu.VMEM((blocks, depth, wide), BF16),
+                pltpu.VMEM((blocks, depth, wide), BF16),
+                pltpu.VMEM((blocks, wide, sd), BF16),
+                pltpu.VMEM((width, sd), BF16),
+                pltpu.SemaphoreType.DMA((count,)),
             ],
         ),
-        compiler_params=params(44),
+        compiler_params=params(42),
         cost_estimate=cost(
             2 * rows * depth * (depth + 2 * units) + 2 * rows * sd * (units + width),
             2 * depth * (depth + 2 * units),
@@ -503,8 +520,10 @@
         *parts[1],
         tok,
         w_out,
-        *near,
-        *far,
+        *near[0],
+        *near[1],
+        far[0],
+        *far[1],
         gain,
         w_gate,
         w_up,
@@ -515,8 +534,13 @@
     return result[0], result[1], result[2:]
 
 
-def down_kernel(level_ref, hidden_ref, weight_ref, out_ref):
-    out_ref[0] = dot(hidden_ref[...], weight_ref[...]).astype(BF16)
+def down_kernel(level_ref, hidden_ref, weight_ref, *outs):
+    result = dot(hidden_ref[...], weight_ref[...]).astype(BF16)
+    for j, out in enumerate(outs):
+
+        @pl.when(pl.program_id(0) == j)
+        def _(out=out):
+            out[...] = result
 
 
 def down_call(level, hidden, w_down, ring):
@@ -525,17 +549,15 @@
     width = depth // ring
     return pl.pallas_call(
         down_kernel,
-        out_shape=jax.ShapeDtypeStruct((ring, rows, width), BF16),
+        out_shape=[jax.ShapeDtypeStruct((rows, width), BF16)] * ring,
         grid_spec=pltpu.PrefetchScalarGridSpec(
             num_scalar_prefetch=1,
             grid=(ring,),
             in_specs=[
                 whole((rows, units)),
-                pl.BlockSpec(
-                    (units, width), lambda j, level: (0, (level[0] + 2 * ring - 1 - j) % ring)
-                ),
+                pl.BlockSpec((units, width), lambda j, level: (0, level[0] ^ (ring - 1 - j))),
             ],
-            out_specs=pl.BlockSpec((1, rows, width), lambda j, level: (j, 0, 0)),
+            out_specs=[whole((rows, width))] * ring,
         ),
         compiler_params=params(24),
         cost_estimate=cost(2 * rows * units * depth, 2 * units * depth),
@@ -555,8 +577,8 @@
     wide = value.astype(F32)
     error = jnp.sum(wide * wide)
     grad_hidden = dot_over(value, s_down_ref[...], (1, 1))
-    grads[0] = dot_over(normed_ref[...], (grad_hidden * gate_ref[...]).astype(BF16), (0, 0))
-    grads[1] = dot_over(normed_ref[...], (grad_hidden * up_ref[...]).astype(BF16), (0, 0))
+    grads[0] = dot_over(normed_ref[...], (grad_hidden * gate_ref[...].astype(F32)).astype(BF16), (0, 0))
+    grads[1] = dot_over(normed_ref[...], (grad_hidden * up_ref[...].astype(F32)).astype(BF16), (0, 0))
     grads[2] = dot_over(hidden_ref[...], value, (0, 0))
     share = grads.shape[1] // (2 * chips)
     for f in range(chips):
@@ -589,7 +611,7 @@
             out_specs=(whole((chips, share, units)), whole((chips, share, units))),
             scratch_shapes=[pltpu.VMEM((rows, sd), BF16), pltpu.VMEM((3, sd, units), F32)],
         ),
-        compiler_params=params(24),
+        compiler_params=params(22),
         cost_estimate=cost(8 * rows * sd * units, 20 * sd * units),
         name="grads",
     )(info, *operands)
@@ -605,7 +627,7 @@
     return pl.pallas_call(
         pair_kernel,
         out_shape=[jax.ShapeDtypeStruct((share, sd), BF16)] * chips,
-        compiler_params=params(16),
+        compiler_params=params(10),
         cost_estimate=cost(keep.size, 8 * keep.size),
         name="pair",
     )(keep, theirs)
@@ -640,7 +662,7 @@
             in_specs=[whole((share, sd))] * (2 * chips),
             out_specs=[whole((rows, sd))] * 3 + [whole((2 * chips, NOTE, HD))],
         ),
-        compiler_params=params(20),
+        compiler_params=params(14),
         cost_estimate=cost(rows * sd, 12 * rows * sd),
         name="finish",
     )(info, *mine, *others)
@@ -728,66 +750,64 @@
     cosine, sine = jnp.cos(angles), jnp.sin(angles)
     cosine = jnp.concatenate([cosine, cosine], axis=1)
     sine = jnp.concatenate([-sine, sine], axis=1)
-    factor = HD ** (-0.5) * math.log2(math.e)
     student_full = jnp.concatenate(student_chunks, axis=0).astype(F32)
     student_normed = rms_scale(student_full).astype(BF16)
+    below = jnp.sum(
+        series_ids[None, :] < jnp.arange(SERIES, dtype=jnp.int32)[:, None], axis=1, dtype=jnp.int32
+    )
+
+    info = number(*source, chip)
+    made, tok_full, stamp = qkv_call(
+        info, token_rings, norm_gain[None, :], cosine, sine, w_query, w_key, w_value
+    )
+
+    held = lax.optimization_barrier((student_normed, projector, stamp))
+    student_normed = held[0]
     s_gate_out = dot(student_normed, s_gate)
     s_up_out = dot(student_normed, s_up)
     sigmoid_gate = jax.nn.sigmoid(s_gate_out)
     up_slope = s_gate_out * sigmoid_gate
     gate_slope = s_up_out * sigmoid_gate * (1.0 + s_gate_out * (1.0 - sigmoid_gate))
     s_hidden = (up_slope * s_up_out).astype(BF16)
+    up_slope, gate_slope = up_slope.astype(BF16), gate_slope.astype(BF16)
     student_part = dot(s_hidden, s_down)
-    projected = dot(w_down, projector).astype(BF16)
-    below = jnp.sum(
-        series_ids[None, :] < jnp.arange(SERIES, dtype=jnp.int32)[:, None], axis=1, dtype=jnp.int32
-    )
-
+    projected = dot(w_down, held[1]).astype(BF16)
     early = (projected, student_part, s_hidden, up_slope, gate_slope, student_normed)
-    info = after(number(*source, chip), *early)
-    made, tok_full, normed = kv_call(
-        info, token_rings, norm_gain[None, :], cosine, sine, w_key, w_value
-    )
-    own_kv = flipped(made)
-    queries = query_call(info, normed, cosine * factor, sine * factor, w_query)
-    own_kv = lax.optimization_barrier((*own_kv, queries[0]))[:chips]
-    other_kv = [swapped(a) for a in own_kv]
 
     slice_cols = depth // dp
     w_slice = lax.dynamic_slice_in_dim(w_out, here * slice_cols, slice_cols, 1)
-    w_slice = after(w_slice, queries[0])
+    w_slice = after(w_slice, stamp)
     w_others = shifted([w_slice] * ring, "tensor")[1:]
-    queries = flipped(queries)
-
-    pairs = lambda a: a.reshape(a.shape[:-2] + (2, half, HD))
-    w_first = after(w_others[0], *queries, *other_kv)
-    near_first = flipped([w_first] * chips)
-    attention_info = jnp.concatenate([below, number(chip, core)])
+
+    own = flipped(made)
+    held = lax.optimization_barrier((*own, *w_others[:2], *early))
+    own, w_others[:2] = held[:chips], held[chips : chips + 2]
+    other = [swapped(a) for a in own]
+    near_first = flipped([w_others[0]] * chips)
+    pairs = lambda a: a.reshape(3, 2, half, HD)
     made = attention_call(
-        attention_info,
-        [pairs(a) for a in queries],
-        [pairs(a) for a in own_kv],
-        [pairs(a) for a in other_kv],
+        jnp.concatenate([below, number(chip, core)]),
+        [pairs(a) for a in own],
+        [pairs(a) for a in other],
     )
     held = lax.optimization_barrier((*made, *w_others[1:], *near_first))
     made, w_rest = held[:chips], jnp.stack(held[chips : chips + ring - 2])
-    attended = flipped(made)
+    attended = lax.optimization_barrier(tuple(flipped(made)))
     parts = [
         ring_gather(jnp.stack(attended[k : k + chips // 2]), "tensor") for k in (0, chips // 2)
     ]
     w_rest = after(w_rest, *attended)
     near_rest = flipped([w_rest] * chips)
-    near_rest = lax.optimization_barrier((*near_rest, *parts[0], *parts[1][:-1]))[:chips]
-    near = (jnp.stack(near_first)[:, None], jnp.stack(near_rest))
-    far = [swapped(after(a, *attended)) for a in near]
+    far_first = swapped(after(jnp.stack(near_first)[:, None], *attended))
+    far_rest = [swapped(after(a, parts[1][1])) for a in near_rest]
 
     hidden, mixed_own, pieces = middle_call(
         number(level, chip, core),
         parts,
         tok_full,
         w_out,
-        near,
-        far,
+        (near_first, near_rest),
+        (far_first, far_rest),
         mlp_gain[None, :],
         w_gate,
         w_up,
@@ -798,19 +818,19 @@
 
     size = rows // ring
     own = lax.dynamic_slice_in_dim(student_full, level * size, size, 0)
-    difference = own + sum(piece.astype(F32) for piece in shifted(pieces, "tensor"))
+    moved = shifted(pieces, "tensor")
+    difference = own + sum(piece.astype(F32) for piece in moved)
     own = (difference * total_rows ** (-0.5)).astype(BF16)
     scaled = shifted([own] * ring, "tensor")
 
-    mlp_part = down_call(level.astype(jnp.int32)[None], hidden, w_down, ring)
-    mlp_part = after(mlp_part, *scaled)
-    mlp_own = mlp_part[0]
-    for s in range(1, ring):
-        mlp_own = step_on(mlp_own, "tensor").astype(F32) + mlp_part[s].astype(F32)
-        mlp_own = mlp_own.astype(BF16) if s < ring - 1 else mlp_own
+    far_theirs, far_mine, near_theirs, kept = down_call(
+        level.astype(jnp.int32)[None], after(hidden, *moved[1:]), w_down, ring
+    )
+    over = lambda value, bit: lax.ppermute(value, "tensor", [(i, i ^ bit) for i in range(ring)])
+    far_sum = over(after(far_theirs, *scaled), 1)
 
     keep, give = grads_call(
-        number(*source, chip, core),
+        after(number(*source, chip, core), kept),
         scaled,
         student_normed,
         s_hidden,
@@ -819,19 +839,24 @@
         gate_slope,
         chips,
     )
-    shares = flipped(pair_call(keep, swapped(give)))
+    shares = pair_call(keep, swapped(give))
+    far_sum = after(far_sum, shares[0]).astype(F32) + far_mine.astype(F32)
+    far_sum = far_sum.astype(BF16)
+    shares = flipped(shares)
     own = sum(share.astype(F32) for share in shares).astype(BF16)
+    own = after(own, far_sum)
     mine = flipped([own] * chips)
     others = [swapped(share) for share in mine]
-    mlp_own = after(mlp_own, *others)
-    teacher = (mixed_own.astype(F32) + mlp_own).astype(BF16)
+
+    mlp_own = over(after(near_theirs, far_sum), 1).astype(F32) + over(far_sum, 2).astype(F32)
+    teacher = mixed_own.astype(F32) + (kept.astype(F32) + mlp_own)
+    teacher = teacher.astype(BF16)
     back = swapped(teacher[half:])
     teacher_out = jnp.where(
         core == 0,
         jnp.concatenate([teacher[:half], back], axis=0),
         jnp.concatenate([back, teacher[:half]], axis=0),
     )
-
     grad_gate, grad_up, grad_down, notes = finish_call(number(chip, core), mine, others)
     return teacher_out, grad_gate, grad_up, grad_down, notes[0, 0, 0] / sd
 
@@ -843,6 +868,7 @@
     fits = (
         dp == 2 * heads
         and heads > 1
+        and ring == 4
         and heads & (heads - 1) == 0
         and w_query.shape[0] == dp * COLS
         and s_gate.shape[0] == s_gate.shape[1]

time: 265 us -> 260 us (0.981)
  starting transfers between devices: 55.6 us -> 47.5 us
  local copies, waits for them, and re-layouts: 16.6 us -> 24.2 us
  matrix products: 12.8 us -> 8.39 us
  Pallas kernels: 53.9 us -> 57.1 us
  waiting for transfers between devices: 114 us -> 111 us
    ppermute x0 -> x3, waiting for transfers between devices: none -> 21.1 us  [paired(): lax.ppermute(value, 'tensor', [(i, i ^ bit) for i in range(ring)])]
    ppermute x21 -> x18, waiting for transfers between devices: 28.7 us -> 14.2 us  [flipped(): lax.ppermute(pieces[f], 'dp', [(i, i ^ 2 * f) for i in range(size)])]
    ppermute x15 -> x12, starting transfers between devices: 19.9 us -> 7.73 us  [step_on(): return lax.ppermute(block, axis, [(i, (i + 1) % size) for i in range(size)])]
    ppermute x15 -> x12, waiting for transfers between devices: 67.7 us -> 56.7 us  [step_on(): return lax.ppermute(block, axis, [(i, (i + 1) % size) for i in range(size)])]
    unnamed x84 -> x90, local copies, waits for them, and re-layouts: 11.9 us -> 18.7 us
    ppermute x15 -> x18, waiting for transfers between devices: 0.04 us -> 5.09 us  [swapped(): return lax.ppermute(value, 'dp', [(i, i ^ 1) for i in range(size)])]
    ppermute x21 -> x18, starting transfers between devices: 24.5 us -> 19.6 us  [flipped(): lax.ppermute(pieces[f], 'dp', [(i, i ^ 2 * f) for i in range(size)])]
    ppermute x9, starting transfers between devices: 8.76 us -> 13.2 us  [shifted(): lax.ppermute(pieces[s], axis, [(i, (i + s) % size) for i in range(size)])]
  transfers between devices with their start and end apart: 60 -> 60, of which waited for: 27 -> 29; matrix products, arithmetic and copies ran while one was open for 8% -> 8% of each run, Pallas kernels for 10% -> 8%
where the time goes in v3:
time: 260 us
  waiting for transfers between devices  111 us (43%)
  Pallas kernels  57.1 us (22%)
  starting transfers between devices  47.5 us (18%)
  local copies, waits for them, and re-layouts  24.2 us (9%)
  other arithmetic  8.73 us (3%)
  matrix products  8.39 us (3%)
  between operations  2.94 us (1%)
    ppermute x12, waiting for transfers between devices, step_on(): return lax.ppermute(block, axis, [(i, (i + 1) % size) for i in range(size)])  56.7 us
    pallas_call x1, Pallas kernels, middle_call(): pl.pallas_call(functools.partial(middle_kernel, ring=ring, chips=chips),...  26.9 us
    ppermute x3, waiting for transfers between devices, paired(): lax.ppermute(value, 'tensor', [(i, i ^ bit) for i in range(ring)])  21.1 us
    ppermute x18, starting transfers between devices, flipped(): lax.ppermute(pieces[f], 'dp', [(i, i ^ 2 * f) for i in range(size)])  19.6 us
    unnamed x90, local copies, waits for them, and re-layouts  18.7 us
    ppermute x18, waiting for transfers between devices, flipped(): lax.ppermute(pieces[f], 'dp', [(i, i ^ 2 * f) for i in range(size)])  14.2 us
    ppermute x9, waiting for transfers between devices, shifted(): lax.ppermute(pieces[s], axis, [(i, (i + s) % size) for i in range(size)])  13.7 us
    ppermute x9, starting transfers between devices, shifted(): lax.ppermute(pieces[s], axis, [(i, (i + s) % size) for i in range(size)])  13.2 us
  transfers between devices with their start and end apart: 60, of which 29 were waited for; matrix products, arithmetic and copies ran while one was open for 8% of the time, Pallas kernels for 8%

profile of v3, /device:TPU:0, one launch (start us, length us, event | category | flops | bytes accessed | tf_op | source)
XLA Modules:
  0.0 259.6 jit_solution(12488718794730986922)
XLA Ops:
  0.7 1.1 dynamic-slice_bitcast_fusion.2
  3.1 3.0 %collective-permute-start = (bf16[256,512]{1,0:T(8,128)(2,1)S(1)}, bf16[256,512]{1,0:T(8,128)(2,1)S(1)}, u32[]{:S(2)}, u32[]{:S(2)}) collective-permute-start(bf16[256,512]{1,0:T(8,128)(2,1)S(1)} %get-tuple-element.135.refs_0_), channel_id=1, source_target_pairs={{0,1},{1,2},{2,3},{3,0},{4,5},{5,6},{6,7},{7,4},{8,9},{9,10},{10,1... | collective-permute-start | bytes 786440 | tf_op jit(solution)/shard_map/ppermute | solution.py:673
  6.2 1.9 dynamic-slice_bitcast_fusion.1
  8.0 1.6 collective-permute-start.4
  9.7 1.8 constant_dynamic-slice_fusion
  11.6 3.7 %collective-permute-done.refs_1_ = bf16[256,512]{1,0:T(8,128)(2,1)S(1)} collective-permute-done((bf16[256,512]{1,0:T(8,128)(2,1)S(1)}, bf16[256,512]{1,0:T(8,128)(2,1)S(1)}, u32[]{:S(2)}, u32[]{:S(2)}) %collective-permute-start) | collective-permute-done | bytes 262176 | tf_op jit(solution)/shard_map/ppermute | solution.py:673
  15.3 5.7 %collective-permute-done.4.refs_5_ = bf16[256,512]{1,0:T(8,128)(2,1)} collective-permute-done((bf16[256,512]{1,0:T(8,128)(2,1)S(1)}, bf16[256,512]{1,0:T(8,128)(2,1)}, u32[]{:S(2)}, u32[]{:S(2)}) %collective-permute-start.4) | collective-permute-done | bytes 262176 | tf_op jit(solution)/shard_map/ppermute | solution.py:673
  21.0 1.0 fusion.3
  22.3 1.4 multiply_reduce_fusion
  23.6 2.9 %collective-permute-done.1.refs_2_ = bf16[256,512]{1,0:T(8,128)(2,1)S(1)} collective-permute-done((bf16[256,512]{1,0:T(8,128)(2,1)S(1)}, bf16[256,512]{1,0:T(8,128)(2,1)S(1)}, u32[]{:S(2)}, u32[]{:S(2)}) %collective-permute-start.1) | collective-permute-done | bytes 262176 | tf_op jit(solution)/shard_map/ppermute | solution.py:673
  26.6 5.7 %collective-permute-done.5.refs_6_ = bf16[256,512]{1,0:T(8,128)(2,1)S(1)} collective-permute-done((bf16[256,512]{1,0:T(8,128)(2,1)}, bf16[256,512]{1,0:T(8,128)(2,1)S(1)}, u32[]{:S(2)}, u32[]{:S(2)}) %collective-permute-start.5) | collective-permute-done | bytes 262176 | tf_op jit(solution)/shard_map/ppermute | solution.py:673
  32.3 1.2 multiply_convert_fusion.2.refs_4_
  33.5 4.4 %collective-permute-done.2.refs_3_ = bf16[256,512]{1,0:T(8,128)(2,1)S(1)} collective-permute-done((bf16[256,512]{1,0:T(8,128)(2,1)S(1)}, bf16[256,512]{1,0:T(8,128)(2,1)S(1)}, u32[]{:S(2)}, u32[]{:S(2)}) %collective-permute-start.2) | collective-permute-done | bytes 262176 | tf_op jit(solution)/shard_map/ppermute | solution.py:673
  37.9 4.9 %collective-permute-done.6.refs_7_ = bf16[256,512]{1,0:T(8,128)(2,1)S(1)} collective-permute-done((bf16[256,512]{1,0:T(8,128)(2,1)S(1)}, bf16[256,512]{1,0:T(8,128)(2,1)S(1)}, u32[]{:S(2)}, u32[]{:S(2)}) %collective-permute-start.6) | collective-permute-done | bytes 262176 | tf_op jit(solution)/shard_map/ppermute | solution.py:673
  43.8 0.9 copy-done.19
  44.7 7.9 %qkv.1 = (bf16[3,512,128]{2,1,0:T(8,128)(2,1)S(1)}, bf16[3,512,128]{2,1,0:T(8,128)(2,1)S(1)}, bf16[3,512,128]{2,1,0:T(8,128)(2,1)S(1)}, bf16[3,512,128]{2,1,0:T(...) custom-call(s32[5]{0:T(128)S(1)} %stack.94.info_ref, bf16[256,512]{1,0:T(8,128)(2,1)S(1)} %get-tuple-element.135.refs_0_, ...), custom_call_target="tpu_custom_call" | custom-call | flops 3221225472 | bytes 6291456 | tf_op jit(solution)/shard_map/qkv/pallas_call | solution.py:232
  52.7 2.3 collective-permute-start.12
  55.0 2.4 collective-permute-start.10
  59.0 5.7 %fusion.refs_26_ = bf16[2048,512]{1,0:T(8,128)(2,1)} fusion(bf16[2048,2048]{1,0:T(8,128)(2,1)S(1)} %bitcast.59, bf16[2048,512]{1,0:T(8,128)(2,1)S(1)} %copy-done.42), kind=kOutput, calls=%fused_computation.1 | convolution fusion | flops 4296015872 | bytes 12582912 | tf_op jit(solution)/shard_map/dot_general | solution.py:166
  64.7 1.8 multiply_convert_fusion
  67.0 5.6 %collective-permute-done.12 = bf16[512,256]{1,0:T(8,128)(2,1)S(1)} collective-permute-done((bf16[512,256]{1,0:T(8,128)(2,1)S(1)}, bf16[512,256]{1,0:T(8,128)(2,1)S(1)}, u32[]{:S(2)}, u32[]{:S(2)}) %collective-permute-start.12) | collective-permute-done | bytes 262176 | tf_op jit(solution)/shard_map/ppermute | solution.py:686
  72.6 1.6 collective-permute-done.8
  75.3 1.9 collective-permute-start.18
  77.3 1.3 collective-permute-start.19
  78.6 1.4 collective-permute-start.20
  80.8 11.6 %attention.1 = (bf16[2,256,128]{2,1,0:T(8,128)(2,1)S(1)}, bf16[2,256,128]{2,1,0:T(8,128)(2,1)S(1)}, bf16[2,256,128]{2,1,0:T(8,128)(2,1)S(1)}, bf16[2,256,128]{2,1,0:T(8,128)(2,1)S(1)}) custom-call(s32[10]{0:T(128)S(1)} %pad_add_fusion.1.info_ref, bf16[3,2,256,128]{3,2,1,0:T(8,128)(2,1)S(1)} %bitcast.60, bf16[3,2,256,128]{3,2,1,0:T(8,128)(2,1)S(1)} %bitcast.62, ...), custom_call_target="tpu_custom_call" | custom-call | flops 2147483648 | bytes 3145728 | tf_op jit(solution)/shard_map/attention/pallas_call | solution.py:331
  92.5 1.4 collective-permute-start.22
  93.9 1.4 collective-permute-start.23
  96.0 2.7 %collective-permute-done.22 = bf16[2,256,128]{2,1,0:T(8,128)(2,1)S(1)} collective-permute-done((bf16[2,256,128]{2,1,0:T(8,128)(2,1)S(1)}, bf16[2,256,128]{2,1,0:T(8,128)(2,1)S(1)}, u32[]{:S(2)}, u32[]{:S(2)}) %collective-permute-start.22) | collective-permute-done | bytes 131104 | tf_op jit(solution)/shard_map/ppermute | solution.py:695
  98.7 2.6 collective-permute-done.23
  101.4 1.0 collective-permute-start.28
  102.4 1.4 collective-permute-start.25
  104.6 7.8 %collective-permute-done.28.refs_5_ = bf16[2,2,256,128]{3,2,1,0:T(8,128)(2,1)S(1)} collective-permute-done((bf16[2,2,256,128]{3,2,1,0:T(8,128)(2,1)S(1)}, bf16[2,2,256,128]{3,2,1,0:T(8,128)(2,1)S(1)}, u32[]{:S(2)}, u32[]{:S(2)}) %collective-permute-start.28) | collective-permute-done | bytes 262176 | tf_op jit(solution)/shard_map/ppermute | solution.py:673
  112.5 1.0 collective-permute-start.32
  113.8 4.3 %collective-permute-done.25.refs_1_ = bf16[2,2,256,128]{3,2,1,0:T(8,128)(2,1)S(1)} collective-permute-done((bf16[2,2,256,128]{3,2,1,0:T(8,128)(2,1)S(1)}, bf16[2,2,256,128]{3,2,1,0:T(8,128)(2,1)S(1)}, u32[]{:S(2)}, u32[]{:S(2)}) %collective-permute-start.25) | collective-permute-done | bytes 262176 | tf_op jit(solution)/shard_map/ppermute | solution.py:673
  118.1 1.1 maximum_bitcast_fusion
  119.2 4.3 %collective-permute-done.29.refs_6_ = bf16[2,2,256,128]{3,2,1,0:T(8,128)(2,1)S(1)} collective-permute-done((bf16[2,2,256,128]{3,2,1,0:T(8,128)(2,1)S(1)}, bf16[2,2,256,128]{3,2,1,0:T(8,128)(2,1)S(1)}, u32[]{:S(2)}, u32[]{:S(2)}) %collective-permute-start.29) | collective-permute-done | bytes 262176 | tf_op jit(solution)/shard_map/ppermute | solution.py:673
  123.5 2.8 %collective-permute-done.26.refs_2_ = bf16[2,2,256,128]{3,2,1,0:T(8,128)(2,1)S(1)} collective-permute-done((bf16[2,2,256,128]{3,2,1,0:T(8,128)(2,1)S(1)}, bf16[2,2,256,128]{3,2,1,0:T(8,128)(2,1)S(1)}, u32[]{:S(2)}, u32[]{:S(2)}) %collective-permute-start.26) | collective-permute-done | bytes 262176 | tf_op jit(solution)/shard_map/ppermute | solution.py:673
  128.8 8.1 %collective-permute-done.30.refs_7_ = bf16[2,2,256,128]{3,2,1,0:T(8,128)(2,1)S(1)} collective-permute-done((bf16[2,2,256,128]{3,2,1,0:T(8,128)(2,1)S(1)}, bf16[2,2,256,128]{3,2,1,0:T(8,128)(2,1)S(1)}, u32[]{:S(2)}, u32[]{:S(2)}) %collective-permute-start.30) | collective-permute-done | bytes 262176 | tf_op jit(solution)/shard_map/ppermute | solution.py:673
  137.6 2.1 collective-permute-done.27.refs_3_
  140.6 2.1 collective-permute-done.36.refs_20_
  143.6 0.9 copy-done.6
  153.1 26.9 %middle.1 = (bf16[512,2048]{1,0:T(8,128)(2,1)}, bf16[512,512]{1,0:T(8,128)(2,1)S(1)}, bf16[128,512]{1,0:T(8,128)(2,1)S(1)}, bf16[128,512]{1,0:T(8,128)(2,1)S(1)}...) custom-call(s32[3]{0:T(128)S(1)} %pad_add_fusion.info_ref, bf16[2,2,256,128]{3,2,1,0:T(8,128)(2,1)S(1)} %copy-done.4, ...), custom_call_target="tpu_custom_call" | custom-call | flops 14227079168 | bytes 25165824 | tf_op jit(solution)/shard_map/middle/pallas_call | solution.py:477
  180.2 3.7 %collective-permute-start.41 = (bf16[128,512]{1,0:T(8,128)(2,1)S(1)}, bf16[128,512]{1,0:T(8,128)(2,1)S(1)}, u32[]{:S(2)}, u32[]{:S(2)}) collective-permute-start(bf16[128,512]{1,0:T(8,128)(2,1)S(1)} %get-tuple-element.105), channel_id=1, source_target_pairs={{0,3},{1,0},{2,1},{3,2},{4,7},{5,4},{6,5},{7,6},{8,11},{9,8},{10,9... | collective-permute-start | bytes 393224 | tf_op jit(solution)/shard_map/ppermute | solution.py:686
  183.9 1.1 maximum_convert_fusion
  185.0 3.4 %collective-permute-done.39 = bf16[128,512]{1,0:T(8,128)(2,1)S(1)} collective-permute-done((bf16[128,512]{1,0:T(8,128)(2,1)S(1)}, bf16[128,512]{1,0:T(8,128)(2,1)S(1)}, u32[]{:S(2)}, u32[]{:S(2)}) %collective-permute-start.39) | collective-permute-done | bytes 131104 | tf_op jit(solution)/shard_map/ppermute | solution.py:686
  188.4 4.7 %collective-permute-done.40 = bf16[128,512]{1,0:T(8,128)(2,1)S(1)} collective-permute-done((bf16[128,512]{1,0:T(8,128)(2,1)S(1)}, bf16[128,512]{1,0:T(8,128)(2,1)S(1)}, u32[]{:S(2)}, u32[]{:S(2)}) %collective-permute-start.40) | collective-permute-done | bytes 131104 | tf_op jit(solution)/shard_map/ppermute | solution.py:686
  193.2 2.6 %collective-permute-start.42 = (bf16[128,512]{1,0:T(8,128)(2,1)S(1)}, bf16[128,512]{1,0:T(8,128)(2,1)S(1)}, u32[]{:S(2)}, u32[]{:S(2)}) collective-permute-start(bf16[128,512]{1,0:T(8,128)(2,1)S(1)} %multiply_convert_fusion.3.refs_0_), channel_id=1, source_target_pairs={{0,1},{1,2},{2,3},{3,0},{4,5},{5,6},{6,7},{7,4},{8,9},{9,10},{10,1... | collective-permute-start | bytes 393224 | tf_op jit(solution)/shard_map/ppermute | solution.py:686
  196.4 1.8 collective-permute-start.44
  198.3 3.4 %copy-done.13 = bf16[2048,2048]{1,0:T(8,128)(2,1)S(1)} copy-done((bf16[2048,2048]{1,0:T(8,128)(2,1)S(1)}, bf16[2048,2048]{1,0:T(8,128)(2,1)}, u32[]{:S(2)}) %copy-start.13) | copy-done | bytes 8388632
  201.6 5.9 %down.1 = (bf16[512,512]{1,0:T(8,128)(2,1)S(1)}, bf16[512,512]{1,0:T(8,128)(2,1)S(1)}, bf16[512,512]{1,0:T(8,128)(2,1)S(1)}, bf16[512,512]{1,0:T(8,128)(2,1)S(1)}) custom-call(s32[1]{0:T(128)} %bitcast.level_ref, bf16[512,2048]{1,0:T(8,128)(2,1)S(1)} %copy-done.37, bf16[2048,2048]{1,0:T(8,128)(2,1)S(1)} %copy-done.13), custom_call_target="tpu_custom_call" | custom-call | flops 4294967296 | bytes 8388608 | tf_op jit(solution)/shard_map/down/pallas_call | solution.py:550
  207.6 2.2 grads.1
  210.9 1.4 collective-permute-done.46.theirs_ref
  212.5 11.8 %collective-permute-done.45 = bf16[512,512]{1,0:T(8,128)(2,1)S(1)} collective-permute-done((bf16[512,512]{1,0:T(8,128)(2,1)S(1)}, bf16[512,512]{1,0:T(8,128)(2,1)S(1)}, u32[]{:S(2)}, u32[]{:S(2)}) %collective-permute-start.45) | collective-permute-done | bytes 524320 | tf_op jit(solution)/shard_map/ppermute | solution.py:829
  225.4 1.6 collective-permute-start.48
  227.5 3.0 %collective-permute-start.52 = (bf16[208,512]{1,0:T(8,128)(2,1)S(1)}, bf16[208,512]{1,0:T(8,128)(2,1)S(1)}, u32[]{:S(2)}, u32[]{:S(2)}) collective-permute-start(bf16[208,512]{1,0:T(8,128)(2,1)S(1)} %get-tuple-element.121), channel_id=1, source_target_pairs={{0,24},{4,28},{8,16},{12,20},{16,8},{20,12},{24,0},{28,4},{1,25},{... | collective-permute-start | bytes 638984 | tf_op jit(solution)/shard_map/ppermute | solution.py:695
  230.5 4.7 %collective-permute-done.50 = bf16[208,512]{1,0:T(8,128)(2,1)S(1)} collective-permute-done((bf16[208,512]{1,0:T(8,128)(2,1)S(1)}, bf16[208,512]{1,0:T(8,128)(2,1)S(1)}, u32[]{:S(2)}, u32[]{:S(2)}) %collective-permute-start.50) | collective-permute-done | bytes 213024 | tf_op jit(solution)/shard_map/ppermute | solution.py:695
  235.2 2.6 %collective-permute-done.51 = bf16[208,512]{1,0:T(8,128)(2,1)S(1)} collective-permute-done((bf16[208,512]{1,0:T(8,128)(2,1)S(1)}, bf16[208,512]{1,0:T(8,128)(2,1)S(1)}, u32[]{:S(2)}, u32[]{:S(2)}) %collective-permute-start.51) | collective-permute-done | bytes 213024 | tf_op jit(solution)/shard_map/ppermute | solution.py:695
  238.0 1.8 collective-permute-start.53
  240.2 1.3 collective-permute-start.55
  241.5 6.5 %collective-permute-done.47 = bf16[512,512]{1,0:T(8,128)(2,1)S(1)} collective-permute-done((bf16[512,512]{1,0:T(8,128)(2,1)S(1)}, bf16[512,512]{1,0:T(8,128)(2,1)S(1)}, u32[]{:S(2)}, u32[]{:S(2)}) %collective-permute-start.47) | collective-permute-done | bytes 524320 | tf_op jit(solution)/shard_map/ppermute | solution.py:829
  248.0 2.7 %collective-permute-done.48 = bf16[512,512]{1,0:T(8,128)(2,1)S(1)} collective-permute-done((bf16[512,512]{1,0:T(8,128)(2,1)S(1)}, bf16[512,512]{1,0:T(8,128)(2,1)S(1)}, u32[]{:S(2)}, u32[]{:S(2)}) %collective-permute-start.48) | collective-permute-done | bytes 524320 | tf_op jit(solution)/shard_map/ppermute | solution.py:829
  253.9 2.4 finish.1
  257.5 1.0 maximum_select_fusion
  (189 shorter events, 30.1 us)
Async XLA Ops:
  0.6 64.1 %copy-start = (bf16[512,512]{1,0:T(8,128)(2,1)S(1)}, bf16[512,512]{1,0:T(8,128)(2,1)}, u32[]{:S(2)}) copy-start(bf16[512,512]{1,0:T(8,128)(2,1)} %param.31) | copy-start | bytes 1572868
  1.8 6.2 %collective-permute-start.3 = (bf16[256,512]{1,0:T(8,128)(2,1)S(1)}, bf16[256,512]{1,0:T(8,128)(2,1)S(1)}, u32[]{:S(2)}, u32[]{:S(2)}) collective-permute-start(bf16[256,512]{1,0:T(8,128)(2,1)S(1)} %get-tuple-element.134), channel_id=1, source_target_pairs={{0,4},{4,0},{8,12},{12,8},{16,20},{20,16},{24,28},{28,24},{1,5},{5... | collective-permute-start | bytes 786440 | tf_op jit(solution)/shard_map/ppermute | solution.py:703
  3.0 8.6 %collective-permute-start.7 = (f32[256]{0:T(256)S(1)}, f32[256]{0:T(256)S(1)}, u32[]{:S(2)}, u32[]{:S(2)}) collective-permute-start(f32[256]{0:T(256)S(1)} %bitcast.78), channel_id=1, source_target_pairs={{0,4},{4,0},{8,12},{12,8},{16,20},{20,16},{24,28},{28,24},{1,5},{5... | collective-permute-start | bytes 3080 | tf_op jit(solution)/shard_map/ppermute | solution.py:703
  3.1 12.2 %collective-permute-start = (bf16[256,512]{1,0:T(8,128)(2,1)S(1)}, bf16[256,512]{1,0:T(8,128)(2,1)S(1)}, u32[]{:S(2)}, u32[]{:S(2)}) collective-permute-start(bf16[256,512]{1,0:T(8,128)(2,1)S(1)} %get-tuple-element.135.refs_0_), channel_id=1, source_target_pairs={{0,1},{1,2},{2,3},{3,0},{4,5},{5,6},{6,7},{7,4},{8,9},{9,10},{10,1... | collective-permute-start | bytes 786440 | tf_op jit(solution)/shard_map/ppermute | solution.py:673
  8.0 14.2 %collective-permute-start.13 = (bf16[256,512]{1,0:T(8,128)(2,1)}, bf16[256,512]{1,0:T(8,128)(2,1)}, u32[]{:S(2)}, u32[]{:S(2)}) collective-permute-start(bf16[256,512]{1,0:T(8,128)(2,1)} %get-tuple-element.133), channel_id=1, source_target_pairs={{0,4},{4,0},{8,12},{12,8},{16,20},{20,16},{24,28},{28,24},{1,5},{5... | collective-permute-start | bytes 786440 | tf_op jit(solution)/shard_map/ppermute | solution.py:703
  8.0 13.0 %collective-permute-start.4 = (bf16[256,512]{1,0:T(8,128)(2,1)S(1)}, bf16[256,512]{1,0:T(8,128)(2,1)}, u32[]{:S(2)}, u32[]{:S(2)}) collective-permute-start(bf16[256,512]{1,0:T(8,128)(2,1)S(1)} %collective-permute-done.3.refs_4_), channel_id=1, source_target_pairs={{0,1},{1,2},{2,3},{3,0},{4,5},{5,6},{6,7},{7,4},{8,9},{9,10},{10,1... | collective-permute-start | bytes 786440 | tf_op jit(solution)/shard_map/ppermute | solution.py:673
  15.3 11.2 %collective-permute-start.1 = (bf16[256,512]{1,0:T(8,128)(2,1)S(1)}, bf16[256,512]{1,0:T(8,128)(2,1)S(1)}, u32[]{:S(2)}, u32[]{:S(2)}) collective-permute-start(bf16[256,512]{1,0:T(8,128)(2,1)S(1)} %collective-permute-done.refs_1_), channel_id=1, source_target_pairs={{0,1},{1,2},{2,3},{3,0},{4,5},{5,6},{6,7},{7,4},{8,9},{9,10},{10,1... | collective-permute-start | bytes 786440 | tf_op jit(solution)/shard_map/ppermute | solution.py:673
  21.0 11.3 %collective-permute-start.5 = (bf16[256,512]{1,0:T(8,128)(2,1)}, bf16[256,512]{1,0:T(8,128)(2,1)S(1)}, u32[]{:S(2)}, u32[]{:S(2)}) collective-permute-start(bf16[256,512]{1,0:T(8,128)(2,1)} %collective-permute-done.4.refs_5_), channel_id=1, source_target_pairs={{0,1},{1,2},{2,3},{3,0},{4,5},{5,6},{6,7},{7,4},{8,9},{9,10},{10,1... | collective-permute-start | bytes 786440 | tf_op jit(solution)/shard_map/ppermute | solution.py:673
  22.3 36.7 %slice-start = ((s8[8388608]{0:T(1024)(128)(4,1)}), s8[4194304]{0:T(1024)(128)(4,1)S(1)}, s32[]{:S(2)}) async-start(s8[8388608]{0:T(1024)(128)(4,1)} %bitcast.58), calls=%async_computation | async-start | bytes 8388608
  26.5 11.4 %collective-permute-start.2 = (bf16[256,512]{1,0:T(8,128)(2,1)S(1)}, bf16[256,512]{1,0:T(8,128)(2,1)S(1)}, u32[]{:S(2)}, u32[]{:S(2)}) collective-permute-start(bf16[256,512]{1,0:T(8,128)(2,1)S(1)} %collective-permute-done.1.refs_2_), channel_id=1, source_target_pairs={{0,1},{1,2},{2,3},{3,0},{4,5},{5,6},{6,7},{7,4},{8,9},{9,10},{10,1... | collective-permute-start | bytes 786440 | tf_op jit(solution)/shard_map/ppermute | solution.py:673
  32.3 10.5 %collective-permute-start.6 = (bf16[256,512]{1,0:T(8,128)(2,1)S(1)}, bf16[256,512]{1,0:T(8,128)(2,1)S(1)}, u32[]{:S(2)}, u32[]{:S(2)}) collective-permute-start(bf16[256,512]{1,0:T(8,128)(2,1)S(1)} %collective-permute-done.5.refs_6_), channel_id=1, source_target_pairs={{0,1},{1,2},{2,3},{3,0},{4,5},{5,6},{6,7},{7,4},{8,9},{9,10},{10,1... | collective-permute-start | bytes 786440 | tf_op jit(solution)/shard_map/ppermute | solution.py:673
  52.7 14.3 %collective-permute-start.11 = (bf16[512,256]{1,0:T(8,128)(2,1)S(1)}, bf16[512,256]{1,0:T(8,128)(2,1)S(1)}, u32[]{:S(2)}, u32[]{:S(2)}) collective-permute-start(bf16[512,256]{1,0:T(8,128)(2,1)S(1)} %copy-done.40), channel_id=1, source_target_pairs={{0,1},{1,2},{2,3},{3,0},{4,5},{5,6},{6,7},{7,4},{8,9},{9,10},{10,1... | collective-permute-start | bytes 786440 | tf_op jit(solution)/shard_map/ppermute | solution.py:686
  52.7 19.8 %collective-permute-start.12 = (bf16[512,256]{1,0:T(8,128)(2,1)S(1)}, bf16[512,256]{1,0:T(8,128)(2,1)S(1)}, u32[]{:S(2)}, u32[]{:S(2)}) collective-permute-start(bf16[512,256]{1,0:T(8,128)(2,1)S(1)} %copy-done.40), channel_id=1, source_target_pairs={{0,2},{1,3},{2,0},{3,1},{4,6},{5,7},{6,4},{7,5},{8,10},{9,11},{10,... | collective-permute-start | bytes 786440 | tf_op jit(solution)/shard_map/ppermute | solution.py:686
  55.0 17.5 %collective-permute-start.10 = (bf16[3,512,128]{2,1,0:T(8,128)(2,1)S(1)}, bf16[3,512,128]{2,1,0:T(8,128)(2,1)S(1)}, u32[]{:S(2)}, u32[]{:S(2)}) collective-permute-start(bf16[3,512,128]{2,1,0:T(8,128)(2,1)S(1)} %get-tuple-element.69), channel_id=1, source_target_pairs={{0,24},{4,28},{8,16},{12,20},{16,8},{20,12},{24,0},{28,4},{1,25},{... | collective-permute-start | bytes 1179656 | tf_op jit(solution)/shard_map/ppermute | solution.py:695
  57.5 16.7 %collective-permute-start.8 = (bf16[3,512,128]{2,1,0:T(8,128)(2,1)S(1)}, bf16[3,512,128]{2,1,0:T(8,128)(2,1)S(1)}, u32[]{:S(2)}, u32[]{:S(2)}) collective-permute-start(bf16[3,512,128]{2,1,0:T(8,128)(2,1)S(1)} %get-tuple-element.67), channel_id=1, source_target_pairs={{0,8},{4,12},{8,0},{12,4},{16,24},{20,28},{24,16},{28,20},{1,9},{5... | collective-permute-start | bytes 1179656 | tf_op jit(solution)/shard_map/ppermute | solution.py:695
  58.0 16.1 %collective-permute-start.9 = (bf16[3,512,128]{2,1,0:T(8,128)(2,1)S(1)}, bf16[3,512,128]{2,1,0:T(8,128)(2,1)S(1)}, u32[]{:S(2)}, u32[]{:S(2)}) collective-permute-start(bf16[3,512,128]{2,1,0:T(8,128)(2,1)S(1)} %get-tuple-element.68), channel_id=1, source_target_pairs={{0,16},{4,20},{8,24},{12,28},{16,0},{20,4},{24,8},{28,12},{1,17},{... | collective-permute-start | bytes 1179656 | tf_op jit(solution)/shard_map/ppermute | solution.py:695
  67.0 51.1 %copy-start.5 = (bf16[512,256]{1,0:T(8,128)(2,1)}, bf16[512,256]{1,0:T(8,128)(2,1)S(1)}, u32[]{:S(2)}) copy-start(bf16[512,256]{1,0:T(8,128)(2,1)S(1)} %collective-permute-done.11.refs_10_) | copy-start | bytes 786436
  74.2 3.1 %collective-permute-start.14 = (bf16[3,512,128]{2,1,0:T(8,128)(2,1)S(1)}, bf16[3,512,128]{2,1,0:T(8,128)(2,1)S(1)}, u32[]{:S(2)}, u32[]{:S(2)}) collective-permute-start(bf16[3,512,128]{2,1,0:T(8,128)(2,1)S(1)} %get-tuple-element.74), channel_id=1, source_target_pairs={{0,4},{4,0},{8,12},{12,8},{16,20},{20,16},{24,28},{28,24},{1,5},{5... | collective-permute-start | bytes 1179656 | tf_op jit(solution)/shard_map/ppermute | solution.py:703
  74.2 4.5 %collective-permute-start.15 = (bf16[3,512,128]{2,1,0:T(8,128)(2,1)S(1)}, bf16[3,512,128]{2,1,0:T(8,128)(2,1)S(1)}, u32[]{:S(2)}, u32[]{:S(2)}) collective-permute-start(bf16[3,512,128]{2,1,0:T(8,128)(2,1)S(1)} %collective-permute-done.8), channel_id=1, source_target_pairs={{0,4},{4,0},{8,12},{12,8},{16,20},{20,16},{24,28},{28,24},{1,5},{5... | collective-permute-start | bytes 1179656 | tf_op jit(solution)/shard_map/ppermute | solution.py:703
  74.7 5.4 %collective-permute-start.16 = (bf16[3,512,128]{2,1,0:T(8,128)(2,1)S(1)}, bf16[3,512,128]{2,1,0:T(8,128)(2,1)S(1)}, u32[]{:S(2)}, u32[]{:S(2)}) collective-permute-start(bf16[3,512,128]{2,1,0:T(8,128)(2,1)S(1)} %collective-permute-done.9), channel_id=1, source_target_pairs={{0,4},{4,0},{8,12},{12,8},{16,20},{20,16},{24,28},{28,24},{1,5},{5... | collective-permute-start | bytes 1179656 | tf_op jit(solution)/shard_map/ppermute | solution.py:703
  74.7 6.2 %collective-permute-start.17 = (bf16[3,512,128]{2,1,0:T(8,128)(2,1)S(1)}, bf16[3,512,128]{2,1,0:T(8,128)(2,1)S(1)}, u32[]{:S(2)}, u32[]{:S(2)}) collective-permute-start(bf16[3,512,128]{2,1,0:T(8,128)(2,1)S(1)} %collective-permute-done.10), channel_id=1, source_target_pairs={{0,4},{4,0},{8,12},{12,8},{16,20},{20,16},{24,28},{28,24},{1,5},{5... | collective-permute-start | bytes 1179656 | tf_op jit(solution)/shard_map/ppermute | solution.py:703
  75.3 17.1 %collective-permute-start.18 = (bf16[512,256]{1,0:T(8,128)(2,1)S(1)}, bf16[512,256]{1,0:T(8,128)(2,1)S(1)}, u32[]{:S(2)}, u32[]{:S(2)}) collective-permute-start(bf16[512,256]{1,0:T(8,128)(2,1)S(1)} %copy-done.40), channel_id=1, source_target_pairs={{0,3},{1,0},{2,1},{3,2},{4,7},{5,4},{6,5},{7,6},{8,11},{9,8},{10,9... | collective-permute-start | bytes 786440 | tf_op jit(solution)/shard_map/ppermute | solution.py:686
  77.3 15.2 %collective-permute-start.19 = (bf16[512,256]{1,0:T(8,128)(2,1)S(1)}, bf16[512,256]{1,0:T(8,128)(2,1)S(1)}, u32[]{:S(2)}, u32[]{:S(2)}) collective-permute-start(bf16[512,256]{1,0:T(8,128)(2,1)S(1)} %collective-permute-done.11.refs_10_), channel_id=1, source_target_pairs={{0,8},{4,12},{8,0},{12,4},{16,24},{20,28},{24,16},{28,20},{1,9},{5... | collective-permute-start | bytes 786440 | tf_op jit(solution)/shard_map/ppermute | solution.py:695
  78.6 13.8 %collective-permute-start.20 = (bf16[512,256]{1,0:T(8,128)(2,1)S(1)}, bf16[512,256]{1,0:T(8,128)(2,1)S(1)}, u32[]{:S(2)}, u32[]{:S(2)}) collective-permute-start(bf16[512,256]{1,0:T(8,128)(2,1)S(1)} %collective-permute-done.11.refs_10_), channel_id=1, source_target_pairs={{0,16},{4,20},{8,24},{12,28},{16,0},{20,4},{24,8},{28,12},{1,17},{... | collective-permute-start | bytes 786440 | tf_op jit(solution)/shard_map/ppermute | solution.py:695
  80.0 12.4 %collective-permute-start.21 = (bf16[512,256]{1,0:T(8,128)(2,1)S(1)}, bf16[512,256]{1,0:T(8,128)(2,1)S(1)}, u32[]{:S(2)}, u32[]{:S(2)}) collective-permute-start(bf16[512,256]{1,0:T(8,128)(2,1)S(1)} %collective-permute-done.11.refs_10_), channel_id=1, source_target_pairs={{0,24},{4,28},{8,16},{12,20},{16,8},{20,12},{24,0},{28,4},{1,25},{... | collective-permute-start | bytes 786440 | tf_op jit(solution)/shard_map/ppermute | solution.py:695
  92.5 6.2 %collective-permute-start.22 = (bf16[2,256,128]{2,1,0:T(8,128)(2,1)S(1)}, bf16[2,256,128]{2,1,0:T(8,128)(2,1)S(1)}, u32[]{:S(2)}, u32[]{:S(2)}) collective-permute-start(bf16[2,256,128]{2,1,0:T(8,128)(2,1)S(1)} %get-tuple-element.85), channel_id=1, source_target_pairs={{0,8},{4,12},{8,0},{12,4},{16,24},{20,28},{24,16},{28,20},{1,9},{5... | collective-permute-start | bytes 393224 | tf_op jit(solution)/shard_map/ppermute | solution.py:695
  93.9 7.4 %collective-permute-start.23 = (bf16[2,256,128]{2,1,0:T(8,128)(2,1)S(1)}, bf16[2,256,128]{2,1,0:T(8,128)(2,1)S(1)}, u32[]{:S(2)}, u32[]{:S(2)}) collective-permute-start(bf16[2,256,128]{2,1,0:T(8,128)(2,1)S(1)} %get-tuple-element.86), channel_id=1, source_target_pairs={{0,16},{4,20},{8,24},{12,28},{16,0},{20,4},{24,8},{28,12},{1,17},{... | collective-permute-start | bytes 393224 | tf_op jit(solution)/shard_map/ppermute | solution.py:695
  95.3 6.0 %collective-permute-start.24 = (bf16[2,256,128]{2,1,0:T(8,128)(2,1)S(1)}, bf16[2,256,128]{2,1,0:T(8,128)(2,1)S(1)}, u32[]{:S(2)}, u32[]{:S(2)}) collective-permute-start(bf16[2,256,128]{2,1,0:T(8,128)(2,1)S(1)} %get-tuple-element.87), channel_id=1, source_target_pairs={{0,24},{4,28},{8,16},{12,20},{16,8},{20,12},{24,0},{28,4},{1,25},{... | collective-permute-start | bytes 393224 | tf_op jit(solution)/shard_map/ppermute | solution.py:695
  101.3 41.3 %copy-start.33 = (f32[2048]{0:T(1024)S(1)}, f32[2048]{0:T(1024)}, u32[]{:S(2)}) copy-start(f32[2048]{0:T(1024)} %param.21) | copy-start | bytes 24580
  101.4 11.1 %collective-permute-start.28 = (bf16[2,2,256,128]{3,2,1,0:T(8,128)(2,1)S(1)}, bf16[2,2,256,128]{3,2,1,0:T(8,128)(2,1)S(1)}, u32[]{:S(2)}, u32[]{:S(2)}) collective-permute-start(bf16[2,2,256,128]{3,2,1,0:T(8,128)(2,1)S(1)} %pad_maximum_fusion.4.refs_4_), channel_id=1, source_target_pairs={{0,1},{1,2},{2,3},{3,0},{4,5},{5,6},{6,7},{7,4},{8,9},{9,10},{10,1... | collective-permute-start | bytes 786440 | tf_op jit(solution)/shard_map/ppermute | solution.py:673
  102.4 15.7 %collective-permute-start.25 = (bf16[2,2,256,128]{3,2,1,0:T(8,128)(2,1)S(1)}, bf16[2,2,256,128]{3,2,1,0:T(8,128)(2,1)S(1)}, u32[]{:S(2)}, u32[]{:S(2)}) collective-permute-start(bf16[2,2,256,128]{3,2,1,0:T(8,128)(2,1)S(1)} %pad_maximum_fusion.3.refs_0_), channel_id=1, source_target_pairs={{0,1},{1,2},{2,3},{3,0},{4,5},{5,6},{6,7},{7,4},{8,9},{9,10},{10,1... | collective-permute-start | bytes 786440 | tf_op jit(solution)/shard_map/ppermute | solution.py:673
  103.9 23.2 %collective-permute-start.33 = (bf16[2,512,256]{2,1,0:T(8,128)(2,1)S(1)}, bf16[2,512,256]{2,1,0:T(8,128)(2,1)}, u32[]{:S(2)}, u32[]{:S(2)}) collective-permute-start(bf16[2,512,256]{2,1,0:T(8,128)(2,1)S(1)} %pad_maximum_fusion.refs_14_), channel_id=1, source_target_pairs={{0,24},{4,28},{8,16},{12,20},{16,8},{20,12},{24,0},{28,4},{1,25},{... | collective-permute-start | bytes 1572872 | tf_op jit(solution)/shard_map/ppermute | solution.py:695
  112.5 11.1 %collective-permute-start.29 = (bf16[2,2,256,128]{3,2,1,0:T(8,128)(2,1)S(1)}, bf16[2,2,256,128]{3,2,1,0:T(8,128)(2,1)S(1)}, u32[]{:S(2)}, u32[]{:S(2)}) collective-permute-start(bf16[2,2,256,128]{3,2,1,0:T(8,128)(2,1)S(1)} %collective-permute-done.28.refs_5_), channel_id=1, source_target_pairs={{0,1},{1,2},{2,3},{3,0},{4,5},{5,6},{6,7},{7,4},{8,9},{9,10},{10,1... | collective-permute-start | bytes 786440 | tf_op jit(solution)/shard_map/ppermute | solution.py:673
  112.5 15.8 %collective-permute-start.32 = (bf16[2,512,256]{2,1,0:T(8,128)(2,1)S(1)}, bf16[2,512,256]{2,1,0:T(8,128)(2,1)}, u32[]{:S(2)}, u32[]{:S(2)}) collective-permute-start(bf16[2,512,256]{2,1,0:T(8,128)(2,1)S(1)} %pad_maximum_fusion.refs_14_), channel_id=1, source_target_pairs={{0,16},{4,20},{8,24},{12,28},{16,0},{20,4},{24,8},{28,12},{1,17},{... | collective-permute-start | bytes 1572872 | tf_op jit(solution)/shard_map/ppermute | solution.py:695
  113.5 14.8 %collective-permute-start.31 = (bf16[2,512,256]{2,1,0:T(8,128)(2,1)S(1)}, bf16[2,512,256]{2,1,0:T(8,128)(2,1)}, u32[]{:S(2)}, u32[]{:S(2)}) collective-permute-start(bf16[2,512,256]{2,1,0:T(8,128)(2,1)S(1)} %pad_maximum_fusion.refs_14_), channel_id=1, source_target_pairs={{0,8},{4,12},{8,0},{12,4},{16,24},{20,28},{24,16},{28,20},{1,9},{5... | collective-permute-start | bytes 1572872 | tf_op jit(solution)/shard_map/ppermute | solution.py:695
  118.1 8.3 %collective-permute-start.26 = (bf16[2,2,256,128]{3,2,1,0:T(8,128)(2,1)S(1)}, bf16[2,2,256,128]{3,2,1,0:T(8,128)(2,1)S(1)}, u32[]{:S(2)}, u32[]{:S(2)}) collective-permute-start(bf16[2,2,256,128]{3,2,1,0:T(8,128)(2,1)S(1)} %collective-permute-done.25.refs_1_), channel_id=1, source_target_pairs={{0,1},{1,2},{2,3},{3,0},{4,5},{5,6},{6,7},{7,4},{8,9},{9,10},{10,1... | collective-permute-start | bytes 786440 | tf_op jit(solution)/shard_map/ppermute | solution.py:673
  123.5 19.1 %collective-permute-start.34 = (bf16[4,1,512,256]{3,2,0,1:T(8,128)(2,1)}, bf16[4,1,512,256]{3,2,0,1:T(8,128)(2,1)}, u32[]{:S(2)}, u32[]{:S(2)}) collective-permute-start(bf16[4,1,512,256]{3,2,0,1:T(8,128)(2,1)} %maximum_bitcast_fusion), channel_id=1, source_target_pairs={{0,4},{4,0},{8,12},{12,8},{16,20},{20,16},{24,28},{28,24},{1,5},{5... | collective-permute-start | bytes 3145736 | tf_op jit(solution)/shard_map/ppermute | solution.py:703
  126.3 10.5 %collective-permute-start.30 = (bf16[2,2,256,128]{3,2,1,0:T(8,128)(2,1)S(1)}, bf16[2,2,256,128]{3,2,1,0:T(8,128)(2,1)S(1)}, u32[]{:S(2)}, u32[]{:S(2)}) collective-permute-start(bf16[2,2,256,128]{3,2,1,0:T(8,128)(2,1)S(1)} %collective-permute-done.29.refs_6_), channel_id=1, source_target_pairs={{0,1},{1,2},{2,3},{3,0},{4,5},{5,6},{6,7},{7,4},{8,9},{9,10},{10,1... | collective-permute-start | bytes 786440 | tf_op jit(solution)/shard_map/ppermute | solution.py:673
  127.1 12.6 %collective-permute-start.27 = (bf16[2,2,256,128]{3,2,1,0:T(8,128)(2,1)S(1)}, bf16[2,2,256,128]{3,2,1,0:T(8,128)(2,1)S(1)}, u32[]{:S(2)}, u32[]{:S(2)}) collective-permute-start(bf16[2,2,256,128]{3,2,1,0:T(8,128)(2,1)S(1)} %collective-permute-done.26.refs_2_), channel_id=1, source_target_pairs={{0,1},{1,2},{2,3},{3,0},{4,5},{5,6},{6,7},{7,4},{8,9},{9,10},{10,1... | collective-permute-start | bytes 786440 | tf_op jit(solution)/shard_map/ppermute | solution.py:673
  128.3 12.2 %collective-permute-start.35 = (bf16[2,512,256]{2,1,0:T(8,128)(2,1)S(1)}, bf16[2,512,256]{2,1,0:T(8,128)(2,1)}, u32[]{:S(2)}, u32[]{:S(2)}) collective-permute-start(bf16[2,512,256]{2,1,0:T(8,128)(2,1)S(1)} %pad_maximum_fusion.refs_14_), channel_id=1, source_target_pairs={{0,4},{4,0},{8,12},{12,8},{16,20},{20,16},{24,28},{28,24},{1,5},{5... | collective-permute-start | bytes 1572872 | tf_op jit(solution)/shard_map/ppermute | solution.py:703
  128.3 12.2 %collective-permute-start.38 = (bf16[2,512,256]{2,1,0:T(8,128)(2,1)}, bf16[2,512,256]{2,1,0:T(8,128)(2,1)}, u32[]{:S(2)}, u32[]{:S(2)}) collective-permute-start(bf16[2,512,256]{2,1,0:T(8,128)(2,1)} %collective-permute-done.33.refs_17_), channel_id=1, source_target_pairs={{0,4},{4,0},{8,12},{12,8},{16,20},{20,16},{24,28},{28,24},{1,5},{5... | collective-permute-start | bytes 1572872 | tf_op jit(solution)/shard_map/ppermute | solution.py:703
  137.6 3.0 %collective-permute-start.37 = (bf16[2,512,256]{2,1,0:T(8,128)(2,1)}, bf16[2,512,256]{2,1,0:T(8,128)(2,1)}, u32[]{:S(2)}, u32[]{:S(2)}) collective-permute-start(bf16[2,512,256]{2,1,0:T(8,128)(2,1)} %collective-permute-done.32.refs_16_), channel_id=1, source_target_pairs={{0,4},{4,0},{8,12},{12,8},{16,20},{20,16},{24,28},{28,24},{1,5},{5... | collective-permute-start | bytes 1572872 | tf_op jit(solution)/shard_map/ppermute | solution.py:703
  140.4 2.3 collective-permute-start.36
  180.1 8.3 %collective-permute-start.39 = (bf16[128,512]{1,0:T(8,128)(2,1)S(1)}, bf16[128,512]{1,0:T(8,128)(2,1)S(1)}, u32[]{:S(2)}, u32[]{:S(2)}) collective-permute-start(bf16[128,512]{1,0:T(8,128)(2,1)S(1)} %get-tuple-element.103), channel_id=1, source_target_pairs={{0,1},{1,2},{2,3},{3,0},{4,5},{5,6},{6,7},{7,4},{8,9},{9,10},{10,1... | collective-permute-start | bytes 393224 | tf_op jit(solution)/shard_map/ppermute | solution.py:686
  180.1 13.0 %collective-permute-start.40 = (bf16[128,512]{1,0:T(8,128)(2,1)S(1)}, bf16[128,512]{1,0:T(8,128)(2,1)S(1)}, u32[]{:S(2)}, u32[]{:S(2)}) collective-permute-start(bf16[128,512]{1,0:T(8,128)(2,1)S(1)} %get-tuple-element.104), channel_id=1, source_target_pairs={{0,2},{1,3},{2,0},{3,1},{4,6},{5,7},{6,4},{7,5},{8,10},{9,11},{10,... | collective-permute-start | bytes 393224 | tf_op jit(solution)/shard_map/ppermute | solution.py:686
  180.2 12.9 %collective-permute-start.41 = (bf16[128,512]{1,0:T(8,128)(2,1)S(1)}, bf16[128,512]{1,0:T(8,128)(2,1)S(1)}, u32[]{:S(2)}, u32[]{:S(2)}) collective-permute-start(bf16[128,512]{1,0:T(8,128)(2,1)S(1)} %get-tuple-element.105), channel_id=1, source_target_pairs={{0,3},{1,0},{2,1},{3,2},{4,7},{5,4},{6,5},{7,6},{8,11},{9,8},{10,9... | collective-permute-start | bytes 393224 | tf_op jit(solution)/shard_map/ppermute | solution.py:686
  193.2 14.4 %collective-permute-start.42 = (bf16[128,512]{1,0:T(8,128)(2,1)S(1)}, bf16[128,512]{1,0:T(8,128)(2,1)S(1)}, u32[]{:S(2)}, u32[]{:S(2)}) collective-permute-start(bf16[128,512]{1,0:T(8,128)(2,1)S(1)} %multiply_convert_fusion.3.refs_0_), channel_id=1, source_target_pairs={{0,1},{1,2},{2,3},{3,0},{4,5},{5,6},{6,7},{7,4},{8,9},{9,10},{10,1... | collective-permute-start | bytes 393224 | tf_op jit(solution)/shard_map/ppermute | solution.py:686
  195.8 11.8 %collective-permute-start.43 = (bf16[128,512]{1,0:T(8,128)(2,1)S(1)}, bf16[128,512]{1,0:T(8,128)(2,1)S(1)}, u32[]{:S(2)}, u32[]{:S(2)}) collective-permute-start(bf16[128,512]{1,0:T(8,128)(2,1)S(1)} %multiply_convert_fusion.3.refs_0_), channel_id=1, source_target_pairs={{0,2},{1,3},{2,0},{3,1},{4,6},{5,7},{6,4},{7,5},{8,10},{9,11},{10,... | collective-permute-start | bytes 393224 | tf_op jit(solution)/shard_map/ppermute | solution.py:686
  196.4 11.2 %collective-permute-start.44 = (bf16[128,512]{1,0:T(8,128)(2,1)S(1)}, bf16[128,512]{1,0:T(8,128)(2,1)S(1)}, u32[]{:S(2)}, u32[]{:S(2)}) collective-permute-start(bf16[128,512]{1,0:T(8,128)(2,1)S(1)} %multiply_convert_fusion.3.refs_0_), channel_id=1, source_target_pairs={{0,3},{1,0},{2,1},{3,2},{4,7},{5,4},{6,5},{7,6},{8,11},{9,8},{10,9... | collective-permute-start | bytes 393224 | tf_op jit(solution)/shard_map/ppermute | solution.py:686
  209.9 2.4 collective-permute-start.46
  209.9 14.3 %collective-permute-start.45 = (bf16[512,512]{1,0:T(8,128)(2,1)S(1)}, bf16[512,512]{1,0:T(8,128)(2,1)S(1)}, u32[]{:S(2)}, u32[]{:S(2)}) collective-permute-start(bf16[512,512]{1,0:T(8,128)(2,1)S(1)} %get-tuple-element.111), channel_id=1, source_target_pairs={{0,1},{1,0},{2,3},{3,2},{4,5},{5,4},{6,7},{7,6},{8,9},{9,8},{10,11... | collective-permute-start | bytes 1572872 | tf_op jit(solution)/shard_map/ppermute | solution.py:829
  224.4 23.6 %collective-permute-start.47 = (bf16[512,512]{1,0:T(8,128)(2,1)S(1)}, bf16[512,512]{1,0:T(8,128)(2,1)S(1)}, u32[]{:S(2)}, u32[]{:S(2)}) collective-permute-start(bf16[512,512]{1,0:T(8,128)(2,1)S(1)} %get-tuple-element.118), channel_id=1, source_target_pairs={{0,1},{1,0},{2,3},{3,2},{4,5},{5,4},{6,7},{7,6},{8,9},{9,8},{10,11... | collective-permute-start | bytes 1572872 | tf_op jit(solution)/shard_map/ppermute | solution.py:829
  225.4 25.4 %collective-permute-start.48 = (bf16[512,512]{1,0:T(8,128)(2,1)S(1)}, bf16[512,512]{1,0:T(8,128)(2,1)S(1)}, u32[]{:S(2)}, u32[]{:S(2)}) collective-permute-start(bf16[512,512]{1,0:T(8,128)(2,1)S(1)} %add_convert_fusion.1), channel_id=1, source_target_pairs={{0,2},{1,3},{2,0},{3,1},{4,6},{5,7},{6,4},{7,5},{8,10},{9,11},{10,... | collective-permute-start | bytes 1572872 | tf_op jit(solution)/shard_map/ppermute | solution.py:829
  227.0 8.2 %collective-permute-start.50 = (bf16[208,512]{1,0:T(8,128)(2,1)S(1)}, bf16[208,512]{1,0:T(8,128)(2,1)S(1)}, u32[]{:S(2)}, u32[]{:S(2)}) collective-permute-start(bf16[208,512]{1,0:T(8,128)(2,1)S(1)} %get-tuple-element.119), channel_id=1, source_target_pairs={{0,8},{4,12},{8,0},{12,4},{16,24},{20,28},{24,16},{28,20},{1,9},{5... | collective-permute-start | bytes 638984 | tf_op jit(solution)/shard_map/ppermute | solution.py:695
  227.0 10.8 %collective-permute-start.51 = (bf16[208,512]{1,0:T(8,128)(2,1)S(1)}, bf16[208,512]{1,0:T(8,128)(2,1)S(1)}, u32[]{:S(2)}, u32[]{:S(2)}) collective-permute-start(bf16[208,512]{1,0:T(8,128)(2,1)S(1)} %get-tuple-element.120), channel_id=1, source_target_pairs={{0,16},{4,20},{8,24},{12,28},{16,0},{20,4},{24,8},{28,12},{1,17},{... | collective-permute-start | bytes 638984 | tf_op jit(solution)/shard_map/ppermute | solution.py:695
  227.5 10.3 %collective-permute-start.52 = (bf16[208,512]{1,0:T(8,128)(2,1)S(1)}, bf16[208,512]{1,0:T(8,128)(2,1)S(1)}, u32[]{:S(2)}, u32[]{:S(2)}) collective-permute-start(bf16[208,512]{1,0:T(8,128)(2,1)S(1)} %get-tuple-element.121), channel_id=1, source_target_pairs={{0,24},{4,28},{8,16},{12,20},{16,8},{20,12},{24,0},{28,4},{1,25},{... | collective-permute-start | bytes 638984 | tf_op jit(solution)/shard_map/ppermute | solution.py:695
  238.0 13.7 %collective-permute-start.53 = (bf16[208,512]{1,0:T(8,128)(2,1)S(1)}, bf16[208,512]{1,0:T(8,128)(2,1)S(1)}, u32[]{:S(2)}, u32[]{:S(2)}) collective-permute-start(bf16[208,512]{1,0:T(8,128)(2,1)S(1)} %add_convert_fusion.2.refs_0_), channel_id=1, source_target_pairs={{0,8},{4,12},{8,0},{12,4},{16,24},{20,28},{24,16},{28,20},{1,9},{5... | collective-permute-start | bytes 638984 | tf_op jit(solution)/shard_map/ppermute | solution.py:695
  239.8 12.0 %collective-permute-start.54 = (bf16[208,512]{1,0:T(8,128)(2,1)S(1)}, bf16[208,512]{1,0:T(8,128)(2,1)S(1)}, u32[]{:S(2)}, u32[]{:S(2)}) collective-permute-start(bf16[208,512]{1,0:T(8,128)(2,1)S(1)} %add_convert_fusion.2.refs_0_), channel_id=1, source_target_pairs={{0,16},{4,20},{8,24},{12,28},{16,0},{20,4},{24,8},{28,12},{1,17},{... | collective-permute-start | bytes 638984 | tf_op jit(solution)/shard_map/ppermute | solution.py:695
  240.2 12.0 %collective-permute-start.55 = (bf16[208,512]{1,0:T(8,128)(2,1)S(1)}, bf16[208,512]{1,0:T(8,128)(2,1)S(1)}, u32[]{:S(2)}, u32[]{:S(2)}) collective-permute-start(bf16[208,512]{1,0:T(8,128)(2,1)S(1)} %add_convert_fusion.2.refs_0_), channel_id=1, source_target_pairs={{0,24},{4,28},{8,16},{12,20},{16,8},{20,12},{24,0},{28,4},{1,25},{... | collective-permute-start | bytes 638984 | tf_op jit(solution)/shard_map/ppermute | solution.py:695
  251.1 6.4 %collective-permute-start.49 = (bf16[256,512]{1,0:T(8,128)(2,1)S(1)}, bf16[256,512]{1,0:T(8,128)(2,1)S(1)}, u32[]{:S(2)}, u32[]{:S(2)}) collective-permute-start(bf16[256,512]{1,0:T(8,128)(2,1)S(1)} %get-tuple-element.131), channel_id=1, source_target_pairs={{0,4},{4,0},{8,12},{12,8},{16,20},{20,16},{24,28},{28,24},{1,5},{5... | collective-permute-start | bytes 786440 | tf_op jit(solution)/shard_map/ppermute | solution.py:703
  251.2 1.8 collective-permute-start.56
  251.7 1.6 collective-permute-start.57
  251.8 1.9 collective-permute-start.58
  252.2 1.7 collective-permute-start.59
  (41 other events, 430.0 us)

commit v4 on v3

--- a/solution.py
+++ b/solution.py
@@ -220,7 +220,7 @@
                 head = head * factor
             made[h, kind] = head.astype(BF16)
     for f in range(heads):
-        outs[f][...] = made[info_ref[ring] ^ f]
+        outs[f][...] = made[info_ref[ring + 1] ^ f]
     stamp_ref[...] = jnp.zeros_like(stamp_ref)
 
 
@@ -256,11 +256,11 @@
     return result[:heads], result[heads], result[heads + 1]
 
 
-def attention_kernel(info_ref, *refs, chips):
+def attention_kernel(first_ref, info_ref, *refs, chips, ring):
     own, other = refs[:chips], refs[chips : 2 * chips]
     outs = refs[2 * chips : 3 * chips]
     keys_all, values_all = refs[3 * chips :]
-    chip, core = info_ref[SERIES], info_ref[SERIES + 1]
+    chip, core = info_ref[ring + 1], info_ref[ring + 2]
     half = outs[0].shape[1]
     span = 2 * half
     for f in range(chips):
@@ -274,7 +274,7 @@
     def first_of(row):
         found = jnp.int32(0)
         for s in range(SERIES):
-            edge = info_ref[s]
+            edge = first_ref[s]
             found = jnp.where(edge <= row, jnp.maximum(found, edge), found)
         return found
 
@@ -287,7 +287,7 @@
         row = first_row + place + jnp.where(place < half, 0, half)
         start = jnp.zeros((1, span), jnp.int32)
         for s in range(SERIES):
-            edge = info_ref[s]
+            edge = first_ref[s]
             start = jnp.where(edge <= row, jnp.maximum(start, edge), start)
         lane = lax.broadcasted_iota(jnp.int32, (span, 1), 0)
 
@@ -325,14 +325,14 @@
         outs[f][1 - core] = (accum / denom).T.astype(BF16)
 
 
-def attention_call(info, own, other):
+def attention_call(first, info, own, other, ring):
     chips = len(own)
     _, _, half, _ = own[0].shape
     return pl.pallas_call(
-        functools.partial(attention_kernel, chips=chips),
+        functools.partial(attention_kernel, chips=chips, ring=ring),
         out_shape=[jax.ShapeDtypeStruct((2, half, HD), BF16)] * chips,
         grid_spec=pltpu.PrefetchScalarGridSpec(
-            num_scalar_prefetch=1,
+            num_scalar_prefetch=2,
             grid=(1,),
             in_specs=[whole((3, 2, half, HD))] * (2 * chips),
             out_specs=[whole((2, half, HD))] * chips,
@@ -348,7 +348,7 @@
             2 * chips * half * 4 * chips * half // 2,
         ),
         name="attention",
-    )(info, *own, *other)
+    )(first, info, *own, *other)
 
 
 def middle_kernel(info_ref, *refs, ring, chips):
@@ -363,7 +363,7 @@
     pieces = refs[8 : 8 + ring]
     attended, mixed, total, near, far, gates, ups, wp, proj, sems = refs[8 + ring :]
     step = pl.program_id(0)
-    level, chip, core = info_ref[0], info_ref[1], info_ref[2]
+    level, chip, core = info_ref[ring], info_ref[ring + 1], info_ref[ring + 2]
     rows, depth = mixed.shape
     half = rows // 2
     width = own_ref.shape[1]
@@ -406,7 +406,7 @@
     def _():
         for c in heads + slices[0]:
             c.start()
-        for c in sum(slices[1:], []) + late + sum(units, []):
+        for c in sum(slices[1:], []) + late:
             c.start()
         for c in heads:
             c.wait()
@@ -417,6 +417,8 @@
         def _(f=f):
             for c in slices[f]:
                 c.wait()
+            for c in sum(units[f::chips], []):
+                c.start()
 
     @pl.when(step < chips)
     def _():
@@ -458,7 +460,7 @@
     def _():
         size = rows // ring
         for s in range(ring):
-            at = pl.ds(pl.multiple_of((level + s) % ring * size, size), size)
+            at = pl.ds(pl.multiple_of(((level + s) & (ring - 1)) * size, size), size)
             pieces[s][...] = total[at, :].astype(BF16)
 
 
@@ -470,7 +472,7 @@
     width = depth // ring
     sd = projector.shape[1]
     blocks = units // wide
-    tile = lambda j, info: (0, jnp.minimum(j, chips - 1) ^ info[1])
+    tile = lambda j, info: (0, jnp.minimum(j, chips - 1) ^ info[ring + 1])
     late = lambda j, info: (0, jnp.maximum(j - chips, 0))
     anywhere = pl.BlockSpec(memory_space=pl.ANY)
     count = 2 * ring * parts[0][0].shape[0] * 2 + 4 * chips + 2 + 3 * blocks
@@ -534,7 +536,7 @@
     return result[0], result[1], result[2:]
 
 
-def down_kernel(level_ref, hidden_ref, weight_ref, *outs):
+def down_kernel(info_ref, hidden_ref, weight_ref, *outs):
     result = dot(hidden_ref[...], weight_ref[...]).astype(BF16)
     for j, out in enumerate(outs):
 
@@ -543,7 +545,7 @@
             out[...] = result
 
 
-def down_call(level, hidden, w_down, ring):
+def down_call(info, hidden, w_down, ring):
     rows, units = hidden.shape
     depth = w_down.shape[1]
     width = depth // ring
@@ -555,21 +557,21 @@
             grid=(ring,),
             in_specs=[
                 whole((rows, units)),
-                pl.BlockSpec((units, width), lambda j, level: (0, level[0] ^ (ring - 1 - j))),
+                pl.BlockSpec((units, width), lambda j, info: (0, info[ring] ^ (ring - 1 - j))),
             ],
             out_specs=[whole((rows, width))] * ring,
         ),
         compiler_params=params(24),
         cost_estimate=cost(2 * rows * units * depth, 2 * units * depth),
         name="down",
-    )(level, hidden, w_down)
+    )(info, hidden, w_down)
 
 
 def grads_kernel(info_ref, *refs, ring, chips):
     pieces = refs[:ring]
     normed_ref, hidden_ref, s_down_ref, up_ref, gate_ref = refs[ring : ring + 5]
     keep_ref, give_ref, scaled, grads = refs[ring + 5 :]
-    chip, core = info_ref[ring], info_ref[ring + 1]
+    chip, core = info_ref[ring + 1], info_ref[ring + 2]
     size, sd = pieces[0].shape
     for s in range(ring):
         scaled[pl.ds(pl.multiple_of(info_ref[s] * size, size), size), :] = pieces[s][...]
@@ -633,11 +635,11 @@
     )(keep, theirs)
 
 
-def finish_kernel(info_ref, *refs, chips):
+def finish_kernel(info_ref, *refs, chips, ring):
     mine, others = refs[:chips], refs[chips : 2 * chips]
     outs = refs[2 * chips : 2 * chips + 3]
     notes = refs[2 * chips + 3]
-    chip, core = info_ref[0], info_ref[1]
+    chip, core = info_ref[ring + 1], info_ref[ring + 2]
     share = (mine[0].shape[0] - NOTE) // 3
     for f in range(chips):
         for part, ref in ((core, mine[f]), (1 - core, others[f])):
@@ -648,12 +650,12 @@
             notes[index] = ref[3 * share :, :HD].astype(F32)
 
 
-def finish_call(info, mine, others):
+def finish_call(info, mine, others, ring):
     chips = len(mine)
     share, sd = mine[0].shape
     rows = (share - NOTE) // 3 * 2 * chips
     return pl.pallas_call(
-        functools.partial(finish_kernel, chips=chips),
+        functools.partial(finish_kernel, chips=chips, ring=ring),
         out_shape=[jax.ShapeDtypeStruct((rows, sd), F32)] * 3
         + [jax.ShapeDtypeStruct((2 * chips, NOTE, HD), F32)],
         grid_spec=pltpu.PrefetchScalarGridSpec(
@@ -731,15 +733,26 @@
     dp, ring = lax.axis_size("dp"), lax.axis_size("tensor")
     here, level = lax.axis_index("dp"), lax.axis_index("tensor")
     chips, half = dp // 2, rows // 2
-    chip, core = here // 2, here % 2
     total_rows = rows * dp
-    number = lambda *values: jnp.stack([jnp.asarray(v, jnp.int32) for v in values])
-    source = [(level - s) % ring for s in range(ring)]
+    size = rows // ring
+    slice_cols = depth // dp
+
+    places = [(level - s) & (ring - 1) for s in range(ring)] + [level, here >> 1, here & 1]
+    slots = lax.broadcasted_iota(jnp.int32, (16,), 0)
+    info = sum(jnp.where(slots == k, place, 0) for k, place in enumerate(places))
+    starts = jnp.stack([here & 1, (here & 1) ^ 1, level * size, here * slice_cols])
+    *starts, zero = [starts[k].astype(jnp.uint32) for k in range(4)] + [jnp.uint32(0)]
+    first_core = (here & 1) == 0
+    tokens, info, first_core, *starts = lax.optimization_barrier(
+        (tokens, info, first_core, *starts)
+    )
 
     def deal(value):
         parts = value.reshape((2, half) + value.shape[1:])
-        kept = lax.dynamic_index_in_dim(parts, core, 0, False)
-        return kept, swapped(lax.dynamic_index_in_dim(parts, 1 - core, 0, False))
+        shape = (1,) + parts.shape[1:]
+        rest = [zero] * (parts.ndim - 1)
+        kept, given = [lax.dynamic_slice(parts, [k, *rest], shape)[0] for k in starts[:2]]
+        return kept, swapped(given)
 
     token_chunks = deal(tokens)
     token_rings = [ring_gather(chunk, "tensor") for chunk in token_chunks]
@@ -756,7 +769,6 @@
         series_ids[None, :] < jnp.arange(SERIES, dtype=jnp.int32)[:, None], axis=1, dtype=jnp.int32
     )
 
-    info = number(*source, chip)
     made, tok_full, stamp = qkv_call(
         info, token_rings, norm_gain[None, :], cosine, sine, w_query, w_key, w_value
     )
@@ -772,10 +784,10 @@
     up_slope, gate_slope = up_slope.astype(BF16), gate_slope.astype(BF16)
     student_part = dot(s_hidden, s_down)
     projected = dot(w_down, held[1]).astype(BF16)
-    early = (projected, student_part, s_hidden, up_slope, gate_slope, student_normed)
-
-    slice_cols = depth // dp
-    w_slice = lax.dynamic_slice_in_dim(w_out, here * slice_cols, slice_cols, 1)
+    student_own = lax.dynamic_slice(student_full, [starts[2], zero], (size, sd))
+    early = (projected, student_part, s_hidden, up_slope, gate_slope, student_normed, student_own)
+
+    w_slice = lax.dynamic_slice(w_out, [zero, starts[3]], (w_out.shape[0], slice_cols))
     w_slice = after(w_slice, stamp)
     w_others = shifted([w_slice] * ring, "tensor")[1:]
 
@@ -786,9 +798,7 @@
     near_first = flipped([w_others[0]] * chips)
     pairs = lambda a: a.reshape(3, 2, half, HD)
     made = attention_call(
-        jnp.concatenate([below, number(chip, core)]),
-        [pairs(a) for a in own],
-        [pairs(a) for a in other],
+        below, info, [pairs(a) for a in own], [pairs(a) for a in other], ring
     )
     held = lax.optimization_barrier((*made, *w_others[1:], *near_first))
     made, w_rest = held[:chips], jnp.stack(held[chips : chips + ring - 2])
@@ -802,7 +812,7 @@
     far_rest = [swapped(after(a, parts[1][1])) for a in near_rest]
 
     hidden, mixed_own, pieces = middle_call(
-        number(level, chip, core),
+        info,
         parts,
         tok_full,
         w_out,
@@ -816,21 +826,20 @@
         student_part,
     )
 
-    size = rows // ring
-    own = lax.dynamic_slice_in_dim(student_full, level * size, size, 0)
+    own = student_own
     moved = shifted(pieces, "tensor")
     difference = own + sum(piece.astype(F32) for piece in moved)
     own = (difference * total_rows ** (-0.5)).astype(BF16)
     scaled = shifted([own] * ring, "tensor")
 
     far_theirs, far_mine, near_theirs, kept = down_call(
-        level.astype(jnp.int32)[None], after(hidden, *moved[1:]), w_down, ring
+        info, after(hidden, *moved[1:]), w_down, ring
     )
     over = lambda value, bit: lax.ppermute(value, "tensor", [(i, i ^ bit) for i in range(ring)])
     far_sum = over(after(far_theirs, *scaled), 1)
 
     keep, give = grads_call(
-        after(number(*source, chip, core), kept),
+        after(info, kept),
         scaled,
         student_normed,
         s_hidden,
@@ -839,25 +848,23 @@
         gate_slope,
         chips,
     )
-    shares = pair_call(keep, swapped(give))
-    far_sum = after(far_sum, shares[0]).astype(F32) + far_mine.astype(F32)
-    far_sum = far_sum.astype(BF16)
-    shares = flipped(shares)
+    far_sum = (after(far_sum, keep).astype(F32) + far_mine.astype(F32)).astype(BF16)
+    shares = flipped(pair_call(keep, after(swapped(give), far_sum)))
     own = sum(share.astype(F32) for share in shares).astype(BF16)
-    own = after(own, far_sum)
     mine = flipped([own] * chips)
     others = [swapped(share) for share in mine]
 
-    mlp_own = over(after(near_theirs, far_sum), 1).astype(F32) + over(far_sum, 2).astype(F32)
+    level_sums = [over(after(near_theirs, far_sum), 1), over(far_sum, 2)]
+    mlp_own = sum(after(value, mine[-1]).astype(F32) for value in level_sums)
     teacher = mixed_own.astype(F32) + (kept.astype(F32) + mlp_own)
     teacher = teacher.astype(BF16)
     back = swapped(teacher[half:])
     teacher_out = jnp.where(
-        core == 0,
+        first_core,
         jnp.concatenate([teacher[:half], back], axis=0),
         jnp.concatenate([back, teacher[:half]], axis=0),
     )
-    grad_gate, grad_up, grad_down, notes = finish_call(number(chip, core), mine, others)
+    grad_gate, grad_up, grad_down, notes = finish_call(info, mine, others, ring)
     return teacher_out, grad_gate, grad_up, grad_down, notes[0, 0, 0] / sd
 
 

time: 260 us -> 243 us (0.935)
  local copies, waits for them, and re-layouts: 24.2 us -> 5.69 us
  waiting for transfers between devices: 111 us -> 124 us
  other arithmetic: 8.73 us -> 4.47 us
  starting transfers between devices: 47.5 us -> 43.8 us
  Pallas kernels: 57.1 us -> 54.2 us
    unnamed x90 -> x28, local copies, waits for them, and re-layouts: 18.7 us -> 1.85 us
    ppermute x12, waiting for transfers between devices: 56.7 us -> 61.8 us  [step_on(): return lax.ppermute(block, axis, [(i, (i + 1) % size) for i in range(size)])]
    ppermute x3, waiting for transfers between devices: 21.1 us -> 26.1 us  [paired(): lax.ppermute(value, 'tensor', [(i, i ^ bit) for i in range(ring)])]
    pallas_call x1, Pallas kernels: 26.9 us -> 22.3 us  [middle_call(): pl.pallas_call(functools.partial(middle_kernel, ring=ring, chips=chips),...]
    ppermute x9, waiting for transfers between devices: 13.7 us -> 17.4 us  [shifted(): lax.ppermute(pieces[s], axis, [(i, (i + s) % size) for i in range(size)])]
  transfers between devices with their start and end apart: 60 -> 60, of which waited for: 29 -> 29; matrix products, arithmetic and copies ran while one was open for 8% -> 6% of each run, Pallas kernels for 8% -> 9%
where the time goes in v4:
time: 243 us
  waiting for transfers between devices  124 us (51%)
  Pallas kernels  54.2 us (22%)
  starting transfers between devices  43.8 us (18%)
  matrix products  7.37 us (3%)
  local copies, waits for them, and re-layouts  5.69 us (2%)
  other arithmetic  4.47 us (2%)
  between operations  2.92 us (1%)
    ppermute x12, waiting for transfers between devices, step_on(): return lax.ppermute(block, axis, [(i, (i + 1) % size) for i in range(size)])  61.8 us
    ppermute x3, waiting for transfers between devices, paired(): lax.ppermute(value, 'tensor', [(i, i ^ bit) for i in range(ring)])  26.1 us
    pallas_call x1, Pallas kernels, middle_call(): pl.pallas_call(functools.partial(middle_kernel, ring=ring, chips=chips),...  22.3 us
    ppermute x18, starting transfers between devices, flipped(): lax.ppermute(pieces[f], 'dp', [(i, i ^ 2 * f) for i in range(size)])  20.8 us
    ppermute x9, waiting for transfers between devices, shifted(): lax.ppermute(pieces[s], axis, [(i, (i + s) % size) for i in range(size)])  17.4 us
    ppermute x18, waiting for transfers between devices, flipped(): lax.ppermute(pieces[f], 'dp', [(i, i ^ 2 * f) for i in range(size)])  15.5 us
    pallas_call x1, Pallas kernels, attention_call(): pl.pallas_call(functools.partial(attention_kernel, chips=chips, ring=ring...  13.8 us
    ppermute x9, starting transfers between devices, shifted(): lax.ppermute(pieces[s], axis, [(i, (i + s) % size) for i in range(size)])  12.6 us
  transfers between devices with their start and end apart: 60, of which 29 were waited for; matrix products, arithmetic and copies ran while one was open for 6% of the time, Pallas kernels for 9%

profile of v4, /device:TPU:0, one launch (start us, length us, event | category | flops | bytes accessed | tf_op | source)
XLA Modules:
  0.0 242.8 jit_solution(707134629378764347)
XLA Ops:
  0.7 0.7 convert_element_type.104
  1.9 1.1 dynamic-slice_bitcast_fusion.2
  3.1 3.0 %collective-permute-start = (bf16[256,512]{1,0:T(8,128)(2,1)S(1)}, bf16[256,512]{1,0:T(8,128)(2,1)S(1)}, u32[]{:S(2)}, u32[]{:S(2)}) collective-permute-start(bf16[256,512]{1,0:T(8,128)(2,1)S(1)} %get-tuple-element.153.refs_0_), channel_id=1, source_target_pairs={{0,1},{1,2},{2,3},{3,0},{4,5},{5,6},{6,7},{7,4},{8,9},{9,10},{10,1... | collective-permute-start | bytes 786440 | tf_op jit(solution)/shard_map/ppermute | solution.py:675
  6.2 1.1 dynamic-slice_bitcast_fusion.1
  7.3 1.1 constant_dynamic-slice_fusion.1
  8.5 1.6 collective-permute-start.4
  10.1 1.0 fusion.3
  11.4 3.9 %collective-permute-done.refs_1_ = bf16[256,512]{1,0:T(8,128)(2,1)S(1)} collective-permute-done((bf16[256,512]{1,0:T(8,128)(2,1)S(1)}, bf16[256,512]{1,0:T(8,128)(2,1)S(1)}, u32[]{:S(2)}, u32[]{:S(2)}) %collective-permute-start) | collective-permute-done | bytes 262176 | tf_op jit(solution)/shard_map/ppermute | solution.py:675
  15.3 5.6 %collective-permute-done.4.refs_5_ = bf16[256,512]{1,0:T(8,128)(2,1)S(1)} collective-permute-done((bf16[256,512]{1,0:T(8,128)(2,1)S(1)}, bf16[256,512]{1,0:T(8,128)(2,1)S(1)}, u32[]{:S(2)}, u32[]{:S(2)}) %collective-permute-start.4) | collective-permute-done | bytes 262176 | tf_op jit(solution)/shard_map/ppermute | solution.py:675
  21.3 5.2 %collective-permute-done.1.refs_2_ = bf16[256,512]{1,0:T(8,128)(2,1)S(1)} collective-permute-done((bf16[256,512]{1,0:T(8,128)(2,1)S(1)}, bf16[256,512]{1,0:T(8,128)(2,1)S(1)}, u32[]{:S(2)}, u32[]{:S(2)}) %collective-permute-start.1) | collective-permute-done | bytes 262176 | tf_op jit(solution)/shard_map/ppermute | solution.py:675
  26.6 5.6 %collective-permute-done.5.refs_6_ = bf16[256,512]{1,0:T(8,128)(2,1)S(1)} collective-permute-done((bf16[256,512]{1,0:T(8,128)(2,1)S(1)}, bf16[256,512]{1,0:T(8,128)(2,1)S(1)}, u32[]{:S(2)}, u32[]{:S(2)}) %collective-permute-start.5) | collective-permute-done | bytes 262176 | tf_op jit(solution)/shard_map/ppermute | solution.py:675
  32.3 5.4 %collective-permute-done.2.refs_3_ = bf16[256,512]{1,0:T(8,128)(2,1)S(1)} collective-permute-done((bf16[256,512]{1,0:T(8,128)(2,1)S(1)}, bf16[256,512]{1,0:T(8,128)(2,1)S(1)}, u32[]{:S(2)}, u32[]{:S(2)}) %collective-permute-start.2) | collective-permute-done | bytes 262176 | tf_op jit(solution)/shard_map/ppermute | solution.py:675
  37.8 5.1 %collective-permute-done.6.refs_7_ = bf16[256,512]{1,0:T(8,128)(2,1)S(1)} collective-permute-done((bf16[256,512]{1,0:T(8,128)(2,1)S(1)}, bf16[256,512]{1,0:T(8,128)(2,1)S(1)}, u32[]{:S(2)}, u32[]{:S(2)}) %collective-permute-start.6) | collective-permute-done | bytes 262176 | tf_op jit(solution)/shard_map/ppermute | solution.py:675
  42.8 6.8 %qkv.1 = (bf16[3,512,128]{2,1,0:T(8,128)(2,1)S(1)}, bf16[3,512,128]{2,1,0:T(8,128)(2,1)S(1)}, bf16[3,512,128]{2,1,0:T(8,128)(2,1)S(1)}, bf16[3,512,128]{2,1,0:T(...) custom-call(s32[16]{0:T(128)S(1)} %fusion.9.info_ref, bf16[256,512]{1,0:T(8,128)(2,1)S(1)} %get-tuple-element.153.refs_0_, ...), custom_call_target="tpu_custom_call" | custom-call | flops 3221225472 | bytes 6291456 | tf_op jit(solution)/shard_map/qkv/pallas_call | solution.py:232
  49.7 0.8 collective-permute-start.12
  50.5 1.6 collective-permute-start.11
  52.1 1.5 collective-permute-start.8
  53.6 1.5 collective-permute-start.9
  56.0 5.7 %fusion.refs_26_ = bf16[2048,512]{1,0:T(8,128)(2,1)} fusion(bf16[2048,2048]{1,0:T(8,128)(2,1)S(1)} %bitcast.52, bf16[2048,512]{1,0:T(8,128)(2,1)S(1)} %copy-done.11), kind=kOutput, calls=%fused_computation.1 | convolution fusion | flops 4296015872 | bytes 12582912 | tf_op jit(solution)/shard_map/dot_general | solution.py:166
  61.7 0.8 multiply_convert_fusion
  63.2 5.3 %collective-permute-done.12 = bf16[512,256]{1,0:T(8,128)(2,1)S(1)} collective-permute-done((bf16[512,256]{1,0:T(8,128)(2,1)S(1)}, bf16[512,256]{1,0:T(8,128)(2,1)S(1)}, u32[]{:S(2)}, u32[]{:S(2)}) %collective-permute-start.12) | collective-permute-done | bytes 262176 | tf_op jit(solution)/shard_map/ppermute | solution.py:688
  68.5 2.9 %collective-permute-done.9 = bf16[3,512,128]{2,1,0:T(8,128)(2,1)S(1)} collective-permute-done((bf16[3,512,128]{2,1,0:T(8,128)(2,1)S(1)}, bf16[3,512,128]{2,1,0:T(8,128)(2,1)S(1)}, u32[]{:S(2)}, u32[]{:S(2)}) %collective-permute-start.9) | collective-permute-done | bytes 393248 | tf_op jit(solution)/shard_map/ppermute | solution.py:697
  72.4 2.2 collective-permute-start.18
  74.7 1.5 collective-permute-start.21
  76.2 1.2 collective-permute-start.20
  77.4 0.8 collective-permute-start.19
  78.3 13.8 %attention.1 = (bf16[2,256,128]{2,1,0:T(8,128)(2,1)S(1)}, bf16[2,256,128]{2,1,0:T(8,128)(2,1)S(1)}, bf16[2,256,128]{2,1,0:T(8,128)(2,1)S(1)}, bf16[2,256,128]{2,1,0:T(8,128)(2,1)S(1)}) custom-call(s32[8]{0:T(128)S(1)} %convert_reduce_fusion.first_ref, s32[16]{0:T(128)S(1)} %fusion.9.info_ref, bf16[3,2,256,128]{3,2,1,0:T(8,128)(2,1)S(1)} %bitcast.54, ...), custom_call_target="tpu_custom_call" | custom-call | flops 2147483648 | bytes 3145728 | tf_op jit(solution)/shard_map/attention/pallas_call | solution.py:331
  92.1 1.3 collective-permute-start.22
  93.4 0.8 collective-permute-start.23
  94.2 1.5 collective-permute-start.24
  95.7 1.5 collective-permute-done.22
  97.2 1.2 collective-permute-done.23
  98.4 2.2 collective-permute-done.24
  101.3 1.5 collective-permute-start.33
  102.9 7.9 %collective-permute-done.25.refs_1_ = bf16[2,2,256,128]{3,2,1,0:T(8,128)(2,1)S(1)} collective-permute-done((bf16[2,2,256,128]{3,2,1,0:T(8,128)(2,1)S(1)}, bf16[2,2,256,128]{3,2,1,0:T(8,128)(2,1)S(1)}, u32[]{:S(2)}, u32[]{:S(2)}) %collective-permute-start.25) | collective-permute-done | bytes 262176 | tf_op jit(solution)/shard_map/ppermute | solution.py:675
  110.8 1.3 collective-permute-start.32
  112.4 4.0 %collective-permute-done.28.refs_5_ = bf16[2,2,256,128]{3,2,1,0:T(8,128)(2,1)S(1)} collective-permute-done((bf16[2,2,256,128]{3,2,1,0:T(8,128)(2,1)S(1)}, bf16[2,2,256,128]{3,2,1,0:T(8,128)(2,1)S(1)}, u32[]{:S(2)}, u32[]{:S(2)}) %collective-permute-start.28) | collective-permute-done | bytes 262176 | tf_op jit(solution)/shard_map/ppermute | solution.py:675
  116.6 3.5 %collective-permute-done.26.refs_2_ = bf16[2,2,256,128]{3,2,1,0:T(8,128)(2,1)S(1)} collective-permute-done((bf16[2,2,256,128]{3,2,1,0:T(8,128)(2,1)S(1)}, bf16[2,2,256,128]{3,2,1,0:T(8,128)(2,1)S(1)}, u32[]{:S(2)}, u32[]{:S(2)}) %collective-permute-start.26) | collective-permute-done | bytes 262176 | tf_op jit(solution)/shard_map/ppermute | solution.py:675
  120.1 4.5 %collective-permute-done.29.refs_6_ = bf16[2,2,256,128]{3,2,1,0:T(8,128)(2,1)S(1)} collective-permute-done((bf16[2,2,256,128]{3,2,1,0:T(8,128)(2,1)S(1)}, bf16[2,2,256,128]{3,2,1,0:T(8,128)(2,1)S(1)}, u32[]{:S(2)}, u32[]{:S(2)}) %collective-permute-start.29) | collective-permute-done | bytes 262176 | tf_op jit(solution)/shard_map/ppermute | solution.py:675
  125.2 8.2 %collective-permute-done.27.refs_3_ = bf16[2,2,256,128]{3,2,1,0:T(8,128)(2,1)S(1)} collective-permute-done((bf16[2,2,256,128]{3,2,1,0:T(8,128)(2,1)S(1)}, bf16[2,2,256,128]{3,2,1,0:T(8,128)(2,1)S(1)}, u32[]{:S(2)}, u32[]{:S(2)}) %collective-permute-start.27) | collective-permute-done | bytes 262176 | tf_op jit(solution)/shard_map/ppermute | solution.py:675
  133.4 2.8 %collective-permute-done.30.refs_7_ = bf16[2,2,256,128]{3,2,1,0:T(8,128)(2,1)S(1)} collective-permute-done((bf16[2,2,256,128]{3,2,1,0:T(8,128)(2,1)S(1)}, bf16[2,2,256,128]{3,2,1,0:T(8,128)(2,1)S(1)}, u32[]{:S(2)}, u32[]{:S(2)}) %collective-permute-start.30) | collective-permute-done | bytes 262176 | tf_op jit(solution)/shard_map/ppermute | solution.py:675
  136.2 1.9 collective-permute-done.36.refs_20_
  138.1 22.3 %middle.1 = (bf16[512,2048]{1,0:T(8,128)(2,1)}, bf16[512,512]{1,0:T(8,128)(2,1)S(1)}, bf16[128,512]{1,0:T(8,128)(2,1)S(1)}, bf16[128,512]{1,0:T(8,128)(2,1)S(1)}...) custom-call(s32[16]{0:T(128)S(1)} %fusion.9.info_ref, ...), custom_call_target="tpu_custom_call" | custom-call | flops 14227079168 | bytes 25165824 | tf_op jit(solution)/shard_map/middle/pallas_call | solution.py:479
  160.6 3.7 %collective-permute-start.41 = (bf16[128,512]{1,0:T(8,128)(2,1)S(1)}, bf16[128,512]{1,0:T(8,128)(2,1)S(1)}, u32[]{:S(2)}, u32[]{:S(2)}) collective-permute-start(bf16[128,512]{1,0:T(8,128)(2,1)S(1)} %get-tuple-element.121), channel_id=1, source_target_pairs={{0,3},{1,0},{2,1},{3,2},{4,7},{5,4},{6,5},{7,6},{8,11},{9,8},{10,9... | collective-permute-start | bytes 393224 | tf_op jit(solution)/shard_map/ppermute | solution.py:688
  164.3 4.5 %collective-permute-done.39 = bf16[128,512]{1,0:T(8,128)(2,1)S(1)} collective-permute-done((bf16[128,512]{1,0:T(8,128)(2,1)S(1)}, bf16[128,512]{1,0:T(8,128)(2,1)S(1)}, u32[]{:S(2)}, u32[]{:S(2)}) %collective-permute-start.39) | collective-permute-done | bytes 131104 | tf_op jit(solution)/shard_map/ppermute | solution.py:688
  168.8 4.7 %collective-permute-done.40 = bf16[128,512]{1,0:T(8,128)(2,1)S(1)} collective-permute-done((bf16[128,512]{1,0:T(8,128)(2,1)S(1)}, bf16[128,512]{1,0:T(8,128)(2,1)S(1)}, u32[]{:S(2)}, u32[]{:S(2)}) %collective-permute-start.40) | collective-permute-done | bytes 131104 | tf_op jit(solution)/shard_map/ppermute | solution.py:688
  173.6 2.7 %collective-permute-start.44 = (bf16[128,512]{1,0:T(8,128)(2,1)S(1)}, bf16[128,512]{1,0:T(8,128)(2,1)S(1)}, u32[]{:S(2)}, u32[]{:S(2)}) collective-permute-start(bf16[128,512]{1,0:T(8,128)(2,1)S(1)} %multiply_convert_fusion.3.refs_0_), channel_id=1, source_target_pairs={{0,3},{1,0},{2,1},{3,2},{4,7},{5,4},{6,5},{7,6},{8,11},{9,8},{10,9... | collective-permute-start | bytes 393224 | tf_op jit(solution)/shard_map/ppermute | solution.py:688
  176.2 1.4 collective-permute-start.43
  177.7 1.6 copy-done.8
  179.3 6.5 %down.1 = (bf16[512,512]{1,0:T(8,128)(2,1)S(1)}, bf16[512,512]{1,0:T(8,128)(2,1)S(1)}, bf16[512,512]{1,0:T(8,128)(2,1)S(1)}, bf16[512,512]{1,0:T(8,128)(2,1)S(1)}) custom-call(s32[16]{0:T(128)S(1)} %fusion.9.info_ref, bf16[512,2048]{1,0:T(8,128)(2,1)S(1)} %copy-done.8, bf16[2048,2048]{1,0:T(8,128)(2,1)S(1)} %bitcast.52), custom_call_target="tpu_custom_call" | custom-call | flops 4294967296 | bytes 8388608 | tf_op jit(solution)/shard_map/down/pallas_call | solution.py:552
  185.8 3.0 %collective-permute-done.43.refs_2_ = bf16[128,512]{1,0:T(8,128)(2,1)S(1)} collective-permute-done((bf16[128,512]{1,0:T(8,128)(2,1)S(1)}, bf16[128,512]{1,0:T(8,128)(2,1)S(1)}, u32[]{:S(2)}, u32[]{:S(2)}) %collective-permute-start.43) | collective-permute-done | bytes 131104 | tf_op jit(solution)/shard_map/ppermute | solution.py:688
  188.8 2.2 grads.1
  191.2 14.3 %collective-permute-done.45 = bf16[512,512]{1,0:T(8,128)(2,1)S(1)} collective-permute-done((bf16[512,512]{1,0:T(8,128)(2,1)S(1)}, bf16[512,512]{1,0:T(8,128)(2,1)S(1)}, u32[]{:S(2)}, u32[]{:S(2)}) %collective-permute-start.45) | collective-permute-done | bytes 524320 | tf_op jit(solution)/shard_map/ppermute | solution.py:838
  205.7 1.6 collective-permute-start.48
  207.8 1.5 collective-permute-start.50
  209.3 0.9 collective-permute-start.52
  210.7 3.2 %collective-permute-done.48 = bf16[208,512]{1,0:T(8,128)(2,1)S(1)} collective-permute-done((bf16[208,512]{1,0:T(8,128)(2,1)S(1)}, bf16[208,512]{1,0:T(8,128)(2,1)S(1)}, u32[]{:S(2)}, u32[]{:S(2)}) %collective-permute-start.48) | collective-permute-done | bytes 213024 | tf_op jit(solution)/shard_map/ppermute | solution.py:697
  214.0 4.5 %collective-permute-done.49 = bf16[208,512]{1,0:T(8,128)(2,1)S(1)} collective-permute-done((bf16[208,512]{1,0:T(8,128)(2,1)S(1)}, bf16[208,512]{1,0:T(8,128)(2,1)S(1)}, u32[]{:S(2)}, u32[]{:S(2)}) %collective-permute-start.49) | collective-permute-done | bytes 213024 | tf_op jit(solution)/shard_map/ppermute | solution.py:697
  218.5 1.2 collective-permute-start.51
  219.8 0.8 collective-permute-start.55
  220.6 1.5 collective-permute-start.54
  222.1 11.9 %collective-permute-done.52 = bf16[512,512]{1,0:T(8,128)(2,1)S(1)} collective-permute-done((bf16[512,512]{1,0:T(8,128)(2,1)S(1)}, bf16[512,512]{1,0:T(8,128)(2,1)S(1)}, u32[]{:S(2)}, u32[]{:S(2)}) %collective-permute-start.52) | collective-permute-done | bytes 524320 | tf_op jit(solution)/shard_map/ppermute | solution.py:838
  237.1 2.4 finish.1
  240.7 1.0 maximum_select_fusion
  (123 shorter events, 11.6 us)
Async XLA Ops:
  0.6 61.1 %copy-start = (bf16[512,512]{1,0:T(8,128)(2,1)S(1)}, bf16[512,512]{1,0:T(8,128)(2,1)}, u32[]{:S(2)}) copy-start(bf16[512,512]{1,0:T(8,128)(2,1)} %param.31) | copy-start | bytes 1572868
  1.4 7.0 %collective-permute-start.7 = (f32[256]{0:T(256)S(1)}, f32[256]{0:T(256)S(1)}, u32[]{:S(2)}, u32[]{:S(2)}) collective-permute-start(f32[256]{0:T(256)S(1)} %bitcast.72), channel_id=1, source_target_pairs={{0,4},{4,0},{8,12},{12,8},{16,20},{20,16},{24,28},{28,24},{1,5},{5... | collective-permute-start | bytes 3080 | tf_op jit(solution)/shard_map/ppermute | solution.py:705
  3.0 5.5 %collective-permute-start.3 = (bf16[256,512]{1,0:T(8,128)(2,1)S(1)}, bf16[256,512]{1,0:T(8,128)(2,1)S(1)}, u32[]{:S(2)}, u32[]{:S(2)}) collective-permute-start(bf16[256,512]{1,0:T(8,128)(2,1)S(1)} %get-tuple-element.152), channel_id=1, source_target_pairs={{0,4},{4,0},{8,12},{12,8},{16,20},{20,16},{24,28},{28,24},{1,5},{5... | collective-permute-start | bytes 786440 | tf_op jit(solution)/shard_map/ppermute | solution.py:705
  3.1 12.2 %collective-permute-start = (bf16[256,512]{1,0:T(8,128)(2,1)S(1)}, bf16[256,512]{1,0:T(8,128)(2,1)S(1)}, u32[]{:S(2)}, u32[]{:S(2)}) collective-permute-start(bf16[256,512]{1,0:T(8,128)(2,1)S(1)} %get-tuple-element.153.refs_0_), channel_id=1, source_target_pairs={{0,1},{1,2},{2,3},{3,0},{4,5},{5,6},{6,7},{7,4},{8,9},{9,10},{10,1... | collective-permute-start | bytes 786440 | tf_op jit(solution)/shard_map/ppermute | solution.py:675
  7.2 13.7 %collective-permute-start.13 = (bf16[256,512]{1,0:T(8,128)(2,1)S(1)}, bf16[256,512]{1,0:T(8,128)(2,1)S(1)}, u32[]{:S(2)}, u32[]{:S(2)}) collective-permute-start(bf16[256,512]{1,0:T(8,128)(2,1)S(1)} %get-tuple-element.151), channel_id=1, source_target_pairs={{0,4},{4,0},{8,12},{12,8},{16,20},{20,16},{24,28},{28,24},{1,5},{5... | collective-permute-start | bytes 786440 | tf_op jit(solution)/shard_map/ppermute | solution.py:705
  8.5 12.4 %collective-permute-start.4 = (bf16[256,512]{1,0:T(8,128)(2,1)S(1)}, bf16[256,512]{1,0:T(8,128)(2,1)S(1)}, u32[]{:S(2)}, u32[]{:S(2)}) collective-permute-start(bf16[256,512]{1,0:T(8,128)(2,1)S(1)} %collective-permute-done.3.refs_4_), channel_id=1, source_target_pairs={{0,1},{1,2},{2,3},{3,0},{4,5},{5,6},{6,7},{7,4},{8,9},{9,10},{10,1... | collective-permute-start | bytes 786440 | tf_op jit(solution)/shard_map/ppermute | solution.py:675
  11.1 31.7 %copy-start.3 = (bf16[2048,512]{1,0:T(8,128)(2,1)S(1)}, bf16[2048,512]{1,0:T(8,128)(2,1)}, u32[]{:S(2)}) copy-start(bf16[2048,512]{1,0:T(8,128)(2,1)} %refs_11_.1) | copy-start | bytes 6291460
  15.3 11.2 %collective-permute-start.1 = (bf16[256,512]{1,0:T(8,128)(2,1)S(1)}, bf16[256,512]{1,0:T(8,128)(2,1)S(1)}, u32[]{:S(2)}, u32[]{:S(2)}) collective-permute-start(bf16[256,512]{1,0:T(8,128)(2,1)S(1)} %collective-permute-done.refs_1_), channel_id=1, source_target_pairs={{0,1},{1,2},{2,3},{3,0},{4,5},{5,6},{6,7},{7,4},{8,9},{9,10},{10,1... | collective-permute-start | bytes 786440 | tf_op jit(solution)/shard_map/ppermute | solution.py:675
  20.9 11.2 %collective-permute-start.5 = (bf16[256,512]{1,0:T(8,128)(2,1)S(1)}, bf16[256,512]{1,0:T(8,128)(2,1)S(1)}, u32[]{:S(2)}, u32[]{:S(2)}) collective-permute-start(bf16[256,512]{1,0:T(8,128)(2,1)S(1)} %collective-permute-done.4.refs_5_), channel_id=1, source_target_pairs={{0,1},{1,2},{2,3},{3,0},{4,5},{5,6},{6,7},{7,4},{8,9},{9,10},{10,1... | collective-permute-start | bytes 786440 | tf_op jit(solution)/shard_map/ppermute | solution.py:675
  21.1 34.9 %slice-start = ((s8[8388608]{0:T(1024)(128)(4,1)}), s8[4194304]{0:T(1024)(128)(4,1)S(1)}, s32[]{:S(2)}) async-start(s8[8388608]{0:T(1024)(128)(4,1)} %bitcast.51), calls=%async_computation | async-start | bytes 8388608
  26.5 11.2 %collective-permute-start.2 = (bf16[256,512]{1,0:T(8,128)(2,1)S(1)}, bf16[256,512]{1,0:T(8,128)(2,1)S(1)}, u32[]{:S(2)}, u32[]{:S(2)}) collective-permute-start(bf16[256,512]{1,0:T(8,128)(2,1)S(1)} %collective-permute-done.1.refs_2_), channel_id=1, source_target_pairs={{0,1},{1,2},{2,3},{3,0},{4,5},{5,6},{6,7},{7,4},{8,9},{9,10},{10,1... | collective-permute-start | bytes 786440 | tf_op jit(solution)/shard_map/ppermute | solution.py:675
  32.1 10.7 %collective-permute-start.6 = (bf16[256,512]{1,0:T(8,128)(2,1)S(1)}, bf16[256,512]{1,0:T(8,128)(2,1)S(1)}, u32[]{:S(2)}, u32[]{:S(2)}) collective-permute-start(bf16[256,512]{1,0:T(8,128)(2,1)S(1)} %collective-permute-done.5.refs_6_), channel_id=1, source_target_pairs={{0,1},{1,2},{2,3},{3,0},{4,5},{5,6},{6,7},{7,4},{8,9},{9,10},{10,1... | collective-permute-start | bytes 786440 | tf_op jit(solution)/shard_map/ppermute | solution.py:675
  49.7 18.8 %collective-permute-start.12 = (bf16[512,256]{1,0:T(8,128)(2,1)S(1)}, bf16[512,256]{1,0:T(8,128)(2,1)S(1)}, u32[]{:S(2)}, u32[]{:S(2)}) collective-permute-start(bf16[512,256]{1,0:T(8,128)(2,1)S(1)} %constant_dynamic-slice_fusion.1), channel_id=1, source_target_pairs={{0,2},{1,3},{2,0},{3,1},{4,6},{5,7},{6,4},{7,5},{8,10},{9,11},{10,... | collective-permute-start | bytes 786440 | tf_op jit(solution)/shard_map/ppermute | solution.py:688
  50.5 18.0 %collective-permute-start.11 = (bf16[512,256]{1,0:T(8,128)(2,1)S(1)}, bf16[512,256]{1,0:T(8,128)(2,1)S(1)}, u32[]{:S(2)}, u32[]{:S(2)}) collective-permute-start(bf16[512,256]{1,0:T(8,128)(2,1)S(1)} %constant_dynamic-slice_fusion.1), channel_id=1, source_target_pairs={{0,1},{1,2},{2,3},{3,0},{4,5},{5,6},{6,7},{7,4},{8,9},{9,10},{10,1... | collective-permute-start | bytes 786440 | tf_op jit(solution)/shard_map/ppermute | solution.py:688
  52.1 16.4 %collective-permute-start.8 = (bf16[3,512,128]{2,1,0:T(8,128)(2,1)S(1)}, bf16[3,512,128]{2,1,0:T(8,128)(2,1)S(1)}, u32[]{:S(2)}, u32[]{:S(2)}) collective-permute-start(bf16[3,512,128]{2,1,0:T(8,128)(2,1)S(1)} %get-tuple-element.81), channel_id=1, source_target_pairs={{0,8},{4,12},{8,0},{12,4},{16,24},{20,28},{24,16},{28,20},{1,9},{5... | collective-permute-start | bytes 1179656 | tf_op jit(solution)/shard_map/ppermute | solution.py:697
  53.6 17.8 %collective-permute-start.9 = (bf16[3,512,128]{2,1,0:T(8,128)(2,1)S(1)}, bf16[3,512,128]{2,1,0:T(8,128)(2,1)S(1)}, u32[]{:S(2)}, u32[]{:S(2)}) collective-permute-start(bf16[3,512,128]{2,1,0:T(8,128)(2,1)S(1)} %get-tuple-element.82), channel_id=1, source_target_pairs={{0,16},{4,20},{8,24},{12,28},{16,0},{20,4},{24,8},{28,12},{1,17},{... | collective-permute-start | bytes 1179656 | tf_op jit(solution)/shard_map/ppermute | solution.py:697
  55.1 16.3 %collective-permute-start.10 = (bf16[3,512,128]{2,1,0:T(8,128)(2,1)S(1)}, bf16[3,512,128]{2,1,0:T(8,128)(2,1)S(1)}, u32[]{:S(2)}, u32[]{:S(2)}) collective-permute-start(bf16[3,512,128]{2,1,0:T(8,128)(2,1)S(1)} %get-tuple-element.83), channel_id=1, source_target_pairs={{0,24},{4,28},{8,16},{12,20},{16,8},{20,12},{24,0},{28,4},{1,25},{... | collective-permute-start | bytes 1179656 | tf_op jit(solution)/shard_map/ppermute | solution.py:697
  71.4 3.3 %collective-permute-start.14 = (bf16[3,512,128]{2,1,0:T(8,128)(2,1)S(1)}, bf16[3,512,128]{2,1,0:T(8,128)(2,1)S(1)}, u32[]{:S(2)}, u32[]{:S(2)}) collective-permute-start(bf16[3,512,128]{2,1,0:T(8,128)(2,1)S(1)} %get-tuple-element.90), channel_id=1, source_target_pairs={{0,4},{4,0},{8,12},{12,8},{16,20},{20,16},{24,28},{28,24},{1,5},{5... | collective-permute-start | bytes 1179656 | tf_op jit(solution)/shard_map/ppermute | solution.py:705
  71.4 4.8 %collective-permute-start.15 = (bf16[3,512,128]{2,1,0:T(8,128)(2,1)S(1)}, bf16[3,512,128]{2,1,0:T(8,128)(2,1)S(1)}, u32[]{:S(2)}, u32[]{:S(2)}) collective-permute-start(bf16[3,512,128]{2,1,0:T(8,128)(2,1)S(1)} %collective-permute-done.8), channel_id=1, source_target_pairs={{0,4},{4,0},{8,12},{12,8},{16,20},{20,16},{24,28},{28,24},{1,5},{5... | collective-permute-start | bytes 1179656 | tf_op jit(solution)/shard_map/ppermute | solution.py:705
  71.9 5.5 %collective-permute-start.16 = (bf16[3,512,128]{2,1,0:T(8,128)(2,1)S(1)}, bf16[3,512,128]{2,1,0:T(8,128)(2,1)S(1)}, u32[]{:S(2)}, u32[]{:S(2)}) collective-permute-start(bf16[3,512,128]{2,1,0:T(8,128)(2,1)S(1)} %collective-permute-done.9), channel_id=1, source_target_pairs={{0,4},{4,0},{8,12},{12,8},{16,20},{20,16},{24,28},{28,24},{1,5},{5... | collective-permute-start | bytes 1179656 | tf_op jit(solution)/shard_map/ppermute | solution.py:705
  71.9 6.4 %collective-permute-start.17 = (bf16[3,512,128]{2,1,0:T(8,128)(2,1)S(1)}, bf16[3,512,128]{2,1,0:T(8,128)(2,1)S(1)}, u32[]{:S(2)}, u32[]{:S(2)}) collective-permute-start(bf16[3,512,128]{2,1,0:T(8,128)(2,1)S(1)} %collective-permute-done.10), channel_id=1, source_target_pairs={{0,4},{4,0},{8,12},{12,8},{16,20},{20,16},{24,28},{28,24},{1,5},{5... | collective-permute-start | bytes 1179656 | tf_op jit(solution)/shard_map/ppermute | solution.py:705
  72.4 19.7 %collective-permute-start.18 = (bf16[512,256]{1,0:T(8,128)(2,1)S(1)}, bf16[512,256]{1,0:T(8,128)(2,1)S(1)}, u32[]{:S(2)}, u32[]{:S(2)}) collective-permute-start(bf16[512,256]{1,0:T(8,128)(2,1)S(1)} %constant_dynamic-slice_fusion.1), channel_id=1, source_target_pairs={{0,3},{1,0},{2,1},{3,2},{4,7},{5,4},{6,5},{7,6},{8,11},{9,8},{10,9... | collective-permute-start | bytes 786440 | tf_op jit(solution)/shard_map/ppermute | solution.py:688
  74.7 17.4 %collective-permute-start.21 = (bf16[512,256]{1,0:T(8,128)(2,1)S(1)}, bf16[512,256]{1,0:T(8,128)(2,1)S(1)}, u32[]{:S(2)}, u32[]{:S(2)}) collective-permute-start(bf16[512,256]{1,0:T(8,128)(2,1)S(1)} %collective-permute-done.11.refs_10_), channel_id=1, source_target_pairs={{0,24},{4,28},{8,16},{12,20},{16,8},{20,12},{24,0},{28,4},{1,25},{... | collective-permute-start | bytes 786440 | tf_op jit(solution)/shard_map/ppermute | solution.py:697
  76.2 15.9 %collective-permute-start.20 = (bf16[512,256]{1,0:T(8,128)(2,1)S(1)}, bf16[512,256]{1,0:T(8,128)(2,1)S(1)}, u32[]{:S(2)}, u32[]{:S(2)}) collective-permute-start(bf16[512,256]{1,0:T(8,128)(2,1)S(1)} %collective-permute-done.11.refs_10_), channel_id=1, source_target_pairs={{0,16},{4,20},{8,24},{12,28},{16,0},{20,4},{24,8},{28,12},{1,17},{... | collective-permute-start | bytes 786440 | tf_op jit(solution)/shard_map/ppermute | solution.py:697
  77.4 14.7 %collective-permute-start.19 = (bf16[512,256]{1,0:T(8,128)(2,1)S(1)}, bf16[512,256]{1,0:T(8,128)(2,1)S(1)}, u32[]{:S(2)}, u32[]{:S(2)}) collective-permute-start(bf16[512,256]{1,0:T(8,128)(2,1)S(1)} %collective-permute-done.11.refs_10_), channel_id=1, source_target_pairs={{0,8},{4,12},{8,0},{12,4},{16,24},{20,28},{24,16},{28,20},{1,9},{5... | collective-permute-start | bytes 786440 | tf_op jit(solution)/shard_map/ppermute | solution.py:697
  92.1 5.0 %collective-permute-start.22 = (bf16[2,256,128]{2,1,0:T(8,128)(2,1)S(1)}, bf16[2,256,128]{2,1,0:T(8,128)(2,1)S(1)}, u32[]{:S(2)}, u32[]{:S(2)}) collective-permute-start(bf16[2,256,128]{2,1,0:T(8,128)(2,1)S(1)} %get-tuple-element.101), channel_id=1, source_target_pairs={{0,8},{4,12},{8,0},{12,4},{16,24},{20,28},{24,16},{28,20},{1,9},{5... | collective-permute-start | bytes 393224 | tf_op jit(solution)/shard_map/ppermute | solution.py:697
  93.4 5.0 %collective-permute-start.23 = (bf16[2,256,128]{2,1,0:T(8,128)(2,1)S(1)}, bf16[2,256,128]{2,1,0:T(8,128)(2,1)S(1)}, u32[]{:S(2)}, u32[]{:S(2)}) collective-permute-start(bf16[2,256,128]{2,1,0:T(8,128)(2,1)S(1)} %get-tuple-element.102), channel_id=1, source_target_pairs={{0,16},{4,20},{8,24},{12,28},{16,0},{20,4},{24,8},{28,12},{1,17},{... | collective-permute-start | bytes 393224 | tf_op jit(solution)/shard_map/ppermute | solution.py:697
  94.2 6.3 %collective-permute-start.24 = (bf16[2,256,128]{2,1,0:T(8,128)(2,1)S(1)}, bf16[2,256,128]{2,1,0:T(8,128)(2,1)S(1)}, u32[]{:S(2)}, u32[]{:S(2)}) collective-permute-start(bf16[2,256,128]{2,1,0:T(8,128)(2,1)S(1)} %get-tuple-element.103), channel_id=1, source_target_pairs={{0,24},{4,28},{8,16},{12,20},{16,8},{20,12},{24,0},{28,4},{1,25},{... | collective-permute-start | bytes 393224 | tf_op jit(solution)/shard_map/ppermute | solution.py:697
  100.6 37.5 %copy-start.6 = (f32[2048]{0:T(1024)S(1)}, f32[2048]{0:T(1024)}, u32[]{:S(2)}) copy-start(f32[2048]{0:T(1024)} %param.21) | copy-start | bytes 24580
  100.6 10.2 %collective-permute-start.25 = (bf16[2,2,256,128]{3,2,1,0:T(8,128)(2,1)S(1)}, bf16[2,2,256,128]{3,2,1,0:T(8,128)(2,1)S(1)}, u32[]{:S(2)}, u32[]{:S(2)}) collective-permute-start(bf16[2,2,256,128]{3,2,1,0:T(8,128)(2,1)S(1)} %pad_maximum_fusion.3.refs_0_), channel_id=1, source_target_pairs={{0,1},{1,2},{2,3},{3,0},{4,5},{5,6},{6,7},{7,4},{8,9},{9,10},{10,1... | collective-permute-start | bytes 786440 | tf_op jit(solution)/shard_map/ppermute | solution.py:675
  100.7 15.7 %collective-permute-start.28 = (bf16[2,2,256,128]{3,2,1,0:T(8,128)(2,1)S(1)}, bf16[2,2,256,128]{3,2,1,0:T(8,128)(2,1)S(1)}, u32[]{:S(2)}, u32[]{:S(2)}) collective-permute-start(bf16[2,2,256,128]{3,2,1,0:T(8,128)(2,1)S(1)} %pad_maximum_fusion.4.refs_4_), channel_id=1, source_target_pairs={{0,1},{1,2},{2,3},{3,0},{4,5},{5,6},{6,7},{7,4},{8,9},{9,10},{10,1... | collective-permute-start | bytes 786440 | tf_op jit(solution)/shard_map/ppermute | solution.py:675
  101.3 23.3 %collective-permute-start.33 = (bf16[2,512,256]{2,1,0:T(8,128)(2,1)S(1)}, bf16[2,512,256]{2,1,0:T(8,128)(2,1)S(1)}, u32[]{:S(2)}, u32[]{:S(2)}) collective-permute-start(bf16[2,512,256]{2,1,0:T(8,128)(2,1)S(1)} %pad_maximum_fusion.refs_14_), channel_id=1, source_target_pairs={{0,24},{4,28},{8,16},{12,20},{16,8},{20,12},{24,0},{28,4},{1,25},{... | collective-permute-start | bytes 1572872 | tf_op jit(solution)/shard_map/ppermute | solution.py:697
  110.8 9.2 %collective-permute-start.26 = (bf16[2,2,256,128]{3,2,1,0:T(8,128)(2,1)S(1)}, bf16[2,2,256,128]{3,2,1,0:T(8,128)(2,1)S(1)}, u32[]{:S(2)}, u32[]{:S(2)}) collective-permute-start(bf16[2,2,256,128]{3,2,1,0:T(8,128)(2,1)S(1)} %collective-permute-done.25.refs_1_), channel_id=1, source_target_pairs={{0,1},{1,2},{2,3},{3,0},{4,5},{5,6},{6,7},{7,4},{8,9},{9,10},{10,1... | collective-permute-start | bytes 786440 | tf_op jit(solution)/shard_map/ppermute | solution.py:675
  110.8 13.8 %collective-permute-start.32 = (bf16[2,512,256]{2,1,0:T(8,128)(2,1)S(1)}, bf16[2,512,256]{2,1,0:T(8,128)(2,1)S(1)}, u32[]{:S(2)}, u32[]{:S(2)}) collective-permute-start(bf16[2,512,256]{2,1,0:T(8,128)(2,1)S(1)} %pad_maximum_fusion.refs_14_), channel_id=1, source_target_pairs={{0,16},{4,20},{8,24},{12,28},{16,0},{20,4},{24,8},{28,12},{1,17},{... | collective-permute-start | bytes 1572872 | tf_op jit(solution)/shard_map/ppermute | solution.py:697
  112.1 12.6 %collective-permute-start.31 = (bf16[2,512,256]{2,1,0:T(8,128)(2,1)S(1)}, bf16[2,512,256]{2,1,0:T(8,128)(2,1)S(1)}, u32[]{:S(2)}, u32[]{:S(2)}) collective-permute-start(bf16[2,512,256]{2,1,0:T(8,128)(2,1)S(1)} %pad_maximum_fusion.refs_14_), channel_id=1, source_target_pairs={{0,8},{4,12},{8,0},{12,4},{16,24},{20,28},{24,16},{28,20},{1,9},{5... | collective-permute-start | bytes 1572872 | tf_op jit(solution)/shard_map/ppermute | solution.py:697
  116.4 8.2 %collective-permute-start.29 = (bf16[2,2,256,128]{3,2,1,0:T(8,128)(2,1)S(1)}, bf16[2,2,256,128]{3,2,1,0:T(8,128)(2,1)S(1)}, u32[]{:S(2)}, u32[]{:S(2)}) collective-permute-start(bf16[2,2,256,128]{3,2,1,0:T(8,128)(2,1)S(1)} %collective-permute-done.28.refs_5_), channel_id=1, source_target_pairs={{0,1},{1,2},{2,3},{3,0},{4,5},{5,6},{6,7},{7,4},{8,9},{9,10},{10,1... | collective-permute-start | bytes 786440 | tf_op jit(solution)/shard_map/ppermute | solution.py:675
  120.1 18.1 %collective-permute-start.34 = (bf16[4,1,512,256]{3,2,0,1:T(8,128)(2,1)S(1)}, bf16[4,1,512,256]{3,2,0,1:T(8,128)(2,1)S(1)}, u32[]{:S(2)}, u32[]{:S(2)}) collective-permute-start(bf16[4,1,512,256]{3,2,0,1:T(8,128)(2,1)S(1)} %maximum_bitcast_fusion), channel_id=1, source_target_pairs={{0,4},{4,0},{8,12},{12,8},{16,20},{20,16},{24,28},{28,24},{1,5},{5... | collective-permute-start | bytes 3145736 | tf_op jit(solution)/shard_map/ppermute | solution.py:705
  124.6 8.8 %collective-permute-start.27 = (bf16[2,2,256,128]{3,2,1,0:T(8,128)(2,1)S(1)}, bf16[2,2,256,128]{3,2,1,0:T(8,128)(2,1)S(1)}, u32[]{:S(2)}, u32[]{:S(2)}) collective-permute-start(bf16[2,2,256,128]{3,2,1,0:T(8,128)(2,1)S(1)} %collective-permute-done.26.refs_2_), channel_id=1, source_target_pairs={{0,1},{1,2},{2,3},{3,0},{4,5},{5,6},{6,7},{7,4},{8,9},{9,10},{10,1... | collective-permute-start | bytes 786440 | tf_op jit(solution)/shard_map/ppermute | solution.py:675
  124.6 11.6 %collective-permute-start.30 = (bf16[2,2,256,128]{3,2,1,0:T(8,128)(2,1)S(1)}, bf16[2,2,256,128]{3,2,1,0:T(8,128)(2,1)S(1)}, u32[]{:S(2)}, u32[]{:S(2)}) collective-permute-start(bf16[2,2,256,128]{3,2,1,0:T(8,128)(2,1)S(1)} %collective-permute-done.29.refs_6_), channel_id=1, source_target_pairs={{0,1},{1,2},{2,3},{3,0},{4,5},{5,6},{6,7},{7,4},{8,9},{9,10},{10,1... | collective-permute-start | bytes 786440 | tf_op jit(solution)/shard_map/ppermute | solution.py:675
  124.6 11.6 %collective-permute-start.35 = (bf16[2,512,256]{2,1,0:T(8,128)(2,1)S(1)}, bf16[2,512,256]{2,1,0:T(8,128)(2,1)S(1)}, u32[]{:S(2)}, u32[]{:S(2)}) collective-permute-start(bf16[2,512,256]{2,1,0:T(8,128)(2,1)S(1)} %pad_maximum_fusion.refs_14_), channel_id=1, source_target_pairs={{0,4},{4,0},{8,12},{12,8},{16,20},{20,16},{24,28},{28,24},{1,5},{5... | collective-permute-start | bytes 1572872 | tf_op jit(solution)/shard_map/ppermute | solution.py:705
  124.7 11.5 %collective-permute-start.38 = (bf16[2,512,256]{2,1,0:T(8,128)(2,1)S(1)}, bf16[2,512,256]{2,1,0:T(8,128)(2,1)S(1)}, u32[]{:S(2)}, u32[]{:S(2)}) collective-permute-start(bf16[2,512,256]{2,1,0:T(8,128)(2,1)S(1)} %collective-permute-done.33.refs_17_), channel_id=1, source_target_pairs={{0,4},{4,0},{8,12},{12,8},{16,20},{20,16},{24,28},{28,24},{1,5},{5... | collective-permute-start | bytes 1572872 | tf_op jit(solution)/shard_map/ppermute | solution.py:705
  133.4 2.8 %collective-permute-start.37 = (bf16[2,512,256]{2,1,0:T(8,128)(2,1)S(1)}, bf16[2,512,256]{2,1,0:T(8,128)(2,1)S(1)}, u32[]{:S(2)}, u32[]{:S(2)}) collective-permute-start(bf16[2,512,256]{2,1,0:T(8,128)(2,1)S(1)} %collective-permute-done.32.refs_16_), channel_id=1, source_target_pairs={{0,4},{4,0},{8,12},{12,8},{16,20},{20,16},{24,28},{28,24},{1,5},{5... | collective-permute-start | bytes 1572872 | tf_op jit(solution)/shard_map/ppermute | solution.py:705
  136.2 1.9 collective-permute-start.36
  160.4 8.3 %collective-permute-start.39 = (bf16[128,512]{1,0:T(8,128)(2,1)S(1)}, bf16[128,512]{1,0:T(8,128)(2,1)S(1)}, u32[]{:S(2)}, u32[]{:S(2)}) collective-permute-start(bf16[128,512]{1,0:T(8,128)(2,1)S(1)} %get-tuple-element.119), channel_id=1, source_target_pairs={{0,1},{1,2},{2,3},{3,0},{4,5},{5,6},{6,7},{7,4},{8,9},{9,10},{10,1... | collective-permute-start | bytes 393224 | tf_op jit(solution)/shard_map/ppermute | solution.py:688
  160.5 12.9 %collective-permute-start.40 = (bf16[128,512]{1,0:T(8,128)(2,1)S(1)}, bf16[128,512]{1,0:T(8,128)(2,1)S(1)}, u32[]{:S(2)}, u32[]{:S(2)}) collective-permute-start(bf16[128,512]{1,0:T(8,128)(2,1)S(1)} %get-tuple-element.120), channel_id=1, source_target_pairs={{0,2},{1,3},{2,0},{3,1},{4,6},{5,7},{6,4},{7,5},{8,10},{9,11},{10,... | collective-permute-start | bytes 393224 | tf_op jit(solution)/shard_map/ppermute | solution.py:688
  160.6 12.9 %collective-permute-start.41 = (bf16[128,512]{1,0:T(8,128)(2,1)S(1)}, bf16[128,512]{1,0:T(8,128)(2,1)S(1)}, u32[]{:S(2)}, u32[]{:S(2)}) collective-permute-start(bf16[128,512]{1,0:T(8,128)(2,1)S(1)} %get-tuple-element.121), channel_id=1, source_target_pairs={{0,3},{1,0},{2,1},{3,2},{4,7},{5,4},{6,5},{7,6},{8,11},{9,8},{10,9... | collective-permute-start | bytes 393224 | tf_op jit(solution)/shard_map/ppermute | solution.py:688
  173.6 12.2 %collective-permute-start.44 = (bf16[128,512]{1,0:T(8,128)(2,1)S(1)}, bf16[128,512]{1,0:T(8,128)(2,1)S(1)}, u32[]{:S(2)}, u32[]{:S(2)}) collective-permute-start(bf16[128,512]{1,0:T(8,128)(2,1)S(1)} %multiply_convert_fusion.3.refs_0_), channel_id=1, source_target_pairs={{0,3},{1,0},{2,1},{3,2},{4,7},{5,4},{6,5},{7,6},{8,11},{9,8},{10,9... | collective-permute-start | bytes 393224 | tf_op jit(solution)/shard_map/ppermute | solution.py:688
  176.2 12.5 %collective-permute-start.43 = (bf16[128,512]{1,0:T(8,128)(2,1)S(1)}, bf16[128,512]{1,0:T(8,128)(2,1)S(1)}, u32[]{:S(2)}, u32[]{:S(2)}) collective-permute-start(bf16[128,512]{1,0:T(8,128)(2,1)S(1)} %multiply_convert_fusion.3.refs_0_), channel_id=1, source_target_pairs={{0,2},{1,3},{2,0},{3,1},{4,6},{5,7},{6,4},{7,5},{8,10},{9,11},{10,... | collective-permute-start | bytes 393224 | tf_op jit(solution)/shard_map/ppermute | solution.py:688
  177.7 11.1 %collective-permute-start.42 = (bf16[128,512]{1,0:T(8,128)(2,1)S(1)}, bf16[128,512]{1,0:T(8,128)(2,1)S(1)}, u32[]{:S(2)}, u32[]{:S(2)}) collective-permute-start(bf16[128,512]{1,0:T(8,128)(2,1)S(1)} %multiply_convert_fusion.3.refs_0_), channel_id=1, source_target_pairs={{0,1},{1,2},{2,3},{3,0},{4,5},{5,6},{6,7},{7,4},{8,9},{9,10},{10,1... | collective-permute-start | bytes 393224 | tf_op jit(solution)/shard_map/ppermute | solution.py:688
  191.0 14.6 %collective-permute-start.47 = (bf16[4,208,512]{2,1,0:T(8,128)(2,1)S(1)}, bf16[4,208,512]{2,1,0:T(8,128)(2,1)S(1)}, u32[]{:S(2)}, u32[]{:S(2)}) collective-permute-start(bf16[4,208,512]{2,1,0:T(8,128)(2,1)S(1)} %get-tuple-element.133), channel_id=1, source_target_pairs={{0,4},{4,0},{8,12},{12,8},{16,20},{20,16},{24,28},{28,24},{1,5},{5... | collective-permute-start | bytes 2555912 | tf_op jit(solution)/shard_map/ppermute | solution.py:705
  191.1 14.3 %collective-permute-start.45 = (bf16[512,512]{1,0:T(8,128)(2,1)S(1)}, bf16[512,512]{1,0:T(8,128)(2,1)S(1)}, u32[]{:S(2)}, u32[]{:S(2)}) collective-permute-start(bf16[512,512]{1,0:T(8,128)(2,1)S(1)} %get-tuple-element.127), channel_id=1, source_target_pairs={{0,1},{1,0},{2,3},{3,2},{4,5},{5,4},{6,7},{7,6},{8,9},{9,8},{10,11... | collective-permute-start | bytes 1572872 | tf_op jit(solution)/shard_map/ppermute | solution.py:838
  205.7 8.2 %collective-permute-start.48 = (bf16[208,512]{1,0:T(8,128)(2,1)S(1)}, bf16[208,512]{1,0:T(8,128)(2,1)S(1)}, u32[]{:S(2)}, u32[]{:S(2)}) collective-permute-start(bf16[208,512]{1,0:T(8,128)(2,1)S(1)} %get-tuple-element.136), channel_id=1, source_target_pairs={{0,8},{4,12},{8,0},{12,4},{16,24},{20,28},{24,16},{28,20},{1,9},{5... | collective-permute-start | bytes 638984 | tf_op jit(solution)/shard_map/ppermute | solution.py:697
  207.3 11.1 %collective-permute-start.49 = (bf16[208,512]{1,0:T(8,128)(2,1)S(1)}, bf16[208,512]{1,0:T(8,128)(2,1)S(1)}, u32[]{:S(2)}, u32[]{:S(2)}) collective-permute-start(bf16[208,512]{1,0:T(8,128)(2,1)S(1)} %get-tuple-element.137), channel_id=1, source_target_pairs={{0,16},{4,20},{8,24},{12,28},{16,0},{20,4},{24,8},{28,12},{1,17},{... | collective-permute-start | bytes 638984 | tf_op jit(solution)/shard_map/ppermute | solution.py:697
  207.8 10.6 %collective-permute-start.50 = (bf16[208,512]{1,0:T(8,128)(2,1)S(1)}, bf16[208,512]{1,0:T(8,128)(2,1)S(1)}, u32[]{:S(2)}, u32[]{:S(2)}) collective-permute-start(bf16[208,512]{1,0:T(8,128)(2,1)S(1)} %get-tuple-element.138), channel_id=1, source_target_pairs={{0,24},{4,28},{8,16},{12,20},{16,8},{20,12},{24,0},{28,4},{1,25},{... | collective-permute-start | bytes 638984 | tf_op jit(solution)/shard_map/ppermute | solution.py:697
  209.3 24.7 %collective-permute-start.52 = (bf16[512,512]{1,0:T(8,128)(2,1)S(1)}, bf16[512,512]{1,0:T(8,128)(2,1)S(1)}, u32[]{:S(2)}, u32[]{:S(2)}) collective-permute-start(bf16[512,512]{1,0:T(8,128)(2,1)S(1)} %add_convert_fusion.1), channel_id=1, source_target_pairs={{0,2},{1,3},{2,0},{3,1},{4,6},{5,7},{6,4},{7,5},{8,10},{9,11},{10,... | collective-permute-start | bytes 1572872 | tf_op jit(solution)/shard_map/ppermute | solution.py:838
  210.2 23.8 %collective-permute-start.46 = (bf16[512,512]{1,0:T(8,128)(2,1)S(1)}, bf16[512,512]{1,0:T(8,128)(2,1)S(1)}, u32[]{:S(2)}, u32[]{:S(2)}) collective-permute-start(bf16[512,512]{1,0:T(8,128)(2,1)S(1)} %get-tuple-element.132), channel_id=1, source_target_pairs={{0,1},{1,0},{2,3},{3,2},{4,5},{5,4},{6,7},{7,6},{8,9},{9,8},{10,11... | collective-permute-start | bytes 1572872 | tf_op jit(solution)/shard_map/ppermute | solution.py:838
  218.5 15.4 %collective-permute-start.51 = (bf16[208,512]{1,0:T(8,128)(2,1)S(1)}, bf16[208,512]{1,0:T(8,128)(2,1)S(1)}, u32[]{:S(2)}, u32[]{:S(2)}) collective-permute-start(bf16[208,512]{1,0:T(8,128)(2,1)S(1)} %add_convert_fusion.2.refs_0_), channel_id=1, source_target_pairs={{0,24},{4,28},{8,16},{12,20},{16,8},{20,12},{24,0},{28,4},{1,25},{... | collective-permute-start | bytes 638984 | tf_op jit(solution)/shard_map/ppermute | solution.py:697
  219.8 15.1 %collective-permute-start.55 = (bf16[208,512]{1,0:T(8,128)(2,1)S(1)}, bf16[208,512]{1,0:T(8,128)(2,1)S(1)}, u32[]{:S(2)}, u32[]{:S(2)}) collective-permute-start(bf16[208,512]{1,0:T(8,128)(2,1)S(1)} %add_convert_fusion.2.refs_0_), channel_id=1, source_target_pairs={{0,16},{4,20},{8,24},{12,28},{16,0},{20,4},{24,8},{28,12},{1,17},{... | collective-permute-start | bytes 638984 | tf_op jit(solution)/shard_map/ppermute | solution.py:697
  220.6 14.4 %collective-permute-start.54 = (bf16[208,512]{1,0:T(8,128)(2,1)S(1)}, bf16[208,512]{1,0:T(8,128)(2,1)S(1)}, u32[]{:S(2)}, u32[]{:S(2)}) collective-permute-start(bf16[208,512]{1,0:T(8,128)(2,1)S(1)} %add_convert_fusion.2.refs_0_), channel_id=1, source_target_pairs={{0,8},{4,12},{8,0},{12,4},{16,24},{20,28},{24,16},{28,20},{1,9},{5... | collective-permute-start | bytes 638984 | tf_op jit(solution)/shard_map/ppermute | solution.py:697
  234.3 6.4 %collective-permute-start.53 = (bf16[256,512]{1,0:T(8,128)(2,1)S(1)}, bf16[256,512]{1,0:T(8,128)(2,1)S(1)}, u32[]{:S(2)}, u32[]{:S(2)}) collective-permute-start(bf16[256,512]{1,0:T(8,128)(2,1)S(1)} %get-tuple-element.149), channel_id=1, source_target_pairs={{0,4},{4,0},{8,12},{12,8},{16,20},{20,16},{24,28},{28,24},{1,5},{5... | collective-permute-start | bytes 786440 | tf_op jit(solution)/shard_map/ppermute | solution.py:705
  234.4 1.8 collective-permute-start.56
  234.9 1.6 collective-permute-start.58
  235.0 1.9 collective-permute-start.57
  235.4 1.7 collective-permute-start.59
  (10 other events, 133.6 us)

commit v5 on v4

--- a/solution.py
+++ b/solution.py
@@ -188,7 +188,7 @@
     blocks = [refs[:ring], refs[ring : 2 * ring]]
     gain_ref, cos_ref, sin_ref, *sources = refs[2 * ring : 2 * ring + 6]
     outs = refs[2 * ring + 6 : 2 * ring + 6 + heads]
-    tok_ref, stamp_ref, normed, made, weights, sems = refs[2 * ring + 6 + heads :]
+    tok_ref, normed, made, weights, sems = refs[2 * ring + 6 + heads :]
     half, width = blocks[0][0].shape
     depth = gain_ref.shape[1]
     copies = [
@@ -221,7 +221,6 @@
             made[h, kind] = head.astype(BF16)
     for f in range(heads):
         outs[f][...] = made[info_ref[ring + 1] ^ f]
-    stamp_ref[...] = jnp.zeros_like(stamp_ref)
 
 
 def qkv_call(info, blocks, gain, cosine, sine, *weights):
@@ -234,14 +233,14 @@
             qkv_kernel, ring=ring, heads=heads, factor=HD ** (-0.5) * math.log2(math.e)
         ),
         out_shape=[jax.ShapeDtypeStruct((3, rows, HD), BF16)] * heads
-        + [jax.ShapeDtypeStruct((rows, depth), BF16), jax.ShapeDtypeStruct((8, HD), F32)],
+        + [jax.ShapeDtypeStruct((rows, depth), BF16)],
         grid_spec=pltpu.PrefetchScalarGridSpec(
             num_scalar_prefetch=1,
             grid=(1,),
             in_specs=[whole((half, width))] * (2 * ring)
             + [whole((1, depth)), whole((rows, HD)), whole((rows, HD))]
             + [pl.BlockSpec(memory_space=pl.ANY)] * 3,
-            out_specs=[whole((3, rows, HD))] * heads + [whole((rows, depth)), whole((8, HD))],
+            out_specs=[whole((3, rows, HD))] * heads + [whole((rows, depth))],
             scratch_shapes=[
                 pltpu.VMEM((rows, depth), BF16),
                 pltpu.VMEM((heads, 3, rows, HD), BF16),
@@ -253,7 +252,7 @@
         cost_estimate=cost(6 * rows * depth * out_cols, 6 * depth * out_cols),
         name="qkv",
     )(info, *blocks[0], *blocks[1], gain, cosine, sine, *weights)
-    return result[:heads], result[heads], result[heads + 1]
+    return result[:heads], result[heads]
 
 
 def attention_kernel(first_ref, info_ref, *refs, chips, ring):
@@ -261,15 +260,12 @@
     outs = refs[2 * chips : 3 * chips]
     keys_all, values_all = refs[3 * chips :]
     chip, core = info_ref[ring + 1], info_ref[ring + 2]
-    half = outs[0].shape[1]
-    span = 2 * half
+    span = outs[0].shape[0]
     for f in range(chips):
         for source, side in ((own[f], core), (other[f], 1 - core)):
-            at = pl.ds(pl.multiple_of(side * half, half), half)
-            for odd, index in ((0, side), (1, 1 - side)):
-                block = 2 * (chip ^ f) + odd
-                keys_all[block, at, :] = source[1, index]
-                values_all[block, :, at] = source[2, index].T
+            block = 2 * (chip ^ f) + side
+            keys_all[block] = source[1]
+            values_all[block] = source[2].T
 
     def first_of(row):
         found = jnp.int32(0)
@@ -279,12 +275,9 @@
         return found
 
     for f in range(chips):
-        even = 2 * (chip ^ f)
-        first_row = even * span + core * half
-        last_row = first_row + span + half - 1
-        query = jnp.concatenate([own[f][0, core], own[f][0, 1 - core]], axis=0)
-        place = lax.broadcasted_iota(jnp.int32, (1, span), 1)
-        row = first_row + place + jnp.where(place < half, 0, half)
+        last = 2 * (chip ^ f) + core
+        query = own[f][0]
+        row = last * span + lax.broadcasted_iota(jnp.int32, (1, span), 1)
         start = jnp.zeros((1, span), jnp.int32)
         for s in range(SERIES):
             edge = first_ref[s]
@@ -307,45 +300,40 @@
             accum = accum * keep + dot(values_all[at], weights.astype(BF16))
             return new_peak, denom, accum
 
-        begin = first_of(first_row) // span
-        full = jnp.minimum(even, (first_of(last_row) + span - 1) // span)
+        begin = first_of(last * span) // span
+        full = jnp.minimum(last, (first_of(last * span + span - 1) + span - 1) // span)
         carry = (
             jnp.full((1, span), -1e30, F32),
             jnp.zeros((1, span), F32),
             jnp.zeros((HD, span), F32),
         )
         carry = lax.fori_loop(begin, full, functools.partial(body, masked=True), carry)
-        carry = lax.fori_loop(full, even, functools.partial(body, masked=False), carry)
-        peak, denom, accum = body(even, carry, masked=True)
-        outs[f][core] = (accum[:, :half] / denom[:, :half]).T.astype(BF16)
-        carry = (peak[:, half:], denom[:, half:], accum[:, half:])
-        _, denom, accum = body(
-            even + 1, carry, True, query[half:], row[:, half:], start[:, half:], lane
-        )
-        outs[f][1 - core] = (accum / denom).T.astype(BF16)
+        carry = lax.fori_loop(full, last, functools.partial(body, masked=False), carry)
+        _, denom, accum = body(last, carry, masked=True)
+        outs[f][...] = (accum / denom).T.astype(BF16)
 
 
 def attention_call(first, info, own, other, ring):
     chips = len(own)
-    _, _, half, _ = own[0].shape
+    _, rows, _ = own[0].shape
     return pl.pallas_call(
         functools.partial(attention_kernel, chips=chips, ring=ring),
-        out_shape=[jax.ShapeDtypeStruct((2, half, HD), BF16)] * chips,
+        out_shape=[jax.ShapeDtypeStruct((rows, HD), BF16)] * chips,
         grid_spec=pltpu.PrefetchScalarGridSpec(
             num_scalar_prefetch=2,
             grid=(1,),
-            in_specs=[whole((3, 2, half, HD))] * (2 * chips),
-            out_specs=[whole((2, half, HD))] * chips,
+            in_specs=[whole((3, rows, HD))] * (2 * chips),
+            out_specs=[whole((rows, HD))] * chips,
             scratch_shapes=[
-                pltpu.VMEM((2 * chips, 2 * half, HD), BF16),
-                pltpu.VMEM((2 * chips, HD, 2 * half), BF16),
+                pltpu.VMEM((2 * chips, rows, HD), BF16),
+                pltpu.VMEM((2 * chips, HD, rows), BF16),
             ],
         ),
         compiler_params=params(24),
         cost_estimate=cost(
-            4 * chips * half * 4 * chips * half * HD,
-            12 * chips * half * HD * 2,
-            2 * chips * half * 4 * chips * half // 2,
+            4 * chips * rows * chips * rows * HD,
+            16 * chips * rows * HD,
+            chips * rows * chips * rows,
         ),
         name="attention",
     )(first, info, *own, *other)
@@ -365,7 +353,6 @@
     step = pl.program_id(0)
     level, chip, core = info_ref[ring], info_ref[ring + 1], info_ref[ring + 2]
     rows, depth = mixed.shape
-    half = rows // 2
     width = own_ref.shape[1]
     blocks, _, wide = gates.shape
 
@@ -376,11 +363,8 @@
         for s, part in enumerate(parts[k]):
             count = part.shape[0]
             for i in range(count):
-                at = s * width + (chip ^ (k * count + i)) * HD
-                at = pl.ds(pl.multiple_of(at, HD), HD)
-                for side in range(2):
-                    rows_at = pl.ds(side * half, half)
-                    heads.append(copy(part.at[i, side], attended.at[rows_at, at]))
+                at = (level ^ info_ref[s]) * width + (chip ^ (k * count + i)) * HD
+                heads.append(copy(part.at[i], attended.at[:, pl.ds(pl.multiple_of(at, HD), HD)]))
     slices = [
         [
             copy(near_first[f], near.at[f, 0]),
@@ -475,7 +459,7 @@
     tile = lambda j, info: (0, jnp.minimum(j, chips - 1) ^ info[ring + 1])
     late = lambda j, info: (0, jnp.maximum(j - chips, 0))
     anywhere = pl.BlockSpec(memory_space=pl.ANY)
-    count = 2 * ring * parts[0][0].shape[0] * 2 + 4 * chips + 2 + 3 * blocks
+    count = 2 * ring * parts[0][0].shape[0] + 4 * chips + 2 + 3 * blocks
     result = pl.pallas_call(
         functools.partial(middle_kernel, ring=ring, chips=chips),
         out_shape=[
@@ -740,41 +724,29 @@
     places = [(level - s) & (ring - 1) for s in range(ring)] + [level, here >> 1, here & 1]
     slots = lax.broadcasted_iota(jnp.int32, (16,), 0)
     info = sum(jnp.where(slots == k, place, 0) for k, place in enumerate(places))
-    starts = jnp.stack([here & 1, (here & 1) ^ 1, level * size, here * slice_cols])
-    *starts, zero = [starts[k].astype(jnp.uint32) for k in range(4)] + [jnp.uint32(0)]
-    first_core = (here & 1) == 0
-    tokens, info, first_core, *starts = lax.optimization_barrier(
-        (tokens, info, first_core, *starts)
-    )
-
-    def deal(value):
-        parts = value.reshape((2, half) + value.shape[1:])
-        shape = (1,) + parts.shape[1:]
-        rest = [zero] * (parts.ndim - 1)
-        kept, given = [lax.dynamic_slice(parts, [k, *rest], shape)[0] for k in starts[:2]]
-        return kept, swapped(given)
-
-    token_chunks = deal(tokens)
-    token_rings = [ring_gather(chunk, "tensor") for chunk in token_chunks]
-    student_chunks = deal(student_in)
-    offset_chunks = deal(offsets.astype(F32))
-
-    angles = jnp.concatenate(offset_chunks)[:, None] * frequencies(HD)[None, :]
+    starts = [level * size, here * slice_cols]
+    *starts, zero = [jnp.asarray(start, jnp.uint32) for start in (*starts, 0)]
+    tokens, info, *starts = lax.optimization_barrier((tokens, info, *starts))
+
+    token_rings = [ring_gather(tokens[k : k + half], "tensor") for k in (0, half)]
+
+    angles = offsets.astype(F32)[:, None] * frequencies(HD)[None, :]
     cosine, sine = jnp.cos(angles), jnp.sin(angles)
     cosine = jnp.concatenate([cosine, cosine], axis=1)
     sine = jnp.concatenate([-sine, sine], axis=1)
-    student_full = jnp.concatenate(student_chunks, axis=0).astype(F32)
+    student_full = student_in.astype(F32)
     student_normed = rms_scale(student_full).astype(BF16)
     below = jnp.sum(
         series_ids[None, :] < jnp.arange(SERIES, dtype=jnp.int32)[:, None], axis=1, dtype=jnp.int32
     )
 
-    made, tok_full, stamp = qkv_call(
+    made, tok_full = qkv_call(
         info, token_rings, norm_gain[None, :], cosine, sine, w_query, w_key, w_value
     )
 
-    held = lax.optimization_barrier((student_normed, projector, stamp))
-    student_normed = held[0]
+    student_normed, projected, tok_full = lax.optimization_barrier(
+        (student_normed, projector, tok_full)
+    )
     s_gate_out = dot(student_normed, s_gate)
     s_up_out = dot(student_normed, s_up)
     sigmoid_gate = jax.nn.sigmoid(s_gate_out)
@@ -783,25 +755,22 @@
     s_hidden = (up_slope * s_up_out).astype(BF16)
     up_slope, gate_slope = up_slope.astype(BF16), gate_slope.astype(BF16)
     student_part = dot(s_hidden, s_down)
-    projected = dot(w_down, held[1]).astype(BF16)
-    student_own = lax.dynamic_slice(student_full, [starts[2], zero], (size, sd))
+    projected = dot(w_down, projected).astype(BF16)
+    student_own = lax.dynamic_slice(student_full, [starts[0], zero], (size, sd))
     early = (projected, student_part, s_hidden, up_slope, gate_slope, student_normed, student_own)
 
-    w_slice = lax.dynamic_slice(w_out, [zero, starts[3]], (w_out.shape[0], slice_cols))
-    w_slice = after(w_slice, stamp)
-    w_others = shifted([w_slice] * ring, "tensor")[1:]
+    over = lambda value, bit: lax.ppermute(value, "tensor", [(i, i ^ bit) for i in range(ring)])
+    w_slice = lax.dynamic_slice(w_out, [zero, starts[1]], (w_out.shape[0], slice_cols))
+    w_slice = after(w_slice, s_gate_out)
+    w_first = over(w_slice, 1)
+    w_rest = over(jnp.stack([w_slice, w_first]), 2)
 
     own = flipped(made)
-    held = lax.optimization_barrier((*own, *w_others[:2], *early))
-    own, w_others[:2] = held[:chips], held[chips : chips + 2]
+    *own, w_first = lax.optimization_barrier((*own, w_first, *early))[: chips + 1]
     other = [swapped(a) for a in own]
-    near_first = flipped([w_others[0]] * chips)
-    pairs = lambda a: a.reshape(3, 2, half, HD)
-    made = attention_call(
-        below, info, [pairs(a) for a in own], [pairs(a) for a in other], ring
-    )
-    held = lax.optimization_barrier((*made, *w_others[1:], *near_first))
-    made, w_rest = held[:chips], jnp.stack(held[chips : chips + ring - 2])
+    near_first = flipped([w_first] * chips)
+    made = attention_call(below, info, own, other, ring)
+    *made, w_rest = lax.optimization_barrier((*made, w_rest, *near_first))[: chips + 1]
     attended = lax.optimization_barrier(tuple(flipped(made)))
     parts = [
         ring_gather(jnp.stack(attended[k : k + chips // 2]), "tensor") for k in (0, chips // 2)
@@ -826,20 +795,16 @@
         student_part,
     )
 
-    own = student_own
-    moved = shifted(pieces, "tensor")
-    difference = own + sum(piece.astype(F32) for piece in moved)
+    far_theirs, far_mine, near_theirs, kept = down_call(info, hidden, w_down, ring)
+
+    moved = lax.optimization_barrier((*shifted(pieces, "tensor"), kept))[:ring]
+    difference = student_own + sum(piece.astype(F32) for piece in moved)
     own = (difference * total_rows ** (-0.5)).astype(BF16)
     scaled = shifted([own] * ring, "tensor")
-
-    far_theirs, far_mine, near_theirs, kept = down_call(
-        info, after(hidden, *moved[1:]), w_down, ring
-    )
-    over = lambda value, bit: lax.ppermute(value, "tensor", [(i, i ^ bit) for i in range(ring)])
-    far_sum = over(after(far_theirs, *scaled), 1)
+    far_sum = over(after(far_theirs, own), 1)
 
     keep, give = grads_call(
-        after(info, kept),
+        info,
         scaled,
         student_normed,
         s_hidden,
@@ -848,22 +813,16 @@
         gate_slope,
         chips,
     )
-    far_sum = (after(far_sum, keep).astype(F32) + far_mine.astype(F32)).astype(BF16)
-    shares = flipped(pair_call(keep, after(swapped(give), far_sum)))
+    shares = pair_call(keep, swapped(give))
+    far_sum = (after(far_sum, shares[0]).astype(F32) + far_mine.astype(F32)).astype(BF16)
+    shares = flipped(shares)
     own = sum(share.astype(F32) for share in shares).astype(BF16)
     mine = flipped([own] * chips)
     others = [swapped(share) for share in mine]
 
     level_sums = [over(after(near_theirs, far_sum), 1), over(far_sum, 2)]
     mlp_own = sum(after(value, mine[-1]).astype(F32) for value in level_sums)
-    teacher = mixed_own.astype(F32) + (kept.astype(F32) + mlp_own)
-    teacher = teacher.astype(BF16)
-    back = swapped(teacher[half:])
-    teacher_out = jnp.where(
-        first_core,
-        jnp.concatenate([teacher[:half], back], axis=0),
-        jnp.concatenate([back, teacher[:half]], axis=0),
-    )
+    teacher_out = (mixed_own.astype(F32) + (kept.astype(F32) + mlp_own)).astype(BF16)
     grad_gate, grad_up, grad_down, notes = finish_call(info, mine, others, ring)
     return teacher_out, grad_gate, grad_up, grad_down, notes[0, 0, 0] / sd
 

time: 243 us -> 248 us (1.021)
  waiting for transfers between devices: 124 us -> 140 us
  Pallas kernels: 54.2 us -> 48.1 us
  starting transfers between devices: 43.8 us -> 38.4 us
    ppermute x18, waiting for transfers between devices: 15.5 us -> 31.3 us  [flipped(): lax.ppermute(pieces[f], 'dp', [(i, i ^ 2 * f) for i in range(size)])]
    pallas_call x1, Pallas kernels: 13.8 us -> 8.25 us  [attention_call(): pl.pallas_call(functools.partial(attention_kernel, chips=chips, ring=ring...]
    ppermute x9 -> x6, waiting for transfers between devices: 17.4 us -> 12.1 us  [shifted(): lax.ppermute(pieces[s], axis, [(i, (i + s) % size) for i in range(size)])]
    ppermute x9 -> x6, starting transfers between devices: 12.6 us -> 7.97 us  [shifted(): lax.ppermute(pieces[s], axis, [(i, (i + s) % size) for i in range(size)])]
    ppermute x12, waiting for transfers between devices: 61.8 us -> 65.1 us  [step_on(): return lax.ppermute(block, axis, [(i, (i + 1) % size) for i in range(size)])]
    ppermute x3 -> x5, waiting for transfers between devices: 26.1 us -> 27 us  [paired(): lax.ppermute(value, 'tensor', [(i, i ^ bit) for i in range(ring)])]
  transfers between devices with their start and end apart: 60 -> 55, of which waited for: 29 -> 33; matrix products, arithmetic and copies ran while one was open for 6% -> 5% of each run, Pallas kernels for 9% -> 6%
where the time goes in v5:
time: 248 us; the launch traced here: 247 us
  waiting for transfers between devices  140 us (56%)
  Pallas kernels  48.1 us (19%)
  starting transfers between devices  38.4 us (15%)
  matrix products  7.32 us (3%)
  other arithmetic  6.13 us (2%)
  local copies, waits for them, and re-layouts  5.07 us (2%)
  between operations  2.85 us (1%)
    ppermute x12, waiting for transfers between devices, step_on(): return lax.ppermute(block, axis, [(i, (i + 1) % size) for i in range(size)])  65.1 us
    ppermute x18, waiting for transfers between devices, flipped(): lax.ppermute(pieces[f], 'dp', [(i, i ^ 2 * f) for i in range(size)])  31.3 us
    ppermute x5, waiting for transfers between devices, paired(): lax.ppermute(value, 'tensor', [(i, i ^ bit) for i in range(ring)])  27 us
    pallas_call x1, Pallas kernels, middle_call(): pl.pallas_call(functools.partial(middle_kernel, ring=ring, chips=chips),...  22.2 us
    ppermute x18, starting transfers between devices, flipped(): lax.ppermute(pieces[f], 'dp', [(i, i ^ 2 * f) for i in range(size)])  21.6 us
    ppermute x6, waiting for transfers between devices, shifted(): lax.ppermute(pieces[s], axis, [(i, (i + s) % size) for i in range(size)])  12.1 us
    pallas_call x1, Pallas kernels, attention_call(): pl.pallas_call(functools.partial(attention_kernel, chips=chips, ring=ring...  8.25 us
    ppermute x6, starting transfers between devices, shifted(): lax.ppermute(pieces[s], axis, [(i, (i + s) % size) for i in range(size)])  7.97 us
  transfers between devices with their start and end apart: 55, of which 33 were waited for; matrix products, arithmetic and copies ran while one was open for 5% of the time, Pallas kernels for 6%

profile of v5, /device:TPU:0, one launch (start us, length us, event | category | flops | bytes accessed | tf_op | source)
XLA Modules:
  0.0 247.5 jit_solution(18286753468325046630)
XLA Ops:
  0.7 1.1 fusion.10
  1.8 3.1 %collective-permute-start.3 = (bf16[256,512]{1,0:T(8,128)(2,1)S(1)}, bf16[256,512]{1,0:T(8,128)(2,1)S(1)}, u32[]{:S(2)}, u32[]{:S(2)}) collective-permute-start(bf16[256,512]{1,0:T(8,128)(2,1)S(1)} %get-tuple-element.140.refs_4_), channel_id=1, source_target_pairs={{0,1},{1,2},{2,3},{3,0},{4,5},{5,6},{6,7},{7,4},{8,9},{9,10},{10,1... | collective-permute-start | bytes 786440 | tf_op jit(solution)/shard_map/ppermute | solution.py:659
  4.9 1.6 collective-permute-start
  7.2 1.0 fusion.3
  8.6 5.5 %collective-permute-done.3.refs_5_ = bf16[256,512]{1,0:T(8,128)(2,1)S(1)} collective-permute-done((bf16[256,512]{1,0:T(8,128)(2,1)S(1)}, bf16[256,512]{1,0:T(8,128)(2,1)S(1)}, u32[]{:S(2)}, u32[]{:S(2)}) %collective-permute-start.3) | collective-permute-done | bytes 262176 | tf_op jit(solution)/shard_map/ppermute | solution.py:659
  14.1 5.6 %collective-permute-done.refs_1_ = bf16[256,512]{1,0:T(8,128)(2,1)S(1)} collective-permute-done((bf16[256,512]{1,0:T(8,128)(2,1)S(1)}, bf16[256,512]{1,0:T(8,128)(2,1)S(1)}, u32[]{:S(2)}, u32[]{:S(2)}) %collective-permute-start) | collective-permute-done | bytes 262176 | tf_op jit(solution)/shard_map/ppermute | solution.py:659
  19.7 1.1 constant_dynamic-slice_fusion.1
  20.9 1.1 convert_element_type.98
  22.0 3.3 %collective-permute-done.4.refs_6_ = bf16[256,512]{1,0:T(8,128)(2,1)S(1)} collective-permute-done((bf16[256,512]{1,0:T(8,128)(2,1)S(1)}, bf16[256,512]{1,0:T(8,128)(2,1)S(1)}, u32[]{:S(2)}, u32[]{:S(2)}) %collective-permute-start.4) | collective-permute-done | bytes 262176 | tf_op jit(solution)/shard_map/ppermute | solution.py:659
  25.3 5.6 %collective-permute-done.1.refs_2_ = bf16[256,512]{1,0:T(8,128)(2,1)S(1)} collective-permute-done((bf16[256,512]{1,0:T(8,128)(2,1)S(1)}, bf16[256,512]{1,0:T(8,128)(2,1)S(1)}, u32[]{:S(2)}, u32[]{:S(2)}) %collective-permute-start.1) | collective-permute-done | bytes 262176 | tf_op jit(solution)/shard_map/ppermute | solution.py:659
  31.1 5.4 %collective-permute-done.5.refs_7_ = bf16[256,512]{1,0:T(8,128)(2,1)S(1)} collective-permute-done((bf16[256,512]{1,0:T(8,128)(2,1)S(1)}, bf16[256,512]{1,0:T(8,128)(2,1)S(1)}, u32[]{:S(2)}, u32[]{:S(2)}) %collective-permute-start.5) | collective-permute-done | bytes 262176 | tf_op jit(solution)/shard_map/ppermute | solution.py:659
  36.5 4.8 %collective-permute-done.2.refs_3_ = bf16[256,512]{1,0:T(8,128)(2,1)S(1)} collective-permute-done((bf16[256,512]{1,0:T(8,128)(2,1)S(1)}, bf16[256,512]{1,0:T(8,128)(2,1)S(1)}, u32[]{:S(2)}, u32[]{:S(2)}) %collective-permute-start.2) | collective-permute-done | bytes 262176 | tf_op jit(solution)/shard_map/ppermute | solution.py:659
  41.4 6.4 %qkv.1 = (bf16[3,512,128]{2,1,0:T(8,128)(2,1)S(1)}, bf16[3,512,128]{2,1,0:T(8,128)(2,1)S(1)}, bf16[3,512,128]{2,1,0:T(8,128)(2,1)S(1)}, bf16[3,512,128]{2,1,0:T(8,128)(2,1)S(1)}, bf16[512,2048]{1,0:T(8,128)(2,1)S(1)}) custom-call(s32[16]{0:T(128)S(1)} %fusion.9.info_ref, bf16[256,512]{1,0:T(8,128)(2,1)S(1)} %get-tuple-element.141.refs_0_, ...), custom_call_target="tpu_custom_call" | custom-call | flops 3221225472 | bytes 6291456 | tf_op jit(solution)/shard_map/qkv/pallas_call | solution.py:231
  47.7 1.6 collective-permute-start.6
  49.3 1.5 collective-permute-start.7
  51.8 0.8 multiply_convert_fusion
  53.3 5.6 %fusion.refs_26_ = bf16[2048,512]{1,0:T(8,128)(2,1)} fusion(bf16[2048,2048]{1,0:T(8,128)(2,1)S(1)} %bitcast.33, bf16[2048,512]{1,0:T(8,128)(2,1)S(1)} %copy-done.12), kind=kOutput, calls=%fused_computation.1 | convolution fusion | flops 4296015872 | bytes 12582912 | tf_op jit(solution)/shard_map/dot_general | solution.py:166
  59.9 7.6 %collective-permute-done.7.refs_2_ = bf16[3,512,128]{2,1,0:T(8,128)(2,1)S(1)} collective-permute-done((bf16[3,512,128]{2,1,0:T(8,128)(2,1)S(1)}, bf16[3,512,128]{2,1,0:T(8,128)(2,1)S(1)}, u32[]{:S(2)}, u32[]{:S(2)}) %collective-permute-start.7) | collective-permute-done | bytes 393248 | tf_op jit(solution)/shard_map/ppermute | solution.py:681
  69.3 1.5 collective-permute-start.17
  70.8 1.2 collective-permute-start.16
  73.0 8.2 %attention.1 = (bf16[512,128]{1,0:T(8,128)(2,1)S(1)}, bf16[512,128]{1,0:T(8,128)(2,1)S(1)}, bf16[512,128]{1,0:T(8,128)(2,1)S(1)}, bf16[512,128]{1,0:T(8,128)(2,1)S(1)}) custom-call(s32[8]{0:T(128)S(1)} %convert_reduce_fusion.first_ref, s32[16]{0:T(128)S(1)} %fusion.9.info_ref, bf16[3,512,128]{2,1,0:T(8,128)(2,1)S(1)} %get-tuple-element.83.refs_0_, ...), custom_call_target="tpu_custom_call" | custom-call | flops 2147483648 | bytes 4194304 | tf_op jit(solution)/shard_map/attention/pallas_call | solution.py:319
  81.2 2.9 %collective-permute-done.16.refs_12_ = bf16[512,256]{1,0:T(8,128)(2,1)S(1)} collective-permute-done((bf16[512,256]{1,0:T(8,128)(2,1)S(1)}, bf16[512,256]{1,0:T(8,128)(2,1)S(1)}, u32[]{:S(2)}, u32[]{:S(2)}) %collective-permute-start.16) | collective-permute-done | bytes 262176 | tf_op jit(solution)/shard_map/ppermute | solution.py:681
  84.2 9.5 %collective-permute-done.14.refs_14_ = bf16[2,512,256]{2,1,0:T(8,128)(2,1)S(1)} collective-permute-done((bf16[2,512,256]{2,1,0:T(8,128)(2,1)S(1)}, bf16[2,512,256]{2,1,0:T(8,128)(2,1)S(1)}, u32[]{:S(2)}, u32[]{:S(2)}) %collective-permute-start.14) | collective-permute-done | bytes 524320 | tf_op jit(solution)/shard_map/ppermute | solution.py:762
  93.7 1.2 collective-permute-start.18
  95.7 1.4 collective-permute-start.20
  97.2 2.6 %collective-permute-done.18 = bf16[512,128]{1,0:T(8,128)(2,1)S(1)} collective-permute-done((bf16[512,128]{1,0:T(8,128)(2,1)S(1)}, bf16[512,128]{1,0:T(8,128)(2,1)S(1)}, u32[]{:S(2)}, u32[]{:S(2)}) %collective-permute-start.18) | collective-permute-done | bytes 131104 | tf_op jit(solution)/shard_map/ppermute | solution.py:681
  99.8 1.5 collective-permute-done.19
  101.2 1.6 collective-permute-done.20
  103.2 1.8 collective-permute-start.29
  104.9 9.1 %collective-permute-done.21.refs_1_ = bf16[2,512,128]{2,1,0:T(8,128)(2,1)S(1)} collective-permute-done((bf16[2,512,128]{2,1,0:T(8,128)(2,1)S(1)}, bf16[2,512,128]{2,1,0:T(8,128)(2,1)S(1)}, u32[]{:S(2)}, u32[]{:S(2)}) %collective-permute-start.21) | collective-permute-done | bytes 262176 | tf_op jit(solution)/shard_map/ppermute | solution.py:659
  114.8 1.5 collective-permute-start.27
  116.3 3.3 %collective-permute-done.24.refs_5_ = bf16[2,512,128]{2,1,0:T(8,128)(2,1)S(1)} collective-permute-done((bf16[2,512,128]{2,1,0:T(8,128)(2,1)S(1)}, bf16[2,512,128]{2,1,0:T(8,128)(2,1)S(1)}, u32[]{:S(2)}, u32[]{:S(2)}) %collective-permute-start.24) | collective-permute-done | bytes 262176 | tf_op jit(solution)/shard_map/ppermute | solution.py:659
  119.8 5.5 %collective-permute-done.22.refs_2_ = bf16[2,512,128]{2,1,0:T(8,128)(2,1)S(1)} collective-permute-done((bf16[2,512,128]{2,1,0:T(8,128)(2,1)S(1)}, bf16[2,512,128]{2,1,0:T(8,128)(2,1)S(1)}, u32[]{:S(2)}, u32[]{:S(2)}) %collective-permute-start.22) | collective-permute-done | bytes 262176 | tf_op jit(solution)/shard_map/ppermute | solution.py:659
  125.2 3.8 %collective-permute-done.25.refs_6_ = bf16[2,512,128]{2,1,0:T(8,128)(2,1)S(1)} collective-permute-done((bf16[2,512,128]{2,1,0:T(8,128)(2,1)S(1)}, bf16[2,512,128]{2,1,0:T(8,128)(2,1)S(1)}, u32[]{:S(2)}, u32[]{:S(2)}) %collective-permute-start.25) | collective-permute-done | bytes 262176 | tf_op jit(solution)/shard_map/ppermute | solution.py:659
  129.6 10.4 %collective-permute-done.23.refs_3_ = bf16[2,512,128]{2,1,0:T(8,128)(2,1)S(1)} collective-permute-done((bf16[2,512,128]{2,1,0:T(8,128)(2,1)S(1)}, bf16[2,512,128]{2,1,0:T(8,128)(2,1)S(1)}, u32[]{:S(2)}, u32[]{:S(2)}) %collective-permute-start.23) | collective-permute-done | bytes 262176 | tf_op jit(solution)/shard_map/ppermute | solution.py:659
  140.0 2.8 %collective-permute-done.26.refs_7_ = bf16[2,512,128]{2,1,0:T(8,128)(2,1)S(1)} collective-permute-done((bf16[2,512,128]{2,1,0:T(8,128)(2,1)S(1)}, bf16[2,512,128]{2,1,0:T(8,128)(2,1)S(1)}, u32[]{:S(2)}, u32[]{:S(2)}) %collective-permute-start.26) | collective-permute-done | bytes 262176 | tf_op jit(solution)/shard_map/ppermute | solution.py:659
  142.9 1.9 collective-permute-done.32.refs_20_
  144.8 22.2 %middle.1 = (bf16[512,2048]{1,0:T(8,128)(2,1)}, bf16[512,512]{1,0:T(8,128)(2,1)S(1)}, bf16[128,512]{1,0:T(8,128)(2,1)S(1)}, bf16[128,512]{1,0:T(8,128)(2,1)S(1)}...) custom-call(s32[16]{0:T(128)S(1)} %fusion.9.info_ref, bf16[2,512,128]{2,1,0:T(8,128)(2,1)S(1)} %pad_maximum_fusion.3.refs_0_, ...), custom_call_target="tpu_custom_call" | custom-call | flops 14227079168 | bytes 25165824 | tf_op jit(solution)/shard_map/middle/pallas_call | solution.py:463
  167.2 3.7 %collective-permute-start.37 = (bf16[128,512]{1,0:T(8,128)(2,1)S(1)}, bf16[128,512]{1,0:T(8,128)(2,1)S(1)}, u32[]{:S(2)}, u32[]{:S(2)}) collective-permute-start(bf16[128,512]{1,0:T(8,128)(2,1)S(1)} %get-tuple-element.116), channel_id=1, source_target_pairs={{0,3},{1,0},{2,1},{3,2},{4,7},{5,4},{6,5},{7,6},{8,11},{9,8},{10,9... | collective-permute-start | bytes 393224 | tf_op jit(solution)/shard_map/ppermute | solution.py:672
  170.9 1.6 copy-done.8
  172.5 6.5 %down.1 = (bf16[512,512]{1,0:T(8,128)(2,1)S(1)}, bf16[512,512]{1,0:T(8,128)(2,1)S(1)}, bf16[512,512]{1,0:T(8,128)(2,1)S(1)}, bf16[512,512]{1,0:T(8,128)(2,1)S(1)}) custom-call(s32[16]{0:T(128)S(1)} %fusion.9.info_ref, bf16[512,2048]{1,0:T(8,128)(2,1)S(1)} %copy-done.8, bf16[2048,2048]{1,0:T(8,128)(2,1)S(1)} %bitcast.33), custom_call_target="tpu_custom_call" | custom-call | flops 4294967296 | bytes 8388608 | tf_op jit(solution)/shard_map/down/pallas_call | solution.py:536
  179.0 1.0 collective-permute-done.36
  180.0 1.1 multiply_convert_fusion.3.refs_0_
  181.1 2.7 %collective-permute-start.41 = (bf16[128,512]{1,0:T(8,128)(2,1)S(1)}, bf16[128,512]{1,0:T(8,128)(2,1)S(1)}, u32[]{:S(2)}, u32[]{:S(2)}) collective-permute-start(bf16[128,512]{1,0:T(8,128)(2,1)S(1)} %multiply_convert_fusion.3.refs_0_), channel_id=1, source_target_pairs={{0,3},{1,0},{2,1},{3,2},{4,7},{5,4},{6,5},{7,6},{8,11},{9,8},{10,9... | collective-permute-start | bytes 393224 | tf_op jit(solution)/shard_map/ppermute | solution.py:672
  183.8 1.4 collective-permute-start.40
  185.2 2.5 %collective-permute-done.41.refs_3_ = bf16[128,512]{1,0:T(8,128)(2,1)S(1)} collective-permute-done((bf16[128,512]{1,0:T(8,128)(2,1)S(1)}, bf16[128,512]{1,0:T(8,128)(2,1)S(1)}, u32[]{:S(2)}, u32[]{:S(2)}) %collective-permute-start.41) | collective-permute-done | bytes 131104 | tf_op jit(solution)/shard_map/ppermute | solution.py:672
  187.7 8.6 %collective-permute-done.40.refs_2_ = bf16[128,512]{1,0:T(8,128)(2,1)S(1)} collective-permute-done((bf16[128,512]{1,0:T(8,128)(2,1)S(1)}, bf16[128,512]{1,0:T(8,128)(2,1)S(1)}, u32[]{:S(2)}, u32[]{:S(2)}) %collective-permute-start.40) | collective-permute-done | bytes 131104 | tf_op jit(solution)/shard_map/ppermute | solution.py:672
  196.3 2.2 grads.1
  198.7 2.3 collective-permute-done.42.theirs_ref
  201.2 11.8 %collective-permute-done.38 = bf16[512,512]{1,0:T(8,128)(2,1)S(1)} collective-permute-done((bf16[512,512]{1,0:T(8,128)(2,1)S(1)}, bf16[512,512]{1,0:T(8,128)(2,1)S(1)}, u32[]{:S(2)}, u32[]{:S(2)}) %collective-permute-start.38) | collective-permute-done | bytes 524320 | tf_op jit(solution)/shard_map/ppermute | solution.py:762
  213.0 1.1 collective-permute-start.45
  214.1 2.3 collective-permute-start.46
  217.0 0.9 collective-permute-start.48
  217.9 3.3 %collective-permute-done.44 = bf16[208,512]{1,0:T(8,128)(2,1)S(1)} collective-permute-done((bf16[208,512]{1,0:T(8,128)(2,1)S(1)}, bf16[208,512]{1,0:T(8,128)(2,1)S(1)}, u32[]{:S(2)}, u32[]{:S(2)}) %collective-permute-start.44) | collective-permute-done | bytes 213024 | tf_op jit(solution)/shard_map/ppermute | solution.py:681
  221.1 3.2 %collective-permute-done.45 = bf16[208,512]{1,0:T(8,128)(2,1)S(1)} collective-permute-done((bf16[208,512]{1,0:T(8,128)(2,1)S(1)}, bf16[208,512]{1,0:T(8,128)(2,1)S(1)}, u32[]{:S(2)}, u32[]{:S(2)}) %collective-permute-start.45) | collective-permute-done | bytes 213024 | tf_op jit(solution)/shard_map/ppermute | solution.py:681
  224.5 1.5 collective-permute-start.50
  226.7 1.4 collective-permute-start.47
  228.0 4.0 %collective-permute-done.50.refs_2_ = bf16[208,512]{1,0:T(8,128)(2,1)S(1)} collective-permute-done((bf16[208,512]{1,0:T(8,128)(2,1)S(1)}, bf16[208,512]{1,0:T(8,128)(2,1)S(1)}, u32[]{:S(2)}, u32[]{:S(2)}) %collective-permute-start.50) | collective-permute-done | bytes 213024 | tf_op jit(solution)/shard_map/ppermute | solution.py:681
  232.0 1.9 collective-permute-done.49.refs_1_
  233.9 2.1 collective-permute-done.47.refs_3_
  236.1 3.8 %collective-permute-done.43 = bf16[512,512]{1,0:T(8,128)(2,1)S(1)} collective-permute-done((bf16[512,512]{1,0:T(8,128)(2,1)S(1)}, bf16[512,512]{1,0:T(8,128)(2,1)S(1)}, u32[]{:S(2)}, u32[]{:S(2)}) %collective-permute-start.43) | collective-permute-done | bytes 524320 | tf_op jit(solution)/shard_map/ppermute | solution.py:762
  239.9 1.8 collective-permute-done.48
  241.7 1.1 add_convert_fusion
  242.8 2.4 finish.1
  (109 shorter events, 11.6 us)
Async XLA Ops:
  0.6 51.1 %copy-start = (bf16[512,512]{1,0:T(8,128)(2,1)S(1)}, bf16[512,512]{1,0:T(8,128)(2,1)}, u32[]{:S(2)}) copy-start(bf16[512,512]{1,0:T(8,128)(2,1)} %param.31) | copy-start | bytes 1572868
  1.8 12.2 %collective-permute-start.3 = (bf16[256,512]{1,0:T(8,128)(2,1)S(1)}, bf16[256,512]{1,0:T(8,128)(2,1)S(1)}, u32[]{:S(2)}, u32[]{:S(2)}) collective-permute-start(bf16[256,512]{1,0:T(8,128)(2,1)S(1)} %get-tuple-element.140.refs_4_), channel_id=1, source_target_pairs={{0,1},{1,2},{2,3},{3,0},{4,5},{5,6},{6,7},{7,4},{8,9},{9,10},{10,1... | collective-permute-start | bytes 786440 | tf_op jit(solution)/shard_map/ppermute | solution.py:659
  4.9 14.8 %collective-permute-start = (bf16[256,512]{1,0:T(8,128)(2,1)S(1)}, bf16[256,512]{1,0:T(8,128)(2,1)S(1)}, u32[]{:S(2)}, u32[]{:S(2)}) collective-permute-start(bf16[256,512]{1,0:T(8,128)(2,1)S(1)} %get-tuple-element.141.refs_0_), channel_id=1, source_target_pairs={{0,1},{1,2},{2,3},{3,0},{4,5},{5,6},{6,7},{7,4},{8,9},{9,10},{10,1... | collective-permute-start | bytes 786440 | tf_op jit(solution)/shard_map/ppermute | solution.py:659
  8.2 33.2 %copy-start.4 = (bf16[2048,512]{1,0:T(8,128)(2,1)S(1)}, bf16[2048,512]{1,0:T(8,128)(2,1)}, u32[]{:S(2)}) copy-start(bf16[2048,512]{1,0:T(8,128)(2,1)} %refs_12_.1) | copy-start | bytes 6291460
  8.4 32.9 %copy-start.3 = (bf16[2048,512]{1,0:T(8,128)(2,1)S(1)}, bf16[2048,512]{1,0:T(8,128)(2,1)}, u32[]{:S(2)}) copy-start(bf16[2048,512]{1,0:T(8,128)(2,1)} %refs_11_.1) | copy-start | bytes 6291460
  8.4 32.9 %copy-start.5 = (f32[2048]{0:T(1024)S(1)}, f32[2048]{0:T(1024)}, u32[]{:S(2)}) copy-start(f32[2048]{0:T(1024)} %param.20) | copy-start | bytes 24580
  14.1 11.2 %collective-permute-start.4 = (bf16[256,512]{1,0:T(8,128)(2,1)S(1)}, bf16[256,512]{1,0:T(8,128)(2,1)S(1)}, u32[]{:S(2)}, u32[]{:S(2)}) collective-permute-start(bf16[256,512]{1,0:T(8,128)(2,1)S(1)} %collective-permute-done.3.refs_5_), channel_id=1, source_target_pairs={{0,1},{1,2},{2,3},{3,0},{4,5},{5,6},{6,7},{7,4},{8,9},{9,10},{10,1... | collective-permute-start | bytes 786440 | tf_op jit(solution)/shard_map/ppermute | solution.py:659
  19.7 11.2 %collective-permute-start.1 = (bf16[256,512]{1,0:T(8,128)(2,1)S(1)}, bf16[256,512]{1,0:T(8,128)(2,1)S(1)}, u32[]{:S(2)}, u32[]{:S(2)}) collective-permute-start(bf16[256,512]{1,0:T(8,128)(2,1)S(1)} %collective-permute-done.refs_1_), channel_id=1, source_target_pairs={{0,1},{1,2},{2,3},{3,0},{4,5},{5,6},{6,7},{7,4},{8,9},{9,10},{10,1... | collective-permute-start | bytes 786440 | tf_op jit(solution)/shard_map/ppermute | solution.py:659
  25.3 11.2 %collective-permute-start.5 = (bf16[256,512]{1,0:T(8,128)(2,1)S(1)}, bf16[256,512]{1,0:T(8,128)(2,1)S(1)}, u32[]{:S(2)}, u32[]{:S(2)}) collective-permute-start(bf16[256,512]{1,0:T(8,128)(2,1)S(1)} %collective-permute-done.4.refs_6_), channel_id=1, source_target_pairs={{0,1},{1,2},{2,3},{3,0},{4,5},{5,6},{6,7},{7,4},{8,9},{9,10},{10,1... | collective-permute-start | bytes 786440 | tf_op jit(solution)/shard_map/ppermute | solution.py:659
  30.9 10.4 %collective-permute-start.2 = (bf16[256,512]{1,0:T(8,128)(2,1)S(1)}, bf16[256,512]{1,0:T(8,128)(2,1)S(1)}, u32[]{:S(2)}, u32[]{:S(2)}) collective-permute-start(bf16[256,512]{1,0:T(8,128)(2,1)S(1)} %collective-permute-done.1.refs_2_), channel_id=1, source_target_pairs={{0,1},{1,2},{2,3},{3,0},{4,5},{5,6},{6,7},{7,4},{8,9},{9,10},{10,1... | collective-permute-start | bytes 786440 | tf_op jit(solution)/shard_map/ppermute | solution.py:659
  31.0 21.8 %slice-start = ((s8[8388608]{0:T(1024)(128)(4,1)}), s8[4194304]{0:T(1024)(128)(4,1)S(1)}, s32[]{:S(2)}) async-start(s8[8388608]{0:T(1024)(128)(4,1)} %bitcast.32), calls=%async_computation | async-start | bytes 8388608
  41.3 10.0 %copy-start.10 = (bf16[512,512]{1,0:T(8,128)(2,1)S(1)}, bf16[512,512]{1,0:T(8,128)(2,1)}, u32[]{:S(2)}) copy-start(bf16[512,512]{1,0:T(8,128)(2,1)} %param.32) | copy-start | bytes 1572868
  41.4 11.4 %slice-start.1 = ((s8[8388608]{0:T(1024)(128)(4,1)}), s8[4194304]{0:T(1024)(128)(4,1)S(1)}, s32[]{:S(2)}) async-start(s8[8388608]{0:T(1024)(128)(4,1)} %bitcast.32), calls=%async_computation.1 | async-start | bytes 8388608
  47.7 12.1 %collective-permute-start.6 = (bf16[3,512,128]{2,1,0:T(8,128)(2,1)S(1)}, bf16[3,512,128]{2,1,0:T(8,128)(2,1)S(1)}, u32[]{:S(2)}, u32[]{:S(2)}) collective-permute-start(bf16[3,512,128]{2,1,0:T(8,128)(2,1)S(1)} %get-tuple-element.74), channel_id=1, source_target_pairs={{0,8},{4,12},{8,0},{12,4},{16,24},{20,28},{24,16},{28,20},{1,9},{5... | collective-permute-start | bytes 1179656 | tf_op jit(solution)/shard_map/ppermute | solution.py:681
  49.3 18.2 %collective-permute-start.7 = (bf16[3,512,128]{2,1,0:T(8,128)(2,1)S(1)}, bf16[3,512,128]{2,1,0:T(8,128)(2,1)S(1)}, u32[]{:S(2)}, u32[]{:S(2)}) collective-permute-start(bf16[3,512,128]{2,1,0:T(8,128)(2,1)S(1)} %get-tuple-element.75), channel_id=1, source_target_pairs={{0,16},{4,20},{8,24},{12,28},{16,0},{20,4},{24,8},{28,12},{1,17},{... | collective-permute-start | bytes 1179656 | tf_op jit(solution)/shard_map/ppermute | solution.py:681
  50.8 16.7 %collective-permute-start.8 = (bf16[3,512,128]{2,1,0:T(8,128)(2,1)S(1)}, bf16[3,512,128]{2,1,0:T(8,128)(2,1)S(1)}, u32[]{:S(2)}, u32[]{:S(2)}) collective-permute-start(bf16[3,512,128]{2,1,0:T(8,128)(2,1)S(1)} %get-tuple-element.76), channel_id=1, source_target_pairs={{0,24},{4,28},{8,16},{12,20},{16,8},{20,12},{24,0},{28,4},{1,25},{... | collective-permute-start | bytes 1179656 | tf_op jit(solution)/shard_map/ppermute | solution.py:681
  52.6 6.8 %collective-permute-start.9 = (bf16[512,256]{1,0:T(8,128)(2,1)S(1)}, bf16[512,256]{1,0:T(8,128)(2,1)S(1)}, u32[]{:S(2)}, u32[]{:S(2)}) collective-permute-start(bf16[512,256]{1,0:T(8,128)(2,1)S(1)} %constant_dynamic-slice_fusion.1), channel_id=1, source_target_pairs={{0,1},{1,0},{2,3},{3,2},{4,5},{5,4},{6,7},{7,6},{8,9},{9,8},{10,11... | collective-permute-start | bytes 786440 | tf_op jit(solution)/shard_map/ppermute | solution.py:762
  58.9 13.9 %copy-start.11 = (s32[4096]{0:T(1024)S(1)}, s32[4096]{0:T(1024)}, u32[]{:S(2)}) copy-start(s32[4096]{0:T(1024)} %param.18) | copy-start | bytes 49156
  67.5 1.8 collective-permute-start.10
  67.5 3.3 %collective-permute-start.11 = (bf16[3,512,128]{2,1,0:T(8,128)(2,1)S(1)}, bf16[3,512,128]{2,1,0:T(8,128)(2,1)S(1)}, u32[]{:S(2)}, u32[]{:S(2)}) collective-permute-start(bf16[3,512,128]{2,1,0:T(8,128)(2,1)S(1)} %collective-permute-done.6.refs_1_), channel_id=1, source_target_pairs={{0,4},{4,0},{8,12},{12,8},{16,20},{20,16},{24,28},{28,24},{1,5},{5... | collective-permute-start | bytes 1179656 | tf_op jit(solution)/shard_map/ppermute | solution.py:689
  68.0 4.0 %collective-permute-start.12 = (bf16[3,512,128]{2,1,0:T(8,128)(2,1)S(1)}, bf16[3,512,128]{2,1,0:T(8,128)(2,1)S(1)}, u32[]{:S(2)}, u32[]{:S(2)}) collective-permute-start(bf16[3,512,128]{2,1,0:T(8,128)(2,1)S(1)} %collective-permute-done.7.refs_2_), channel_id=1, source_target_pairs={{0,4},{4,0},{8,12},{12,8},{16,20},{20,16},{24,28},{28,24},{1,5},{5... | collective-permute-start | bytes 1179656 | tf_op jit(solution)/shard_map/ppermute | solution.py:689
  68.0 4.9 %collective-permute-start.13 = (bf16[3,512,128]{2,1,0:T(8,128)(2,1)S(1)}, bf16[3,512,128]{2,1,0:T(8,128)(2,1)S(1)}, u32[]{:S(2)}, u32[]{:S(2)}) collective-permute-start(bf16[3,512,128]{2,1,0:T(8,128)(2,1)S(1)} %collective-permute-done.8.refs_3_), channel_id=1, source_target_pairs={{0,4},{4,0},{8,12},{12,8},{16,20},{20,16},{24,28},{28,24},{1,5},{5... | collective-permute-start | bytes 1179656 | tf_op jit(solution)/shard_map/ppermute | solution.py:689
  68.6 25.1 %collective-permute-start.14 = (bf16[2,512,256]{2,1,0:T(8,128)(2,1)S(1)}, bf16[2,512,256]{2,1,0:T(8,128)(2,1)S(1)}, u32[]{:S(2)}, u32[]{:S(2)}) collective-permute-start(bf16[2,512,256]{2,1,0:T(8,128)(2,1)S(1)} %pad_maximum_fusion), channel_id=1, source_target_pairs={{0,2},{1,3},{2,0},{3,1},{4,6},{5,7},{6,4},{7,5},{8,10},{9,11},{10,... | collective-permute-start | bytes 1572872 | tf_op jit(solution)/shard_map/ppermute | solution.py:762
  69.3 11.9 %collective-permute-start.17 = (bf16[512,256]{1,0:T(8,128)(2,1)S(1)}, bf16[512,256]{1,0:T(8,128)(2,1)S(1)}, u32[]{:S(2)}, u32[]{:S(2)}) collective-permute-start(bf16[512,256]{1,0:T(8,128)(2,1)S(1)} %collective-permute-done.9.refs_10_), channel_id=1, source_target_pairs={{0,24},{4,28},{8,16},{12,20},{16,8},{20,12},{24,0},{28,4},{1,25},{... | collective-permute-start | bytes 786440 | tf_op jit(solution)/shard_map/ppermute | solution.py:681
  70.8 13.3 %collective-permute-start.16 = (bf16[512,256]{1,0:T(8,128)(2,1)S(1)}, bf16[512,256]{1,0:T(8,128)(2,1)S(1)}, u32[]{:S(2)}, u32[]{:S(2)}) collective-permute-start(bf16[512,256]{1,0:T(8,128)(2,1)S(1)} %collective-permute-done.9.refs_10_), channel_id=1, source_target_pairs={{0,16},{4,20},{8,24},{12,28},{16,0},{20,4},{24,8},{28,12},{1,17},{... | collective-permute-start | bytes 786440 | tf_op jit(solution)/shard_map/ppermute | solution.py:681
  72.0 12.2 %collective-permute-start.15 = (bf16[512,256]{1,0:T(8,128)(2,1)S(1)}, bf16[512,256]{1,0:T(8,128)(2,1)S(1)}, u32[]{:S(2)}, u32[]{:S(2)}) collective-permute-start(bf16[512,256]{1,0:T(8,128)(2,1)S(1)} %collective-permute-done.9.refs_10_), channel_id=1, source_target_pairs={{0,8},{4,12},{8,0},{12,4},{16,24},{20,28},{24,16},{28,20},{1,9},{5... | collective-permute-start | bytes 786440 | tf_op jit(solution)/shard_map/ppermute | solution.py:681
  81.2 63.6 %copy-start.6 = (f32[2048]{0:T(1024)S(1)}, f32[2048]{0:T(1024)}, u32[]{:S(2)}) copy-start(f32[2048]{0:T(1024)} %param.21) | copy-start | bytes 24580
  93.7 6.1 %collective-permute-start.18 = (bf16[512,128]{1,0:T(8,128)(2,1)S(1)}, bf16[512,128]{1,0:T(8,128)(2,1)S(1)}, u32[]{:S(2)}, u32[]{:S(2)}) collective-permute-start(bf16[512,128]{1,0:T(8,128)(2,1)S(1)} %get-tuple-element.93), channel_id=1, source_target_pairs={{0,8},{4,12},{8,0},{12,4},{16,24},{20,28},{24,16},{28,20},{1,9},{5... | collective-permute-start | bytes 393224 | tf_op jit(solution)/shard_map/ppermute | solution.py:681
  94.9 6.3 %collective-permute-start.19 = (bf16[512,128]{1,0:T(8,128)(2,1)S(1)}, bf16[512,128]{1,0:T(8,128)(2,1)S(1)}, u32[]{:S(2)}, u32[]{:S(2)}) collective-permute-start(bf16[512,128]{1,0:T(8,128)(2,1)S(1)} %get-tuple-element.94), channel_id=1, source_target_pairs={{0,16},{4,20},{8,24},{12,28},{16,0},{20,4},{24,8},{28,12},{1,17},{... | collective-permute-start | bytes 393224 | tf_op jit(solution)/shard_map/ppermute | solution.py:681
  95.7 7.1 %collective-permute-start.20 = (bf16[512,128]{1,0:T(8,128)(2,1)S(1)}, bf16[512,128]{1,0:T(8,128)(2,1)S(1)}, u32[]{:S(2)}, u32[]{:S(2)}) collective-permute-start(bf16[512,128]{1,0:T(8,128)(2,1)S(1)} %get-tuple-element.95), channel_id=1, source_target_pairs={{0,24},{4,28},{8,16},{12,20},{16,8},{20,12},{24,0},{28,4},{1,25},{... | collective-permute-start | bytes 393224 | tf_op jit(solution)/shard_map/ppermute | solution.py:681
  102.9 11.1 %collective-permute-start.21 = (bf16[2,512,128]{2,1,0:T(8,128)(2,1)S(1)}, bf16[2,512,128]{2,1,0:T(8,128)(2,1)S(1)}, u32[]{:S(2)}, u32[]{:S(2)}) collective-permute-start(bf16[2,512,128]{2,1,0:T(8,128)(2,1)S(1)} %pad_maximum_fusion.3.refs_0_), channel_id=1, source_target_pairs={{0,1},{1,2},{2,3},{3,0},{4,5},{5,6},{6,7},{7,4},{8,9},{9,10},{10,1... | collective-permute-start | bytes 786440 | tf_op jit(solution)/shard_map/ppermute | solution.py:659
  103.0 16.6 %collective-permute-start.24 = (bf16[2,512,128]{2,1,0:T(8,128)(2,1)S(1)}, bf16[2,512,128]{2,1,0:T(8,128)(2,1)S(1)}, u32[]{:S(2)}, u32[]{:S(2)}) collective-permute-start(bf16[2,512,128]{2,1,0:T(8,128)(2,1)S(1)} %pad_maximum_fusion.4.refs_4_), channel_id=1, source_target_pairs={{0,1},{1,2},{2,3},{3,0},{4,5},{5,6},{6,7},{7,4},{8,9},{9,10},{10,1... | collective-permute-start | bytes 786440 | tf_op jit(solution)/shard_map/ppermute | solution.py:659
  103.2 25.9 %collective-permute-start.29 = (bf16[2,512,256]{2,1,0:T(8,128)(2,1)S(1)}, bf16[2,512,256]{2,1,0:T(8,128)(2,1)S(1)}, u32[]{:S(2)}, u32[]{:S(2)}) collective-permute-start(bf16[2,512,256]{2,1,0:T(8,128)(2,1)S(1)} %collective-permute-done.14.refs_14_), channel_id=1, source_target_pairs={{0,24},{4,28},{8,16},{12,20},{16,8},{20,12},{24,0},{28,4},{1,25},{... | collective-permute-start | bytes 1572872 | tf_op jit(solution)/shard_map/ppermute | solution.py:681
  114.0 11.2 %collective-permute-start.22 = (bf16[2,512,128]{2,1,0:T(8,128)(2,1)S(1)}, bf16[2,512,128]{2,1,0:T(8,128)(2,1)S(1)}, u32[]{:S(2)}, u32[]{:S(2)}) collective-permute-start(bf16[2,512,128]{2,1,0:T(8,128)(2,1)S(1)} %collective-permute-done.21.refs_1_), channel_id=1, source_target_pairs={{0,1},{1,2},{2,3},{3,0},{4,5},{5,6},{6,7},{7,4},{8,9},{9,10},{10,1... | collective-permute-start | bytes 786440 | tf_op jit(solution)/shard_map/ppermute | solution.py:659
  114.0 15.0 %collective-permute-start.28 = (bf16[2,512,256]{2,1,0:T(8,128)(2,1)S(1)}, bf16[2,512,256]{2,1,0:T(8,128)(2,1)S(1)}, u32[]{:S(2)}, u32[]{:S(2)}) collective-permute-start(bf16[2,512,256]{2,1,0:T(8,128)(2,1)S(1)} %collective-permute-done.14.refs_14_), channel_id=1, source_target_pairs={{0,16},{4,20},{8,24},{12,28},{16,0},{20,4},{24,8},{28,12},{1,17},{... | collective-permute-start | bytes 1572872 | tf_op jit(solution)/shard_map/ppermute | solution.py:681
  114.8 14.3 %collective-permute-start.27 = (bf16[2,512,256]{2,1,0:T(8,128)(2,1)S(1)}, bf16[2,512,256]{2,1,0:T(8,128)(2,1)S(1)}, u32[]{:S(2)}, u32[]{:S(2)}) collective-permute-start(bf16[2,512,256]{2,1,0:T(8,128)(2,1)S(1)} %collective-permute-done.14.refs_14_), channel_id=1, source_target_pairs={{0,8},{4,12},{8,0},{12,4},{16,24},{20,28},{24,16},{28,20},{1,9},{5... | collective-permute-start | bytes 1572872 | tf_op jit(solution)/shard_map/ppermute | solution.py:681
  119.6 9.4 %collective-permute-start.25 = (bf16[2,512,128]{2,1,0:T(8,128)(2,1)S(1)}, bf16[2,512,128]{2,1,0:T(8,128)(2,1)S(1)}, u32[]{:S(2)}, u32[]{:S(2)}) collective-permute-start(bf16[2,512,128]{2,1,0:T(8,128)(2,1)S(1)} %collective-permute-done.24.refs_5_), channel_id=1, source_target_pairs={{0,1},{1,2},{2,3},{3,0},{4,5},{5,6},{6,7},{7,4},{8,9},{9,10},{10,1... | collective-permute-start | bytes 786440 | tf_op jit(solution)/shard_map/ppermute | solution.py:659
  125.2 19.6 %collective-permute-start.30 = (bf16[4,1,512,256]{3,2,0,1:T(8,128)(2,1)S(1)}, bf16[4,1,512,256]{3,2,0,1:T(8,128)(2,1)S(1)}, u32[]{:S(2)}, u32[]{:S(2)}) collective-permute-start(bf16[4,1,512,256]{3,2,0,1:T(8,128)(2,1)S(1)} %maximum_bitcast_fusion), channel_id=1, source_target_pairs={{0,4},{4,0},{8,12},{12,8},{16,20},{20,16},{24,28},{28,24},{1,5},{5... | collective-permute-start | bytes 3145736 | tf_op jit(solution)/shard_map/ppermute | solution.py:689
  129.0 11.0 %collective-permute-start.23 = (bf16[2,512,128]{2,1,0:T(8,128)(2,1)S(1)}, bf16[2,512,128]{2,1,0:T(8,128)(2,1)S(1)}, u32[]{:S(2)}, u32[]{:S(2)}) collective-permute-start(bf16[2,512,128]{2,1,0:T(8,128)(2,1)S(1)} %collective-permute-done.22.refs_2_), channel_id=1, source_target_pairs={{0,1},{1,2},{2,3},{3,0},{4,5},{5,6},{6,7},{7,4},{8,9},{9,10},{10,1... | collective-permute-start | bytes 786440 | tf_op jit(solution)/shard_map/ppermute | solution.py:659
  129.0 13.9 %collective-permute-start.26 = (bf16[2,512,128]{2,1,0:T(8,128)(2,1)S(1)}, bf16[2,512,128]{2,1,0:T(8,128)(2,1)S(1)}, u32[]{:S(2)}, u32[]{:S(2)}) collective-permute-start(bf16[2,512,128]{2,1,0:T(8,128)(2,1)S(1)} %collective-permute-done.25.refs_6_), channel_id=1, source_target_pairs={{0,1},{1,2},{2,3},{3,0},{4,5},{5,6},{6,7},{7,4},{8,9},{9,10},{10,1... | collective-permute-start | bytes 786440 | tf_op jit(solution)/shard_map/ppermute | solution.py:659
  129.0 13.9 %collective-permute-start.31 = (bf16[2,512,256]{2,1,0:T(8,128)(2,1)S(1)}, bf16[2,512,256]{2,1,0:T(8,128)(2,1)S(1)}, u32[]{:S(2)}, u32[]{:S(2)}) collective-permute-start(bf16[2,512,256]{2,1,0:T(8,128)(2,1)S(1)} %collective-permute-done.14.refs_14_), channel_id=1, source_target_pairs={{0,4},{4,0},{8,12},{12,8},{16,20},{20,16},{24,28},{28,24},{1,5},{5... | collective-permute-start | bytes 1572872 | tf_op jit(solution)/shard_map/ppermute | solution.py:689
  129.1 13.8 %collective-permute-start.34 = (bf16[2,512,256]{2,1,0:T(8,128)(2,1)S(1)}, bf16[2,512,256]{2,1,0:T(8,128)(2,1)S(1)}, u32[]{:S(2)}, u32[]{:S(2)}) collective-permute-start(bf16[2,512,256]{2,1,0:T(8,128)(2,1)S(1)} %collective-permute-done.29.refs_17_), channel_id=1, source_target_pairs={{0,4},{4,0},{8,12},{12,8},{16,20},{20,16},{24,28},{28,24},{1,5},{5... | collective-permute-start | bytes 1572872 | tf_op jit(solution)/shard_map/ppermute | solution.py:689
  140.0 2.9 %collective-permute-start.33 = (bf16[2,512,256]{2,1,0:T(8,128)(2,1)S(1)}, bf16[2,512,256]{2,1,0:T(8,128)(2,1)S(1)}, u32[]{:S(2)}, u32[]{:S(2)}) collective-permute-start(bf16[2,512,256]{2,1,0:T(8,128)(2,1)S(1)} %collective-permute-done.28.refs_16_), channel_id=1, source_target_pairs={{0,4},{4,0},{8,12},{12,8},{16,20},{20,16},{24,28},{28,24},{1,5},{5... | collective-permute-start | bytes 1572872 | tf_op jit(solution)/shard_map/ppermute | solution.py:689
  142.9 1.9 collective-permute-start.32
  167.0 12.0 %collective-permute-start.35 = (bf16[128,512]{1,0:T(8,128)(2,1)S(1)}, bf16[128,512]{1,0:T(8,128)(2,1)S(1)}, u32[]{:S(2)}, u32[]{:S(2)}) collective-permute-start(bf16[128,512]{1,0:T(8,128)(2,1)S(1)} %get-tuple-element.114), channel_id=1, source_target_pairs={{0,1},{1,2},{2,3},{3,0},{4,5},{5,6},{6,7},{7,4},{8,9},{9,10},{10,1... | collective-permute-start | bytes 393224 | tf_op jit(solution)/shard_map/ppermute | solution.py:672
  167.1 12.9 %collective-permute-start.36 = (bf16[128,512]{1,0:T(8,128)(2,1)S(1)}, bf16[128,512]{1,0:T(8,128)(2,1)S(1)}, u32[]{:S(2)}, u32[]{:S(2)}) collective-permute-start(bf16[128,512]{1,0:T(8,128)(2,1)S(1)} %get-tuple-element.115), channel_id=1, source_target_pairs={{0,2},{1,3},{2,0},{3,1},{4,6},{5,7},{6,4},{7,5},{8,10},{9,11},{10,... | collective-permute-start | bytes 393224 | tf_op jit(solution)/shard_map/ppermute | solution.py:672
  167.2 12.9 %collective-permute-start.37 = (bf16[128,512]{1,0:T(8,128)(2,1)S(1)}, bf16[128,512]{1,0:T(8,128)(2,1)S(1)}, u32[]{:S(2)}, u32[]{:S(2)}) collective-permute-start(bf16[128,512]{1,0:T(8,128)(2,1)S(1)} %get-tuple-element.116), channel_id=1, source_target_pairs={{0,3},{1,0},{2,1},{3,2},{4,7},{5,4},{6,5},{7,6},{8,11},{9,8},{10,9... | collective-permute-start | bytes 393224 | tf_op jit(solution)/shard_map/ppermute | solution.py:672
  181.1 6.6 %collective-permute-start.41 = (bf16[128,512]{1,0:T(8,128)(2,1)S(1)}, bf16[128,512]{1,0:T(8,128)(2,1)S(1)}, u32[]{:S(2)}, u32[]{:S(2)}) collective-permute-start(bf16[128,512]{1,0:T(8,128)(2,1)S(1)} %multiply_convert_fusion.3.refs_0_), channel_id=1, source_target_pairs={{0,3},{1,0},{2,1},{3,2},{4,7},{5,4},{6,5},{7,6},{8,11},{9,8},{10,9... | collective-permute-start | bytes 393224 | tf_op jit(solution)/shard_map/ppermute | solution.py:672
  183.8 12.5 %collective-permute-start.40 = (bf16[128,512]{1,0:T(8,128)(2,1)S(1)}, bf16[128,512]{1,0:T(8,128)(2,1)S(1)}, u32[]{:S(2)}, u32[]{:S(2)}) collective-permute-start(bf16[128,512]{1,0:T(8,128)(2,1)S(1)} %multiply_convert_fusion.3.refs_0_), channel_id=1, source_target_pairs={{0,2},{1,3},{2,0},{3,1},{4,6},{5,7},{6,4},{7,5},{8,10},{9,11},{10,... | collective-permute-start | bytes 393224 | tf_op jit(solution)/shard_map/ppermute | solution.py:672
  185.2 11.1 %collective-permute-start.39 = (bf16[128,512]{1,0:T(8,128)(2,1)S(1)}, bf16[128,512]{1,0:T(8,128)(2,1)S(1)}, u32[]{:S(2)}, u32[]{:S(2)}) collective-permute-start(bf16[128,512]{1,0:T(8,128)(2,1)S(1)} %multiply_convert_fusion.3.refs_0_), channel_id=1, source_target_pairs={{0,1},{1,2},{2,3},{3,0},{4,5},{5,6},{6,7},{7,4},{8,9},{9,10},{10,1... | collective-permute-start | bytes 393224 | tf_op jit(solution)/shard_map/ppermute | solution.py:672
  198.6 2.4 collective-permute-start.42
  198.6 14.3 %collective-permute-start.38 = (bf16[512,512]{1,0:T(8,128)(2,1)S(1)}, bf16[512,512]{1,0:T(8,128)(2,1)S(1)}, u32[]{:S(2)}, u32[]{:S(2)}) collective-permute-start(bf16[512,512]{1,0:T(8,128)(2,1)S(1)} %get-tuple-element.121), channel_id=1, source_target_pairs={{0,1},{1,0},{2,3},{3,2},{4,5},{5,4},{6,7},{7,6},{8,9},{9,8},{10,11... | collective-permute-start | bytes 1572872 | tf_op jit(solution)/shard_map/ppermute | solution.py:762
  213.0 8.2 %collective-permute-start.44 = (bf16[208,512]{1,0:T(8,128)(2,1)S(1)}, bf16[208,512]{1,0:T(8,128)(2,1)S(1)}, u32[]{:S(2)}, u32[]{:S(2)}) collective-permute-start(bf16[208,512]{1,0:T(8,128)(2,1)S(1)} %get-tuple-element.128), channel_id=1, source_target_pairs={{0,8},{4,12},{8,0},{12,4},{16,24},{20,28},{24,16},{28,20},{1,9},{5... | collective-permute-start | bytes 638984 | tf_op jit(solution)/shard_map/ppermute | solution.py:681
  213.0 11.4 %collective-permute-start.45 = (bf16[208,512]{1,0:T(8,128)(2,1)S(1)}, bf16[208,512]{1,0:T(8,128)(2,1)S(1)}, u32[]{:S(2)}, u32[]{:S(2)}) collective-permute-start(bf16[208,512]{1,0:T(8,128)(2,1)S(1)} %get-tuple-element.129), channel_id=1, source_target_pairs={{0,16},{4,20},{8,24},{12,28},{16,0},{20,4},{24,8},{28,12},{1,17},{... | collective-permute-start | bytes 638984 | tf_op jit(solution)/shard_map/ppermute | solution.py:681
  214.1 10.2 %collective-permute-start.46 = (bf16[208,512]{1,0:T(8,128)(2,1)S(1)}, bf16[208,512]{1,0:T(8,128)(2,1)S(1)}, u32[]{:S(2)}, u32[]{:S(2)}) collective-permute-start(bf16[208,512]{1,0:T(8,128)(2,1)S(1)} %get-tuple-element.130), channel_id=1, source_target_pairs={{0,24},{4,28},{8,16},{12,20},{16,8},{20,12},{24,0},{28,4},{1,25},{... | collective-permute-start | bytes 638984 | tf_op jit(solution)/shard_map/ppermute | solution.py:681
  216.6 23.3 %collective-permute-start.43 = (bf16[512,512]{1,0:T(8,128)(2,1)S(1)}, bf16[512,512]{1,0:T(8,128)(2,1)S(1)}, u32[]{:S(2)}, u32[]{:S(2)}) collective-permute-start(bf16[512,512]{1,0:T(8,128)(2,1)S(1)} %get-tuple-element.127), channel_id=1, source_target_pairs={{0,1},{1,0},{2,3},{3,2},{4,5},{5,4},{6,7},{7,6},{8,9},{9,8},{10,11... | collective-permute-start | bytes 1572872 | tf_op jit(solution)/shard_map/ppermute | solution.py:762
  217.0 24.7 %collective-permute-start.48 = (bf16[512,512]{1,0:T(8,128)(2,1)S(1)}, bf16[512,512]{1,0:T(8,128)(2,1)S(1)}, u32[]{:S(2)}, u32[]{:S(2)}) collective-permute-start(bf16[512,512]{1,0:T(8,128)(2,1)S(1)} %add_convert_fusion.1), channel_id=1, source_target_pairs={{0,2},{1,3},{2,0},{3,1},{4,6},{5,7},{6,4},{7,5},{8,10},{9,11},{10,... | collective-permute-start | bytes 1572872 | tf_op jit(solution)/shard_map/ppermute | solution.py:762
  224.5 7.5 %collective-permute-start.50 = (bf16[208,512]{1,0:T(8,128)(2,1)S(1)}, bf16[208,512]{1,0:T(8,128)(2,1)S(1)}, u32[]{:S(2)}, u32[]{:S(2)}) collective-permute-start(bf16[208,512]{1,0:T(8,128)(2,1)S(1)} %add_convert_fusion.2.refs_0_), channel_id=1, source_target_pairs={{0,16},{4,20},{8,24},{12,28},{16,0},{20,4},{24,8},{28,12},{1,17},{... | collective-permute-start | bytes 638984 | tf_op jit(solution)/shard_map/ppermute | solution.py:681
  226.0 7.9 %collective-permute-start.49 = (bf16[208,512]{1,0:T(8,128)(2,1)S(1)}, bf16[208,512]{1,0:T(8,128)(2,1)S(1)}, u32[]{:S(2)}, u32[]{:S(2)}) collective-permute-start(bf16[208,512]{1,0:T(8,128)(2,1)S(1)} %add_convert_fusion.2.refs_0_), channel_id=1, source_target_pairs={{0,8},{4,12},{8,0},{12,4},{16,24},{20,28},{24,16},{28,20},{1,9},{5... | collective-permute-start | bytes 638984 | tf_op jit(solution)/shard_map/ppermute | solution.py:681
  226.7 9.4 %collective-permute-start.47 = (bf16[208,512]{1,0:T(8,128)(2,1)S(1)}, bf16[208,512]{1,0:T(8,128)(2,1)S(1)}, u32[]{:S(2)}, u32[]{:S(2)}) collective-permute-start(bf16[208,512]{1,0:T(8,128)(2,1)S(1)} %add_convert_fusion.2.refs_0_), channel_id=1, source_target_pairs={{0,24},{4,28},{8,16},{12,20},{16,8},{20,12},{24,0},{28,4},{1,25},{... | collective-permute-start | bytes 638984 | tf_op jit(solution)/shard_map/ppermute | solution.py:681
  232.0 10.7 %collective-permute-start.51 = (bf16[208,512]{1,0:T(8,128)(2,1)S(1)}, bf16[208,512]{1,0:T(8,128)(2,1)S(1)}, u32[]{:S(2)}, u32[]{:S(2)}) collective-permute-start(bf16[208,512]{1,0:T(8,128)(2,1)S(1)} %add_convert_fusion.2.refs_0_), channel_id=1, source_target_pairs={{0,4},{4,0},{8,12},{12,8},{16,20},{20,16},{24,28},{28,24},{1,5},{5... | collective-permute-start | bytes 638984 | tf_op jit(solution)/shard_map/ppermute | solution.py:689
  233.9 8.8 %collective-permute-start.53 = (bf16[208,512]{1,0:T(8,128)(2,1)S(1)}, bf16[208,512]{1,0:T(8,128)(2,1)S(1)}, u32[]{:S(2)}, u32[]{:S(2)}) collective-permute-start(bf16[208,512]{1,0:T(8,128)(2,1)S(1)} %collective-permute-done.50.refs_2_), channel_id=1, source_target_pairs={{0,4},{4,0},{8,12},{12,8},{16,20},{20,16},{24,28},{28,24},{1,5},{5... | collective-permute-start | bytes 638984 | tf_op jit(solution)/shard_map/ppermute | solution.py:689
  236.1 6.7 %collective-permute-start.52 = (bf16[208,512]{1,0:T(8,128)(2,1)S(1)}, bf16[208,512]{1,0:T(8,128)(2,1)S(1)}, u32[]{:S(2)}, u32[]{:S(2)}) collective-permute-start(bf16[208,512]{1,0:T(8,128)(2,1)S(1)} %collective-permute-done.49.refs_1_), channel_id=1, source_target_pairs={{0,4},{4,0},{8,12},{12,8},{16,20},{20,16},{24,28},{28,24},{1,5},{5... | collective-permute-start | bytes 638984 | tf_op jit(solution)/shard_map/ppermute | solution.py:689
  239.9 2.9 %collective-permute-start.54 = (bf16[208,512]{1,0:T(8,128)(2,1)S(1)}, bf16[208,512]{1,0:T(8,128)(2,1)S(1)}, u32[]{:S(2)}, u32[]{:S(2)}) collective-permute-start(bf16[208,512]{1,0:T(8,128)(2,1)S(1)} %collective-permute-done.47.refs_3_), channel_id=1, source_target_pairs={{0,4},{4,0},{8,12},{12,8},{16,20},{20,16},{24,28},{28,24},{1,5},{5... | collective-permute-start | bytes 638984 | tf_op jit(solution)/shard_map/ppermute | solution.py:689
  (6 other events, 26.8 us)

commit v6 on v5

--- a/solution.py
+++ b/solution.py
@@ -762,15 +762,17 @@
     over = lambda value, bit: lax.ppermute(value, "tensor", [(i, i ^ bit) for i in range(ring)])
     w_slice = lax.dynamic_slice(w_out, [zero, starts[1]], (w_out.shape[0], slice_cols))
     w_slice = after(w_slice, s_gate_out)
-    w_first = over(w_slice, 1)
-    w_rest = over(jnp.stack([w_slice, w_first]), 2)
+    w_first, w_second = over(w_slice, 1), over(w_slice, 2)
 
     own = flipped(made)
-    *own, w_first = lax.optimization_barrier((*own, w_first, *early))[: chips + 1]
+    own = lax.optimization_barrier((*own, *early))[:chips]
+    w_first, w_second = lax.optimization_barrier((w_first, w_second, *own))[:2]
+    w_third = over(w_second, 1)
     other = [swapped(a) for a in own]
     near_first = flipped([w_first] * chips)
     made = attention_call(below, info, own, other, ring)
-    *made, w_rest = lax.optimization_barrier((*made, w_rest, *near_first))[: chips + 1]
+    *made, w_third = lax.optimization_barrier((*made, w_third, *near_first))[: chips + 1]
+    w_rest = jnp.stack([w_second, w_third])
     attended = lax.optimization_barrier(tuple(flipped(made)))
     parts = [
         ring_gather(jnp.stack(attended[k : k + chips // 2]), "tensor") for k in (0, chips // 2)
@@ -804,7 +806,7 @@
     far_sum = over(after(far_theirs, own), 1)
 
     keep, give = grads_call(
-        info,
+        after(info, far_sum),
         scaled,
         student_normed,
         s_hidden,
@@ -814,7 +816,7 @@
         chips,
     )
     shares = pair_call(keep, swapped(give))
-    far_sum = (after(far_sum, shares[0]).astype(F32) + far_mine.astype(F32)).astype(BF16)
+    far_sum = (far_sum.astype(F32) + far_mine.astype(F32)).astype(BF16)
     shares = flipped(shares)
     own = sum(share.astype(F32) for share in shares).astype(BF16)
     mine = flipped([own] * chips)

time: 248 us -> 245 us (0.988)
  waiting for transfers between devices: 140 us -> 129 us
  starting transfers between devices: 38.4 us -> 44.6 us
    ppermute x18, waiting for transfers between devices: 31.3 us -> 22.2 us  [flipped(): lax.ppermute(pieces[f], 'dp', [(i, i ^ 2 * f) for i in range(size)])]
    ppermute x5 -> x6, waiting for transfers between devices: 27 us -> 33.7 us  [paired(): lax.ppermute(value, 'tensor', [(i, i ^ bit) for i in range(ring)])]
    ppermute x6, waiting for transfers between devices: 12.1 us -> 5.45 us  [shifted(): lax.ppermute(pieces[s], axis, [(i, (i + s) % size) for i in range(size)])]
    ppermute x5 -> x6, starting transfers between devices: 2.1 us -> 6.08 us  [paired(): lax.ppermute(value, 'tensor', [(i, i ^ bit) for i in range(ring)])]
    ppermute x12, starting transfers between devices: 5 us -> 7.65 us  [step_on(): return lax.ppermute(block, axis, [(i, (i + 1) % size) for i in range(size)])]
  transfers between devices with their start and end apart: 55 -> 56, of which waited for: 33 -> 29; matrix products, arithmetic and copies ran while one was open for 5% -> 6% of each run, Pallas kernels for 6% -> 7%
where the time goes in v6:
time: 245 us; the launch traced here: 244 us
  waiting for transfers between devices  129 us (53%)
  Pallas kernels  49.8 us (20%)
  starting transfers between devices  44.6 us (18%)
  matrix products  7.37 us (3%)
  other arithmetic  6.14 us (3%)
  local copies, waits for them, and re-layouts  4.46 us (2%)
  between operations  2.78 us (1%)
    ppermute x12, waiting for transfers between devices, step_on(): return lax.ppermute(block, axis, [(i, (i + 1) % size) for i in range(size)])  63.2 us
    ppermute x6, waiting for transfers between devices, paired(): lax.ppermute(value, 'tensor', [(i, i ^ bit) for i in range(ring)])  33.7 us
    ppermute x18, waiting for transfers between devices, flipped(): lax.ppermute(pieces[f], 'dp', [(i, i ^ 2 * f) for i in range(size)])  22.2 us
    pallas_call x1, Pallas kernels, middle_call(): pl.pallas_call(functools.partial(middle_kernel, ring=ring, chips=chips),...  22.2 us
    ppermute x18, starting transfers between devices, flipped(): lax.ppermute(pieces[f], 'dp', [(i, i ^ 2 * f) for i in range(size)])  21.8 us
    pallas_call x1, Pallas kernels, attention_call(): pl.pallas_call(functools.partial(attention_kernel, chips=chips, ring=ring...  9.95 us
    ppermute x12, starting transfers between devices, step_on(): return lax.ppermute(block, axis, [(i, (i + 1) % size) for i in range(size)])  7.65 us
    dot_general x4, matrix products, dot(): return jnp.dot(a, b, preferred_element_type=F32)  7.37 us
  transfers between devices with their start and end apart: 56, of which 29 were waited for; matrix products, arithmetic and copies ran while one was open for 6% of the time, Pallas kernels for 7%

profile of v6, /device:TPU:0, one launch (start us, length us, event | category | flops | bytes accessed | tf_op | source)
XLA Modules:
  0.0 244.2 jit_solution(9834809756707740568)
XLA Ops:
  0.7 1.1 fusion.10
  1.8 3.1 %collective-permute-start.3 = (bf16[256,512]{1,0:T(8,128)(2,1)S(1)}, bf16[256,512]{1,0:T(8,128)(2,1)S(1)}, u32[]{:S(2)}, u32[]{:S(2)}) collective-permute-start(bf16[256,512]{1,0:T(8,128)(2,1)S(1)} %get-tuple-element.142.refs_4_), channel_id=1, source_target_pairs={{0,1},{1,2},{2,3},{3,0},{4,5},{5,6},{6,7},{7,4},{8,9},{9,10},{10,1... | collective-permute-start | bytes 786440 | tf_op jit(solution)/shard_map/ppermute | solution.py:659
  4.9 1.6 collective-permute-start
  7.2 1.0 fusion.3
  8.6 5.5 %collective-permute-done.3.refs_5_ = bf16[256,512]{1,0:T(8,128)(2,1)S(1)} collective-permute-done((bf16[256,512]{1,0:T(8,128)(2,1)S(1)}, bf16[256,512]{1,0:T(8,128)(2,1)S(1)}, u32[]{:S(2)}, u32[]{:S(2)}) %collective-permute-start.3) | collective-permute-done | bytes 262176 | tf_op jit(solution)/shard_map/ppermute | solution.py:659
  14.1 5.6 %collective-permute-done.refs_1_ = bf16[256,512]{1,0:T(8,128)(2,1)S(1)} collective-permute-done((bf16[256,512]{1,0:T(8,128)(2,1)S(1)}, bf16[256,512]{1,0:T(8,128)(2,1)S(1)}, u32[]{:S(2)}, u32[]{:S(2)}) %collective-permute-start) | collective-permute-done | bytes 262176 | tf_op jit(solution)/shard_map/ppermute | solution.py:659
  19.7 1.1 constant_dynamic-slice_fusion
  20.9 1.1 convert_element_type.98
  22.0 3.3 %collective-permute-done.4.refs_6_ = bf16[256,512]{1,0:T(8,128)(2,1)S(1)} collective-permute-done((bf16[256,512]{1,0:T(8,128)(2,1)S(1)}, bf16[256,512]{1,0:T(8,128)(2,1)S(1)}, u32[]{:S(2)}, u32[]{:S(2)}) %collective-permute-start.4) | collective-permute-done | bytes 262176 | tf_op jit(solution)/shard_map/ppermute | solution.py:659
  25.3 5.6 %collective-permute-done.1.refs_2_ = bf16[256,512]{1,0:T(8,128)(2,1)S(1)} collective-permute-done((bf16[256,512]{1,0:T(8,128)(2,1)S(1)}, bf16[256,512]{1,0:T(8,128)(2,1)S(1)}, u32[]{:S(2)}, u32[]{:S(2)}) %collective-permute-start.1) | collective-permute-done | bytes 262176 | tf_op jit(solution)/shard_map/ppermute | solution.py:659
  31.1 5.4 %collective-permute-done.5.refs_7_ = bf16[256,512]{1,0:T(8,128)(2,1)S(1)} collective-permute-done((bf16[256,512]{1,0:T(8,128)(2,1)S(1)}, bf16[256,512]{1,0:T(8,128)(2,1)S(1)}, u32[]{:S(2)}, u32[]{:S(2)}) %collective-permute-start.5) | collective-permute-done | bytes 262176 | tf_op jit(solution)/shard_map/ppermute | solution.py:659
  36.5 4.8 %collective-permute-done.2.refs_3_ = bf16[256,512]{1,0:T(8,128)(2,1)S(1)} collective-permute-done((bf16[256,512]{1,0:T(8,128)(2,1)S(1)}, bf16[256,512]{1,0:T(8,128)(2,1)S(1)}, u32[]{:S(2)}, u32[]{:S(2)}) %collective-permute-start.2) | collective-permute-done | bytes 262176 | tf_op jit(solution)/shard_map/ppermute | solution.py:659
  41.4 6.3 %qkv.1 = (bf16[3,512,128]{2,1,0:T(8,128)(2,1)S(1)}, bf16[3,512,128]{2,1,0:T(8,128)(2,1)S(1)}, bf16[3,512,128]{2,1,0:T(8,128)(2,1)S(1)}, bf16[3,512,128]{2,1,0:T(8,128)(2,1)S(1)}, bf16[512,2048]{1,0:T(8,128)(2,1)S(1)}) custom-call(s32[16]{0:T(128)S(1)} %fusion.9.info_ref, bf16[256,512]{1,0:T(8,128)(2,1)S(1)} %get-tuple-element.143.refs_0_, ...), custom_call_target="tpu_custom_call" | custom-call | flops 3221225472 | bytes 6291456 | tf_op jit(solution)/shard_map/qkv/pallas_call | solution.py:231
  47.7 1.6 collective-permute-start.6
  49.3 1.5 collective-permute-start.7
  51.7 0.8 multiply_convert_fusion
  53.4 5.7 %fusion.refs_26_ = bf16[2048,512]{1,0:T(8,128)(2,1)} fusion(bf16[2048,2048]{1,0:T(8,128)(2,1)S(1)} %bitcast.32, bf16[2048,512]{1,0:T(8,128)(2,1)S(1)} %copy-done.12), kind=kOutput, calls=%fused_computation.1 | convolution fusion | flops 4296015872 | bytes 12582912 | tf_op jit(solution)/shard_map/dot_general | solution.py:166
  59.9 7.6 %collective-permute-done.7.refs_2_ = bf16[3,512,128]{2,1,0:T(8,128)(2,1)S(1)} collective-permute-done((bf16[3,512,128]{2,1,0:T(8,128)(2,1)S(1)}, bf16[3,512,128]{2,1,0:T(8,128)(2,1)S(1)}, u32[]{:S(2)}, u32[]{:S(2)}) %collective-permute-start.7) | collective-permute-done | bytes 393248 | tf_op jit(solution)/shard_map/ppermute | solution.py:681
  68.5 8.2 %collective-permute-done.13.refs_10_ = bf16[512,256]{1,0:T(8,128)(2,1)S(1)} collective-permute-done((bf16[512,256]{1,0:T(8,128)(2,1)S(1)}, bf16[512,256]{1,0:T(8,128)(2,1)S(1)}, u32[]{:S(2)}, u32[]{:S(2)}) %collective-permute-start.13) | collective-permute-done | bytes 262176 | tf_op jit(solution)/shard_map/ppermute | solution.py:762
  76.7 1.5 collective-permute-start.18
  78.2 1.2 collective-permute-start.17
  79.4 0.8 collective-permute-start.16
  80.7 10.0 %attention.1 = (bf16[512,128]{1,0:T(8,128)(2,1)S(1)}, bf16[512,128]{1,0:T(8,128)(2,1)S(1)}, bf16[512,128]{1,0:T(8,128)(2,1)S(1)}, bf16[512,128]{1,0:T(8,128)(2,1)S(1)}) custom-call(s32[8]{0:T(128)S(1)} %convert_reduce_fusion.first_ref, s32[16]{0:T(128)S(1)} %fusion.9.info_ref, bf16[3,512,128]{2,1,0:T(8,128)(2,1)S(1)} %get-tuple-element.82.refs_0_, ...), custom_call_target="tpu_custom_call" | custom-call | flops 2147483648 | bytes 4194304 | tf_op jit(solution)/shard_map/attention/pallas_call | solution.py:319
  90.7 1.3 collective-permute-start.19
  92.0 0.8 collective-permute-start.20
  92.8 1.4 collective-permute-start.21
  94.2 2.7 %collective-permute-done.19 = bf16[512,128]{1,0:T(8,128)(2,1)S(1)} collective-permute-done((bf16[512,128]{1,0:T(8,128)(2,1)S(1)}, bf16[512,128]{1,0:T(8,128)(2,1)S(1)}, u32[]{:S(2)}, u32[]{:S(2)}) %collective-permute-start.19) | collective-permute-done | bytes 131104 | tf_op jit(solution)/shard_map/ppermute | solution.py:681
  96.9 4.1 %collective-permute-done.20 = bf16[512,128]{1,0:T(8,128)(2,1)S(1)} collective-permute-done((bf16[512,128]{1,0:T(8,128)(2,1)S(1)}, bf16[512,128]{1,0:T(8,128)(2,1)S(1)}, u32[]{:S(2)}, u32[]{:S(2)}) %collective-permute-start.20) | collective-permute-done | bytes 131104 | tf_op jit(solution)/shard_map/ppermute | solution.py:681
  101.1 1.5 collective-permute-start.22
  102.6 0.8 collective-permute-start.25
  103.5 1.8 collective-permute-start.30
  105.3 6.9 %collective-permute-done.22.refs_1_ = bf16[2,512,128]{2,1,0:T(8,128)(2,1)S(1)} collective-permute-done((bf16[2,512,128]{2,1,0:T(8,128)(2,1)S(1)}, bf16[2,512,128]{2,1,0:T(8,128)(2,1)S(1)}, u32[]{:S(2)}, u32[]{:S(2)}) %collective-permute-start.22) | collective-permute-done | bytes 262176 | tf_op jit(solution)/shard_map/ppermute | solution.py:659
  112.9 1.5 collective-permute-start.28
  114.4 3.3 %collective-permute-done.25.refs_5_ = bf16[2,512,128]{2,1,0:T(8,128)(2,1)S(1)} collective-permute-done((bf16[2,512,128]{2,1,0:T(8,128)(2,1)S(1)}, bf16[2,512,128]{2,1,0:T(8,128)(2,1)S(1)}, u32[]{:S(2)}, u32[]{:S(2)}) %collective-permute-start.25) | collective-permute-done | bytes 262176 | tf_op jit(solution)/shard_map/ppermute | solution.py:659
  117.9 5.5 %collective-permute-done.23.refs_2_ = bf16[2,512,128]{2,1,0:T(8,128)(2,1)S(1)} collective-permute-done((bf16[2,512,128]{2,1,0:T(8,128)(2,1)S(1)}, bf16[2,512,128]{2,1,0:T(8,128)(2,1)S(1)}, u32[]{:S(2)}, u32[]{:S(2)}) %collective-permute-start.23) | collective-permute-done | bytes 262176 | tf_op jit(solution)/shard_map/ppermute | solution.py:659
  123.4 4.4 %collective-permute-done.26.refs_6_ = bf16[2,512,128]{2,1,0:T(8,128)(2,1)S(1)} collective-permute-done((bf16[2,512,128]{2,1,0:T(8,128)(2,1)S(1)}, bf16[2,512,128]{2,1,0:T(8,128)(2,1)S(1)}, u32[]{:S(2)}, u32[]{:S(2)}) %collective-permute-start.26) | collective-permute-done | bytes 262176 | tf_op jit(solution)/shard_map/ppermute | solution.py:659
  129.4 9.4 %collective-permute-done.24.refs_3_ = bf16[2,512,128]{2,1,0:T(8,128)(2,1)S(1)} collective-permute-done((bf16[2,512,128]{2,1,0:T(8,128)(2,1)S(1)}, bf16[2,512,128]{2,1,0:T(8,128)(2,1)S(1)}, u32[]{:S(2)}, u32[]{:S(2)}) %collective-permute-start.24) | collective-permute-done | bytes 262176 | tf_op jit(solution)/shard_map/ppermute | solution.py:659
  138.8 3.5 %collective-permute-done.27.refs_7_ = bf16[2,512,128]{2,1,0:T(8,128)(2,1)S(1)} collective-permute-done((bf16[2,512,128]{2,1,0:T(8,128)(2,1)S(1)}, bf16[2,512,128]{2,1,0:T(8,128)(2,1)S(1)}, u32[]{:S(2)}, u32[]{:S(2)}) %collective-permute-start.27) | collective-permute-done | bytes 262176 | tf_op jit(solution)/shard_map/ppermute | solution.py:659
  142.4 1.9 collective-permute-done.33.refs_20_
  144.3 22.2 %middle.1 = (bf16[512,2048]{1,0:T(8,128)(2,1)}, bf16[512,512]{1,0:T(8,128)(2,1)S(1)}, bf16[128,512]{1,0:T(8,128)(2,1)S(1)}, bf16[128,512]{1,0:T(8,128)(2,1)S(1)}...) custom-call(s32[16]{0:T(128)S(1)} %fusion.9.info_ref, bf16[2,512,128]{2,1,0:T(8,128)(2,1)S(1)} %pad_maximum_fusion.3.refs_0_, ...), custom_call_target="tpu_custom_call" | custom-call | flops 14227079168 | bytes 25165824 | tf_op jit(solution)/shard_map/middle/pallas_call | solution.py:463
  166.6 3.7 %collective-permute-start.38 = (bf16[128,512]{1,0:T(8,128)(2,1)S(1)}, bf16[128,512]{1,0:T(8,128)(2,1)S(1)}, u32[]{:S(2)}, u32[]{:S(2)}) collective-permute-start(bf16[128,512]{1,0:T(8,128)(2,1)S(1)} %get-tuple-element.118), channel_id=1, source_target_pairs={{0,3},{1,0},{2,1},{3,2},{4,7},{5,4},{6,5},{7,6},{8,11},{9,8},{10,9... | collective-permute-start | bytes 393224 | tf_op jit(solution)/shard_map/ppermute | solution.py:672
  170.4 1.6 copy-done.8
  171.9 6.5 %down.1 = (bf16[512,512]{1,0:T(8,128)(2,1)S(1)}, bf16[512,512]{1,0:T(8,128)(2,1)S(1)}, bf16[512,512]{1,0:T(8,128)(2,1)S(1)}, bf16[512,512]{1,0:T(8,128)(2,1)S(1)}) custom-call(s32[16]{0:T(128)S(1)} %fusion.9.info_ref, bf16[512,2048]{1,0:T(8,128)(2,1)S(1)} %copy-done.8, bf16[2048,2048]{1,0:T(8,128)(2,1)S(1)} %bitcast.32), custom_call_target="tpu_custom_call" | custom-call | flops 4294967296 | bytes 8388608 | tf_op jit(solution)/shard_map/down/pallas_call | solution.py:536
  178.5 1.0 collective-permute-done.37
  179.5 1.1 multiply_convert_fusion.3.refs_0_
  180.6 2.6 %collective-permute-start.39 = (bf16[512,512]{1,0:T(8,128)(2,1)S(1)}, bf16[512,512]{1,0:T(8,128)(2,1)S(1)}, u32[]{:S(2)}, u32[]{:S(2)}) collective-permute-start(bf16[512,512]{1,0:T(8,128)(2,1)S(1)} %get-tuple-element.123), channel_id=1, source_target_pairs={{0,1},{1,0},{2,3},{3,2},{4,5},{5,4},{6,7},{7,6},{8,9},{9,8},{10,11... | collective-permute-start | bytes 1572872 | tf_op jit(solution)/shard_map/ppermute | solution.py:762
  183.7 1.1 collective-permute-start.42
  184.7 1.1 collective-permute-start.41
  185.8 13.0 %collective-permute-done.39 = bf16[512,512]{1,0:T(8,128)(2,1)S(1)} collective-permute-done((bf16[512,512]{1,0:T(8,128)(2,1)S(1)}, bf16[512,512]{1,0:T(8,128)(2,1)S(1)}, u32[]{:S(2)}, u32[]{:S(2)}) %collective-permute-start.39) | collective-permute-done | bytes 524320 | tf_op jit(solution)/shard_map/ppermute | solution.py:762
  198.8 2.8 %collective-permute-done.43.refs_3_ = bf16[128,512]{1,0:T(8,128)(2,1)S(1)} collective-permute-done((bf16[128,512]{1,0:T(8,128)(2,1)S(1)}, bf16[128,512]{1,0:T(8,128)(2,1)S(1)}, u32[]{:S(2)}, u32[]{:S(2)}) %collective-permute-start.43) | collective-permute-done | bytes 131104 | tf_op jit(solution)/shard_map/ppermute | solution.py:672
  201.6 1.7 collective-permute-done.41.refs_1_
  203.3 2.2 grads.1
  205.6 2.4 collective-permute-done.44.theirs_ref
  208.1 1.3 collective-permute-start.45
  209.4 1.5 collective-permute-start.46
  211.8 1.1 collective-permute-start.49
  212.9 1.3 collective-permute-start.40
  214.2 2.1 collective-permute-done.45
  216.3 4.7 %collective-permute-done.46 = bf16[208,512]{1,0:T(8,128)(2,1)S(1)} collective-permute-done((bf16[208,512]{1,0:T(8,128)(2,1)S(1)}, bf16[208,512]{1,0:T(8,128)(2,1)S(1)}, u32[]{:S(2)}, u32[]{:S(2)}) %collective-permute-start.46) | collective-permute-done | bytes 213024 | tf_op jit(solution)/shard_map/ppermute | solution.py:681
  221.1 1.6 collective-permute-start.48
  222.7 1.2 collective-permute-start.51
  224.7 12.5 %collective-permute-done.49 = bf16[512,512]{1,0:T(8,128)(2,1)S(1)} collective-permute-done((bf16[512,512]{1,0:T(8,128)(2,1)S(1)}, bf16[512,512]{1,0:T(8,128)(2,1)S(1)}, u32[]{:S(2)}, u32[]{:S(2)}) %collective-permute-start.49) | collective-permute-done | bytes 524320 | tf_op jit(solution)/shard_map/ppermute | solution.py:762
  238.2 1.1 add_convert_fusion
  239.5 2.4 finish.1
  (111 shorter events, 12.5 us)
Async XLA Ops:
  0.6 51.1 %copy-start = (bf16[512,512]{1,0:T(8,128)(2,1)S(1)}, bf16[512,512]{1,0:T(8,128)(2,1)}, u32[]{:S(2)}) copy-start(bf16[512,512]{1,0:T(8,128)(2,1)} %param.31) | copy-start | bytes 1572868
  1.8 12.2 %collective-permute-start.3 = (bf16[256,512]{1,0:T(8,128)(2,1)S(1)}, bf16[256,512]{1,0:T(8,128)(2,1)S(1)}, u32[]{:S(2)}, u32[]{:S(2)}) collective-permute-start(bf16[256,512]{1,0:T(8,128)(2,1)S(1)} %get-tuple-element.142.refs_4_), channel_id=1, source_target_pairs={{0,1},{1,2},{2,3},{3,0},{4,5},{5,6},{6,7},{7,4},{8,9},{9,10},{10,1... | collective-permute-start | bytes 786440 | tf_op jit(solution)/shard_map/ppermute | solution.py:659
  4.9 14.8 %collective-permute-start = (bf16[256,512]{1,0:T(8,128)(2,1)S(1)}, bf16[256,512]{1,0:T(8,128)(2,1)S(1)}, u32[]{:S(2)}, u32[]{:S(2)}) collective-permute-start(bf16[256,512]{1,0:T(8,128)(2,1)S(1)} %get-tuple-element.143.refs_0_), channel_id=1, source_target_pairs={{0,1},{1,2},{2,3},{3,0},{4,5},{5,6},{6,7},{7,4},{8,9},{9,10},{10,1... | collective-permute-start | bytes 786440 | tf_op jit(solution)/shard_map/ppermute | solution.py:659
  8.2 33.2 %copy-start.4 = (bf16[2048,512]{1,0:T(8,128)(2,1)S(1)}, bf16[2048,512]{1,0:T(8,128)(2,1)}, u32[]{:S(2)}) copy-start(bf16[2048,512]{1,0:T(8,128)(2,1)} %refs_12_.1) | copy-start | bytes 6291460
  8.4 32.9 %copy-start.3 = (bf16[2048,512]{1,0:T(8,128)(2,1)S(1)}, bf16[2048,512]{1,0:T(8,128)(2,1)}, u32[]{:S(2)}) copy-start(bf16[2048,512]{1,0:T(8,128)(2,1)} %refs_11_.1) | copy-start | bytes 6291460
  8.4 32.9 %copy-start.5 = (f32[2048]{0:T(1024)S(1)}, f32[2048]{0:T(1024)}, u32[]{:S(2)}) copy-start(f32[2048]{0:T(1024)} %param.20) | copy-start | bytes 24580
  14.1 11.2 %collective-permute-start.4 = (bf16[256,512]{1,0:T(8,128)(2,1)S(1)}, bf16[256,512]{1,0:T(8,128)(2,1)S(1)}, u32[]{:S(2)}, u32[]{:S(2)}) collective-permute-start(bf16[256,512]{1,0:T(8,128)(2,1)S(1)} %collective-permute-done.3.refs_5_), channel_id=1, source_target_pairs={{0,1},{1,2},{2,3},{3,0},{4,5},{5,6},{6,7},{7,4},{8,9},{9,10},{10,1... | collective-permute-start | bytes 786440 | tf_op jit(solution)/shard_map/ppermute | solution.py:659
  19.7 11.2 %collective-permute-start.1 = (bf16[256,512]{1,0:T(8,128)(2,1)S(1)}, bf16[256,512]{1,0:T(8,128)(2,1)S(1)}, u32[]{:S(2)}, u32[]{:S(2)}) collective-permute-start(bf16[256,512]{1,0:T(8,128)(2,1)S(1)} %collective-permute-done.refs_1_), channel_id=1, source_target_pairs={{0,1},{1,2},{2,3},{3,0},{4,5},{5,6},{6,7},{7,4},{8,9},{9,10},{10,1... | collective-permute-start | bytes 786440 | tf_op jit(solution)/shard_map/ppermute | solution.py:659
  25.3 11.2 %collective-permute-start.5 = (bf16[256,512]{1,0:T(8,128)(2,1)S(1)}, bf16[256,512]{1,0:T(8,128)(2,1)S(1)}, u32[]{:S(2)}, u32[]{:S(2)}) collective-permute-start(bf16[256,512]{1,0:T(8,128)(2,1)S(1)} %collective-permute-done.4.refs_6_), channel_id=1, source_target_pairs={{0,1},{1,2},{2,3},{3,0},{4,5},{5,6},{6,7},{7,4},{8,9},{9,10},{10,1... | collective-permute-start | bytes 786440 | tf_op jit(solution)/shard_map/ppermute | solution.py:659
  30.9 10.4 %collective-permute-start.2 = (bf16[256,512]{1,0:T(8,128)(2,1)S(1)}, bf16[256,512]{1,0:T(8,128)(2,1)S(1)}, u32[]{:S(2)}, u32[]{:S(2)}) collective-permute-start(bf16[256,512]{1,0:T(8,128)(2,1)S(1)} %collective-permute-done.1.refs_2_), channel_id=1, source_target_pairs={{0,1},{1,2},{2,3},{3,0},{4,5},{5,6},{6,7},{7,4},{8,9},{9,10},{10,1... | collective-permute-start | bytes 786440 | tf_op jit(solution)/shard_map/ppermute | solution.py:659
  31.0 22.5 %slice-start = ((s8[8388608]{0:T(1024)(128)(4,1)}), s8[4194304]{0:T(1024)(128)(4,1)S(1)}, s32[]{:S(2)}) async-start(s8[8388608]{0:T(1024)(128)(4,1)} %bitcast.31), calls=%async_computation | async-start | bytes 8388608
  41.4 12.1 %slice-start.1 = ((s8[8388608]{0:T(1024)(128)(4,1)}), s8[4194304]{0:T(1024)(128)(4,1)S(1)}, s32[]{:S(2)}) async-start(s8[8388608]{0:T(1024)(128)(4,1)} %bitcast.31), calls=%async_computation.1 | async-start | bytes 8388608
  47.7 12.1 %collective-permute-start.6 = (bf16[3,512,128]{2,1,0:T(8,128)(2,1)S(1)}, bf16[3,512,128]{2,1,0:T(8,128)(2,1)S(1)}, u32[]{:S(2)}, u32[]{:S(2)}) collective-permute-start(bf16[3,512,128]{2,1,0:T(8,128)(2,1)S(1)} %get-tuple-element.75), channel_id=1, source_target_pairs={{0,8},{4,12},{8,0},{12,4},{16,24},{20,28},{24,16},{28,20},{1,9},{5... | collective-permute-start | bytes 1179656 | tf_op jit(solution)/shard_map/ppermute | solution.py:681
  49.3 18.2 %collective-permute-start.7 = (bf16[3,512,128]{2,1,0:T(8,128)(2,1)S(1)}, bf16[3,512,128]{2,1,0:T(8,128)(2,1)S(1)}, u32[]{:S(2)}, u32[]{:S(2)}) collective-permute-start(bf16[3,512,128]{2,1,0:T(8,128)(2,1)S(1)} %get-tuple-element.76), channel_id=1, source_target_pairs={{0,16},{4,20},{8,24},{12,28},{16,0},{20,4},{24,8},{28,12},{1,17},{... | collective-permute-start | bytes 1179656 | tf_op jit(solution)/shard_map/ppermute | solution.py:681
  50.8 16.7 %collective-permute-start.8 = (bf16[3,512,128]{2,1,0:T(8,128)(2,1)S(1)}, bf16[3,512,128]{2,1,0:T(8,128)(2,1)S(1)}, u32[]{:S(2)}, u32[]{:S(2)}) collective-permute-start(bf16[3,512,128]{2,1,0:T(8,128)(2,1)S(1)} %get-tuple-element.77), channel_id=1, source_target_pairs={{0,24},{4,28},{8,16},{12,20},{16,8},{20,12},{24,0},{28,4},{1,25},{... | collective-permute-start | bytes 1179656 | tf_op jit(solution)/shard_map/ppermute | solution.py:681
  52.6 15.9 %collective-permute-start.14 = (bf16[512,256]{1,0:T(8,128)(2,1)S(1)}, bf16[512,256]{1,0:T(8,128)(2,1)S(1)}, u32[]{:S(2)}, u32[]{:S(2)}) collective-permute-start(bf16[512,256]{1,0:T(8,128)(2,1)S(1)} %constant_dynamic-slice_fusion), channel_id=1, source_target_pairs={{0,2},{1,3},{2,0},{3,1},{4,6},{5,7},{6,4},{7,5},{8,10},{9,11},{10,... | collective-permute-start | bytes 786440 | tf_op jit(solution)/shard_map/ppermute | solution.py:762
  59.1 21.4 %copy-start.11 = (s32[4096]{0:T(1024)S(1)}, s32[4096]{0:T(1024)}, u32[]{:S(2)}) copy-start(s32[4096]{0:T(1024)} %param.18) | copy-start | bytes 49156
  67.5 10.7 %collective-permute-start.9 = (bf16[3,512,128]{2,1,0:T(8,128)(2,1)S(1)}, bf16[3,512,128]{2,1,0:T(8,128)(2,1)S(1)}, u32[]{:S(2)}, u32[]{:S(2)}) collective-permute-start(bf16[3,512,128]{2,1,0:T(8,128)(2,1)S(1)} %get-tuple-element.82.refs_0_), channel_id=1, source_target_pairs={{0,4},{4,0},{8,12},{12,8},{16,20},{20,16},{24,28},{28,24},{1,5},{5... | collective-permute-start | bytes 1179656 | tf_op jit(solution)/shard_map/ppermute | solution.py:689
  67.5 11.9 %collective-permute-start.10 = (bf16[3,512,128]{2,1,0:T(8,128)(2,1)S(1)}, bf16[3,512,128]{2,1,0:T(8,128)(2,1)S(1)}, u32[]{:S(2)}, u32[]{:S(2)}) collective-permute-start(bf16[3,512,128]{2,1,0:T(8,128)(2,1)S(1)} %collective-permute-done.6.refs_1_), channel_id=1, source_target_pairs={{0,4},{4,0},{8,12},{12,8},{16,20},{20,16},{24,28},{28,24},{1,5},{5... | collective-permute-start | bytes 1179656 | tf_op jit(solution)/shard_map/ppermute | solution.py:689
  68.0 12.2 %collective-permute-start.11 = (bf16[3,512,128]{2,1,0:T(8,128)(2,1)S(1)}, bf16[3,512,128]{2,1,0:T(8,128)(2,1)S(1)}, u32[]{:S(2)}, u32[]{:S(2)}) collective-permute-start(bf16[3,512,128]{2,1,0:T(8,128)(2,1)S(1)} %collective-permute-done.7.refs_2_), channel_id=1, source_target_pairs={{0,4},{4,0},{8,12},{12,8},{16,20},{20,16},{24,28},{28,24},{1,5},{5... | collective-permute-start | bytes 1179656 | tf_op jit(solution)/shard_map/ppermute | solution.py:689
  68.0 12.7 %collective-permute-start.12 = (bf16[3,512,128]{2,1,0:T(8,128)(2,1)S(1)}, bf16[3,512,128]{2,1,0:T(8,128)(2,1)S(1)}, u32[]{:S(2)}, u32[]{:S(2)}) collective-permute-start(bf16[3,512,128]{2,1,0:T(8,128)(2,1)S(1)} %collective-permute-done.8.refs_3_), channel_id=1, source_target_pairs={{0,4},{4,0},{8,12},{12,8},{16,20},{20,16},{24,28},{28,24},{1,5},{5... | collective-permute-start | bytes 1179656 | tf_op jit(solution)/shard_map/ppermute | solution.py:689
  68.5 8.2 %collective-permute-start.13 = (bf16[512,256]{1,0:T(8,128)(2,1)S(1)}, bf16[512,256]{1,0:T(8,128)(2,1)S(1)}, u32[]{:S(2)}, u32[]{:S(2)}) collective-permute-start(bf16[512,256]{1,0:T(8,128)(2,1)S(1)} %constant_dynamic-slice_fusion), channel_id=1, source_target_pairs={{0,1},{1,0},{2,3},{3,2},{4,5},{5,4},{6,7},{7,6},{8,9},{9,8},{10,11... | collective-permute-start | bytes 786440 | tf_op jit(solution)/shard_map/ppermute | solution.py:762
  76.7 13.9 %collective-permute-start.18 = (bf16[512,256]{1,0:T(8,128)(2,1)S(1)}, bf16[512,256]{1,0:T(8,128)(2,1)S(1)}, u32[]{:S(2)}, u32[]{:S(2)}) collective-permute-start(bf16[512,256]{1,0:T(8,128)(2,1)S(1)} %collective-permute-done.13.refs_10_), channel_id=1, source_target_pairs={{0,24},{4,28},{8,16},{12,20},{16,8},{20,12},{24,0},{28,4},{1,25},{... | collective-permute-start | bytes 786440 | tf_op jit(solution)/shard_map/ppermute | solution.py:681
  78.2 12.4 %collective-permute-start.17 = (bf16[512,256]{1,0:T(8,128)(2,1)S(1)}, bf16[512,256]{1,0:T(8,128)(2,1)S(1)}, u32[]{:S(2)}, u32[]{:S(2)}) collective-permute-start(bf16[512,256]{1,0:T(8,128)(2,1)S(1)} %collective-permute-done.13.refs_10_), channel_id=1, source_target_pairs={{0,16},{4,20},{8,24},{12,28},{16,0},{20,4},{24,8},{28,12},{1,17},{... | collective-permute-start | bytes 786440 | tf_op jit(solution)/shard_map/ppermute | solution.py:681
  79.4 11.3 %collective-permute-start.16 = (bf16[512,256]{1,0:T(8,128)(2,1)S(1)}, bf16[512,256]{1,0:T(8,128)(2,1)S(1)}, u32[]{:S(2)}, u32[]{:S(2)}) collective-permute-start(bf16[512,256]{1,0:T(8,128)(2,1)S(1)} %collective-permute-done.13.refs_10_), channel_id=1, source_target_pairs={{0,8},{4,12},{8,0},{12,4},{16,24},{20,28},{24,16},{28,20},{1,9},{5... | collective-permute-start | bytes 786440 | tf_op jit(solution)/shard_map/ppermute | solution.py:681
  80.2 10.4 %collective-permute-start.15 = (bf16[512,256]{1,0:T(8,128)(2,1)S(1)}, bf16[512,256]{1,0:T(8,128)(2,1)S(1)}, u32[]{:S(2)}, u32[]{:S(2)}) collective-permute-start(bf16[512,256]{1,0:T(8,128)(2,1)S(1)} %collective-permute-done.14), channel_id=1, source_target_pairs={{0,1},{1,0},{2,3},{3,2},{4,5},{5,4},{6,7},{7,6},{8,9},{9,8},{10,11... | collective-permute-start | bytes 786440 | tf_op jit(solution)/shard_map/ppermute | solution.py:762
  90.7 6.2 %collective-permute-start.19 = (bf16[512,128]{1,0:T(8,128)(2,1)S(1)}, bf16[512,128]{1,0:T(8,128)(2,1)S(1)}, u32[]{:S(2)}, u32[]{:S(2)}) collective-permute-start(bf16[512,128]{1,0:T(8,128)(2,1)S(1)} %get-tuple-element.95), channel_id=1, source_target_pairs={{0,8},{4,12},{8,0},{12,4},{16,24},{20,28},{24,16},{28,20},{1,9},{5... | collective-permute-start | bytes 393224 | tf_op jit(solution)/shard_map/ppermute | solution.py:681
  92.0 9.1 %collective-permute-start.20 = (bf16[512,128]{1,0:T(8,128)(2,1)S(1)}, bf16[512,128]{1,0:T(8,128)(2,1)S(1)}, u32[]{:S(2)}, u32[]{:S(2)}) collective-permute-start(bf16[512,128]{1,0:T(8,128)(2,1)S(1)} %get-tuple-element.96), channel_id=1, source_target_pairs={{0,16},{4,20},{8,24},{12,28},{16,0},{20,4},{24,8},{28,12},{1,17},{... | collective-permute-start | bytes 393224 | tf_op jit(solution)/shard_map/ppermute | solution.py:681
  92.8 8.3 %collective-permute-start.21 = (bf16[512,128]{1,0:T(8,128)(2,1)S(1)}, bf16[512,128]{1,0:T(8,128)(2,1)S(1)}, u32[]{:S(2)}, u32[]{:S(2)}) collective-permute-start(bf16[512,128]{1,0:T(8,128)(2,1)S(1)} %get-tuple-element.97), channel_id=1, source_target_pairs={{0,24},{4,28},{8,16},{12,20},{16,8},{20,12},{24,0},{28,4},{1,25},{... | collective-permute-start | bytes 393224 | tf_op jit(solution)/shard_map/ppermute | solution.py:681
  101.1 43.2 %copy-start.6 = (f32[2048]{0:T(1024)S(1)}, f32[2048]{0:T(1024)}, u32[]{:S(2)}) copy-start(f32[2048]{0:T(1024)} %param.21) | copy-start | bytes 24580
  101.1 11.1 %collective-permute-start.22 = (bf16[2,512,128]{2,1,0:T(8,128)(2,1)S(1)}, bf16[2,512,128]{2,1,0:T(8,128)(2,1)S(1)}, u32[]{:S(2)}, u32[]{:S(2)}) collective-permute-start(bf16[2,512,128]{2,1,0:T(8,128)(2,1)S(1)} %pad_maximum_fusion.3.refs_0_), channel_id=1, source_target_pairs={{0,1},{1,2},{2,3},{3,0},{4,5},{5,6},{6,7},{7,4},{8,9},{9,10},{10,1... | collective-permute-start | bytes 786440 | tf_op jit(solution)/shard_map/ppermute | solution.py:659
  102.6 15.2 %collective-permute-start.25 = (bf16[2,512,128]{2,1,0:T(8,128)(2,1)S(1)}, bf16[2,512,128]{2,1,0:T(8,128)(2,1)S(1)}, u32[]{:S(2)}, u32[]{:S(2)}) collective-permute-start(bf16[2,512,128]{2,1,0:T(8,128)(2,1)S(1)} %pad_maximum_fusion.4.refs_4_), channel_id=1, source_target_pairs={{0,1},{1,2},{2,3},{3,0},{4,5},{5,6},{6,7},{7,4},{8,9},{9,10},{10,1... | collective-permute-start | bytes 786440 | tf_op jit(solution)/shard_map/ppermute | solution.py:659
  103.5 24.3 %collective-permute-start.30 = (bf16[2,512,256]{2,1,0:T(8,128)(2,1)S(1)}, bf16[2,512,256]{2,1,0:T(8,128)(2,1)S(1)}, u32[]{:S(2)}, u32[]{:S(2)}) collective-permute-start(bf16[2,512,256]{2,1,0:T(8,128)(2,1)S(1)} %pad_maximum_fusion.refs_14_), channel_id=1, source_target_pairs={{0,24},{4,28},{8,16},{12,20},{16,8},{20,12},{24,0},{28,4},{1,25},{... | collective-permute-start | bytes 1572872 | tf_op jit(solution)/shard_map/ppermute | solution.py:681
  112.1 11.2 %collective-permute-start.23 = (bf16[2,512,128]{2,1,0:T(8,128)(2,1)S(1)}, bf16[2,512,128]{2,1,0:T(8,128)(2,1)S(1)}, u32[]{:S(2)}, u32[]{:S(2)}) collective-permute-start(bf16[2,512,128]{2,1,0:T(8,128)(2,1)S(1)} %collective-permute-done.22.refs_1_), channel_id=1, source_target_pairs={{0,1},{1,2},{2,3},{3,0},{4,5},{5,6},{6,7},{7,4},{8,9},{9,10},{10,1... | collective-permute-start | bytes 786440 | tf_op jit(solution)/shard_map/ppermute | solution.py:659
  112.1 16.8 %collective-permute-start.29 = (bf16[2,512,256]{2,1,0:T(8,128)(2,1)S(1)}, bf16[2,512,256]{2,1,0:T(8,128)(2,1)S(1)}, u32[]{:S(2)}, u32[]{:S(2)}) collective-permute-start(bf16[2,512,256]{2,1,0:T(8,128)(2,1)S(1)} %pad_maximum_fusion.refs_14_), channel_id=1, source_target_pairs={{0,16},{4,20},{8,24},{12,28},{16,0},{20,4},{24,8},{28,12},{1,17},{... | collective-permute-start | bytes 1572872 | tf_op jit(solution)/shard_map/ppermute | solution.py:681
  112.9 16.0 %collective-permute-start.28 = (bf16[2,512,256]{2,1,0:T(8,128)(2,1)S(1)}, bf16[2,512,256]{2,1,0:T(8,128)(2,1)S(1)}, u32[]{:S(2)}, u32[]{:S(2)}) collective-permute-start(bf16[2,512,256]{2,1,0:T(8,128)(2,1)S(1)} %pad_maximum_fusion.refs_14_), channel_id=1, source_target_pairs={{0,8},{4,12},{8,0},{12,4},{16,24},{20,28},{24,16},{28,20},{1,9},{5... | collective-permute-start | bytes 1572872 | tf_op jit(solution)/shard_map/ppermute | solution.py:681
  117.8 10.0 %collective-permute-start.26 = (bf16[2,512,128]{2,1,0:T(8,128)(2,1)S(1)}, bf16[2,512,128]{2,1,0:T(8,128)(2,1)S(1)}, u32[]{:S(2)}, u32[]{:S(2)}) collective-permute-start(bf16[2,512,128]{2,1,0:T(8,128)(2,1)S(1)} %collective-permute-done.25.refs_5_), channel_id=1, source_target_pairs={{0,1},{1,2},{2,3},{3,0},{4,5},{5,6},{6,7},{7,4},{8,9},{9,10},{10,1... | collective-permute-start | bytes 786440 | tf_op jit(solution)/shard_map/ppermute | solution.py:659
  123.4 20.9 %collective-permute-start.31 = (bf16[4,1,512,256]{3,2,0,1:T(8,128)(2,1)S(1)}, bf16[4,1,512,256]{3,2,0,1:T(8,128)(2,1)S(1)}, u32[]{:S(2)}, u32[]{:S(2)}) collective-permute-start(bf16[4,1,512,256]{3,2,0,1:T(8,128)(2,1)S(1)} %maximum_bitcast_fusion), channel_id=1, source_target_pairs={{0,4},{4,0},{8,12},{12,8},{16,20},{20,16},{24,28},{28,24},{1,5},{5... | collective-permute-start | bytes 3145736 | tf_op jit(solution)/shard_map/ppermute | solution.py:689
  127.8 11.0 %collective-permute-start.24 = (bf16[2,512,128]{2,1,0:T(8,128)(2,1)S(1)}, bf16[2,512,128]{2,1,0:T(8,128)(2,1)S(1)}, u32[]{:S(2)}, u32[]{:S(2)}) collective-permute-start(bf16[2,512,128]{2,1,0:T(8,128)(2,1)S(1)} %collective-permute-done.23.refs_2_), channel_id=1, source_target_pairs={{0,1},{1,2},{2,3},{3,0},{4,5},{5,6},{6,7},{7,4},{8,9},{9,10},{10,1... | collective-permute-start | bytes 786440 | tf_op jit(solution)/shard_map/ppermute | solution.py:659
  127.8 14.5 %collective-permute-start.27 = (bf16[2,512,128]{2,1,0:T(8,128)(2,1)S(1)}, bf16[2,512,128]{2,1,0:T(8,128)(2,1)S(1)}, u32[]{:S(2)}, u32[]{:S(2)}) collective-permute-start(bf16[2,512,128]{2,1,0:T(8,128)(2,1)S(1)} %collective-permute-done.26.refs_6_), channel_id=1, source_target_pairs={{0,1},{1,2},{2,3},{3,0},{4,5},{5,6},{6,7},{7,4},{8,9},{9,10},{10,1... | collective-permute-start | bytes 786440 | tf_op jit(solution)/shard_map/ppermute | solution.py:659
  128.9 13.5 %collective-permute-start.32 = (bf16[2,512,256]{2,1,0:T(8,128)(2,1)S(1)}, bf16[2,512,256]{2,1,0:T(8,128)(2,1)S(1)}, u32[]{:S(2)}, u32[]{:S(2)}) collective-permute-start(bf16[2,512,256]{2,1,0:T(8,128)(2,1)S(1)} %pad_maximum_fusion.refs_14_), channel_id=1, source_target_pairs={{0,4},{4,0},{8,12},{12,8},{16,20},{20,16},{24,28},{28,24},{1,5},{5... | collective-permute-start | bytes 1572872 | tf_op jit(solution)/shard_map/ppermute | solution.py:689
  128.9 13.4 %collective-permute-start.35 = (bf16[2,512,256]{2,1,0:T(8,128)(2,1)S(1)}, bf16[2,512,256]{2,1,0:T(8,128)(2,1)S(1)}, u32[]{:S(2)}, u32[]{:S(2)}) collective-permute-start(bf16[2,512,256]{2,1,0:T(8,128)(2,1)S(1)} %collective-permute-done.30.refs_17_), channel_id=1, source_target_pairs={{0,4},{4,0},{8,12},{12,8},{16,20},{20,16},{24,28},{28,24},{1,5},{5... | collective-permute-start | bytes 1572872 | tf_op jit(solution)/shard_map/ppermute | solution.py:689
  138.8 3.5 %collective-permute-start.34 = (bf16[2,512,256]{2,1,0:T(8,128)(2,1)S(1)}, bf16[2,512,256]{2,1,0:T(8,128)(2,1)S(1)}, u32[]{:S(2)}, u32[]{:S(2)}) collective-permute-start(bf16[2,512,256]{2,1,0:T(8,128)(2,1)S(1)} %collective-permute-done.29.refs_16_), channel_id=1, source_target_pairs={{0,4},{4,0},{8,12},{12,8},{16,20},{20,16},{24,28},{28,24},{1,5},{5... | collective-permute-start | bytes 1572872 | tf_op jit(solution)/shard_map/ppermute | solution.py:689
  142.4 1.9 collective-permute-start.33
  166.5 12.0 %collective-permute-start.36 = (bf16[128,512]{1,0:T(8,128)(2,1)S(1)}, bf16[128,512]{1,0:T(8,128)(2,1)S(1)}, u32[]{:S(2)}, u32[]{:S(2)}) collective-permute-start(bf16[128,512]{1,0:T(8,128)(2,1)S(1)} %get-tuple-element.116), channel_id=1, source_target_pairs={{0,1},{1,2},{2,3},{3,0},{4,5},{5,6},{6,7},{7,4},{8,9},{9,10},{10,1... | collective-permute-start | bytes 393224 | tf_op jit(solution)/shard_map/ppermute | solution.py:672
  166.5 13.0 %collective-permute-start.37 = (bf16[128,512]{1,0:T(8,128)(2,1)S(1)}, bf16[128,512]{1,0:T(8,128)(2,1)S(1)}, u32[]{:S(2)}, u32[]{:S(2)}) collective-permute-start(bf16[128,512]{1,0:T(8,128)(2,1)S(1)} %get-tuple-element.117), channel_id=1, source_target_pairs={{0,2},{1,3},{2,0},{3,1},{4,6},{5,7},{6,4},{7,5},{8,10},{9,11},{10,... | collective-permute-start | bytes 393224 | tf_op jit(solution)/shard_map/ppermute | solution.py:672
  166.6 12.9 %collective-permute-start.38 = (bf16[128,512]{1,0:T(8,128)(2,1)S(1)}, bf16[128,512]{1,0:T(8,128)(2,1)S(1)}, u32[]{:S(2)}, u32[]{:S(2)}) collective-permute-start(bf16[128,512]{1,0:T(8,128)(2,1)S(1)} %get-tuple-element.118), channel_id=1, source_target_pairs={{0,3},{1,0},{2,1},{3,2},{4,7},{5,4},{6,5},{7,6},{8,11},{9,8},{10,9... | collective-permute-start | bytes 393224 | tf_op jit(solution)/shard_map/ppermute | solution.py:672
  180.6 18.3 %collective-permute-start.39 = (bf16[512,512]{1,0:T(8,128)(2,1)S(1)}, bf16[512,512]{1,0:T(8,128)(2,1)S(1)}, u32[]{:S(2)}, u32[]{:S(2)}) collective-permute-start(bf16[512,512]{1,0:T(8,128)(2,1)S(1)} %get-tuple-element.123), channel_id=1, source_target_pairs={{0,1},{1,0},{2,3},{3,2},{4,5},{5,4},{6,7},{7,6},{8,9},{9,8},{10,11... | collective-permute-start | bytes 1572872 | tf_op jit(solution)/shard_map/ppermute | solution.py:762
  183.2 18.4 %collective-permute-start.43 = (bf16[128,512]{1,0:T(8,128)(2,1)S(1)}, bf16[128,512]{1,0:T(8,128)(2,1)S(1)}, u32[]{:S(2)}, u32[]{:S(2)}) collective-permute-start(bf16[128,512]{1,0:T(8,128)(2,1)S(1)} %multiply_convert_fusion.3.refs_0_), channel_id=1, source_target_pairs={{0,3},{1,0},{2,1},{3,2},{4,7},{5,4},{6,5},{7,6},{8,11},{9,8},{10,9... | collective-permute-start | bytes 393224 | tf_op jit(solution)/shard_map/ppermute | solution.py:672
  183.7 18.0 %collective-permute-start.42 = (bf16[128,512]{1,0:T(8,128)(2,1)S(1)}, bf16[128,512]{1,0:T(8,128)(2,1)S(1)}, u32[]{:S(2)}, u32[]{:S(2)}) collective-permute-start(bf16[128,512]{1,0:T(8,128)(2,1)S(1)} %multiply_convert_fusion.3.refs_0_), channel_id=1, source_target_pairs={{0,2},{1,3},{2,0},{3,1},{4,6},{5,7},{6,4},{7,5},{8,10},{9,11},{10,... | collective-permute-start | bytes 393224 | tf_op jit(solution)/shard_map/ppermute | solution.py:672
  184.7 18.5 %collective-permute-start.41 = (bf16[128,512]{1,0:T(8,128)(2,1)S(1)}, bf16[128,512]{1,0:T(8,128)(2,1)S(1)}, u32[]{:S(2)}, u32[]{:S(2)}) collective-permute-start(bf16[128,512]{1,0:T(8,128)(2,1)S(1)} %multiply_convert_fusion.3.refs_0_), channel_id=1, source_target_pairs={{0,1},{1,2},{2,3},{3,0},{4,5},{5,6},{6,7},{7,4},{8,9},{9,10},{10,1... | collective-permute-start | bytes 393224 | tf_op jit(solution)/shard_map/ppermute | solution.py:672
  205.5 2.4 %collective-permute-start.44 = (bf16[4,208,512]{2,1,0:T(8,128)(2,1)S(1)}, bf16[4,208,512]{2,1,0:T(8,128)(2,1)S(1)}, u32[]{:S(2)}, u32[]{:S(2)}) collective-permute-start(bf16[4,208,512]{2,1,0:T(8,128)(2,1)S(1)} %get-tuple-element.128), channel_id=1, source_target_pairs={{0,4},{4,0},{8,12},{12,8},{16,20},{20,16},{24,28},{28,24},{1,5},{5... | collective-permute-start | bytes 2555912 | tf_op jit(solution)/shard_map/ppermute | solution.py:689
  208.1 8.2 %collective-permute-start.45 = (bf16[208,512]{1,0:T(8,128)(2,1)S(1)}, bf16[208,512]{1,0:T(8,128)(2,1)S(1)}, u32[]{:S(2)}, u32[]{:S(2)}) collective-permute-start(bf16[208,512]{1,0:T(8,128)(2,1)S(1)} %get-tuple-element.130), channel_id=1, source_target_pairs={{0,8},{4,12},{8,0},{12,4},{16,24},{20,28},{24,16},{28,20},{1,9},{5... | collective-permute-start | bytes 638984 | tf_op jit(solution)/shard_map/ppermute | solution.py:681
  209.4 11.6 %collective-permute-start.46 = (bf16[208,512]{1,0:T(8,128)(2,1)S(1)}, bf16[208,512]{1,0:T(8,128)(2,1)S(1)}, u32[]{:S(2)}, u32[]{:S(2)}) collective-permute-start(bf16[208,512]{1,0:T(8,128)(2,1)S(1)} %get-tuple-element.131), channel_id=1, source_target_pairs={{0,16},{4,20},{8,24},{12,28},{16,0},{20,4},{24,8},{28,12},{1,17},{... | collective-permute-start | bytes 638984 | tf_op jit(solution)/shard_map/ppermute | solution.py:681
  211.0 10.0 %collective-permute-start.47 = (bf16[208,512]{1,0:T(8,128)(2,1)S(1)}, bf16[208,512]{1,0:T(8,128)(2,1)S(1)}, u32[]{:S(2)}, u32[]{:S(2)}) collective-permute-start(bf16[208,512]{1,0:T(8,128)(2,1)S(1)} %get-tuple-element.132), channel_id=1, source_target_pairs={{0,24},{4,28},{8,16},{12,20},{16,8},{20,12},{24,0},{28,4},{1,25},{... | collective-permute-start | bytes 638984 | tf_op jit(solution)/shard_map/ppermute | solution.py:681
  211.8 25.3 %collective-permute-start.49 = (bf16[512,512]{1,0:T(8,128)(2,1)S(1)}, bf16[512,512]{1,0:T(8,128)(2,1)S(1)}, u32[]{:S(2)}, u32[]{:S(2)}) collective-permute-start(bf16[512,512]{1,0:T(8,128)(2,1)S(1)} %add_convert_fusion.1), channel_id=1, source_target_pairs={{0,2},{1,3},{2,0},{3,1},{4,6},{5,7},{6,4},{7,5},{8,10},{9,11},{10,... | collective-permute-start | bytes 1572872 | tf_op jit(solution)/shard_map/ppermute | solution.py:762
  212.9 24.3 %collective-permute-start.40 = (bf16[512,512]{1,0:T(8,128)(2,1)S(1)}, bf16[512,512]{1,0:T(8,128)(2,1)S(1)}, u32[]{:S(2)}, u32[]{:S(2)}) collective-permute-start(bf16[512,512]{1,0:T(8,128)(2,1)S(1)} %get-tuple-element.125), channel_id=1, source_target_pairs={{0,1},{1,0},{2,3},{3,2},{4,5},{5,4},{6,7},{7,6},{8,9},{9,8},{10,11... | collective-permute-start | bytes 1572872 | tf_op jit(solution)/shard_map/ppermute | solution.py:762
  221.1 16.0 %collective-permute-start.48 = (bf16[208,512]{1,0:T(8,128)(2,1)S(1)}, bf16[208,512]{1,0:T(8,128)(2,1)S(1)}, u32[]{:S(2)}, u32[]{:S(2)}) collective-permute-start(bf16[208,512]{1,0:T(8,128)(2,1)S(1)} %add_convert_fusion.2.refs_0_), channel_id=1, source_target_pairs={{0,24},{4,28},{8,16},{12,20},{16,8},{20,12},{24,0},{28,4},{1,25},{... | collective-permute-start | bytes 638984 | tf_op jit(solution)/shard_map/ppermute | solution.py:681
  222.7 15.0 %collective-permute-start.51 = (bf16[208,512]{1,0:T(8,128)(2,1)S(1)}, bf16[208,512]{1,0:T(8,128)(2,1)S(1)}, u32[]{:S(2)}, u32[]{:S(2)}) collective-permute-start(bf16[208,512]{1,0:T(8,128)(2,1)S(1)} %add_convert_fusion.2.refs_0_), channel_id=1, source_target_pairs={{0,16},{4,20},{8,24},{12,28},{16,0},{20,4},{24,8},{28,12},{1,17},{... | collective-permute-start | bytes 638984 | tf_op jit(solution)/shard_map/ppermute | solution.py:681
  223.9 13.8 %collective-permute-start.50 = (bf16[208,512]{1,0:T(8,128)(2,1)S(1)}, bf16[208,512]{1,0:T(8,128)(2,1)S(1)}, u32[]{:S(2)}, u32[]{:S(2)}) collective-permute-start(bf16[208,512]{1,0:T(8,128)(2,1)S(1)} %add_convert_fusion.2.refs_0_), channel_id=1, source_target_pairs={{0,8},{4,12},{8,0},{12,4},{16,24},{20,28},{24,16},{28,20},{1,9},{5... | collective-permute-start | bytes 638984 | tf_op jit(solution)/shard_map/ppermute | solution.py:681
  237.1 2.1 collective-permute-start.52
  237.2 2.4 collective-permute-start.55
  237.7 1.6 collective-permute-start.54
  237.7 1.8 collective-permute-start.53
  (7 other events, 37.2 us)

commit v7 on v6

--- a/solution.py
+++ b/solution.py
@@ -300,6 +300,21 @@
             accum = accum * keep + dot(values_all[at], weights.astype(BF16))
             return new_peak, denom, accum
 
+        def pair(turn, carry, query=query, full=None):
+            peak, denom, accum = carry
+            at = full + 2 * turn
+            blocks = (at, at + 1)
+            scores = [dot_over(keys_all[block], query, (1, 1)) for block in blocks]
+            tops = [jnp.max(score, axis=0, keepdims=True) for score in scores]
+            new_peak = jnp.maximum(peak, jnp.maximum(*tops))
+            keep = jnp.exp2(peak - new_peak)
+            denom, accum = denom * keep, accum * keep
+            for block, score in zip(blocks, scores):
+                weights = jnp.exp2(score - new_peak)
+                denom += jnp.sum(weights, axis=0, keepdims=True)
+                accum += dot(values_all[block], weights.astype(BF16))
+            return new_peak, denom, accum
+
         begin = first_of(last * span) // span
         full = jnp.minimum(last, (first_of(last * span + span - 1) + span - 1) // span)
         carry = (
@@ -308,7 +323,10 @@
             jnp.zeros((HD, span), F32),
         )
         carry = lax.fori_loop(begin, full, functools.partial(body, masked=True), carry)
-        carry = lax.fori_loop(full, last, functools.partial(body, masked=False), carry)
+        turns = (last - full) // 2
+        carry = lax.fori_loop(0, turns, functools.partial(pair, full=full), carry)
+        rest = full + 2 * turns
+        carry = lax.fori_loop(rest, last, functools.partial(body, masked=False), carry)
         _, denom, accum = body(last, carry, masked=True)
         outs[f][...] = (accum / denom).T.astype(BF16)
 
@@ -761,12 +779,12 @@
 
     over = lambda value, bit: lax.ppermute(value, "tensor", [(i, i ^ bit) for i in range(ring)])
     w_slice = lax.dynamic_slice(w_out, [zero, starts[1]], (w_out.shape[0], slice_cols))
-    w_slice = after(w_slice, s_gate_out)
+    w_slice, tok_full = lax.optimization_barrier((w_slice, tok_full))
     w_first, w_second = over(w_slice, 1), over(w_slice, 2)
 
     own = flipped(made)
-    own = lax.optimization_barrier((*own, *early))[:chips]
-    w_first, w_second = lax.optimization_barrier((w_first, w_second, *own))[:2]
+    held = lax.optimization_barrier((*own, w_first, w_second, *early))
+    own, (w_first, w_second) = held[:chips], held[chips : chips + 2]
     w_third = over(w_second, 1)
     other = [swapped(a) for a in own]
     near_first = flipped([w_first] * chips)

time: 245 us -> 238 us (0.971)
  waiting for transfers between devices: 129 us -> 121 us
    ppermute x6, waiting for transfers between devices: 33.7 us -> 26.3 us  [paired(): lax.ppermute(value, 'tensor', [(i, i ^ bit) for i in range(ring)])]
  transfers between devices with their start and end apart: 56 -> 56, of which waited for: 29 -> 30; matrix products, arithmetic and copies ran while one was open for 6% -> 6% of each run, Pallas kernels for 7% -> 6%
where the time goes in v7:
time: 238 us; the launch traced here: 236 us
  waiting for transfers between devices  121 us (51%)
  Pallas kernels  48.6 us (20%)
  starting transfers between devices  45.1 us (19%)
  matrix products  7.34 us (3%)
  other arithmetic  6.13 us (3%)
  local copies, waits for them, and re-layouts  4.64 us (2%)
  between operations  2.82 us (1%)
    ppermute x12, waiting for transfers between devices, step_on(): return lax.ppermute(block, axis, [(i, (i + 1) % size) for i in range(size)])  63.3 us
    ppermute x6, waiting for transfers between devices, paired(): lax.ppermute(value, 'tensor', [(i, i ^ bit) for i in range(ring)])  26.3 us
    pallas_call x1, Pallas kernels, middle_call(): pl.pallas_call(functools.partial(middle_kernel, ring=ring, chips=chips),...  22.2 us
    ppermute x18, waiting for transfers between devices, flipped(): lax.ppermute(pieces[f], 'dp', [(i, i ^ 2 * f) for i in range(size)])  21.8 us
    ppermute x18, starting transfers between devices, flipped(): lax.ppermute(pieces[f], 'dp', [(i, i ^ 2 * f) for i in range(size)])  21.7 us
    pallas_call x1, Pallas kernels, attention_call(): pl.pallas_call(functools.partial(attention_kernel, chips=chips, ring=ring...  8.7 us
    ppermute x6, starting transfers between devices, paired(): lax.ppermute(value, 'tensor', [(i, i ^ bit) for i in range(ring)])  7.82 us
    dot_general x4, matrix products, dot(): return jnp.dot(a, b, preferred_element_type=F32)  7.34 us
  transfers between devices with their start and end apart: 56, of which 30 were waited for; matrix products, arithmetic and copies ran while one was open for 6% of the time, Pallas kernels for 6%

profile of v7, /device:TPU:0, one launch (start us, length us, event | category | flops | bytes accessed | tf_op | source)
XLA Modules:
  0.0 235.9 jit_solution(18069854991832574279)
XLA Ops:
  0.7 1.1 fusion.10
  1.8 3.1 %collective-permute-start.3 = (bf16[256,512]{1,0:T(8,128)(2,1)S(1)}, bf16[256,512]{1,0:T(8,128)(2,1)S(1)}, u32[]{:S(2)}, u32[]{:S(2)}) collective-permute-start(bf16[256,512]{1,0:T(8,128)(2,1)S(1)} %get-tuple-element.144.refs_4_), channel_id=1, source_target_pairs={{0,1},{1,2},{2,3},{3,0},{4,5},{5,6},{6,7},{7,4},{8,9},{9,10},{10,1... | collective-permute-start | bytes 786440 | tf_op jit(solution)/shard_map/ppermute | solution.py:677
  4.9 1.6 collective-permute-start
  7.2 1.0 fusion.3
  8.6 5.5 %collective-permute-done.3.refs_5_ = bf16[256,512]{1,0:T(8,128)(2,1)S(1)} collective-permute-done((bf16[256,512]{1,0:T(8,128)(2,1)S(1)}, bf16[256,512]{1,0:T(8,128)(2,1)S(1)}, u32[]{:S(2)}, u32[]{:S(2)}) %collective-permute-start.3) | collective-permute-done | bytes 262176 | tf_op jit(solution)/shard_map/ppermute | solution.py:677
  14.1 5.6 %collective-permute-done.refs_1_ = bf16[256,512]{1,0:T(8,128)(2,1)S(1)} collective-permute-done((bf16[256,512]{1,0:T(8,128)(2,1)S(1)}, bf16[256,512]{1,0:T(8,128)(2,1)S(1)}, u32[]{:S(2)}, u32[]{:S(2)}) %collective-permute-start) | collective-permute-done | bytes 262176 | tf_op jit(solution)/shard_map/ppermute | solution.py:677
  19.7 1.1 constant_dynamic-slice_fusion.1
  20.9 1.1 convert_element_type.98
  22.0 3.3 %collective-permute-done.4.refs_6_ = bf16[256,512]{1,0:T(8,128)(2,1)S(1)} collective-permute-done((bf16[256,512]{1,0:T(8,128)(2,1)S(1)}, bf16[256,512]{1,0:T(8,128)(2,1)S(1)}, u32[]{:S(2)}, u32[]{:S(2)}) %collective-permute-start.4) | collective-permute-done | bytes 262176 | tf_op jit(solution)/shard_map/ppermute | solution.py:677
  25.3 5.6 %collective-permute-done.1.refs_2_ = bf16[256,512]{1,0:T(8,128)(2,1)S(1)} collective-permute-done((bf16[256,512]{1,0:T(8,128)(2,1)S(1)}, bf16[256,512]{1,0:T(8,128)(2,1)S(1)}, u32[]{:S(2)}, u32[]{:S(2)}) %collective-permute-start.1) | collective-permute-done | bytes 262176 | tf_op jit(solution)/shard_map/ppermute | solution.py:677
  31.1 5.4 %collective-permute-done.5.refs_7_ = bf16[256,512]{1,0:T(8,128)(2,1)S(1)} collective-permute-done((bf16[256,512]{1,0:T(8,128)(2,1)S(1)}, bf16[256,512]{1,0:T(8,128)(2,1)S(1)}, u32[]{:S(2)}, u32[]{:S(2)}) %collective-permute-start.5) | collective-permute-done | bytes 262176 | tf_op jit(solution)/shard_map/ppermute | solution.py:677
  36.5 4.8 %collective-permute-done.2.refs_3_ = bf16[256,512]{1,0:T(8,128)(2,1)S(1)} collective-permute-done((bf16[256,512]{1,0:T(8,128)(2,1)S(1)}, bf16[256,512]{1,0:T(8,128)(2,1)S(1)}, u32[]{:S(2)}, u32[]{:S(2)}) %collective-permute-start.2) | collective-permute-done | bytes 262176 | tf_op jit(solution)/shard_map/ppermute | solution.py:677
  41.4 6.3 %qkv.1 = (bf16[3,512,128]{2,1,0:T(8,128)(2,1)S(1)}, bf16[3,512,128]{2,1,0:T(8,128)(2,1)S(1)}, bf16[3,512,128]{2,1,0:T(8,128)(2,1)S(1)}, bf16[3,512,128]{2,1,0:T(8,128)(2,1)S(1)}, bf16[512,2048]{1,0:T(8,128)(2,1)S(1)}) custom-call(s32[16]{0:T(128)S(1)} %fusion.9.info_ref, bf16[256,512]{1,0:T(8,128)(2,1)S(1)} %get-tuple-element.145.refs_0_, ...), custom_call_target="tpu_custom_call" | custom-call | flops 3221225472 | bytes 6291456 | tf_op jit(solution)/shard_map/qkv/pallas_call | solution.py:231
  48.5 1.6 collective-permute-start.9
  50.1 1.5 collective-permute-start.6
  51.6 1.5 collective-permute-start.7
  54.1 5.6 %fusion.refs_26_ = bf16[2048,512]{1,0:T(8,128)(2,1)} fusion(bf16[2048,2048]{1,0:T(8,128)(2,1)S(1)} %bitcast.32, bf16[2048,512]{1,0:T(8,128)(2,1)S(1)} %copy-done.12), kind=kOutput, calls=%fused_computation.1 | convolution fusion | flops 4296015872 | bytes 12582912 | tf_op jit(solution)/shard_map/dot_general | solution.py:166
  59.7 0.8 multiply_convert_fusion
  61.2 0.9 collective-permute-done.6.refs_1_
  62.2 7.0 %collective-permute-done.7.refs_2_ = bf16[3,512,128]{2,1,0:T(8,128)(2,1)S(1)} collective-permute-done((bf16[3,512,128]{2,1,0:T(8,128)(2,1)S(1)}, bf16[3,512,128]{2,1,0:T(8,128)(2,1)S(1)}, u32[]{:S(2)}, u32[]{:S(2)}) %collective-permute-start.7) | collective-permute-done | bytes 393248 | tf_op jit(solution)/shard_map/ppermute | solution.py:699
  70.2 1.5 collective-permute-start.18
  71.7 1.2 collective-permute-start.17
  74.3 8.7 %attention.1 = (bf16[512,128]{1,0:T(8,128)(2,1)S(1)}, bf16[512,128]{1,0:T(8,128)(2,1)S(1)}, bf16[512,128]{1,0:T(8,128)(2,1)S(1)}, bf16[512,128]{1,0:T(8,128)(2,1)S(1)}) custom-call(s32[8]{0:T(128)S(1)} %convert_reduce_fusion.first_ref, s32[16]{0:T(128)S(1)} %fusion.9.info_ref, bf16[3,512,128]{2,1,0:T(8,128)(2,1)S(1)} %get-tuple-element.86.refs_0_, ...), custom_call_target="tpu_custom_call" | custom-call | flops 2147483648 | bytes 4194304 | tf_op jit(solution)/shard_map/attention/pallas_call | solution.py:337
  83.0 1.9 collective-permute-done.17.refs_12_
  85.0 1.1 collective-permute-start.19
  87.0 1.5 collective-permute-start.21
  88.5 2.5 %collective-permute-done.19 = bf16[512,128]{1,0:T(8,128)(2,1)S(1)} collective-permute-done((bf16[512,128]{1,0:T(8,128)(2,1)S(1)}, bf16[512,128]{1,0:T(8,128)(2,1)S(1)}, u32[]{:S(2)}, u32[]{:S(2)}) %collective-permute-start.19) | collective-permute-done | bytes 131104 | tf_op jit(solution)/shard_map/ppermute | solution.py:699
  91.0 1.5 collective-permute-done.20
  92.5 1.6 collective-permute-done.21
  94.7 1.1 collective-permute-start.25
  95.9 1.8 collective-permute-start.30
  97.7 7.6 %collective-permute-done.22.refs_1_ = bf16[2,512,128]{2,1,0:T(8,128)(2,1)S(1)} collective-permute-done((bf16[2,512,128]{2,1,0:T(8,128)(2,1)S(1)}, bf16[2,512,128]{2,1,0:T(8,128)(2,1)S(1)}, u32[]{:S(2)}, u32[]{:S(2)}) %collective-permute-start.22) | collective-permute-done | bytes 262176 | tf_op jit(solution)/shard_map/ppermute | solution.py:677
  106.1 1.5 collective-permute-start.28
  107.6 3.3 %collective-permute-done.25.refs_5_ = bf16[2,512,128]{2,1,0:T(8,128)(2,1)S(1)} collective-permute-done((bf16[2,512,128]{2,1,0:T(8,128)(2,1)S(1)}, bf16[2,512,128]{2,1,0:T(8,128)(2,1)S(1)}, u32[]{:S(2)}, u32[]{:S(2)}) %collective-permute-start.25) | collective-permute-done | bytes 262176 | tf_op jit(solution)/shard_map/ppermute | solution.py:677
  111.0 5.5 %collective-permute-done.23.refs_2_ = bf16[2,512,128]{2,1,0:T(8,128)(2,1)S(1)} collective-permute-done((bf16[2,512,128]{2,1,0:T(8,128)(2,1)S(1)}, bf16[2,512,128]{2,1,0:T(8,128)(2,1)S(1)}, u32[]{:S(2)}, u32[]{:S(2)}) %collective-permute-start.23) | collective-permute-done | bytes 262176 | tf_op jit(solution)/shard_map/ppermute | solution.py:677
  116.5 3.7 %collective-permute-done.26.refs_6_ = bf16[2,512,128]{2,1,0:T(8,128)(2,1)S(1)} collective-permute-done((bf16[2,512,128]{2,1,0:T(8,128)(2,1)S(1)}, bf16[2,512,128]{2,1,0:T(8,128)(2,1)S(1)}, u32[]{:S(2)}, u32[]{:S(2)}) %collective-permute-start.26) | collective-permute-done | bytes 262176 | tf_op jit(solution)/shard_map/ppermute | solution.py:677
  121.0 10.2 %collective-permute-done.24.refs_3_ = bf16[2,512,128]{2,1,0:T(8,128)(2,1)S(1)} collective-permute-done((bf16[2,512,128]{2,1,0:T(8,128)(2,1)S(1)}, bf16[2,512,128]{2,1,0:T(8,128)(2,1)S(1)}, u32[]{:S(2)}, u32[]{:S(2)}) %collective-permute-start.24) | collective-permute-done | bytes 262176 | tf_op jit(solution)/shard_map/ppermute | solution.py:677
  131.3 2.8 %collective-permute-done.27.refs_7_ = bf16[2,512,128]{2,1,0:T(8,128)(2,1)S(1)} collective-permute-done((bf16[2,512,128]{2,1,0:T(8,128)(2,1)S(1)}, bf16[2,512,128]{2,1,0:T(8,128)(2,1)S(1)}, u32[]{:S(2)}, u32[]{:S(2)}) %collective-permute-start.27) | collective-permute-done | bytes 262176 | tf_op jit(solution)/shard_map/ppermute | solution.py:677
  134.1 1.9 collective-permute-done.33.refs_20_
  136.0 22.2 %middle.1 = (bf16[512,2048]{1,0:T(8,128)(2,1)}, bf16[512,512]{1,0:T(8,128)(2,1)S(1)}, bf16[128,512]{1,0:T(8,128)(2,1)S(1)}, bf16[128,512]{1,0:T(8,128)(2,1)S(1)}...) custom-call(s32[16]{0:T(128)S(1)} %fusion.9.info_ref, bf16[2,512,128]{2,1,0:T(8,128)(2,1)S(1)} %pad_maximum_fusion.3.refs_0_, ...), custom_call_target="tpu_custom_call" | custom-call | flops 14227079168 | bytes 25165824 | tf_op jit(solution)/shard_map/middle/pallas_call | solution.py:481
  158.4 3.7 %collective-permute-start.38 = (bf16[128,512]{1,0:T(8,128)(2,1)S(1)}, bf16[128,512]{1,0:T(8,128)(2,1)S(1)}, u32[]{:S(2)}, u32[]{:S(2)}) collective-permute-start(bf16[128,512]{1,0:T(8,128)(2,1)S(1)} %get-tuple-element.120), channel_id=1, source_target_pairs={{0,3},{1,0},{2,1},{3,2},{4,7},{5,4},{6,5},{7,6},{8,11},{9,8},{10,9... | collective-permute-start | bytes 393224 | tf_op jit(solution)/shard_map/ppermute | solution.py:690
  162.1 1.6 copy-done.8
  163.7 6.5 %down.1 = (bf16[512,512]{1,0:T(8,128)(2,1)S(1)}, bf16[512,512]{1,0:T(8,128)(2,1)S(1)}, bf16[512,512]{1,0:T(8,128)(2,1)S(1)}, bf16[512,512]{1,0:T(8,128)(2,1)S(1)}) custom-call(s32[16]{0:T(128)S(1)} %fusion.9.info_ref, bf16[512,2048]{1,0:T(8,128)(2,1)S(1)} %copy-done.8, bf16[2048,2048]{1,0:T(8,128)(2,1)S(1)} %bitcast.32), custom_call_target="tpu_custom_call" | custom-call | flops 4294967296 | bytes 8388608 | tf_op jit(solution)/shard_map/down/pallas_call | solution.py:554
  170.2 1.0 collective-permute-done.37
  171.2 1.1 multiply_convert_fusion.3.refs_0_
  172.3 2.6 %collective-permute-start.39 = (bf16[512,512]{1,0:T(8,128)(2,1)S(1)}, bf16[512,512]{1,0:T(8,128)(2,1)S(1)}, u32[]{:S(2)}, u32[]{:S(2)}) collective-permute-start(bf16[512,512]{1,0:T(8,128)(2,1)S(1)} %get-tuple-element.125), channel_id=1, source_target_pairs={{0,1},{1,0},{2,3},{3,2},{4,5},{5,4},{6,7},{7,6},{8,9},{9,8},{10,11... | collective-permute-start | bytes 1572872 | tf_op jit(solution)/shard_map/ppermute | solution.py:780
  175.4 1.1 collective-permute-start.42
  176.5 1.1 collective-permute-start.41
  177.6 13.0 %collective-permute-done.39 = bf16[512,512]{1,0:T(8,128)(2,1)S(1)} collective-permute-done((bf16[512,512]{1,0:T(8,128)(2,1)S(1)}, bf16[512,512]{1,0:T(8,128)(2,1)S(1)}, u32[]{:S(2)}, u32[]{:S(2)}) %collective-permute-start.39) | collective-permute-done | bytes 524320 | tf_op jit(solution)/shard_map/ppermute | solution.py:780
  190.6 2.8 %collective-permute-done.43.refs_3_ = bf16[128,512]{1,0:T(8,128)(2,1)S(1)} collective-permute-done((bf16[128,512]{1,0:T(8,128)(2,1)S(1)}, bf16[128,512]{1,0:T(8,128)(2,1)S(1)}, u32[]{:S(2)}, u32[]{:S(2)}) %collective-permute-start.43) | collective-permute-done | bytes 131104 | tf_op jit(solution)/shard_map/ppermute | solution.py:690
  193.4 1.7 collective-permute-done.41.refs_1_
  195.0 2.2 grads.1
  197.3 2.4 %collective-permute-done.44.theirs_ref = bf16[4,208,512]{2,1,0:T(8,128)(2,1)S(1)} collective-permute-done((bf16[4,208,512]{2,1,0:T(8,128)(2,1)S(1)}, bf16[4,208,512]{2,1,0:T(8,128)(2,1)S(1)}, u32[]{:S(2)}, u32[]{:S(2)}) %collective-permute-start.44) | collective-permute-done | bytes 852000 | tf_op jit(solution)/shard_map/ppermute | solution.py:707
  199.9 1.2 collective-permute-start.46
  201.1 2.3 collective-permute-start.47
  203.5 1.1 collective-permute-start.49
  204.6 1.3 collective-permute-start.40
  205.9 2.1 collective-permute-done.45
  208.0 3.8 %collective-permute-done.46 = bf16[208,512]{1,0:T(8,128)(2,1)S(1)} collective-permute-done((bf16[208,512]{1,0:T(8,128)(2,1)S(1)}, bf16[208,512]{1,0:T(8,128)(2,1)S(1)}, u32[]{:S(2)}, u32[]{:S(2)}) %collective-permute-start.46) | collective-permute-done | bytes 213024 | tf_op jit(solution)/shard_map/ppermute | solution.py:699
  212.0 1.6 collective-permute-start.48
  213.5 1.6 collective-permute-start.51
  215.5 13.3 %collective-permute-done.49 = bf16[512,512]{1,0:T(8,128)(2,1)S(1)} collective-permute-done((bf16[512,512]{1,0:T(8,128)(2,1)S(1)}, bf16[512,512]{1,0:T(8,128)(2,1)S(1)}, u32[]{:S(2)}, u32[]{:S(2)}) %collective-permute-start.49) | collective-permute-done | bytes 524320 | tf_op jit(solution)/shard_map/ppermute | solution.py:780
  229.9 1.1 add_convert_fusion
  231.2 2.4 %finish.1 = (f32[512,512]{1,0:T(8,128)}, f32[512,512]{1,0:T(8,128)}, f32[512,512]{1,0:T(8,128)}, f32[8,16,128]{2,1,0:T(8,128)S(1)}) custom-call(s32[16]{0:T(128)S(1)} %fusion.9.info_ref, bf16[208,512]{1,0:T(8,128)(2,1)S(1)} %add_convert_fusion.2.refs_0_, bf16[208,512]{1,0:T(8,128)(2,1)S(1)} %collective-permute-done.50.refs_1_, ...), custom_call_target="tpu_custom_call" | custom-call | flops 262144 | bytes 3145728 | tf_op jit(solution)/shard_map/finish/pallas_call | solution.py:659
  (111 shorter events, 12.8 us)
Async XLA Ops:
  0.6 59.1 %copy-start = (bf16[512,512]{1,0:T(8,128)(2,1)S(1)}, bf16[512,512]{1,0:T(8,128)(2,1)}, u32[]{:S(2)}) copy-start(bf16[512,512]{1,0:T(8,128)(2,1)} %param.31) | copy-start | bytes 1572868
  1.8 12.2 %collective-permute-start.3 = (bf16[256,512]{1,0:T(8,128)(2,1)S(1)}, bf16[256,512]{1,0:T(8,128)(2,1)S(1)}, u32[]{:S(2)}, u32[]{:S(2)}) collective-permute-start(bf16[256,512]{1,0:T(8,128)(2,1)S(1)} %get-tuple-element.144.refs_4_), channel_id=1, source_target_pairs={{0,1},{1,2},{2,3},{3,0},{4,5},{5,6},{6,7},{7,4},{8,9},{9,10},{10,1... | collective-permute-start | bytes 786440 | tf_op jit(solution)/shard_map/ppermute | solution.py:677
  4.9 14.8 %collective-permute-start = (bf16[256,512]{1,0:T(8,128)(2,1)S(1)}, bf16[256,512]{1,0:T(8,128)(2,1)S(1)}, u32[]{:S(2)}, u32[]{:S(2)}) collective-permute-start(bf16[256,512]{1,0:T(8,128)(2,1)S(1)} %get-tuple-element.145.refs_0_), channel_id=1, source_target_pairs={{0,1},{1,2},{2,3},{3,0},{4,5},{5,6},{6,7},{7,4},{8,9},{9,10},{10,1... | collective-permute-start | bytes 786440 | tf_op jit(solution)/shard_map/ppermute | solution.py:677
  8.2 33.2 %copy-start.4 = (bf16[2048,512]{1,0:T(8,128)(2,1)S(1)}, bf16[2048,512]{1,0:T(8,128)(2,1)}, u32[]{:S(2)}) copy-start(bf16[2048,512]{1,0:T(8,128)(2,1)} %refs_12_.1) | copy-start | bytes 6291460
  8.4 32.9 %copy-start.3 = (bf16[2048,512]{1,0:T(8,128)(2,1)S(1)}, bf16[2048,512]{1,0:T(8,128)(2,1)}, u32[]{:S(2)}) copy-start(bf16[2048,512]{1,0:T(8,128)(2,1)} %refs_11_.1) | copy-start | bytes 6291460
  8.4 32.9 %copy-start.5 = (f32[2048]{0:T(1024)S(1)}, f32[2048]{0:T(1024)}, u32[]{:S(2)}) copy-start(f32[2048]{0:T(1024)} %param.20) | copy-start | bytes 24580
  14.1 11.2 %collective-permute-start.4 = (bf16[256,512]{1,0:T(8,128)(2,1)S(1)}, bf16[256,512]{1,0:T(8,128)(2,1)S(1)}, u32[]{:S(2)}, u32[]{:S(2)}) collective-permute-start(bf16[256,512]{1,0:T(8,128)(2,1)S(1)} %collective-permute-done.3.refs_5_), channel_id=1, source_target_pairs={{0,1},{1,2},{2,3},{3,0},{4,5},{5,6},{6,7},{7,4},{8,9},{9,10},{10,1... | collective-permute-start | bytes 786440 | tf_op jit(solution)/shard_map/ppermute | solution.py:677
  19.7 11.2 %collective-permute-start.1 = (bf16[256,512]{1,0:T(8,128)(2,1)S(1)}, bf16[256,512]{1,0:T(8,128)(2,1)S(1)}, u32[]{:S(2)}, u32[]{:S(2)}) collective-permute-start(bf16[256,512]{1,0:T(8,128)(2,1)S(1)} %collective-permute-done.refs_1_), channel_id=1, source_target_pairs={{0,1},{1,2},{2,3},{3,0},{4,5},{5,6},{6,7},{7,4},{8,9},{9,10},{10,1... | collective-permute-start | bytes 786440 | tf_op jit(solution)/shard_map/ppermute | solution.py:677
  20.9 33.2 %slice-start = ((s8[8388608]{0:T(1024)(128)(4,1)}), s8[4194304]{0:T(1024)(128)(4,1)S(1)}, s32[]{:S(2)}) async-start(s8[8388608]{0:T(1024)(128)(4,1)} %bitcast.31), calls=%async_computation | async-start | bytes 8388608
  25.3 11.2 %collective-permute-start.5 = (bf16[256,512]{1,0:T(8,128)(2,1)S(1)}, bf16[256,512]{1,0:T(8,128)(2,1)S(1)}, u32[]{:S(2)}, u32[]{:S(2)}) collective-permute-start(bf16[256,512]{1,0:T(8,128)(2,1)S(1)} %collective-permute-done.4.refs_6_), channel_id=1, source_target_pairs={{0,1},{1,2},{2,3},{3,0},{4,5},{5,6},{6,7},{7,4},{8,9},{9,10},{10,1... | collective-permute-start | bytes 786440 | tf_op jit(solution)/shard_map/ppermute | solution.py:677
  30.9 10.4 %collective-permute-start.2 = (bf16[256,512]{1,0:T(8,128)(2,1)S(1)}, bf16[256,512]{1,0:T(8,128)(2,1)S(1)}, u32[]{:S(2)}, u32[]{:S(2)}) collective-permute-start(bf16[256,512]{1,0:T(8,128)(2,1)S(1)} %collective-permute-done.1.refs_2_), channel_id=1, source_target_pairs={{0,1},{1,2},{2,3},{3,0},{4,5},{5,6},{6,7},{7,4},{8,9},{9,10},{10,1... | collective-permute-start | bytes 786440 | tf_op jit(solution)/shard_map/ppermute | solution.py:677
  41.4 12.7 %slice-start.1 = ((s8[8388608]{0:T(1024)(128)(4,1)}), s8[4194304]{0:T(1024)(128)(4,1)S(1)}, s32[]{:S(2)}) async-start(s8[8388608]{0:T(1024)(128)(4,1)} %bitcast.31), calls=%async_computation.1 | async-start | bytes 8388608
  47.7 13.5 %collective-permute-start.10 = (bf16[512,256]{1,0:T(8,128)(2,1)S(1)}, bf16[512,256]{1,0:T(8,128)(2,1)S(1)}, u32[]{:S(2)}, u32[]{:S(2)}) collective-permute-start(bf16[512,256]{1,0:T(8,128)(2,1)S(1)} %constant_dynamic-slice_fusion.1), channel_id=1, source_target_pairs={{0,2},{1,3},{2,0},{3,1},{4,6},{5,7},{6,4},{7,5},{8,10},{9,11},{10,... | collective-permute-start | bytes 786440 | tf_op jit(solution)/shard_map/ppermute | solution.py:780
  48.5 12.7 %collective-permute-start.9 = (bf16[512,256]{1,0:T(8,128)(2,1)S(1)}, bf16[512,256]{1,0:T(8,128)(2,1)S(1)}, u32[]{:S(2)}, u32[]{:S(2)}) collective-permute-start(bf16[512,256]{1,0:T(8,128)(2,1)S(1)} %constant_dynamic-slice_fusion.1), channel_id=1, source_target_pairs={{0,1},{1,0},{2,3},{3,2},{4,5},{5,4},{6,7},{7,6},{8,9},{9,8},{10,11... | collective-permute-start | bytes 786440 | tf_op jit(solution)/shard_map/ppermute | solution.py:780
  50.1 12.1 %collective-permute-start.6 = (bf16[3,512,128]{2,1,0:T(8,128)(2,1)S(1)}, bf16[3,512,128]{2,1,0:T(8,128)(2,1)S(1)}, u32[]{:S(2)}, u32[]{:S(2)}) collective-permute-start(bf16[3,512,128]{2,1,0:T(8,128)(2,1)S(1)} %get-tuple-element.76), channel_id=1, source_target_pairs={{0,8},{4,12},{8,0},{12,4},{16,24},{20,28},{24,16},{28,20},{1,9},{5... | collective-permute-start | bytes 1179656 | tf_op jit(solution)/shard_map/ppermute | solution.py:699
  51.6 17.6 %collective-permute-start.7 = (bf16[3,512,128]{2,1,0:T(8,128)(2,1)S(1)}, bf16[3,512,128]{2,1,0:T(8,128)(2,1)S(1)}, u32[]{:S(2)}, u32[]{:S(2)}) collective-permute-start(bf16[3,512,128]{2,1,0:T(8,128)(2,1)S(1)} %get-tuple-element.77), channel_id=1, source_target_pairs={{0,16},{4,20},{8,24},{12,28},{16,0},{20,4},{24,8},{28,12},{1,17},{... | collective-permute-start | bytes 1179656 | tf_op jit(solution)/shard_map/ppermute | solution.py:699
  53.1 16.1 %collective-permute-start.8 = (bf16[3,512,128]{2,1,0:T(8,128)(2,1)S(1)}, bf16[3,512,128]{2,1,0:T(8,128)(2,1)S(1)}, u32[]{:S(2)}, u32[]{:S(2)}) collective-permute-start(bf16[3,512,128]{2,1,0:T(8,128)(2,1)S(1)} %get-tuple-element.78), channel_id=1, source_target_pairs={{0,24},{4,28},{8,16},{12,20},{16,8},{20,12},{24,0},{28,4},{1,25},{... | collective-permute-start | bytes 1179656 | tf_op jit(solution)/shard_map/ppermute | solution.py:699
  60.6 13.6 %copy-start.11 = (s32[4096]{0:T(1024)S(1)}, s32[4096]{0:T(1024)}, u32[]{:S(2)}) copy-start(s32[4096]{0:T(1024)} %param.18) | copy-start | bytes 49156
  69.2 2.5 %collective-permute-start.11 = (bf16[3,512,128]{2,1,0:T(8,128)(2,1)S(1)}, bf16[3,512,128]{2,1,0:T(8,128)(2,1)S(1)}, u32[]{:S(2)}, u32[]{:S(2)}) collective-permute-start(bf16[3,512,128]{2,1,0:T(8,128)(2,1)S(1)} %get-tuple-element.86.refs_0_), channel_id=1, source_target_pairs={{0,4},{4,0},{8,12},{12,8},{16,20},{20,16},{24,28},{28,24},{1,5},{5... | collective-permute-start | bytes 1179656 | tf_op jit(solution)/shard_map/ppermute | solution.py:707
  69.2 3.7 %collective-permute-start.12 = (bf16[3,512,128]{2,1,0:T(8,128)(2,1)S(1)}, bf16[3,512,128]{2,1,0:T(8,128)(2,1)S(1)}, u32[]{:S(2)}, u32[]{:S(2)}) collective-permute-start(bf16[3,512,128]{2,1,0:T(8,128)(2,1)S(1)} %collective-permute-done.6.refs_1_), channel_id=1, source_target_pairs={{0,4},{4,0},{8,12},{12,8},{16,20},{20,16},{24,28},{28,24},{1,5},{5... | collective-permute-start | bytes 1179656 | tf_op jit(solution)/shard_map/ppermute | solution.py:707
  69.7 4.0 %collective-permute-start.13 = (bf16[3,512,128]{2,1,0:T(8,128)(2,1)S(1)}, bf16[3,512,128]{2,1,0:T(8,128)(2,1)S(1)}, u32[]{:S(2)}, u32[]{:S(2)}) collective-permute-start(bf16[3,512,128]{2,1,0:T(8,128)(2,1)S(1)} %collective-permute-done.7.refs_2_), channel_id=1, source_target_pairs={{0,4},{4,0},{8,12},{12,8},{16,20},{20,16},{24,28},{28,24},{1,5},{5... | collective-permute-start | bytes 1179656 | tf_op jit(solution)/shard_map/ppermute | solution.py:707
  69.7 4.6 %collective-permute-start.14 = (bf16[3,512,128]{2,1,0:T(8,128)(2,1)S(1)}, bf16[3,512,128]{2,1,0:T(8,128)(2,1)S(1)}, u32[]{:S(2)}, u32[]{:S(2)}) collective-permute-start(bf16[3,512,128]{2,1,0:T(8,128)(2,1)S(1)} %collective-permute-done.8.refs_3_), channel_id=1, source_target_pairs={{0,4},{4,0},{8,12},{12,8},{16,20},{20,16},{24,28},{28,24},{1,5},{5... | collective-permute-start | bytes 1179656 | tf_op jit(solution)/shard_map/ppermute | solution.py:707
  70.2 12.8 %collective-permute-start.18 = (bf16[512,256]{1,0:T(8,128)(2,1)S(1)}, bf16[512,256]{1,0:T(8,128)(2,1)S(1)}, u32[]{:S(2)}, u32[]{:S(2)}) collective-permute-start(bf16[512,256]{1,0:T(8,128)(2,1)S(1)} %collective-permute-done.9.refs_10_), channel_id=1, source_target_pairs={{0,24},{4,28},{8,16},{12,20},{16,8},{20,12},{24,0},{28,4},{1,25},{... | collective-permute-start | bytes 786440 | tf_op jit(solution)/shard_map/ppermute | solution.py:699
  71.7 13.2 %collective-permute-start.17 = (bf16[512,256]{1,0:T(8,128)(2,1)S(1)}, bf16[512,256]{1,0:T(8,128)(2,1)S(1)}, u32[]{:S(2)}, u32[]{:S(2)}) collective-permute-start(bf16[512,256]{1,0:T(8,128)(2,1)S(1)} %collective-permute-done.9.refs_10_), channel_id=1, source_target_pairs={{0,16},{4,20},{8,24},{12,28},{16,0},{20,4},{24,8},{28,12},{1,17},{... | collective-permute-start | bytes 786440 | tf_op jit(solution)/shard_map/ppermute | solution.py:699
  72.9 12.1 %collective-permute-start.16 = (bf16[512,256]{1,0:T(8,128)(2,1)S(1)}, bf16[512,256]{1,0:T(8,128)(2,1)S(1)}, u32[]{:S(2)}, u32[]{:S(2)}) collective-permute-start(bf16[512,256]{1,0:T(8,128)(2,1)S(1)} %collective-permute-done.9.refs_10_), channel_id=1, source_target_pairs={{0,8},{4,12},{8,0},{12,4},{16,24},{20,28},{24,16},{28,20},{1,9},{5... | collective-permute-start | bytes 786440 | tf_op jit(solution)/shard_map/ppermute | solution.py:699
  73.7 9.3 %collective-permute-start.15 = (bf16[512,256]{1,0:T(8,128)(2,1)S(1)}, bf16[512,256]{1,0:T(8,128)(2,1)S(1)}, u32[]{:S(2)}, u32[]{:S(2)}) collective-permute-start(bf16[512,256]{1,0:T(8,128)(2,1)S(1)} %collective-permute-done.10), channel_id=1, source_target_pairs={{0,1},{1,0},{2,3},{3,2},{4,5},{5,4},{6,7},{7,6},{8,9},{9,8},{10,11... | collective-permute-start | bytes 786440 | tf_op jit(solution)/shard_map/ppermute | solution.py:780
  85.0 6.0 %collective-permute-start.19 = (bf16[512,128]{1,0:T(8,128)(2,1)S(1)}, bf16[512,128]{1,0:T(8,128)(2,1)S(1)}, u32[]{:S(2)}, u32[]{:S(2)}) collective-permute-start(bf16[512,128]{1,0:T(8,128)(2,1)S(1)} %get-tuple-element.97), channel_id=1, source_target_pairs={{0,8},{4,12},{8,0},{12,4},{16,24},{20,28},{24,16},{28,20},{1,9},{5... | collective-permute-start | bytes 393224 | tf_op jit(solution)/shard_map/ppermute | solution.py:699
  86.2 6.3 %collective-permute-start.20 = (bf16[512,128]{1,0:T(8,128)(2,1)S(1)}, bf16[512,128]{1,0:T(8,128)(2,1)S(1)}, u32[]{:S(2)}, u32[]{:S(2)}) collective-permute-start(bf16[512,128]{1,0:T(8,128)(2,1)S(1)} %get-tuple-element.98), channel_id=1, source_target_pairs={{0,16},{4,20},{8,24},{12,28},{16,0},{20,4},{24,8},{28,12},{1,17},{... | collective-permute-start | bytes 393224 | tf_op jit(solution)/shard_map/ppermute | solution.py:699
  87.0 7.1 %collective-permute-start.21 = (bf16[512,128]{1,0:T(8,128)(2,1)S(1)}, bf16[512,128]{1,0:T(8,128)(2,1)S(1)}, u32[]{:S(2)}, u32[]{:S(2)}) collective-permute-start(bf16[512,128]{1,0:T(8,128)(2,1)S(1)} %get-tuple-element.99), channel_id=1, source_target_pairs={{0,24},{4,28},{8,16},{12,20},{16,8},{20,12},{24,0},{28,4},{1,25},{... | collective-permute-start | bytes 393224 | tf_op jit(solution)/shard_map/ppermute | solution.py:699
  94.1 41.9 %copy-start.6 = (f32[2048]{0:T(1024)S(1)}, f32[2048]{0:T(1024)}, u32[]{:S(2)}) copy-start(f32[2048]{0:T(1024)} %param.21) | copy-start | bytes 24580
  94.2 11.1 %collective-permute-start.22 = (bf16[2,512,128]{2,1,0:T(8,128)(2,1)S(1)}, bf16[2,512,128]{2,1,0:T(8,128)(2,1)S(1)}, u32[]{:S(2)}, u32[]{:S(2)}) collective-permute-start(bf16[2,512,128]{2,1,0:T(8,128)(2,1)S(1)} %pad_maximum_fusion.3.refs_0_), channel_id=1, source_target_pairs={{0,1},{1,2},{2,3},{3,0},{4,5},{5,6},{6,7},{7,4},{8,9},{9,10},{10,1... | collective-permute-start | bytes 786440 | tf_op jit(solution)/shard_map/ppermute | solution.py:677
  94.7 16.2 %collective-permute-start.25 = (bf16[2,512,128]{2,1,0:T(8,128)(2,1)S(1)}, bf16[2,512,128]{2,1,0:T(8,128)(2,1)S(1)}, u32[]{:S(2)}, u32[]{:S(2)}) collective-permute-start(bf16[2,512,128]{2,1,0:T(8,128)(2,1)S(1)} %pad_maximum_fusion.4.refs_4_), channel_id=1, source_target_pairs={{0,1},{1,2},{2,3},{3,0},{4,5},{5,6},{6,7},{7,4},{8,9},{9,10},{10,1... | collective-permute-start | bytes 786440 | tf_op jit(solution)/shard_map/ppermute | solution.py:677
  95.9 24.4 %collective-permute-start.30 = (bf16[2,512,256]{2,1,0:T(8,128)(2,1)S(1)}, bf16[2,512,256]{2,1,0:T(8,128)(2,1)S(1)}, u32[]{:S(2)}, u32[]{:S(2)}) collective-permute-start(bf16[2,512,256]{2,1,0:T(8,128)(2,1)S(1)} %pad_maximum_fusion.refs_14_), channel_id=1, source_target_pairs={{0,24},{4,28},{8,16},{12,20},{16,8},{20,12},{24,0},{28,4},{1,25},{... | collective-permute-start | bytes 1572872 | tf_op jit(solution)/shard_map/ppermute | solution.py:699
  105.3 11.2 %collective-permute-start.23 = (bf16[2,512,128]{2,1,0:T(8,128)(2,1)S(1)}, bf16[2,512,128]{2,1,0:T(8,128)(2,1)S(1)}, u32[]{:S(2)}, u32[]{:S(2)}) collective-permute-start(bf16[2,512,128]{2,1,0:T(8,128)(2,1)S(1)} %collective-permute-done.22.refs_1_), channel_id=1, source_target_pairs={{0,1},{1,2},{2,3},{3,0},{4,5},{5,6},{6,7},{7,4},{8,9},{9,10},{10,1... | collective-permute-start | bytes 786440 | tf_op jit(solution)/shard_map/ppermute | solution.py:677
  105.3 15.3 %collective-permute-start.29 = (bf16[2,512,256]{2,1,0:T(8,128)(2,1)S(1)}, bf16[2,512,256]{2,1,0:T(8,128)(2,1)S(1)}, u32[]{:S(2)}, u32[]{:S(2)}) collective-permute-start(bf16[2,512,256]{2,1,0:T(8,128)(2,1)S(1)} %pad_maximum_fusion.refs_14_), channel_id=1, source_target_pairs={{0,16},{4,20},{8,24},{12,28},{16,0},{20,4},{24,8},{28,12},{1,17},{... | collective-permute-start | bytes 1572872 | tf_op jit(solution)/shard_map/ppermute | solution.py:699
  106.1 14.4 %collective-permute-start.28 = (bf16[2,512,256]{2,1,0:T(8,128)(2,1)S(1)}, bf16[2,512,256]{2,1,0:T(8,128)(2,1)S(1)}, u32[]{:S(2)}, u32[]{:S(2)}) collective-permute-start(bf16[2,512,256]{2,1,0:T(8,128)(2,1)S(1)} %pad_maximum_fusion.refs_14_), channel_id=1, source_target_pairs={{0,8},{4,12},{8,0},{12,4},{16,24},{20,28},{24,16},{28,20},{1,9},{5... | collective-permute-start | bytes 1572872 | tf_op jit(solution)/shard_map/ppermute | solution.py:699
  110.9 9.4 %collective-permute-start.26 = (bf16[2,512,128]{2,1,0:T(8,128)(2,1)S(1)}, bf16[2,512,128]{2,1,0:T(8,128)(2,1)S(1)}, u32[]{:S(2)}, u32[]{:S(2)}) collective-permute-start(bf16[2,512,128]{2,1,0:T(8,128)(2,1)S(1)} %collective-permute-done.25.refs_5_), channel_id=1, source_target_pairs={{0,1},{1,2},{2,3},{3,0},{4,5},{5,6},{6,7},{7,4},{8,9},{9,10},{10,1... | collective-permute-start | bytes 786440 | tf_op jit(solution)/shard_map/ppermute | solution.py:677
  116.5 19.5 %collective-permute-start.31 = (bf16[4,1,512,256]{3,2,0,1:T(8,128)(2,1)S(1)}, bf16[4,1,512,256]{3,2,0,1:T(8,128)(2,1)S(1)}, u32[]{:S(2)}, u32[]{:S(2)}) collective-permute-start(bf16[4,1,512,256]{3,2,0,1:T(8,128)(2,1)S(1)} %maximum_bitcast_fusion), channel_id=1, source_target_pairs={{0,4},{4,0},{8,12},{12,8},{16,20},{20,16},{24,28},{28,24},{1,5},{5... | collective-permute-start | bytes 3145736 | tf_op jit(solution)/shard_map/ppermute | solution.py:707
  120.2 11.0 %collective-permute-start.24 = (bf16[2,512,128]{2,1,0:T(8,128)(2,1)S(1)}, bf16[2,512,128]{2,1,0:T(8,128)(2,1)S(1)}, u32[]{:S(2)}, u32[]{:S(2)}) collective-permute-start(bf16[2,512,128]{2,1,0:T(8,128)(2,1)S(1)} %collective-permute-done.23.refs_2_), channel_id=1, source_target_pairs={{0,1},{1,2},{2,3},{3,0},{4,5},{5,6},{6,7},{7,4},{8,9},{9,10},{10,1... | collective-permute-start | bytes 786440 | tf_op jit(solution)/shard_map/ppermute | solution.py:677
  120.2 13.9 %collective-permute-start.27 = (bf16[2,512,128]{2,1,0:T(8,128)(2,1)S(1)}, bf16[2,512,128]{2,1,0:T(8,128)(2,1)S(1)}, u32[]{:S(2)}, u32[]{:S(2)}) collective-permute-start(bf16[2,512,128]{2,1,0:T(8,128)(2,1)S(1)} %collective-permute-done.26.refs_6_), channel_id=1, source_target_pairs={{0,1},{1,2},{2,3},{3,0},{4,5},{5,6},{6,7},{7,4},{8,9},{9,10},{10,1... | collective-permute-start | bytes 786440 | tf_op jit(solution)/shard_map/ppermute | solution.py:677
  120.5 13.6 %collective-permute-start.32 = (bf16[2,512,256]{2,1,0:T(8,128)(2,1)S(1)}, bf16[2,512,256]{2,1,0:T(8,128)(2,1)S(1)}, u32[]{:S(2)}, u32[]{:S(2)}) collective-permute-start(bf16[2,512,256]{2,1,0:T(8,128)(2,1)S(1)} %pad_maximum_fusion.refs_14_), channel_id=1, source_target_pairs={{0,4},{4,0},{8,12},{12,8},{16,20},{20,16},{24,28},{28,24},{1,5},{5... | collective-permute-start | bytes 1572872 | tf_op jit(solution)/shard_map/ppermute | solution.py:707
  120.5 13.6 %collective-permute-start.35 = (bf16[2,512,256]{2,1,0:T(8,128)(2,1)S(1)}, bf16[2,512,256]{2,1,0:T(8,128)(2,1)S(1)}, u32[]{:S(2)}, u32[]{:S(2)}) collective-permute-start(bf16[2,512,256]{2,1,0:T(8,128)(2,1)S(1)} %collective-permute-done.30.refs_17_), channel_id=1, source_target_pairs={{0,4},{4,0},{8,12},{12,8},{16,20},{20,16},{24,28},{28,24},{1,5},{5... | collective-permute-start | bytes 1572872 | tf_op jit(solution)/shard_map/ppermute | solution.py:707
  131.3 2.8 %collective-permute-start.34 = (bf16[2,512,256]{2,1,0:T(8,128)(2,1)S(1)}, bf16[2,512,256]{2,1,0:T(8,128)(2,1)S(1)}, u32[]{:S(2)}, u32[]{:S(2)}) collective-permute-start(bf16[2,512,256]{2,1,0:T(8,128)(2,1)S(1)} %collective-permute-done.29.refs_16_), channel_id=1, source_target_pairs={{0,4},{4,0},{8,12},{12,8},{16,20},{20,16},{24,28},{28,24},{1,5},{5... | collective-permute-start | bytes 1572872 | tf_op jit(solution)/shard_map/ppermute | solution.py:707
  134.1 1.9 collective-permute-start.33
  158.2 12.0 %collective-permute-start.36 = (bf16[128,512]{1,0:T(8,128)(2,1)S(1)}, bf16[128,512]{1,0:T(8,128)(2,1)S(1)}, u32[]{:S(2)}, u32[]{:S(2)}) collective-permute-start(bf16[128,512]{1,0:T(8,128)(2,1)S(1)} %get-tuple-element.118), channel_id=1, source_target_pairs={{0,1},{1,2},{2,3},{3,0},{4,5},{5,6},{6,7},{7,4},{8,9},{9,10},{10,1... | collective-permute-start | bytes 393224 | tf_op jit(solution)/shard_map/ppermute | solution.py:690
  158.3 12.9 %collective-permute-start.37 = (bf16[128,512]{1,0:T(8,128)(2,1)S(1)}, bf16[128,512]{1,0:T(8,128)(2,1)S(1)}, u32[]{:S(2)}, u32[]{:S(2)}) collective-permute-start(bf16[128,512]{1,0:T(8,128)(2,1)S(1)} %get-tuple-element.119), channel_id=1, source_target_pairs={{0,2},{1,3},{2,0},{3,1},{4,6},{5,7},{6,4},{7,5},{8,10},{9,11},{10,... | collective-permute-start | bytes 393224 | tf_op jit(solution)/shard_map/ppermute | solution.py:690
  158.4 12.9 %collective-permute-start.38 = (bf16[128,512]{1,0:T(8,128)(2,1)S(1)}, bf16[128,512]{1,0:T(8,128)(2,1)S(1)}, u32[]{:S(2)}, u32[]{:S(2)}) collective-permute-start(bf16[128,512]{1,0:T(8,128)(2,1)S(1)} %get-tuple-element.120), channel_id=1, source_target_pairs={{0,3},{1,0},{2,1},{3,2},{4,7},{5,4},{6,5},{7,6},{8,11},{9,8},{10,9... | collective-permute-start | bytes 393224 | tf_op jit(solution)/shard_map/ppermute | solution.py:690
  172.3 18.3 %collective-permute-start.39 = (bf16[512,512]{1,0:T(8,128)(2,1)S(1)}, bf16[512,512]{1,0:T(8,128)(2,1)S(1)}, u32[]{:S(2)}, u32[]{:S(2)}) collective-permute-start(bf16[512,512]{1,0:T(8,128)(2,1)S(1)} %get-tuple-element.125), channel_id=1, source_target_pairs={{0,1},{1,0},{2,3},{3,2},{4,5},{5,4},{6,7},{7,6},{8,9},{9,8},{10,11... | collective-permute-start | bytes 1572872 | tf_op jit(solution)/shard_map/ppermute | solution.py:780
  175.0 18.4 %collective-permute-start.43 = (bf16[128,512]{1,0:T(8,128)(2,1)S(1)}, bf16[128,512]{1,0:T(8,128)(2,1)S(1)}, u32[]{:S(2)}, u32[]{:S(2)}) collective-permute-start(bf16[128,512]{1,0:T(8,128)(2,1)S(1)} %multiply_convert_fusion.3.refs_0_), channel_id=1, source_target_pairs={{0,3},{1,0},{2,1},{3,2},{4,7},{5,4},{6,5},{7,6},{8,11},{9,8},{10,9... | collective-permute-start | bytes 393224 | tf_op jit(solution)/shard_map/ppermute | solution.py:690
  175.4 18.0 %collective-permute-start.42 = (bf16[128,512]{1,0:T(8,128)(2,1)S(1)}, bf16[128,512]{1,0:T(8,128)(2,1)S(1)}, u32[]{:S(2)}, u32[]{:S(2)}) collective-permute-start(bf16[128,512]{1,0:T(8,128)(2,1)S(1)} %multiply_convert_fusion.3.refs_0_), channel_id=1, source_target_pairs={{0,2},{1,3},{2,0},{3,1},{4,6},{5,7},{6,4},{7,5},{8,10},{9,11},{10,... | collective-permute-start | bytes 393224 | tf_op jit(solution)/shard_map/ppermute | solution.py:690
  176.5 18.5 %collective-permute-start.41 = (bf16[128,512]{1,0:T(8,128)(2,1)S(1)}, bf16[128,512]{1,0:T(8,128)(2,1)S(1)}, u32[]{:S(2)}, u32[]{:S(2)}) collective-permute-start(bf16[128,512]{1,0:T(8,128)(2,1)S(1)} %multiply_convert_fusion.3.refs_0_), channel_id=1, source_target_pairs={{0,1},{1,2},{2,3},{3,0},{4,5},{5,6},{6,7},{7,4},{8,9},{9,10},{10,1... | collective-permute-start | bytes 393224 | tf_op jit(solution)/shard_map/ppermute | solution.py:690
  197.3 2.4 %collective-permute-start.44 = (bf16[4,208,512]{2,1,0:T(8,128)(2,1)S(1)}, bf16[4,208,512]{2,1,0:T(8,128)(2,1)S(1)}, u32[]{:S(2)}, u32[]{:S(2)}) collective-permute-start(bf16[4,208,512]{2,1,0:T(8,128)(2,1)S(1)} %get-tuple-element.130), channel_id=1, source_target_pairs={{0,4},{4,0},{8,12},{12,8},{16,20},{20,16},{24,28},{28,24},{1,5},{5... | collective-permute-start | bytes 2555912 | tf_op jit(solution)/shard_map/ppermute | solution.py:707
  199.8 8.2 %collective-permute-start.45 = (bf16[208,512]{1,0:T(8,128)(2,1)S(1)}, bf16[208,512]{1,0:T(8,128)(2,1)S(1)}, u32[]{:S(2)}, u32[]{:S(2)}) collective-permute-start(bf16[208,512]{1,0:T(8,128)(2,1)S(1)} %get-tuple-element.132), channel_id=1, source_target_pairs={{0,8},{4,12},{8,0},{12,4},{16,24},{20,28},{24,16},{28,20},{1,9},{5... | collective-permute-start | bytes 638984 | tf_op jit(solution)/shard_map/ppermute | solution.py:699
  199.9 11.9 %collective-permute-start.46 = (bf16[208,512]{1,0:T(8,128)(2,1)S(1)}, bf16[208,512]{1,0:T(8,128)(2,1)S(1)}, u32[]{:S(2)}, u32[]{:S(2)}) collective-permute-start(bf16[208,512]{1,0:T(8,128)(2,1)S(1)} %get-tuple-element.133), channel_id=1, source_target_pairs={{0,16},{4,20},{8,24},{12,28},{16,0},{20,4},{24,8},{28,12},{1,17},{... | collective-permute-start | bytes 638984 | tf_op jit(solution)/shard_map/ppermute | solution.py:699
  201.1 10.7 %collective-permute-start.47 = (bf16[208,512]{1,0:T(8,128)(2,1)S(1)}, bf16[208,512]{1,0:T(8,128)(2,1)S(1)}, u32[]{:S(2)}, u32[]{:S(2)}) collective-permute-start(bf16[208,512]{1,0:T(8,128)(2,1)S(1)} %get-tuple-element.134), channel_id=1, source_target_pairs={{0,24},{4,28},{8,16},{12,20},{16,8},{20,12},{24,0},{28,4},{1,25},{... | collective-permute-start | bytes 638984 | tf_op jit(solution)/shard_map/ppermute | solution.py:699
  203.5 25.3 %collective-permute-start.49 = (bf16[512,512]{1,0:T(8,128)(2,1)S(1)}, bf16[512,512]{1,0:T(8,128)(2,1)S(1)}, u32[]{:S(2)}, u32[]{:S(2)}) collective-permute-start(bf16[512,512]{1,0:T(8,128)(2,1)S(1)} %add_convert_fusion.1), channel_id=1, source_target_pairs={{0,2},{1,3},{2,0},{3,1},{4,6},{5,7},{6,4},{7,5},{8,10},{9,11},{10,... | collective-permute-start | bytes 1572872 | tf_op jit(solution)/shard_map/ppermute | solution.py:780
  204.6 24.3 %collective-permute-start.40 = (bf16[512,512]{1,0:T(8,128)(2,1)S(1)}, bf16[512,512]{1,0:T(8,128)(2,1)S(1)}, u32[]{:S(2)}, u32[]{:S(2)}) collective-permute-start(bf16[512,512]{1,0:T(8,128)(2,1)S(1)} %get-tuple-element.127), channel_id=1, source_target_pairs={{0,1},{1,0},{2,3},{3,2},{4,5},{5,4},{6,7},{7,6},{8,9},{9,8},{10,11... | collective-permute-start | bytes 1572872 | tf_op jit(solution)/shard_map/ppermute | solution.py:780
  212.0 16.9 %collective-permute-start.48 = (bf16[208,512]{1,0:T(8,128)(2,1)S(1)}, bf16[208,512]{1,0:T(8,128)(2,1)S(1)}, u32[]{:S(2)}, u32[]{:S(2)}) collective-permute-start(bf16[208,512]{1,0:T(8,128)(2,1)S(1)} %add_convert_fusion.2.refs_0_), channel_id=1, source_target_pairs={{0,24},{4,28},{8,16},{12,20},{16,8},{20,12},{24,0},{28,4},{1,25},{... | collective-permute-start | bytes 638984 | tf_op jit(solution)/shard_map/ppermute | solution.py:699
  213.5 15.9 %collective-permute-start.51 = (bf16[208,512]{1,0:T(8,128)(2,1)S(1)}, bf16[208,512]{1,0:T(8,128)(2,1)S(1)}, u32[]{:S(2)}, u32[]{:S(2)}) collective-permute-start(bf16[208,512]{1,0:T(8,128)(2,1)S(1)} %add_convert_fusion.2.refs_0_), channel_id=1, source_target_pairs={{0,16},{4,20},{8,24},{12,28},{16,0},{20,4},{24,8},{28,12},{1,17},{... | collective-permute-start | bytes 638984 | tf_op jit(solution)/shard_map/ppermute | solution.py:699
  215.2 14.3 %collective-permute-start.50 = (bf16[208,512]{1,0:T(8,128)(2,1)S(1)}, bf16[208,512]{1,0:T(8,128)(2,1)S(1)}, u32[]{:S(2)}, u32[]{:S(2)}) collective-permute-start(bf16[208,512]{1,0:T(8,128)(2,1)S(1)} %add_convert_fusion.2.refs_0_), channel_id=1, source_target_pairs={{0,8},{4,12},{8,0},{12,4},{16,24},{20,28},{24,16},{28,20},{1,9},{5... | collective-permute-start | bytes 638984 | tf_op jit(solution)/shard_map/ppermute | solution.py:699
  228.9 2.1 collective-permute-start.52
  228.9 2.4 %collective-permute-start.55 = (bf16[208,512]{1,0:T(8,128)(2,1)S(1)}, bf16[208,512]{1,0:T(8,128)(2,1)S(1)}, u32[]{:S(2)}, u32[]{:S(2)}) collective-permute-start(bf16[208,512]{1,0:T(8,128)(2,1)S(1)} %collective-permute-done.48.refs_3_), channel_id=1, source_target_pairs={{0,4},{4,0},{8,12},{12,8},{16,20},{20,16},{24,28},{28,24},{1,5},{5... | collective-permute-start | bytes 638984 | tf_op jit(solution)/shard_map/ppermute | solution.py:707
  229.4 1.6 collective-permute-start.54
  229.5 1.8 collective-permute-start.53
  (7 other events, 45.9 us)

commit v8 on v7

--- a/solution.py
+++ b/solution.py
@@ -547,24 +547,25 @@
             out[...] = result
 
 
-def down_call(info, hidden, w_down, ring):
+def down_call(info, hidden, w_down, ring, first_flip, last_flip):
     rows, units = hidden.shape
     depth = w_down.shape[1]
     width = depth // ring
+    count = first_flip - last_flip + 1
     return pl.pallas_call(
         down_kernel,
-        out_shape=[jax.ShapeDtypeStruct((rows, width), BF16)] * ring,
+        out_shape=[jax.ShapeDtypeStruct((rows, width), BF16)] * count,
         grid_spec=pltpu.PrefetchScalarGridSpec(
             num_scalar_prefetch=1,
-            grid=(ring,),
+            grid=(count,),
             in_specs=[
                 whole((rows, units)),
-                pl.BlockSpec((units, width), lambda j, info: (0, info[ring] ^ (ring - 1 - j))),
+                pl.BlockSpec((units, width), lambda j, info: (0, info[ring] ^ (first_flip - j))),
             ],
-            out_specs=[whole((rows, width))] * ring,
+            out_specs=[whole((rows, width))] * count,
         ),
         compiler_params=params(24),
-        cost_estimate=cost(2 * rows * units * depth, 2 * units * depth),
+        cost_estimate=cost(2 * rows * units * width * count, 2 * units * width * count),
         name="down",
     )(info, hidden, w_down)
 
@@ -815,13 +816,13 @@
         student_part,
     )
 
-    far_theirs, far_mine, near_theirs, kept = down_call(info, hidden, w_down, ring)
+    far_sum = over(down_call(info, hidden, w_down, ring, 3, 3)[0], 1)
+    far_mine, near_theirs, kept = down_call(info, hidden, w_down, ring, 2, 0)
 
     moved = lax.optimization_barrier((*shifted(pieces, "tensor"), kept))[:ring]
     difference = student_own + sum(piece.astype(F32) for piece in moved)
     own = (difference * total_rows ** (-0.5)).astype(BF16)
     scaled = shifted([own] * ring, "tensor")
-    far_sum = over(after(far_theirs, own), 1)
 
     keep, give = grads_call(
         after(info, far_sum),

time: 238 us -> 232 us (0.975); the launches traced: 236 us -> 233 us
  waiting for transfers between devices: 121 us -> 118 us
    ppermute x6, waiting for transfers between devices: 26.3 us -> 21.6 us  [paired(): lax.ppermute(value, 'tensor', [(i, i ^ bit) for i in range(ring)])]
    pallas_call x1 -> x2, Pallas kernels: 6.54 us -> 6.81 us  [down_call(): pl.pallas_call(down_kernel, out_shape=[jax.ShapeDtypeStruct((rows, width)...]
  transfers between devices with their start and end apart: 56 -> 56, of which waited for: 30 -> 31; matrix products, arithmetic and copies ran while one was open for 6% -> 6% of each run, Pallas kernels for 6% -> 6%
where the time goes in v8:
time: 232 us; the launch traced here: 233 us
  waiting for transfers between devices  118 us (51%)
  Pallas kernels  48 us (21%)
  starting transfers between devices  45.1 us (19%)
  matrix products  7.36 us (3%)
  other arithmetic  6.13 us (3%)
  local copies, waits for them, and re-layouts  5.94 us (3%)
  between operations  2.81 us (1%)
    ppermute x12, waiting for transfers between devices, step_on(): return lax.ppermute(block, axis, [(i, (i + 1) % size) for i in range(size)])  63.3 us
    pallas_call x1, Pallas kernels, middle_call(): pl.pallas_call(functools.partial(middle_kernel, ring=ring, chips=chips),...  22.1 us
    ppermute x18, waiting for transfers between devices, flipped(): lax.ppermute(pieces[f], 'dp', [(i, i ^ 2 * f) for i in range(size)])  21.8 us
    ppermute x18, starting transfers between devices, flipped(): lax.ppermute(pieces[f], 'dp', [(i, i ^ 2 * f) for i in range(size)])  21.7 us
    ppermute x6, waiting for transfers between devices, paired(): lax.ppermute(value, 'tensor', [(i, i ^ bit) for i in range(ring)])  21.6 us
    pallas_call x1, Pallas kernels, attention_call(): pl.pallas_call(functools.partial(attention_kernel, chips=chips, ring=ring...  7.96 us
    ppermute x6, starting transfers between devices, shifted(): lax.ppermute(pieces[s], axis, [(i, (i + s) % size) for i in range(size)])  7.96 us
    dot_general x4, matrix products, dot(): return jnp.dot(a, b, preferred_element_type=F32)  7.36 us
  transfers between devices with their start and end apart: 56, of which 31 were waited for; matrix products, arithmetic and copies ran while one was open for 6% of the time, Pallas kernels for 6%

profile of v8, /device:TPU:0, one launch (start us, length us, event | category | flops | bytes accessed | tf_op | source)
XLA Modules:
  0.0 232.9 jit_solution(16082025396855630658)
XLA Ops:
  0.7 1.1 fusion.10
  1.8 3.1 %collective-permute-start.3 = (bf16[256,512]{1,0:T(8,128)(2,1)S(1)}, bf16[256,512]{1,0:T(8,128)(2,1)S(1)}, u32[]{:S(2)}, u32[]{:S(2)}) collective-permute-start(bf16[256,512]{1,0:T(8,128)(2,1)S(1)} %get-tuple-element.140.refs_4_), channel_id=1, source_target_pairs={{0,1},{1,2},{2,3},{3,0},{4,5},{5,6},{6,7},{7,4},{8,9},{9,10},{10,1... | collective-permute-start | bytes 786440 | tf_op jit(solution)/shard_map/ppermute | solution.py:678
  4.9 1.6 collective-permute-start
  7.2 1.0 fusion.3
  8.6 5.5 %collective-permute-done.3.refs_5_ = bf16[256,512]{1,0:T(8,128)(2,1)S(1)} collective-permute-done((bf16[256,512]{1,0:T(8,128)(2,1)S(1)}, bf16[256,512]{1,0:T(8,128)(2,1)S(1)}, u32[]{:S(2)}, u32[]{:S(2)}) %collective-permute-start.3) | collective-permute-done | bytes 262176 | tf_op jit(solution)/shard_map/ppermute | solution.py:678
  14.1 5.6 %collective-permute-done.refs_1_ = bf16[256,512]{1,0:T(8,128)(2,1)S(1)} collective-permute-done((bf16[256,512]{1,0:T(8,128)(2,1)S(1)}, bf16[256,512]{1,0:T(8,128)(2,1)S(1)}, u32[]{:S(2)}, u32[]{:S(2)}) %collective-permute-start) | collective-permute-done | bytes 262176 | tf_op jit(solution)/shard_map/ppermute | solution.py:678
  19.7 1.1 constant_dynamic-slice_fusion.1
  20.9 1.1 convert_element_type.98
  22.0 3.3 %collective-permute-done.4.refs_6_ = bf16[256,512]{1,0:T(8,128)(2,1)S(1)} collective-permute-done((bf16[256,512]{1,0:T(8,128)(2,1)S(1)}, bf16[256,512]{1,0:T(8,128)(2,1)S(1)}, u32[]{:S(2)}, u32[]{:S(2)}) %collective-permute-start.4) | collective-permute-done | bytes 262176 | tf_op jit(solution)/shard_map/ppermute | solution.py:678
  25.3 5.6 %collective-permute-done.1.refs_2_ = bf16[256,512]{1,0:T(8,128)(2,1)S(1)} collective-permute-done((bf16[256,512]{1,0:T(8,128)(2,1)S(1)}, bf16[256,512]{1,0:T(8,128)(2,1)S(1)}, u32[]{:S(2)}, u32[]{:S(2)}) %collective-permute-start.1) | collective-permute-done | bytes 262176 | tf_op jit(solution)/shard_map/ppermute | solution.py:678
  31.1 5.4 %collective-permute-done.5.refs_7_ = bf16[256,512]{1,0:T(8,128)(2,1)S(1)} collective-permute-done((bf16[256,512]{1,0:T(8,128)(2,1)S(1)}, bf16[256,512]{1,0:T(8,128)(2,1)S(1)}, u32[]{:S(2)}, u32[]{:S(2)}) %collective-permute-start.5) | collective-permute-done | bytes 262176 | tf_op jit(solution)/shard_map/ppermute | solution.py:678
  36.5 4.8 %collective-permute-done.2.refs_3_ = bf16[256,512]{1,0:T(8,128)(2,1)S(1)} collective-permute-done((bf16[256,512]{1,0:T(8,128)(2,1)S(1)}, bf16[256,512]{1,0:T(8,128)(2,1)S(1)}, u32[]{:S(2)}, u32[]{:S(2)}) %collective-permute-start.2) | collective-permute-done | bytes 262176 | tf_op jit(solution)/shard_map/ppermute | solution.py:678
  41.4 6.3 %qkv.1 = (bf16[3,512,128]{2,1,0:T(8,128)(2,1)S(1)}, bf16[3,512,128]{2,1,0:T(8,128)(2,1)S(1)}, bf16[3,512,128]{2,1,0:T(8,128)(2,1)S(1)}, bf16[3,512,128]{2,1,0:T(8,128)(2,1)S(1)}, bf16[512,2048]{1,0:T(8,128)(2,1)S(1)}) custom-call(s32[16]{0:T(128)S(1)} %fusion.9.info_ref, bf16[256,512]{1,0:T(8,128)(2,1)S(1)} %get-tuple-element.141.refs_0_, ...), custom_call_target="tpu_custom_call" | custom-call | flops 3221225472 | bytes 6291456 | tf_op jit(solution)/shard_map/qkv/pallas_call | solution.py:231
  47.7 1.3 copy-done.8
  49.8 1.6 collective-permute-start.9
  51.3 1.5 collective-permute-start.6
  52.8 1.5 collective-permute-start.7
  55.3 5.6 %fusion.refs_26_ = bf16[2048,512]{1,0:T(8,128)(2,1)} fusion(bf16[2048,2048]{1,0:T(8,128)(2,1)S(1)} %bitcast.27, bf16[2048,512]{1,0:T(8,128)(2,1)S(1)} %copy-done.12), kind=kOutput, calls=%fused_computation.1 | convolution fusion | flops 4296015872 | bytes 12582912 | tf_op jit(solution)/shard_map/dot_general | solution.py:166
  61.0 0.8 multiply_convert_fusion
  62.5 0.9 collective-permute-done.6.refs_1_
  63.4 7.0 %collective-permute-done.7.refs_2_ = bf16[3,512,128]{2,1,0:T(8,128)(2,1)S(1)} collective-permute-done((bf16[3,512,128]{2,1,0:T(8,128)(2,1)S(1)}, bf16[3,512,128]{2,1,0:T(8,128)(2,1)S(1)}, u32[]{:S(2)}, u32[]{:S(2)}) %collective-permute-start.7) | collective-permute-done | bytes 393248 | tf_op jit(solution)/shard_map/ppermute | solution.py:700
  71.4 1.5 collective-permute-start.18
  72.9 1.2 collective-permute-start.17
  75.5 8.0 %attention.1 = (bf16[512,128]{1,0:T(8,128)(2,1)S(1)}, bf16[512,128]{1,0:T(8,128)(2,1)S(1)}, bf16[512,128]{1,0:T(8,128)(2,1)S(1)}, bf16[512,128]{1,0:T(8,128)(2,1)S(1)}) custom-call(s32[8]{0:T(128)S(1)} %convert_reduce_fusion.first_ref, s32[16]{0:T(128)S(1)} %fusion.9.info_ref, bf16[3,512,128]{2,1,0:T(8,128)(2,1)S(1)} %get-tuple-element.84.refs_0_, ...), custom_call_target="tpu_custom_call" | custom-call | flops 2147483648 | bytes 4194304 | tf_op jit(solution)/shard_map/attention/pallas_call | solution.py:337
  83.5 2.7 %collective-permute-done.17.refs_12_ = bf16[512,256]{1,0:T(8,128)(2,1)S(1)} collective-permute-done((bf16[512,256]{1,0:T(8,128)(2,1)S(1)}, bf16[512,256]{1,0:T(8,128)(2,1)S(1)}, u32[]{:S(2)}, u32[]{:S(2)}) %collective-permute-start.17) | collective-permute-done | bytes 262176 | tf_op jit(solution)/shard_map/ppermute | solution.py:700
  86.3 1.1 collective-permute-start.19
  88.2 1.5 collective-permute-start.21
  89.8 2.5 %collective-permute-done.19 = bf16[512,128]{1,0:T(8,128)(2,1)S(1)} collective-permute-done((bf16[512,128]{1,0:T(8,128)(2,1)S(1)}, bf16[512,128]{1,0:T(8,128)(2,1)S(1)}, u32[]{:S(2)}, u32[]{:S(2)}) %collective-permute-start.19) | collective-permute-done | bytes 131104 | tf_op jit(solution)/shard_map/ppermute | solution.py:700
  92.2 1.5 collective-permute-done.20
  93.7 1.6 collective-permute-done.21
  95.9 1.1 collective-permute-start.25
  97.1 1.8 collective-permute-start.30
  98.9 7.6 %collective-permute-done.22.refs_1_ = bf16[2,512,128]{2,1,0:T(8,128)(2,1)S(1)} collective-permute-done((bf16[2,512,128]{2,1,0:T(8,128)(2,1)S(1)}, bf16[2,512,128]{2,1,0:T(8,128)(2,1)S(1)}, u32[]{:S(2)}, u32[]{:S(2)}) %collective-permute-start.22) | collective-permute-done | bytes 262176 | tf_op jit(solution)/shard_map/ppermute | solution.py:678
  106.5 0.8 collective-permute-start.29
  107.3 1.5 collective-permute-start.28
  108.8 3.3 %collective-permute-done.25.refs_5_ = bf16[2,512,128]{2,1,0:T(8,128)(2,1)S(1)} collective-permute-done((bf16[2,512,128]{2,1,0:T(8,128)(2,1)S(1)}, bf16[2,512,128]{2,1,0:T(8,128)(2,1)S(1)}, u32[]{:S(2)}, u32[]{:S(2)}) %collective-permute-start.25) | collective-permute-done | bytes 262176 | tf_op jit(solution)/shard_map/ppermute | solution.py:678
  112.2 5.5 %collective-permute-done.23.refs_2_ = bf16[2,512,128]{2,1,0:T(8,128)(2,1)S(1)} collective-permute-done((bf16[2,512,128]{2,1,0:T(8,128)(2,1)S(1)}, bf16[2,512,128]{2,1,0:T(8,128)(2,1)S(1)}, u32[]{:S(2)}, u32[]{:S(2)}) %collective-permute-start.23) | collective-permute-done | bytes 262176 | tf_op jit(solution)/shard_map/ppermute | solution.py:678
  117.7 3.7 %collective-permute-done.26.refs_6_ = bf16[2,512,128]{2,1,0:T(8,128)(2,1)S(1)} collective-permute-done((bf16[2,512,128]{2,1,0:T(8,128)(2,1)S(1)}, bf16[2,512,128]{2,1,0:T(8,128)(2,1)S(1)}, u32[]{:S(2)}, u32[]{:S(2)}) %collective-permute-start.26) | collective-permute-done | bytes 262176 | tf_op jit(solution)/shard_map/ppermute | solution.py:678
  122.2 10.2 %collective-permute-done.24.refs_3_ = bf16[2,512,128]{2,1,0:T(8,128)(2,1)S(1)} collective-permute-done((bf16[2,512,128]{2,1,0:T(8,128)(2,1)S(1)}, bf16[2,512,128]{2,1,0:T(8,128)(2,1)S(1)}, u32[]{:S(2)}, u32[]{:S(2)}) %collective-permute-start.24) | collective-permute-done | bytes 262176 | tf_op jit(solution)/shard_map/ppermute | solution.py:678
  132.5 2.8 %collective-permute-done.27.refs_7_ = bf16[2,512,128]{2,1,0:T(8,128)(2,1)S(1)} collective-permute-done((bf16[2,512,128]{2,1,0:T(8,128)(2,1)S(1)}, bf16[2,512,128]{2,1,0:T(8,128)(2,1)S(1)}, u32[]{:S(2)}, u32[]{:S(2)}) %collective-permute-start.27) | collective-permute-done | bytes 262176 | tf_op jit(solution)/shard_map/ppermute | solution.py:678
  135.3 1.9 collective-permute-done.33.refs_20_
  137.2 22.1 %middle.1 = (bf16[512,2048]{1,0:T(8,128)(2,1)}, bf16[512,512]{1,0:T(8,128)(2,1)S(1)}, bf16[128,512]{1,0:T(8,128)(2,1)S(1)}, bf16[128,512]{1,0:T(8,128)(2,1)S(1)}...) custom-call(s32[16]{0:T(128)S(1)} %fusion.9.info_ref, bf16[2,512,128]{2,1,0:T(8,128)(2,1)S(1)} %pad_maximum_fusion.3.refs_0_, ...), custom_call_target="tpu_custom_call" | custom-call | flops 14227079168 | bytes 25165824 | tf_op jit(solution)/shard_map/middle/pallas_call | solution.py:481
  159.5 3.7 %collective-permute-start.40 = (bf16[128,512]{1,0:T(8,128)(2,1)S(1)}, bf16[128,512]{1,0:T(8,128)(2,1)S(1)}, u32[]{:S(2)}, u32[]{:S(2)}) collective-permute-start(bf16[128,512]{1,0:T(8,128)(2,1)S(1)} %get-tuple-element.120), channel_id=1, source_target_pairs={{0,3},{1,0},{2,1},{3,2},{4,7},{5,4},{6,5},{7,6},{8,11},{9,8},{10,9... | collective-permute-start | bytes 393224 | tf_op jit(solution)/shard_map/ppermute | solution.py:691
  163.2 1.6 copy-done.2
  164.8 1.8 down.3
  167.2 5.0 %down.2 = (bf16[512,512]{1,0:T(8,128)(2,1)S(1)}, bf16[512,512]{1,0:T(8,128)(2,1)S(1)}, bf16[512,512]{1,0:T(8,128)(2,1)S(1)}) custom-call(s32[16]{0:T(128)S(1)} %fusion.9.info_ref, bf16[512,2048]{1,0:T(8,128)(2,1)S(1)} %copy-done.2, bf16[2048,2048]{1,0:T(8,128)(2,1)S(1)} %bitcast.27), custom_call_target="tpu_custom_call" | custom-call | flops 3221225472 | bytes 6291456 | tf_op jit(solution)/shard_map/down/pallas_call | solution.py:555
  172.3 1.1 multiply_convert_fusion.3.refs_0_
  173.4 2.9 %collective-permute-start.43 = (bf16[128,512]{1,0:T(8,128)(2,1)S(1)}, bf16[128,512]{1,0:T(8,128)(2,1)S(1)}, u32[]{:S(2)}, u32[]{:S(2)}) collective-permute-start(bf16[128,512]{1,0:T(8,128)(2,1)S(1)} %multiply_convert_fusion.3.refs_0_), channel_id=1, source_target_pairs={{0,3},{1,0},{2,1},{3,2},{4,7},{5,4},{6,5},{7,6},{8,11},{9,8},{10,9... | collective-permute-start | bytes 393224 | tf_op jit(solution)/shard_map/ppermute | solution.py:691
  176.3 1.2 collective-permute-start.42
  177.5 8.1 %collective-permute-done.36 = bf16[512,512]{1,0:T(8,128)(2,1)S(1)} collective-permute-done((bf16[512,512]{1,0:T(8,128)(2,1)S(1)}, bf16[512,512]{1,0:T(8,128)(2,1)S(1)}, u32[]{:S(2)}, u32[]{:S(2)}) %collective-permute-start.36) | collective-permute-done | bytes 524320 | tf_op jit(solution)/shard_map/ppermute | solution.py:781
  185.6 2.7 %collective-permute-done.43.refs_3_ = bf16[128,512]{1,0:T(8,128)(2,1)S(1)} collective-permute-done((bf16[128,512]{1,0:T(8,128)(2,1)S(1)}, bf16[128,512]{1,0:T(8,128)(2,1)S(1)}, u32[]{:S(2)}, u32[]{:S(2)}) %collective-permute-start.43) | collective-permute-done | bytes 131104 | tf_op jit(solution)/shard_map/ppermute | solution.py:691
  188.3 3.7 %collective-permute-done.41.refs_1_ = bf16[128,512]{1,0:T(8,128)(2,1)S(1)} collective-permute-done((bf16[128,512]{1,0:T(8,128)(2,1)S(1)}, bf16[128,512]{1,0:T(8,128)(2,1)S(1)}, u32[]{:S(2)}, u32[]{:S(2)}) %collective-permute-start.41) | collective-permute-done | bytes 131104 | tf_op jit(solution)/shard_map/ppermute | solution.py:691
  192.0 2.2 grads.1
  194.4 2.4 %collective-permute-done.44.theirs_ref = bf16[4,208,512]{2,1,0:T(8,128)(2,1)S(1)} collective-permute-done((bf16[4,208,512]{2,1,0:T(8,128)(2,1)S(1)}, bf16[4,208,512]{2,1,0:T(8,128)(2,1)S(1)}, u32[]{:S(2)}, u32[]{:S(2)}) %collective-permute-start.44) | collective-permute-done | bytes 852000 | tf_op jit(solution)/shard_map/ppermute | solution.py:708
  197.0 1.2 collective-permute-start.46
  198.2 2.3 collective-permute-start.47
  201.2 2.5 %collective-permute-start.37 = (bf16[512,512]{1,0:T(8,128)(2,1)S(1)}, bf16[512,512]{1,0:T(8,128)(2,1)S(1)}, u32[]{:S(2)}, u32[]{:S(2)}) collective-permute-start(bf16[512,512]{1,0:T(8,128)(2,1)S(1)} %get-tuple-element.115), channel_id=1, source_target_pairs={{0,1},{1,0},{2,3},{3,2},{4,5},{5,4},{6,7},{7,6},{8,9},{9,8},{10,11... | collective-permute-start | bytes 1572872 | tf_op jit(solution)/shard_map/ppermute | solution.py:781
  203.7 1.3 collective-permute-done.45
  205.1 3.8 %collective-permute-done.46 = bf16[208,512]{1,0:T(8,128)(2,1)S(1)} collective-permute-done((bf16[208,512]{1,0:T(8,128)(2,1)S(1)}, bf16[208,512]{1,0:T(8,128)(2,1)S(1)}, u32[]{:S(2)}, u32[]{:S(2)}) %collective-permute-start.46) | collective-permute-done | bytes 213024 | tf_op jit(solution)/shard_map/ppermute | solution.py:700
  209.0 1.6 collective-permute-start.48
  210.6 1.6 collective-permute-start.51
  212.6 13.3 %collective-permute-done.49 = bf16[512,512]{1,0:T(8,128)(2,1)S(1)} collective-permute-done((bf16[512,512]{1,0:T(8,128)(2,1)S(1)}, bf16[512,512]{1,0:T(8,128)(2,1)S(1)}, u32[]{:S(2)}, u32[]{:S(2)}) %collective-permute-start.49) | collective-permute-done | bytes 524320 | tf_op jit(solution)/shard_map/ppermute | solution.py:781
  226.9 1.1 add_convert_fusion
  228.3 2.4 %finish.1 = (f32[512,512]{1,0:T(8,128)}, f32[512,512]{1,0:T(8,128)}, f32[512,512]{1,0:T(8,128)}, f32[8,16,128]{2,1,0:T(8,128)S(1)}) custom-call(s32[16]{0:T(128)S(1)} %fusion.9.info_ref, bf16[208,512]{1,0:T(8,128)(2,1)S(1)} %add_convert_fusion.2.refs_0_, bf16[208,512]{1,0:T(8,128)(2,1)S(1)} %collective-permute-done.50.refs_1_, ...), custom_call_target="tpu_custom_call" | custom-call | flops 262144 | bytes 3145728 | tf_op jit(solution)/shard_map/finish/pallas_call | solution.py:660
  (112 shorter events, 12.8 us)
Async XLA Ops:
  0.6 60.3 %copy-start = (bf16[512,512]{1,0:T(8,128)(2,1)S(1)}, bf16[512,512]{1,0:T(8,128)(2,1)}, u32[]{:S(2)}) copy-start(bf16[512,512]{1,0:T(8,128)(2,1)} %param.31) | copy-start | bytes 1572868
  1.8 12.2 %collective-permute-start.3 = (bf16[256,512]{1,0:T(8,128)(2,1)S(1)}, bf16[256,512]{1,0:T(8,128)(2,1)S(1)}, u32[]{:S(2)}, u32[]{:S(2)}) collective-permute-start(bf16[256,512]{1,0:T(8,128)(2,1)S(1)} %get-tuple-element.140.refs_4_), channel_id=1, source_target_pairs={{0,1},{1,2},{2,3},{3,0},{4,5},{5,6},{6,7},{7,4},{8,9},{9,10},{10,1... | collective-permute-start | bytes 786440 | tf_op jit(solution)/shard_map/ppermute | solution.py:678
  4.9 14.8 %collective-permute-start = (bf16[256,512]{1,0:T(8,128)(2,1)S(1)}, bf16[256,512]{1,0:T(8,128)(2,1)S(1)}, u32[]{:S(2)}, u32[]{:S(2)}) collective-permute-start(bf16[256,512]{1,0:T(8,128)(2,1)S(1)} %get-tuple-element.141.refs_0_), channel_id=1, source_target_pairs={{0,1},{1,2},{2,3},{3,0},{4,5},{5,6},{6,7},{7,4},{8,9},{9,10},{10,1... | collective-permute-start | bytes 786440 | tf_op jit(solution)/shard_map/ppermute | solution.py:678
  8.2 33.2 %copy-start.5 = (bf16[2048,512]{1,0:T(8,128)(2,1)S(1)}, bf16[2048,512]{1,0:T(8,128)(2,1)}, u32[]{:S(2)}) copy-start(bf16[2048,512]{1,0:T(8,128)(2,1)} %refs_12_.1) | copy-start | bytes 6291460
  8.4 32.9 %copy-start.4 = (bf16[2048,512]{1,0:T(8,128)(2,1)S(1)}, bf16[2048,512]{1,0:T(8,128)(2,1)}, u32[]{:S(2)}) copy-start(bf16[2048,512]{1,0:T(8,128)(2,1)} %refs_11_.1) | copy-start | bytes 6291460
  8.4 32.9 %copy-start.6 = (f32[2048]{0:T(1024)S(1)}, f32[2048]{0:T(1024)}, u32[]{:S(2)}) copy-start(f32[2048]{0:T(1024)} %param.20) | copy-start | bytes 24580
  14.1 11.2 %collective-permute-start.4 = (bf16[256,512]{1,0:T(8,128)(2,1)S(1)}, bf16[256,512]{1,0:T(8,128)(2,1)S(1)}, u32[]{:S(2)}, u32[]{:S(2)}) collective-permute-start(bf16[256,512]{1,0:T(8,128)(2,1)S(1)} %collective-permute-done.3.refs_5_), channel_id=1, source_target_pairs={{0,1},{1,2},{2,3},{3,0},{4,5},{5,6},{6,7},{7,4},{8,9},{9,10},{10,1... | collective-permute-start | bytes 786440 | tf_op jit(solution)/shard_map/ppermute | solution.py:678
  19.7 11.2 %collective-permute-start.1 = (bf16[256,512]{1,0:T(8,128)(2,1)S(1)}, bf16[256,512]{1,0:T(8,128)(2,1)S(1)}, u32[]{:S(2)}, u32[]{:S(2)}) collective-permute-start(bf16[256,512]{1,0:T(8,128)(2,1)S(1)} %collective-permute-done.refs_1_), channel_id=1, source_target_pairs={{0,1},{1,2},{2,3},{3,0},{4,5},{5,6},{6,7},{7,4},{8,9},{9,10},{10,1... | collective-permute-start | bytes 786440 | tf_op jit(solution)/shard_map/ppermute | solution.py:678
  20.9 34.4 %slice-start = ((s8[8388608]{0:T(1024)(128)(4,1)}), s8[4194304]{0:T(1024)(128)(4,1)S(1)}, s32[]{:S(2)}) async-start(s8[8388608]{0:T(1024)(128)(4,1)} %bitcast.26), calls=%async_computation | async-start | bytes 8388608
  25.3 11.2 %collective-permute-start.5 = (bf16[256,512]{1,0:T(8,128)(2,1)S(1)}, bf16[256,512]{1,0:T(8,128)(2,1)S(1)}, u32[]{:S(2)}, u32[]{:S(2)}) collective-permute-start(bf16[256,512]{1,0:T(8,128)(2,1)S(1)} %collective-permute-done.4.refs_6_), channel_id=1, source_target_pairs={{0,1},{1,2},{2,3},{3,0},{4,5},{5,6},{6,7},{7,4},{8,9},{9,10},{10,1... | collective-permute-start | bytes 786440 | tf_op jit(solution)/shard_map/ppermute | solution.py:678
  30.9 10.4 %collective-permute-start.2 = (bf16[256,512]{1,0:T(8,128)(2,1)S(1)}, bf16[256,512]{1,0:T(8,128)(2,1)S(1)}, u32[]{:S(2)}, u32[]{:S(2)}) collective-permute-start(bf16[256,512]{1,0:T(8,128)(2,1)S(1)} %collective-permute-done.1.refs_2_), channel_id=1, source_target_pairs={{0,1},{1,2},{2,3},{3,0},{4,5},{5,6},{6,7},{7,4},{8,9},{9,10},{10,1... | collective-permute-start | bytes 786440 | tf_op jit(solution)/shard_map/ppermute | solution.py:678
  41.4 13.9 %slice-start.1 = ((s8[8388608]{0:T(1024)(128)(4,1)}), s8[4194304]{0:T(1024)(128)(4,1)S(1)}, s32[]{:S(2)}) async-start(s8[8388608]{0:T(1024)(128)(4,1)} %bitcast.26), calls=%async_computation.1 | async-start | bytes 8388608
  49.0 13.4 %collective-permute-start.10 = (bf16[512,256]{1,0:T(8,128)(2,1)S(1)}, bf16[512,256]{1,0:T(8,128)(2,1)S(1)}, u32[]{:S(2)}, u32[]{:S(2)}) collective-permute-start(bf16[512,256]{1,0:T(8,128)(2,1)S(1)} %constant_dynamic-slice_fusion.1), channel_id=1, source_target_pairs={{0,2},{1,3},{2,0},{3,1},{4,6},{5,7},{6,4},{7,5},{8,10},{9,11},{10,... | collective-permute-start | bytes 786440 | tf_op jit(solution)/shard_map/ppermute | solution.py:781
  49.8 12.7 %collective-permute-start.9 = (bf16[512,256]{1,0:T(8,128)(2,1)S(1)}, bf16[512,256]{1,0:T(8,128)(2,1)S(1)}, u32[]{:S(2)}, u32[]{:S(2)}) collective-permute-start(bf16[512,256]{1,0:T(8,128)(2,1)S(1)} %constant_dynamic-slice_fusion.1), channel_id=1, source_target_pairs={{0,1},{1,0},{2,3},{3,2},{4,5},{5,4},{6,7},{7,6},{8,9},{9,8},{10,11... | collective-permute-start | bytes 786440 | tf_op jit(solution)/shard_map/ppermute | solution.py:781
  51.3 12.1 %collective-permute-start.6 = (bf16[3,512,128]{2,1,0:T(8,128)(2,1)S(1)}, bf16[3,512,128]{2,1,0:T(8,128)(2,1)S(1)}, u32[]{:S(2)}, u32[]{:S(2)}) collective-permute-start(bf16[3,512,128]{2,1,0:T(8,128)(2,1)S(1)} %get-tuple-element.74), channel_id=1, source_target_pairs={{0,8},{4,12},{8,0},{12,4},{16,24},{20,28},{24,16},{28,20},{1,9},{5... | collective-permute-start | bytes 1179656 | tf_op jit(solution)/shard_map/ppermute | solution.py:700
  52.8 17.6 %collective-permute-start.7 = (bf16[3,512,128]{2,1,0:T(8,128)(2,1)S(1)}, bf16[3,512,128]{2,1,0:T(8,128)(2,1)S(1)}, u32[]{:S(2)}, u32[]{:S(2)}) collective-permute-start(bf16[3,512,128]{2,1,0:T(8,128)(2,1)S(1)} %get-tuple-element.75), channel_id=1, source_target_pairs={{0,16},{4,20},{8,24},{12,28},{16,0},{20,4},{24,8},{28,12},{1,17},{... | collective-permute-start | bytes 1179656 | tf_op jit(solution)/shard_map/ppermute | solution.py:700
  54.4 16.1 %collective-permute-start.8 = (bf16[3,512,128]{2,1,0:T(8,128)(2,1)S(1)}, bf16[3,512,128]{2,1,0:T(8,128)(2,1)S(1)}, u32[]{:S(2)}, u32[]{:S(2)}) collective-permute-start(bf16[3,512,128]{2,1,0:T(8,128)(2,1)S(1)} %get-tuple-element.76), channel_id=1, source_target_pairs={{0,24},{4,28},{8,16},{12,20},{16,8},{20,12},{24,0},{28,4},{1,25},{... | collective-permute-start | bytes 1179656 | tf_op jit(solution)/shard_map/ppermute | solution.py:700
  61.8 13.6 %copy-start.11 = (s32[4096]{0:T(1024)S(1)}, s32[4096]{0:T(1024)}, u32[]{:S(2)}) copy-start(s32[4096]{0:T(1024)} %param.18) | copy-start | bytes 49156
  70.4 2.5 %collective-permute-start.11 = (bf16[3,512,128]{2,1,0:T(8,128)(2,1)S(1)}, bf16[3,512,128]{2,1,0:T(8,128)(2,1)S(1)}, u32[]{:S(2)}, u32[]{:S(2)}) collective-permute-start(bf16[3,512,128]{2,1,0:T(8,128)(2,1)S(1)} %get-tuple-element.84.refs_0_), channel_id=1, source_target_pairs={{0,4},{4,0},{8,12},{12,8},{16,20},{20,16},{24,28},{28,24},{1,5},{5... | collective-permute-start | bytes 1179656 | tf_op jit(solution)/shard_map/ppermute | solution.py:708
  70.4 3.7 %collective-permute-start.12 = (bf16[3,512,128]{2,1,0:T(8,128)(2,1)S(1)}, bf16[3,512,128]{2,1,0:T(8,128)(2,1)S(1)}, u32[]{:S(2)}, u32[]{:S(2)}) collective-permute-start(bf16[3,512,128]{2,1,0:T(8,128)(2,1)S(1)} %collective-permute-done.6.refs_1_), channel_id=1, source_target_pairs={{0,4},{4,0},{8,12},{12,8},{16,20},{20,16},{24,28},{28,24},{1,5},{5... | collective-permute-start | bytes 1179656 | tf_op jit(solution)/shard_map/ppermute | solution.py:708
  70.9 4.0 %collective-permute-start.13 = (bf16[3,512,128]{2,1,0:T(8,128)(2,1)S(1)}, bf16[3,512,128]{2,1,0:T(8,128)(2,1)S(1)}, u32[]{:S(2)}, u32[]{:S(2)}) collective-permute-start(bf16[3,512,128]{2,1,0:T(8,128)(2,1)S(1)} %collective-permute-done.7.refs_2_), channel_id=1, source_target_pairs={{0,4},{4,0},{8,12},{12,8},{16,20},{20,16},{24,28},{28,24},{1,5},{5... | collective-permute-start | bytes 1179656 | tf_op jit(solution)/shard_map/ppermute | solution.py:708
  70.9 4.6 %collective-permute-start.14 = (bf16[3,512,128]{2,1,0:T(8,128)(2,1)S(1)}, bf16[3,512,128]{2,1,0:T(8,128)(2,1)S(1)}, u32[]{:S(2)}, u32[]{:S(2)}) collective-permute-start(bf16[3,512,128]{2,1,0:T(8,128)(2,1)S(1)} %collective-permute-done.8.refs_3_), channel_id=1, source_target_pairs={{0,4},{4,0},{8,12},{12,8},{16,20},{20,16},{24,28},{28,24},{1,5},{5... | collective-permute-start | bytes 1179656 | tf_op jit(solution)/shard_map/ppermute | solution.py:708
  71.4 12.1 %collective-permute-start.18 = (bf16[512,256]{1,0:T(8,128)(2,1)S(1)}, bf16[512,256]{1,0:T(8,128)(2,1)S(1)}, u32[]{:S(2)}, u32[]{:S(2)}) collective-permute-start(bf16[512,256]{1,0:T(8,128)(2,1)S(1)} %collective-permute-done.9.refs_10_), channel_id=1, source_target_pairs={{0,24},{4,28},{8,16},{12,20},{16,8},{20,12},{24,0},{28,4},{1,25},{... | collective-permute-start | bytes 786440 | tf_op jit(solution)/shard_map/ppermute | solution.py:700
  72.9 13.2 %collective-permute-start.17 = (bf16[512,256]{1,0:T(8,128)(2,1)S(1)}, bf16[512,256]{1,0:T(8,128)(2,1)S(1)}, u32[]{:S(2)}, u32[]{:S(2)}) collective-permute-start(bf16[512,256]{1,0:T(8,128)(2,1)S(1)} %collective-permute-done.9.refs_10_), channel_id=1, source_target_pairs={{0,16},{4,20},{8,24},{12,28},{16,0},{20,4},{24,8},{28,12},{1,17},{... | collective-permute-start | bytes 786440 | tf_op jit(solution)/shard_map/ppermute | solution.py:700
  74.1 12.1 %collective-permute-start.16 = (bf16[512,256]{1,0:T(8,128)(2,1)S(1)}, bf16[512,256]{1,0:T(8,128)(2,1)S(1)}, u32[]{:S(2)}, u32[]{:S(2)}) collective-permute-start(bf16[512,256]{1,0:T(8,128)(2,1)S(1)} %collective-permute-done.9.refs_10_), channel_id=1, source_target_pairs={{0,8},{4,12},{8,0},{12,4},{16,24},{20,28},{24,16},{28,20},{1,9},{5... | collective-permute-start | bytes 786440 | tf_op jit(solution)/shard_map/ppermute | solution.py:700
  74.9 8.6 %collective-permute-start.15 = (bf16[512,256]{1,0:T(8,128)(2,1)S(1)}, bf16[512,256]{1,0:T(8,128)(2,1)S(1)}, u32[]{:S(2)}, u32[]{:S(2)}) collective-permute-start(bf16[512,256]{1,0:T(8,128)(2,1)S(1)} %collective-permute-done.10), channel_id=1, source_target_pairs={{0,1},{1,0},{2,3},{3,2},{4,5},{5,4},{6,7},{7,6},{8,9},{9,8},{10,11... | collective-permute-start | bytes 786440 | tf_op jit(solution)/shard_map/ppermute | solution.py:781
  86.3 6.0 %collective-permute-start.19 = (bf16[512,128]{1,0:T(8,128)(2,1)S(1)}, bf16[512,128]{1,0:T(8,128)(2,1)S(1)}, u32[]{:S(2)}, u32[]{:S(2)}) collective-permute-start(bf16[512,128]{1,0:T(8,128)(2,1)S(1)} %get-tuple-element.95), channel_id=1, source_target_pairs={{0,8},{4,12},{8,0},{12,4},{16,24},{20,28},{24,16},{28,20},{1,9},{5... | collective-permute-start | bytes 393224 | tf_op jit(solution)/shard_map/ppermute | solution.py:700
  87.4 6.3 %collective-permute-start.20 = (bf16[512,128]{1,0:T(8,128)(2,1)S(1)}, bf16[512,128]{1,0:T(8,128)(2,1)S(1)}, u32[]{:S(2)}, u32[]{:S(2)}) collective-permute-start(bf16[512,128]{1,0:T(8,128)(2,1)S(1)} %get-tuple-element.96), channel_id=1, source_target_pairs={{0,16},{4,20},{8,24},{12,28},{16,0},{20,4},{24,8},{28,12},{1,17},{... | collective-permute-start | bytes 393224 | tf_op jit(solution)/shard_map/ppermute | solution.py:700
  88.2 7.1 %collective-permute-start.21 = (bf16[512,128]{1,0:T(8,128)(2,1)S(1)}, bf16[512,128]{1,0:T(8,128)(2,1)S(1)}, u32[]{:S(2)}, u32[]{:S(2)}) collective-permute-start(bf16[512,128]{1,0:T(8,128)(2,1)S(1)} %get-tuple-element.97), channel_id=1, source_target_pairs={{0,24},{4,28},{8,16},{12,20},{16,8},{20,12},{24,0},{28,4},{1,25},{... | collective-permute-start | bytes 393224 | tf_op jit(solution)/shard_map/ppermute | solution.py:700
  95.4 41.9 %copy-start.7 = (f32[2048]{0:T(1024)S(1)}, f32[2048]{0:T(1024)}, u32[]{:S(2)}) copy-start(f32[2048]{0:T(1024)} %param.21) | copy-start | bytes 24580
  95.4 11.1 %collective-permute-start.22 = (bf16[2,512,128]{2,1,0:T(8,128)(2,1)S(1)}, bf16[2,512,128]{2,1,0:T(8,128)(2,1)S(1)}, u32[]{:S(2)}, u32[]{:S(2)}) collective-permute-start(bf16[2,512,128]{2,1,0:T(8,128)(2,1)S(1)} %pad_maximum_fusion.3.refs_0_), channel_id=1, source_target_pairs={{0,1},{1,2},{2,3},{3,0},{4,5},{5,6},{6,7},{7,4},{8,9},{9,10},{10,1... | collective-permute-start | bytes 786440 | tf_op jit(solution)/shard_map/ppermute | solution.py:678
  95.9 16.2 %collective-permute-start.25 = (bf16[2,512,128]{2,1,0:T(8,128)(2,1)S(1)}, bf16[2,512,128]{2,1,0:T(8,128)(2,1)S(1)}, u32[]{:S(2)}, u32[]{:S(2)}) collective-permute-start(bf16[2,512,128]{2,1,0:T(8,128)(2,1)S(1)} %pad_maximum_fusion.4.refs_4_), channel_id=1, source_target_pairs={{0,1},{1,2},{2,3},{3,0},{4,5},{5,6},{6,7},{7,4},{8,9},{9,10},{10,1... | collective-permute-start | bytes 786440 | tf_op jit(solution)/shard_map/ppermute | solution.py:678
  97.1 24.4 %collective-permute-start.30 = (bf16[2,512,256]{2,1,0:T(8,128)(2,1)S(1)}, bf16[2,512,256]{2,1,0:T(8,128)(2,1)S(1)}, u32[]{:S(2)}, u32[]{:S(2)}) collective-permute-start(bf16[2,512,256]{2,1,0:T(8,128)(2,1)S(1)} %pad_maximum_fusion.refs_14_), channel_id=1, source_target_pairs={{0,24},{4,28},{8,16},{12,20},{16,8},{20,12},{24,0},{28,4},{1,25},{... | collective-permute-start | bytes 1572872 | tf_op jit(solution)/shard_map/ppermute | solution.py:700
  106.5 11.2 %collective-permute-start.23 = (bf16[2,512,128]{2,1,0:T(8,128)(2,1)S(1)}, bf16[2,512,128]{2,1,0:T(8,128)(2,1)S(1)}, u32[]{:S(2)}, u32[]{:S(2)}) collective-permute-start(bf16[2,512,128]{2,1,0:T(8,128)(2,1)S(1)} %collective-permute-done.22.refs_1_), channel_id=1, source_target_pairs={{0,1},{1,2},{2,3},{3,0},{4,5},{5,6},{6,7},{7,4},{8,9},{9,10},{10,1... | collective-permute-start | bytes 786440 | tf_op jit(solution)/shard_map/ppermute | solution.py:678
  106.5 15.2 %collective-permute-start.29 = (bf16[2,512,256]{2,1,0:T(8,128)(2,1)S(1)}, bf16[2,512,256]{2,1,0:T(8,128)(2,1)S(1)}, u32[]{:S(2)}, u32[]{:S(2)}) collective-permute-start(bf16[2,512,256]{2,1,0:T(8,128)(2,1)S(1)} %pad_maximum_fusion.refs_14_), channel_id=1, source_target_pairs={{0,16},{4,20},{8,24},{12,28},{16,0},{20,4},{24,8},{28,12},{1,17},{... | collective-permute-start | bytes 1572872 | tf_op jit(solution)/shard_map/ppermute | solution.py:700
  107.3 14.4 %collective-permute-start.28 = (bf16[2,512,256]{2,1,0:T(8,128)(2,1)S(1)}, bf16[2,512,256]{2,1,0:T(8,128)(2,1)S(1)}, u32[]{:S(2)}, u32[]{:S(2)}) collective-permute-start(bf16[2,512,256]{2,1,0:T(8,128)(2,1)S(1)} %pad_maximum_fusion.refs_14_), channel_id=1, source_target_pairs={{0,8},{4,12},{8,0},{12,4},{16,24},{20,28},{24,16},{28,20},{1,9},{5... | collective-permute-start | bytes 1572872 | tf_op jit(solution)/shard_map/ppermute | solution.py:700
  112.1 9.4 %collective-permute-start.26 = (bf16[2,512,128]{2,1,0:T(8,128)(2,1)S(1)}, bf16[2,512,128]{2,1,0:T(8,128)(2,1)S(1)}, u32[]{:S(2)}, u32[]{:S(2)}) collective-permute-start(bf16[2,512,128]{2,1,0:T(8,128)(2,1)S(1)} %collective-permute-done.25.refs_5_), channel_id=1, source_target_pairs={{0,1},{1,2},{2,3},{3,0},{4,5},{5,6},{6,7},{7,4},{8,9},{9,10},{10,1... | collective-permute-start | bytes 786440 | tf_op jit(solution)/shard_map/ppermute | solution.py:678
  117.7 19.5 %collective-permute-start.31 = (bf16[4,1,512,256]{3,2,0,1:T(8,128)(2,1)S(1)}, bf16[4,1,512,256]{3,2,0,1:T(8,128)(2,1)S(1)}, u32[]{:S(2)}, u32[]{:S(2)}) collective-permute-start(bf16[4,1,512,256]{3,2,0,1:T(8,128)(2,1)S(1)} %maximum_bitcast_fusion), channel_id=1, source_target_pairs={{0,4},{4,0},{8,12},{12,8},{16,20},{20,16},{24,28},{28,24},{1,5},{5... | collective-permute-start | bytes 3145736 | tf_op jit(solution)/shard_map/ppermute | solution.py:708
  121.5 11.0 %collective-permute-start.24 = (bf16[2,512,128]{2,1,0:T(8,128)(2,1)S(1)}, bf16[2,512,128]{2,1,0:T(8,128)(2,1)S(1)}, u32[]{:S(2)}, u32[]{:S(2)}) collective-permute-start(bf16[2,512,128]{2,1,0:T(8,128)(2,1)S(1)} %collective-permute-done.23.refs_2_), channel_id=1, source_target_pairs={{0,1},{1,2},{2,3},{3,0},{4,5},{5,6},{6,7},{7,4},{8,9},{9,10},{10,1... | collective-permute-start | bytes 786440 | tf_op jit(solution)/shard_map/ppermute | solution.py:678
  121.5 13.9 %collective-permute-start.27 = (bf16[2,512,128]{2,1,0:T(8,128)(2,1)S(1)}, bf16[2,512,128]{2,1,0:T(8,128)(2,1)S(1)}, u32[]{:S(2)}, u32[]{:S(2)}) collective-permute-start(bf16[2,512,128]{2,1,0:T(8,128)(2,1)S(1)} %collective-permute-done.26.refs_6_), channel_id=1, source_target_pairs={{0,1},{1,2},{2,3},{3,0},{4,5},{5,6},{6,7},{7,4},{8,9},{9,10},{10,1... | collective-permute-start | bytes 786440 | tf_op jit(solution)/shard_map/ppermute | solution.py:678
  121.7 13.6 %collective-permute-start.32 = (bf16[2,512,256]{2,1,0:T(8,128)(2,1)S(1)}, bf16[2,512,256]{2,1,0:T(8,128)(2,1)S(1)}, u32[]{:S(2)}, u32[]{:S(2)}) collective-permute-start(bf16[2,512,256]{2,1,0:T(8,128)(2,1)S(1)} %pad_maximum_fusion.refs_14_), channel_id=1, source_target_pairs={{0,4},{4,0},{8,12},{12,8},{16,20},{20,16},{24,28},{28,24},{1,5},{5... | collective-permute-start | bytes 1572872 | tf_op jit(solution)/shard_map/ppermute | solution.py:708
  121.7 13.6 %collective-permute-start.35 = (bf16[2,512,256]{2,1,0:T(8,128)(2,1)S(1)}, bf16[2,512,256]{2,1,0:T(8,128)(2,1)S(1)}, u32[]{:S(2)}, u32[]{:S(2)}) collective-permute-start(bf16[2,512,256]{2,1,0:T(8,128)(2,1)S(1)} %collective-permute-done.30.refs_17_), channel_id=1, source_target_pairs={{0,4},{4,0},{8,12},{12,8},{16,20},{20,16},{24,28},{28,24},{1,5},{5... | collective-permute-start | bytes 1572872 | tf_op jit(solution)/shard_map/ppermute | solution.py:708
  132.5 2.8 %collective-permute-start.34 = (bf16[2,512,256]{2,1,0:T(8,128)(2,1)S(1)}, bf16[2,512,256]{2,1,0:T(8,128)(2,1)S(1)}, u32[]{:S(2)}, u32[]{:S(2)}) collective-permute-start(bf16[2,512,256]{2,1,0:T(8,128)(2,1)S(1)} %collective-permute-done.29.refs_16_), channel_id=1, source_target_pairs={{0,4},{4,0},{8,12},{12,8},{16,20},{20,16},{24,28},{28,24},{1,5},{5... | collective-permute-start | bytes 1572872 | tf_op jit(solution)/shard_map/ppermute | solution.py:708
  135.3 1.9 collective-permute-start.33
  159.3 12.9 %collective-permute-start.38 = (bf16[128,512]{1,0:T(8,128)(2,1)S(1)}, bf16[128,512]{1,0:T(8,128)(2,1)S(1)}, u32[]{:S(2)}, u32[]{:S(2)}) collective-permute-start(bf16[128,512]{1,0:T(8,128)(2,1)S(1)} %get-tuple-element.118), channel_id=1, source_target_pairs={{0,1},{1,2},{2,3},{3,0},{4,5},{5,6},{6,7},{7,4},{8,9},{9,10},{10,1... | collective-permute-start | bytes 393224 | tf_op jit(solution)/shard_map/ppermute | solution.py:691
  159.4 13.0 %collective-permute-start.39 = (bf16[128,512]{1,0:T(8,128)(2,1)S(1)}, bf16[128,512]{1,0:T(8,128)(2,1)S(1)}, u32[]{:S(2)}, u32[]{:S(2)}) collective-permute-start(bf16[128,512]{1,0:T(8,128)(2,1)S(1)} %get-tuple-element.119), channel_id=1, source_target_pairs={{0,2},{1,3},{2,0},{3,1},{4,6},{5,7},{6,4},{7,5},{8,10},{9,11},{10,... | collective-permute-start | bytes 393224 | tf_op jit(solution)/shard_map/ppermute | solution.py:691
  159.5 12.9 %collective-permute-start.40 = (bf16[128,512]{1,0:T(8,128)(2,1)S(1)}, bf16[128,512]{1,0:T(8,128)(2,1)S(1)}, u32[]{:S(2)}, u32[]{:S(2)}) collective-permute-start(bf16[128,512]{1,0:T(8,128)(2,1)S(1)} %get-tuple-element.120), channel_id=1, source_target_pairs={{0,3},{1,0},{2,1},{3,2},{4,7},{5,4},{6,5},{7,6},{8,11},{9,8},{10,9... | collective-permute-start | bytes 393224 | tf_op jit(solution)/shard_map/ppermute | solution.py:691
  166.6 19.1 %collective-permute-start.36 = (bf16[512,512]{1,0:T(8,128)(2,1)S(1)}, bf16[512,512]{1,0:T(8,128)(2,1)S(1)}, u32[]{:S(2)}, u32[]{:S(2)}) collective-permute-start(bf16[512,512]{1,0:T(8,128)(2,1)S(1)} %down.3), channel_id=1, source_target_pairs={{0,1},{1,0},{2,3},{3,2},{4,5},{5,4},{6,7},{7,6},{8,9},{9,8},{10,11... | collective-permute-start | bytes 1572872 | tf_op jit(solution)/shard_map/ppermute | solution.py:781
  173.4 14.9 %collective-permute-start.43 = (bf16[128,512]{1,0:T(8,128)(2,1)S(1)}, bf16[128,512]{1,0:T(8,128)(2,1)S(1)}, u32[]{:S(2)}, u32[]{:S(2)}) collective-permute-start(bf16[128,512]{1,0:T(8,128)(2,1)S(1)} %multiply_convert_fusion.3.refs_0_), channel_id=1, source_target_pairs={{0,3},{1,0},{2,1},{3,2},{4,7},{5,4},{6,5},{7,6},{8,11},{9,8},{10,9... | collective-permute-start | bytes 393224 | tf_op jit(solution)/shard_map/ppermute | solution.py:691
  176.3 12.0 %collective-permute-start.42 = (bf16[128,512]{1,0:T(8,128)(2,1)S(1)}, bf16[128,512]{1,0:T(8,128)(2,1)S(1)}, u32[]{:S(2)}, u32[]{:S(2)}) collective-permute-start(bf16[128,512]{1,0:T(8,128)(2,1)S(1)} %multiply_convert_fusion.3.refs_0_), channel_id=1, source_target_pairs={{0,2},{1,3},{2,0},{3,1},{4,6},{5,7},{6,4},{7,5},{8,10},{9,11},{10,... | collective-permute-start | bytes 393224 | tf_op jit(solution)/shard_map/ppermute | solution.py:691
  177.5 14.6 %collective-permute-start.41 = (bf16[128,512]{1,0:T(8,128)(2,1)S(1)}, bf16[128,512]{1,0:T(8,128)(2,1)S(1)}, u32[]{:S(2)}, u32[]{:S(2)}) collective-permute-start(bf16[128,512]{1,0:T(8,128)(2,1)S(1)} %multiply_convert_fusion.3.refs_0_), channel_id=1, source_target_pairs={{0,1},{1,2},{2,3},{3,0},{4,5},{5,6},{6,7},{7,4},{8,9},{9,10},{10,1... | collective-permute-start | bytes 393224 | tf_op jit(solution)/shard_map/ppermute | solution.py:691
  194.3 2.4 %collective-permute-start.44 = (bf16[4,208,512]{2,1,0:T(8,128)(2,1)S(1)}, bf16[4,208,512]{2,1,0:T(8,128)(2,1)S(1)}, u32[]{:S(2)}, u32[]{:S(2)}) collective-permute-start(bf16[4,208,512]{2,1,0:T(8,128)(2,1)S(1)} %get-tuple-element.126), channel_id=1, source_target_pairs={{0,4},{4,0},{8,12},{12,8},{16,20},{20,16},{24,28},{28,24},{1,5},{5... | collective-permute-start | bytes 2555912 | tf_op jit(solution)/shard_map/ppermute | solution.py:708
  196.9 8.2 %collective-permute-start.45 = (bf16[208,512]{1,0:T(8,128)(2,1)S(1)}, bf16[208,512]{1,0:T(8,128)(2,1)S(1)}, u32[]{:S(2)}, u32[]{:S(2)}) collective-permute-start(bf16[208,512]{1,0:T(8,128)(2,1)S(1)} %get-tuple-element.128), channel_id=1, source_target_pairs={{0,8},{4,12},{8,0},{12,4},{16,24},{20,28},{24,16},{28,20},{1,9},{5... | collective-permute-start | bytes 638984 | tf_op jit(solution)/shard_map/ppermute | solution.py:700
  197.0 11.9 %collective-permute-start.46 = (bf16[208,512]{1,0:T(8,128)(2,1)S(1)}, bf16[208,512]{1,0:T(8,128)(2,1)S(1)}, u32[]{:S(2)}, u32[]{:S(2)}) collective-permute-start(bf16[208,512]{1,0:T(8,128)(2,1)S(1)} %get-tuple-element.129), channel_id=1, source_target_pairs={{0,16},{4,20},{8,24},{12,28},{16,0},{20,4},{24,8},{28,12},{1,17},{... | collective-permute-start | bytes 638984 | tf_op jit(solution)/shard_map/ppermute | solution.py:700
  198.2 10.7 %collective-permute-start.47 = (bf16[208,512]{1,0:T(8,128)(2,1)S(1)}, bf16[208,512]{1,0:T(8,128)(2,1)S(1)}, u32[]{:S(2)}, u32[]{:S(2)}) collective-permute-start(bf16[208,512]{1,0:T(8,128)(2,1)S(1)} %get-tuple-element.130), channel_id=1, source_target_pairs={{0,24},{4,28},{8,16},{12,20},{16,8},{20,12},{24,0},{28,4},{1,25},{... | collective-permute-start | bytes 638984 | tf_op jit(solution)/shard_map/ppermute | solution.py:700
  200.6 25.3 %collective-permute-start.49 = (bf16[512,512]{1,0:T(8,128)(2,1)S(1)}, bf16[512,512]{1,0:T(8,128)(2,1)S(1)}, u32[]{:S(2)}, u32[]{:S(2)}) collective-permute-start(bf16[512,512]{1,0:T(8,128)(2,1)S(1)} %add_convert_fusion.1), channel_id=1, source_target_pairs={{0,2},{1,3},{2,0},{3,1},{4,6},{5,7},{6,4},{7,5},{8,10},{9,11},{10,... | collective-permute-start | bytes 1572872 | tf_op jit(solution)/shard_map/ppermute | solution.py:781
  201.2 24.8 %collective-permute-start.37 = (bf16[512,512]{1,0:T(8,128)(2,1)S(1)}, bf16[512,512]{1,0:T(8,128)(2,1)S(1)}, u32[]{:S(2)}, u32[]{:S(2)}) collective-permute-start(bf16[512,512]{1,0:T(8,128)(2,1)S(1)} %get-tuple-element.115), channel_id=1, source_target_pairs={{0,1},{1,0},{2,3},{3,2},{4,5},{5,4},{6,7},{7,6},{8,9},{9,8},{10,11... | collective-permute-start | bytes 1572872 | tf_op jit(solution)/shard_map/ppermute | solution.py:781
  209.0 16.9 %collective-permute-start.48 = (bf16[208,512]{1,0:T(8,128)(2,1)S(1)}, bf16[208,512]{1,0:T(8,128)(2,1)S(1)}, u32[]{:S(2)}, u32[]{:S(2)}) collective-permute-start(bf16[208,512]{1,0:T(8,128)(2,1)S(1)} %add_convert_fusion.2.refs_0_), channel_id=1, source_target_pairs={{0,24},{4,28},{8,16},{12,20},{16,8},{20,12},{24,0},{28,4},{1,25},{... | collective-permute-start | bytes 638984 | tf_op jit(solution)/shard_map/ppermute | solution.py:700
  210.6 15.8 %collective-permute-start.51 = (bf16[208,512]{1,0:T(8,128)(2,1)S(1)}, bf16[208,512]{1,0:T(8,128)(2,1)S(1)}, u32[]{:S(2)}, u32[]{:S(2)}) collective-permute-start(bf16[208,512]{1,0:T(8,128)(2,1)S(1)} %add_convert_fusion.2.refs_0_), channel_id=1, source_target_pairs={{0,16},{4,20},{8,24},{12,28},{16,0},{20,4},{24,8},{28,12},{1,17},{... | collective-permute-start | bytes 638984 | tf_op jit(solution)/shard_map/ppermute | solution.py:700
  212.2 14.3 %collective-permute-start.50 = (bf16[208,512]{1,0:T(8,128)(2,1)S(1)}, bf16[208,512]{1,0:T(8,128)(2,1)S(1)}, u32[]{:S(2)}, u32[]{:S(2)}) collective-permute-start(bf16[208,512]{1,0:T(8,128)(2,1)S(1)} %add_convert_fusion.2.refs_0_), channel_id=1, source_target_pairs={{0,8},{4,12},{8,0},{12,4},{16,24},{20,28},{24,16},{28,20},{1,9},{5... | collective-permute-start | bytes 638984 | tf_op jit(solution)/shard_map/ppermute | solution.py:700
  225.9 2.1 collective-permute-start.52
  226.0 2.2 collective-permute-start.55
  226.4 1.6 collective-permute-start.54
  226.6 1.7 collective-permute-start.53
  (7 other events, 36.4 us)

commit v9 on v8

--- a/solution.py
+++ b/solution.py
@@ -381,7 +381,8 @@
         for s, part in enumerate(parts[k]):
             count = part.shape[0]
             for i in range(count):
-                at = (level ^ info_ref[s]) * width + (chip ^ (k * count + i)) * HD
+                flip = level ^ info_ref[s]
+                at = ((flip & 1) * 2 + (flip >> 1)) * width + (chip ^ (k * count + i)) * HD
                 heads.append(copy(part.at[i], attended.at[:, pl.ds(pl.multiple_of(at, HD), HD)]))
     slices = [
         [
@@ -780,18 +781,16 @@
 
     over = lambda value, bit: lax.ppermute(value, "tensor", [(i, i ^ bit) for i in range(ring)])
     w_slice = lax.dynamic_slice(w_out, [zero, starts[1]], (w_out.shape[0], slice_cols))
-    w_slice, tok_full = lax.optimization_barrier((w_slice, tok_full))
-    w_first, w_second = over(w_slice, 1), over(w_slice, 2)
+    w_slice, tok_full, _ = lax.optimization_barrier((w_slice, tok_full, s_gate_out))
+    w_first = over(w_slice, 2)
 
     own = flipped(made)
-    held = lax.optimization_barrier((*own, w_first, w_second, *early))
-    own, (w_first, w_second) = held[:chips], held[chips : chips + 2]
-    w_third = over(w_second, 1)
+    *own, w_first = lax.optimization_barrier((*own, w_first, *early))[: chips + 1]
+    w_rest = over(jnp.stack([w_slice, w_first]), 1)
     other = [swapped(a) for a in own]
     near_first = flipped([w_first] * chips)
     made = attention_call(below, info, own, other, ring)
-    *made, w_third = lax.optimization_barrier((*made, w_third, *near_first))[: chips + 1]
-    w_rest = jnp.stack([w_second, w_third])
+    *made, w_rest = lax.optimization_barrier((*made, w_rest, *near_first))[: chips + 1]
     attended = lax.optimization_barrier(tuple(flipped(made)))
     parts = [
         ring_gather(jnp.stack(attended[k : k + chips // 2]), "tensor") for k in (0, chips // 2)

time: 232 us -> 232 us (level)
    ppermute x6 -> x5, waiting for transfers between devices: 21.6 us -> 26.8 us  [paired(): lax.ppermute(value, 'tensor', [(i, i ^ bit) for i in range(ring)])]
    ppermute x18, waiting for transfers between devices: 21.8 us -> 16.7 us  [flipped(): lax.ppermute(pieces[f], 'dp', [(i, i ^ 2 * f) for i in range(size)])]
    ppermute x6 -> x5, starting transfers between devices: 6.5 us -> 4.62 us  [paired(): lax.ppermute(value, 'tensor', [(i, i ^ bit) for i in range(ring)])]
  transfers between devices with their start and end apart: 56 -> 55, of which waited for: 31 -> 32; matrix products, arithmetic and copies ran while one was open for 6% -> 6% of each run, Pallas kernels for 6% -> 7%
where the time goes in v9:
time: 232 us
  waiting for transfers between devices  118 us (51%)
  Pallas kernels  48.6 us (21%)
  starting transfers between devices  43.4 us (19%)
  matrix products  7.38 us (3%)
  other arithmetic  6.12 us (3%)
  local copies, waits for them, and re-layouts  5.76 us (2%)
  between operations  2.78 us (1%)
    ppermute x12, waiting for transfers between devices, step_on(): return lax.ppermute(block, axis, [(i, (i + 1) % size) for i in range(size)])  63 us
    ppermute x5, waiting for transfers between devices, paired(): lax.ppermute(value, 'tensor', [(i, i ^ bit) for i in range(ring)])  26.8 us
    pallas_call x1, Pallas kernels, middle_call(): pl.pallas_call(functools.partial(middle_kernel, ring=ring, chips=chips),...  22.1 us
    ppermute x18, starting transfers between devices, flipped(): lax.ppermute(pieces[f], 'dp', [(i, i ^ 2 * f) for i in range(size)])  21.6 us
    ppermute x18, waiting for transfers between devices, flipped(): lax.ppermute(pieces[f], 'dp', [(i, i ^ 2 * f) for i in range(size)])  16.7 us
    pallas_call x1, Pallas kernels, attention_call(): pl.pallas_call(functools.partial(attention_kernel, chips=chips, ring=ring...  8.6 us
    ppermute x6, starting transfers between devices, shifted(): lax.ppermute(pieces[s], axis, [(i, (i + s) % size) for i in range(size)])  7.97 us
    dot_general x4, matrix products, dot(): return jnp.dot(a, b, preferred_element_type=F32)  7.38 us
  transfers between devices with their start and end apart: 55, of which 32 were waited for; matrix products, arithmetic and copies ran while one was open for 6% of the time, Pallas kernels for 7%

profile of v9, /device:TPU:0, one launch (start us, length us, event | category | flops | bytes accessed | tf_op | source)
XLA Modules:
  0.0 232.2 jit_solution(10804455667898032754)
XLA Ops:
  0.7 1.1 fusion.10
  1.8 3.1 %collective-permute-start.3 = (bf16[256,512]{1,0:T(8,128)(2,1)S(1)}, bf16[256,512]{1,0:T(8,128)(2,1)S(1)}, u32[]{:S(2)}, u32[]{:S(2)}) collective-permute-start(bf16[256,512]{1,0:T(8,128)(2,1)S(1)} %get-tuple-element.138.refs_4_), channel_id=1, source_target_pairs={{0,1},{1,2},{2,3},{3,0},{4,5},{5,6},{6,7},{7,4},{8,9},{9,10},{10,1... | collective-permute-start | bytes 786440 | tf_op jit(solution)/shard_map/ppermute | solution.py:679
  4.9 1.6 collective-permute-start
  7.2 1.0 fusion.3
  8.6 5.5 %collective-permute-done.3.refs_5_ = bf16[256,512]{1,0:T(8,128)(2,1)S(1)} collective-permute-done((bf16[256,512]{1,0:T(8,128)(2,1)S(1)}, bf16[256,512]{1,0:T(8,128)(2,1)S(1)}, u32[]{:S(2)}, u32[]{:S(2)}) %collective-permute-start.3) | collective-permute-done | bytes 262176 | tf_op jit(solution)/shard_map/ppermute | solution.py:679
  14.1 5.6 %collective-permute-done.refs_1_ = bf16[256,512]{1,0:T(8,128)(2,1)S(1)} collective-permute-done((bf16[256,512]{1,0:T(8,128)(2,1)S(1)}, bf16[256,512]{1,0:T(8,128)(2,1)S(1)}, u32[]{:S(2)}, u32[]{:S(2)}) %collective-permute-start) | collective-permute-done | bytes 262176 | tf_op jit(solution)/shard_map/ppermute | solution.py:679
  19.7 1.1 constant_dynamic-slice_fusion.1
  20.9 1.1 convert_element_type.98
  22.0 3.3 %collective-permute-done.4.refs_6_ = bf16[256,512]{1,0:T(8,128)(2,1)S(1)} collective-permute-done((bf16[256,512]{1,0:T(8,128)(2,1)S(1)}, bf16[256,512]{1,0:T(8,128)(2,1)S(1)}, u32[]{:S(2)}, u32[]{:S(2)}) %collective-permute-start.4) | collective-permute-done | bytes 262176 | tf_op jit(solution)/shard_map/ppermute | solution.py:679
  25.3 5.6 %collective-permute-done.1.refs_2_ = bf16[256,512]{1,0:T(8,128)(2,1)S(1)} collective-permute-done((bf16[256,512]{1,0:T(8,128)(2,1)S(1)}, bf16[256,512]{1,0:T(8,128)(2,1)S(1)}, u32[]{:S(2)}, u32[]{:S(2)}) %collective-permute-start.1) | collective-permute-done | bytes 262176 | tf_op jit(solution)/shard_map/ppermute | solution.py:679
  31.1 5.4 %collective-permute-done.5.refs_7_ = bf16[256,512]{1,0:T(8,128)(2,1)S(1)} collective-permute-done((bf16[256,512]{1,0:T(8,128)(2,1)S(1)}, bf16[256,512]{1,0:T(8,128)(2,1)S(1)}, u32[]{:S(2)}, u32[]{:S(2)}) %collective-permute-start.5) | collective-permute-done | bytes 262176 | tf_op jit(solution)/shard_map/ppermute | solution.py:679
  36.5 4.8 %collective-permute-done.2.refs_3_ = bf16[256,512]{1,0:T(8,128)(2,1)S(1)} collective-permute-done((bf16[256,512]{1,0:T(8,128)(2,1)S(1)}, bf16[256,512]{1,0:T(8,128)(2,1)S(1)}, u32[]{:S(2)}, u32[]{:S(2)}) %collective-permute-start.2) | collective-permute-done | bytes 262176 | tf_op jit(solution)/shard_map/ppermute | solution.py:679
  41.4 6.3 %qkv.1 = (bf16[3,512,128]{2,1,0:T(8,128)(2,1)S(1)}, bf16[3,512,128]{2,1,0:T(8,128)(2,1)S(1)}, bf16[3,512,128]{2,1,0:T(8,128)(2,1)S(1)}, bf16[3,512,128]{2,1,0:T(8,128)(2,1)S(1)}, bf16[512,2048]{1,0:T(8,128)(2,1)S(1)}) custom-call(s32[16]{0:T(128)S(1)} %fusion.9.info_ref, bf16[256,512]{1,0:T(8,128)(2,1)S(1)} %get-tuple-element.139.refs_0_, ...), custom_call_target="tpu_custom_call" | custom-call | flops 3221225472 | bytes 6291456 | tf_op jit(solution)/shard_map/qkv/pallas_call | solution.py:231
  47.7 1.3 copy-done.8
  49.0 1.5 collective-permute-start.6
  50.5 1.5 collective-permute-start.7
  53.0 0.8 multiply_convert_fusion
  54.7 5.7 %fusion.refs_26_ = bf16[2048,512]{1,0:T(8,128)(2,1)} fusion(bf16[2048,2048]{1,0:T(8,128)(2,1)S(1)} %bitcast.26, bf16[2048,512]{1,0:T(8,128)(2,1)S(1)} %copy-done.12), kind=kOutput, calls=%fused_computation.1 | convolution fusion | flops 4296015872 | bytes 12582912 | tf_op jit(solution)/shard_map/dot_general | solution.py:166
  60.8 5.2 %collective-permute-done.9.refs_10_ = bf16[512,256]{1,0:T(8,128)(2,1)S(1)} collective-permute-done((bf16[512,256]{1,0:T(8,128)(2,1)S(1)}, bf16[512,256]{1,0:T(8,128)(2,1)S(1)}, u32[]{:S(2)}, u32[]{:S(2)}) %collective-permute-start.9) | collective-permute-done | bytes 262176 | tf_op jit(solution)/shard_map/ppermute | solution.py:782
  65.9 2.8 %collective-permute-done.7.refs_2_ = bf16[3,512,128]{2,1,0:T(8,128)(2,1)S(1)} collective-permute-done((bf16[3,512,128]{2,1,0:T(8,128)(2,1)S(1)}, bf16[3,512,128]{2,1,0:T(8,128)(2,1)S(1)}, u32[]{:S(2)}, u32[]{:S(2)}) %collective-permute-start.7) | collective-permute-done | bytes 393248 | tf_op jit(solution)/shard_map/ppermute | solution.py:701
  70.5 1.5 collective-permute-start.17
  72.0 1.2 collective-permute-start.16
  74.1 8.6 %attention.1 = (bf16[512,128]{1,0:T(8,128)(2,1)S(1)}, bf16[512,128]{1,0:T(8,128)(2,1)S(1)}, bf16[512,128]{1,0:T(8,128)(2,1)S(1)}, bf16[512,128]{1,0:T(8,128)(2,1)S(1)}) custom-call(s32[8]{0:T(128)S(1)} %convert_reduce_fusion.first_ref, s32[16]{0:T(128)S(1)} %fusion.9.info_ref, bf16[3,512,128]{2,1,0:T(8,128)(2,1)S(1)} %get-tuple-element.83.refs_0_, ...), custom_call_target="tpu_custom_call" | custom-call | flops 2147483648 | bytes 4194304 | tf_op jit(solution)/shard_map/attention/pallas_call | solution.py:337
  82.7 2.6 %collective-permute-done.16.refs_12_ = bf16[512,256]{1,0:T(8,128)(2,1)S(1)} collective-permute-done((bf16[512,256]{1,0:T(8,128)(2,1)S(1)}, bf16[512,256]{1,0:T(8,128)(2,1)S(1)}, u32[]{:S(2)}, u32[]{:S(2)}) %collective-permute-start.16) | collective-permute-done | bytes 262176 | tf_op jit(solution)/shard_map/ppermute | solution.py:701
  85.4 1.1 collective-permute-start.18
  87.4 1.5 collective-permute-start.20
  88.9 2.5 %collective-permute-done.18 = bf16[512,128]{1,0:T(8,128)(2,1)S(1)} collective-permute-done((bf16[512,128]{1,0:T(8,128)(2,1)S(1)}, bf16[512,128]{1,0:T(8,128)(2,1)S(1)}, u32[]{:S(2)}, u32[]{:S(2)}) %collective-permute-start.18) | collective-permute-done | bytes 131104 | tf_op jit(solution)/shard_map/ppermute | solution.py:701
  91.4 1.5 collective-permute-done.19
  92.9 1.6 collective-permute-done.20
  94.5 1.1 collective-permute-start.21
  95.7 0.8 collective-permute-start.24
  96.5 1.7 collective-permute-start.29
  98.2 7.4 %collective-permute-done.21.refs_1_ = bf16[2,512,128]{2,1,0:T(8,128)(2,1)S(1)} collective-permute-done((bf16[2,512,128]{2,1,0:T(8,128)(2,1)S(1)}, bf16[2,512,128]{2,1,0:T(8,128)(2,1)S(1)}, u32[]{:S(2)}, u32[]{:S(2)}) %collective-permute-start.21) | collective-permute-done | bytes 262176 | tf_op jit(solution)/shard_map/ppermute | solution.py:679
  105.6 0.8 collective-permute-start.28
  106.5 1.5 collective-permute-start.27
  108.0 3.3 %collective-permute-done.24.refs_5_ = bf16[2,512,128]{2,1,0:T(8,128)(2,1)S(1)} collective-permute-done((bf16[2,512,128]{2,1,0:T(8,128)(2,1)S(1)}, bf16[2,512,128]{2,1,0:T(8,128)(2,1)S(1)}, u32[]{:S(2)}, u32[]{:S(2)}) %collective-permute-start.24) | collective-permute-done | bytes 262176 | tf_op jit(solution)/shard_map/ppermute | solution.py:679
  111.4 5.5 %collective-permute-done.22.refs_2_ = bf16[2,512,128]{2,1,0:T(8,128)(2,1)S(1)} collective-permute-done((bf16[2,512,128]{2,1,0:T(8,128)(2,1)S(1)}, bf16[2,512,128]{2,1,0:T(8,128)(2,1)S(1)}, u32[]{:S(2)}, u32[]{:S(2)}) %collective-permute-start.22) | collective-permute-done | bytes 262176 | tf_op jit(solution)/shard_map/ppermute | solution.py:679
  116.9 3.7 %collective-permute-done.25.refs_6_ = bf16[2,512,128]{2,1,0:T(8,128)(2,1)S(1)} collective-permute-done((bf16[2,512,128]{2,1,0:T(8,128)(2,1)S(1)}, bf16[2,512,128]{2,1,0:T(8,128)(2,1)S(1)}, u32[]{:S(2)}, u32[]{:S(2)}) %collective-permute-start.25) | collective-permute-done | bytes 262176 | tf_op jit(solution)/shard_map/ppermute | solution.py:679
  121.6 10.1 %collective-permute-done.23.refs_3_ = bf16[2,512,128]{2,1,0:T(8,128)(2,1)S(1)} collective-permute-done((bf16[2,512,128]{2,1,0:T(8,128)(2,1)S(1)}, bf16[2,512,128]{2,1,0:T(8,128)(2,1)S(1)}, u32[]{:S(2)}, u32[]{:S(2)}) %collective-permute-start.23) | collective-permute-done | bytes 262176 | tf_op jit(solution)/shard_map/ppermute | solution.py:679
  131.7 2.8 %collective-permute-done.26.refs_7_ = bf16[2,512,128]{2,1,0:T(8,128)(2,1)S(1)} collective-permute-done((bf16[2,512,128]{2,1,0:T(8,128)(2,1)S(1)}, bf16[2,512,128]{2,1,0:T(8,128)(2,1)S(1)}, u32[]{:S(2)}, u32[]{:S(2)}) %collective-permute-start.26) | collective-permute-done | bytes 262176 | tf_op jit(solution)/shard_map/ppermute | solution.py:679
  134.5 1.9 collective-permute-done.32.refs_20_
  136.4 22.1 %middle.1 = (bf16[512,2048]{1,0:T(8,128)(2,1)}, bf16[512,512]{1,0:T(8,128)(2,1)S(1)}, bf16[128,512]{1,0:T(8,128)(2,1)S(1)}, bf16[128,512]{1,0:T(8,128)(2,1)S(1)}...) custom-call(s32[16]{0:T(128)S(1)} %fusion.9.info_ref, bf16[2,512,128]{2,1,0:T(8,128)(2,1)S(1)} %pad_maximum_fusion.3.refs_0_, ...), custom_call_target="tpu_custom_call" | custom-call | flops 14227079168 | bytes 25165824 | tf_op jit(solution)/shard_map/middle/pallas_call | solution.py:482
  158.6 3.7 %collective-permute-start.39 = (bf16[128,512]{1,0:T(8,128)(2,1)S(1)}, bf16[128,512]{1,0:T(8,128)(2,1)S(1)}, u32[]{:S(2)}, u32[]{:S(2)}) collective-permute-start(bf16[128,512]{1,0:T(8,128)(2,1)S(1)} %get-tuple-element.118), channel_id=1, source_target_pairs={{0,3},{1,0},{2,1},{3,2},{4,7},{5,4},{6,5},{7,6},{8,11},{9,8},{10,9... | collective-permute-start | bytes 393224 | tf_op jit(solution)/shard_map/ppermute | solution.py:692
  162.4 1.6 copy-done.2
  164.0 1.8 down.3
  166.4 5.0 %down.2 = (bf16[512,512]{1,0:T(8,128)(2,1)S(1)}, bf16[512,512]{1,0:T(8,128)(2,1)S(1)}, bf16[512,512]{1,0:T(8,128)(2,1)S(1)}) custom-call(s32[16]{0:T(128)S(1)} %fusion.9.info_ref, bf16[512,2048]{1,0:T(8,128)(2,1)S(1)} %copy-done.2, bf16[2048,2048]{1,0:T(8,128)(2,1)S(1)} %bitcast.26), custom_call_target="tpu_custom_call" | custom-call | flops 3221225472 | bytes 6291456 | tf_op jit(solution)/shard_map/down/pallas_call | solution.py:556
  171.5 1.1 multiply_convert_fusion.3.refs_0_
  172.6 2.9 %collective-permute-start.42 = (bf16[128,512]{1,0:T(8,128)(2,1)S(1)}, bf16[128,512]{1,0:T(8,128)(2,1)S(1)}, u32[]{:S(2)}, u32[]{:S(2)}) collective-permute-start(bf16[128,512]{1,0:T(8,128)(2,1)S(1)} %multiply_convert_fusion.3.refs_0_), channel_id=1, source_target_pairs={{0,3},{1,0},{2,1},{3,2},{4,7},{5,4},{6,5},{7,6},{8,11},{9,8},{10,9... | collective-permute-start | bytes 393224 | tf_op jit(solution)/shard_map/ppermute | solution.py:692
  175.5 1.2 collective-permute-start.41
  176.7 8.1 %collective-permute-done.35 = bf16[512,512]{1,0:T(8,128)(2,1)S(1)} collective-permute-done((bf16[512,512]{1,0:T(8,128)(2,1)S(1)}, bf16[512,512]{1,0:T(8,128)(2,1)S(1)}, u32[]{:S(2)}, u32[]{:S(2)}) %collective-permute-start.35) | collective-permute-done | bytes 524320 | tf_op jit(solution)/shard_map/ppermute | solution.py:782
  184.8 2.7 %collective-permute-done.42.refs_3_ = bf16[128,512]{1,0:T(8,128)(2,1)S(1)} collective-permute-done((bf16[128,512]{1,0:T(8,128)(2,1)S(1)}, bf16[128,512]{1,0:T(8,128)(2,1)S(1)}, u32[]{:S(2)}, u32[]{:S(2)}) %collective-permute-start.42) | collective-permute-done | bytes 131104 | tf_op jit(solution)/shard_map/ppermute | solution.py:692
  187.5 3.7 %collective-permute-done.40.refs_1_ = bf16[128,512]{1,0:T(8,128)(2,1)S(1)} collective-permute-done((bf16[128,512]{1,0:T(8,128)(2,1)S(1)}, bf16[128,512]{1,0:T(8,128)(2,1)S(1)}, u32[]{:S(2)}, u32[]{:S(2)}) %collective-permute-start.40) | collective-permute-done | bytes 131104 | tf_op jit(solution)/shard_map/ppermute | solution.py:692
  191.2 2.2 grads.1
  193.6 2.4 %collective-permute-done.43.theirs_ref = bf16[4,208,512]{2,1,0:T(8,128)(2,1)S(1)} collective-permute-done((bf16[4,208,512]{2,1,0:T(8,128)(2,1)S(1)}, bf16[4,208,512]{2,1,0:T(8,128)(2,1)S(1)}, u32[]{:S(2)}, u32[]{:S(2)}) %collective-permute-start.43) | collective-permute-done | bytes 852000 | tf_op jit(solution)/shard_map/ppermute | solution.py:709
  196.2 1.2 collective-permute-start.45
  197.4 2.3 collective-permute-start.46
  200.4 2.5 %collective-permute-start.36 = (bf16[512,512]{1,0:T(8,128)(2,1)S(1)}, bf16[512,512]{1,0:T(8,128)(2,1)S(1)}, u32[]{:S(2)}, u32[]{:S(2)}) collective-permute-start(bf16[512,512]{1,0:T(8,128)(2,1)S(1)} %get-tuple-element.113), channel_id=1, source_target_pairs={{0,1},{1,0},{2,3},{3,2},{4,5},{5,4},{6,7},{7,6},{8,9},{9,8},{10,11... | collective-permute-start | bytes 1572872 | tf_op jit(solution)/shard_map/ppermute | solution.py:782
  202.9 1.3 collective-permute-done.44
  204.3 3.8 %collective-permute-done.45 = bf16[208,512]{1,0:T(8,128)(2,1)S(1)} collective-permute-done((bf16[208,512]{1,0:T(8,128)(2,1)S(1)}, bf16[208,512]{1,0:T(8,128)(2,1)S(1)}, u32[]{:S(2)}, u32[]{:S(2)}) %collective-permute-start.45) | collective-permute-done | bytes 213024 | tf_op jit(solution)/shard_map/ppermute | solution.py:701
  208.2 1.5 collective-permute-start.47
  209.8 1.6 collective-permute-start.50
  211.8 13.3 %collective-permute-done.48 = bf16[512,512]{1,0:T(8,128)(2,1)S(1)} collective-permute-done((bf16[512,512]{1,0:T(8,128)(2,1)S(1)}, bf16[512,512]{1,0:T(8,128)(2,1)S(1)}, u32[]{:S(2)}, u32[]{:S(2)}) %collective-permute-start.48) | collective-permute-done | bytes 524320 | tf_op jit(solution)/shard_map/ppermute | solution.py:782
  226.1 1.1 add_convert_fusion
  227.5 2.4 %finish.1 = (f32[512,512]{1,0:T(8,128)}, f32[512,512]{1,0:T(8,128)}, f32[512,512]{1,0:T(8,128)}, f32[8,16,128]{2,1,0:T(8,128)S(1)}) custom-call(s32[16]{0:T(128)S(1)} %fusion.9.info_ref, bf16[208,512]{1,0:T(8,128)(2,1)S(1)} %add_convert_fusion.2.refs_0_, bf16[208,512]{1,0:T(8,128)(2,1)S(1)} %collective-permute-done.49.refs_1_, ...), custom_call_target="tpu_custom_call" | custom-call | flops 262144 | bytes 3145728 | tf_op jit(solution)/shard_map/finish/pallas_call | solution.py:661
  (110 shorter events, 12.6 us)
Async XLA Ops:
  0.6 52.3 %copy-start = (bf16[512,512]{1,0:T(8,128)(2,1)S(1)}, bf16[512,512]{1,0:T(8,128)(2,1)}, u32[]{:S(2)}) copy-start(bf16[512,512]{1,0:T(8,128)(2,1)} %param.31) | copy-start | bytes 1572868
  1.8 12.2 %collective-permute-start.3 = (bf16[256,512]{1,0:T(8,128)(2,1)S(1)}, bf16[256,512]{1,0:T(8,128)(2,1)S(1)}, u32[]{:S(2)}, u32[]{:S(2)}) collective-permute-start(bf16[256,512]{1,0:T(8,128)(2,1)S(1)} %get-tuple-element.138.refs_4_), channel_id=1, source_target_pairs={{0,1},{1,2},{2,3},{3,0},{4,5},{5,6},{6,7},{7,4},{8,9},{9,10},{10,1... | collective-permute-start | bytes 786440 | tf_op jit(solution)/shard_map/ppermute | solution.py:679
  4.9 14.8 %collective-permute-start = (bf16[256,512]{1,0:T(8,128)(2,1)S(1)}, bf16[256,512]{1,0:T(8,128)(2,1)S(1)}, u32[]{:S(2)}, u32[]{:S(2)}) collective-permute-start(bf16[256,512]{1,0:T(8,128)(2,1)S(1)} %get-tuple-element.139.refs_0_), channel_id=1, source_target_pairs={{0,1},{1,2},{2,3},{3,0},{4,5},{5,6},{6,7},{7,4},{8,9},{9,10},{10,1... | collective-permute-start | bytes 786440 | tf_op jit(solution)/shard_map/ppermute | solution.py:679
  8.2 33.2 %copy-start.5 = (bf16[2048,512]{1,0:T(8,128)(2,1)S(1)}, bf16[2048,512]{1,0:T(8,128)(2,1)}, u32[]{:S(2)}) copy-start(bf16[2048,512]{1,0:T(8,128)(2,1)} %refs_12_.1) | copy-start | bytes 6291460
  8.4 32.9 %copy-start.4 = (bf16[2048,512]{1,0:T(8,128)(2,1)S(1)}, bf16[2048,512]{1,0:T(8,128)(2,1)}, u32[]{:S(2)}) copy-start(bf16[2048,512]{1,0:T(8,128)(2,1)} %refs_11_.1) | copy-start | bytes 6291460
  8.4 32.9 %copy-start.6 = (f32[2048]{0:T(1024)S(1)}, f32[2048]{0:T(1024)}, u32[]{:S(2)}) copy-start(f32[2048]{0:T(1024)} %param.20) | copy-start | bytes 24580
  14.1 11.2 %collective-permute-start.4 = (bf16[256,512]{1,0:T(8,128)(2,1)S(1)}, bf16[256,512]{1,0:T(8,128)(2,1)S(1)}, u32[]{:S(2)}, u32[]{:S(2)}) collective-permute-start(bf16[256,512]{1,0:T(8,128)(2,1)S(1)} %collective-permute-done.3.refs_5_), channel_id=1, source_target_pairs={{0,1},{1,2},{2,3},{3,0},{4,5},{5,6},{6,7},{7,4},{8,9},{9,10},{10,1... | collective-permute-start | bytes 786440 | tf_op jit(solution)/shard_map/ppermute | solution.py:679
  19.7 11.2 %collective-permute-start.1 = (bf16[256,512]{1,0:T(8,128)(2,1)S(1)}, bf16[256,512]{1,0:T(8,128)(2,1)S(1)}, u32[]{:S(2)}, u32[]{:S(2)}) collective-permute-start(bf16[256,512]{1,0:T(8,128)(2,1)S(1)} %collective-permute-done.refs_1_), channel_id=1, source_target_pairs={{0,1},{1,2},{2,3},{3,0},{4,5},{5,6},{6,7},{7,4},{8,9},{9,10},{10,1... | collective-permute-start | bytes 786440 | tf_op jit(solution)/shard_map/ppermute | solution.py:679
  25.3 11.2 %collective-permute-start.5 = (bf16[256,512]{1,0:T(8,128)(2,1)S(1)}, bf16[256,512]{1,0:T(8,128)(2,1)S(1)}, u32[]{:S(2)}, u32[]{:S(2)}) collective-permute-start(bf16[256,512]{1,0:T(8,128)(2,1)S(1)} %collective-permute-done.4.refs_6_), channel_id=1, source_target_pairs={{0,1},{1,2},{2,3},{3,0},{4,5},{5,6},{6,7},{7,4},{8,9},{9,10},{10,1... | collective-permute-start | bytes 786440 | tf_op jit(solution)/shard_map/ppermute | solution.py:679
  30.9 10.4 %collective-permute-start.2 = (bf16[256,512]{1,0:T(8,128)(2,1)S(1)}, bf16[256,512]{1,0:T(8,128)(2,1)S(1)}, u32[]{:S(2)}, u32[]{:S(2)}) collective-permute-start(bf16[256,512]{1,0:T(8,128)(2,1)S(1)} %collective-permute-done.1.refs_2_), channel_id=1, source_target_pairs={{0,1},{1,2},{2,3},{3,0},{4,5},{5,6},{6,7},{7,4},{8,9},{9,10},{10,1... | collective-permute-start | bytes 786440 | tf_op jit(solution)/shard_map/ppermute | solution.py:679
  31.0 23.7 %slice-start = ((s8[8388608]{0:T(1024)(128)(4,1)}), s8[4194304]{0:T(1024)(128)(4,1)S(1)}, s32[]{:S(2)}) async-start(s8[8388608]{0:T(1024)(128)(4,1)} %bitcast.25), calls=%async_computation | async-start | bytes 8388608
  41.3 11.2 %copy-start.10 = (bf16[512,512]{1,0:T(8,128)(2,1)S(1)}, bf16[512,512]{1,0:T(8,128)(2,1)}, u32[]{:S(2)}) copy-start(bf16[512,512]{1,0:T(8,128)(2,1)} %param.32) | copy-start | bytes 1572868
  41.4 13.3 %slice-start.1 = ((s8[8388608]{0:T(1024)(128)(4,1)}), s8[4194304]{0:T(1024)(128)(4,1)S(1)}, s32[]{:S(2)}) async-start(s8[8388608]{0:T(1024)(128)(4,1)} %bitcast.25), calls=%async_computation.1 | async-start | bytes 8388608
  49.0 16.9 %collective-permute-start.6 = (bf16[3,512,128]{2,1,0:T(8,128)(2,1)S(1)}, bf16[3,512,128]{2,1,0:T(8,128)(2,1)S(1)}, u32[]{:S(2)}, u32[]{:S(2)}) collective-permute-start(bf16[3,512,128]{2,1,0:T(8,128)(2,1)S(1)} %get-tuple-element.73), channel_id=1, source_target_pairs={{0,8},{4,12},{8,0},{12,4},{16,24},{20,28},{24,16},{28,20},{1,9},{5... | collective-permute-start | bytes 1179656 | tf_op jit(solution)/shard_map/ppermute | solution.py:701
  50.5 18.2 %collective-permute-start.7 = (bf16[3,512,128]{2,1,0:T(8,128)(2,1)S(1)}, bf16[3,512,128]{2,1,0:T(8,128)(2,1)S(1)}, u32[]{:S(2)}, u32[]{:S(2)}) collective-permute-start(bf16[3,512,128]{2,1,0:T(8,128)(2,1)S(1)} %get-tuple-element.74), channel_id=1, source_target_pairs={{0,16},{4,20},{8,24},{12,28},{16,0},{20,4},{24,8},{28,12},{1,17},{... | collective-permute-start | bytes 1179656 | tf_op jit(solution)/shard_map/ppermute | solution.py:701
  52.0 16.7 %collective-permute-start.8 = (bf16[3,512,128]{2,1,0:T(8,128)(2,1)S(1)}, bf16[3,512,128]{2,1,0:T(8,128)(2,1)S(1)}, u32[]{:S(2)}, u32[]{:S(2)}) collective-permute-start(bf16[3,512,128]{2,1,0:T(8,128)(2,1)S(1)} %get-tuple-element.75), channel_id=1, source_target_pairs={{0,24},{4,28},{8,16},{12,20},{16,8},{20,12},{24,0},{28,4},{1,25},{... | collective-permute-start | bytes 1179656 | tf_op jit(solution)/shard_map/ppermute | solution.py:701
  53.9 12.1 %collective-permute-start.9 = (bf16[512,256]{1,0:T(8,128)(2,1)S(1)}, bf16[512,256]{1,0:T(8,128)(2,1)S(1)}, u32[]{:S(2)}, u32[]{:S(2)}) collective-permute-start(bf16[512,256]{1,0:T(8,128)(2,1)S(1)} %constant_dynamic-slice_fusion.1), channel_id=1, source_target_pairs={{0,2},{1,3},{2,0},{3,1},{4,6},{5,7},{6,4},{7,5},{8,10},{9,11},{10,... | collective-permute-start | bytes 786440 | tf_op jit(solution)/shard_map/ppermute | solution.py:782
  60.3 13.6 %copy-start.11 = (s32[4096]{0:T(1024)S(1)}, s32[4096]{0:T(1024)}, u32[]{:S(2)}) copy-start(s32[4096]{0:T(1024)} %param.18) | copy-start | bytes 49156
  68.7 1.7 collective-permute-start.10
  68.7 3.2 %collective-permute-start.11 = (bf16[3,512,128]{2,1,0:T(8,128)(2,1)S(1)}, bf16[3,512,128]{2,1,0:T(8,128)(2,1)S(1)}, u32[]{:S(2)}, u32[]{:S(2)}) collective-permute-start(bf16[3,512,128]{2,1,0:T(8,128)(2,1)S(1)} %collective-permute-done.6.refs_1_), channel_id=1, source_target_pairs={{0,4},{4,0},{8,12},{12,8},{16,20},{20,16},{24,28},{28,24},{1,5},{5... | collective-permute-start | bytes 1179656 | tf_op jit(solution)/shard_map/ppermute | solution.py:709
  69.2 3.9 %collective-permute-start.12 = (bf16[3,512,128]{2,1,0:T(8,128)(2,1)S(1)}, bf16[3,512,128]{2,1,0:T(8,128)(2,1)S(1)}, u32[]{:S(2)}, u32[]{:S(2)}) collective-permute-start(bf16[3,512,128]{2,1,0:T(8,128)(2,1)S(1)} %collective-permute-done.7.refs_2_), channel_id=1, source_target_pairs={{0,4},{4,0},{8,12},{12,8},{16,20},{20,16},{24,28},{28,24},{1,5},{5... | collective-permute-start | bytes 1179656 | tf_op jit(solution)/shard_map/ppermute | solution.py:709
  69.2 4.9 %collective-permute-start.13 = (bf16[3,512,128]{2,1,0:T(8,128)(2,1)S(1)}, bf16[3,512,128]{2,1,0:T(8,128)(2,1)S(1)}, u32[]{:S(2)}, u32[]{:S(2)}) collective-permute-start(bf16[3,512,128]{2,1,0:T(8,128)(2,1)S(1)} %collective-permute-done.8.refs_3_), channel_id=1, source_target_pairs={{0,4},{4,0},{8,12},{12,8},{16,20},{20,16},{24,28},{28,24},{1,5},{5... | collective-permute-start | bytes 1179656 | tf_op jit(solution)/shard_map/ppermute | solution.py:709
  69.8 15.6 %collective-permute-start.14 = (bf16[2,512,256]{2,1,0:T(8,128)(2,1)S(1)}, bf16[2,512,256]{2,1,0:T(8,128)(2,1)S(1)}, u32[]{:S(2)}, u32[]{:S(2)}) collective-permute-start(bf16[2,512,256]{2,1,0:T(8,128)(2,1)S(1)} %pad_maximum_fusion), channel_id=1, source_target_pairs={{0,1},{1,0},{2,3},{3,2},{4,5},{5,4},{6,7},{7,6},{8,9},{9,8},{10,11... | collective-permute-start | bytes 1572872 | tf_op jit(solution)/shard_map/ppermute | solution.py:782
  70.5 12.3 %collective-permute-start.17 = (bf16[512,256]{1,0:T(8,128)(2,1)S(1)}, bf16[512,256]{1,0:T(8,128)(2,1)S(1)}, u32[]{:S(2)}, u32[]{:S(2)}) collective-permute-start(bf16[512,256]{1,0:T(8,128)(2,1)S(1)} %collective-permute-done.9.refs_10_), channel_id=1, source_target_pairs={{0,24},{4,28},{8,16},{12,20},{16,8},{20,12},{24,0},{28,4},{1,25},{... | collective-permute-start | bytes 786440 | tf_op jit(solution)/shard_map/ppermute | solution.py:701
  72.0 13.4 %collective-permute-start.16 = (bf16[512,256]{1,0:T(8,128)(2,1)S(1)}, bf16[512,256]{1,0:T(8,128)(2,1)S(1)}, u32[]{:S(2)}, u32[]{:S(2)}) collective-permute-start(bf16[512,256]{1,0:T(8,128)(2,1)S(1)} %collective-permute-done.9.refs_10_), channel_id=1, source_target_pairs={{0,16},{4,20},{8,24},{12,28},{16,0},{20,4},{24,8},{28,12},{1,17},{... | collective-permute-start | bytes 786440 | tf_op jit(solution)/shard_map/ppermute | solution.py:701
  73.2 12.3 %collective-permute-start.15 = (bf16[512,256]{1,0:T(8,128)(2,1)S(1)}, bf16[512,256]{1,0:T(8,128)(2,1)S(1)}, u32[]{:S(2)}, u32[]{:S(2)}) collective-permute-start(bf16[512,256]{1,0:T(8,128)(2,1)S(1)} %collective-permute-done.9.refs_10_), channel_id=1, source_target_pairs={{0,8},{4,12},{8,0},{12,4},{16,24},{20,28},{24,16},{28,20},{1,9},{5... | collective-permute-start | bytes 786440 | tf_op jit(solution)/shard_map/ppermute | solution.py:701
  82.7 53.7 %copy-start.7 = (f32[2048]{0:T(1024)S(1)}, f32[2048]{0:T(1024)}, u32[]{:S(2)}) copy-start(f32[2048]{0:T(1024)} %param.21) | copy-start | bytes 24580
  85.4 6.0 %collective-permute-start.18 = (bf16[512,128]{1,0:T(8,128)(2,1)S(1)}, bf16[512,128]{1,0:T(8,128)(2,1)S(1)}, u32[]{:S(2)}, u32[]{:S(2)}) collective-permute-start(bf16[512,128]{1,0:T(8,128)(2,1)S(1)} %get-tuple-element.93), channel_id=1, source_target_pairs={{0,8},{4,12},{8,0},{12,4},{16,24},{20,28},{24,16},{28,20},{1,9},{5... | collective-permute-start | bytes 393224 | tf_op jit(solution)/shard_map/ppermute | solution.py:701
  86.6 6.3 %collective-permute-start.19 = (bf16[512,128]{1,0:T(8,128)(2,1)S(1)}, bf16[512,128]{1,0:T(8,128)(2,1)S(1)}, u32[]{:S(2)}, u32[]{:S(2)}) collective-permute-start(bf16[512,128]{1,0:T(8,128)(2,1)S(1)} %get-tuple-element.94), channel_id=1, source_target_pairs={{0,16},{4,20},{8,24},{12,28},{16,0},{20,4},{24,8},{28,12},{1,17},{... | collective-permute-start | bytes 393224 | tf_op jit(solution)/shard_map/ppermute | solution.py:701
  87.4 7.1 %collective-permute-start.20 = (bf16[512,128]{1,0:T(8,128)(2,1)S(1)}, bf16[512,128]{1,0:T(8,128)(2,1)S(1)}, u32[]{:S(2)}, u32[]{:S(2)}) collective-permute-start(bf16[512,128]{1,0:T(8,128)(2,1)S(1)} %get-tuple-element.95), channel_id=1, source_target_pairs={{0,24},{4,28},{8,16},{12,20},{16,8},{20,12},{24,0},{28,4},{1,25},{... | collective-permute-start | bytes 393224 | tf_op jit(solution)/shard_map/ppermute | solution.py:701
  94.5 11.1 %collective-permute-start.21 = (bf16[2,512,128]{2,1,0:T(8,128)(2,1)S(1)}, bf16[2,512,128]{2,1,0:T(8,128)(2,1)S(1)}, u32[]{:S(2)}, u32[]{:S(2)}) collective-permute-start(bf16[2,512,128]{2,1,0:T(8,128)(2,1)S(1)} %pad_maximum_fusion.3.refs_0_), channel_id=1, source_target_pairs={{0,1},{1,2},{2,3},{3,0},{4,5},{5,6},{6,7},{7,4},{8,9},{9,10},{10,1... | collective-permute-start | bytes 786440 | tf_op jit(solution)/shard_map/ppermute | solution.py:679
  95.7 15.6 %collective-permute-start.24 = (bf16[2,512,128]{2,1,0:T(8,128)(2,1)S(1)}, bf16[2,512,128]{2,1,0:T(8,128)(2,1)S(1)}, u32[]{:S(2)}, u32[]{:S(2)}) collective-permute-start(bf16[2,512,128]{2,1,0:T(8,128)(2,1)S(1)} %pad_maximum_fusion.4.refs_4_), channel_id=1, source_target_pairs={{0,1},{1,2},{2,3},{3,0},{4,5},{5,6},{6,7},{7,4},{8,9},{9,10},{10,1... | collective-permute-start | bytes 786440 | tf_op jit(solution)/shard_map/ppermute | solution.py:679
  96.5 24.1 %collective-permute-start.29 = (bf16[2,512,256]{2,1,0:T(8,128)(2,1)S(1)}, bf16[2,512,256]{2,1,0:T(8,128)(2,1)S(1)}, u32[]{:S(2)}, u32[]{:S(2)}) collective-permute-start(bf16[2,512,256]{2,1,0:T(8,128)(2,1)S(1)} %collective-permute-done.14.refs_14_), channel_id=1, source_target_pairs={{0,24},{4,28},{8,16},{12,20},{16,8},{20,12},{24,0},{28,4},{1,25},{... | collective-permute-start | bytes 1572872 | tf_op jit(solution)/shard_map/ppermute | solution.py:701
  105.6 11.2 %collective-permute-start.22 = (bf16[2,512,128]{2,1,0:T(8,128)(2,1)S(1)}, bf16[2,512,128]{2,1,0:T(8,128)(2,1)S(1)}, u32[]{:S(2)}, u32[]{:S(2)}) collective-permute-start(bf16[2,512,128]{2,1,0:T(8,128)(2,1)S(1)} %collective-permute-done.21.refs_1_), channel_id=1, source_target_pairs={{0,1},{1,2},{2,3},{3,0},{4,5},{5,6},{6,7},{7,4},{8,9},{9,10},{10,1... | collective-permute-start | bytes 786440 | tf_op jit(solution)/shard_map/ppermute | solution.py:679
  105.6 15.4 %collective-permute-start.28 = (bf16[2,512,256]{2,1,0:T(8,128)(2,1)S(1)}, bf16[2,512,256]{2,1,0:T(8,128)(2,1)S(1)}, u32[]{:S(2)}, u32[]{:S(2)}) collective-permute-start(bf16[2,512,256]{2,1,0:T(8,128)(2,1)S(1)} %collective-permute-done.14.refs_14_), channel_id=1, source_target_pairs={{0,16},{4,20},{8,24},{12,28},{16,0},{20,4},{24,8},{28,12},{1,17},{... | collective-permute-start | bytes 1572872 | tf_op jit(solution)/shard_map/ppermute | solution.py:701
  106.5 14.6 %collective-permute-start.27 = (bf16[2,512,256]{2,1,0:T(8,128)(2,1)S(1)}, bf16[2,512,256]{2,1,0:T(8,128)(2,1)S(1)}, u32[]{:S(2)}, u32[]{:S(2)}) collective-permute-start(bf16[2,512,256]{2,1,0:T(8,128)(2,1)S(1)} %collective-permute-done.14.refs_14_), channel_id=1, source_target_pairs={{0,8},{4,12},{8,0},{12,4},{16,24},{20,28},{24,16},{28,20},{1,9},{5... | collective-permute-start | bytes 1572872 | tf_op jit(solution)/shard_map/ppermute | solution.py:701
  111.3 9.4 %collective-permute-start.25 = (bf16[2,512,128]{2,1,0:T(8,128)(2,1)S(1)}, bf16[2,512,128]{2,1,0:T(8,128)(2,1)S(1)}, u32[]{:S(2)}, u32[]{:S(2)}) collective-permute-start(bf16[2,512,128]{2,1,0:T(8,128)(2,1)S(1)} %collective-permute-done.24.refs_5_), channel_id=1, source_target_pairs={{0,1},{1,2},{2,3},{3,0},{4,5},{5,6},{6,7},{7,4},{8,9},{9,10},{10,1... | collective-permute-start | bytes 786440 | tf_op jit(solution)/shard_map/ppermute | solution.py:679
  116.9 19.5 %collective-permute-start.30 = (bf16[4,1,512,256]{3,2,0,1:T(8,128)(2,1)S(1)}, bf16[4,1,512,256]{3,2,0,1:T(8,128)(2,1)S(1)}, u32[]{:S(2)}, u32[]{:S(2)}) collective-permute-start(bf16[4,1,512,256]{3,2,0,1:T(8,128)(2,1)S(1)} %maximum_bitcast_fusion), channel_id=1, source_target_pairs={{0,4},{4,0},{8,12},{12,8},{16,20},{20,16},{24,28},{28,24},{1,5},{5... | collective-permute-start | bytes 3145736 | tf_op jit(solution)/shard_map/ppermute | solution.py:709
  120.6 11.0 %collective-permute-start.23 = (bf16[2,512,128]{2,1,0:T(8,128)(2,1)S(1)}, bf16[2,512,128]{2,1,0:T(8,128)(2,1)S(1)}, u32[]{:S(2)}, u32[]{:S(2)}) collective-permute-start(bf16[2,512,128]{2,1,0:T(8,128)(2,1)S(1)} %collective-permute-done.22.refs_2_), channel_id=1, source_target_pairs={{0,1},{1,2},{2,3},{3,0},{4,5},{5,6},{6,7},{7,4},{8,9},{9,10},{10,1... | collective-permute-start | bytes 786440 | tf_op jit(solution)/shard_map/ppermute | solution.py:679
  120.6 13.9 %collective-permute-start.26 = (bf16[2,512,128]{2,1,0:T(8,128)(2,1)S(1)}, bf16[2,512,128]{2,1,0:T(8,128)(2,1)S(1)}, u32[]{:S(2)}, u32[]{:S(2)}) collective-permute-start(bf16[2,512,128]{2,1,0:T(8,128)(2,1)S(1)} %collective-permute-done.25.refs_6_), channel_id=1, source_target_pairs={{0,1},{1,2},{2,3},{3,0},{4,5},{5,6},{6,7},{7,4},{8,9},{9,10},{10,1... | collective-permute-start | bytes 786440 | tf_op jit(solution)/shard_map/ppermute | solution.py:679
  121.0 13.4 %collective-permute-start.31 = (bf16[2,512,256]{2,1,0:T(8,128)(2,1)S(1)}, bf16[2,512,256]{2,1,0:T(8,128)(2,1)S(1)}, u32[]{:S(2)}, u32[]{:S(2)}) collective-permute-start(bf16[2,512,256]{2,1,0:T(8,128)(2,1)S(1)} %collective-permute-done.14.refs_14_), channel_id=1, source_target_pairs={{0,4},{4,0},{8,12},{12,8},{16,20},{20,16},{24,28},{28,24},{1,5},{5... | collective-permute-start | bytes 1572872 | tf_op jit(solution)/shard_map/ppermute | solution.py:709
  121.0 13.4 %collective-permute-start.34 = (bf16[2,512,256]{2,1,0:T(8,128)(2,1)S(1)}, bf16[2,512,256]{2,1,0:T(8,128)(2,1)S(1)}, u32[]{:S(2)}, u32[]{:S(2)}) collective-permute-start(bf16[2,512,256]{2,1,0:T(8,128)(2,1)S(1)} %collective-permute-done.29.refs_17_), channel_id=1, source_target_pairs={{0,4},{4,0},{8,12},{12,8},{16,20},{20,16},{24,28},{28,24},{1,5},{5... | collective-permute-start | bytes 1572872 | tf_op jit(solution)/shard_map/ppermute | solution.py:709
  131.7 2.8 %collective-permute-start.33 = (bf16[2,512,256]{2,1,0:T(8,128)(2,1)S(1)}, bf16[2,512,256]{2,1,0:T(8,128)(2,1)S(1)}, u32[]{:S(2)}, u32[]{:S(2)}) collective-permute-start(bf16[2,512,256]{2,1,0:T(8,128)(2,1)S(1)} %collective-permute-done.28.refs_16_), channel_id=1, source_target_pairs={{0,4},{4,0},{8,12},{12,8},{16,20},{20,16},{24,28},{28,24},{1,5},{5... | collective-permute-start | bytes 1572872 | tf_op jit(solution)/shard_map/ppermute | solution.py:709
  134.5 1.9 collective-permute-start.32
  158.5 12.9 %collective-permute-start.37 = (bf16[128,512]{1,0:T(8,128)(2,1)S(1)}, bf16[128,512]{1,0:T(8,128)(2,1)S(1)}, u32[]{:S(2)}, u32[]{:S(2)}) collective-permute-start(bf16[128,512]{1,0:T(8,128)(2,1)S(1)} %get-tuple-element.116), channel_id=1, source_target_pairs={{0,1},{1,2},{2,3},{3,0},{4,5},{5,6},{6,7},{7,4},{8,9},{9,10},{10,1... | collective-permute-start | bytes 393224 | tf_op jit(solution)/shard_map/ppermute | solution.py:692
  158.6 12.9 %collective-permute-start.38 = (bf16[128,512]{1,0:T(8,128)(2,1)S(1)}, bf16[128,512]{1,0:T(8,128)(2,1)S(1)}, u32[]{:S(2)}, u32[]{:S(2)}) collective-permute-start(bf16[128,512]{1,0:T(8,128)(2,1)S(1)} %get-tuple-element.117), channel_id=1, source_target_pairs={{0,2},{1,3},{2,0},{3,1},{4,6},{5,7},{6,4},{7,5},{8,10},{9,11},{10,... | collective-permute-start | bytes 393224 | tf_op jit(solution)/shard_map/ppermute | solution.py:692
  158.6 12.9 %collective-permute-start.39 = (bf16[128,512]{1,0:T(8,128)(2,1)S(1)}, bf16[128,512]{1,0:T(8,128)(2,1)S(1)}, u32[]{:S(2)}, u32[]{:S(2)}) collective-permute-start(bf16[128,512]{1,0:T(8,128)(2,1)S(1)} %get-tuple-element.118), channel_id=1, source_target_pairs={{0,3},{1,0},{2,1},{3,2},{4,7},{5,4},{6,5},{7,6},{8,11},{9,8},{10,9... | collective-permute-start | bytes 393224 | tf_op jit(solution)/shard_map/ppermute | solution.py:692
  165.8 19.1 %collective-permute-start.35 = (bf16[512,512]{1,0:T(8,128)(2,1)S(1)}, bf16[512,512]{1,0:T(8,128)(2,1)S(1)}, u32[]{:S(2)}, u32[]{:S(2)}) collective-permute-start(bf16[512,512]{1,0:T(8,128)(2,1)S(1)} %down.3), channel_id=1, source_target_pairs={{0,1},{1,0},{2,3},{3,2},{4,5},{5,4},{6,7},{7,6},{8,9},{9,8},{10,11... | collective-permute-start | bytes 1572872 | tf_op jit(solution)/shard_map/ppermute | solution.py:782
  172.6 14.9 %collective-permute-start.42 = (bf16[128,512]{1,0:T(8,128)(2,1)S(1)}, bf16[128,512]{1,0:T(8,128)(2,1)S(1)}, u32[]{:S(2)}, u32[]{:S(2)}) collective-permute-start(bf16[128,512]{1,0:T(8,128)(2,1)S(1)} %multiply_convert_fusion.3.refs_0_), channel_id=1, source_target_pairs={{0,3},{1,0},{2,1},{3,2},{4,7},{5,4},{6,5},{7,6},{8,11},{9,8},{10,9... | collective-permute-start | bytes 393224 | tf_op jit(solution)/shard_map/ppermute | solution.py:692
  175.5 12.0 %collective-permute-start.41 = (bf16[128,512]{1,0:T(8,128)(2,1)S(1)}, bf16[128,512]{1,0:T(8,128)(2,1)S(1)}, u32[]{:S(2)}, u32[]{:S(2)}) collective-permute-start(bf16[128,512]{1,0:T(8,128)(2,1)S(1)} %multiply_convert_fusion.3.refs_0_), channel_id=1, source_target_pairs={{0,2},{1,3},{2,0},{3,1},{4,6},{5,7},{6,4},{7,5},{8,10},{9,11},{10,... | collective-permute-start | bytes 393224 | tf_op jit(solution)/shard_map/ppermute | solution.py:692
  176.7 14.6 %collective-permute-start.40 = (bf16[128,512]{1,0:T(8,128)(2,1)S(1)}, bf16[128,512]{1,0:T(8,128)(2,1)S(1)}, u32[]{:S(2)}, u32[]{:S(2)}) collective-permute-start(bf16[128,512]{1,0:T(8,128)(2,1)S(1)} %multiply_convert_fusion.3.refs_0_), channel_id=1, source_target_pairs={{0,1},{1,2},{2,3},{3,0},{4,5},{5,6},{6,7},{7,4},{8,9},{9,10},{10,1... | collective-permute-start | bytes 393224 | tf_op jit(solution)/shard_map/ppermute | solution.py:692
  193.5 2.4 %collective-permute-start.43 = (bf16[4,208,512]{2,1,0:T(8,128)(2,1)S(1)}, bf16[4,208,512]{2,1,0:T(8,128)(2,1)S(1)}, u32[]{:S(2)}, u32[]{:S(2)}) collective-permute-start(bf16[4,208,512]{2,1,0:T(8,128)(2,1)S(1)} %get-tuple-element.124), channel_id=1, source_target_pairs={{0,4},{4,0},{8,12},{12,8},{16,20},{20,16},{24,28},{28,24},{1,5},{5... | collective-permute-start | bytes 2555912 | tf_op jit(solution)/shard_map/ppermute | solution.py:709
  196.1 8.2 %collective-permute-start.44 = (bf16[208,512]{1,0:T(8,128)(2,1)S(1)}, bf16[208,512]{1,0:T(8,128)(2,1)S(1)}, u32[]{:S(2)}, u32[]{:S(2)}) collective-permute-start(bf16[208,512]{1,0:T(8,128)(2,1)S(1)} %get-tuple-element.126), channel_id=1, source_target_pairs={{0,8},{4,12},{8,0},{12,4},{16,24},{20,28},{24,16},{28,20},{1,9},{5... | collective-permute-start | bytes 638984 | tf_op jit(solution)/shard_map/ppermute | solution.py:701
  196.2 11.9 %collective-permute-start.45 = (bf16[208,512]{1,0:T(8,128)(2,1)S(1)}, bf16[208,512]{1,0:T(8,128)(2,1)S(1)}, u32[]{:S(2)}, u32[]{:S(2)}) collective-permute-start(bf16[208,512]{1,0:T(8,128)(2,1)S(1)} %get-tuple-element.127), channel_id=1, source_target_pairs={{0,16},{4,20},{8,24},{12,28},{16,0},{20,4},{24,8},{28,12},{1,17},{... | collective-permute-start | bytes 638984 | tf_op jit(solution)/shard_map/ppermute | solution.py:701
  197.4 10.7 %collective-permute-start.46 = (bf16[208,512]{1,0:T(8,128)(2,1)S(1)}, bf16[208,512]{1,0:T(8,128)(2,1)S(1)}, u32[]{:S(2)}, u32[]{:S(2)}) collective-permute-start(bf16[208,512]{1,0:T(8,128)(2,1)S(1)} %get-tuple-element.128), channel_id=1, source_target_pairs={{0,24},{4,28},{8,16},{12,20},{16,8},{20,12},{24,0},{28,4},{1,25},{... | collective-permute-start | bytes 638984 | tf_op jit(solution)/shard_map/ppermute | solution.py:701
  199.8 25.3 %collective-permute-start.48 = (bf16[512,512]{1,0:T(8,128)(2,1)S(1)}, bf16[512,512]{1,0:T(8,128)(2,1)S(1)}, u32[]{:S(2)}, u32[]{:S(2)}) collective-permute-start(bf16[512,512]{1,0:T(8,128)(2,1)S(1)} %add_convert_fusion.1), channel_id=1, source_target_pairs={{0,2},{1,3},{2,0},{3,1},{4,6},{5,7},{6,4},{7,5},{8,10},{9,11},{10,... | collective-permute-start | bytes 1572872 | tf_op jit(solution)/shard_map/ppermute | solution.py:782
  200.4 24.8 %collective-permute-start.36 = (bf16[512,512]{1,0:T(8,128)(2,1)S(1)}, bf16[512,512]{1,0:T(8,128)(2,1)S(1)}, u32[]{:S(2)}, u32[]{:S(2)}) collective-permute-start(bf16[512,512]{1,0:T(8,128)(2,1)S(1)} %get-tuple-element.113), channel_id=1, source_target_pairs={{0,1},{1,0},{2,3},{3,2},{4,5},{5,4},{6,7},{7,6},{8,9},{9,8},{10,11... | collective-permute-start | bytes 1572872 | tf_op jit(solution)/shard_map/ppermute | solution.py:782
  208.2 16.9 %collective-permute-start.47 = (bf16[208,512]{1,0:T(8,128)(2,1)S(1)}, bf16[208,512]{1,0:T(8,128)(2,1)S(1)}, u32[]{:S(2)}, u32[]{:S(2)}) collective-permute-start(bf16[208,512]{1,0:T(8,128)(2,1)S(1)} %add_convert_fusion.2.refs_0_), channel_id=1, source_target_pairs={{0,24},{4,28},{8,16},{12,20},{16,8},{20,12},{24,0},{28,4},{1,25},{... | collective-permute-start | bytes 638984 | tf_op jit(solution)/shard_map/ppermute | solution.py:701
  209.8 15.8 %collective-permute-start.50 = (bf16[208,512]{1,0:T(8,128)(2,1)S(1)}, bf16[208,512]{1,0:T(8,128)(2,1)S(1)}, u32[]{:S(2)}, u32[]{:S(2)}) collective-permute-start(bf16[208,512]{1,0:T(8,128)(2,1)S(1)} %add_convert_fusion.2.refs_0_), channel_id=1, source_target_pairs={{0,16},{4,20},{8,24},{12,28},{16,0},{20,4},{24,8},{28,12},{1,17},{... | collective-permute-start | bytes 638984 | tf_op jit(solution)/shard_map/ppermute | solution.py:701
  211.4 14.3 %collective-permute-start.49 = (bf16[208,512]{1,0:T(8,128)(2,1)S(1)}, bf16[208,512]{1,0:T(8,128)(2,1)S(1)}, u32[]{:S(2)}, u32[]{:S(2)}) collective-permute-start(bf16[208,512]{1,0:T(8,128)(2,1)S(1)} %add_convert_fusion.2.refs_0_), channel_id=1, source_target_pairs={{0,8},{4,12},{8,0},{12,4},{16,24},{20,28},{24,16},{28,20},{1,9},{5... | collective-permute-start | bytes 638984 | tf_op jit(solution)/shard_map/ppermute | solution.py:701
  225.1 2.1 collective-permute-start.51
  225.2 2.2 collective-permute-start.54
  225.6 1.6 collective-permute-start.53
  225.8 1.7 collective-permute-start.52
  (6 other events, 23.7 us)

commit v10 on v9

--- a/solution.py
+++ b/solution.py
@@ -188,7 +188,7 @@
     blocks = [refs[:ring], refs[ring : 2 * ring]]
     gain_ref, cos_ref, sin_ref, *sources = refs[2 * ring : 2 * ring + 6]
     outs = refs[2 * ring + 6 : 2 * ring + 6 + heads]
-    tok_ref, normed, made, weights, sems = refs[2 * ring + 6 + heads :]
+    tok_ref, stamp_ref, normed, made, weights, sems = refs[2 * ring + 6 + heads :]
     half, width = blocks[0][0].shape
     depth = gain_ref.shape[1]
     copies = [
@@ -221,6 +221,7 @@
             made[h, kind] = head.astype(BF16)
     for f in range(heads):
         outs[f][...] = made[info_ref[ring + 1] ^ f]
+    stamp_ref[...] = jnp.zeros_like(stamp_ref)
 
 
 def qkv_call(info, blocks, gain, cosine, sine, *weights):
@@ -233,14 +234,14 @@
             qkv_kernel, ring=ring, heads=heads, factor=HD ** (-0.5) * math.log2(math.e)
         ),
         out_shape=[jax.ShapeDtypeStruct((3, rows, HD), BF16)] * heads
-        + [jax.ShapeDtypeStruct((rows, depth), BF16)],
+        + [jax.ShapeDtypeStruct((rows, depth), BF16), jax.ShapeDtypeStruct((8, HD), F32)],
         grid_spec=pltpu.PrefetchScalarGridSpec(
             num_scalar_prefetch=1,
             grid=(1,),
             in_specs=[whole((half, width))] * (2 * ring)
             + [whole((1, depth)), whole((rows, HD)), whole((rows, HD))]
             + [pl.BlockSpec(memory_space=pl.ANY)] * 3,
-            out_specs=[whole((3, rows, HD))] * heads + [whole((rows, depth))],
+            out_specs=[whole((3, rows, HD))] * heads + [whole((rows, depth)), whole((8, HD))],
             scratch_shapes=[
                 pltpu.VMEM((rows, depth), BF16),
                 pltpu.VMEM((heads, 3, rows, HD), BF16),
@@ -252,13 +253,13 @@
         cost_estimate=cost(6 * rows * depth * out_cols, 6 * depth * out_cols),
         name="qkv",
     )(info, *blocks[0], *blocks[1], gain, cosine, sine, *weights)
-    return result[:heads], result[heads]
+    return result[:heads], result[heads], result[heads + 1]
 
 
 def attention_kernel(first_ref, info_ref, *refs, chips, ring):
     own, other = refs[:chips], refs[chips : 2 * chips]
-    outs = refs[2 * chips : 3 * chips]
-    keys_all, values_all = refs[3 * chips :]
+    outs = refs[2 * chips + 1 : 3 * chips + 1]
+    keys_all, values_all = refs[3 * chips + 1 :]
     chip, core = info_ref[ring + 1], info_ref[ring + 2]
     span = outs[0].shape[0]
     for f in range(chips):
@@ -286,7 +287,8 @@
 
         def body(at, carry, masked, query=query, row=row, start=start, lane=lane):
             peak, denom, accum = carry
-            scores = dot_over(keys_all[at], query, (1, 1))
+            count = lane.shape[0]
+            scores = dot_over(keys_all[at, :count], query, (1, 1))
             if masked:
                 column = lane + at * span
                 allowed = (column >= start) & (column <= row)
@@ -297,7 +299,7 @@
                 weights = jnp.where(allowed, weights, 0.0)
             keep = jnp.exp2(peak - new_peak)
             denom = denom * keep + jnp.sum(weights, axis=0, keepdims=True)
-            accum = accum * keep + dot(values_all[at], weights.astype(BF16))
+            accum = accum * keep + dot(values_all[at, :, :count], weights.astype(BF16))
             return new_peak, denom, accum
 
         def pair(turn, carry, query=query, full=None):
@@ -327,11 +329,16 @@
         carry = lax.fori_loop(0, turns, functools.partial(pair, full=full), carry)
         rest = full + 2 * turns
         carry = lax.fori_loop(rest, last, functools.partial(body, masked=False), carry)
-        _, denom, accum = body(last, carry, masked=True)
-        outs[f][...] = (accum / denom).T.astype(BF16)
-
-
-def attention_call(first, info, own, other, ring):
+        half = span // 2
+        for at in (slice(0, half), slice(half, span)):
+            part = tuple(value[:, at] for value in carry)
+            _, denom, accum = body(
+                last, part, True, query[at], row[:, at], start[:, at], lane[: at.stop]
+            )
+            outs[f][at] = (accum / denom).T.astype(BF16)
+
+
+def attention_call(first, info, own, other, stamp, ring):
     chips = len(own)
     _, rows, _ = own[0].shape
     return pl.pallas_call(
@@ -340,7 +347,7 @@
         grid_spec=pltpu.PrefetchScalarGridSpec(
             num_scalar_prefetch=2,
             grid=(1,),
-            in_specs=[whole((3, rows, HD))] * (2 * chips),
+            in_specs=[whole((3, rows, HD))] * (2 * chips) + [whole(stamp.shape)],
             out_specs=[whole((rows, HD))] * chips,
             scratch_shapes=[
                 pltpu.VMEM((2 * chips, rows, HD), BF16),
@@ -354,7 +361,7 @@
             chips * rows * chips * rows,
         ),
         name="attention",
-    )(first, info, *own, *other)
+    )(first, info, *own, *other, stamp)
 
 
 def middle_kernel(info_ref, *refs, ring, chips):
@@ -760,13 +767,11 @@
         series_ids[None, :] < jnp.arange(SERIES, dtype=jnp.int32)[:, None], axis=1, dtype=jnp.int32
     )
 
-    made, tok_full = qkv_call(
+    made, tok_full, stamp = qkv_call(
         info, token_rings, norm_gain[None, :], cosine, sine, w_query, w_key, w_value
     )
 
-    student_normed, projected, tok_full = lax.optimization_barrier(
-        (student_normed, projector, tok_full)
-    )
+    student_normed, projected, stamp = lax.optimization_barrier((student_normed, projector, stamp))
     s_gate_out = dot(student_normed, s_gate)
     s_up_out = dot(student_normed, s_up)
     sigmoid_gate = jax.nn.sigmoid(s_gate_out)
@@ -781,7 +786,7 @@
 
     over = lambda value, bit: lax.ppermute(value, "tensor", [(i, i ^ bit) for i in range(ring)])
     w_slice = lax.dynamic_slice(w_out, [zero, starts[1]], (w_out.shape[0], slice_cols))
-    w_slice, tok_full, _ = lax.optimization_barrier((w_slice, tok_full, s_gate_out))
+    w_slice, stamp, _ = lax.optimization_barrier((w_slice, stamp, s_gate_out))
     w_first = over(w_slice, 2)
 
     own = flipped(made)
@@ -789,9 +794,9 @@
     w_rest = over(jnp.stack([w_slice, w_first]), 1)
     other = [swapped(a) for a in own]
     near_first = flipped([w_first] * chips)
-    made = attention_call(below, info, own, other, ring)
-    *made, w_rest = lax.optimization_barrier((*made, w_rest, *near_first))[: chips + 1]
-    attended = lax.optimization_barrier(tuple(flipped(made)))
+    made = attention_call(below, info, own, other, stamp, ring)
+    attended = lax.optimization_barrier((*flipped(made), w_rest, *near_first))
+    w_rest, near_first, attended = attended[chips], attended[chips + 1 :], attended[:chips]
     parts = [
         ring_gather(jnp.stack(attended[k : k + chips // 2]), "tensor") for k in (0, chips // 2)
     ]

time: 232 us -> 233 us (level)
  transfers between devices with their start and end apart: 55 -> 55, of which waited for: 32 -> 30; matrix products, arithmetic and copies ran while one was open for 6% -> 6% of each run, Pallas kernels for 7% -> 7%
where the time goes in v10:
time: 233 us; the launch traced here: 235 us
  waiting for transfers between devices  117 us (50%)
  Pallas kernels  50.4 us (22%)
  starting transfers between devices  45.5 us (20%)
  matrix products  7.34 us (3%)
  other arithmetic  6.12 us (3%)
  local copies, waits for them, and re-layouts  5.76 us (2%)
  between operations  2.76 us (1%)
    ppermute x12, waiting for transfers between devices, step_on(): return lax.ppermute(block, axis, [(i, (i + 1) % size) for i in range(size)])  64.5 us
    ppermute x5, waiting for transfers between devices, paired(): lax.ppermute(value, 'tensor', [(i, i ^ bit) for i in range(ring)])  26.6 us
    ppermute x18, starting transfers between devices, flipped(): lax.ppermute(pieces[f], 'dp', [(i, i ^ 2 * f) for i in range(size)])  22.6 us
    pallas_call x1, Pallas kernels, middle_call(): pl.pallas_call(functools.partial(middle_kernel, ring=ring, chips=chips),...  22.1 us
    ppermute x18, waiting for transfers between devices, flipped(): lax.ppermute(pieces[f], 'dp', [(i, i ^ 2 * f) for i in range(size)])  14.5 us
    pallas_call x1, Pallas kernels, attention_call(): pl.pallas_call(functools.partial(attention_kernel, chips=chips, ring=ring...  10.3 us
    ppermute x6, starting transfers between devices, shifted(): lax.ppermute(pieces[s], axis, [(i, (i + s) % size) for i in range(size)])  7.97 us
    ppermute x12, starting transfers between devices, step_on(): return lax.ppermute(block, axis, [(i, (i + 1) % size) for i in range(size)])  7.8 us
  transfers between devices with their start and end apart: 55, of which 30 were waited for; matrix products, arithmetic and copies ran while one was open for 6% of the time, Pallas kernels for 7%

profile of v10, /device:TPU:0, one launch (start us, length us, event | category | flops | bytes accessed | tf_op | source)
XLA Modules:
  0.0 235.1 jit_solution(27501529671659387)
XLA Ops:
  0.7 1.1 fusion.10
  1.8 3.1 %collective-permute-start.3 = (bf16[256,512]{1,0:T(8,128)(2,1)S(1)}, bf16[256,512]{1,0:T(8,128)(2,1)S(1)}, u32[]{:S(2)}, u32[]{:S(2)}) collective-permute-start(bf16[256,512]{1,0:T(8,128)(2,1)S(1)} %get-tuple-element.140.refs_4_), channel_id=1, source_target_pairs={{0,1},{1,2},{2,3},{3,0},{4,5},{5,6},{6,7},{7,4},{8,9},{9,10},{10,1... | collective-permute-start | bytes 786440 | tf_op jit(solution)/shard_map/ppermute | solution.py:686
  4.9 1.6 collective-permute-start
  7.2 1.0 fusion.3
  8.6 5.5 %collective-permute-done.3.refs_5_ = bf16[256,512]{1,0:T(8,128)(2,1)S(1)} collective-permute-done((bf16[256,512]{1,0:T(8,128)(2,1)S(1)}, bf16[256,512]{1,0:T(8,128)(2,1)S(1)}, u32[]{:S(2)}, u32[]{:S(2)}) %collective-permute-start.3) | collective-permute-done | bytes 262176 | tf_op jit(solution)/shard_map/ppermute | solution.py:686
  14.1 5.6 %collective-permute-done.refs_1_ = bf16[256,512]{1,0:T(8,128)(2,1)S(1)} collective-permute-done((bf16[256,512]{1,0:T(8,128)(2,1)S(1)}, bf16[256,512]{1,0:T(8,128)(2,1)S(1)}, u32[]{:S(2)}, u32[]{:S(2)}) %collective-permute-start) | collective-permute-done | bytes 262176 | tf_op jit(solution)/shard_map/ppermute | solution.py:686
  19.7 1.1 constant_dynamic-slice_fusion.1
  20.9 1.1 convert_element_type.98
  22.0 3.3 %collective-permute-done.4.refs_6_ = bf16[256,512]{1,0:T(8,128)(2,1)S(1)} collective-permute-done((bf16[256,512]{1,0:T(8,128)(2,1)S(1)}, bf16[256,512]{1,0:T(8,128)(2,1)S(1)}, u32[]{:S(2)}, u32[]{:S(2)}) %collective-permute-start.4) | collective-permute-done | bytes 262176 | tf_op jit(solution)/shard_map/ppermute | solution.py:686
  25.3 5.6 %collective-permute-done.1.refs_2_ = bf16[256,512]{1,0:T(8,128)(2,1)S(1)} collective-permute-done((bf16[256,512]{1,0:T(8,128)(2,1)S(1)}, bf16[256,512]{1,0:T(8,128)(2,1)S(1)}, u32[]{:S(2)}, u32[]{:S(2)}) %collective-permute-start.1) | collective-permute-done | bytes 262176 | tf_op jit(solution)/shard_map/ppermute | solution.py:686
  31.1 5.4 %collective-permute-done.5.refs_7_ = bf16[256,512]{1,0:T(8,128)(2,1)S(1)} collective-permute-done((bf16[256,512]{1,0:T(8,128)(2,1)S(1)}, bf16[256,512]{1,0:T(8,128)(2,1)S(1)}, u32[]{:S(2)}, u32[]{:S(2)}) %collective-permute-start.5) | collective-permute-done | bytes 262176 | tf_op jit(solution)/shard_map/ppermute | solution.py:686
  36.5 4.8 %collective-permute-done.2.refs_3_ = bf16[256,512]{1,0:T(8,128)(2,1)S(1)} collective-permute-done((bf16[256,512]{1,0:T(8,128)(2,1)S(1)}, bf16[256,512]{1,0:T(8,128)(2,1)S(1)}, u32[]{:S(2)}, u32[]{:S(2)}) %collective-permute-start.2) | collective-permute-done | bytes 262176 | tf_op jit(solution)/shard_map/ppermute | solution.py:686
  41.4 6.4 %qkv.1 = (bf16[3,512,128]{2,1,0:T(8,128)(2,1)S(1)}, bf16[3,512,128]{2,1,0:T(8,128)(2,1)S(1)}, bf16[3,512,128]{2,1,0:T(8,128)(2,1)S(1)}, bf16[3,512,128]{2,1,0:T(...) custom-call(s32[16]{0:T(128)S(1)} %fusion.9.info_ref, ...), custom_call_target="tpu_custom_call" | custom-call | flops 3221225472 | bytes 6291456 | tf_op jit(solution)/shard_map/qkv/pallas_call | solution.py:232
  47.7 1.3 copy-done.8
  49.0 1.5 collective-permute-start.6
  50.5 1.5 collective-permute-start.7
  53.0 0.8 multiply_convert_fusion
  54.7 5.6 %fusion.refs_26_ = bf16[2048,512]{1,0:T(8,128)(2,1)} fusion(bf16[2048,2048]{1,0:T(8,128)(2,1)S(1)} %bitcast.27, bf16[2048,512]{1,0:T(8,128)(2,1)S(1)} %copy-done.12), kind=kOutput, calls=%fused_computation.1 | convolution fusion | flops 4296015872 | bytes 12582912 | tf_op jit(solution)/shard_map/dot_general | solution.py:166
  60.7 5.2 %collective-permute-done.9.refs_10_ = bf16[512,256]{1,0:T(8,128)(2,1)S(1)} collective-permute-done((bf16[512,256]{1,0:T(8,128)(2,1)S(1)}, bf16[512,256]{1,0:T(8,128)(2,1)S(1)}, u32[]{:S(2)}, u32[]{:S(2)}) %collective-permute-start.9) | collective-permute-done | bytes 262176 | tf_op jit(solution)/shard_map/ppermute | solution.py:787
  65.9 2.8 %collective-permute-done.7.refs_2_ = bf16[3,512,128]{2,1,0:T(8,128)(2,1)S(1)} collective-permute-done((bf16[3,512,128]{2,1,0:T(8,128)(2,1)S(1)}, bf16[3,512,128]{2,1,0:T(8,128)(2,1)S(1)}, u32[]{:S(2)}, u32[]{:S(2)}) %collective-permute-start.7) | collective-permute-done | bytes 393248 | tf_op jit(solution)/shard_map/ppermute | solution.py:708
  70.5 1.5 collective-permute-start.20
  72.0 1.2 collective-permute-start.19
  73.3 0.9 collective-permute-start.18
  74.2 10.3 %attention.1 = (bf16[512,128]{1,0:T(8,128)(2,1)S(1)}, bf16[512,128]{1,0:T(8,128)(2,1)S(1)}, bf16[512,128]{1,0:T(8,128)(2,1)S(1)}, bf16[512,128]{1,0:T(8,128)(2,1)S(1)}) custom-call(s32[8]{0:T(128)S(1)} %convert_reduce_fusion.first_ref, s32[16]{0:T(128)S(1)} %fusion.9.info_ref, bf16[3,512,128]{2,1,0:T(8,128)(2,1)S(1)} %get-tuple-element.84.refs_0_, ...), custom_call_target="tpu_custom_call" | custom-call | flops 2147483648 | bytes 4194304 | tf_op jit(solution)/shard_map/attention/pallas_call | solution.py:344
  84.5 1.3 collective-permute-start.14
  86.6 1.4 collective-permute-start.16
  88.1 1.7 collective-permute-done.14
  89.8 1.8 collective-permute-done.15
  91.6 2.3 collective-permute-done.16
  94.0 1.8 collective-permute-start.21
  95.8 0.8 collective-permute-start.24
  96.6 2.2 collective-permute-start.29
  98.8 6.2 %collective-permute-done.21.refs_1_ = bf16[2,512,128]{2,1,0:T(8,128)(2,1)S(1)} collective-permute-done((bf16[2,512,128]{2,1,0:T(8,128)(2,1)S(1)}, bf16[2,512,128]{2,1,0:T(8,128)(2,1)S(1)}, u32[]{:S(2)}, u32[]{:S(2)}) %collective-permute-start.21) | collective-permute-done | bytes 262176 | tf_op jit(solution)/shard_map/ppermute | solution.py:686
  105.0 1.2 collective-permute-start.28
  106.2 1.5 collective-permute-start.27
  107.7 2.9 %collective-permute-done.24.refs_5_ = bf16[2,512,128]{2,1,0:T(8,128)(2,1)S(1)} collective-permute-done((bf16[2,512,128]{2,1,0:T(8,128)(2,1)S(1)}, bf16[2,512,128]{2,1,0:T(8,128)(2,1)S(1)}, u32[]{:S(2)}, u32[]{:S(2)}) %collective-permute-start.24) | collective-permute-done | bytes 262176 | tf_op jit(solution)/shard_map/ppermute | solution.py:686
  110.8 5.5 %collective-permute-done.22.refs_2_ = bf16[2,512,128]{2,1,0:T(8,128)(2,1)S(1)} collective-permute-done((bf16[2,512,128]{2,1,0:T(8,128)(2,1)S(1)}, bf16[2,512,128]{2,1,0:T(8,128)(2,1)S(1)}, u32[]{:S(2)}, u32[]{:S(2)}) %collective-permute-start.22) | collective-permute-done | bytes 262176 | tf_op jit(solution)/shard_map/ppermute | solution.py:686
  116.2 5.5 %collective-permute-done.25.refs_6_ = bf16[2,512,128]{2,1,0:T(8,128)(2,1)S(1)} collective-permute-done((bf16[2,512,128]{2,1,0:T(8,128)(2,1)S(1)}, bf16[2,512,128]{2,1,0:T(8,128)(2,1)S(1)}, u32[]{:S(2)}, u32[]{:S(2)}) %collective-permute-start.25) | collective-permute-done | bytes 262176 | tf_op jit(solution)/shard_map/ppermute | solution.py:686
  123.1 9.6 %collective-permute-done.23.refs_3_ = bf16[2,512,128]{2,1,0:T(8,128)(2,1)S(1)} collective-permute-done((bf16[2,512,128]{2,1,0:T(8,128)(2,1)S(1)}, bf16[2,512,128]{2,1,0:T(8,128)(2,1)S(1)}, u32[]{:S(2)}, u32[]{:S(2)}) %collective-permute-start.23) | collective-permute-done | bytes 262176 | tf_op jit(solution)/shard_map/ppermute | solution.py:686
  132.7 4.7 %collective-permute-done.26.refs_7_ = bf16[2,512,128]{2,1,0:T(8,128)(2,1)S(1)} collective-permute-done((bf16[2,512,128]{2,1,0:T(8,128)(2,1)S(1)}, bf16[2,512,128]{2,1,0:T(8,128)(2,1)S(1)}, u32[]{:S(2)}, u32[]{:S(2)}) %collective-permute-start.26) | collective-permute-done | bytes 262176 | tf_op jit(solution)/shard_map/ppermute | solution.py:686
  137.4 1.9 collective-permute-done.32.refs_20_
  139.3 22.1 %middle.1 = (bf16[512,2048]{1,0:T(8,128)(2,1)}, bf16[512,512]{1,0:T(8,128)(2,1)S(1)}, bf16[128,512]{1,0:T(8,128)(2,1)S(1)}, bf16[128,512]{1,0:T(8,128)(2,1)S(1)}...) custom-call(s32[16]{0:T(128)S(1)} %fusion.9.info_ref, bf16[2,512,128]{2,1,0:T(8,128)(2,1)S(1)} %pad_maximum_fusion.3.refs_0_, ...), custom_call_target="tpu_custom_call" | custom-call | flops 14227079168 | bytes 25165824 | tf_op jit(solution)/shard_map/middle/pallas_call | solution.py:489
  161.6 3.7 %collective-permute-start.39 = (bf16[128,512]{1,0:T(8,128)(2,1)S(1)}, bf16[128,512]{1,0:T(8,128)(2,1)S(1)}, u32[]{:S(2)}, u32[]{:S(2)}) collective-permute-start(bf16[128,512]{1,0:T(8,128)(2,1)S(1)} %get-tuple-element.120), channel_id=1, source_target_pairs={{0,3},{1,0},{2,1},{3,2},{4,7},{5,4},{6,5},{7,6},{8,11},{9,8},{10,9... | collective-permute-start | bytes 393224 | tf_op jit(solution)/shard_map/ppermute | solution.py:699
  165.3 1.6 copy-done.2
  166.9 1.8 down.3
  169.3 5.0 %down.2 = (bf16[512,512]{1,0:T(8,128)(2,1)S(1)}, bf16[512,512]{1,0:T(8,128)(2,1)S(1)}, bf16[512,512]{1,0:T(8,128)(2,1)S(1)}) custom-call(s32[16]{0:T(128)S(1)} %fusion.9.info_ref, bf16[512,2048]{1,0:T(8,128)(2,1)S(1)} %copy-done.2, bf16[2048,2048]{1,0:T(8,128)(2,1)S(1)} %bitcast.27), custom_call_target="tpu_custom_call" | custom-call | flops 3221225472 | bytes 6291456 | tf_op jit(solution)/shard_map/down/pallas_call | solution.py:563
  174.4 1.1 multiply_convert_fusion.3.refs_0_
  175.5 2.9 %collective-permute-start.42 = (bf16[128,512]{1,0:T(8,128)(2,1)S(1)}, bf16[128,512]{1,0:T(8,128)(2,1)S(1)}, u32[]{:S(2)}, u32[]{:S(2)}) collective-permute-start(bf16[128,512]{1,0:T(8,128)(2,1)S(1)} %multiply_convert_fusion.3.refs_0_), channel_id=1, source_target_pairs={{0,3},{1,0},{2,1},{3,2},{4,7},{5,4},{6,5},{7,6},{8,11},{9,8},{10,9... | collective-permute-start | bytes 393224 | tf_op jit(solution)/shard_map/ppermute | solution.py:699
  178.4 1.2 collective-permute-start.41
  179.6 8.1 %collective-permute-done.35 = bf16[512,512]{1,0:T(8,128)(2,1)S(1)} collective-permute-done((bf16[512,512]{1,0:T(8,128)(2,1)S(1)}, bf16[512,512]{1,0:T(8,128)(2,1)S(1)}, u32[]{:S(2)}, u32[]{:S(2)}) %collective-permute-start.35) | collective-permute-done | bytes 524320 | tf_op jit(solution)/shard_map/ppermute | solution.py:787
  187.7 2.7 %collective-permute-done.42.refs_3_ = bf16[128,512]{1,0:T(8,128)(2,1)S(1)} collective-permute-done((bf16[128,512]{1,0:T(8,128)(2,1)S(1)}, bf16[128,512]{1,0:T(8,128)(2,1)S(1)}, u32[]{:S(2)}, u32[]{:S(2)}) %collective-permute-start.42) | collective-permute-done | bytes 131104 | tf_op jit(solution)/shard_map/ppermute | solution.py:699
  190.4 3.7 %collective-permute-done.40.refs_1_ = bf16[128,512]{1,0:T(8,128)(2,1)S(1)} collective-permute-done((bf16[128,512]{1,0:T(8,128)(2,1)S(1)}, bf16[128,512]{1,0:T(8,128)(2,1)S(1)}, u32[]{:S(2)}, u32[]{:S(2)}) %collective-permute-start.40) | collective-permute-done | bytes 131104 | tf_op jit(solution)/shard_map/ppermute | solution.py:699
  194.2 2.2 grads.1
  196.4 2.4 %collective-permute-done.43.theirs_ref = bf16[4,208,512]{2,1,0:T(8,128)(2,1)S(1)} collective-permute-done((bf16[4,208,512]{2,1,0:T(8,128)(2,1)S(1)}, bf16[4,208,512]{2,1,0:T(8,128)(2,1)S(1)}, u32[]{:S(2)}, u32[]{:S(2)}) %collective-permute-start.43) | collective-permute-done | bytes 852000 | tf_op jit(solution)/shard_map/ppermute | solution.py:716
  199.6 1.6 collective-permute-start.45
  201.2 1.4 collective-permute-start.46
  203.3 2.5 %collective-permute-start.36 = (bf16[512,512]{1,0:T(8,128)(2,1)S(1)}, bf16[512,512]{1,0:T(8,128)(2,1)S(1)}, u32[]{:S(2)}, u32[]{:S(2)}) collective-permute-start(bf16[512,512]{1,0:T(8,128)(2,1)S(1)} %get-tuple-element.115), channel_id=1, source_target_pairs={{0,1},{1,0},{2,3},{3,2},{4,5},{5,4},{6,7},{7,6},{8,9},{9,8},{10,11... | collective-permute-start | bytes 1572872 | tf_op jit(solution)/shard_map/ppermute | solution.py:787
  205.8 1.3 collective-permute-done.44
  207.1 4.1 %collective-permute-done.45 = bf16[208,512]{1,0:T(8,128)(2,1)S(1)} collective-permute-done((bf16[208,512]{1,0:T(8,128)(2,1)S(1)}, bf16[208,512]{1,0:T(8,128)(2,1)S(1)}, u32[]{:S(2)}, u32[]{:S(2)}) %collective-permute-start.45) | collective-permute-done | bytes 213024 | tf_op jit(solution)/shard_map/ppermute | solution.py:708
  211.3 1.6 collective-permute-start.47
  212.9 1.4 collective-permute-start.50
  214.9 13.1 %collective-permute-done.48 = bf16[512,512]{1,0:T(8,128)(2,1)S(1)} collective-permute-done((bf16[512,512]{1,0:T(8,128)(2,1)S(1)}, bf16[512,512]{1,0:T(8,128)(2,1)S(1)}, u32[]{:S(2)}, u32[]{:S(2)}) %collective-permute-start.48) | collective-permute-done | bytes 524320 | tf_op jit(solution)/shard_map/ppermute | solution.py:787
  229.0 1.1 add_convert_fusion
  230.4 2.4 %finish.1 = (f32[512,512]{1,0:T(8,128)}, f32[512,512]{1,0:T(8,128)}, f32[512,512]{1,0:T(8,128)}, f32[8,16,128]{2,1,0:T(8,128)S(1)}) custom-call(s32[16]{0:T(128)S(1)} %fusion.9.info_ref, bf16[208,512]{1,0:T(8,128)(2,1)S(1)} %add_convert_fusion.2.refs_0_, bf16[208,512]{1,0:T(8,128)(2,1)S(1)} %collective-permute-done.49.refs_1_, ...), custom_call_target="tpu_custom_call" | custom-call | flops 262144 | bytes 3145728 | tf_op jit(solution)/shard_map/finish/pallas_call | solution.py:668
  (110 shorter events, 12.9 us)
Async XLA Ops:
  0.6 52.3 %copy-start = (bf16[512,512]{1,0:T(8,128)(2,1)S(1)}, bf16[512,512]{1,0:T(8,128)(2,1)}, u32[]{:S(2)}) copy-start(bf16[512,512]{1,0:T(8,128)(2,1)} %param.31) | copy-start | bytes 1572868
  1.8 12.2 %collective-permute-start.3 = (bf16[256,512]{1,0:T(8,128)(2,1)S(1)}, bf16[256,512]{1,0:T(8,128)(2,1)S(1)}, u32[]{:S(2)}, u32[]{:S(2)}) collective-permute-start(bf16[256,512]{1,0:T(8,128)(2,1)S(1)} %get-tuple-element.140.refs_4_), channel_id=1, source_target_pairs={{0,1},{1,2},{2,3},{3,0},{4,5},{5,6},{6,7},{7,4},{8,9},{9,10},{10,1... | collective-permute-start | bytes 786440 | tf_op jit(solution)/shard_map/ppermute | solution.py:686
  4.9 14.8 %collective-permute-start = (bf16[256,512]{1,0:T(8,128)(2,1)S(1)}, bf16[256,512]{1,0:T(8,128)(2,1)S(1)}, u32[]{:S(2)}, u32[]{:S(2)}) collective-permute-start(bf16[256,512]{1,0:T(8,128)(2,1)S(1)} %get-tuple-element.141.refs_0_), channel_id=1, source_target_pairs={{0,1},{1,2},{2,3},{3,0},{4,5},{5,6},{6,7},{7,4},{8,9},{9,10},{10,1... | collective-permute-start | bytes 786440 | tf_op jit(solution)/shard_map/ppermute | solution.py:686
  8.2 33.2 %copy-start.5 = (bf16[2048,512]{1,0:T(8,128)(2,1)S(1)}, bf16[2048,512]{1,0:T(8,128)(2,1)}, u32[]{:S(2)}) copy-start(bf16[2048,512]{1,0:T(8,128)(2,1)} %refs_12_.1) | copy-start | bytes 6291460
  8.4 32.9 %copy-start.4 = (bf16[2048,512]{1,0:T(8,128)(2,1)S(1)}, bf16[2048,512]{1,0:T(8,128)(2,1)}, u32[]{:S(2)}) copy-start(bf16[2048,512]{1,0:T(8,128)(2,1)} %refs_11_.1) | copy-start | bytes 6291460
  8.4 32.9 %copy-start.6 = (f32[2048]{0:T(1024)S(1)}, f32[2048]{0:T(1024)}, u32[]{:S(2)}) copy-start(f32[2048]{0:T(1024)} %param.20) | copy-start | bytes 24580
  14.1 11.2 %collective-permute-start.4 = (bf16[256,512]{1,0:T(8,128)(2,1)S(1)}, bf16[256,512]{1,0:T(8,128)(2,1)S(1)}, u32[]{:S(2)}, u32[]{:S(2)}) collective-permute-start(bf16[256,512]{1,0:T(8,128)(2,1)S(1)} %collective-permute-done.3.refs_5_), channel_id=1, source_target_pairs={{0,1},{1,2},{2,3},{3,0},{4,5},{5,6},{6,7},{7,4},{8,9},{9,10},{10,1... | collective-permute-start | bytes 786440 | tf_op jit(solution)/shard_map/ppermute | solution.py:686
  19.7 11.2 %collective-permute-start.1 = (bf16[256,512]{1,0:T(8,128)(2,1)S(1)}, bf16[256,512]{1,0:T(8,128)(2,1)S(1)}, u32[]{:S(2)}, u32[]{:S(2)}) collective-permute-start(bf16[256,512]{1,0:T(8,128)(2,1)S(1)} %collective-permute-done.refs_1_), channel_id=1, source_target_pairs={{0,1},{1,2},{2,3},{3,0},{4,5},{5,6},{6,7},{7,4},{8,9},{9,10},{10,1... | collective-permute-start | bytes 786440 | tf_op jit(solution)/shard_map/ppermute | solution.py:686
  25.3 11.2 %collective-permute-start.5 = (bf16[256,512]{1,0:T(8,128)(2,1)S(1)}, bf16[256,512]{1,0:T(8,128)(2,1)S(1)}, u32[]{:S(2)}, u32[]{:S(2)}) collective-permute-start(bf16[256,512]{1,0:T(8,128)(2,1)S(1)} %collective-permute-done.4.refs_6_), channel_id=1, source_target_pairs={{0,1},{1,2},{2,3},{3,0},{4,5},{5,6},{6,7},{7,4},{8,9},{9,10},{10,1... | collective-permute-start | bytes 786440 | tf_op jit(solution)/shard_map/ppermute | solution.py:686
  30.9 10.4 %collective-permute-start.2 = (bf16[256,512]{1,0:T(8,128)(2,1)S(1)}, bf16[256,512]{1,0:T(8,128)(2,1)S(1)}, u32[]{:S(2)}, u32[]{:S(2)}) collective-permute-start(bf16[256,512]{1,0:T(8,128)(2,1)S(1)} %collective-permute-done.1.refs_2_), channel_id=1, source_target_pairs={{0,1},{1,2},{2,3},{3,0},{4,5},{5,6},{6,7},{7,4},{8,9},{9,10},{10,1... | collective-permute-start | bytes 786440 | tf_op jit(solution)/shard_map/ppermute | solution.py:686
  31.0 23.7 %slice-start = ((s8[8388608]{0:T(1024)(128)(4,1)}), s8[4194304]{0:T(1024)(128)(4,1)S(1)}, s32[]{:S(2)}) async-start(s8[8388608]{0:T(1024)(128)(4,1)} %bitcast.26), calls=%async_computation | async-start | bytes 8388608
  41.3 11.2 %copy-start.10 = (bf16[512,512]{1,0:T(8,128)(2,1)S(1)}, bf16[512,512]{1,0:T(8,128)(2,1)}, u32[]{:S(2)}) copy-start(bf16[512,512]{1,0:T(8,128)(2,1)} %param.32) | copy-start | bytes 1572868
  41.4 13.3 %slice-start.1 = ((s8[8388608]{0:T(1024)(128)(4,1)}), s8[4194304]{0:T(1024)(128)(4,1)S(1)}, s32[]{:S(2)}) async-start(s8[8388608]{0:T(1024)(128)(4,1)} %bitcast.26), calls=%async_computation.1 | async-start | bytes 8388608
  49.0 16.9 %collective-permute-start.6 = (bf16[3,512,128]{2,1,0:T(8,128)(2,1)S(1)}, bf16[3,512,128]{2,1,0:T(8,128)(2,1)S(1)}, u32[]{:S(2)}, u32[]{:S(2)}) collective-permute-start(bf16[3,512,128]{2,1,0:T(8,128)(2,1)S(1)} %get-tuple-element.74), channel_id=1, source_target_pairs={{0,8},{4,12},{8,0},{12,4},{16,24},{20,28},{24,16},{28,20},{1,9},{5... | collective-permute-start | bytes 1179656 | tf_op jit(solution)/shard_map/ppermute | solution.py:708
  50.5 18.2 %collective-permute-start.7 = (bf16[3,512,128]{2,1,0:T(8,128)(2,1)S(1)}, bf16[3,512,128]{2,1,0:T(8,128)(2,1)S(1)}, u32[]{:S(2)}, u32[]{:S(2)}) collective-permute-start(bf16[3,512,128]{2,1,0:T(8,128)(2,1)S(1)} %get-tuple-element.75), channel_id=1, source_target_pairs={{0,16},{4,20},{8,24},{12,28},{16,0},{20,4},{24,8},{28,12},{1,17},{... | collective-permute-start | bytes 1179656 | tf_op jit(solution)/shard_map/ppermute | solution.py:708
  52.1 16.7 %collective-permute-start.8 = (bf16[3,512,128]{2,1,0:T(8,128)(2,1)S(1)}, bf16[3,512,128]{2,1,0:T(8,128)(2,1)S(1)}, u32[]{:S(2)}, u32[]{:S(2)}) collective-permute-start(bf16[3,512,128]{2,1,0:T(8,128)(2,1)S(1)} %get-tuple-element.76), channel_id=1, source_target_pairs={{0,24},{4,28},{8,16},{12,20},{16,8},{20,12},{24,0},{28,4},{1,25},{... | collective-permute-start | bytes 1179656 | tf_op jit(solution)/shard_map/ppermute | solution.py:708
  53.9 12.1 %collective-permute-start.9 = (bf16[512,256]{1,0:T(8,128)(2,1)S(1)}, bf16[512,256]{1,0:T(8,128)(2,1)S(1)}, u32[]{:S(2)}, u32[]{:S(2)}) collective-permute-start(bf16[512,256]{1,0:T(8,128)(2,1)S(1)} %constant_dynamic-slice_fusion.1), channel_id=1, source_target_pairs={{0,2},{1,3},{2,0},{3,1},{4,6},{5,7},{6,4},{7,5},{8,10},{9,11},{10,... | collective-permute-start | bytes 786440 | tf_op jit(solution)/shard_map/ppermute | solution.py:787
  60.3 12.9 %copy-start.11 = (s32[4096]{0:T(1024)S(1)}, s32[4096]{0:T(1024)}, u32[]{:S(2)}) copy-start(s32[4096]{0:T(1024)} %param.18) | copy-start | bytes 49156
  68.7 1.7 collective-permute-start.10
  68.7 3.2 %collective-permute-start.11 = (bf16[3,512,128]{2,1,0:T(8,128)(2,1)S(1)}, bf16[3,512,128]{2,1,0:T(8,128)(2,1)S(1)}, u32[]{:S(2)}, u32[]{:S(2)}) collective-permute-start(bf16[3,512,128]{2,1,0:T(8,128)(2,1)S(1)} %collective-permute-done.6.refs_1_), channel_id=1, source_target_pairs={{0,4},{4,0},{8,12},{12,8},{16,20},{20,16},{24,28},{28,24},{1,5},{5... | collective-permute-start | bytes 1179656 | tf_op jit(solution)/shard_map/ppermute | solution.py:716
  69.2 4.1 %collective-permute-start.12 = (bf16[3,512,128]{2,1,0:T(8,128)(2,1)S(1)}, bf16[3,512,128]{2,1,0:T(8,128)(2,1)S(1)}, u32[]{:S(2)}, u32[]{:S(2)}) collective-permute-start(bf16[3,512,128]{2,1,0:T(8,128)(2,1)S(1)} %collective-permute-done.7.refs_2_), channel_id=1, source_target_pairs={{0,4},{4,0},{8,12},{12,8},{16,20},{20,16},{24,28},{28,24},{1,5},{5... | collective-permute-start | bytes 1179656 | tf_op jit(solution)/shard_map/ppermute | solution.py:716
  69.3 4.9 %collective-permute-start.13 = (bf16[3,512,128]{2,1,0:T(8,128)(2,1)S(1)}, bf16[3,512,128]{2,1,0:T(8,128)(2,1)S(1)}, u32[]{:S(2)}, u32[]{:S(2)}) collective-permute-start(bf16[3,512,128]{2,1,0:T(8,128)(2,1)S(1)} %collective-permute-done.8.refs_3_), channel_id=1, source_target_pairs={{0,4},{4,0},{8,12},{12,8},{16,20},{20,16},{24,28},{28,24},{1,5},{5... | collective-permute-start | bytes 1179656 | tf_op jit(solution)/shard_map/ppermute | solution.py:716
  69.8 24.1 %collective-permute-start.17 = (bf16[2,512,256]{2,1,0:T(8,128)(2,1)S(1)}, bf16[2,512,256]{2,1,0:T(8,128)(2,1)S(1)}, u32[]{:S(2)}, u32[]{:S(2)}) collective-permute-start(bf16[2,512,256]{2,1,0:T(8,128)(2,1)S(1)} %pad_maximum_fusion), channel_id=1, source_target_pairs={{0,1},{1,0},{2,3},{3,2},{4,5},{5,4},{6,7},{7,6},{8,9},{9,8},{10,11... | collective-permute-start | bytes 1572872 | tf_op jit(solution)/shard_map/ppermute | solution.py:787
  70.5 15.3 %collective-permute-start.20 = (bf16[512,256]{1,0:T(8,128)(2,1)S(1)}, bf16[512,256]{1,0:T(8,128)(2,1)S(1)}, u32[]{:S(2)}, u32[]{:S(2)}) collective-permute-start(bf16[512,256]{1,0:T(8,128)(2,1)S(1)} %collective-permute-done.9.refs_10_), channel_id=1, source_target_pairs={{0,24},{4,28},{8,16},{12,20},{16,8},{20,12},{24,0},{28,4},{1,25},{... | collective-permute-start | bytes 786440 | tf_op jit(solution)/shard_map/ppermute | solution.py:708
  72.0 14.7 %collective-permute-start.19 = (bf16[512,256]{1,0:T(8,128)(2,1)S(1)}, bf16[512,256]{1,0:T(8,128)(2,1)S(1)}, u32[]{:S(2)}, u32[]{:S(2)}) collective-permute-start(bf16[512,256]{1,0:T(8,128)(2,1)S(1)} %collective-permute-done.9.refs_10_), channel_id=1, source_target_pairs={{0,16},{4,20},{8,24},{12,28},{16,0},{20,4},{24,8},{28,12},{1,17},{... | collective-permute-start | bytes 786440 | tf_op jit(solution)/shard_map/ppermute | solution.py:708
  73.3 14.8 %collective-permute-start.18 = (bf16[512,256]{1,0:T(8,128)(2,1)S(1)}, bf16[512,256]{1,0:T(8,128)(2,1)S(1)}, u32[]{:S(2)}, u32[]{:S(2)}) collective-permute-start(bf16[512,256]{1,0:T(8,128)(2,1)S(1)} %collective-permute-done.9.refs_10_), channel_id=1, source_target_pairs={{0,8},{4,12},{8,0},{12,4},{16,24},{20,28},{24,16},{28,20},{1,9},{5... | collective-permute-start | bytes 786440 | tf_op jit(solution)/shard_map/ppermute | solution.py:708
  84.5 54.8 %copy-start.7 = (f32[2048]{0:T(1024)S(1)}, f32[2048]{0:T(1024)}, u32[]{:S(2)}) copy-start(f32[2048]{0:T(1024)} %param.21) | copy-start | bytes 24580
  84.5 5.3 %collective-permute-start.14 = (bf16[512,128]{1,0:T(8,128)(2,1)S(1)}, bf16[512,128]{1,0:T(8,128)(2,1)S(1)}, u32[]{:S(2)}, u32[]{:S(2)}) collective-permute-start(bf16[512,128]{1,0:T(8,128)(2,1)S(1)} %get-tuple-element.90), channel_id=1, source_target_pairs={{0,8},{4,12},{8,0},{12,4},{16,24},{20,28},{24,16},{28,20},{1,9},{5... | collective-permute-start | bytes 393224 | tf_op jit(solution)/shard_map/ppermute | solution.py:708
  85.8 5.8 %collective-permute-start.15 = (bf16[512,128]{1,0:T(8,128)(2,1)S(1)}, bf16[512,128]{1,0:T(8,128)(2,1)S(1)}, u32[]{:S(2)}, u32[]{:S(2)}) collective-permute-start(bf16[512,128]{1,0:T(8,128)(2,1)S(1)} %get-tuple-element.91), channel_id=1, source_target_pairs={{0,16},{4,20},{8,24},{12,28},{16,0},{20,4},{24,8},{28,12},{1,17},{... | collective-permute-start | bytes 393224 | tf_op jit(solution)/shard_map/ppermute | solution.py:708
  86.6 7.3 %collective-permute-start.16 = (bf16[512,128]{1,0:T(8,128)(2,1)S(1)}, bf16[512,128]{1,0:T(8,128)(2,1)S(1)}, u32[]{:S(2)}, u32[]{:S(2)}) collective-permute-start(bf16[512,128]{1,0:T(8,128)(2,1)S(1)} %get-tuple-element.92), channel_id=1, source_target_pairs={{0,24},{4,28},{8,16},{12,20},{16,8},{20,12},{24,0},{28,4},{1,25},{... | collective-permute-start | bytes 393224 | tf_op jit(solution)/shard_map/ppermute | solution.py:708
  94.0 11.0 %collective-permute-start.21 = (bf16[2,512,128]{2,1,0:T(8,128)(2,1)S(1)}, bf16[2,512,128]{2,1,0:T(8,128)(2,1)S(1)}, u32[]{:S(2)}, u32[]{:S(2)}) collective-permute-start(bf16[2,512,128]{2,1,0:T(8,128)(2,1)S(1)} %pad_maximum_fusion.3.refs_0_), channel_id=1, source_target_pairs={{0,1},{1,2},{2,3},{3,0},{4,5},{5,6},{6,7},{7,4},{8,9},{9,10},{10,1... | collective-permute-start | bytes 786440 | tf_op jit(solution)/shard_map/ppermute | solution.py:686
  95.8 14.9 %collective-permute-start.24 = (bf16[2,512,128]{2,1,0:T(8,128)(2,1)S(1)}, bf16[2,512,128]{2,1,0:T(8,128)(2,1)S(1)}, u32[]{:S(2)}, u32[]{:S(2)}) collective-permute-start(bf16[2,512,128]{2,1,0:T(8,128)(2,1)S(1)} %pad_maximum_fusion.4.refs_4_), channel_id=1, source_target_pairs={{0,1},{1,2},{2,3},{3,0},{4,5},{5,6},{6,7},{7,4},{8,9},{9,10},{10,1... | collective-permute-start | bytes 786440 | tf_op jit(solution)/shard_map/ppermute | solution.py:686
  96.6 25.2 %collective-permute-start.29 = (bf16[2,512,256]{2,1,0:T(8,128)(2,1)S(1)}, bf16[2,512,256]{2,1,0:T(8,128)(2,1)S(1)}, u32[]{:S(2)}, u32[]{:S(2)}) collective-permute-start(bf16[2,512,256]{2,1,0:T(8,128)(2,1)S(1)} %collective-permute-done.17.refs_14_), channel_id=1, source_target_pairs={{0,24},{4,28},{8,16},{12,20},{16,8},{20,12},{24,0},{28,4},{1,25},{... | collective-permute-start | bytes 1572872 | tf_op jit(solution)/shard_map/ppermute | solution.py:708
  105.0 11.2 %collective-permute-start.22 = (bf16[2,512,128]{2,1,0:T(8,128)(2,1)S(1)}, bf16[2,512,128]{2,1,0:T(8,128)(2,1)S(1)}, u32[]{:S(2)}, u32[]{:S(2)}) collective-permute-start(bf16[2,512,128]{2,1,0:T(8,128)(2,1)S(1)} %collective-permute-done.21.refs_1_), channel_id=1, source_target_pairs={{0,1},{1,2},{2,3},{3,0},{4,5},{5,6},{6,7},{7,4},{8,9},{9,10},{10,1... | collective-permute-start | bytes 786440 | tf_op jit(solution)/shard_map/ppermute | solution.py:686
  105.0 17.6 %collective-permute-start.28 = (bf16[2,512,256]{2,1,0:T(8,128)(2,1)S(1)}, bf16[2,512,256]{2,1,0:T(8,128)(2,1)S(1)}, u32[]{:S(2)}, u32[]{:S(2)}) collective-permute-start(bf16[2,512,256]{2,1,0:T(8,128)(2,1)S(1)} %collective-permute-done.17.refs_14_), channel_id=1, source_target_pairs={{0,16},{4,20},{8,24},{12,28},{16,0},{20,4},{24,8},{28,12},{1,17},{... | collective-permute-start | bytes 1572872 | tf_op jit(solution)/shard_map/ppermute | solution.py:708
  106.2 16.4 %collective-permute-start.27 = (bf16[2,512,256]{2,1,0:T(8,128)(2,1)S(1)}, bf16[2,512,256]{2,1,0:T(8,128)(2,1)S(1)}, u32[]{:S(2)}, u32[]{:S(2)}) collective-permute-start(bf16[2,512,256]{2,1,0:T(8,128)(2,1)S(1)} %collective-permute-done.17.refs_14_), channel_id=1, source_target_pairs={{0,8},{4,12},{8,0},{12,4},{16,24},{20,28},{24,16},{28,20},{1,9},{5... | collective-permute-start | bytes 1572872 | tf_op jit(solution)/shard_map/ppermute | solution.py:708
  110.6 11.1 %collective-permute-start.25 = (bf16[2,512,128]{2,1,0:T(8,128)(2,1)S(1)}, bf16[2,512,128]{2,1,0:T(8,128)(2,1)S(1)}, u32[]{:S(2)}, u32[]{:S(2)}) collective-permute-start(bf16[2,512,128]{2,1,0:T(8,128)(2,1)S(1)} %collective-permute-done.24.refs_5_), channel_id=1, source_target_pairs={{0,1},{1,2},{2,3},{3,0},{4,5},{5,6},{6,7},{7,4},{8,9},{9,10},{10,1... | collective-permute-start | bytes 786440 | tf_op jit(solution)/shard_map/ppermute | solution.py:686
  116.2 23.1 %collective-permute-start.30 = (bf16[4,1,512,256]{3,2,0,1:T(8,128)(2,1)S(1)}, bf16[4,1,512,256]{3,2,0,1:T(8,128)(2,1)S(1)}, u32[]{:S(2)}, u32[]{:S(2)}) collective-permute-start(bf16[4,1,512,256]{3,2,0,1:T(8,128)(2,1)S(1)} %maximum_bitcast_fusion), channel_id=1, source_target_pairs={{0,4},{4,0},{8,12},{12,8},{16,20},{20,16},{24,28},{28,24},{1,5},{5... | collective-permute-start | bytes 3145736 | tf_op jit(solution)/shard_map/ppermute | solution.py:716
  121.8 11.0 %collective-permute-start.23 = (bf16[2,512,128]{2,1,0:T(8,128)(2,1)S(1)}, bf16[2,512,128]{2,1,0:T(8,128)(2,1)S(1)}, u32[]{:S(2)}, u32[]{:S(2)}) collective-permute-start(bf16[2,512,128]{2,1,0:T(8,128)(2,1)S(1)} %collective-permute-done.22.refs_2_), channel_id=1, source_target_pairs={{0,1},{1,2},{2,3},{3,0},{4,5},{5,6},{6,7},{7,4},{8,9},{9,10},{10,1... | collective-permute-start | bytes 786440 | tf_op jit(solution)/shard_map/ppermute | solution.py:686
  121.8 15.6 %collective-permute-start.26 = (bf16[2,512,128]{2,1,0:T(8,128)(2,1)S(1)}, bf16[2,512,128]{2,1,0:T(8,128)(2,1)S(1)}, u32[]{:S(2)}, u32[]{:S(2)}) collective-permute-start(bf16[2,512,128]{2,1,0:T(8,128)(2,1)S(1)} %collective-permute-done.25.refs_6_), channel_id=1, source_target_pairs={{0,1},{1,2},{2,3},{3,0},{4,5},{5,6},{6,7},{7,4},{8,9},{9,10},{10,1... | collective-permute-start | bytes 786440 | tf_op jit(solution)/shard_map/ppermute | solution.py:686
  122.6 14.8 %collective-permute-start.31 = (bf16[2,512,256]{2,1,0:T(8,128)(2,1)S(1)}, bf16[2,512,256]{2,1,0:T(8,128)(2,1)S(1)}, u32[]{:S(2)}, u32[]{:S(2)}) collective-permute-start(bf16[2,512,256]{2,1,0:T(8,128)(2,1)S(1)} %collective-permute-done.17.refs_14_), channel_id=1, source_target_pairs={{0,4},{4,0},{8,12},{12,8},{16,20},{20,16},{24,28},{28,24},{1,5},{5... | collective-permute-start | bytes 1572872 | tf_op jit(solution)/shard_map/ppermute | solution.py:716
  122.6 14.8 %collective-permute-start.34 = (bf16[2,512,256]{2,1,0:T(8,128)(2,1)S(1)}, bf16[2,512,256]{2,1,0:T(8,128)(2,1)S(1)}, u32[]{:S(2)}, u32[]{:S(2)}) collective-permute-start(bf16[2,512,256]{2,1,0:T(8,128)(2,1)S(1)} %collective-permute-done.29.refs_17_), channel_id=1, source_target_pairs={{0,4},{4,0},{8,12},{12,8},{16,20},{20,16},{24,28},{28,24},{1,5},{5... | collective-permute-start | bytes 1572872 | tf_op jit(solution)/shard_map/ppermute | solution.py:716
  132.7 4.7 %collective-permute-start.33 = (bf16[2,512,256]{2,1,0:T(8,128)(2,1)S(1)}, bf16[2,512,256]{2,1,0:T(8,128)(2,1)S(1)}, u32[]{:S(2)}, u32[]{:S(2)}) collective-permute-start(bf16[2,512,256]{2,1,0:T(8,128)(2,1)S(1)} %collective-permute-done.28.refs_16_), channel_id=1, source_target_pairs={{0,4},{4,0},{8,12},{12,8},{16,20},{20,16},{24,28},{28,24},{1,5},{5... | collective-permute-start | bytes 1572872 | tf_op jit(solution)/shard_map/ppermute | solution.py:716
  137.4 1.9 collective-permute-start.32
  161.4 12.9 %collective-permute-start.37 = (bf16[128,512]{1,0:T(8,128)(2,1)S(1)}, bf16[128,512]{1,0:T(8,128)(2,1)S(1)}, u32[]{:S(2)}, u32[]{:S(2)}) collective-permute-start(bf16[128,512]{1,0:T(8,128)(2,1)S(1)} %get-tuple-element.118), channel_id=1, source_target_pairs={{0,1},{1,2},{2,3},{3,0},{4,5},{5,6},{6,7},{7,4},{8,9},{9,10},{10,1... | collective-permute-start | bytes 393224 | tf_op jit(solution)/shard_map/ppermute | solution.py:699
  161.5 12.9 %collective-permute-start.38 = (bf16[128,512]{1,0:T(8,128)(2,1)S(1)}, bf16[128,512]{1,0:T(8,128)(2,1)S(1)}, u32[]{:S(2)}, u32[]{:S(2)}) collective-permute-start(bf16[128,512]{1,0:T(8,128)(2,1)S(1)} %get-tuple-element.119), channel_id=1, source_target_pairs={{0,2},{1,3},{2,0},{3,1},{4,6},{5,7},{6,4},{7,5},{8,10},{9,11},{10,... | collective-permute-start | bytes 393224 | tf_op jit(solution)/shard_map/ppermute | solution.py:699
  161.6 12.9 %collective-permute-start.39 = (bf16[128,512]{1,0:T(8,128)(2,1)S(1)}, bf16[128,512]{1,0:T(8,128)(2,1)S(1)}, u32[]{:S(2)}, u32[]{:S(2)}) collective-permute-start(bf16[128,512]{1,0:T(8,128)(2,1)S(1)} %get-tuple-element.120), channel_id=1, source_target_pairs={{0,3},{1,0},{2,1},{3,2},{4,7},{5,4},{6,5},{7,6},{8,11},{9,8},{10,9... | collective-permute-start | bytes 393224 | tf_op jit(solution)/shard_map/ppermute | solution.py:699
  168.7 19.0 %collective-permute-start.35 = (bf16[512,512]{1,0:T(8,128)(2,1)S(1)}, bf16[512,512]{1,0:T(8,128)(2,1)S(1)}, u32[]{:S(2)}, u32[]{:S(2)}) collective-permute-start(bf16[512,512]{1,0:T(8,128)(2,1)S(1)} %down.3), channel_id=1, source_target_pairs={{0,1},{1,0},{2,3},{3,2},{4,5},{5,4},{6,7},{7,6},{8,9},{9,8},{10,11... | collective-permute-start | bytes 1572872 | tf_op jit(solution)/shard_map/ppermute | solution.py:787
  175.5 14.9 %collective-permute-start.42 = (bf16[128,512]{1,0:T(8,128)(2,1)S(1)}, bf16[128,512]{1,0:T(8,128)(2,1)S(1)}, u32[]{:S(2)}, u32[]{:S(2)}) collective-permute-start(bf16[128,512]{1,0:T(8,128)(2,1)S(1)} %multiply_convert_fusion.3.refs_0_), channel_id=1, source_target_pairs={{0,3},{1,0},{2,1},{3,2},{4,7},{5,4},{6,5},{7,6},{8,11},{9,8},{10,9... | collective-permute-start | bytes 393224 | tf_op jit(solution)/shard_map/ppermute | solution.py:699
  178.4 12.0 %collective-permute-start.41 = (bf16[128,512]{1,0:T(8,128)(2,1)S(1)}, bf16[128,512]{1,0:T(8,128)(2,1)S(1)}, u32[]{:S(2)}, u32[]{:S(2)}) collective-permute-start(bf16[128,512]{1,0:T(8,128)(2,1)S(1)} %multiply_convert_fusion.3.refs_0_), channel_id=1, source_target_pairs={{0,2},{1,3},{2,0},{3,1},{4,6},{5,7},{6,4},{7,5},{8,10},{9,11},{10,... | collective-permute-start | bytes 393224 | tf_op jit(solution)/shard_map/ppermute | solution.py:699
  179.6 14.6 %collective-permute-start.40 = (bf16[128,512]{1,0:T(8,128)(2,1)S(1)}, bf16[128,512]{1,0:T(8,128)(2,1)S(1)}, u32[]{:S(2)}, u32[]{:S(2)}) collective-permute-start(bf16[128,512]{1,0:T(8,128)(2,1)S(1)} %multiply_convert_fusion.3.refs_0_), channel_id=1, source_target_pairs={{0,1},{1,2},{2,3},{3,0},{4,5},{5,6},{6,7},{7,4},{8,9},{9,10},{10,1... | collective-permute-start | bytes 393224 | tf_op jit(solution)/shard_map/ppermute | solution.py:699
  196.4 2.4 %collective-permute-start.43 = (bf16[4,208,512]{2,1,0:T(8,128)(2,1)S(1)}, bf16[4,208,512]{2,1,0:T(8,128)(2,1)S(1)}, u32[]{:S(2)}, u32[]{:S(2)}) collective-permute-start(bf16[4,208,512]{2,1,0:T(8,128)(2,1)S(1)} %get-tuple-element.126), channel_id=1, source_target_pairs={{0,4},{4,0},{8,12},{12,8},{16,20},{20,16},{24,28},{28,24},{1,5},{5... | collective-permute-start | bytes 2555912 | tf_op jit(solution)/shard_map/ppermute | solution.py:716
  199.0 8.2 %collective-permute-start.44 = (bf16[208,512]{1,0:T(8,128)(2,1)S(1)}, bf16[208,512]{1,0:T(8,128)(2,1)S(1)}, u32[]{:S(2)}, u32[]{:S(2)}) collective-permute-start(bf16[208,512]{1,0:T(8,128)(2,1)S(1)} %get-tuple-element.128), channel_id=1, source_target_pairs={{0,8},{4,12},{8,0},{12,4},{16,24},{20,28},{24,16},{28,20},{1,9},{5... | collective-permute-start | bytes 638984 | tf_op jit(solution)/shard_map/ppermute | solution.py:708
  199.6 11.6 %collective-permute-start.45 = (bf16[208,512]{1,0:T(8,128)(2,1)S(1)}, bf16[208,512]{1,0:T(8,128)(2,1)S(1)}, u32[]{:S(2)}, u32[]{:S(2)}) collective-permute-start(bf16[208,512]{1,0:T(8,128)(2,1)S(1)} %get-tuple-element.129), channel_id=1, source_target_pairs={{0,16},{4,20},{8,24},{12,28},{16,0},{20,4},{24,8},{28,12},{1,17},{... | collective-permute-start | bytes 638984 | tf_op jit(solution)/shard_map/ppermute | solution.py:708
  201.2 10.0 %collective-permute-start.46 = (bf16[208,512]{1,0:T(8,128)(2,1)S(1)}, bf16[208,512]{1,0:T(8,128)(2,1)S(1)}, u32[]{:S(2)}, u32[]{:S(2)}) collective-permute-start(bf16[208,512]{1,0:T(8,128)(2,1)S(1)} %get-tuple-element.130), channel_id=1, source_target_pairs={{0,24},{4,28},{8,16},{12,20},{16,8},{20,12},{24,0},{28,4},{1,25},{... | collective-permute-start | bytes 638984 | tf_op jit(solution)/shard_map/ppermute | solution.py:708
  202.7 25.3 %collective-permute-start.48 = (bf16[512,512]{1,0:T(8,128)(2,1)S(1)}, bf16[512,512]{1,0:T(8,128)(2,1)S(1)}, u32[]{:S(2)}, u32[]{:S(2)}) collective-permute-start(bf16[512,512]{1,0:T(8,128)(2,1)S(1)} %add_convert_fusion.1), channel_id=1, source_target_pairs={{0,2},{1,3},{2,0},{3,1},{4,6},{5,7},{6,4},{7,5},{8,10},{9,11},{10,... | collective-permute-start | bytes 1572872 | tf_op jit(solution)/shard_map/ppermute | solution.py:787
  203.3 24.8 %collective-permute-start.36 = (bf16[512,512]{1,0:T(8,128)(2,1)S(1)}, bf16[512,512]{1,0:T(8,128)(2,1)S(1)}, u32[]{:S(2)}, u32[]{:S(2)}) collective-permute-start(bf16[512,512]{1,0:T(8,128)(2,1)S(1)} %get-tuple-element.115), channel_id=1, source_target_pairs={{0,1},{1,0},{2,3},{3,2},{4,5},{5,4},{6,7},{7,6},{8,9},{9,8},{10,11... | collective-permute-start | bytes 1572872 | tf_op jit(solution)/shard_map/ppermute | solution.py:787
  211.3 16.7 %collective-permute-start.47 = (bf16[208,512]{1,0:T(8,128)(2,1)S(1)}, bf16[208,512]{1,0:T(8,128)(2,1)S(1)}, u32[]{:S(2)}, u32[]{:S(2)}) collective-permute-start(bf16[208,512]{1,0:T(8,128)(2,1)S(1)} %add_convert_fusion.2.refs_0_), channel_id=1, source_target_pairs={{0,24},{4,28},{8,16},{12,20},{16,8},{20,12},{24,0},{28,4},{1,25},{... | collective-permute-start | bytes 638984 | tf_op jit(solution)/shard_map/ppermute | solution.py:708
  212.9 15.6 %collective-permute-start.50 = (bf16[208,512]{1,0:T(8,128)(2,1)S(1)}, bf16[208,512]{1,0:T(8,128)(2,1)S(1)}, u32[]{:S(2)}, u32[]{:S(2)}) collective-permute-start(bf16[208,512]{1,0:T(8,128)(2,1)S(1)} %add_convert_fusion.2.refs_0_), channel_id=1, source_target_pairs={{0,16},{4,20},{8,24},{12,28},{16,0},{20,4},{24,8},{28,12},{1,17},{... | collective-permute-start | bytes 638984 | tf_op jit(solution)/shard_map/ppermute | solution.py:708
  214.3 14.4 %collective-permute-start.49 = (bf16[208,512]{1,0:T(8,128)(2,1)S(1)}, bf16[208,512]{1,0:T(8,128)(2,1)S(1)}, u32[]{:S(2)}, u32[]{:S(2)}) collective-permute-start(bf16[208,512]{1,0:T(8,128)(2,1)S(1)} %add_convert_fusion.2.refs_0_), channel_id=1, source_target_pairs={{0,8},{4,12},{8,0},{12,4},{16,24},{20,28},{24,16},{28,20},{1,9},{5... | collective-permute-start | bytes 638984 | tf_op jit(solution)/shard_map/ppermute | solution.py:708
  228.0 2.1 collective-permute-start.51
  228.1 2.2 collective-permute-start.54
  228.5 1.6 collective-permute-start.53
  228.7 1.7 collective-permute-start.52
  (6 other events, 23.7 us)

commit v11 on v10

--- a/solution.py
+++ b/solution.py
@@ -188,7 +188,7 @@
     blocks = [refs[:ring], refs[ring : 2 * ring]]
     gain_ref, cos_ref, sin_ref, *sources = refs[2 * ring : 2 * ring + 6]
     outs = refs[2 * ring + 6 : 2 * ring + 6 + heads]
-    tok_ref, stamp_ref, normed, made, weights, sems = refs[2 * ring + 6 + heads :]
+    tok_ref, stamp_ref, normed, made, weights, tokens, sems = refs[2 * ring + 6 + heads :]
     half, width = blocks[0][0].shape
     depth = gain_ref.shape[1]
     copies = [
@@ -207,8 +207,10 @@
         for s, block in enumerate(blocks[k]):
             at = pl.ds(pl.multiple_of(info_ref[s] * width, 128), width)
             part = block[...]
-            tok_ref[mine, at] = part
+            tokens[mine, at] = part
             normed[mine, at] = (part.astype(F32) * scale * gain_ref[:, at]).astype(BF16)
+    keep = pltpu.make_async_copy(tokens, tok_ref, sems.at[3])
+    keep.start()
     for kind, copy in enumerate(copies):
         copy.wait()
         result = dot(normed[...], weights[kind])
@@ -222,6 +224,7 @@
     for f in range(heads):
         outs[f][...] = made[info_ref[ring + 1] ^ f]
     stamp_ref[...] = jnp.zeros_like(stamp_ref)
+    keep.wait()
 
 
 def qkv_call(info, blocks, gain, cosine, sine, *weights):
@@ -241,12 +244,14 @@
             in_specs=[whole((half, width))] * (2 * ring)
             + [whole((1, depth)), whole((rows, HD)), whole((rows, HD))]
             + [pl.BlockSpec(memory_space=pl.ANY)] * 3,
-            out_specs=[whole((3, rows, HD))] * heads + [whole((rows, depth)), whole((8, HD))],
+            out_specs=[whole((3, rows, HD))] * heads
+            + [pl.BlockSpec(memory_space=pltpu.HBM), whole((8, HD))],
             scratch_shapes=[
                 pltpu.VMEM((rows, depth), BF16),
                 pltpu.VMEM((heads, 3, rows, HD), BF16),
                 pltpu.VMEM((3, depth, out_cols), BF16),
-                pltpu.SemaphoreType.DMA((3,)),
+                pltpu.VMEM((rows, depth), BF16),
+                pltpu.SemaphoreType.DMA((4,)),
             ],
         ),
         compiler_params=params(42),
@@ -287,8 +292,7 @@
 
         def body(at, carry, masked, query=query, row=row, start=start, lane=lane):
             peak, denom, accum = carry
-            count = lane.shape[0]
-            scores = dot_over(keys_all[at, :count], query, (1, 1))
+            scores = dot_over(keys_all[at], query, (1, 1))
             if masked:
                 column = lane + at * span
                 allowed = (column >= start) & (column <= row)
@@ -299,7 +303,7 @@
                 weights = jnp.where(allowed, weights, 0.0)
             keep = jnp.exp2(peak - new_peak)
             denom = denom * keep + jnp.sum(weights, axis=0, keepdims=True)
-            accum = accum * keep + dot(values_all[at, :, :count], weights.astype(BF16))
+            accum = accum * keep + dot(values_all[at], weights.astype(BF16))
             return new_peak, denom, accum
 
         def pair(turn, carry, query=query, full=None):
@@ -329,13 +333,8 @@
         carry = lax.fori_loop(0, turns, functools.partial(pair, full=full), carry)
         rest = full + 2 * turns
         carry = lax.fori_loop(rest, last, functools.partial(body, masked=False), carry)
-        half = span // 2
-        for at in (slice(0, half), slice(half, span)):
-            part = tuple(value[:, at] for value in carry)
-            _, denom, accum = body(
-                last, part, True, query[at], row[:, at], start[:, at], lane[: at.stop]
-            )
-            outs[f][at] = (accum / denom).T.astype(BF16)
+        _, denom, accum = body(last, carry, masked=True)
+        outs[f][...] = (accum / denom).T.astype(BF16)
 
 
 def attention_call(first, info, own, other, stamp, ring):
@@ -649,7 +648,7 @@
 def finish_kernel(info_ref, *refs, chips, ring):
     mine, others = refs[:chips], refs[chips : 2 * chips]
     outs = refs[2 * chips : 2 * chips + 3]
-    notes = refs[2 * chips + 3]
+    error_ref, notes = refs[2 * chips + 3 :]
     chip, core = info_ref[ring + 1], info_ref[ring + 2]
     share = (mine[0].shape[0] - NOTE) // 3
     for f in range(chips):
@@ -659,6 +658,7 @@
             for k in range(3):
                 outs[k][at, :] = ref[k * share : (k + 1) * share].astype(F32)
             notes[index] = ref[3 * share :, :HD].astype(F32)
+    error_ref[0, 0] = jnp.max(notes[0]) / mine[0].shape[1]
 
 
 def finish_call(info, mine, others, ring):
@@ -668,12 +668,13 @@
     return pl.pallas_call(
         functools.partial(finish_kernel, chips=chips, ring=ring),
         out_shape=[jax.ShapeDtypeStruct((rows, sd), F32)] * 3
-        + [jax.ShapeDtypeStruct((2 * chips, NOTE, HD), F32)],
+        + [jax.ShapeDtypeStruct((1, 1), F32)],
         grid_spec=pltpu.PrefetchScalarGridSpec(
             num_scalar_prefetch=1,
             grid=(1,),
             in_specs=[whole((share, sd))] * (2 * chips),
-            out_specs=[whole((rows, sd))] * 3 + [whole((2 * chips, NOTE, HD))],
+            out_specs=[whole((rows, sd))] * 3 + [pl.BlockSpec(memory_space=pltpu.SMEM)],
+            scratch_shapes=[pltpu.VMEM((2 * chips, NOTE, HD), F32)],
         ),
         compiler_params=params(14),
         cost_estimate=cost(rows * sd, 12 * rows * sd),
@@ -848,8 +849,8 @@
     level_sums = [over(after(near_theirs, far_sum), 1), over(far_sum, 2)]
     mlp_own = sum(after(value, mine[-1]).astype(F32) for value in level_sums)
     teacher_out = (mixed_own.astype(F32) + (kept.astype(F32) + mlp_own)).astype(BF16)
-    grad_gate, grad_up, grad_down, notes = finish_call(info, mine, others, ring)
-    return teacher_out, grad_gate, grad_up, grad_down, notes[0, 0, 0] / sd
+    grad_gate, grad_up, grad_down, error = finish_call(info, mine, others, ring)
+    return teacher_out, grad_gate, grad_up, grad_down, error.reshape(())
 
 
 def local(*args):

time: 233 us -> 230 us (0.987)
  no operation moved by 1% of the time
where the time goes in v11:
time: 230 us; the launch traced here: 232 us
  waiting for transfers between devices  117 us (51%)
  Pallas kernels  49.9 us (22%)
  starting transfers between devices  45.4 us (20%)
  matrix products  7.35 us (3%)
  other arithmetic  6.12 us (3%)
  local copies, waits for them, and re-layouts  5.25 us (2%)
    ppermute x12, waiting for transfers between devices, step_on(): return lax.ppermute(block, axis, [(i, (i + 1) % size) for i in range(size)])  64.6 us
    ppermute x5, waiting for transfers between devices, paired(): lax.ppermute(value, 'tensor', [(i, i ^ bit) for i in range(ring)])  26.5 us
    ppermute x18, starting transfers between devices, flipped(): lax.ppermute(pieces[f], 'dp', [(i, i ^ 2 * f) for i in range(size)])  22.6 us
    pallas_call x1, Pallas kernels, middle_call(): pl.pallas_call(functools.partial(middle_kernel, ring=ring, chips=chips),...  22.1 us
    ppermute x18, waiting for transfers between devices, flipped(): lax.ppermute(pieces[f], 'dp', [(i, i ^ 2 * f) for i in range(size)])  14.6 us
    pallas_call x1, Pallas kernels, attention_call(): pl.pallas_call(functools.partial(attention_kernel, chips=chips, ring=ring...  9.67 us
    ppermute x6, starting transfers between devices, shifted(): lax.ppermute(pieces[s], axis, [(i, (i + s) % size) for i in range(size)])  7.97 us
    ppermute x12, starting transfers between devices, step_on(): return lax.ppermute(block, axis, [(i, (i + 1) % size) for i in range(size)])  7.74 us
  transfers between devices with their start and end apart: 55, of which 30 were waited for; matrix products, arithmetic and copies ran while one was open for 6% of the time, Pallas kernels for 7%

profile of v11, /device:TPU:0, one launch (start us, length us, event | category | flops | bytes accessed | tf_op | source)
XLA Modules:
  0.0 232.5 jit_solution(10678023862254423621)
XLA Ops:
  0.7 1.1 fusion.10
  1.8 3.1 %collective-permute-start.3 = (bf16[256,512]{1,0:T(8,128)(2,1)S(1)}, bf16[256,512]{1,0:T(8,128)(2,1)S(1)}, u32[]{:S(2)}, u32[]{:S(2)}) collective-permute-start(bf16[256,512]{1,0:T(8,128)(2,1)S(1)} %get-tuple-element.140.refs_4_), channel_id=1, source_target_pairs={{0,1},{1,2},{2,3},{3,0},{4,5},{5,6},{6,7},{7,4},{8,9},{9,10},{10,1... | collective-permute-start | bytes 786440 | tf_op jit(solution)/shard_map/ppermute | solution.py:687
  4.9 1.6 collective-permute-start
  7.2 1.0 fusion.3
  8.6 5.5 %collective-permute-done.3.refs_5_ = bf16[256,512]{1,0:T(8,128)(2,1)S(1)} collective-permute-done((bf16[256,512]{1,0:T(8,128)(2,1)S(1)}, bf16[256,512]{1,0:T(8,128)(2,1)S(1)}, u32[]{:S(2)}, u32[]{:S(2)}) %collective-permute-start.3) | collective-permute-done | bytes 262176 | tf_op jit(solution)/shard_map/ppermute | solution.py:687
  14.1 5.6 %collective-permute-done.refs_1_ = bf16[256,512]{1,0:T(8,128)(2,1)S(1)} collective-permute-done((bf16[256,512]{1,0:T(8,128)(2,1)S(1)}, bf16[256,512]{1,0:T(8,128)(2,1)S(1)}, u32[]{:S(2)}, u32[]{:S(2)}) %collective-permute-start) | collective-permute-done | bytes 262176 | tf_op jit(solution)/shard_map/ppermute | solution.py:687
  19.7 1.1 constant_dynamic-slice_fusion.1
  20.9 1.1 convert_element_type.98
  22.0 3.3 %collective-permute-done.4.refs_6_ = bf16[256,512]{1,0:T(8,128)(2,1)S(1)} collective-permute-done((bf16[256,512]{1,0:T(8,128)(2,1)S(1)}, bf16[256,512]{1,0:T(8,128)(2,1)S(1)}, u32[]{:S(2)}, u32[]{:S(2)}) %collective-permute-start.4) | collective-permute-done | bytes 262176 | tf_op jit(solution)/shard_map/ppermute | solution.py:687
  25.3 5.6 %collective-permute-done.1.refs_2_ = bf16[256,512]{1,0:T(8,128)(2,1)S(1)} collective-permute-done((bf16[256,512]{1,0:T(8,128)(2,1)S(1)}, bf16[256,512]{1,0:T(8,128)(2,1)S(1)}, u32[]{:S(2)}, u32[]{:S(2)}) %collective-permute-start.1) | collective-permute-done | bytes 262176 | tf_op jit(solution)/shard_map/ppermute | solution.py:687
  31.1 5.4 %collective-permute-done.5.refs_7_ = bf16[256,512]{1,0:T(8,128)(2,1)S(1)} collective-permute-done((bf16[256,512]{1,0:T(8,128)(2,1)S(1)}, bf16[256,512]{1,0:T(8,128)(2,1)S(1)}, u32[]{:S(2)}, u32[]{:S(2)}) %collective-permute-start.5) | collective-permute-done | bytes 262176 | tf_op jit(solution)/shard_map/ppermute | solution.py:687
  36.5 4.8 %collective-permute-done.2.refs_3_ = bf16[256,512]{1,0:T(8,128)(2,1)S(1)} collective-permute-done((bf16[256,512]{1,0:T(8,128)(2,1)S(1)}, bf16[256,512]{1,0:T(8,128)(2,1)S(1)}, u32[]{:S(2)}, u32[]{:S(2)}) %collective-permute-start.2) | collective-permute-done | bytes 262176 | tf_op jit(solution)/shard_map/ppermute | solution.py:687
  41.4 6.5 %qkv.1 = (bf16[3,512,128]{2,1,0:T(8,128)(2,1)S(1)}, bf16[3,512,128]{2,1,0:T(8,128)(2,1)S(1)}, bf16[3,512,128]{2,1,0:T(8,128)(2,1)S(1)}, bf16[3,512,128]{2,1,0:T(...) custom-call(s32[16]{0:T(128)S(1)} %fusion.9.info_ref, ...), custom_call_target="tpu_custom_call" | custom-call | flops 3221225472 | bytes 6291456 | tf_op jit(solution)/shard_map/qkv/pallas_call | solution.py:235
  47.9 1.3 copy-done.8
  49.2 1.5 collective-permute-start.6
  50.7 1.5 collective-permute-start.7
  53.1 0.8 multiply_convert_fusion
  54.8 5.6 %fusion.refs_26_ = bf16[2048,512]{1,0:T(8,128)(2,1)} fusion(bf16[2048,2048]{1,0:T(8,128)(2,1)S(1)} %bitcast.27, bf16[2048,512]{1,0:T(8,128)(2,1)S(1)} %copy-done.12), kind=kOutput, calls=%fused_computation.1 | convolution fusion | flops 4296015872 | bytes 12582912 | tf_op jit(solution)/shard_map/dot_general | solution.py:166
  60.9 5.2 %collective-permute-done.9.refs_10_ = bf16[512,256]{1,0:T(8,128)(2,1)S(1)} collective-permute-done((bf16[512,256]{1,0:T(8,128)(2,1)S(1)}, bf16[512,256]{1,0:T(8,128)(2,1)S(1)}, u32[]{:S(2)}, u32[]{:S(2)}) %collective-permute-start.9) | collective-permute-done | bytes 262176 | tf_op jit(solution)/shard_map/ppermute | solution.py:788
  66.1 2.8 %collective-permute-done.7.refs_2_ = bf16[3,512,128]{2,1,0:T(8,128)(2,1)S(1)} collective-permute-done((bf16[3,512,128]{2,1,0:T(8,128)(2,1)S(1)}, bf16[3,512,128]{2,1,0:T(8,128)(2,1)S(1)}, u32[]{:S(2)}, u32[]{:S(2)}) %collective-permute-start.7) | collective-permute-done | bytes 393248 | tf_op jit(solution)/shard_map/ppermute | solution.py:709
  70.6 1.5 collective-permute-start.20
  72.1 1.2 collective-permute-start.19
  73.5 0.9 collective-permute-start.18
  74.3 9.7 %attention.1 = (bf16[512,128]{1,0:T(8,128)(2,1)S(1)}, bf16[512,128]{1,0:T(8,128)(2,1)S(1)}, bf16[512,128]{1,0:T(8,128)(2,1)S(1)}, bf16[512,128]{1,0:T(8,128)(2,1)S(1)}) custom-call(s32[8]{0:T(128)S(1)} %convert_reduce_fusion.first_ref, s32[16]{0:T(128)S(1)} %fusion.9.info_ref, bf16[3,512,128]{2,1,0:T(8,128)(2,1)S(1)} %get-tuple-element.84.refs_0_, ...), custom_call_target="tpu_custom_call" | custom-call | flops 2147483648 | bytes 4194304 | tf_op jit(solution)/shard_map/attention/pallas_call | solution.py:343
  84.0 1.3 collective-permute-start.14
  85.3 0.8 collective-permute-start.15
  86.1 1.4 collective-permute-start.16
  87.6 1.8 collective-permute-done.14
  89.3 1.7 collective-permute-done.15
  91.1 2.4 %collective-permute-done.16 = bf16[512,128]{1,0:T(8,128)(2,1)S(1)} collective-permute-done((bf16[512,128]{1,0:T(8,128)(2,1)S(1)}, bf16[512,128]{1,0:T(8,128)(2,1)S(1)}, u32[]{:S(2)}, u32[]{:S(2)}) %collective-permute-start.16) | collective-permute-done | bytes 131104 | tf_op jit(solution)/shard_map/ppermute | solution.py:709
  93.5 1.7 collective-permute-start.21
  96.0 2.2 collective-permute-start.29
  98.3 6.2 %collective-permute-done.21.refs_1_ = bf16[2,512,128]{2,1,0:T(8,128)(2,1)S(1)} collective-permute-done((bf16[2,512,128]{2,1,0:T(8,128)(2,1)S(1)}, bf16[2,512,128]{2,1,0:T(8,128)(2,1)S(1)}, u32[]{:S(2)}, u32[]{:S(2)}) %collective-permute-start.21) | collective-permute-done | bytes 262176 | tf_op jit(solution)/shard_map/ppermute | solution.py:687
  104.5 1.2 collective-permute-start.28
  105.6 1.5 collective-permute-start.27
  107.1 3.0 %collective-permute-done.24.refs_5_ = bf16[2,512,128]{2,1,0:T(8,128)(2,1)S(1)} collective-permute-done((bf16[2,512,128]{2,1,0:T(8,128)(2,1)S(1)}, bf16[2,512,128]{2,1,0:T(8,128)(2,1)S(1)}, u32[]{:S(2)}, u32[]{:S(2)}) %collective-permute-start.24) | collective-permute-done | bytes 262176 | tf_op jit(solution)/shard_map/ppermute | solution.py:687
  110.2 5.5 %collective-permute-done.22.refs_2_ = bf16[2,512,128]{2,1,0:T(8,128)(2,1)S(1)} collective-permute-done((bf16[2,512,128]{2,1,0:T(8,128)(2,1)S(1)}, bf16[2,512,128]{2,1,0:T(8,128)(2,1)S(1)}, u32[]{:S(2)}, u32[]{:S(2)}) %collective-permute-start.22) | collective-permute-done | bytes 262176 | tf_op jit(solution)/shard_map/ppermute | solution.py:687
  115.7 5.5 %collective-permute-done.25.refs_6_ = bf16[2,512,128]{2,1,0:T(8,128)(2,1)S(1)} collective-permute-done((bf16[2,512,128]{2,1,0:T(8,128)(2,1)S(1)}, bf16[2,512,128]{2,1,0:T(8,128)(2,1)S(1)}, u32[]{:S(2)}, u32[]{:S(2)}) %collective-permute-start.25) | collective-permute-done | bytes 262176 | tf_op jit(solution)/shard_map/ppermute | solution.py:687
  122.6 9.6 %collective-permute-done.23.refs_3_ = bf16[2,512,128]{2,1,0:T(8,128)(2,1)S(1)} collective-permute-done((bf16[2,512,128]{2,1,0:T(8,128)(2,1)S(1)}, bf16[2,512,128]{2,1,0:T(8,128)(2,1)S(1)}, u32[]{:S(2)}, u32[]{:S(2)}) %collective-permute-start.23) | collective-permute-done | bytes 262176 | tf_op jit(solution)/shard_map/ppermute | solution.py:687
  132.2 4.7 %collective-permute-done.26.refs_7_ = bf16[2,512,128]{2,1,0:T(8,128)(2,1)S(1)} collective-permute-done((bf16[2,512,128]{2,1,0:T(8,128)(2,1)S(1)}, bf16[2,512,128]{2,1,0:T(8,128)(2,1)S(1)}, u32[]{:S(2)}, u32[]{:S(2)}) %collective-permute-start.26) | collective-permute-done | bytes 262176 | tf_op jit(solution)/shard_map/ppermute | solution.py:687
  136.9 1.9 collective-permute-done.32.refs_20_
  138.8 22.1 %middle.1 = (bf16[512,2048]{1,0:T(8,128)(2,1)}, bf16[512,512]{1,0:T(8,128)(2,1)S(1)}, bf16[128,512]{1,0:T(8,128)(2,1)S(1)}, bf16[128,512]{1,0:T(8,128)(2,1)S(1)}...) custom-call(s32[16]{0:T(128)S(1)} %fusion.9.info_ref, bf16[2,512,128]{2,1,0:T(8,128)(2,1)S(1)} %pad_maximum_fusion.3.refs_0_, ...), custom_call_target="tpu_custom_call" | custom-call | flops 14227079168 | bytes 25165824 | tf_op jit(solution)/shard_map/middle/pallas_call | solution.py:488
  161.0 3.7 %collective-permute-start.39 = (bf16[128,512]{1,0:T(8,128)(2,1)S(1)}, bf16[128,512]{1,0:T(8,128)(2,1)S(1)}, u32[]{:S(2)}, u32[]{:S(2)}) collective-permute-start(bf16[128,512]{1,0:T(8,128)(2,1)S(1)} %get-tuple-element.120), channel_id=1, source_target_pairs={{0,3},{1,0},{2,1},{3,2},{4,7},{5,4},{6,5},{7,6},{8,11},{9,8},{10,9... | collective-permute-start | bytes 393224 | tf_op jit(solution)/shard_map/ppermute | solution.py:700
  164.8 1.6 copy-done.2
  166.3 1.8 down.3
  168.8 5.0 %down.2 = (bf16[512,512]{1,0:T(8,128)(2,1)S(1)}, bf16[512,512]{1,0:T(8,128)(2,1)S(1)}, bf16[512,512]{1,0:T(8,128)(2,1)S(1)}) custom-call(s32[16]{0:T(128)S(1)} %fusion.9.info_ref, bf16[512,2048]{1,0:T(8,128)(2,1)S(1)} %copy-done.2, bf16[2048,2048]{1,0:T(8,128)(2,1)S(1)} %bitcast.27), custom_call_target="tpu_custom_call" | custom-call | flops 3221225472 | bytes 6291456 | tf_op jit(solution)/shard_map/down/pallas_call | solution.py:562
  173.9 1.1 multiply_convert_fusion.3.refs_0_
  175.0 2.9 %collective-permute-start.42 = (bf16[128,512]{1,0:T(8,128)(2,1)S(1)}, bf16[128,512]{1,0:T(8,128)(2,1)S(1)}, u32[]{:S(2)}, u32[]{:S(2)}) collective-permute-start(bf16[128,512]{1,0:T(8,128)(2,1)S(1)} %multiply_convert_fusion.3.refs_0_), channel_id=1, source_target_pairs={{0,3},{1,0},{2,1},{3,2},{4,7},{5,4},{6,5},{7,6},{8,11},{9,8},{10,9... | collective-permute-start | bytes 393224 | tf_op jit(solution)/shard_map/ppermute | solution.py:700
  177.9 1.2 collective-permute-start.41
  179.1 8.1 %collective-permute-done.35 = bf16[512,512]{1,0:T(8,128)(2,1)S(1)} collective-permute-done((bf16[512,512]{1,0:T(8,128)(2,1)S(1)}, bf16[512,512]{1,0:T(8,128)(2,1)S(1)}, u32[]{:S(2)}, u32[]{:S(2)}) %collective-permute-start.35) | collective-permute-done | bytes 524320 | tf_op jit(solution)/shard_map/ppermute | solution.py:788
  187.2 2.7 %collective-permute-done.42.refs_3_ = bf16[128,512]{1,0:T(8,128)(2,1)S(1)} collective-permute-done((bf16[128,512]{1,0:T(8,128)(2,1)S(1)}, bf16[128,512]{1,0:T(8,128)(2,1)S(1)}, u32[]{:S(2)}, u32[]{:S(2)}) %collective-permute-start.42) | collective-permute-done | bytes 131104 | tf_op jit(solution)/shard_map/ppermute | solution.py:700
  189.9 3.7 %collective-permute-done.40.refs_1_ = bf16[128,512]{1,0:T(8,128)(2,1)S(1)} collective-permute-done((bf16[128,512]{1,0:T(8,128)(2,1)S(1)}, bf16[128,512]{1,0:T(8,128)(2,1)S(1)}, u32[]{:S(2)}, u32[]{:S(2)}) %collective-permute-start.40) | collective-permute-done | bytes 131104 | tf_op jit(solution)/shard_map/ppermute | solution.py:700
  193.6 2.2 grads.1
  195.9 2.4 %collective-permute-done.43.theirs_ref = bf16[4,208,512]{2,1,0:T(8,128)(2,1)S(1)} collective-permute-done((bf16[4,208,512]{2,1,0:T(8,128)(2,1)S(1)}, bf16[4,208,512]{2,1,0:T(8,128)(2,1)S(1)}, u32[]{:S(2)}, u32[]{:S(2)}) %collective-permute-start.43) | collective-permute-done | bytes 852000 | tf_op jit(solution)/shard_map/ppermute | solution.py:717
  199.2 1.5 collective-permute-start.45
  200.7 1.3 collective-permute-start.46
  202.8 2.5 %collective-permute-start.36 = (bf16[512,512]{1,0:T(8,128)(2,1)S(1)}, bf16[512,512]{1,0:T(8,128)(2,1)S(1)}, u32[]{:S(2)}, u32[]{:S(2)}) collective-permute-start(bf16[512,512]{1,0:T(8,128)(2,1)S(1)} %get-tuple-element.115), channel_id=1, source_target_pairs={{0,1},{1,0},{2,3},{3,2},{4,5},{5,4},{6,7},{7,6},{8,9},{9,8},{10,11... | collective-permute-start | bytes 1572872 | tf_op jit(solution)/shard_map/ppermute | solution.py:788
  205.3 1.3 collective-permute-done.44
  206.6 4.1 %collective-permute-done.45 = bf16[208,512]{1,0:T(8,128)(2,1)S(1)} collective-permute-done((bf16[208,512]{1,0:T(8,128)(2,1)S(1)}, bf16[208,512]{1,0:T(8,128)(2,1)S(1)}, u32[]{:S(2)}, u32[]{:S(2)}) %collective-permute-start.45) | collective-permute-done | bytes 213024 | tf_op jit(solution)/shard_map/ppermute | solution.py:709
  210.9 1.5 collective-permute-start.47
  212.4 1.3 collective-permute-start.50
  214.4 13.0 %collective-permute-done.48 = bf16[512,512]{1,0:T(8,128)(2,1)S(1)} collective-permute-done((bf16[512,512]{1,0:T(8,128)(2,1)S(1)}, bf16[512,512]{1,0:T(8,128)(2,1)S(1)}, u32[]{:S(2)}, u32[]{:S(2)}) %collective-permute-start.48) | collective-permute-done | bytes 524320 | tf_op jit(solution)/shard_map/ppermute | solution.py:788
  228.5 1.1 add_convert_fusion
  229.8 2.4 %finish.1 = (f32[512,512]{1,0:T(8,128)}, f32[512,512]{1,0:T(8,128)}, f32[512,512]{1,0:T(8,128)}, f32[1,1]{1,0:T(1,128)}) custom-call(s32[16]{0:T(128)S(1)} %fusion.9.info_ref, bf16[208,512]{1,0:T(8,128)(2,1)S(1)} %add_convert_fusion.2.refs_0_, bf16[208,512]{1,0:T(8,128)(2,1)S(1)} %collective-permute-done.49.refs_1_, ...), custom_call_target="tpu_custom_call" | custom-call | flops 262144 | bytes 3145728 | tf_op jit(solution)/shard_map/finish/pallas_call | solution.py:668
  (109 shorter events, 12.6 us)
Async XLA Ops:
  0.6 52.5 %copy-start = (bf16[512,512]{1,0:T(8,128)(2,1)S(1)}, bf16[512,512]{1,0:T(8,128)(2,1)}, u32[]{:S(2)}) copy-start(bf16[512,512]{1,0:T(8,128)(2,1)} %param.31) | copy-start | bytes 1572868
  1.8 12.2 %collective-permute-start.3 = (bf16[256,512]{1,0:T(8,128)(2,1)S(1)}, bf16[256,512]{1,0:T(8,128)(2,1)S(1)}, u32[]{:S(2)}, u32[]{:S(2)}) collective-permute-start(bf16[256,512]{1,0:T(8,128)(2,1)S(1)} %get-tuple-element.140.refs_4_), channel_id=1, source_target_pairs={{0,1},{1,2},{2,3},{3,0},{4,5},{5,6},{6,7},{7,4},{8,9},{9,10},{10,1... | collective-permute-start | bytes 786440 | tf_op jit(solution)/shard_map/ppermute | solution.py:687
  4.9 14.8 %collective-permute-start = (bf16[256,512]{1,0:T(8,128)(2,1)S(1)}, bf16[256,512]{1,0:T(8,128)(2,1)S(1)}, u32[]{:S(2)}, u32[]{:S(2)}) collective-permute-start(bf16[256,512]{1,0:T(8,128)(2,1)S(1)} %get-tuple-element.141.refs_0_), channel_id=1, source_target_pairs={{0,1},{1,2},{2,3},{3,0},{4,5},{5,6},{6,7},{7,4},{8,9},{9,10},{10,1... | collective-permute-start | bytes 786440 | tf_op jit(solution)/shard_map/ppermute | solution.py:687
  8.2 33.2 %copy-start.5 = (bf16[2048,512]{1,0:T(8,128)(2,1)S(1)}, bf16[2048,512]{1,0:T(8,128)(2,1)}, u32[]{:S(2)}) copy-start(bf16[2048,512]{1,0:T(8,128)(2,1)} %refs_12_.1) | copy-start | bytes 6291460
  8.4 32.9 %copy-start.4 = (bf16[2048,512]{1,0:T(8,128)(2,1)S(1)}, bf16[2048,512]{1,0:T(8,128)(2,1)}, u32[]{:S(2)}) copy-start(bf16[2048,512]{1,0:T(8,128)(2,1)} %refs_11_.1) | copy-start | bytes 6291460
  8.4 32.9 %copy-start.6 = (f32[2048]{0:T(1024)S(1)}, f32[2048]{0:T(1024)}, u32[]{:S(2)}) copy-start(f32[2048]{0:T(1024)} %param.20) | copy-start | bytes 24580
  14.1 11.2 %collective-permute-start.4 = (bf16[256,512]{1,0:T(8,128)(2,1)S(1)}, bf16[256,512]{1,0:T(8,128)(2,1)S(1)}, u32[]{:S(2)}, u32[]{:S(2)}) collective-permute-start(bf16[256,512]{1,0:T(8,128)(2,1)S(1)} %collective-permute-done.3.refs_5_), channel_id=1, source_target_pairs={{0,1},{1,2},{2,3},{3,0},{4,5},{5,6},{6,7},{7,4},{8,9},{9,10},{10,1... | collective-permute-start | bytes 786440 | tf_op jit(solution)/shard_map/ppermute | solution.py:687
  19.7 11.2 %collective-permute-start.1 = (bf16[256,512]{1,0:T(8,128)(2,1)S(1)}, bf16[256,512]{1,0:T(8,128)(2,1)S(1)}, u32[]{:S(2)}, u32[]{:S(2)}) collective-permute-start(bf16[256,512]{1,0:T(8,128)(2,1)S(1)} %collective-permute-done.refs_1_), channel_id=1, source_target_pairs={{0,1},{1,2},{2,3},{3,0},{4,5},{5,6},{6,7},{7,4},{8,9},{9,10},{10,1... | collective-permute-start | bytes 786440 | tf_op jit(solution)/shard_map/ppermute | solution.py:687
  25.3 11.2 %collective-permute-start.5 = (bf16[256,512]{1,0:T(8,128)(2,1)S(1)}, bf16[256,512]{1,0:T(8,128)(2,1)S(1)}, u32[]{:S(2)}, u32[]{:S(2)}) collective-permute-start(bf16[256,512]{1,0:T(8,128)(2,1)S(1)} %collective-permute-done.4.refs_6_), channel_id=1, source_target_pairs={{0,1},{1,2},{2,3},{3,0},{4,5},{5,6},{6,7},{7,4},{8,9},{9,10},{10,1... | collective-permute-start | bytes 786440 | tf_op jit(solution)/shard_map/ppermute | solution.py:687
  30.9 10.4 %collective-permute-start.2 = (bf16[256,512]{1,0:T(8,128)(2,1)S(1)}, bf16[256,512]{1,0:T(8,128)(2,1)S(1)}, u32[]{:S(2)}, u32[]{:S(2)}) collective-permute-start(bf16[256,512]{1,0:T(8,128)(2,1)S(1)} %collective-permute-done.1.refs_2_), channel_id=1, source_target_pairs={{0,1},{1,2},{2,3},{3,0},{4,5},{5,6},{6,7},{7,4},{8,9},{9,10},{10,1... | collective-permute-start | bytes 786440 | tf_op jit(solution)/shard_map/ppermute | solution.py:687
  31.0 23.8 %slice-start = ((s8[8388608]{0:T(1024)(128)(4,1)}), s8[4194304]{0:T(1024)(128)(4,1)S(1)}, s32[]{:S(2)}) async-start(s8[8388608]{0:T(1024)(128)(4,1)} %bitcast.26), calls=%async_computation | async-start | bytes 8388608
  41.3 11.3 %copy-start.10 = (bf16[512,512]{1,0:T(8,128)(2,1)S(1)}, bf16[512,512]{1,0:T(8,128)(2,1)}, u32[]{:S(2)}) copy-start(bf16[512,512]{1,0:T(8,128)(2,1)} %param.32) | copy-start | bytes 1572868
  41.4 13.4 %slice-start.1 = ((s8[8388608]{0:T(1024)(128)(4,1)}), s8[4194304]{0:T(1024)(128)(4,1)S(1)}, s32[]{:S(2)}) async-start(s8[8388608]{0:T(1024)(128)(4,1)} %bitcast.26), calls=%async_computation.1 | async-start | bytes 8388608
  49.2 16.9 %collective-permute-start.6 = (bf16[3,512,128]{2,1,0:T(8,128)(2,1)S(1)}, bf16[3,512,128]{2,1,0:T(8,128)(2,1)S(1)}, u32[]{:S(2)}, u32[]{:S(2)}) collective-permute-start(bf16[3,512,128]{2,1,0:T(8,128)(2,1)S(1)} %get-tuple-element.74), channel_id=1, source_target_pairs={{0,8},{4,12},{8,0},{12,4},{16,24},{20,28},{24,16},{28,20},{1,9},{5... | collective-permute-start | bytes 1179656 | tf_op jit(solution)/shard_map/ppermute | solution.py:709
  50.7 18.2 %collective-permute-start.7 = (bf16[3,512,128]{2,1,0:T(8,128)(2,1)S(1)}, bf16[3,512,128]{2,1,0:T(8,128)(2,1)S(1)}, u32[]{:S(2)}, u32[]{:S(2)}) collective-permute-start(bf16[3,512,128]{2,1,0:T(8,128)(2,1)S(1)} %get-tuple-element.75), channel_id=1, source_target_pairs={{0,16},{4,20},{8,24},{12,28},{16,0},{20,4},{24,8},{28,12},{1,17},{... | collective-permute-start | bytes 1179656 | tf_op jit(solution)/shard_map/ppermute | solution.py:709
  52.2 16.7 %collective-permute-start.8 = (bf16[3,512,128]{2,1,0:T(8,128)(2,1)S(1)}, bf16[3,512,128]{2,1,0:T(8,128)(2,1)S(1)}, u32[]{:S(2)}, u32[]{:S(2)}) collective-permute-start(bf16[3,512,128]{2,1,0:T(8,128)(2,1)S(1)} %get-tuple-element.76), channel_id=1, source_target_pairs={{0,24},{4,28},{8,16},{12,20},{16,8},{20,12},{24,0},{28,4},{1,25},{... | collective-permute-start | bytes 1179656 | tf_op jit(solution)/shard_map/ppermute | solution.py:709
  54.0 12.1 %collective-permute-start.9 = (bf16[512,256]{1,0:T(8,128)(2,1)S(1)}, bf16[512,256]{1,0:T(8,128)(2,1)S(1)}, u32[]{:S(2)}, u32[]{:S(2)}) collective-permute-start(bf16[512,256]{1,0:T(8,128)(2,1)S(1)} %constant_dynamic-slice_fusion.1), channel_id=1, source_target_pairs={{0,2},{1,3},{2,0},{3,1},{4,6},{5,7},{6,4},{7,5},{8,10},{9,11},{10,... | collective-permute-start | bytes 786440 | tf_op jit(solution)/shard_map/ppermute | solution.py:788
  60.4 12.9 %copy-start.11 = (s32[4096]{0:T(1024)S(1)}, s32[4096]{0:T(1024)}, u32[]{:S(2)}) copy-start(s32[4096]{0:T(1024)} %param.18) | copy-start | bytes 49156
  68.9 1.7 collective-permute-start.10
  68.9 3.2 %collective-permute-start.11 = (bf16[3,512,128]{2,1,0:T(8,128)(2,1)S(1)}, bf16[3,512,128]{2,1,0:T(8,128)(2,1)S(1)}, u32[]{:S(2)}, u32[]{:S(2)}) collective-permute-start(bf16[3,512,128]{2,1,0:T(8,128)(2,1)S(1)} %collective-permute-done.6.refs_1_), channel_id=1, source_target_pairs={{0,4},{4,0},{8,12},{12,8},{16,20},{20,16},{24,28},{28,24},{1,5},{5... | collective-permute-start | bytes 1179656 | tf_op jit(solution)/shard_map/ppermute | solution.py:717
  69.4 4.1 %collective-permute-start.12 = (bf16[3,512,128]{2,1,0:T(8,128)(2,1)S(1)}, bf16[3,512,128]{2,1,0:T(8,128)(2,1)S(1)}, u32[]{:S(2)}, u32[]{:S(2)}) collective-permute-start(bf16[3,512,128]{2,1,0:T(8,128)(2,1)S(1)} %collective-permute-done.7.refs_2_), channel_id=1, source_target_pairs={{0,4},{4,0},{8,12},{12,8},{16,20},{20,16},{24,28},{28,24},{1,5},{5... | collective-permute-start | bytes 1179656 | tf_op jit(solution)/shard_map/ppermute | solution.py:717
  69.4 4.9 %collective-permute-start.13 = (bf16[3,512,128]{2,1,0:T(8,128)(2,1)S(1)}, bf16[3,512,128]{2,1,0:T(8,128)(2,1)S(1)}, u32[]{:S(2)}, u32[]{:S(2)}) collective-permute-start(bf16[3,512,128]{2,1,0:T(8,128)(2,1)S(1)} %collective-permute-done.8.refs_3_), channel_id=1, source_target_pairs={{0,4},{4,0},{8,12},{12,8},{16,20},{20,16},{24,28},{28,24},{1,5},{5... | collective-permute-start | bytes 1179656 | tf_op jit(solution)/shard_map/ppermute | solution.py:717
  70.0 23.5 %collective-permute-start.17 = (bf16[2,512,256]{2,1,0:T(8,128)(2,1)S(1)}, bf16[2,512,256]{2,1,0:T(8,128)(2,1)S(1)}, u32[]{:S(2)}, u32[]{:S(2)}) collective-permute-start(bf16[2,512,256]{2,1,0:T(8,128)(2,1)S(1)} %pad_maximum_fusion), channel_id=1, source_target_pairs={{0,1},{1,0},{2,3},{3,2},{4,5},{5,4},{6,7},{7,6},{8,9},{9,8},{10,11... | collective-permute-start | bytes 1572872 | tf_op jit(solution)/shard_map/ppermute | solution.py:788
  70.6 14.7 %collective-permute-start.20 = (bf16[512,256]{1,0:T(8,128)(2,1)S(1)}, bf16[512,256]{1,0:T(8,128)(2,1)S(1)}, u32[]{:S(2)}, u32[]{:S(2)}) collective-permute-start(bf16[512,256]{1,0:T(8,128)(2,1)S(1)} %collective-permute-done.9.refs_10_), channel_id=1, source_target_pairs={{0,24},{4,28},{8,16},{12,20},{16,8},{20,12},{24,0},{28,4},{1,25},{... | collective-permute-start | bytes 786440 | tf_op jit(solution)/shard_map/ppermute | solution.py:709
  72.1 14.0 %collective-permute-start.19 = (bf16[512,256]{1,0:T(8,128)(2,1)S(1)}, bf16[512,256]{1,0:T(8,128)(2,1)S(1)}, u32[]{:S(2)}, u32[]{:S(2)}) collective-permute-start(bf16[512,256]{1,0:T(8,128)(2,1)S(1)} %collective-permute-done.9.refs_10_), channel_id=1, source_target_pairs={{0,16},{4,20},{8,24},{12,28},{16,0},{20,4},{24,8},{28,12},{1,17},{... | collective-permute-start | bytes 786440 | tf_op jit(solution)/shard_map/ppermute | solution.py:709
  73.5 14.1 %collective-permute-start.18 = (bf16[512,256]{1,0:T(8,128)(2,1)S(1)}, bf16[512,256]{1,0:T(8,128)(2,1)S(1)}, u32[]{:S(2)}, u32[]{:S(2)}) collective-permute-start(bf16[512,256]{1,0:T(8,128)(2,1)S(1)} %collective-permute-done.9.refs_10_), channel_id=1, source_target_pairs={{0,8},{4,12},{8,0},{12,4},{16,24},{20,28},{24,16},{28,20},{1,9},{5... | collective-permute-start | bytes 786440 | tf_op jit(solution)/shard_map/ppermute | solution.py:709
  84.0 54.8 %copy-start.7 = (f32[2048]{0:T(1024)S(1)}, f32[2048]{0:T(1024)}, u32[]{:S(2)}) copy-start(f32[2048]{0:T(1024)} %param.21) | copy-start | bytes 24580
  84.0 5.3 %collective-permute-start.14 = (bf16[512,128]{1,0:T(8,128)(2,1)S(1)}, bf16[512,128]{1,0:T(8,128)(2,1)S(1)}, u32[]{:S(2)}, u32[]{:S(2)}) collective-permute-start(bf16[512,128]{1,0:T(8,128)(2,1)S(1)} %get-tuple-element.90), channel_id=1, source_target_pairs={{0,8},{4,12},{8,0},{12,4},{16,24},{20,28},{24,16},{28,20},{1,9},{5... | collective-permute-start | bytes 393224 | tf_op jit(solution)/shard_map/ppermute | solution.py:709
  85.3 5.8 %collective-permute-start.15 = (bf16[512,128]{1,0:T(8,128)(2,1)S(1)}, bf16[512,128]{1,0:T(8,128)(2,1)S(1)}, u32[]{:S(2)}, u32[]{:S(2)}) collective-permute-start(bf16[512,128]{1,0:T(8,128)(2,1)S(1)} %get-tuple-element.91), channel_id=1, source_target_pairs={{0,16},{4,20},{8,24},{12,28},{16,0},{20,4},{24,8},{28,12},{1,17},{... | collective-permute-start | bytes 393224 | tf_op jit(solution)/shard_map/ppermute | solution.py:709
  86.1 7.3 %collective-permute-start.16 = (bf16[512,128]{1,0:T(8,128)(2,1)S(1)}, bf16[512,128]{1,0:T(8,128)(2,1)S(1)}, u32[]{:S(2)}, u32[]{:S(2)}) collective-permute-start(bf16[512,128]{1,0:T(8,128)(2,1)S(1)} %get-tuple-element.92), channel_id=1, source_target_pairs={{0,24},{4,28},{8,16},{12,20},{16,8},{20,12},{24,0},{28,4},{1,25},{... | collective-permute-start | bytes 393224 | tf_op jit(solution)/shard_map/ppermute | solution.py:709
  93.5 11.0 %collective-permute-start.21 = (bf16[2,512,128]{2,1,0:T(8,128)(2,1)S(1)}, bf16[2,512,128]{2,1,0:T(8,128)(2,1)S(1)}, u32[]{:S(2)}, u32[]{:S(2)}) collective-permute-start(bf16[2,512,128]{2,1,0:T(8,128)(2,1)S(1)} %pad_maximum_fusion.3.refs_0_), channel_id=1, source_target_pairs={{0,1},{1,2},{2,3},{3,0},{4,5},{5,6},{6,7},{7,4},{8,9},{9,10},{10,1... | collective-permute-start | bytes 786440 | tf_op jit(solution)/shard_map/ppermute | solution.py:687
  95.2 14.9 %collective-permute-start.24 = (bf16[2,512,128]{2,1,0:T(8,128)(2,1)S(1)}, bf16[2,512,128]{2,1,0:T(8,128)(2,1)S(1)}, u32[]{:S(2)}, u32[]{:S(2)}) collective-permute-start(bf16[2,512,128]{2,1,0:T(8,128)(2,1)S(1)} %pad_maximum_fusion.4.refs_4_), channel_id=1, source_target_pairs={{0,1},{1,2},{2,3},{3,0},{4,5},{5,6},{6,7},{7,4},{8,9},{9,10},{10,1... | collective-permute-start | bytes 786440 | tf_op jit(solution)/shard_map/ppermute | solution.py:687
  96.0 25.2 %collective-permute-start.29 = (bf16[2,512,256]{2,1,0:T(8,128)(2,1)S(1)}, bf16[2,512,256]{2,1,0:T(8,128)(2,1)S(1)}, u32[]{:S(2)}, u32[]{:S(2)}) collective-permute-start(bf16[2,512,256]{2,1,0:T(8,128)(2,1)S(1)} %collective-permute-done.17.refs_14_), channel_id=1, source_target_pairs={{0,24},{4,28},{8,16},{12,20},{16,8},{20,12},{24,0},{28,4},{1,25},{... | collective-permute-start | bytes 1572872 | tf_op jit(solution)/shard_map/ppermute | solution.py:709
  104.5 11.2 %collective-permute-start.22 = (bf16[2,512,128]{2,1,0:T(8,128)(2,1)S(1)}, bf16[2,512,128]{2,1,0:T(8,128)(2,1)S(1)}, u32[]{:S(2)}, u32[]{:S(2)}) collective-permute-start(bf16[2,512,128]{2,1,0:T(8,128)(2,1)S(1)} %collective-permute-done.21.refs_1_), channel_id=1, source_target_pairs={{0,1},{1,2},{2,3},{3,0},{4,5},{5,6},{6,7},{7,4},{8,9},{9,10},{10,1... | collective-permute-start | bytes 786440 | tf_op jit(solution)/shard_map/ppermute | solution.py:687
  104.5 17.6 %collective-permute-start.28 = (bf16[2,512,256]{2,1,0:T(8,128)(2,1)S(1)}, bf16[2,512,256]{2,1,0:T(8,128)(2,1)S(1)}, u32[]{:S(2)}, u32[]{:S(2)}) collective-permute-start(bf16[2,512,256]{2,1,0:T(8,128)(2,1)S(1)} %collective-permute-done.17.refs_14_), channel_id=1, source_target_pairs={{0,16},{4,20},{8,24},{12,28},{16,0},{20,4},{24,8},{28,12},{1,17},{... | collective-permute-start | bytes 1572872 | tf_op jit(solution)/shard_map/ppermute | solution.py:709
  105.6 16.4 %collective-permute-start.27 = (bf16[2,512,256]{2,1,0:T(8,128)(2,1)S(1)}, bf16[2,512,256]{2,1,0:T(8,128)(2,1)S(1)}, u32[]{:S(2)}, u32[]{:S(2)}) collective-permute-start(bf16[2,512,256]{2,1,0:T(8,128)(2,1)S(1)} %collective-permute-done.17.refs_14_), channel_id=1, source_target_pairs={{0,8},{4,12},{8,0},{12,4},{16,24},{20,28},{24,16},{28,20},{1,9},{5... | collective-permute-start | bytes 1572872 | tf_op jit(solution)/shard_map/ppermute | solution.py:709
  110.1 11.1 %collective-permute-start.25 = (bf16[2,512,128]{2,1,0:T(8,128)(2,1)S(1)}, bf16[2,512,128]{2,1,0:T(8,128)(2,1)S(1)}, u32[]{:S(2)}, u32[]{:S(2)}) collective-permute-start(bf16[2,512,128]{2,1,0:T(8,128)(2,1)S(1)} %collective-permute-done.24.refs_5_), channel_id=1, source_target_pairs={{0,1},{1,2},{2,3},{3,0},{4,5},{5,6},{6,7},{7,4},{8,9},{9,10},{10,1... | collective-permute-start | bytes 786440 | tf_op jit(solution)/shard_map/ppermute | solution.py:687
  115.7 23.1 %collective-permute-start.30 = (bf16[4,1,512,256]{3,2,0,1:T(8,128)(2,1)S(1)}, bf16[4,1,512,256]{3,2,0,1:T(8,128)(2,1)S(1)}, u32[]{:S(2)}, u32[]{:S(2)}) collective-permute-start(bf16[4,1,512,256]{3,2,0,1:T(8,128)(2,1)S(1)} %maximum_bitcast_fusion), channel_id=1, source_target_pairs={{0,4},{4,0},{8,12},{12,8},{16,20},{20,16},{24,28},{28,24},{1,5},{5... | collective-permute-start | bytes 3145736 | tf_op jit(solution)/shard_map/ppermute | solution.py:717
  121.2 11.0 %collective-permute-start.23 = (bf16[2,512,128]{2,1,0:T(8,128)(2,1)S(1)}, bf16[2,512,128]{2,1,0:T(8,128)(2,1)S(1)}, u32[]{:S(2)}, u32[]{:S(2)}) collective-permute-start(bf16[2,512,128]{2,1,0:T(8,128)(2,1)S(1)} %collective-permute-done.22.refs_2_), channel_id=1, source_target_pairs={{0,1},{1,2},{2,3},{3,0},{4,5},{5,6},{6,7},{7,4},{8,9},{9,10},{10,1... | collective-permute-start | bytes 786440 | tf_op jit(solution)/shard_map/ppermute | solution.py:687
  121.2 15.6 %collective-permute-start.26 = (bf16[2,512,128]{2,1,0:T(8,128)(2,1)S(1)}, bf16[2,512,128]{2,1,0:T(8,128)(2,1)S(1)}, u32[]{:S(2)}, u32[]{:S(2)}) collective-permute-start(bf16[2,512,128]{2,1,0:T(8,128)(2,1)S(1)} %collective-permute-done.25.refs_6_), channel_id=1, source_target_pairs={{0,1},{1,2},{2,3},{3,0},{4,5},{5,6},{6,7},{7,4},{8,9},{9,10},{10,1... | collective-permute-start | bytes 786440 | tf_op jit(solution)/shard_map/ppermute | solution.py:687
  122.1 14.8 %collective-permute-start.31 = (bf16[2,512,256]{2,1,0:T(8,128)(2,1)S(1)}, bf16[2,512,256]{2,1,0:T(8,128)(2,1)S(1)}, u32[]{:S(2)}, u32[]{:S(2)}) collective-permute-start(bf16[2,512,256]{2,1,0:T(8,128)(2,1)S(1)} %collective-permute-done.17.refs_14_), channel_id=1, source_target_pairs={{0,4},{4,0},{8,12},{12,8},{16,20},{20,16},{24,28},{28,24},{1,5},{5... | collective-permute-start | bytes 1572872 | tf_op jit(solution)/shard_map/ppermute | solution.py:717
  122.1 14.8 %collective-permute-start.34 = (bf16[2,512,256]{2,1,0:T(8,128)(2,1)S(1)}, bf16[2,512,256]{2,1,0:T(8,128)(2,1)S(1)}, u32[]{:S(2)}, u32[]{:S(2)}) collective-permute-start(bf16[2,512,256]{2,1,0:T(8,128)(2,1)S(1)} %collective-permute-done.29.refs_17_), channel_id=1, source_target_pairs={{0,4},{4,0},{8,12},{12,8},{16,20},{20,16},{24,28},{28,24},{1,5},{5... | collective-permute-start | bytes 1572872 | tf_op jit(solution)/shard_map/ppermute | solution.py:717
  132.2 4.7 %collective-permute-start.33 = (bf16[2,512,256]{2,1,0:T(8,128)(2,1)S(1)}, bf16[2,512,256]{2,1,0:T(8,128)(2,1)S(1)}, u32[]{:S(2)}, u32[]{:S(2)}) collective-permute-start(bf16[2,512,256]{2,1,0:T(8,128)(2,1)S(1)} %collective-permute-done.28.refs_16_), channel_id=1, source_target_pairs={{0,4},{4,0},{8,12},{12,8},{16,20},{20,16},{24,28},{28,24},{1,5},{5... | collective-permute-start | bytes 1572872 | tf_op jit(solution)/shard_map/ppermute | solution.py:717
  136.9 1.9 collective-permute-start.32
  160.9 12.9 %collective-permute-start.37 = (bf16[128,512]{1,0:T(8,128)(2,1)S(1)}, bf16[128,512]{1,0:T(8,128)(2,1)S(1)}, u32[]{:S(2)}, u32[]{:S(2)}) collective-permute-start(bf16[128,512]{1,0:T(8,128)(2,1)S(1)} %get-tuple-element.118), channel_id=1, source_target_pairs={{0,1},{1,2},{2,3},{3,0},{4,5},{5,6},{6,7},{7,4},{8,9},{9,10},{10,1... | collective-permute-start | bytes 393224 | tf_op jit(solution)/shard_map/ppermute | solution.py:700
  160.9 13.0 %collective-permute-start.38 = (bf16[128,512]{1,0:T(8,128)(2,1)S(1)}, bf16[128,512]{1,0:T(8,128)(2,1)S(1)}, u32[]{:S(2)}, u32[]{:S(2)}) collective-permute-start(bf16[128,512]{1,0:T(8,128)(2,1)S(1)} %get-tuple-element.119), channel_id=1, source_target_pairs={{0,2},{1,3},{2,0},{3,1},{4,6},{5,7},{6,4},{7,5},{8,10},{9,11},{10,... | collective-permute-start | bytes 393224 | tf_op jit(solution)/shard_map/ppermute | solution.py:700
  161.0 12.9 %collective-permute-start.39 = (bf16[128,512]{1,0:T(8,128)(2,1)S(1)}, bf16[128,512]{1,0:T(8,128)(2,1)S(1)}, u32[]{:S(2)}, u32[]{:S(2)}) collective-permute-start(bf16[128,512]{1,0:T(8,128)(2,1)S(1)} %get-tuple-element.120), channel_id=1, source_target_pairs={{0,3},{1,0},{2,1},{3,2},{4,7},{5,4},{6,5},{7,6},{8,11},{9,8},{10,9... | collective-permute-start | bytes 393224 | tf_op jit(solution)/shard_map/ppermute | solution.py:700
  168.2 19.0 %collective-permute-start.35 = (bf16[512,512]{1,0:T(8,128)(2,1)S(1)}, bf16[512,512]{1,0:T(8,128)(2,1)S(1)}, u32[]{:S(2)}, u32[]{:S(2)}) collective-permute-start(bf16[512,512]{1,0:T(8,128)(2,1)S(1)} %down.3), channel_id=1, source_target_pairs={{0,1},{1,0},{2,3},{3,2},{4,5},{5,4},{6,7},{7,6},{8,9},{9,8},{10,11... | collective-permute-start | bytes 1572872 | tf_op jit(solution)/shard_map/ppermute | solution.py:788
  175.0 14.9 %collective-permute-start.42 = (bf16[128,512]{1,0:T(8,128)(2,1)S(1)}, bf16[128,512]{1,0:T(8,128)(2,1)S(1)}, u32[]{:S(2)}, u32[]{:S(2)}) collective-permute-start(bf16[128,512]{1,0:T(8,128)(2,1)S(1)} %multiply_convert_fusion.3.refs_0_), channel_id=1, source_target_pairs={{0,3},{1,0},{2,1},{3,2},{4,7},{5,4},{6,5},{7,6},{8,11},{9,8},{10,9... | collective-permute-start | bytes 393224 | tf_op jit(solution)/shard_map/ppermute | solution.py:700
  177.9 12.0 %collective-permute-start.41 = (bf16[128,512]{1,0:T(8,128)(2,1)S(1)}, bf16[128,512]{1,0:T(8,128)(2,1)S(1)}, u32[]{:S(2)}, u32[]{:S(2)}) collective-permute-start(bf16[128,512]{1,0:T(8,128)(2,1)S(1)} %multiply_convert_fusion.3.refs_0_), channel_id=1, source_target_pairs={{0,2},{1,3},{2,0},{3,1},{4,6},{5,7},{6,4},{7,5},{8,10},{9,11},{10,... | collective-permute-start | bytes 393224 | tf_op jit(solution)/shard_map/ppermute | solution.py:700
  179.1 14.6 %collective-permute-start.40 = (bf16[128,512]{1,0:T(8,128)(2,1)S(1)}, bf16[128,512]{1,0:T(8,128)(2,1)S(1)}, u32[]{:S(2)}, u32[]{:S(2)}) collective-permute-start(bf16[128,512]{1,0:T(8,128)(2,1)S(1)} %multiply_convert_fusion.3.refs_0_), channel_id=1, source_target_pairs={{0,1},{1,2},{2,3},{3,0},{4,5},{5,6},{6,7},{7,4},{8,9},{9,10},{10,1... | collective-permute-start | bytes 393224 | tf_op jit(solution)/shard_map/ppermute | solution.py:700
  195.8 2.4 %collective-permute-start.43 = (bf16[4,208,512]{2,1,0:T(8,128)(2,1)S(1)}, bf16[4,208,512]{2,1,0:T(8,128)(2,1)S(1)}, u32[]{:S(2)}, u32[]{:S(2)}) collective-permute-start(bf16[4,208,512]{2,1,0:T(8,128)(2,1)S(1)} %get-tuple-element.126), channel_id=1, source_target_pairs={{0,4},{4,0},{8,12},{12,8},{16,20},{20,16},{24,28},{28,24},{1,5},{5... | collective-permute-start | bytes 2555912 | tf_op jit(solution)/shard_map/ppermute | solution.py:717
  198.5 8.2 %collective-permute-start.44 = (bf16[208,512]{1,0:T(8,128)(2,1)S(1)}, bf16[208,512]{1,0:T(8,128)(2,1)S(1)}, u32[]{:S(2)}, u32[]{:S(2)}) collective-permute-start(bf16[208,512]{1,0:T(8,128)(2,1)S(1)} %get-tuple-element.128), channel_id=1, source_target_pairs={{0,8},{4,12},{8,0},{12,4},{16,24},{20,28},{24,16},{28,20},{1,9},{5... | collective-permute-start | bytes 638984 | tf_op jit(solution)/shard_map/ppermute | solution.py:709
  199.2 11.6 %collective-permute-start.45 = (bf16[208,512]{1,0:T(8,128)(2,1)S(1)}, bf16[208,512]{1,0:T(8,128)(2,1)S(1)}, u32[]{:S(2)}, u32[]{:S(2)}) collective-permute-start(bf16[208,512]{1,0:T(8,128)(2,1)S(1)} %get-tuple-element.129), channel_id=1, source_target_pairs={{0,16},{4,20},{8,24},{12,28},{16,0},{20,4},{24,8},{28,12},{1,17},{... | collective-permute-start | bytes 638984 | tf_op jit(solution)/shard_map/ppermute | solution.py:709
  200.7 10.1 %collective-permute-start.46 = (bf16[208,512]{1,0:T(8,128)(2,1)S(1)}, bf16[208,512]{1,0:T(8,128)(2,1)S(1)}, u32[]{:S(2)}, u32[]{:S(2)}) collective-permute-start(bf16[208,512]{1,0:T(8,128)(2,1)S(1)} %get-tuple-element.130), channel_id=1, source_target_pairs={{0,24},{4,28},{8,16},{12,20},{16,8},{20,12},{24,0},{28,4},{1,25},{... | collective-permute-start | bytes 638984 | tf_op jit(solution)/shard_map/ppermute | solution.py:709
  202.2 25.3 %collective-permute-start.48 = (bf16[512,512]{1,0:T(8,128)(2,1)S(1)}, bf16[512,512]{1,0:T(8,128)(2,1)S(1)}, u32[]{:S(2)}, u32[]{:S(2)}) collective-permute-start(bf16[512,512]{1,0:T(8,128)(2,1)S(1)} %add_convert_fusion.1), channel_id=1, source_target_pairs={{0,2},{1,3},{2,0},{3,1},{4,6},{5,7},{6,4},{7,5},{8,10},{9,11},{10,... | collective-permute-start | bytes 1572872 | tf_op jit(solution)/shard_map/ppermute | solution.py:788
  202.8 24.8 %collective-permute-start.36 = (bf16[512,512]{1,0:T(8,128)(2,1)S(1)}, bf16[512,512]{1,0:T(8,128)(2,1)S(1)}, u32[]{:S(2)}, u32[]{:S(2)}) collective-permute-start(bf16[512,512]{1,0:T(8,128)(2,1)S(1)} %get-tuple-element.115), channel_id=1, source_target_pairs={{0,1},{1,0},{2,3},{3,2},{4,5},{5,4},{6,7},{7,6},{8,9},{9,8},{10,11... | collective-permute-start | bytes 1572872 | tf_op jit(solution)/shard_map/ppermute | solution.py:788
  210.9 16.6 %collective-permute-start.47 = (bf16[208,512]{1,0:T(8,128)(2,1)S(1)}, bf16[208,512]{1,0:T(8,128)(2,1)S(1)}, u32[]{:S(2)}, u32[]{:S(2)}) collective-permute-start(bf16[208,512]{1,0:T(8,128)(2,1)S(1)} %add_convert_fusion.2.refs_0_), channel_id=1, source_target_pairs={{0,24},{4,28},{8,16},{12,20},{16,8},{20,12},{24,0},{28,4},{1,25},{... | collective-permute-start | bytes 638984 | tf_op jit(solution)/shard_map/ppermute | solution.py:709
  212.4 15.5 %collective-permute-start.50 = (bf16[208,512]{1,0:T(8,128)(2,1)S(1)}, bf16[208,512]{1,0:T(8,128)(2,1)S(1)}, u32[]{:S(2)}, u32[]{:S(2)}) collective-permute-start(bf16[208,512]{1,0:T(8,128)(2,1)S(1)} %add_convert_fusion.2.refs_0_), channel_id=1, source_target_pairs={{0,16},{4,20},{8,24},{12,28},{16,0},{20,4},{24,8},{28,12},{1,17},{... | collective-permute-start | bytes 638984 | tf_op jit(solution)/shard_map/ppermute | solution.py:709
  213.8 14.4 %collective-permute-start.49 = (bf16[208,512]{1,0:T(8,128)(2,1)S(1)}, bf16[208,512]{1,0:T(8,128)(2,1)S(1)}, u32[]{:S(2)}, u32[]{:S(2)}) collective-permute-start(bf16[208,512]{1,0:T(8,128)(2,1)S(1)} %add_convert_fusion.2.refs_0_), channel_id=1, source_target_pairs={{0,8},{4,12},{8,0},{12,4},{16,24},{20,28},{24,16},{28,20},{1,9},{5... | collective-permute-start | bytes 638984 | tf_op jit(solution)/shard_map/ppermute | solution.py:709
  227.5 2.1 collective-permute-start.51
  227.6 2.2 collective-permute-start.54
  228.0 1.6 collective-permute-start.53
  228.1 1.7 collective-permute-start.52
  (6 other events, 22.6 us)

commit v12 on v11

--- a/solution.py
+++ b/solution.py
@@ -254,7 +254,7 @@
                 pltpu.SemaphoreType.DMA((4,)),
             ],
         ),
-        compiler_params=params(42),
+        compiler_params=params(30),
         cost_estimate=cost(6 * rows * depth * out_cols, 6 * depth * out_cols),
         name="qkv",
     )(info, *blocks[0], *blocks[1], gain, cosine, sine, *weights)

time: 230 us -> 232 us (level); the launches traced: 232 us -> 232 us
  no operation moved by 1% of the time
where the time goes in v12:
time: 232 us
  waiting for transfers between devices  117 us (50%)
  Pallas kernels  50 us (22%)
  starting transfers between devices  45.5 us (20%)
  matrix products  7.4 us (3%)
  other arithmetic  6.12 us (3%)
  local copies, waits for them, and re-layouts  4.03 us (2%)
    ppermute x12, waiting for transfers between devices, step_on(): return lax.ppermute(block, axis, [(i, (i + 1) % size) for i in range(size)])  64.6 us
    ppermute x5, waiting for transfers between devices, paired(): lax.ppermute(value, 'tensor', [(i, i ^ bit) for i in range(ring)])  26.5 us
    ppermute x18, starting transfers between devices, flipped(): lax.ppermute(pieces[f], 'dp', [(i, i ^ 2 * f) for i in range(size)])  22.7 us
    pallas_call x1, Pallas kernels, middle_call(): pl.pallas_call(functools.partial(middle_kernel, ring=ring, chips=chips),...  22.1 us
    ppermute x18, waiting for transfers between devices, flipped(): lax.ppermute(pieces[f], 'dp', [(i, i ^ 2 * f) for i in range(size)])  14.5 us
    pallas_call x1, Pallas kernels, attention_call(): pl.pallas_call(functools.partial(attention_kernel, chips=chips, ring=ring...  9.65 us
    ppermute x6, starting transfers between devices, shifted(): lax.ppermute(pieces[s], axis, [(i, (i + s) % size) for i in range(size)])  7.97 us
    ppermute x12, starting transfers between devices, step_on(): return lax.ppermute(block, axis, [(i, (i + 1) % size) for i in range(size)])  7.77 us
  transfers between devices with their start and end apart: 55, of which 30 were waited for; matrix products, arithmetic and copies ran while one was open for 6% of the time, Pallas kernels for 7%

profile of v12, /device:TPU:0, one launch (start us, length us, event | category | flops | bytes accessed | tf_op | source)
XLA Modules:
  0.0 231.5 jit_solution(723804625801942611)
XLA Ops:
  0.7 1.2 fusion.10
  1.9 3.1 %collective-permute-start.3 = (bf16[256,512]{1,0:T(8,128)(2,1)S(1)}, bf16[256,512]{1,0:T(8,128)(2,1)S(1)}, u32[]{:S(2)}, u32[]{:S(2)}) collective-permute-start(bf16[256,512]{1,0:T(8,128)(2,1)S(1)} %get-tuple-element.140.refs_4_), channel_id=1, source_target_pairs={{0,1},{1,2},{2,3},{3,0},{4,5},{5,6},{6,7},{7,4},{8,9},{9,10},{10,1... | collective-permute-start | bytes 786440 | tf_op jit(solution)/shard_map/ppermute | solution.py:687
  5.0 1.6 collective-permute-start
  7.3 1.0 fusion.3
  8.7 5.5 %collective-permute-done.3.refs_5_ = bf16[256,512]{1,0:T(8,128)(2,1)S(1)} collective-permute-done((bf16[256,512]{1,0:T(8,128)(2,1)S(1)}, bf16[256,512]{1,0:T(8,128)(2,1)S(1)}, u32[]{:S(2)}, u32[]{:S(2)}) %collective-permute-start.3) | collective-permute-done | bytes 262176 | tf_op jit(solution)/shard_map/ppermute | solution.py:687
  14.2 5.6 %collective-permute-done.refs_1_ = bf16[256,512]{1,0:T(8,128)(2,1)S(1)} collective-permute-done((bf16[256,512]{1,0:T(8,128)(2,1)S(1)}, bf16[256,512]{1,0:T(8,128)(2,1)S(1)}, u32[]{:S(2)}, u32[]{:S(2)}) %collective-permute-start) | collective-permute-done | bytes 262176 | tf_op jit(solution)/shard_map/ppermute | solution.py:687
  19.8 1.1 constant_dynamic-slice_fusion.1
  20.9 1.1 convert_element_type.98
  22.1 3.3 %collective-permute-done.4.refs_6_ = bf16[256,512]{1,0:T(8,128)(2,1)S(1)} collective-permute-done((bf16[256,512]{1,0:T(8,128)(2,1)S(1)}, bf16[256,512]{1,0:T(8,128)(2,1)S(1)}, u32[]{:S(2)}, u32[]{:S(2)}) %collective-permute-start.4) | collective-permute-done | bytes 262176 | tf_op jit(solution)/shard_map/ppermute | solution.py:687
  25.4 5.6 %collective-permute-done.1.refs_2_ = bf16[256,512]{1,0:T(8,128)(2,1)S(1)} collective-permute-done((bf16[256,512]{1,0:T(8,128)(2,1)S(1)}, bf16[256,512]{1,0:T(8,128)(2,1)S(1)}, u32[]{:S(2)}, u32[]{:S(2)}) %collective-permute-start.1) | collective-permute-done | bytes 262176 | tf_op jit(solution)/shard_map/ppermute | solution.py:687
  31.2 5.4 %collective-permute-done.5.refs_7_ = bf16[256,512]{1,0:T(8,128)(2,1)S(1)} collective-permute-done((bf16[256,512]{1,0:T(8,128)(2,1)S(1)}, bf16[256,512]{1,0:T(8,128)(2,1)S(1)}, u32[]{:S(2)}, u32[]{:S(2)}) %collective-permute-start.5) | collective-permute-done | bytes 262176 | tf_op jit(solution)/shard_map/ppermute | solution.py:687
  36.6 4.8 %collective-permute-done.2.refs_3_ = bf16[256,512]{1,0:T(8,128)(2,1)S(1)} collective-permute-done((bf16[256,512]{1,0:T(8,128)(2,1)S(1)}, bf16[256,512]{1,0:T(8,128)(2,1)S(1)}, u32[]{:S(2)}, u32[]{:S(2)}) %collective-permute-start.2) | collective-permute-done | bytes 262176 | tf_op jit(solution)/shard_map/ppermute | solution.py:687
  41.5 6.6 %qkv.1 = (bf16[3,512,128]{2,1,0:T(8,128)(2,1)S(1)}, bf16[3,512,128]{2,1,0:T(8,128)(2,1)S(1)}, bf16[3,512,128]{2,1,0:T(8,128)(2,1)S(1)}, bf16[3,512,128]{2,1,0:T(...) custom-call(s32[16]{0:T(128)S(1)} %fusion.9.info_ref, ...), custom_call_target="tpu_custom_call" | custom-call | flops 3221225472 | bytes 6291456 | tf_op jit(solution)/shard_map/qkv/pallas_call | solution.py:235
  48.1 1.6 collective-permute-start.6
  49.7 1.5 collective-permute-start.7
  52.1 0.8 multiply_convert_fusion
  53.8 5.7 %fusion.refs_26_ = bf16[2048,512]{1,0:T(8,128)(2,1)} fusion(bf16[2048,2048]{1,0:T(8,128)(2,1)S(1)} %bitcast.27, bf16[2048,512]{1,0:T(8,128)(2,1)S(1)} %copy-done.13), kind=kOutput, calls=%fused_computation.1 | convolution fusion | flops 4296015872 | bytes 12582912 | tf_op jit(solution)/shard_map/dot_general | solution.py:166
  59.9 5.1 %collective-permute-done.9.refs_10_ = bf16[512,256]{1,0:T(8,128)(2,1)S(1)} collective-permute-done((bf16[512,256]{1,0:T(8,128)(2,1)S(1)}, bf16[512,256]{1,0:T(8,128)(2,1)S(1)}, u32[]{:S(2)}, u32[]{:S(2)}) %collective-permute-start.9) | collective-permute-done | bytes 262176 | tf_op jit(solution)/shard_map/ppermute | solution.py:788
  65.1 2.8 %collective-permute-done.7.refs_2_ = bf16[3,512,128]{2,1,0:T(8,128)(2,1)S(1)} collective-permute-done((bf16[3,512,128]{2,1,0:T(8,128)(2,1)S(1)}, bf16[3,512,128]{2,1,0:T(8,128)(2,1)S(1)}, u32[]{:S(2)}, u32[]{:S(2)}) %collective-permute-start.7) | collective-permute-done | bytes 393248 | tf_op jit(solution)/shard_map/ppermute | solution.py:709
  69.6 1.5 collective-permute-start.20
  71.1 1.2 collective-permute-start.19
  72.5 0.9 collective-permute-start.18
  73.3 9.7 %attention.1 = (bf16[512,128]{1,0:T(8,128)(2,1)S(1)}, bf16[512,128]{1,0:T(8,128)(2,1)S(1)}, bf16[512,128]{1,0:T(8,128)(2,1)S(1)}, bf16[512,128]{1,0:T(8,128)(2,1)S(1)}) custom-call(s32[8]{0:T(128)S(1)} %convert_reduce_fusion.first_ref, s32[16]{0:T(128)S(1)} %fusion.9.info_ref, bf16[3,512,128]{2,1,0:T(8,128)(2,1)S(1)} %get-tuple-element.84.refs_0_, ...), custom_call_target="tpu_custom_call" | custom-call | flops 2147483648 | bytes 4194304 | tf_op jit(solution)/shard_map/attention/pallas_call | solution.py:343
  83.0 1.3 collective-permute-start.14
  84.3 0.8 collective-permute-start.15
  85.1 1.4 collective-permute-start.16
  86.5 1.7 collective-permute-done.14
  88.3 1.9 collective-permute-done.15
  90.2 2.2 collective-permute-done.16
  92.5 1.7 collective-permute-start.21
  94.2 0.8 collective-permute-start.24
  95.1 2.2 collective-permute-start.29
  97.3 6.2 %collective-permute-done.21.refs_1_ = bf16[2,512,128]{2,1,0:T(8,128)(2,1)S(1)} collective-permute-done((bf16[2,512,128]{2,1,0:T(8,128)(2,1)S(1)}, bf16[2,512,128]{2,1,0:T(8,128)(2,1)S(1)}, u32[]{:S(2)}, u32[]{:S(2)}) %collective-permute-start.21) | collective-permute-done | bytes 262176 | tf_op jit(solution)/shard_map/ppermute | solution.py:687
  103.5 1.2 collective-permute-start.28
  104.7 1.5 collective-permute-start.27
  106.2 2.9 %collective-permute-done.24.refs_5_ = bf16[2,512,128]{2,1,0:T(8,128)(2,1)S(1)} collective-permute-done((bf16[2,512,128]{2,1,0:T(8,128)(2,1)S(1)}, bf16[2,512,128]{2,1,0:T(8,128)(2,1)S(1)}, u32[]{:S(2)}, u32[]{:S(2)}) %collective-permute-start.24) | collective-permute-done | bytes 262176 | tf_op jit(solution)/shard_map/ppermute | solution.py:687
  109.2 5.5 %collective-permute-done.22.refs_2_ = bf16[2,512,128]{2,1,0:T(8,128)(2,1)S(1)} collective-permute-done((bf16[2,512,128]{2,1,0:T(8,128)(2,1)S(1)}, bf16[2,512,128]{2,1,0:T(8,128)(2,1)S(1)}, u32[]{:S(2)}, u32[]{:S(2)}) %collective-permute-start.22) | collective-permute-done | bytes 262176 | tf_op jit(solution)/shard_map/ppermute | solution.py:687
  114.7 5.5 %collective-permute-done.25.refs_6_ = bf16[2,512,128]{2,1,0:T(8,128)(2,1)S(1)} collective-permute-done((bf16[2,512,128]{2,1,0:T(8,128)(2,1)S(1)}, bf16[2,512,128]{2,1,0:T(8,128)(2,1)S(1)}, u32[]{:S(2)}, u32[]{:S(2)}) %collective-permute-start.25) | collective-permute-done | bytes 262176 | tf_op jit(solution)/shard_map/ppermute | solution.py:687
  121.6 9.6 %collective-permute-done.23.refs_3_ = bf16[2,512,128]{2,1,0:T(8,128)(2,1)S(1)} collective-permute-done((bf16[2,512,128]{2,1,0:T(8,128)(2,1)S(1)}, bf16[2,512,128]{2,1,0:T(8,128)(2,1)S(1)}, u32[]{:S(2)}, u32[]{:S(2)}) %collective-permute-start.23) | collective-permute-done | bytes 262176 | tf_op jit(solution)/shard_map/ppermute | solution.py:687
  131.2 4.7 %collective-permute-done.26.refs_7_ = bf16[2,512,128]{2,1,0:T(8,128)(2,1)S(1)} collective-permute-done((bf16[2,512,128]{2,1,0:T(8,128)(2,1)S(1)}, bf16[2,512,128]{2,1,0:T(8,128)(2,1)S(1)}, u32[]{:S(2)}, u32[]{:S(2)}) %collective-permute-start.26) | collective-permute-done | bytes 262176 | tf_op jit(solution)/shard_map/ppermute | solution.py:687
  135.9 1.9 collective-permute-done.32.refs_20_
  137.8 22.1 %middle.1 = (bf16[512,2048]{1,0:T(8,128)(2,1)}, bf16[512,512]{1,0:T(8,128)(2,1)S(1)}, bf16[128,512]{1,0:T(8,128)(2,1)S(1)}, bf16[128,512]{1,0:T(8,128)(2,1)S(1)}...) custom-call(s32[16]{0:T(128)S(1)} %fusion.9.info_ref, bf16[2,512,128]{2,1,0:T(8,128)(2,1)S(1)} %pad_maximum_fusion.3.refs_0_, ...), custom_call_target="tpu_custom_call" | custom-call | flops 14227079168 | bytes 25165824 | tf_op jit(solution)/shard_map/middle/pallas_call | solution.py:488
  160.1 3.7 %collective-permute-start.39 = (bf16[128,512]{1,0:T(8,128)(2,1)S(1)}, bf16[128,512]{1,0:T(8,128)(2,1)S(1)}, u32[]{:S(2)}, u32[]{:S(2)}) collective-permute-start(bf16[128,512]{1,0:T(8,128)(2,1)S(1)} %get-tuple-element.120), channel_id=1, source_target_pairs={{0,3},{1,0},{2,1},{3,2},{4,7},{5,4},{6,5},{7,6},{8,11},{9,8},{10,9... | collective-permute-start | bytes 393224 | tf_op jit(solution)/shard_map/ppermute | solution.py:700
  163.8 1.6 copy-done.2
  165.4 1.8 down.3
  167.8 5.0 %down.2 = (bf16[512,512]{1,0:T(8,128)(2,1)S(1)}, bf16[512,512]{1,0:T(8,128)(2,1)S(1)}, bf16[512,512]{1,0:T(8,128)(2,1)S(1)}) custom-call(s32[16]{0:T(128)S(1)} %fusion.9.info_ref, bf16[512,2048]{1,0:T(8,128)(2,1)S(1)} %copy-done.2, bf16[2048,2048]{1,0:T(8,128)(2,1)S(1)} %bitcast.27), custom_call_target="tpu_custom_call" | custom-call | flops 3221225472 | bytes 6291456 | tf_op jit(solution)/shard_map/down/pallas_call | solution.py:562
  172.9 1.1 multiply_convert_fusion.3.refs_0_
  174.0 2.9 %collective-permute-start.42 = (bf16[128,512]{1,0:T(8,128)(2,1)S(1)}, bf16[128,512]{1,0:T(8,128)(2,1)S(1)}, u32[]{:S(2)}, u32[]{:S(2)}) collective-permute-start(bf16[128,512]{1,0:T(8,128)(2,1)S(1)} %multiply_convert_fusion.3.refs_0_), channel_id=1, source_target_pairs={{0,3},{1,0},{2,1},{3,2},{4,7},{5,4},{6,5},{7,6},{8,11},{9,8},{10,9... | collective-permute-start | bytes 393224 | tf_op jit(solution)/shard_map/ppermute | solution.py:700
  176.9 1.2 collective-permute-start.41
  178.1 8.1 %collective-permute-done.35 = bf16[512,512]{1,0:T(8,128)(2,1)S(1)} collective-permute-done((bf16[512,512]{1,0:T(8,128)(2,1)S(1)}, bf16[512,512]{1,0:T(8,128)(2,1)S(1)}, u32[]{:S(2)}, u32[]{:S(2)}) %collective-permute-start.35) | collective-permute-done | bytes 524320 | tf_op jit(solution)/shard_map/ppermute | solution.py:788
  186.2 2.7 %collective-permute-done.42.refs_3_ = bf16[128,512]{1,0:T(8,128)(2,1)S(1)} collective-permute-done((bf16[128,512]{1,0:T(8,128)(2,1)S(1)}, bf16[128,512]{1,0:T(8,128)(2,1)S(1)}, u32[]{:S(2)}, u32[]{:S(2)}) %collective-permute-start.42) | collective-permute-done | bytes 131104 | tf_op jit(solution)/shard_map/ppermute | solution.py:700
  188.9 3.7 %collective-permute-done.40.refs_1_ = bf16[128,512]{1,0:T(8,128)(2,1)S(1)} collective-permute-done((bf16[128,512]{1,0:T(8,128)(2,1)S(1)}, bf16[128,512]{1,0:T(8,128)(2,1)S(1)}, u32[]{:S(2)}, u32[]{:S(2)}) %collective-permute-start.40) | collective-permute-done | bytes 131104 | tf_op jit(solution)/shard_map/ppermute | solution.py:700
  192.7 2.2 grads.1
  195.0 2.4 %collective-permute-done.43.theirs_ref = bf16[4,208,512]{2,1,0:T(8,128)(2,1)S(1)} collective-permute-done((bf16[4,208,512]{2,1,0:T(8,128)(2,1)S(1)}, bf16[4,208,512]{2,1,0:T(8,128)(2,1)S(1)}, u32[]{:S(2)}, u32[]{:S(2)}) %collective-permute-start.43) | collective-permute-done | bytes 852000 | tf_op jit(solution)/shard_map/ppermute | solution.py:717
  198.2 1.5 collective-permute-start.45
  199.7 1.4 collective-permute-start.46
  201.9 2.5 %collective-permute-start.36 = (bf16[512,512]{1,0:T(8,128)(2,1)S(1)}, bf16[512,512]{1,0:T(8,128)(2,1)S(1)}, u32[]{:S(2)}, u32[]{:S(2)}) collective-permute-start(bf16[512,512]{1,0:T(8,128)(2,1)S(1)} %get-tuple-element.115), channel_id=1, source_target_pairs={{0,1},{1,0},{2,3},{3,2},{4,5},{5,4},{6,7},{7,6},{8,9},{9,8},{10,11... | collective-permute-start | bytes 1572872 | tf_op jit(solution)/shard_map/ppermute | solution.py:788
  204.4 1.3 collective-permute-done.44
  205.7 4.0 %collective-permute-done.45 = bf16[208,512]{1,0:T(8,128)(2,1)S(1)} collective-permute-done((bf16[208,512]{1,0:T(8,128)(2,1)S(1)}, bf16[208,512]{1,0:T(8,128)(2,1)S(1)}, u32[]{:S(2)}, u32[]{:S(2)}) %collective-permute-start.45) | collective-permute-done | bytes 213024 | tf_op jit(solution)/shard_map/ppermute | solution.py:709
  209.9 1.6 collective-permute-start.47
  211.4 1.4 collective-permute-start.50
  213.4 13.1 %collective-permute-done.48 = bf16[512,512]{1,0:T(8,128)(2,1)S(1)} collective-permute-done((bf16[512,512]{1,0:T(8,128)(2,1)S(1)}, bf16[512,512]{1,0:T(8,128)(2,1)S(1)}, u32[]{:S(2)}, u32[]{:S(2)}) %collective-permute-start.48) | collective-permute-done | bytes 524320 | tf_op jit(solution)/shard_map/ppermute | solution.py:788
  227.6 1.1 add_convert_fusion
  228.9 2.4 %finish.1 = (f32[512,512]{1,0:T(8,128)}, f32[512,512]{1,0:T(8,128)}, f32[512,512]{1,0:T(8,128)}, f32[1,1]{1,0:T(1,128)}) custom-call(s32[16]{0:T(128)S(1)} %fusion.9.info_ref, bf16[208,512]{1,0:T(8,128)(2,1)S(1)} %add_convert_fusion.2.refs_0_, bf16[208,512]{1,0:T(8,128)(2,1)S(1)} %collective-permute-done.49.refs_1_, ...), custom_call_target="tpu_custom_call" | custom-call | flops 262144 | bytes 3145728 | tf_op jit(solution)/shard_map/finish/pallas_call | solution.py:668
  (111 shorter events, 11.6 us)
Async XLA Ops:
  0.6 51.5 %copy-start = (bf16[512,512]{1,0:T(8,128)(2,1)S(1)}, bf16[512,512]{1,0:T(8,128)(2,1)}, u32[]{:S(2)}) copy-start(bf16[512,512]{1,0:T(8,128)(2,1)} %param.31) | copy-start | bytes 1572868
  0.7 40.7 %copy-start.6 = (bf16[2048,512]{1,0:T(8,128)(2,1)S(1)}, bf16[2048,512]{1,0:T(8,128)(2,1)}, u32[]{:S(2)}) copy-start(bf16[2048,512]{1,0:T(8,128)(2,1)} %refs_13_.1) | copy-start | bytes 6291460
  1.9 12.2 %collective-permute-start.3 = (bf16[256,512]{1,0:T(8,128)(2,1)S(1)}, bf16[256,512]{1,0:T(8,128)(2,1)S(1)}, u32[]{:S(2)}, u32[]{:S(2)}) collective-permute-start(bf16[256,512]{1,0:T(8,128)(2,1)S(1)} %get-tuple-element.140.refs_4_), channel_id=1, source_target_pairs={{0,1},{1,2},{2,3},{3,0},{4,5},{5,6},{6,7},{7,4},{8,9},{9,10},{10,1... | collective-permute-start | bytes 786440 | tf_op jit(solution)/shard_map/ppermute | solution.py:687
  5.0 14.8 %collective-permute-start = (bf16[256,512]{1,0:T(8,128)(2,1)S(1)}, bf16[256,512]{1,0:T(8,128)(2,1)S(1)}, u32[]{:S(2)}, u32[]{:S(2)}) collective-permute-start(bf16[256,512]{1,0:T(8,128)(2,1)S(1)} %get-tuple-element.141.refs_0_), channel_id=1, source_target_pairs={{0,1},{1,2},{2,3},{3,0},{4,5},{5,6},{6,7},{7,4},{8,9},{9,10},{10,1... | collective-permute-start | bytes 786440 | tf_op jit(solution)/shard_map/ppermute | solution.py:687
  8.3 33.2 %copy-start.5 = (bf16[2048,512]{1,0:T(8,128)(2,1)S(1)}, bf16[2048,512]{1,0:T(8,128)(2,1)}, u32[]{:S(2)}) copy-start(bf16[2048,512]{1,0:T(8,128)(2,1)} %refs_12_.1) | copy-start | bytes 6291460
  8.5 32.9 %copy-start.4 = (bf16[2048,512]{1,0:T(8,128)(2,1)S(1)}, bf16[2048,512]{1,0:T(8,128)(2,1)}, u32[]{:S(2)}) copy-start(bf16[2048,512]{1,0:T(8,128)(2,1)} %refs_11_.1) | copy-start | bytes 6291460
  8.5 32.9 %copy-start.7 = (f32[2048]{0:T(1024)S(1)}, f32[2048]{0:T(1024)}, u32[]{:S(2)}) copy-start(f32[2048]{0:T(1024)} %param.20) | copy-start | bytes 24580
  14.2 11.2 %collective-permute-start.4 = (bf16[256,512]{1,0:T(8,128)(2,1)S(1)}, bf16[256,512]{1,0:T(8,128)(2,1)S(1)}, u32[]{:S(2)}, u32[]{:S(2)}) collective-permute-start(bf16[256,512]{1,0:T(8,128)(2,1)S(1)} %collective-permute-done.3.refs_5_), channel_id=1, source_target_pairs={{0,1},{1,2},{2,3},{3,0},{4,5},{5,6},{6,7},{7,4},{8,9},{9,10},{10,1... | collective-permute-start | bytes 786440 | tf_op jit(solution)/shard_map/ppermute | solution.py:687
  19.8 11.2 %collective-permute-start.1 = (bf16[256,512]{1,0:T(8,128)(2,1)S(1)}, bf16[256,512]{1,0:T(8,128)(2,1)S(1)}, u32[]{:S(2)}, u32[]{:S(2)}) collective-permute-start(bf16[256,512]{1,0:T(8,128)(2,1)S(1)} %collective-permute-done.refs_1_), channel_id=1, source_target_pairs={{0,1},{1,2},{2,3},{3,0},{4,5},{5,6},{6,7},{7,4},{8,9},{9,10},{10,1... | collective-permute-start | bytes 786440 | tf_op jit(solution)/shard_map/ppermute | solution.py:687
  25.4 11.2 %collective-permute-start.5 = (bf16[256,512]{1,0:T(8,128)(2,1)S(1)}, bf16[256,512]{1,0:T(8,128)(2,1)S(1)}, u32[]{:S(2)}, u32[]{:S(2)}) collective-permute-start(bf16[256,512]{1,0:T(8,128)(2,1)S(1)} %collective-permute-done.4.refs_6_), channel_id=1, source_target_pairs={{0,1},{1,2},{2,3},{3,0},{4,5},{5,6},{6,7},{7,4},{8,9},{9,10},{10,1... | collective-permute-start | bytes 786440 | tf_op jit(solution)/shard_map/ppermute | solution.py:687
  31.0 10.4 %collective-permute-start.2 = (bf16[256,512]{1,0:T(8,128)(2,1)S(1)}, bf16[256,512]{1,0:T(8,128)(2,1)S(1)}, u32[]{:S(2)}, u32[]{:S(2)}) collective-permute-start(bf16[256,512]{1,0:T(8,128)(2,1)S(1)} %collective-permute-done.1.refs_2_), channel_id=1, source_target_pairs={{0,1},{1,2},{2,3},{3,0},{4,5},{5,6},{6,7},{7,4},{8,9},{9,10},{10,1... | collective-permute-start | bytes 786440 | tf_op jit(solution)/shard_map/ppermute | solution.py:687
  31.0 22.8 %slice-start = ((s8[8388608]{0:T(1024)(128)(4,1)}), s8[4194304]{0:T(1024)(128)(4,1)S(1)}, s32[]{:S(2)}) async-start(s8[8388608]{0:T(1024)(128)(4,1)} %bitcast.26), calls=%async_computation | async-start | bytes 8388608
  41.4 12.4 %slice-start.1 = ((s8[8388608]{0:T(1024)(128)(4,1)}), s8[4194304]{0:T(1024)(128)(4,1)S(1)}, s32[]{:S(2)}) async-start(s8[8388608]{0:T(1024)(128)(4,1)} %bitcast.26), calls=%async_computation.1 | async-start | bytes 8388608
  48.1 17.0 %collective-permute-start.6 = (bf16[3,512,128]{2,1,0:T(8,128)(2,1)S(1)}, bf16[3,512,128]{2,1,0:T(8,128)(2,1)S(1)}, u32[]{:S(2)}, u32[]{:S(2)}) collective-permute-start(bf16[3,512,128]{2,1,0:T(8,128)(2,1)S(1)} %get-tuple-element.74), channel_id=1, source_target_pairs={{0,8},{4,12},{8,0},{12,4},{16,24},{20,28},{24,16},{28,20},{1,9},{5... | collective-permute-start | bytes 1179656 | tf_op jit(solution)/shard_map/ppermute | solution.py:709
  49.7 18.2 %collective-permute-start.7 = (bf16[3,512,128]{2,1,0:T(8,128)(2,1)S(1)}, bf16[3,512,128]{2,1,0:T(8,128)(2,1)S(1)}, u32[]{:S(2)}, u32[]{:S(2)}) collective-permute-start(bf16[3,512,128]{2,1,0:T(8,128)(2,1)S(1)} %get-tuple-element.75), channel_id=1, source_target_pairs={{0,16},{4,20},{8,24},{12,28},{16,0},{20,4},{24,8},{28,12},{1,17},{... | collective-permute-start | bytes 1179656 | tf_op jit(solution)/shard_map/ppermute | solution.py:709
  51.2 16.7 %collective-permute-start.8 = (bf16[3,512,128]{2,1,0:T(8,128)(2,1)S(1)}, bf16[3,512,128]{2,1,0:T(8,128)(2,1)S(1)}, u32[]{:S(2)}, u32[]{:S(2)}) collective-permute-start(bf16[3,512,128]{2,1,0:T(8,128)(2,1)S(1)} %get-tuple-element.76), channel_id=1, source_target_pairs={{0,24},{4,28},{8,16},{12,20},{16,8},{20,12},{24,0},{28,4},{1,25},{... | collective-permute-start | bytes 1179656 | tf_op jit(solution)/shard_map/ppermute | solution.py:709
  53.0 12.1 %collective-permute-start.9 = (bf16[512,256]{1,0:T(8,128)(2,1)S(1)}, bf16[512,256]{1,0:T(8,128)(2,1)S(1)}, u32[]{:S(2)}, u32[]{:S(2)}) collective-permute-start(bf16[512,256]{1,0:T(8,128)(2,1)S(1)} %constant_dynamic-slice_fusion.1), channel_id=1, source_target_pairs={{0,2},{1,3},{2,0},{3,1},{4,6},{5,7},{6,4},{7,5},{8,10},{9,11},{10,... | collective-permute-start | bytes 786440 | tf_op jit(solution)/shard_map/ppermute | solution.py:788
  59.5 12.8 %copy-start.12 = (s32[4096]{0:T(1024)S(1)}, s32[4096]{0:T(1024)}, u32[]{:S(2)}) copy-start(s32[4096]{0:T(1024)} %param.18) | copy-start | bytes 49156
  67.9 1.7 collective-permute-start.10
  67.9 3.2 %collective-permute-start.11 = (bf16[3,512,128]{2,1,0:T(8,128)(2,1)S(1)}, bf16[3,512,128]{2,1,0:T(8,128)(2,1)S(1)}, u32[]{:S(2)}, u32[]{:S(2)}) collective-permute-start(bf16[3,512,128]{2,1,0:T(8,128)(2,1)S(1)} %collective-permute-done.6.refs_1_), channel_id=1, source_target_pairs={{0,4},{4,0},{8,12},{12,8},{16,20},{20,16},{24,28},{28,24},{1,5},{5... | collective-permute-start | bytes 1179656 | tf_op jit(solution)/shard_map/ppermute | solution.py:717
  68.4 4.1 %collective-permute-start.12 = (bf16[3,512,128]{2,1,0:T(8,128)(2,1)S(1)}, bf16[3,512,128]{2,1,0:T(8,128)(2,1)S(1)}, u32[]{:S(2)}, u32[]{:S(2)}) collective-permute-start(bf16[3,512,128]{2,1,0:T(8,128)(2,1)S(1)} %collective-permute-done.7.refs_2_), channel_id=1, source_target_pairs={{0,4},{4,0},{8,12},{12,8},{16,20},{20,16},{24,28},{28,24},{1,5},{5... | collective-permute-start | bytes 1179656 | tf_op jit(solution)/shard_map/ppermute | solution.py:717
  68.4 4.9 %collective-permute-start.13 = (bf16[3,512,128]{2,1,0:T(8,128)(2,1)S(1)}, bf16[3,512,128]{2,1,0:T(8,128)(2,1)S(1)}, u32[]{:S(2)}, u32[]{:S(2)}) collective-permute-start(bf16[3,512,128]{2,1,0:T(8,128)(2,1)S(1)} %collective-permute-done.8.refs_3_), channel_id=1, source_target_pairs={{0,4},{4,0},{8,12},{12,8},{16,20},{20,16},{24,28},{28,24},{1,5},{5... | collective-permute-start | bytes 1179656 | tf_op jit(solution)/shard_map/ppermute | solution.py:717
  69.0 23.5 %collective-permute-start.17 = (bf16[2,512,256]{2,1,0:T(8,128)(2,1)S(1)}, bf16[2,512,256]{2,1,0:T(8,128)(2,1)S(1)}, u32[]{:S(2)}, u32[]{:S(2)}) collective-permute-start(bf16[2,512,256]{2,1,0:T(8,128)(2,1)S(1)} %pad_maximum_fusion), channel_id=1, source_target_pairs={{0,1},{1,0},{2,3},{3,2},{4,5},{5,4},{6,7},{7,6},{8,9},{9,8},{10,11... | collective-permute-start | bytes 1572872 | tf_op jit(solution)/shard_map/ppermute | solution.py:788
  69.6 14.7 %collective-permute-start.20 = (bf16[512,256]{1,0:T(8,128)(2,1)S(1)}, bf16[512,256]{1,0:T(8,128)(2,1)S(1)}, u32[]{:S(2)}, u32[]{:S(2)}) collective-permute-start(bf16[512,256]{1,0:T(8,128)(2,1)S(1)} %collective-permute-done.9.refs_10_), channel_id=1, source_target_pairs={{0,24},{4,28},{8,16},{12,20},{16,8},{20,12},{24,0},{28,4},{1,25},{... | collective-permute-start | bytes 786440 | tf_op jit(solution)/shard_map/ppermute | solution.py:709
  71.1 14.0 %collective-permute-start.19 = (bf16[512,256]{1,0:T(8,128)(2,1)S(1)}, bf16[512,256]{1,0:T(8,128)(2,1)S(1)}, u32[]{:S(2)}, u32[]{:S(2)}) collective-permute-start(bf16[512,256]{1,0:T(8,128)(2,1)S(1)} %collective-permute-done.9.refs_10_), channel_id=1, source_target_pairs={{0,16},{4,20},{8,24},{12,28},{16,0},{20,4},{24,8},{28,12},{1,17},{... | collective-permute-start | bytes 786440 | tf_op jit(solution)/shard_map/ppermute | solution.py:709
  72.5 14.1 %collective-permute-start.18 = (bf16[512,256]{1,0:T(8,128)(2,1)S(1)}, bf16[512,256]{1,0:T(8,128)(2,1)S(1)}, u32[]{:S(2)}, u32[]{:S(2)}) collective-permute-start(bf16[512,256]{1,0:T(8,128)(2,1)S(1)} %collective-permute-done.9.refs_10_), channel_id=1, source_target_pairs={{0,8},{4,12},{8,0},{12,4},{16,24},{20,28},{24,16},{28,20},{1,9},{5... | collective-permute-start | bytes 786440 | tf_op jit(solution)/shard_map/ppermute | solution.py:709
  83.0 54.9 %copy-start.8 = (f32[2048]{0:T(1024)S(1)}, f32[2048]{0:T(1024)}, u32[]{:S(2)}) copy-start(f32[2048]{0:T(1024)} %param.21) | copy-start | bytes 24580
  83.0 5.3 %collective-permute-start.14 = (bf16[512,128]{1,0:T(8,128)(2,1)S(1)}, bf16[512,128]{1,0:T(8,128)(2,1)S(1)}, u32[]{:S(2)}, u32[]{:S(2)}) collective-permute-start(bf16[512,128]{1,0:T(8,128)(2,1)S(1)} %get-tuple-element.90), channel_id=1, source_target_pairs={{0,8},{4,12},{8,0},{12,4},{16,24},{20,28},{24,16},{28,20},{1,9},{5... | collective-permute-start | bytes 393224 | tf_op jit(solution)/shard_map/ppermute | solution.py:709
  84.3 5.9 %collective-permute-start.15 = (bf16[512,128]{1,0:T(8,128)(2,1)S(1)}, bf16[512,128]{1,0:T(8,128)(2,1)S(1)}, u32[]{:S(2)}, u32[]{:S(2)}) collective-permute-start(bf16[512,128]{1,0:T(8,128)(2,1)S(1)} %get-tuple-element.91), channel_id=1, source_target_pairs={{0,16},{4,20},{8,24},{12,28},{16,0},{20,4},{24,8},{28,12},{1,17},{... | collective-permute-start | bytes 393224 | tf_op jit(solution)/shard_map/ppermute | solution.py:709
  85.1 7.3 %collective-permute-start.16 = (bf16[512,128]{1,0:T(8,128)(2,1)S(1)}, bf16[512,128]{1,0:T(8,128)(2,1)S(1)}, u32[]{:S(2)}, u32[]{:S(2)}) collective-permute-start(bf16[512,128]{1,0:T(8,128)(2,1)S(1)} %get-tuple-element.92), channel_id=1, source_target_pairs={{0,24},{4,28},{8,16},{12,20},{16,8},{20,12},{24,0},{28,4},{1,25},{... | collective-permute-start | bytes 393224 | tf_op jit(solution)/shard_map/ppermute | solution.py:709
  92.5 11.0 %collective-permute-start.21 = (bf16[2,512,128]{2,1,0:T(8,128)(2,1)S(1)}, bf16[2,512,128]{2,1,0:T(8,128)(2,1)S(1)}, u32[]{:S(2)}, u32[]{:S(2)}) collective-permute-start(bf16[2,512,128]{2,1,0:T(8,128)(2,1)S(1)} %pad_maximum_fusion.3.refs_0_), channel_id=1, source_target_pairs={{0,1},{1,2},{2,3},{3,0},{4,5},{5,6},{6,7},{7,4},{8,9},{9,10},{10,1... | collective-permute-start | bytes 786440 | tf_op jit(solution)/shard_map/ppermute | solution.py:687
  94.2 14.9 %collective-permute-start.24 = (bf16[2,512,128]{2,1,0:T(8,128)(2,1)S(1)}, bf16[2,512,128]{2,1,0:T(8,128)(2,1)S(1)}, u32[]{:S(2)}, u32[]{:S(2)}) collective-permute-start(bf16[2,512,128]{2,1,0:T(8,128)(2,1)S(1)} %pad_maximum_fusion.4.refs_4_), channel_id=1, source_target_pairs={{0,1},{1,2},{2,3},{3,0},{4,5},{5,6},{6,7},{7,4},{8,9},{9,10},{10,1... | collective-permute-start | bytes 786440 | tf_op jit(solution)/shard_map/ppermute | solution.py:687
  95.1 25.2 %collective-permute-start.29 = (bf16[2,512,256]{2,1,0:T(8,128)(2,1)S(1)}, bf16[2,512,256]{2,1,0:T(8,128)(2,1)S(1)}, u32[]{:S(2)}, u32[]{:S(2)}) collective-permute-start(bf16[2,512,256]{2,1,0:T(8,128)(2,1)S(1)} %collective-permute-done.17.refs_14_), channel_id=1, source_target_pairs={{0,24},{4,28},{8,16},{12,20},{16,8},{20,12},{24,0},{28,4},{1,25},{... | collective-permute-start | bytes 1572872 | tf_op jit(solution)/shard_map/ppermute | solution.py:709
  103.5 11.2 %collective-permute-start.22 = (bf16[2,512,128]{2,1,0:T(8,128)(2,1)S(1)}, bf16[2,512,128]{2,1,0:T(8,128)(2,1)S(1)}, u32[]{:S(2)}, u32[]{:S(2)}) collective-permute-start(bf16[2,512,128]{2,1,0:T(8,128)(2,1)S(1)} %collective-permute-done.21.refs_1_), channel_id=1, source_target_pairs={{0,1},{1,2},{2,3},{3,0},{4,5},{5,6},{6,7},{7,4},{8,9},{9,10},{10,1... | collective-permute-start | bytes 786440 | tf_op jit(solution)/shard_map/ppermute | solution.py:687
  103.5 17.6 %collective-permute-start.28 = (bf16[2,512,256]{2,1,0:T(8,128)(2,1)S(1)}, bf16[2,512,256]{2,1,0:T(8,128)(2,1)S(1)}, u32[]{:S(2)}, u32[]{:S(2)}) collective-permute-start(bf16[2,512,256]{2,1,0:T(8,128)(2,1)S(1)} %collective-permute-done.17.refs_14_), channel_id=1, source_target_pairs={{0,16},{4,20},{8,24},{12,28},{16,0},{20,4},{24,8},{28,12},{1,17},{... | collective-permute-start | bytes 1572872 | tf_op jit(solution)/shard_map/ppermute | solution.py:709
  104.7 16.4 %collective-permute-start.27 = (bf16[2,512,256]{2,1,0:T(8,128)(2,1)S(1)}, bf16[2,512,256]{2,1,0:T(8,128)(2,1)S(1)}, u32[]{:S(2)}, u32[]{:S(2)}) collective-permute-start(bf16[2,512,256]{2,1,0:T(8,128)(2,1)S(1)} %collective-permute-done.17.refs_14_), channel_id=1, source_target_pairs={{0,8},{4,12},{8,0},{12,4},{16,24},{20,28},{24,16},{28,20},{1,9},{5... | collective-permute-start | bytes 1572872 | tf_op jit(solution)/shard_map/ppermute | solution.py:709
  109.1 11.2 %collective-permute-start.25 = (bf16[2,512,128]{2,1,0:T(8,128)(2,1)S(1)}, bf16[2,512,128]{2,1,0:T(8,128)(2,1)S(1)}, u32[]{:S(2)}, u32[]{:S(2)}) collective-permute-start(bf16[2,512,128]{2,1,0:T(8,128)(2,1)S(1)} %collective-permute-done.24.refs_5_), channel_id=1, source_target_pairs={{0,1},{1,2},{2,3},{3,0},{4,5},{5,6},{6,7},{7,4},{8,9},{9,10},{10,1... | collective-permute-start | bytes 786440 | tf_op jit(solution)/shard_map/ppermute | solution.py:687
  114.7 23.1 %collective-permute-start.30 = (bf16[4,1,512,256]{3,2,0,1:T(8,128)(2,1)S(1)}, bf16[4,1,512,256]{3,2,0,1:T(8,128)(2,1)S(1)}, u32[]{:S(2)}, u32[]{:S(2)}) collective-permute-start(bf16[4,1,512,256]{3,2,0,1:T(8,128)(2,1)S(1)} %maximum_bitcast_fusion), channel_id=1, source_target_pairs={{0,4},{4,0},{8,12},{12,8},{16,20},{20,16},{24,28},{28,24},{1,5},{5... | collective-permute-start | bytes 3145736 | tf_op jit(solution)/shard_map/ppermute | solution.py:717
  120.3 11.0 %collective-permute-start.23 = (bf16[2,512,128]{2,1,0:T(8,128)(2,1)S(1)}, bf16[2,512,128]{2,1,0:T(8,128)(2,1)S(1)}, u32[]{:S(2)}, u32[]{:S(2)}) collective-permute-start(bf16[2,512,128]{2,1,0:T(8,128)(2,1)S(1)} %collective-permute-done.22.refs_2_), channel_id=1, source_target_pairs={{0,1},{1,2},{2,3},{3,0},{4,5},{5,6},{6,7},{7,4},{8,9},{9,10},{10,1... | collective-permute-start | bytes 786440 | tf_op jit(solution)/shard_map/ppermute | solution.py:687
  120.3 15.6 %collective-permute-start.26 = (bf16[2,512,128]{2,1,0:T(8,128)(2,1)S(1)}, bf16[2,512,128]{2,1,0:T(8,128)(2,1)S(1)}, u32[]{:S(2)}, u32[]{:S(2)}) collective-permute-start(bf16[2,512,128]{2,1,0:T(8,128)(2,1)S(1)} %collective-permute-done.25.refs_6_), channel_id=1, source_target_pairs={{0,1},{1,2},{2,3},{3,0},{4,5},{5,6},{6,7},{7,4},{8,9},{9,10},{10,1... | collective-permute-start | bytes 786440 | tf_op jit(solution)/shard_map/ppermute | solution.py:687
  121.1 14.8 %collective-permute-start.31 = (bf16[2,512,256]{2,1,0:T(8,128)(2,1)S(1)}, bf16[2,512,256]{2,1,0:T(8,128)(2,1)S(1)}, u32[]{:S(2)}, u32[]{:S(2)}) collective-permute-start(bf16[2,512,256]{2,1,0:T(8,128)(2,1)S(1)} %collective-permute-done.17.refs_14_), channel_id=1, source_target_pairs={{0,4},{4,0},{8,12},{12,8},{16,20},{20,16},{24,28},{28,24},{1,5},{5... | collective-permute-start | bytes 1572872 | tf_op jit(solution)/shard_map/ppermute | solution.py:717
  121.1 14.8 %collective-permute-start.34 = (bf16[2,512,256]{2,1,0:T(8,128)(2,1)S(1)}, bf16[2,512,256]{2,1,0:T(8,128)(2,1)S(1)}, u32[]{:S(2)}, u32[]{:S(2)}) collective-permute-start(bf16[2,512,256]{2,1,0:T(8,128)(2,1)S(1)} %collective-permute-done.29.refs_17_), channel_id=1, source_target_pairs={{0,4},{4,0},{8,12},{12,8},{16,20},{20,16},{24,28},{28,24},{1,5},{5... | collective-permute-start | bytes 1572872 | tf_op jit(solution)/shard_map/ppermute | solution.py:717
  131.2 4.7 %collective-permute-start.33 = (bf16[2,512,256]{2,1,0:T(8,128)(2,1)S(1)}, bf16[2,512,256]{2,1,0:T(8,128)(2,1)S(1)}, u32[]{:S(2)}, u32[]{:S(2)}) collective-permute-start(bf16[2,512,256]{2,1,0:T(8,128)(2,1)S(1)} %collective-permute-done.28.refs_16_), channel_id=1, source_target_pairs={{0,4},{4,0},{8,12},{12,8},{16,20},{20,16},{24,28},{28,24},{1,5},{5... | collective-permute-start | bytes 1572872 | tf_op jit(solution)/shard_map/ppermute | solution.py:717
  135.9 1.9 collective-permute-start.32
  159.9 12.9 %collective-permute-start.37 = (bf16[128,512]{1,0:T(8,128)(2,1)S(1)}, bf16[128,512]{1,0:T(8,128)(2,1)S(1)}, u32[]{:S(2)}, u32[]{:S(2)}) collective-permute-start(bf16[128,512]{1,0:T(8,128)(2,1)S(1)} %get-tuple-element.118), channel_id=1, source_target_pairs={{0,1},{1,2},{2,3},{3,0},{4,5},{5,6},{6,7},{7,4},{8,9},{9,10},{10,1... | collective-permute-start | bytes 393224 | tf_op jit(solution)/shard_map/ppermute | solution.py:700
  160.0 13.0 %collective-permute-start.38 = (bf16[128,512]{1,0:T(8,128)(2,1)S(1)}, bf16[128,512]{1,0:T(8,128)(2,1)S(1)}, u32[]{:S(2)}, u32[]{:S(2)}) collective-permute-start(bf16[128,512]{1,0:T(8,128)(2,1)S(1)} %get-tuple-element.119), channel_id=1, source_target_pairs={{0,2},{1,3},{2,0},{3,1},{4,6},{5,7},{6,4},{7,5},{8,10},{9,11},{10,... | collective-permute-start | bytes 393224 | tf_op jit(solution)/shard_map/ppermute | solution.py:700
  160.1 12.9 %collective-permute-start.39 = (bf16[128,512]{1,0:T(8,128)(2,1)S(1)}, bf16[128,512]{1,0:T(8,128)(2,1)S(1)}, u32[]{:S(2)}, u32[]{:S(2)}) collective-permute-start(bf16[128,512]{1,0:T(8,128)(2,1)S(1)} %get-tuple-element.120), channel_id=1, source_target_pairs={{0,3},{1,0},{2,1},{3,2},{4,7},{5,4},{6,5},{7,6},{8,11},{9,8},{10,9... | collective-permute-start | bytes 393224 | tf_op jit(solution)/shard_map/ppermute | solution.py:700
  167.2 19.1 %collective-permute-start.35 = (bf16[512,512]{1,0:T(8,128)(2,1)S(1)}, bf16[512,512]{1,0:T(8,128)(2,1)S(1)}, u32[]{:S(2)}, u32[]{:S(2)}) collective-permute-start(bf16[512,512]{1,0:T(8,128)(2,1)S(1)} %down.3), channel_id=1, source_target_pairs={{0,1},{1,0},{2,3},{3,2},{4,5},{5,4},{6,7},{7,6},{8,9},{9,8},{10,11... | collective-permute-start | bytes 1572872 | tf_op jit(solution)/shard_map/ppermute | solution.py:788
  174.0 14.9 %collective-permute-start.42 = (bf16[128,512]{1,0:T(8,128)(2,1)S(1)}, bf16[128,512]{1,0:T(8,128)(2,1)S(1)}, u32[]{:S(2)}, u32[]{:S(2)}) collective-permute-start(bf16[128,512]{1,0:T(8,128)(2,1)S(1)} %multiply_convert_fusion.3.refs_0_), channel_id=1, source_target_pairs={{0,3},{1,0},{2,1},{3,2},{4,7},{5,4},{6,5},{7,6},{8,11},{9,8},{10,9... | collective-permute-start | bytes 393224 | tf_op jit(solution)/shard_map/ppermute | solution.py:700
  176.9 12.0 %collective-permute-start.41 = (bf16[128,512]{1,0:T(8,128)(2,1)S(1)}, bf16[128,512]{1,0:T(8,128)(2,1)S(1)}, u32[]{:S(2)}, u32[]{:S(2)}) collective-permute-start(bf16[128,512]{1,0:T(8,128)(2,1)S(1)} %multiply_convert_fusion.3.refs_0_), channel_id=1, source_target_pairs={{0,2},{1,3},{2,0},{3,1},{4,6},{5,7},{6,4},{7,5},{8,10},{9,11},{10,... | collective-permute-start | bytes 393224 | tf_op jit(solution)/shard_map/ppermute | solution.py:700
  178.1 14.6 %collective-permute-start.40 = (bf16[128,512]{1,0:T(8,128)(2,1)S(1)}, bf16[128,512]{1,0:T(8,128)(2,1)S(1)}, u32[]{:S(2)}, u32[]{:S(2)}) collective-permute-start(bf16[128,512]{1,0:T(8,128)(2,1)S(1)} %multiply_convert_fusion.3.refs_0_), channel_id=1, source_target_pairs={{0,1},{1,2},{2,3},{3,0},{4,5},{5,6},{6,7},{7,4},{8,9},{9,10},{10,1... | collective-permute-start | bytes 393224 | tf_op jit(solution)/shard_map/ppermute | solution.py:700
  194.9 2.4 %collective-permute-start.43 = (bf16[4,208,512]{2,1,0:T(8,128)(2,1)S(1)}, bf16[4,208,512]{2,1,0:T(8,128)(2,1)S(1)}, u32[]{:S(2)}, u32[]{:S(2)}) collective-permute-start(bf16[4,208,512]{2,1,0:T(8,128)(2,1)S(1)} %get-tuple-element.126), channel_id=1, source_target_pairs={{0,4},{4,0},{8,12},{12,8},{16,20},{20,16},{24,28},{28,24},{1,5},{5... | collective-permute-start | bytes 2555912 | tf_op jit(solution)/shard_map/ppermute | solution.py:717
  197.5 8.2 %collective-permute-start.44 = (bf16[208,512]{1,0:T(8,128)(2,1)S(1)}, bf16[208,512]{1,0:T(8,128)(2,1)S(1)}, u32[]{:S(2)}, u32[]{:S(2)}) collective-permute-start(bf16[208,512]{1,0:T(8,128)(2,1)S(1)} %get-tuple-element.128), channel_id=1, source_target_pairs={{0,8},{4,12},{8,0},{12,4},{16,24},{20,28},{24,16},{28,20},{1,9},{5... | collective-permute-start | bytes 638984 | tf_op jit(solution)/shard_map/ppermute | solution.py:709
  198.2 11.6 %collective-permute-start.45 = (bf16[208,512]{1,0:T(8,128)(2,1)S(1)}, bf16[208,512]{1,0:T(8,128)(2,1)S(1)}, u32[]{:S(2)}, u32[]{:S(2)}) collective-permute-start(bf16[208,512]{1,0:T(8,128)(2,1)S(1)} %get-tuple-element.129), channel_id=1, source_target_pairs={{0,16},{4,20},{8,24},{12,28},{16,0},{20,4},{24,8},{28,12},{1,17},{... | collective-permute-start | bytes 638984 | tf_op jit(solution)/shard_map/ppermute | solution.py:709
  199.7 10.0 %collective-permute-start.46 = (bf16[208,512]{1,0:T(8,128)(2,1)S(1)}, bf16[208,512]{1,0:T(8,128)(2,1)S(1)}, u32[]{:S(2)}, u32[]{:S(2)}) collective-permute-start(bf16[208,512]{1,0:T(8,128)(2,1)S(1)} %get-tuple-element.130), channel_id=1, source_target_pairs={{0,24},{4,28},{8,16},{12,20},{16,8},{20,12},{24,0},{28,4},{1,25},{... | collective-permute-start | bytes 638984 | tf_op jit(solution)/shard_map/ppermute | solution.py:709
  201.2 25.3 %collective-permute-start.48 = (bf16[512,512]{1,0:T(8,128)(2,1)S(1)}, bf16[512,512]{1,0:T(8,128)(2,1)S(1)}, u32[]{:S(2)}, u32[]{:S(2)}) collective-permute-start(bf16[512,512]{1,0:T(8,128)(2,1)S(1)} %add_convert_fusion.1), channel_id=1, source_target_pairs={{0,2},{1,3},{2,0},{3,1},{4,6},{5,7},{6,4},{7,5},{8,10},{9,11},{10,... | collective-permute-start | bytes 1572872 | tf_op jit(solution)/shard_map/ppermute | solution.py:788
  201.9 24.8 %collective-permute-start.36 = (bf16[512,512]{1,0:T(8,128)(2,1)S(1)}, bf16[512,512]{1,0:T(8,128)(2,1)S(1)}, u32[]{:S(2)}, u32[]{:S(2)}) collective-permute-start(bf16[512,512]{1,0:T(8,128)(2,1)S(1)} %get-tuple-element.115), channel_id=1, source_target_pairs={{0,1},{1,0},{2,3},{3,2},{4,5},{5,4},{6,7},{7,6},{8,9},{9,8},{10,11... | collective-permute-start | bytes 1572872 | tf_op jit(solution)/shard_map/ppermute | solution.py:788
  209.9 16.7 %collective-permute-start.47 = (bf16[208,512]{1,0:T(8,128)(2,1)S(1)}, bf16[208,512]{1,0:T(8,128)(2,1)S(1)}, u32[]{:S(2)}, u32[]{:S(2)}) collective-permute-start(bf16[208,512]{1,0:T(8,128)(2,1)S(1)} %add_convert_fusion.2.refs_0_), channel_id=1, source_target_pairs={{0,24},{4,28},{8,16},{12,20},{16,8},{20,12},{24,0},{28,4},{1,25},{... | collective-permute-start | bytes 638984 | tf_op jit(solution)/shard_map/ppermute | solution.py:709
  211.4 15.6 %collective-permute-start.50 = (bf16[208,512]{1,0:T(8,128)(2,1)S(1)}, bf16[208,512]{1,0:T(8,128)(2,1)S(1)}, u32[]{:S(2)}, u32[]{:S(2)}) collective-permute-start(bf16[208,512]{1,0:T(8,128)(2,1)S(1)} %add_convert_fusion.2.refs_0_), channel_id=1, source_target_pairs={{0,16},{4,20},{8,24},{12,28},{16,0},{20,4},{24,8},{28,12},{1,17},{... | collective-permute-start | bytes 638984 | tf_op jit(solution)/shard_map/ppermute | solution.py:709
  212.9 14.3 %collective-permute-start.49 = (bf16[208,512]{1,0:T(8,128)(2,1)S(1)}, bf16[208,512]{1,0:T(8,128)(2,1)S(1)}, u32[]{:S(2)}, u32[]{:S(2)}) collective-permute-start(bf16[208,512]{1,0:T(8,128)(2,1)S(1)} %add_convert_fusion.2.refs_0_), channel_id=1, source_target_pairs={{0,8},{4,12},{8,0},{12,4},{16,24},{20,28},{24,16},{28,20},{1,9},{5... | collective-permute-start | bytes 638984 | tf_op jit(solution)/shard_map/ppermute | solution.py:709
  226.5 2.1 collective-permute-start.51
  226.7 2.2 collective-permute-start.54
  227.0 1.6 collective-permute-start.53
  227.2 1.7 collective-permute-start.52
  (7 other events, 36.5 us)
